TPU v7x, 32 devices: a whole 2x2x4 slice. The times are simulated.
32 devices in a mesh: section: 2 (over y), sample: 4 (over z), seq: 4 (over x, core).
Axes of the slice: x: 2, y: 2, z: 4, core: 2. Of those that a mesh axis runs over, the one named last changes fastest.
Arguments:
- first_rows: bfloat16 [2, 4, 512, 2048], P('section', 'sample', 'seq'), may hold values from -10 to 10
- second_rows: bfloat16 [2, 4, 512, 2048], P('section', 'sample', 'seq'), may hold values from -6 to 6
- alignment: int32 [4, 4, 2], P('sample', 'seq'), may hold values from 0 to 3, as said below
- diffusion_mask: int32 [4, 512], P('sample', 'seq'), may hold values 0 or 1
- source_length: int32 [4], P('sample'), may hold values from 256 to 512, as said below
- target_length: int32 [4], P('sample'), may hold values from 256 to 512
Outputs:
- grad_first: bfloat16 [2, 4, 512, 2048], P('section', 'sample', 'seq')
- grad_second: bfloat16 [2, 4, 512, 2048], P('section', 'sample', 'seq')
Inputs may be any that keep to these rules, and one draw needn't show every extreme that they name: `alignment`: each list names 2 different blocks from t - 1 to t + 1 for target block t; where block t holds a target position below the target length, every listed block starts below the source length. `source_length`: at least the sample's target length.
All inputs are finite; a program needn't handle non-finite values. No bound on the sum of `diffusion_mask` on one device may be relied on, other than what follows from the above.
Results may differ from a plain program's by a relative error of at most 0.013.
Values may be sent and summed in bfloat16 or wider, within the bound.
No kernel may reach another device: no remote copies, remote signals or barrier semaphores. Data moves between devices by JAX's collectives and lax.ppermute only.
A program may use at most 64 MiB of HBM per device.

v0:
```python
import jax
import jax.numpy as jnp
from jax import lax
from jax.sharding import PartitionSpec as P

HEADS = 32
HDIM = 64
INNER = 2048
BLK = 128
NLIST = 2
WIN = 1


def shifted(array, axis, by):
    count = lax.axis_size(axis)
    pairs = [(i, i + by) for i in range(count) if 0 <= i + by < count]
    return lax.ppermute(array, axis, pairs)


def padded(array, sides, width):
    for axis, dim in sides:
        count, length = (lax.axis_size(axis), array.shape[dim])
        up = [(i, (i + 1) % count) for i in range(count - 1)]
        down = [(j, i) for i, j in up]
        last = lax.slice_in_dim(array, length - width, length, axis=dim)
        first = lax.slice_in_dim(array, 0, width, axis=dim)
        before = lax.ppermute(last, axis, up)
        after = lax.ppermute(first, axis, down)
        array = jnp.concatenate([before, array, after], axis=dim)
    return array


def attend_local(query_blk, cot_blk, key_rows, value_rows, key_valid, query_valid, cot_keep):
    scale = HDIM ** (-0.5)
    queries = query_blk.reshape(BLK, HEADS, HDIM)
    keys = key_rows.reshape(NLIST * BLK, HEADS, HDIM)
    values = value_rows.reshape(NLIST * BLK, HEADS, HDIM)
    scores = jnp.einsum("qhd,khd->hqk", queries, keys, preferred_element_type=jnp.float32) * scale
    scores = jnp.where(key_valid[None, None, :], scores, -1e30)
    peak = jnp.max(scores, axis=-1, keepdims=True)
    expo = jnp.exp(scores - peak)
    probs = expo / jnp.sum(expo, axis=-1, keepdims=True)
    probs_low = probs.astype(jnp.bfloat16)
    attended = jnp.einsum("hqk,khd->qhd", probs_low, values, preferred_element_type=jnp.float32)
    attended = jnp.where(query_valid[:, None, None], attended, jnp.float32(0.0))
    out_low = attended.astype(jnp.bfloat16)
    cot = cot_blk.reshape(BLK, HEADS, HDIM)
    cot = jnp.where(cot_keep[:, None, None], cot, jnp.zeros_like(cot))
    delta = jnp.einsum("qhd,qhd->hq", cot, out_low, preferred_element_type=jnp.float32)[:, :, None]
    dprob = jnp.einsum("qhd,khd->hqk", cot, values, preferred_element_type=jnp.float32)
    dscore_low = (probs * (dprob - delta)).astype(jnp.bfloat16)
    dvalue = jnp.einsum("hqk,qhd->khd", probs_low, cot, preferred_element_type=jnp.float32)
    dquery = (
        jnp.einsum("hqk,khd->qhd", dscore_low, keys, preferred_element_type=jnp.float32) * scale
    )
    dkey = (
        jnp.einsum("hqk,qhd->khd", dscore_low, queries, preferred_element_type=jnp.float32) * scale
    )
    return (
        out_low.reshape(BLK, INNER),
        dquery.astype(jnp.bfloat16).reshape(BLK, INNER),
        dkey.reshape(NLIST * BLK, INNER),
        dvalue.reshape(NLIST * BLK, INNER),
    )


def on_device(first_rows, second_rows, alignment, diffusion_mask, source_length, target_length):
    rows_here = first_rows.shape[2]
    width = first_rows.shape[3]
    block_count = alignment.shape[1]
    rim = WIN * BLK
    section_id = lax.axis_index("section")
    shard_id = lax.axis_index("seq")
    on_encoder = section_id == 0
    holding = jnp.stack([first_rows[0, 0], second_rows[0, 0]])
    memory = shifted(holding, "section", 1)
    window = padded(memory, (("seq", 1),), rim)
    window_start = shard_id * rows_here - rim
    source_len = source_length[0]
    target_len = target_length[0]
    query_blocks = holding[0].reshape(block_count, BLK, width)
    cot_blocks = holding[1].reshape(block_count, BLK, width)
    mask_blocks = diffusion_mask[0].reshape(block_count, BLK)
    lists_here = alignment[0]
    inside = jnp.arange(BLK, dtype=jnp.int32)

    def step(carry, index):
        key_grad, value_grad = carry
        chosen = lists_here[index]
        starts = [chosen[slot] * BLK - window_start for slot in range(NLIST)]
        key_rows = jnp.concatenate(
            [lax.dynamic_slice_in_dim(window[0], starts[slot], BLK, 0) for slot in range(NLIST)], 0
        )
        value_rows = jnp.concatenate(
            [lax.dynamic_slice_in_dim(window[1], starts[slot], BLK, 0) for slot in range(NLIST)], 0
        )
        key_pos = (chosen[:, None] * BLK + inside[None, :]).reshape(NLIST * BLK)
        key_valid = key_pos < source_len
        row_pos = (shard_id * block_count + index) * BLK + inside
        query_valid = row_pos < target_len
        cot_keep = query_valid & (mask_blocks[index] == 1)
        out_low, dquery, dkey, dvalue = attend_local(
            query_blocks[index],
            cot_blocks[index],
            key_rows,
            value_rows,
            key_valid,
            query_valid,
            cot_keep,
        )
        for slot in range(NLIST):
            older_key = lax.dynamic_slice_in_dim(key_grad, starts[slot], BLK, 0)
            key_grad = lax.dynamic_update_slice_in_dim(
                key_grad, older_key + dkey[slot * BLK : (slot + 1) * BLK], starts[slot], 0
            )
            older_value = lax.dynamic_slice_in_dim(value_grad, starts[slot], BLK, 0)
            value_grad = lax.dynamic_update_slice_in_dim(
                value_grad, older_value + dvalue[slot * BLK : (slot + 1) * BLK], starts[slot], 0
            )
        return ((key_grad, value_grad), (out_low, dquery))

    span = rows_here + 2 * rim
    start = (jnp.zeros((span, width), jnp.float32), jnp.zeros((span, width), jnp.float32))
    (key_grad, value_grad), (outs, dqueries) = lax.scan(
        step, start, jnp.arange(block_count, dtype=jnp.int32)
    )
    grads = jnp.stack([key_grad, value_grad])
    middle = grads[:, rim : rim + rows_here]
    from_below = shifted(grads[:, rows_here + rim :], "seq", 1)
    from_above = shifted(grads[:, :rim], "seq", -1)
    middle = middle.at[:, :rim].add(from_below)
    middle = middle.at[:, rows_here - rim :].add(from_above)
    memory_grads = middle.astype(jnp.bfloat16)
    memory_grads = shifted(memory_grads, "section", -1)
    first_out = jnp.where(on_encoder, memory_grads[0], dqueries.reshape(rows_here, width))
    second_out = jnp.where(on_encoder, memory_grads[1], outs.reshape(rows_here, width))
    return (first_out[None, None], second_out[None, None])


def solution(mesh):
    placed = (
        P("section", "sample", "seq", None),
        P("section", "sample", "seq", None),
        P("sample", "seq", None),
        P("sample", "seq"),
        P("sample"),
        P("sample"),
    )
    return jax.shard_map(
        on_device,
        mesh=mesh,
        in_specs=placed,
        out_specs=(P("section", "sample", "seq", None), P("section", "sample", "seq", None)),
        check_vma=False,
    )
```

profile of v0, /device:TPU:18, one launch (start us, length us, event | category | flops | bytes accessed | tf_op | source)
XLA Modules:
  0.0 135.4 jit_solution(1680602268866607138)
XLA Ops:
  0.7 1.4 pad_maximum_fusion.1
  2.0 3.5 %collective-permute-start = (bf16[2,128,2048]{2,1,0:T(8,128)(2,1)S(1)}, bf16[2,128,2048]{2,1,0:T(8,128)(2,1)S(1)}, u32[]{:S(2)}, u32[]{:S(2)}) collective-permute-start(bf16[2,128,2048]{2,1,0:T(8,128)(2,1)S(1)} %pad_maximum_fusion.1), channel_id=1, source_target_pairs={{0,16},{1,17},{2,18},{3,19},{4,20},{5,21},{6,22},{7,23},{8,24},{9,... | collective-permute-start | bytes 3145736 | tf_op jit(solution)/shard_map/ppermute | solution.py:17
  5.5 22.3 %collective-permute-done = bf16[2,128,2048]{2,1,0:T(8,128)(2,1)S(1)} collective-permute-done((bf16[2,128,2048]{2,1,0:T(8,128)(2,1)S(1)}, bf16[2,128,2048]{2,1,0:T(8,128)(2,1)S(1)}, u32[]{:S(2)}, u32[]{:S(2)}) %collective-permute-start) | collective-permute-done | bytes 1048608 | tf_op jit(solution)/shard_map/ppermute | solution.py:17
  27.8 1.9 %collective-permute-start.1 = (bf16[2,128,2048]{2,1,0:T(8,128)(2,1)S(1)}, bf16[2,128,2048]{2,1,0:T(8,128)(2,1)}, u32[]{:S(2)}, u32[]{:S(2)}) collective-permute-start(bf16[2,128,2048]{2,1,0:T(8,128)(2,1)S(1)} %collective-permute-done), channel_id=1, source_target_pairs={{0,1},{1,2},{2,3},{4,5},{5,6},{6,7},{8,9},{9,10},{10,11},{12,13},{... | collective-permute-start | bytes 3145736 | tf_op jit(solution)/shard_map/ppermute | solution.py:27
  29.8 1.3 copy.29
  31.4 3.6 %collective-permute-start.2 = (bf16[2,128,2048]{2,1,0:T(8,128)(2,1)S(1)}, bf16[2,128,2048]{2,1,0:T(8,128)(2,1)}, u32[]{:S(2)}, u32[]{:S(2)}) collective-permute-start(bf16[2,128,2048]{2,1,0:T(8,128)(2,1)S(1)} %collective-permute-done), channel_id=1, source_target_pairs={{1,0},{2,1},{3,2},{5,4},{6,5},{7,6},{9,8},{10,9},{11,10},{13,12},{... | collective-permute-start | bytes 3145736 | tf_op jit(solution)/shard_map/ppermute | solution.py:28
  35.0 0.6 fusion.33
  38.3 5.7 %collective-permute-done.1 = bf16[2,128,2048]{2,1,0:T(8,128)(2,1)} collective-permute-done((bf16[2,128,2048]{2,1,0:T(8,128)(2,1)S(1)}, bf16[2,128,2048]{2,1,0:T(8,128)(2,1)}, u32[]{:S(2)}, u32[]{:S(2)}) %collective-permute-start.1) | collective-permute-done | bytes 1048608 | tf_op jit(solution)/shard_map/ppermute | solution.py:27
  44.1 1.3 constant_dynamic-update-slice_fusion.2
  45.5 1.9 %collective-permute-done.2 = bf16[2,128,2048]{2,1,0:T(8,128)(2,1)} collective-permute-done((bf16[2,128,2048]{2,1,0:T(8,128)(2,1)S(1)}, bf16[2,128,2048]{2,1,0:T(8,128)(2,1)}, u32[]{:S(2)}, u32[]{:S(2)}) %collective-permute-start.2) | collective-permute-done | bytes 1048608 | tf_op jit(solution)/shard_map/ppermute | solution.py:28
  47.3 1.3 constant_dynamic-update-slice_fusion
  48.7 0.4 fusion.30
  49.2 1.0 copy.27
  50.2 1.0 copy.26
  51.5 0.3 copy.30
  51.8 1.8 %fusion.17 = f32[32,256,128]{2,1,0:T(8,128)S(1)} fusion(bf16[128,32,64]{0,2,1:T(8,128)(2,1)S(1)} %bitcast.72, bf16[128,32,64]{0,2,1:T(8,128)(2,1)S(1)} %bitcast.84, bf16[128,32,64]{0,2,1:T(8,128)(2,1)} %bitcast.85), kind=kOutput, calls=%fused_computation.35 | convolution fusion | flops 136314880 | bytes 5767168 | tf_op jit(solution)/shard_map/while/body/eval_jaxpr/qhd,khd->hqk/dot_general | solution.py:38
  53.6 1.7 %fusion.34 = (f32[32,128]{1,0:T(8,128)S(1)}, f32[32,128,256]{1,2,0:T(8,128)S(1)}) fusion(f32[32,256,128]{2,1,0:T(8,128)S(1)} %fusion.17, pred[256]{0:T(512)(128)(4,1)S(1)} %compare_bitcast_fusion), kind=kOutput, calls=%fused_computation.68 | output fusion | flops 6291711 | bytes 8405248 | tf_op jit(solution)/shard_map/while/body/eval_jaxpr/sub | solution.py:41
  55.3 0.5 fusion.13
  55.9 2.2 %convolution_bitcast_fusion = f32[256,32,64]{0,2,1:T(8,128)} fusion(bf16[32,128,256]{1,2,0:T(8,128)(2,1)S(1)} %fusion.13, bf16[128,32,64]{0,2,1:T(8,128)(2,1)S(1)} %bitcast.78, pred[128]{0:T(512)(128)(4,1)S(1)} %get-tuple-element.87), kind=kOutput, calls=%fused_computation.23 | convolution fusion | flops 134479872 | bytes 4718720 | tf_op jit(solution)/shard_map/while/body/eval_jaxpr/hqk,qhd->khd/dot_general | solution.py:52
  58.1 1.3 fusion.16
  59.4 1.0 multiply_convert_fusion
  60.4 0.8 multiply_bitcast_fusion
  61.3 1.3 fusion.31
  62.6 0.3 copy.35
  62.9 0.4 broadcast.163.clone
  63.6 1.4 %copy-done.2 = f32[384,2048]{1,0:T(8,128)} copy-done((f32[384,2048]{1,0:T(8,128)}, f32[384,2048]{1,0:T(8,128)S(1)}, u32[]{:S(2)}) %copy-start.2) | copy-done | bytes 3145752
  65.0 2.6 %copy.36 = f32[128,2048]{1,0:T(8,128)} copy(f32[128,2048]{0,1:T(8,128)} %bitcast.75) | data formatting | bytes 2097152 | tf_op jit(solution)/shard_map/while/body/eval_jaxpr/slice | solution.py:114
  67.6 3.2 %fusion.32 = (f32[128,32,64]{0,2,1:T(8,128)}, f32[128,32,64]{0,2,1:T(8,128)}) fusion(f32[256,32,64]{0,2,1:T(8,128)} %convolution_bitcast_fusion), kind=kLoop, calls=%fused_computation.66 | loop fusion | bytes 4194304 | tf_op jit(solution)/shard_map/while/body/eval_jaxpr/slice | solution.py:118
  70.8 2.6 %copy.38 = f32[128,2048]{1,0:T(8,128)} copy(f32[128,2048]{0,1:T(8,128)} %bitcast.77) | data formatting | bytes 2097152 | tf_op jit(solution)/shard_map/while/body/eval_jaxpr/slice | solution.py:118
  73.4 0.4 broadcast.163.clone.1
  73.7 0.9 copy-done.3
  74.7 1.7 %copy.60 = f32[1,384,2048]{2,1,0:T(8,128)} copy(f32[1,384,2048]{2,1,0:T(8,128)S(1)} %bitcast.70) | data formatting | bytes 6291456
  76.4 1.1 copy-done.1
  77.5 2.5 %copy.39 = f32[128,2048]{1,0:T(8,128)} copy(f32[128,2048]{0,1:T(8,128)} %bitcast.74) | data formatting | bytes 2097152 | tf_op jit(solution)/shard_map/while/body/eval_jaxpr/slice | solution.py:118
  80.0 1.8 %bitcast_dynamic-update-slice_fusion.1 = f32[1,384,2048]{2,1,0:T(8,128)S(1)} fusion(f32[1,384,2048]{2,1,0:T(8,128)S(1)} %copy.58, s32[]{:T(128)S(6)} %select_n.70, f32[128,2048]{1,0:T(8,128)} %copy.36, f32[384,2048]{1,0:T(8,128)} %copy-done.2), kind=kLoop, calls=%fused_computation.32 | loop fusion | flops 262144 | bytes 3145732 | tf_op jit(solution)/shard_map/while/body/eval_jaxpr/dynamic_update_slice | solution.py:113
  81.8 0.7 copy-done
  82.6 1.7 %bitcast_dynamic-update-slice_fusion = f32[1,384,2048]{2,1,0:T(8,128)S(1)} fusion(f32[1,384,2048]{2,1,0:T(8,128)S(1)} %copy-done, s32[]{:T(128)S(6)} %select_n.70, f32[128,2048]{1,0:T(8,128)} %copy.39, f32[384,2048]{1,0:T(8,128)} %copy-done.1), kind=kLoop, calls=%fused_computation.31 | loop fusion | flops 262144 | bytes 3145732 | tf_op jit(solution)/shard_map/while/body/eval_jaxpr/dynamic_update_slice | solution.py:117
  84.2 0.5 fusion.5
  84.7 3.9 %collective-permute-start.4 = (f32[2,128,2048]{2,1,0:T(8,128)S(1)}, f32[2,128,2048]{2,1,0:T(8,128)S(1)}, u32[]{:S(2)}, u32[]{:S(2)}) collective-permute-start(f32[2,128,2048]{2,1,0:T(8,128)S(1)} %get-tuple-element.90), channel_id=1, source_target_pairs={{1,0},{2,1},{3,2},{5,4},{6,5},{7,6},{9,8},{10,9},{11,10},{13,12},{... | collective-permute-start | bytes 6291464 | tf_op jit(solution)/shard_map/ppermute | solution.py:17
  88.7 1.9 %collective-permute-start.3 = (f32[2,128,2048]{2,1,0:T(8,128)S(1)}, f32[2,128,2048]{2,1,0:T(8,128)S(1)}, u32[]{:S(2)}, u32[]{:S(2)}) collective-permute-start(f32[2,128,2048]{2,1,0:T(8,128)S(1)} %get-tuple-element.89), channel_id=1, source_target_pairs={{0,1},{1,2},{2,3},{4,5},{5,6},{6,7},{8,9},{9,10},{10,11},{12,13},{... | collective-permute-start | bytes 6291464 | tf_op jit(solution)/shard_map/ppermute | solution.py:17
  90.6 21.6 %collective-permute-done.4 = f32[2,128,2048]{2,1,0:T(8,128)S(1)} collective-permute-done((f32[2,128,2048]{2,1,0:T(8,128)S(1)}, f32[2,128,2048]{2,1,0:T(8,128)S(1)}, u32[]{:S(2)}, u32[]{:S(2)}) %collective-permute-start.4) | collective-permute-done | bytes 2097184 | tf_op jit(solution)/shard_map/ppermute | solution.py:17
  112.2 3.8 %collective-permute-done.3 = f32[2,128,2048]{2,1,0:T(8,128)S(1)} collective-permute-done((f32[2,128,2048]{2,1,0:T(8,128)S(1)}, f32[2,128,2048]{2,1,0:T(8,128)S(1)}, u32[]{:S(2)}, u32[]{:S(2)}) %collective-permute-start.3) | collective-permute-done | bytes 2097184 | tf_op jit(solution)/shard_map/ppermute | solution.py:17
  116.0 1.4 %fusion.9 = bf16[2,128,2048]{2,1,0:T(8,128)(2,1)} fusion(f32[2,128,2048]{2,1,0:T(8,128)S(1)} %collective-permute-done.4, f32[2,128,2048]{2,1,0:T(8,128)S(1)} %collective-permute-done.3, f32[1,384,2048]{2,1,0:T(8,128)S(1)} %bitcast_dynamic-update-slice_fusion.1, f32[1,384,2048]{2,1,0:T(8,128)S(1)} %bitcast_dynamic-update-slice_fusion), kind=kLoop, calls=%fused_computation.15 | loop fusion | flops 2097152 | bytes 11534336 | tf_op jit(solution)/shard_map/convert_element_type | solution.py:133
  117.4 1.3 collective-permute-start.5
  118.7 1.2 copy.42
  120.0 2.4 %fusion.15 = bf16[32,64,128]{2,1,0:T(8,128)(2,1)S(1)} fusion(bf16[32,128,256]{1,2,0:T(8,128)(2,1)} %copy-done.4, bf16[128,32,64]{0,2,1:T(8,128)(2,1)} %bitcast.83, bf16[128,32,64]{0,2,1:T(8,128)(2,1)} %bitcast.86), kind=kOutput, calls=%fused_computation.27 | convolution fusion | flops 136839168 | bytes 3670016 | tf_op jit(solution)/shard_map/while/body/eval_jaxpr/hqk,khd->qhd/dot_general | solution.py:54
  122.6 11.7 %collective-permute-done.5 = bf16[2,128,2048]{2,1,0:T(8,128)(2,1)S(1)} collective-permute-done((bf16[2,128,2048]{2,1,0:T(8,128)(2,1)}, bf16[2,128,2048]{2,1,0:T(8,128)(2,1)S(1)}, u32[]{:S(2)}, u32[]{:S(2)}) %collective-permute-start.5) | collective-permute-done | bytes 1048608 | tf_op jit(solution)/shard_map/ppermute | solution.py:17
  134.3 1.1 fusion.18
  (25 shorter events, 1.5 us)
Async XLA Ops:
  0.6 30.5 %copy-start.5 = (bf16[1,1,128,2048]{3,2,1,0:T(8,128)(2,1)S(1)}, bf16[1,1,128,2048]{3,2,1,0:T(8,128)(2,1)}, u32[]{:S(2)}) copy-start(bf16[1,1,128,2048]{3,2,1,0:T(8,128)(2,1)} %param.14) | copy-start | bytes 1572868
  0.6 30.7 %copy-start.7 = (s32[1,1,2]{2,1,0:T(1,128)S(1)}, s32[1,1,2]{2,1,0:T(1,128)}, u32[]{:S(2)}) copy-start(s32[1,1,2]{2,1,0:T(1,128)} %param.16) | copy-start | bytes 28
  0.7 37.7 %copy-start.8 = (s32[1,128]{1,0:T(1,128)S(1)}, s32[1,128]{1,0:T(1,128)}, u32[]{:S(2)}) copy-start(s32[1,128]{1,0:T(1,128)} %param.17) | copy-start | bytes 1540
  2.0 25.8 %collective-permute-start = (bf16[2,128,2048]{2,1,0:T(8,128)(2,1)S(1)}, bf16[2,128,2048]{2,1,0:T(8,128)(2,1)S(1)}, u32[]{:S(2)}, u32[]{:S(2)}) collective-permute-start(bf16[2,128,2048]{2,1,0:T(8,128)(2,1)S(1)} %pad_maximum_fusion.1), channel_id=1, source_target_pairs={{0,16},{1,17},{2,18},{3,19},{4,20},{5,21},{6,22},{7,23},{8,24},{9,... | collective-permute-start | bytes 3145736 | tf_op jit(solution)/shard_map/ppermute | solution.py:17
  27.8 16.2 %collective-permute-start.1 = (bf16[2,128,2048]{2,1,0:T(8,128)(2,1)S(1)}, bf16[2,128,2048]{2,1,0:T(8,128)(2,1)}, u32[]{:S(2)}, u32[]{:S(2)}) collective-permute-start(bf16[2,128,2048]{2,1,0:T(8,128)(2,1)S(1)} %collective-permute-done), channel_id=1, source_target_pairs={{0,1},{1,2},{2,3},{4,5},{5,6},{6,7},{8,9},{9,10},{10,11},{12,13},{... | collective-permute-start | bytes 3145736 | tf_op jit(solution)/shard_map/ppermute | solution.py:27
  31.4 15.9 %collective-permute-start.2 = (bf16[2,128,2048]{2,1,0:T(8,128)(2,1)S(1)}, bf16[2,128,2048]{2,1,0:T(8,128)(2,1)}, u32[]{:S(2)}, u32[]{:S(2)}) collective-permute-start(bf16[2,128,2048]{2,1,0:T(8,128)(2,1)S(1)} %collective-permute-done), channel_id=1, source_target_pairs={{1,0},{2,1},{3,2},{5,4},{6,5},{7,6},{9,8},{10,9},{11,10},{13,12},{... | collective-permute-start | bytes 3145736 | tf_op jit(solution)/shard_map/ppermute | solution.py:28
  50.2 1.6 %copy-start.6 = (bf16[1,128,2048]{1,2,0:T(8,128)(2,1)S(1)}, bf16[1,128,2048]{1,2,0:T(8,128)(2,1)}, u32[]{:S(2)}) copy-start(bf16[1,128,2048]{1,2,0:T(8,128)(2,1)} %copy.27) | copy-start | bytes 1572868
  60.4 2.1 %copy-start.4 = (bf16[32,128,256]{1,2,0:T(8,128)(2,1)}, bf16[32,128,256]{1,2,0:T(8,128)(2,1)S(1)}, u32[]{:S(2)}) copy-start(bf16[32,128,256]{1,2,0:T(8,128)(2,1)S(1)} %multiply_convert_fusion) | copy-start | bytes 6291460
  63.4 1.7 %copy-start.2 = (f32[384,2048]{1,0:T(8,128)}, f32[384,2048]{1,0:T(8,128)S(1)}, u32[]{:S(2)}) copy-start(f32[384,2048]{1,0:T(8,128)S(1)} %constant_dynamic-update-slice_fusion.4) | copy-start | bytes 9437188
  73.4 1.2 copy-start.3
  74.7 2.8 %copy-start.1 = (f32[384,2048]{1,0:T(8,128)}, f32[384,2048]{1,0:T(8,128)S(1)}, u32[]{:S(2)}) copy-start(f32[384,2048]{1,0:T(8,128)S(1)} %constant_dynamic-update-slice_fusion.3) | copy-start | bytes 9437188
  80.0 2.5 %copy-start = (f32[1,384,2048]{2,1,0:T(8,128)S(1)}, f32[1,384,2048]{2,1,0:T(8,128)}, u32[]{:S(2)}) copy-start(f32[1,384,2048]{2,1,0:T(8,128)} %copy.60) | copy-start | bytes 9437188
  84.7 27.5 %collective-permute-start.4 = (f32[2,128,2048]{2,1,0:T(8,128)S(1)}, f32[2,128,2048]{2,1,0:T(8,128)S(1)}, u32[]{:S(2)}, u32[]{:S(2)}) collective-permute-start(f32[2,128,2048]{2,1,0:T(8,128)S(1)} %get-tuple-element.90), channel_id=1, source_target_pairs={{1,0},{2,1},{3,2},{5,4},{6,5},{7,6},{9,8},{10,9},{11,10},{13,12},{... | collective-permute-start | bytes 6291464 | tf_op jit(solution)/shard_map/ppermute | solution.py:17
  88.7 27.4 %collective-permute-start.3 = (f32[2,128,2048]{2,1,0:T(8,128)S(1)}, f32[2,128,2048]{2,1,0:T(8,128)S(1)}, u32[]{:S(2)}, u32[]{:S(2)}) collective-permute-start(f32[2,128,2048]{2,1,0:T(8,128)S(1)} %get-tuple-element.89), channel_id=1, source_target_pairs={{0,1},{1,2},{2,3},{4,5},{5,6},{6,7},{8,9},{9,10},{10,11},{12,13},{... | collective-permute-start | bytes 6291464 | tf_op jit(solution)/shard_map/ppermute | solution.py:17
  117.4 16.9 %collective-permute-start.5 = (bf16[2,128,2048]{2,1,0:T(8,128)(2,1)}, bf16[2,128,2048]{2,1,0:T(8,128)(2,1)S(1)}, u32[]{:S(2)}, u32[]{:S(2)}) collective-permute-start(bf16[2,128,2048]{2,1,0:T(8,128)(2,1)} %fusion.9), channel_id=1, source_target_pairs={{16,0},{17,1},{18,2},{19,3},{20,4},{21,5},{22,6},{23,7},{24,8},{25... | collective-permute-start | bytes 3145736 | tf_op jit(solution)/shard_map/ppermute | solution.py:17
where the time goes:
time: 136 us; the launch traced here: 135 us
  waiting for transfers between devices  67 us (49%)
  local copies, waits for them, and re-layouts  28.8 us (21%)
  starting transfers between devices  16.2 us (12%)
  other arithmetic  10.1 us (7%)
  matrix products  9.64 us (7%)
  between operations  3.58 us (3%)
    ppermute x4, waiting for transfers between devices, shifted(): return lax.ppermute(array, axis, pairs)  59.4 us
    ppermute x4, starting transfers between devices, shifted(): return lax.ppermute(array, axis, pairs)  10.6 us
    unnamed x24, local copies, waits for them, and re-layouts  9 us
    slice x3, local copies, waits for them, and re-layouts, step(): dvalue[slot * BLK:(slot + 1) * BLK]  8.29 us
    ppermute x1, waiting for transfers between devices, padded(): before = lax.ppermute(last, axis, up)  5.73 us
    slice x3, local copies, waits for them, and re-layouts, step(): dkey[slot * BLK:(slot + 1) * BLK]  4.17 us
    ppermute x1, starting transfers between devices, padded(): after = lax.ppermute(first, axis, down)  3.64 us
  transfers between devices with their start and end apart: 6, of which 6 were waited for; matrix products, arithmetic and copies ran while one was open for 6% of the time, Pallas kernels for 0%

commit v1 on v0

v1 whole, which is shorter than its diff:
```python
import functools

import jax
import jax.numpy as jnp
from jax import lax
from jax.experimental import pallas as pl
from jax.experimental.pallas import tpu as pltpu
from jax.sharding import PartitionSpec as P

HDIM = 64
BLK = 128
NLIST = 2
LANES = 128
SCALE = HDIM ** (-0.5)
FLOOR = -1e30


def contract(left, right, left_dim, right_dim):
    return lax.dot_general(
        left, right, (((left_dim,), (right_dim,)), ((), ())), preferred_element_type=jnp.float32
    )


def attend_kernel(seq_count, lists, lengths, rows, out, key_grad, value_grad):
    per_device = rows.shape[2] // BLK
    block_count = seq_count * per_device
    width = rows.shape[3]
    tile = min(width, LANES)
    heads = tile // HDIM
    source_len = lengths[0]
    target_len = lengths[1]
    key_grad[...] = jnp.zeros_like(key_grad)
    value_grad[...] = jnp.zeros_like(value_grad)
    key_inside = lax.broadcasted_iota(jnp.int32, (BLK, 1), 0)
    lane_head = lax.broadcasted_iota(jnp.int32, (BLK, tile), 1) // HDIM

    def place(block):
        if per_device == 1:
            return block, pl.ds(0, BLK)
        return block // per_device, pl.ds((block % per_device) * BLK, BLK)

    def step(block, carry):
        chosen = [lists[block, slot] for slot in range(NLIST)]
        places = [place(index) for index in chosen]
        target, target_rows = place(block)
        key_valid = jnp.concatenate(
            [index * BLK + key_inside < source_len for index in chosen], axis=0
        )
        live = block * BLK + key_inside < target_len
        for first in range(0, width, tile):
            lanes = pl.ds(first, tile)
            keys = jnp.concatenate([rows[dev, 0, here, lanes] for dev, here in places], axis=0)
            values = jnp.concatenate([rows[dev, 1, here, lanes] for dev, here in places], axis=0)
            queries = rows[seq_count + target, 0, target_rows, lanes] * jnp.bfloat16(SCALE)
            cots = rows[seq_count + target, 1, target_rows, lanes]
            none = jnp.zeros_like(queries)
            queries = jnp.concatenate(
                [jnp.where(lane_head == head, queries, none) for head in range(heads)], axis=0
            )
            cots = jnp.concatenate(
                [jnp.where(lane_head == head, cots, none) for head in range(heads)], axis=0
            )
            scores = jnp.where(key_valid, contract(keys, queries, 1, 1), FLOOR)
            expo = jnp.exp(scores - jnp.max(scores, axis=0, keepdims=True))
            probs = expo * (1.0 / jnp.sum(expo, axis=0, keepdims=True))
            dprob = contract(values, cots, 1, 1)
            delta = jnp.sum(probs * dprob, axis=0, keepdims=True)
            probs_low = probs.astype(jnp.bfloat16)
            dscore_low = (probs * (dprob - delta)).astype(jnp.bfloat16)
            dvalue = contract(probs_low, cots, 1, 0)
            dkey = contract(dscore_low, queries, 1, 0)
            attended = contract(probs_low, values, 0, 0)
            dquery = contract(dscore_low, keys, 0, 0)
            for head in range(1, heads):
                mine = lane_head == head
                attended = jnp.where(mine, attended[head * BLK : (head + 1) * BLK], attended[:BLK])
                dquery = jnp.where(mine, dquery[head * BLK : (head + 1) * BLK], dquery[:BLK])
            attended = jnp.where(live, attended, 0.0)
            out[seq_count + target, 0, target_rows, lanes] = (dquery * SCALE).astype(jnp.bfloat16)
            out[seq_count + target, 1, target_rows, lanes] = attended.astype(jnp.bfloat16)
            for slot, (dev, here) in enumerate(places):
                part = slice(slot * BLK, (slot + 1) * BLK)
                key_grad[dev, here, lanes] += dkey[part]
                value_grad[dev, here, lanes] += dvalue[part]
        return carry

    lax.fori_loop(0, block_count, step, 0)
    out[:seq_count, 0] = key_grad[...].astype(jnp.bfloat16)
    out[:seq_count, 1] = value_grad[...].astype(jnp.bfloat16)


def attend(seq_count, lists, lengths, rows):
    grads = (seq_count, rows.shape[2], rows.shape[3])
    block_count = lists.shape[0]
    pairs = block_count * NLIST * BLK * BLK * rows.shape[3]
    vmem = pl.BlockSpec(memory_space=pltpu.VMEM)
    smem = pl.BlockSpec(memory_space=pltpu.SMEM)
    return pl.pallas_call(
        functools.partial(attend_kernel, seq_count),
        out_shape=jax.ShapeDtypeStruct(rows.shape, rows.dtype),
        in_specs=[smem, smem, vmem],
        out_specs=vmem,
        scratch_shapes=[pltpu.VMEM(grads, jnp.float32), pltpu.VMEM(grads, jnp.float32)],
        compiler_params=pltpu.CompilerParams(vmem_limit_bytes=32 * 1024 * 1024),
        cost_estimate=pl.CostEstimate(
            flops=10 * pairs, bytes_accessed=4 * rows.size, transcendentals=pairs // HDIM
        ),
        name="attend",
    )(lists, lengths, rows)


def on_device(first_rows, second_rows, alignment, diffusion_mask, source_length, target_length):
    axes = ("section", "seq")
    seq_count = lax.axis_size("seq")
    parts = lax.axis_size("section") * seq_count
    rows_here = first_rows.shape[2]
    width = first_rows.shape[3]
    on_encoder = lax.axis_index("section") == 0
    row_pos = lax.axis_index("seq") * rows_here + jnp.arange(rows_here, dtype=jnp.int32)
    keep = on_encoder | ((row_pos < target_length[0]) & (diffusion_mask[0] == 1))
    second = jnp.where(keep[:, None], second_rows[0, 0], jnp.zeros_like(second_rows[0, 0]))
    held = jnp.stack([first_rows[0, 0], second])
    held = held.reshape(2, rows_here, parts, width // parts).transpose(2, 0, 1, 3)
    lists = lax.all_gather(alignment[0], "seq", axis=0, tiled=True)
    lengths = jnp.concatenate([source_length, target_length])
    rows = lax.all_to_all(held, axes, 0, 0, tiled=True)
    grads = attend(seq_count, lists, lengths, rows)
    grads = lax.all_to_all(grads, axes, 0, 0, tiled=True)
    grads = grads.transpose(1, 2, 0, 3).reshape(2, rows_here, width)
    return (grads[0][None, None], grads[1][None, None])


def solution(mesh):
    placed = (
        P("section", "sample", "seq", None),
        P("section", "sample", "seq", None),
        P("sample", "seq", None),
        P("sample", "seq"),
        P("sample"),
        P("sample"),
    )
    return jax.shard_map(
        on_device,
        mesh=mesh,
        in_specs=placed,
        out_specs=(P("section", "sample", "seq", None), P("section", "sample", "seq", None)),
        check_vma=False,
    )
```

time: 136 us -> 53.2 us (0.39)
  the two profiles are of different devices: /device:TPU:18 before, /device:TPU:0 now
where the time goes in v1:
time: 53.2 us; the launch traced here: 52.9 us
  blocking collectives  33.3 us (63%)
  local copies, waits for them, and re-layouts  6.14 us (12%)
  starting transfers between devices  5.3 us (10%)
  Pallas kernels  4.86 us (9%)
  between operations  2.02 us (4%)
  other arithmetic  1.26 us (2%)
    all_to_all x1, blocking collectives, on_device(): grads = lax.all_to_all(grads, axes, 0, 0, tiled=True)  18 us
    all_gather x1, blocking collectives, on_device(): lists = lax.all_gather(alignment[0], 'seq', axis=0, tiled=True)  15.3 us
    all_to_all x1, starting transfers between devices, on_device(): rows = lax.all_to_all(held, axes, 0, 0, tiled=True)  5.3 us
    unnamed x10, local copies, waits for them, and re-layouts  5.08 us
    pallas_call x1, Pallas kernels, attend(): pl.pallas_call(functools.partial(attend_kernel, seq_count), out_shape=jax...  4.86 us
    transpose x1, other arithmetic, on_device(): held.reshape(2, rows_here, parts, width // parts).transpose(2, 0, 1, 3)  1.07 us
  transfers between devices with their start and end apart: 1, of which 0 were waited for; matrix products, arithmetic and copies ran while one was open for 0% of the time, Pallas kernels for 0%

profile of v1, /device:TPU:0, one launch (start us, length us, event | category | flops | bytes accessed | tf_op | source)
XLA Modules:
  0.0 52.9 jit_solution(15157328208948478713)
XLA Ops:
  1.3 1.3 %copy.22 = bf16[1,1,128,2048]{2,3,1,0:T(8,128)(2,1)S(1)} copy(bf16[1,1,128,2048]{3,2,1,0:T(8,128)(2,1)} %param.7) | data formatting | bytes 1048576 | tf_op args[1]
  2.6 0.0 copy-start
  2.6 0.2 copy.23
  2.8 0.8 %copy-done = bf16[1,1,128,2048]{3,2,1,0:T(8,128)(2,1)S(1)} copy-done((bf16[1,1,128,2048]{3,2,1,0:T(8,128)(2,1)S(1)}, bf16[1,1,128,2048]{3,2,1,0:T(8,128)(2,1)}, u32[]{:S(2)}) %copy-start) | copy-done | bytes 524312
  3.6 0.3 copy.21
  3.9 0.2 copy.24
  4.2 0.0 copy-start.1
  4.2 0.6 %copy-done.1 = s32[1,128]{1,0:T(1,128)S(1)} copy-done((s32[1,128]{1,0:T(1,128)S(1)}, s32[1,128]{1,0:T(1,128)}, u32[]{:S(2)}) %copy-start.1) | copy-done | bytes 536
  4.8 0.1 broadcast_select_fusion
  4.9 1.1 %maximum_bitcast_fusion = bf16[8,2,128,256]{3,2,1,0:T(8,128)(2,1)} fusion(bf16[1,128,8,256]{3,1,0,2:T(8,128)(2,1)S(1)} %broadcast_select_fusion, bf16[1,128,8,256]{3,1,0,2:T(8,128)(2,1)S(1)} %copy.24), kind=kLoop, calls=%fused_computation | loop fusion | flops 524288 | bytes 2097152 | tf_op jit(solution)/shard_map/transpose | solution.py:123
  6.0 0.0 copy-start.2
  6.0 5.3 %all-to-all-start = ((bf16[8,2,128,256]{3,2,1,0:T(8,128)(2,1)}), bf16[8,2,128,256]{3,2,1,0:T(8,128)(2,1)S(1)}, u32[]{:S(2)}, u32[]{:S(2)}) async-start(bf16[8,2,128,256]{3,2,1,0:T(8,128)(2,1)} %maximum_bitcast_fusion), calls=%async_computation | async-start | bytes 2097152 | tf_op jit(solution)/shard_map/all_to_all | solution.py:126
  11.3 0.0 copy-done.2
  11.3 15.3 %all-gather = s32[4,1,2]{2,1,0:T(1,128)S(1)} all-gather(s32[1,1,2]{2,1,0:T(1,128)S(1)} %copy-done.2), channel_id=2, replica_groups=mesh['section'=2,'sample'=4,'seq'=4] {'seq'}, dimensions={0}, use_global_device_ids=true | all-gather | bytes 40 | tf_op jit(solution)/shard_map/all_gather | solution.py:124
  27.3 0.1 pad_add_fusion.lengths
  27.3 0.0 all-to-all-done.rows
  27.3 4.9 %attend.1 = bf16[8,2,128,256]{3,2,1,0:T(8,128)(2,1)S(1)} custom-call(s32[4,2]{1,0:T(4,128)S(1)} %bitcast.14, s32[2]{0:T(128)S(1)} %pad_add_fusion.lengths, bf16[8,2,128,256]{3,2,1,0:T(8,128)(2,1)S(1)} %all-to-all-done.rows), custom_call_target="tpu_custom_call" | custom-call | flops 335544320 | bytes 2097152 | tf_op jit(solution)/shard_map/attend/pallas_call | solution.py:98
  32.2 18.0 %all_to_all.10 = bf16[8,2,128,256]{3,2,1,0:T(8,128)(2,1)S(1)} all-to-all(bf16[8,2,128,256]{3,2,1,0:T(8,128)(2,1)S(1)} %attend.1), channel_id=1, replica_groups=mesh['section'=2,'sample'=4,'seq'=4] {'section','seq'}, dimensions={0} | all-to-all | bytes 2097152 | tf_op jit(solution)/shard_map/all_to_all | solution.py:128
  50.2 0.1 fusion.1
  50.3 0.3 copy.26
  50.6 1.0 %copy.28 = bf16[1,1,128,2048]{3,2,1,0:T(8,128)(2,1)} copy(bf16[1,1,128,2048]{2,3,1,0:T(8,128)(2,1)S(1)} %bitcast.16) | data formatting | bytes 1048576
  51.6 0.3 copy.27
  51.9 1.0 %copy.29 = bf16[1,1,128,2048]{3,2,1,0:T(8,128)(2,1)} copy(bf16[1,1,128,2048]{2,3,1,0:T(8,128)(2,1)S(1)} %bitcast.17) | data formatting | bytes 1048576
  (1 shorter events, 0.0 us)
Async XLA Ops:
  2.6 1.0 %copy-start = (bf16[1,1,128,2048]{3,2,1,0:T(8,128)(2,1)S(1)}, bf16[1,1,128,2048]{3,2,1,0:T(8,128)(2,1)}, u32[]{:S(2)}) copy-start(bf16[1,1,128,2048]{3,2,1,0:T(8,128)(2,1)} %param.6) | copy-start | bytes 1572868
  4.2 0.7 %copy-start.1 = (s32[1,128]{1,0:T(1,128)S(1)}, s32[1,128]{1,0:T(1,128)}, u32[]{:S(2)}) copy-start(s32[1,128]{1,0:T(1,128)} %param.9) | copy-start | bytes 1540
  6.0 5.3 %copy-start.2 = (s32[1,1,2]{2,1,0:T(1,128)S(1)}, s32[1,1,2]{2,1,0:T(1,128)}, u32[]{:S(2)}) copy-start(s32[1,1,2]{2,1,0:T(1,128)} %param.8) | copy-start | bytes 28
  6.0 21.3 %all-to-all-start = ((bf16[8,2,128,256]{3,2,1,0:T(8,128)(2,1)}), bf16[8,2,128,256]{3,2,1,0:T(8,128)(2,1)S(1)}, u32[]{:S(2)}, u32[]{:S(2)}) async-start(bf16[8,2,128,256]{3,2,1,0:T(8,128)(2,1)} %maximum_bitcast_fusion), calls=%async_computation | async-start | bytes 2097152 | tf_op jit(solution)/shard_map/all_to_all | solution.py:126

commit v2 on v1

--- a/solution.py
+++ b/solution.py
@@ -10,9 +10,14 @@
 HDIM = 64
 BLK = 128
 NLIST = 2
+WIN = 1
+SPAN = 2 * WIN + 1
 LANES = 128
+TAIL = 16
 SCALE = HDIM ** (-0.5)
 FLOOR = -1e30
+VMEM_LIMIT = 32 * 1024 * 1024
+AXES = ("section", "seq")
 
 
 def contract(left, right, left_dim, right_dim):
@@ -21,17 +26,15 @@
     )
 
 
-def attend_kernel(seq_count, lists, lengths, rows, out, key_grad, value_grad):
+def attend_sample(seq_count, listed, source_len, target_len, rows, out, key_grad, value_grad):
     per_device = rows.shape[2] // BLK
     block_count = seq_count * per_device
     width = rows.shape[3]
     tile = min(width, LANES)
     heads = tile // HDIM
-    source_len = lengths[0]
-    target_len = lengths[1]
     key_grad[...] = jnp.zeros_like(key_grad)
     value_grad[...] = jnp.zeros_like(value_grad)
-    key_inside = lax.broadcasted_iota(jnp.int32, (BLK, 1), 0)
+    inside = lax.broadcasted_iota(jnp.int32, (BLK, 1), 0)
     lane_head = lax.broadcasted_iota(jnp.int32, (BLK, tile), 1) // HDIM
 
     def place(block):
@@ -40,13 +43,13 @@
         return block // per_device, pl.ds((block % per_device) * BLK, BLK)
 
     def step(block, carry):
-        chosen = [lists[block, slot] for slot in range(NLIST)]
+        chosen = [listed(block, slot) for slot in range(NLIST)]
         places = [place(index) for index in chosen]
         target, target_rows = place(block)
         key_valid = jnp.concatenate(
-            [index * BLK + key_inside < source_len for index in chosen], axis=0
+            [index * BLK + inside < source_len for index in chosen], axis=0
         )
-        live = block * BLK + key_inside < target_len
+        live = block * BLK + inside < target_len
         for first in range(0, width, tile):
             lanes = pl.ds(first, tile)
             keys = jnp.concatenate([rows[dev, 0, here, lanes] for dev, here in places], axis=0)
@@ -89,45 +92,173 @@
     out[:seq_count, 1] = value_grad[...].astype(jnp.bfloat16)
 
 
-def attend(seq_count, lists, lengths, rows):
-    grads = (seq_count, rows.shape[2], rows.shape[3])
-    block_count = lists.shape[0]
-    pairs = block_count * NLIST * BLK * BLK * rows.shape[3]
-    vmem = pl.BlockSpec(memory_space=pltpu.VMEM)
-    smem = pl.BlockSpec(memory_space=pltpu.SMEM)
-    return pl.pallas_call(
-        functools.partial(attend_kernel, seq_count),
-        out_shape=jax.ShapeDtypeStruct(rows.shape, rows.dtype),
-        in_specs=[smem, smem, vmem],
-        out_specs=vmem,
-        scratch_shapes=[pltpu.VMEM(grads, jnp.float32), pltpu.VMEM(grads, jnp.float32)],
-        compiler_params=pltpu.CompilerParams(vmem_limit_bytes=32 * 1024 * 1024),
-        cost_estimate=pl.CostEstimate(
-            flops=10 * pairs, bytes_accessed=4 * rows.size, transcendentals=pairs // HDIM
-        ),
-        name="attend",
-    )(lists, lengths, rows)
-
-
-def on_device(first_rows, second_rows, alignment, diffusion_mask, source_length, target_length):
-    axes = ("section", "seq")
+def attend_cost(block_count, width):
+    pairs = block_count * NLIST * BLK * BLK * width
+    return pl.CostEstimate(
+        flops=10 * pairs,
+        bytes_accessed=16 * block_count * BLK * width,
+        transcendentals=pairs // HDIM,
+    )
+
+
+def specs(count, space):
+    return [pl.BlockSpec(memory_space=space)] * count
+
+
+def gathered_kernel(seq_count, lists, lengths, rows, out, key_grad, value_grad):
+    def listed(block, slot):
+        return lists[block, slot]
+
+    attend_sample(
+        seq_count, listed, lengths[0], lengths[1], rows, out, key_grad, value_grad
+    )
+
+
+def by_all_to_all(first_rows, second_rows, alignment, diffusion_mask, lengths):
     seq_count = lax.axis_size("seq")
     parts = lax.axis_size("section") * seq_count
     rows_here = first_rows.shape[2]
     width = first_rows.shape[3]
     on_encoder = lax.axis_index("section") == 0
     row_pos = lax.axis_index("seq") * rows_here + jnp.arange(rows_here, dtype=jnp.int32)
-    keep = on_encoder | ((row_pos < target_length[0]) & (diffusion_mask[0] == 1))
+    keep = on_encoder | ((row_pos < lengths[1]) & (diffusion_mask[0] == 1))
     second = jnp.where(keep[:, None], second_rows[0, 0], jnp.zeros_like(second_rows[0, 0]))
     held = jnp.stack([first_rows[0, 0], second])
     held = held.reshape(2, rows_here, parts, width // parts).transpose(2, 0, 1, 3)
     lists = lax.all_gather(alignment[0], "seq", axis=0, tiled=True)
-    lengths = jnp.concatenate([source_length, target_length])
-    rows = lax.all_to_all(held, axes, 0, 0, tiled=True)
-    grads = attend(seq_count, lists, lengths, rows)
-    grads = lax.all_to_all(grads, axes, 0, 0, tiled=True)
+    rows = lax.all_to_all(held, AXES, 0, 0, tiled=True)
+    grads = pltpu.VMEM((seq_count, rows_here, width // parts), jnp.float32)
+    grads = pl.pallas_call(
+        functools.partial(gathered_kernel, seq_count),
+        out_shape=jax.ShapeDtypeStruct(rows.shape, rows.dtype),
+        in_specs=specs(2, pltpu.SMEM) + specs(1, pltpu.VMEM),
+        out_specs=pl.BlockSpec(memory_space=pltpu.VMEM),
+        scratch_shapes=[grads, grads],
+        compiler_params=pltpu.CompilerParams(vmem_limit_bytes=VMEM_LIMIT),
+        cost_estimate=attend_cost(lists.shape[0], width // parts),
+        name="attend_gathered",
+    )(lists, lengths, rows)
+    grads = lax.all_to_all(grads, AXES, 0, 0, tiled=True)
     grads = grads.transpose(1, 2, 0, 3).reshape(2, rows_here, width)
     return (grads[0][None, None], grads[1][None, None])
+
+
+def pack_kernel(seq_count, me, lengths, lists, mask, first, second, *outs):
+    here = me[0] % seq_count
+    share = outs[0].shape[1]
+    positions = here * BLK + lax.broadcasted_iota(jnp.int32, (1, BLK), 1)
+    keep = ((positions < lengths[1]) & (mask[...] == 1)) | (me[0] < seq_count)
+    keep = jnp.broadcast_to(jnp.where(keep, 1.0, 0.0), (BLK, BLK)).T.astype(jnp.bfloat16)
+    keep = jnp.concatenate([keep] * (share // LANES), axis=1)
+    base = here - WIN
+    code = (lists[0, 0, 0] - base) * SPAN + lists[0, 0, 1] - base
+    for step, out in enumerate(outs):
+        lanes = pl.ds(pl.multiple_of((me[0] ^ step) * share, LANES), share)
+        out[:BLK] = first[0, 0, :, lanes]
+        out[BLK : 2 * BLK] = second[0, 0, :, lanes] * keep
+        if step < seq_count:
+            out[2 * BLK :] = jnp.full((TAIL, share), code, jnp.int32).astype(
+                jnp.float32
+            ).astype(jnp.bfloat16)
+
+
+def attend_kernel(seq_count, me, lengths, *refs):
+    parts = 2 * seq_count
+    shares, outs = refs[:parts], refs[parts : 2 * parts]
+    rows, result, key_grad, value_grad, lists = refs[2 * parts :]
+    here = me[0] % seq_count
+    for step, share in enumerate(shares):
+        source = me[0] ^ step
+        rows[source, 0] = share[:BLK]
+        rows[source, 1] = share[BLK : 2 * BLK]
+        if step < seq_count:
+            tail = share[2 * BLK :, :LANES].astype(jnp.float32)
+            lists[here ^ step] = jnp.max(tail).astype(jnp.int32)
+
+    def listed(block, slot):
+        code = lists[block]
+        return block - WIN + (code // SPAN if slot == 0 else code % SPAN)
+
+    attend_sample(
+        seq_count, listed, lengths[0], lengths[1], rows, result, key_grad, value_grad
+    )
+    for step, out in enumerate(outs):
+        out[:BLK] = result[me[0] ^ step, 0]
+        out[BLK:] = result[me[0] ^ step, 1]
+
+
+def unpack_kernel(me, *refs):
+    shares, (first, second) = refs[:-2], refs[-2:]
+    width = shares[0].shape[1]
+    for step, share in enumerate(shares):
+        lanes = pl.ds(pl.multiple_of((me[0] ^ step) * width, LANES), width)
+        first[0, 0, :, lanes] = share[:BLK]
+        second[0, 0, :, lanes] = share[BLK:]
+
+
+def swapped(shares, order):
+    moved = list(shares)
+    for step in order:
+        pairs = [(dev, dev ^ step) for dev in range(len(shares))]
+        moved[step] = lax.ppermute(shares[step], AXES, pairs)
+    return moved
+
+
+def by_pairs(first_rows, second_rows, alignment, diffusion_mask, lengths):
+    seq_count = lax.axis_size("seq")
+    parts = 2 * seq_count
+    width = first_rows.shape[3]
+    share = width // parts
+    kind = first_rows.dtype
+    me = (lax.axis_index("section") * seq_count + lax.axis_index("seq")).reshape(1)
+    params = pltpu.CompilerParams(vmem_limit_bytes=VMEM_LIMIT)
+    order = [*range(seq_count, parts), *range(seq_count - 1, 0, -1)]
+    tails = [TAIL if step < seq_count else 0 for step in range(parts)]
+    shares = pl.pallas_call(
+        functools.partial(pack_kernel, seq_count),
+        out_shape=[jax.ShapeDtypeStruct((2 * BLK + tail, share), kind) for tail in tails],
+        in_specs=specs(3, pltpu.SMEM) + specs(3, pltpu.VMEM),
+        out_specs=specs(parts, pltpu.VMEM),
+        compiler_params=params,
+        name="pack",
+    )(me, lengths, alignment, diffusion_mask, first_rows, second_rows)
+    shares = swapped(shares, order)
+    rows = pltpu.VMEM((parts, 2, BLK, share), kind)
+    grads = pltpu.VMEM((seq_count, BLK, share), jnp.float32)
+    shares = pl.pallas_call(
+        functools.partial(attend_kernel, seq_count),
+        out_shape=[jax.ShapeDtypeStruct((2 * BLK, share), kind)] * parts,
+        in_specs=specs(2, pltpu.SMEM) + specs(parts, pltpu.VMEM),
+        out_specs=specs(parts, pltpu.VMEM),
+        scratch_shapes=[rows, rows, grads, grads, pltpu.SMEM((seq_count,), jnp.int32)],
+        compiler_params=params,
+        cost_estimate=attend_cost(seq_count, share),
+        name="attend",
+    )(me, lengths, *shares)
+    shares = swapped(shares, order)
+    out_shape = jax.ShapeDtypeStruct((1, 1, BLK, width), kind)
+    return pl.pallas_call(
+        unpack_kernel,
+        out_shape=[out_shape, out_shape],
+        in_specs=specs(1, pltpu.SMEM) + specs(parts, pltpu.VMEM),
+        out_specs=specs(2, pltpu.VMEM),
+        compiler_params=params,
+        name="unpack",
+    )(me, *shares)
+
+
+def on_device(first_rows, second_rows, alignment, diffusion_mask, source_length, target_length):
+    seq_count = lax.axis_size("seq")
+    parts = lax.axis_size("section") * seq_count
+    lengths = jnp.concatenate([source_length, target_length])
+    paired = (
+        parts == 2 * seq_count
+        and seq_count & (seq_count - 1) == 0
+        and first_rows.shape[2] == BLK
+        and first_rows.shape[3] % (parts * LANES) == 0
+    )
+    work = by_pairs if paired else by_all_to_all
+    return tuple(work(first_rows, second_rows, alignment, diffusion_mask, lengths))
 
 
 def solution(mesh):

time: 53.2 us -> 46.2 us (0.87)
  blocking collectives: 33.3 us -> 0 us
  waiting for transfers between devices: 0.01 us -> 18.6 us
  starting transfers between devices: 5.3 us -> 15.7 us
  local copies, waits for them, and re-layouts: 6.14 us -> 2.75 us
  Pallas kernels: 4.86 us -> 6.84 us
  other arithmetic: 1.26 us -> 0.08 us
    ppermute x0 -> x14, waiting for transfers between devices: none -> 18.6 us  [swapped(): moved[step] = lax.ppermute(shares[step], AXES, pairs)]
    all_to_all x1 -> x0, blocking collectives: 18 us -> none  [on_device(): grads = lax.all_to_all(grads, axes, 0, 0, tiled=True)]
    ppermute x0 -> x14, starting transfers between devices: none -> 15.7 us  [swapped(): moved[step] = lax.ppermute(shares[step], AXES, pairs)]
    all_gather x1 -> x0, blocking collectives: 15.3 us -> none  [on_device(): lists = lax.all_gather(alignment[0], 'seq', axis=0, tiled=True)]
    all_to_all x1 -> x0, starting transfers between devices: 5.3 us -> none  [on_device(): rows = lax.all_to_all(held, axes, 0, 0, tiled=True)]
    unnamed x10 -> x8, local copies, waits for them, and re-layouts: 5.08 us -> 2.75 us
    pallas_call x1 -> x3, Pallas kernels: 4.86 us -> 6.84 us  [the longest x1 5.05 us: by_pairs(): pl.pallas_call(functools.partial(attend_kernel, seq_count), out_shape=[ja...]
    transpose x1 -> x0, other arithmetic: 1.07 us -> none  [on_device(): held.reshape(2, rows_here, parts, width // parts).transpose(2, 0, 1, 3)]
  transfers between devices with their start and end apart: 1 -> 14, of which waited for: 0 -> 7; matrix products, arithmetic and copies ran while one was open for 0% -> 0% of each run, Pallas kernels for 0% -> 0%
where the time goes in v2:
time: 46.2 us; the launch traced here: 46 us
  waiting for transfers between devices  18.6 us (40%)
  starting transfers between devices  15.7 us (34%)
  Pallas kernels  6.84 us (15%)
  local copies, waits for them, and re-layouts  2.75 us (6%)
  between operations  1.96 us (4%)
    ppermute x14, waiting for transfers between devices, swapped(): moved[step] = lax.ppermute(shares[step], AXES, pairs)  18.6 us
    ppermute x14, starting transfers between devices, swapped(): moved[step] = lax.ppermute(shares[step], AXES, pairs)  15.7 us
    pallas_call x1, Pallas kernels, by_pairs(): pl.pallas_call(functools.partial(attend_kernel, seq_count), out_shape=[ja...  5.05 us
    unnamed x8, local copies, waits for them, and re-layouts  2.75 us
    pallas_call x1, Pallas kernels, by_pairs(): pl.pallas_call(unpack_kernel, out_shape=[out_shape, out_shape], in_specs=...  1.1 us
  transfers between devices with their start and end apart: 14, of which 7 were waited for; matrix products, arithmetic and copies ran while one was open for 0% of the time, Pallas kernels for 0%

profile of v2, /device:TPU:0, one launch (start us, length us, event | category | flops | bytes accessed | tf_op | source)
XLA Modules:
  0.0 46.0 jit_solution(11689748847484824529)
XLA Ops:
  1.9 0.1 pad_add_fusion.lengths
  2.0 0.0 copy-start.2
  2.0 0.0 copy-start.3
  2.0 0.7 %copy-done.2 = s32[1,1,2]{2,1,0:T(1,128)S(1)} copy-done((s32[1,1,2]{2,1,0:T(1,128)S(1)}, s32[1,1,2]{2,1,0:T(1,128)}, u32[]{:S(2)}) %copy-start.2) | copy-done | bytes 32
  2.7 0.0 copy-done.3
  2.7 0.0 copy-start
  2.7 1.0 %copy-done = bf16[1,1,128,2048]{3,2,1,0:T(8,128)(2,1)S(1)} copy-done((bf16[1,1,128,2048]{3,2,1,0:T(8,128)(2,1)S(1)}, bf16[1,1,128,2048]{3,2,1,0:T(8,128)(2,1)}, u32[]{:S(2)}) %copy-start) | copy-done | bytes 524312
  3.7 0.0 copy-start.1
  3.7 1.0 %copy-done.1 = bf16[1,1,128,2048]{3,2,1,0:T(8,128)(2,1)S(1)} copy-done((bf16[1,1,128,2048]{3,2,1,0:T(8,128)(2,1)S(1)}, bf16[1,1,128,2048]{3,2,1,0:T(8,128)(2,1)}, u32[]{:S(2)}) %copy-start.1) | copy-done | bytes 524312
  4.8 0.7 %pack.1 = (bf16[272,256]{1,0:T(8,128)(2,1)S(1)}, bf16[272,256]{1,0:T(8,128)(2,1)S(1)}, bf16[272,256]{1,0:T(8,128)(2,1)S(1)}, bf16[272,256]{1,0:T(8,128)(2,1)S(1)...) custom-call(s32[1]{0:T(128)} %bitcast.me, ...), custom_call_target="tpu_custom_call" | custom-call | tf_op jit(solution)/shard_map/pack/pallas_call | solution.py:217
  5.5 3.0 %collective-permute-start.3 = (bf16[256,256]{1,0:T(8,128)(2,1)S(1)}, bf16[256,256]{1,0:T(8,128)(2,1)S(1)}, u32[]{:S(2)}, u32[]{:S(2)}) collective-permute-start(bf16[256,256]{1,0:T(8,128)(2,1)S(1)} %get-tuple-element.22), channel_id=1, source_target_pairs={{0,16},{1,17},{2,18},{3,19},{16,0},{17,1},{18,2},{19,3},{4,20},{5,... | collective-permute-start | bytes 393224 | tf_op jit(solution)/shard_map/ppermute | solution.py:203
  8.5 0.0 collective-permute-start.4
  8.5 0.2 collective-permute-start
  8.7 1.9 %collective-permute-start.1 = (bf16[272,256]{1,0:T(8,128)(2,1)S(1)}, bf16[272,256]{1,0:T(8,128)(2,1)S(1)}, u32[]{:S(2)}, u32[]{:S(2)}) collective-permute-start(bf16[272,256]{1,0:T(8,128)(2,1)S(1)} %get-tuple-element.20), channel_id=1, source_target_pairs={{0,2},{1,3},{2,0},{3,1},{16,18},{17,19},{18,16},{19,17},{4,6},{5,7... | collective-permute-start | bytes 417800 | tf_op jit(solution)/shard_map/ppermute | solution.py:203
  10.6 0.0 collective-permute-start.2
  10.6 1.8 %collective-permute-done.3.refs_4_ = bf16[256,256]{1,0:T(8,128)(2,1)S(1)} collective-permute-done((bf16[256,256]{1,0:T(8,128)(2,1)S(1)}, bf16[256,256]{1,0:T(8,128)(2,1)S(1)}, u32[]{:S(2)}, u32[]{:S(2)}) %collective-permute-start.3) | collective-permute-done | bytes 131104 | tf_op jit(solution)/shard_map/ppermute | solution.py:203
  12.4 3.4 %collective-permute-start.5 = (bf16[256,256]{1,0:T(8,128)(2,1)S(1)}, bf16[256,256]{1,0:T(8,128)(2,1)S(1)}, u32[]{:S(2)}, u32[]{:S(2)}) collective-permute-start(bf16[256,256]{1,0:T(8,128)(2,1)S(1)} %get-tuple-element.24), channel_id=1, source_target_pairs={{0,18},{1,19},{2,16},{3,17},{16,2},{17,3},{18,0},{19,1},{4,22},{5,... | collective-permute-start | bytes 393224 | tf_op jit(solution)/shard_map/ppermute | solution.py:203
  15.8 0.0 collective-permute-done.4.refs_5_
  15.8 1.4 %collective-permute-start.6 = (bf16[256,256]{1,0:T(8,128)(2,1)S(1)}, bf16[256,256]{1,0:T(8,128)(2,1)S(1)}, u32[]{:S(2)}, u32[]{:S(2)}) collective-permute-start(bf16[256,256]{1,0:T(8,128)(2,1)S(1)} %get-tuple-element.25), channel_id=1, source_target_pairs={{0,19},{1,18},{2,17},{3,16},{16,3},{17,2},{18,1},{19,0},{4,23},{5,... | collective-permute-start | bytes 393224 | tf_op jit(solution)/shard_map/ppermute | solution.py:203
  17.2 5.2 %collective-permute-done.5.refs_6_ = bf16[256,256]{1,0:T(8,128)(2,1)S(1)} collective-permute-done((bf16[256,256]{1,0:T(8,128)(2,1)S(1)}, bf16[256,256]{1,0:T(8,128)(2,1)S(1)}, u32[]{:S(2)}, u32[]{:S(2)}) %collective-permute-start.5) | collective-permute-done | bytes 131104 | tf_op jit(solution)/shard_map/ppermute | solution.py:203
  22.4 0.9 %collective-permute-done.6.refs_7_ = bf16[256,256]{1,0:T(8,128)(2,1)S(1)} collective-permute-done((bf16[256,256]{1,0:T(8,128)(2,1)S(1)}, bf16[256,256]{1,0:T(8,128)(2,1)S(1)}, u32[]{:S(2)}, u32[]{:S(2)}) %collective-permute-start.6) | collective-permute-done | bytes 131104 | tf_op jit(solution)/shard_map/ppermute | solution.py:203
  23.3 0.0 collective-permute-done.refs_1_
  23.3 0.0 collective-permute-done.1.refs_2_
  23.3 0.0 collective-permute-done.2.refs_3_
  23.3 5.1 %attend.1 = (bf16[256,256]{1,0:T(8,128)(2,1)S(1)}, bf16[256,256]{1,0:T(8,128)(2,1)S(1)}, bf16[256,256]{1,0:T(8,128)(2,1)S(1)}, bf16[256,256]{1,0:T(8,128)(2,1)S(...) custom-call(s32[1]{0:T(128)} %bitcast.me, ...), custom_call_target="tpu_custom_call" | custom-call | flops 335544320 | bytes 2097152 | tf_op jit(solution)/shard_map/attend/pallas_call | solution.py:228
  28.4 0.9 %collective-permute-start.7 = (bf16[256,256]{1,0:T(8,128)(2,1)S(1)}, bf16[256,256]{1,0:T(8,128)(2,1)S(1)}, u32[]{:S(2)}, u32[]{:S(2)}) collective-permute-start(bf16[256,256]{1,0:T(8,128)(2,1)S(1)} %get-tuple-element.27), channel_id=1, source_target_pairs={{0,1},{1,0},{2,3},{3,2},{16,17},{17,16},{18,19},{19,18},{4,5},{5,4... | collective-permute-start | bytes 393224 | tf_op jit(solution)/shard_map/ppermute | solution.py:203
  29.2 1.5 %collective-permute-start.8 = (bf16[256,256]{1,0:T(8,128)(2,1)S(1)}, bf16[256,256]{1,0:T(8,128)(2,1)S(1)}, u32[]{:S(2)}, u32[]{:S(2)}) collective-permute-start(bf16[256,256]{1,0:T(8,128)(2,1)S(1)} %get-tuple-element.28), channel_id=1, source_target_pairs={{0,2},{1,3},{2,0},{3,1},{16,18},{17,19},{18,16},{19,17},{4,6},{5,7... | collective-permute-start | bytes 393224 | tf_op jit(solution)/shard_map/ppermute | solution.py:203
  30.7 0.0 collective-permute-start.9
  30.7 0.5 %collective-permute-start.10 = (bf16[256,256]{1,0:T(8,128)(2,1)S(1)}, bf16[256,256]{1,0:T(8,128)(2,1)S(1)}, u32[]{:S(2)}, u32[]{:S(2)}) collective-permute-start(bf16[256,256]{1,0:T(8,128)(2,1)S(1)} %get-tuple-element.30), channel_id=1, source_target_pairs={{0,16},{1,17},{2,18},{3,19},{16,0},{17,1},{18,2},{19,3},{4,20},{5,... | collective-permute-start | bytes 393224 | tf_op jit(solution)/shard_map/ppermute | solution.py:203
  31.2 1.5 %collective-permute-start.11 = (bf16[256,256]{1,0:T(8,128)(2,1)S(1)}, bf16[256,256]{1,0:T(8,128)(2,1)S(1)}, u32[]{:S(2)}, u32[]{:S(2)}) collective-permute-start(bf16[256,256]{1,0:T(8,128)(2,1)S(1)} %get-tuple-element.31), channel_id=1, source_target_pairs={{0,17},{1,16},{2,19},{3,18},{16,1},{17,0},{18,3},{19,2},{4,21},{5,... | collective-permute-start | bytes 393224 | tf_op jit(solution)/shard_map/ppermute | solution.py:203
  32.7 0.0 collective-permute-done.7.refs_1_
  32.7 1.4 %collective-permute-start.12 = (bf16[256,256]{1,0:T(8,128)(2,1)S(1)}, bf16[256,256]{1,0:T(8,128)(2,1)S(1)}, u32[]{:S(2)}, u32[]{:S(2)}) collective-permute-start(bf16[256,256]{1,0:T(8,128)(2,1)S(1)} %get-tuple-element.32), channel_id=1, source_target_pairs={{0,18},{1,19},{2,16},{3,17},{16,2},{17,3},{18,0},{19,1},{4,22},{5,... | collective-permute-start | bytes 393224 | tf_op jit(solution)/shard_map/ppermute | solution.py:203
  34.1 1.4 %collective-permute-done.8.refs_2_ = bf16[256,256]{1,0:T(8,128)(2,1)S(1)} collective-permute-done((bf16[256,256]{1,0:T(8,128)(2,1)S(1)}, bf16[256,256]{1,0:T(8,128)(2,1)S(1)}, u32[]{:S(2)}, u32[]{:S(2)}) %collective-permute-start.8) | collective-permute-done | bytes 131104 | tf_op jit(solution)/shard_map/ppermute | solution.py:203
  35.6 0.0 collective-permute-start.13
  35.6 1.8 %collective-permute-done.9.refs_3_ = bf16[256,256]{1,0:T(8,128)(2,1)S(1)} collective-permute-done((bf16[256,256]{1,0:T(8,128)(2,1)S(1)}, bf16[256,256]{1,0:T(8,128)(2,1)S(1)}, u32[]{:S(2)}, u32[]{:S(2)}) %collective-permute-start.9) | collective-permute-done | bytes 131104 | tf_op jit(solution)/shard_map/ppermute | solution.py:203
  37.4 0.3 collective-permute-done.10.refs_4_
  37.7 7.2 %collective-permute-done.11.refs_5_ = bf16[256,256]{1,0:T(8,128)(2,1)S(1)} collective-permute-done((bf16[256,256]{1,0:T(8,128)(2,1)S(1)}, bf16[256,256]{1,0:T(8,128)(2,1)S(1)}, u32[]{:S(2)}, u32[]{:S(2)}) %collective-permute-start.11) | collective-permute-done | bytes 131104 | tf_op jit(solution)/shard_map/ppermute | solution.py:203
  44.8 0.0 collective-permute-done.12.refs_6_
  44.9 0.0 collective-permute-done.13.refs_7_
  44.9 1.1 %unpack.1 = (bf16[1,1,128,2048]{3,2,1,0:T(8,128)(2,1)}, bf16[1,1,128,2048]{3,2,1,0:T(8,128)(2,1)}) custom-call(s32[1]{0:T(128)} %bitcast.me, bf16[256,256]{1,0:T(8,128)(2,1)S(1)} %get-tuple-element.26.refs_0_, bf16[256,256]{1,0:T(8,128)(2,1)S(1)} %collective-permute-done.7.refs_1_, bf16[256,256]{1,0:T(8,128)(2,1)S(1)} %collective-permute-done.8.refs_2_, ...), custom_call_target="tpu_custom_call" | custom-call | tf_op jit(solution)/shard_map/unpack/pallas_call | solution.py:240
Async XLA Ops:
  2.0 0.7 %copy-start.2 = (s32[1,1,2]{2,1,0:T(1,128)S(1)}, s32[1,1,2]{2,1,0:T(1,128)}, u32[]{:S(2)}) copy-start(s32[1,1,2]{2,1,0:T(1,128)} %lists.1) | copy-start | bytes 28
  2.0 0.7 %copy-start.3 = (s32[1,128]{1,0:T(1,128)S(1)}, s32[1,128]{1,0:T(1,128)}, u32[]{:S(2)}) copy-start(s32[1,128]{1,0:T(1,128)} %mask.1) | copy-start | bytes 1540
  2.7 1.0 %copy-start = (bf16[1,1,128,2048]{3,2,1,0:T(8,128)(2,1)S(1)}, bf16[1,1,128,2048]{3,2,1,0:T(8,128)(2,1)}, u32[]{:S(2)}) copy-start(bf16[1,1,128,2048]{3,2,1,0:T(8,128)(2,1)} %first.1) | copy-start | bytes 1572868
  3.7 1.0 %copy-start.1 = (bf16[1,1,128,2048]{3,2,1,0:T(8,128)(2,1)S(1)}, bf16[1,1,128,2048]{3,2,1,0:T(8,128)(2,1)}, u32[]{:S(2)}) copy-start(bf16[1,1,128,2048]{3,2,1,0:T(8,128)(2,1)} %second.1) | copy-start | bytes 1572868
  5.5 7.0 %collective-permute-start.3 = (bf16[256,256]{1,0:T(8,128)(2,1)S(1)}, bf16[256,256]{1,0:T(8,128)(2,1)S(1)}, u32[]{:S(2)}, u32[]{:S(2)}) collective-permute-start(bf16[256,256]{1,0:T(8,128)(2,1)S(1)} %get-tuple-element.22), channel_id=1, source_target_pairs={{0,16},{1,17},{2,18},{3,19},{16,0},{17,1},{18,2},{19,3},{4,20},{5,... | collective-permute-start | bytes 393224 | tf_op jit(solution)/shard_map/ppermute | solution.py:203
  8.5 7.3 %collective-permute-start.4 = (bf16[256,256]{1,0:T(8,128)(2,1)S(1)}, bf16[256,256]{1,0:T(8,128)(2,1)S(1)}, u32[]{:S(2)}, u32[]{:S(2)}) collective-permute-start(bf16[256,256]{1,0:T(8,128)(2,1)S(1)} %get-tuple-element.23), channel_id=1, source_target_pairs={{0,17},{1,16},{2,19},{3,18},{16,1},{17,0},{18,3},{19,2},{4,21},{5,... | collective-permute-start | bytes 393224 | tf_op jit(solution)/shard_map/ppermute | solution.py:203
  8.5 14.8 %collective-permute-start = (bf16[272,256]{1,0:T(8,128)(2,1)S(1)}, bf16[272,256]{1,0:T(8,128)(2,1)S(1)}, u32[]{:S(2)}, u32[]{:S(2)}) collective-permute-start(bf16[272,256]{1,0:T(8,128)(2,1)S(1)} %get-tuple-element.19), channel_id=1, source_target_pairs={{0,1},{1,0},{2,3},{3,2},{16,17},{17,16},{18,19},{19,18},{4,5},{5,4... | collective-permute-start | bytes 417800 | tf_op jit(solution)/shard_map/ppermute | solution.py:203
  8.7 14.6 %collective-permute-start.1 = (bf16[272,256]{1,0:T(8,128)(2,1)S(1)}, bf16[272,256]{1,0:T(8,128)(2,1)S(1)}, u32[]{:S(2)}, u32[]{:S(2)}) collective-permute-start(bf16[272,256]{1,0:T(8,128)(2,1)S(1)} %get-tuple-element.20), channel_id=1, source_target_pairs={{0,2},{1,3},{2,0},{3,1},{16,18},{17,19},{18,16},{19,17},{4,6},{5,7... | collective-permute-start | bytes 417800 | tf_op jit(solution)/shard_map/ppermute | solution.py:203
  10.6 12.7 %collective-permute-start.2 = (bf16[272,256]{1,0:T(8,128)(2,1)S(1)}, bf16[272,256]{1,0:T(8,128)(2,1)S(1)}, u32[]{:S(2)}, u32[]{:S(2)}) collective-permute-start(bf16[272,256]{1,0:T(8,128)(2,1)S(1)} %get-tuple-element.21), channel_id=1, source_target_pairs={{0,3},{1,2},{2,1},{3,0},{16,19},{17,18},{18,17},{19,16},{4,7},{5,6... | collective-permute-start | bytes 417800 | tf_op jit(solution)/shard_map/ppermute | solution.py:203
  12.4 10.0 %collective-permute-start.5 = (bf16[256,256]{1,0:T(8,128)(2,1)S(1)}, bf16[256,256]{1,0:T(8,128)(2,1)S(1)}, u32[]{:S(2)}, u32[]{:S(2)}) collective-permute-start(bf16[256,256]{1,0:T(8,128)(2,1)S(1)} %get-tuple-element.24), channel_id=1, source_target_pairs={{0,18},{1,19},{2,16},{3,17},{16,2},{17,3},{18,0},{19,1},{4,22},{5,... | collective-permute-start | bytes 393224 | tf_op jit(solution)/shard_map/ppermute | solution.py:203
  15.8 7.5 %collective-permute-start.6 = (bf16[256,256]{1,0:T(8,128)(2,1)S(1)}, bf16[256,256]{1,0:T(8,128)(2,1)S(1)}, u32[]{:S(2)}, u32[]{:S(2)}) collective-permute-start(bf16[256,256]{1,0:T(8,128)(2,1)S(1)} %get-tuple-element.25), channel_id=1, source_target_pairs={{0,19},{1,18},{2,17},{3,16},{16,3},{17,2},{18,1},{19,0},{4,23},{5,... | collective-permute-start | bytes 393224 | tf_op jit(solution)/shard_map/ppermute | solution.py:203
  28.4 4.3 %collective-permute-start.7 = (bf16[256,256]{1,0:T(8,128)(2,1)S(1)}, bf16[256,256]{1,0:T(8,128)(2,1)S(1)}, u32[]{:S(2)}, u32[]{:S(2)}) collective-permute-start(bf16[256,256]{1,0:T(8,128)(2,1)S(1)} %get-tuple-element.27), channel_id=1, source_target_pairs={{0,1},{1,0},{2,3},{3,2},{16,17},{17,16},{18,19},{19,18},{4,5},{5,4... | collective-permute-start | bytes 393224 | tf_op jit(solution)/shard_map/ppermute | solution.py:203
  29.2 6.4 %collective-permute-start.8 = (bf16[256,256]{1,0:T(8,128)(2,1)S(1)}, bf16[256,256]{1,0:T(8,128)(2,1)S(1)}, u32[]{:S(2)}, u32[]{:S(2)}) collective-permute-start(bf16[256,256]{1,0:T(8,128)(2,1)S(1)} %get-tuple-element.28), channel_id=1, source_target_pairs={{0,2},{1,3},{2,0},{3,1},{16,18},{17,19},{18,16},{19,17},{4,6},{5,7... | collective-permute-start | bytes 393224 | tf_op jit(solution)/shard_map/ppermute | solution.py:203
  30.7 6.7 %collective-permute-start.9 = (bf16[256,256]{1,0:T(8,128)(2,1)S(1)}, bf16[256,256]{1,0:T(8,128)(2,1)S(1)}, u32[]{:S(2)}, u32[]{:S(2)}) collective-permute-start(bf16[256,256]{1,0:T(8,128)(2,1)S(1)} %get-tuple-element.29), channel_id=1, source_target_pairs={{0,3},{1,2},{2,1},{3,0},{16,19},{17,18},{18,17},{19,16},{4,7},{5,6... | collective-permute-start | bytes 393224 | tf_op jit(solution)/shard_map/ppermute | solution.py:203
  30.7 7.0 %collective-permute-start.10 = (bf16[256,256]{1,0:T(8,128)(2,1)S(1)}, bf16[256,256]{1,0:T(8,128)(2,1)S(1)}, u32[]{:S(2)}, u32[]{:S(2)}) collective-permute-start(bf16[256,256]{1,0:T(8,128)(2,1)S(1)} %get-tuple-element.30), channel_id=1, source_target_pairs={{0,16},{1,17},{2,18},{3,19},{16,0},{17,1},{18,2},{19,3},{4,20},{5,... | collective-permute-start | bytes 393224 | tf_op jit(solution)/shard_map/ppermute | solution.py:203
  31.2 13.6 %collective-permute-start.11 = (bf16[256,256]{1,0:T(8,128)(2,1)S(1)}, bf16[256,256]{1,0:T(8,128)(2,1)S(1)}, u32[]{:S(2)}, u32[]{:S(2)}) collective-permute-start(bf16[256,256]{1,0:T(8,128)(2,1)S(1)} %get-tuple-element.31), channel_id=1, source_target_pairs={{0,17},{1,16},{2,19},{3,18},{16,1},{17,0},{18,3},{19,2},{4,21},{5,... | collective-permute-start | bytes 393224 | tf_op jit(solution)/shard_map/ppermute | solution.py:203
  32.7 12.1 %collective-permute-start.12 = (bf16[256,256]{1,0:T(8,128)(2,1)S(1)}, bf16[256,256]{1,0:T(8,128)(2,1)S(1)}, u32[]{:S(2)}, u32[]{:S(2)}) collective-permute-start(bf16[256,256]{1,0:T(8,128)(2,1)S(1)} %get-tuple-element.32), channel_id=1, source_target_pairs={{0,18},{1,19},{2,16},{3,17},{16,2},{17,3},{18,0},{19,1},{4,22},{5,... | collective-permute-start | bytes 393224 | tf_op jit(solution)/shard_map/ppermute | solution.py:203
  35.6 9.3 %collective-permute-start.13 = (bf16[256,256]{1,0:T(8,128)(2,1)S(1)}, bf16[256,256]{1,0:T(8,128)(2,1)S(1)}, u32[]{:S(2)}, u32[]{:S(2)}) collective-permute-start(bf16[256,256]{1,0:T(8,128)(2,1)S(1)} %get-tuple-element.33), channel_id=1, source_target_pairs={{0,19},{1,18},{2,17},{3,16},{16,3},{17,2},{18,1},{19,0},{4,23},{5,... | collective-permute-start | bytes 393224 | tf_op jit(solution)/shard_map/ppermute | solution.py:203

commit v3 on v2

--- a/solution.py
+++ b/solution.py
@@ -105,23 +105,23 @@
     return [pl.BlockSpec(memory_space=space)] * count
 
 
-def gathered_kernel(seq_count, lists, lengths, rows, out, key_grad, value_grad):
+def gathered_kernel(seq_count, lists, source_len, target_len, rows, out, key_grad, value_grad):
     def listed(block, slot):
         return lists[block, slot]
 
     attend_sample(
-        seq_count, listed, lengths[0], lengths[1], rows, out, key_grad, value_grad
-    )
-
-
-def by_all_to_all(first_rows, second_rows, alignment, diffusion_mask, lengths):
+        seq_count, listed, source_len[0], target_len[0], rows, out, key_grad, value_grad
+    )
+
+
+def by_all_to_all(first_rows, second_rows, alignment, diffusion_mask, source_length, target_length):
     seq_count = lax.axis_size("seq")
     parts = lax.axis_size("section") * seq_count
     rows_here = first_rows.shape[2]
     width = first_rows.shape[3]
     on_encoder = lax.axis_index("section") == 0
     row_pos = lax.axis_index("seq") * rows_here + jnp.arange(rows_here, dtype=jnp.int32)
-    keep = on_encoder | ((row_pos < lengths[1]) & (diffusion_mask[0] == 1))
+    keep = on_encoder | ((row_pos < target_length[0]) & (diffusion_mask[0] == 1))
     second = jnp.where(keep[:, None], second_rows[0, 0], jnp.zeros_like(second_rows[0, 0]))
     held = jnp.stack([first_rows[0, 0], second])
     held = held.reshape(2, rows_here, parts, width // parts).transpose(2, 0, 1, 3)
@@ -131,44 +131,61 @@
     grads = pl.pallas_call(
         functools.partial(gathered_kernel, seq_count),
         out_shape=jax.ShapeDtypeStruct(rows.shape, rows.dtype),
-        in_specs=specs(2, pltpu.SMEM) + specs(1, pltpu.VMEM),
+        in_specs=specs(3, pltpu.SMEM) + specs(1, pltpu.VMEM),
         out_specs=pl.BlockSpec(memory_space=pltpu.VMEM),
         scratch_shapes=[grads, grads],
         compiler_params=pltpu.CompilerParams(vmem_limit_bytes=VMEM_LIMIT),
         cost_estimate=attend_cost(lists.shape[0], width // parts),
         name="attend_gathered",
-    )(lists, lengths, rows)
+    )(lists, source_length, target_length, rows)
     grads = lax.all_to_all(grads, AXES, 0, 0, tiled=True)
     grads = grads.transpose(1, 2, 0, 3).reshape(2, rows_here, width)
     return (grads[0][None, None], grads[1][None, None])
 
 
-def pack_kernel(seq_count, me, lengths, lists, mask, first, second, *outs):
-    here = me[0] % seq_count
+def device_index(seq_count):
+    return lax.axis_index("section") * seq_count + lax.axis_index("seq")
+
+
+def pack_kernel(seq_count, order, target_len, lists, mask, first, second, *refs):
+    outs, sem = refs[:-1], refs[-1]
+    me = device_index(seq_count)
+    here = me % seq_count
     share = outs[0].shape[1]
+    copies = []
+    for slot, (step, out) in enumerate(zip(order, outs)):
+        lanes = pl.ds(pl.multiple_of((me ^ step) * share, LANES), share)
+        pair = [
+            pltpu.make_async_copy(
+                source.at[0, 0, :, lanes], out.at[pl.ds(half * BLK, BLK)], sem.at[half, slot]
+            )
+            for half, source in enumerate((first, second))
+        ]
+        for copy in pair:
+            copy.start()
+        copies.append(pair)
     positions = here * BLK + lax.broadcasted_iota(jnp.int32, (1, BLK), 1)
-    keep = ((positions < lengths[1]) & (mask[...] == 1)) | (me[0] < seq_count)
+    keep = ((positions < target_len[0]) & (mask[...] == 1)) | (me < seq_count)
     keep = jnp.broadcast_to(jnp.where(keep, 1.0, 0.0), (BLK, BLK)).T.astype(jnp.bfloat16)
     keep = jnp.concatenate([keep] * (share // LANES), axis=1)
     base = here - WIN
     code = (lists[0, 0, 0] - base) * SPAN + lists[0, 0, 1] - base
-    for step, out in enumerate(outs):
-        lanes = pl.ds(pl.multiple_of((me[0] ^ step) * share, LANES), share)
-        out[:BLK] = first[0, 0, :, lanes]
-        out[BLK : 2 * BLK] = second[0, 0, :, lanes] * keep
-        if step < seq_count:
-            out[2 * BLK :] = jnp.full((TAIL, share), code, jnp.int32).astype(
-                jnp.float32
-            ).astype(jnp.bfloat16)
-
-
-def attend_kernel(seq_count, me, lengths, *refs):
+    tail = jnp.full((TAIL, share), code, jnp.int32).astype(jnp.float32).astype(jnp.bfloat16)
+    for out, pair in zip(outs, copies):
+        for copy in pair:
+            copy.wait()
+        out[BLK : 2 * BLK] = out[BLK : 2 * BLK] * keep
+        out[2 * BLK :] = tail
+
+
+def attend_kernel(seq_count, order, source_len, target_len, *refs):
     parts = 2 * seq_count
     shares, outs = refs[:parts], refs[parts : 2 * parts]
     rows, result, key_grad, value_grad, lists = refs[2 * parts :]
-    here = me[0] % seq_count
-    for step, share in enumerate(shares):
-        source = me[0] ^ step
+    me = device_index(seq_count)
+    here = me % seq_count
+    for step, share in zip(order, shares):
+        source = me ^ step
         rows[source, 0] = share[:BLK]
         rows[source, 1] = share[BLK : 2 * BLK]
         if step < seq_count:
@@ -180,53 +197,62 @@
         return block - WIN + (code // SPAN if slot == 0 else code % SPAN)
 
     attend_sample(
-        seq_count, listed, lengths[0], lengths[1], rows, result, key_grad, value_grad
-    )
-    for step, out in enumerate(outs):
-        out[:BLK] = result[me[0] ^ step, 0]
-        out[BLK:] = result[me[0] ^ step, 1]
-
-
-def unpack_kernel(me, *refs):
-    shares, (first, second) = refs[:-2], refs[-2:]
+        seq_count, listed, source_len[0], target_len[0], rows, result, key_grad, value_grad
+    )
+    for step, out in zip(order, outs):
+        out[:BLK] = result[me ^ step, 0]
+        out[BLK:] = result[me ^ step, 1]
+
+
+def unpack_kernel(seq_count, order, *refs):
+    shares, (first, second, sem) = refs[:-3], refs[-3:]
     width = shares[0].shape[1]
-    for step, share in enumerate(shares):
-        lanes = pl.ds(pl.multiple_of((me[0] ^ step) * width, LANES), width)
-        first[0, 0, :, lanes] = share[:BLK]
-        second[0, 0, :, lanes] = share[BLK:]
+    me = device_index(seq_count)
+    copies = []
+    for slot, (step, share) in enumerate(zip(order, shares)):
+        lanes = pl.ds(pl.multiple_of((me ^ step) * width, LANES), width)
+        for half, result in enumerate((first, second)):
+            copy = pltpu.make_async_copy(
+                share.at[pl.ds(half * BLK, BLK)], result.at[0, 0, :, lanes], sem.at[half, slot]
+            )
+            copy.start()
+            copies.append(copy)
+    for copy in copies:
+        copy.wait()
 
 
 def swapped(shares, order):
-    moved = list(shares)
-    for step in order:
-        pairs = [(dev, dev ^ step) for dev in range(len(shares))]
-        moved[step] = lax.ppermute(shares[step], AXES, pairs)
-    return moved
-
-
-def by_pairs(first_rows, second_rows, alignment, diffusion_mask, lengths):
+    parts = len(order)
+    return [
+        lax.ppermute(share, AXES, [(dev, dev ^ step) for dev in range(parts)]) if step else share
+        for step, share in zip(order, shares)
+    ]
+
+
+def by_pairs(first_rows, second_rows, alignment, diffusion_mask, source_length, target_length):
     seq_count = lax.axis_size("seq")
     parts = 2 * seq_count
     width = first_rows.shape[3]
     share = width // parts
     kind = first_rows.dtype
-    me = (lax.axis_index("section") * seq_count + lax.axis_index("seq")).reshape(1)
     params = pltpu.CompilerParams(vmem_limit_bytes=VMEM_LIMIT)
-    order = [*range(seq_count, parts), *range(seq_count - 1, 0, -1)]
-    tails = [TAIL if step < seq_count else 0 for step in range(parts)]
+    order = sorted(range(parts), key=lambda step: (-(step >= seq_count), -(step >> 1 & 1), step))
+    order = [step for step in order if step > 1] + [1, 0]
+    sems = pltpu.SemaphoreType.DMA((2, parts))
     shares = pl.pallas_call(
-        functools.partial(pack_kernel, seq_count),
-        out_shape=[jax.ShapeDtypeStruct((2 * BLK + tail, share), kind) for tail in tails],
-        in_specs=specs(3, pltpu.SMEM) + specs(3, pltpu.VMEM),
+        functools.partial(pack_kernel, seq_count, order),
+        out_shape=[jax.ShapeDtypeStruct((2 * BLK + TAIL, share), kind)] * parts,
+        in_specs=specs(2, pltpu.SMEM) + specs(1, pltpu.VMEM) + specs(2, pltpu.HBM),
         out_specs=specs(parts, pltpu.VMEM),
+        scratch_shapes=[sems],
         compiler_params=params,
         name="pack",
-    )(me, lengths, alignment, diffusion_mask, first_rows, second_rows)
+    )(target_length, alignment, diffusion_mask, first_rows, second_rows)
     shares = swapped(shares, order)
     rows = pltpu.VMEM((parts, 2, BLK, share), kind)
     grads = pltpu.VMEM((seq_count, BLK, share), jnp.float32)
     shares = pl.pallas_call(
-        functools.partial(attend_kernel, seq_count),
+        functools.partial(attend_kernel, seq_count, order),
         out_shape=[jax.ShapeDtypeStruct((2 * BLK, share), kind)] * parts,
         in_specs=specs(2, pltpu.SMEM) + specs(parts, pltpu.VMEM),
         out_specs=specs(parts, pltpu.VMEM),
@@ -234,23 +260,23 @@
         compiler_params=params,
         cost_estimate=attend_cost(seq_count, share),
         name="attend",
-    )(me, lengths, *shares)
+    )(source_length, target_length, *shares)
     shares = swapped(shares, order)
     out_shape = jax.ShapeDtypeStruct((1, 1, BLK, width), kind)
     return pl.pallas_call(
-        unpack_kernel,
+        functools.partial(unpack_kernel, seq_count, order),
         out_shape=[out_shape, out_shape],
-        in_specs=specs(1, pltpu.SMEM) + specs(parts, pltpu.VMEM),
-        out_specs=specs(2, pltpu.VMEM),
+        in_specs=specs(parts, pltpu.VMEM),
+        out_specs=specs(2, pltpu.HBM),
+        scratch_shapes=[sems],
         compiler_params=params,
         name="unpack",
-    )(me, *shares)
+    )(*shares)
 
 
 def on_device(first_rows, second_rows, alignment, diffusion_mask, source_length, target_length):
     seq_count = lax.axis_size("seq")
     parts = lax.axis_size("section") * seq_count
-    lengths = jnp.concatenate([source_length, target_length])
     paired = (
         parts == 2 * seq_count
         and seq_count & (seq_count - 1) == 0
@@ -258,7 +284,9 @@
         and first_rows.shape[3] % (parts * LANES) == 0
     )
     work = by_pairs if paired else by_all_to_all
-    return tuple(work(first_rows, second_rows, alignment, diffusion_mask, lengths))
+    return tuple(
+        work(first_rows, second_rows, alignment, diffusion_mask, source_length, target_length)
+    )
 
 
 def solution(mesh):

time: 46.2 us -> 41.8 us (0.905)
  waiting for transfers between devices: 18.6 us -> 16.6 us
  starting transfers between devices: 15.7 us -> 14.1 us
  local copies, waits for them, and re-layouts: 2.75 us -> 2.08 us
    ppermute x14, waiting for transfers between devices: 18.6 us -> 16.6 us  [swapped(): lax.ppermute(share, AXES, [(dev, dev ^ step) for dev in range(parts)])]
    ppermute x14, starting transfers between devices: 15.7 us -> 14.1 us  [swapped(): lax.ppermute(share, AXES, [(dev, dev ^ step) for dev in range(parts)])]
    unnamed x8, local copies, waits for them, and re-layouts: 2.75 us -> 2.08 us
  transfers between devices with their start and end apart: 14 -> 14, of which waited for: 7 -> 8; matrix products, arithmetic and copies ran while one was open for 0% -> 0% of each run, Pallas kernels for 0% -> 0%
where the time goes in v3:
time: 41.8 us; the launch traced here: 41.6 us
  waiting for transfers between devices  16.6 us (40%)
  starting transfers between devices  14.1 us (34%)
  Pallas kernels  6.68 us (16%)
  local copies, waits for them, and re-layouts  2.08 us (5%)
  between operations  2.03 us (5%)
    ppermute x14, waiting for transfers between devices, swapped(): lax.ppermute(share, AXES, [(dev, dev ^ step) for dev in range(parts)])  16.6 us
    ppermute x14, starting transfers between devices, swapped(): lax.ppermute(share, AXES, [(dev, dev ^ step) for dev in range(parts)])  14.1 us
    pallas_call x1, Pallas kernels, by_pairs(): pl.pallas_call(functools.partial(attend_kernel, seq_count, order), out_sh...  4.53 us
    unnamed x8, local copies, waits for them, and re-layouts  2.08 us
    pallas_call x1, Pallas kernels, by_pairs(): pl.pallas_call(functools.partial(unpack_kernel, seq_count, order), out_sh...  1.1 us
    pallas_call x1, Pallas kernels, by_pairs(): pl.pallas_call(functools.partial(pack_kernel, seq_count, order), out_shap...  1.05 us
  transfers between devices with their start and end apart: 14, of which 8 were waited for; matrix products, arithmetic and copies ran while one was open for 0% of the time, Pallas kernels for 0%

profile of v3, /device:TPU:0, one launch (start us, length us, event | category | flops | bytes accessed | tf_op | source)
XLA Modules:
  0.0 41.6 jit_solution(1804869375346922281)
XLA Ops:
  0.6 0.0 copy-start.3
  0.6 0.0 copy-start.2
  1.3 0.0 copy-done.3
  1.3 0.0 copy-done.2
  1.3 0.0 copy-start
  1.3 1.0 %copy-done = bf16[1,1,128,2048]{3,2,1,0:T(8,128)(2,1)S(1)} copy-done((bf16[1,1,128,2048]{3,2,1,0:T(8,128)(2,1)S(1)}, bf16[1,1,128,2048]{3,2,1,0:T(8,128)(2,1)}, u32[]{:S(2)}) %copy-start) | copy-done | bytes 524312
  2.4 0.0 copy-start.1
  2.4 1.0 %copy-done.1 = bf16[1,1,128,2048]{3,2,1,0:T(8,128)(2,1)S(1)} copy-done((bf16[1,1,128,2048]{3,2,1,0:T(8,128)(2,1)S(1)}, bf16[1,1,128,2048]{3,2,1,0:T(8,128)(2,1)}, u32[]{:S(2)}) %copy-start.1) | copy-done | bytes 524312
  3.4 1.0 %pack.1 = (bf16[272,256]{1,0:T(8,128)(2,1)S(1)}, bf16[272,256]{1,0:T(8,128)(2,1)S(1)}, bf16[272,256]{1,0:T(8,128)(2,1)S(1)}, bf16[272,256]{1,0:T(8,128)(2,1)S(1)...) custom-call(s32[1]{0:T(128)S(6)} %copy.9.target_len, ...), custom_call_target="tpu_custom_call" | custom-call | tf_op jit(solution)/shard_map/pack/pallas_call | solution.py:242
  4.5 4.0 %collective-permute-start = (bf16[272,256]{1,0:T(8,128)(2,1)S(1)}, bf16[272,256]{1,0:T(8,128)(2,1)S(1)}, u32[]{:S(2)}, u32[]{:S(2)}) collective-permute-start(bf16[272,256]{1,0:T(8,128)(2,1)S(1)} %get-tuple-element.18), channel_id=1, source_target_pairs={{0,18},{1,19},{2,16},{3,17},{16,2},{17,3},{18,0},{19,1},{4,22},{5,... | collective-permute-start | bytes 417800 | tf_op jit(solution)/shard_map/ppermute | solution.py:227
  8.4 0.0 collective-permute-start.1
  8.4 1.2 %collective-permute-start.2 = (bf16[272,256]{1,0:T(8,128)(2,1)S(1)}, bf16[272,256]{1,0:T(8,128)(2,1)S(1)}, u32[]{:S(2)}, u32[]{:S(2)}) collective-permute-start(bf16[272,256]{1,0:T(8,128)(2,1)S(1)} %get-tuple-element.20), channel_id=1, source_target_pairs={{0,16},{1,17},{2,18},{3,19},{16,0},{17,1},{18,2},{19,3},{4,20},{5,... | collective-permute-start | bytes 417800 | tf_op jit(solution)/shard_map/ppermute | solution.py:227
  9.6 0.6 %collective-permute-start.3 = (bf16[272,256]{1,0:T(8,128)(2,1)S(1)}, bf16[272,256]{1,0:T(8,128)(2,1)S(1)}, u32[]{:S(2)}, u32[]{:S(2)}) collective-permute-start(bf16[272,256]{1,0:T(8,128)(2,1)S(1)} %get-tuple-element.21), channel_id=1, source_target_pairs={{0,17},{1,16},{2,19},{3,18},{16,1},{17,0},{18,3},{19,2},{4,21},{5,... | collective-permute-start | bytes 417800 | tf_op jit(solution)/shard_map/ppermute | solution.py:227
  10.2 1.7 %collective-permute-start.4 = (bf16[272,256]{1,0:T(8,128)(2,1)S(1)}, bf16[272,256]{1,0:T(8,128)(2,1)S(1)}, u32[]{:S(2)}, u32[]{:S(2)}) collective-permute-start(bf16[272,256]{1,0:T(8,128)(2,1)S(1)} %get-tuple-element.22), channel_id=1, source_target_pairs={{0,2},{1,3},{2,0},{3,1},{16,18},{17,19},{18,16},{19,17},{4,6},{5,7... | collective-permute-start | bytes 417800 | tf_op jit(solution)/shard_map/ppermute | solution.py:227
  11.9 0.7 %collective-permute-done.refs_0_ = bf16[272,256]{1,0:T(8,128)(2,1)S(1)} collective-permute-done((bf16[272,256]{1,0:T(8,128)(2,1)S(1)}, bf16[272,256]{1,0:T(8,128)(2,1)S(1)}, u32[]{:S(2)}, u32[]{:S(2)}) %collective-permute-start) | collective-permute-done | bytes 139296 | tf_op jit(solution)/shard_map/ppermute | solution.py:227
  12.6 0.0 collective-permute-start.5
  12.6 3.0 %collective-permute-done.1.refs_1_ = bf16[272,256]{1,0:T(8,128)(2,1)S(1)} collective-permute-done((bf16[272,256]{1,0:T(8,128)(2,1)S(1)}, bf16[272,256]{1,0:T(8,128)(2,1)S(1)}, u32[]{:S(2)}, u32[]{:S(2)}) %collective-permute-start.1) | collective-permute-done | bytes 139296 | tf_op jit(solution)/shard_map/ppermute | solution.py:227
  15.5 0.0 collective-permute-start.6
  16.2 1.9 %collective-permute-done.2.refs_2_ = bf16[272,256]{1,0:T(8,128)(2,1)S(1)} collective-permute-done((bf16[272,256]{1,0:T(8,128)(2,1)S(1)}, bf16[272,256]{1,0:T(8,128)(2,1)S(1)}, u32[]{:S(2)}, u32[]{:S(2)}) %collective-permute-start.2) | collective-permute-done | bytes 139296 | tf_op jit(solution)/shard_map/ppermute | solution.py:227
  18.1 2.9 %collective-permute-done.3.refs_3_ = bf16[272,256]{1,0:T(8,128)(2,1)S(1)} collective-permute-done((bf16[272,256]{1,0:T(8,128)(2,1)S(1)}, bf16[272,256]{1,0:T(8,128)(2,1)S(1)}, u32[]{:S(2)}, u32[]{:S(2)}) %collective-permute-start.3) | collective-permute-done | bytes 139296 | tf_op jit(solution)/shard_map/ppermute | solution.py:227
  21.0 0.0 collective-permute-done.4.refs_4_
  21.0 0.0 collective-permute-done.5.refs_5_
  21.0 0.0 collective-permute-done.6.refs_6_
  21.0 4.5 %attend.1 = (bf16[256,256]{1,0:T(8,128)(2,1)S(1)}, bf16[256,256]{1,0:T(8,128)(2,1)S(1)}, bf16[256,256]{1,0:T(8,128)(2,1)S(1)}, bf16[256,256]{1,0:T(8,128)(2,1)S(...) custom-call(s32[1]{0:T(128)S(6)} %copy.8.source_len, ...), custom_call_target="tpu_custom_call" | custom-call | flops 335544320 | bytes 2097152 | tf_op jit(solution)/shard_map/attend/pallas_call | solution.py:254
  25.6 2.8 %collective-permute-start.7 = (bf16[256,256]{1,0:T(8,128)(2,1)S(1)}, bf16[256,256]{1,0:T(8,128)(2,1)S(1)}, u32[]{:S(2)}, u32[]{:S(2)}) collective-permute-start(bf16[256,256]{1,0:T(8,128)(2,1)S(1)} %get-tuple-element.26), channel_id=1, source_target_pairs={{0,18},{1,19},{2,16},{3,17},{16,2},{17,3},{18,0},{19,1},{4,22},{5,... | collective-permute-start | bytes 393224 | tf_op jit(solution)/shard_map/ppermute | solution.py:227
  28.3 0.0 collective-permute-start.8
  28.3 1.4 %collective-permute-start.9 = (bf16[256,256]{1,0:T(8,128)(2,1)S(1)}, bf16[256,256]{1,0:T(8,128)(2,1)S(1)}, u32[]{:S(2)}, u32[]{:S(2)}) collective-permute-start(bf16[256,256]{1,0:T(8,128)(2,1)S(1)} %get-tuple-element.28), channel_id=1, source_target_pairs={{0,16},{1,17},{2,18},{3,19},{16,0},{17,1},{18,2},{19,3},{4,20},{5,... | collective-permute-start | bytes 393224 | tf_op jit(solution)/shard_map/ppermute | solution.py:227
  29.8 0.3 collective-permute-start.10
  30.1 1.7 %collective-permute-start.11 = (bf16[256,256]{1,0:T(8,128)(2,1)S(1)}, bf16[256,256]{1,0:T(8,128)(2,1)S(1)}, u32[]{:S(2)}, u32[]{:S(2)}) collective-permute-start(bf16[256,256]{1,0:T(8,128)(2,1)S(1)} %get-tuple-element.30), channel_id=1, source_target_pairs={{0,2},{1,3},{2,0},{3,1},{16,18},{17,19},{18,16},{19,17},{4,6},{5,7... | collective-permute-start | bytes 393224 | tf_op jit(solution)/shard_map/ppermute | solution.py:227
  31.8 0.4 collective-permute-done.7.refs_0_
  32.2 0.5 %collective-permute-start.12 = (bf16[256,256]{1,0:T(8,128)(2,1)S(1)}, bf16[256,256]{1,0:T(8,128)(2,1)S(1)}, u32[]{:S(2)}, u32[]{:S(2)}) collective-permute-start(bf16[256,256]{1,0:T(8,128)(2,1)S(1)} %get-tuple-element.31), channel_id=1, source_target_pairs={{0,3},{1,2},{2,1},{3,0},{16,19},{17,18},{18,17},{19,16},{4,7},{5,6... | collective-permute-start | bytes 393224 | tf_op jit(solution)/shard_map/ppermute | solution.py:227
  32.7 2.4 %collective-permute-done.8.refs_1_ = bf16[256,256]{1,0:T(8,128)(2,1)S(1)} collective-permute-done((bf16[256,256]{1,0:T(8,128)(2,1)S(1)}, bf16[256,256]{1,0:T(8,128)(2,1)S(1)}, u32[]{:S(2)}, u32[]{:S(2)}) %collective-permute-start.8) | collective-permute-done | bytes 131104 | tf_op jit(solution)/shard_map/ppermute | solution.py:227
  35.1 0.1 collective-permute-start.13
  35.1 2.6 %collective-permute-done.9.refs_2_ = bf16[256,256]{1,0:T(8,128)(2,1)S(1)} collective-permute-done((bf16[256,256]{1,0:T(8,128)(2,1)S(1)}, bf16[256,256]{1,0:T(8,128)(2,1)S(1)}, u32[]{:S(2)}, u32[]{:S(2)}) %collective-permute-start.9) | collective-permute-done | bytes 131104 | tf_op jit(solution)/shard_map/ppermute | solution.py:227
  37.8 2.7 %collective-permute-done.10.refs_3_ = bf16[256,256]{1,0:T(8,128)(2,1)S(1)} collective-permute-done((bf16[256,256]{1,0:T(8,128)(2,1)S(1)}, bf16[256,256]{1,0:T(8,128)(2,1)S(1)}, u32[]{:S(2)}, u32[]{:S(2)}) %collective-permute-start.10) | collective-permute-done | bytes 131104 | tf_op jit(solution)/shard_map/ppermute | solution.py:227
  40.5 0.0 collective-permute-done.11.refs_4_
  40.5 0.0 collective-permute-done.12.refs_5_
  40.5 0.0 collective-permute-done.13.refs_6_
  40.5 1.1 %unpack.1 = (bf16[1,1,128,2048]{3,2,1,0:T(8,128)(2,1)}, bf16[1,1,128,2048]{3,2,1,0:T(8,128)(2,1)}) custom-call(bf16[256,256]{1,0:T(8,128)(2,1)S(1)} %collective-permute-done.7.refs_0_, bf16[256,256]{1,0:T(8,128)(2,1)S(1)} %collective-permute-done.8.refs_1_, bf16[256,256]{1,0:T(8,128)(2,1)S(1)} %collective-permute-done.9.refs_2_, ...), custom_call_target="tpu_custom_call" | custom-call | tf_op jit(solution)/shard_map/unpack/pallas_call | solution.py:266
Async XLA Ops:
  0.6 0.7 %copy-start.3 = (s32[1,128]{1,0:T(1,128)S(1)}, s32[1,128]{1,0:T(1,128)}, u32[]{:S(2)}) copy-start(s32[1,128]{1,0:T(1,128)} %mask.1) | copy-start | bytes 1540
  0.6 0.7 %copy-start.2 = (s32[1,1,2]{2,1,0:T(1,128)S(1)}, s32[1,1,2]{2,1,0:T(1,128)}, u32[]{:S(2)}) copy-start(s32[1,1,2]{2,1,0:T(1,128)} %lists.1) | copy-start | bytes 28
  1.3 1.0 %copy-start = (bf16[1,1,128,2048]{3,2,1,0:T(8,128)(2,1)S(1)}, bf16[1,1,128,2048]{3,2,1,0:T(8,128)(2,1)}, u32[]{:S(2)}) copy-start(bf16[1,1,128,2048]{3,2,1,0:T(8,128)(2,1)} %first.1) | copy-start | bytes 1572868
  2.4 1.0 %copy-start.1 = (bf16[1,1,128,2048]{3,2,1,0:T(8,128)(2,1)S(1)}, bf16[1,1,128,2048]{3,2,1,0:T(8,128)(2,1)}, u32[]{:S(2)}) copy-start(bf16[1,1,128,2048]{3,2,1,0:T(8,128)(2,1)} %second.1) | copy-start | bytes 1572868
  4.5 8.1 %collective-permute-start = (bf16[272,256]{1,0:T(8,128)(2,1)S(1)}, bf16[272,256]{1,0:T(8,128)(2,1)S(1)}, u32[]{:S(2)}, u32[]{:S(2)}) collective-permute-start(bf16[272,256]{1,0:T(8,128)(2,1)S(1)} %get-tuple-element.18), channel_id=1, source_target_pairs={{0,18},{1,19},{2,16},{3,17},{16,2},{17,3},{18,0},{19,1},{4,22},{5,... | collective-permute-start | bytes 417800 | tf_op jit(solution)/shard_map/ppermute | solution.py:227
  8.4 7.1 %collective-permute-start.1 = (bf16[272,256]{1,0:T(8,128)(2,1)S(1)}, bf16[272,256]{1,0:T(8,128)(2,1)S(1)}, u32[]{:S(2)}, u32[]{:S(2)}) collective-permute-start(bf16[272,256]{1,0:T(8,128)(2,1)S(1)} %get-tuple-element.19), channel_id=1, source_target_pairs={{0,19},{1,18},{2,17},{3,16},{16,3},{17,2},{18,1},{19,0},{4,23},{5,... | collective-permute-start | bytes 417800 | tf_op jit(solution)/shard_map/ppermute | solution.py:227
  8.4 9.7 %collective-permute-start.2 = (bf16[272,256]{1,0:T(8,128)(2,1)S(1)}, bf16[272,256]{1,0:T(8,128)(2,1)S(1)}, u32[]{:S(2)}, u32[]{:S(2)}) collective-permute-start(bf16[272,256]{1,0:T(8,128)(2,1)S(1)} %get-tuple-element.20), channel_id=1, source_target_pairs={{0,16},{1,17},{2,18},{3,19},{16,0},{17,1},{18,2},{19,3},{4,20},{5,... | collective-permute-start | bytes 417800 | tf_op jit(solution)/shard_map/ppermute | solution.py:227
  9.6 11.4 %collective-permute-start.3 = (bf16[272,256]{1,0:T(8,128)(2,1)S(1)}, bf16[272,256]{1,0:T(8,128)(2,1)S(1)}, u32[]{:S(2)}, u32[]{:S(2)}) collective-permute-start(bf16[272,256]{1,0:T(8,128)(2,1)S(1)} %get-tuple-element.21), channel_id=1, source_target_pairs={{0,17},{1,16},{2,19},{3,18},{16,1},{17,0},{18,3},{19,2},{4,21},{5,... | collective-permute-start | bytes 417800 | tf_op jit(solution)/shard_map/ppermute | solution.py:227
  10.2 10.8 %collective-permute-start.4 = (bf16[272,256]{1,0:T(8,128)(2,1)S(1)}, bf16[272,256]{1,0:T(8,128)(2,1)S(1)}, u32[]{:S(2)}, u32[]{:S(2)}) collective-permute-start(bf16[272,256]{1,0:T(8,128)(2,1)S(1)} %get-tuple-element.22), channel_id=1, source_target_pairs={{0,2},{1,3},{2,0},{3,1},{16,18},{17,19},{18,16},{19,17},{4,6},{5,7... | collective-permute-start | bytes 417800 | tf_op jit(solution)/shard_map/ppermute | solution.py:227
  12.6 8.5 %collective-permute-start.5 = (bf16[272,256]{1,0:T(8,128)(2,1)S(1)}, bf16[272,256]{1,0:T(8,128)(2,1)S(1)}, u32[]{:S(2)}, u32[]{:S(2)}) collective-permute-start(bf16[272,256]{1,0:T(8,128)(2,1)S(1)} %get-tuple-element.23), channel_id=1, source_target_pairs={{0,3},{1,2},{2,1},{3,0},{16,19},{17,18},{18,17},{19,16},{4,7},{5,6... | collective-permute-start | bytes 417800 | tf_op jit(solution)/shard_map/ppermute | solution.py:227
  15.5 5.5 %collective-permute-start.6 = (bf16[272,256]{1,0:T(8,128)(2,1)S(1)}, bf16[272,256]{1,0:T(8,128)(2,1)S(1)}, u32[]{:S(2)}, u32[]{:S(2)}) collective-permute-start(bf16[272,256]{1,0:T(8,128)(2,1)S(1)} %get-tuple-element.24), channel_id=1, source_target_pairs={{0,1},{1,0},{2,3},{3,2},{16,17},{17,16},{18,19},{19,18},{4,5},{5,4... | collective-permute-start | bytes 417800 | tf_op jit(solution)/shard_map/ppermute | solution.py:227
  25.6 6.6 %collective-permute-start.7 = (bf16[256,256]{1,0:T(8,128)(2,1)S(1)}, bf16[256,256]{1,0:T(8,128)(2,1)S(1)}, u32[]{:S(2)}, u32[]{:S(2)}) collective-permute-start(bf16[256,256]{1,0:T(8,128)(2,1)S(1)} %get-tuple-element.26), channel_id=1, source_target_pairs={{0,18},{1,19},{2,16},{3,17},{16,2},{17,3},{18,0},{19,1},{4,22},{5,... | collective-permute-start | bytes 393224 | tf_op jit(solution)/shard_map/ppermute | solution.py:227
  28.3 6.7 %collective-permute-start.8 = (bf16[256,256]{1,0:T(8,128)(2,1)S(1)}, bf16[256,256]{1,0:T(8,128)(2,1)S(1)}, u32[]{:S(2)}, u32[]{:S(2)}) collective-permute-start(bf16[256,256]{1,0:T(8,128)(2,1)S(1)} %get-tuple-element.27), channel_id=1, source_target_pairs={{0,19},{1,18},{2,17},{3,16},{16,3},{17,2},{18,1},{19,0},{4,23},{5,... | collective-permute-start | bytes 393224 | tf_op jit(solution)/shard_map/ppermute | solution.py:227
  28.3 9.4 %collective-permute-start.9 = (bf16[256,256]{1,0:T(8,128)(2,1)S(1)}, bf16[256,256]{1,0:T(8,128)(2,1)S(1)}, u32[]{:S(2)}, u32[]{:S(2)}) collective-permute-start(bf16[256,256]{1,0:T(8,128)(2,1)S(1)} %get-tuple-element.28), channel_id=1, source_target_pairs={{0,16},{1,17},{2,18},{3,19},{16,0},{17,1},{18,2},{19,3},{4,20},{5,... | collective-permute-start | bytes 393224 | tf_op jit(solution)/shard_map/ppermute | solution.py:227
  29.8 10.7 %collective-permute-start.10 = (bf16[256,256]{1,0:T(8,128)(2,1)S(1)}, bf16[256,256]{1,0:T(8,128)(2,1)S(1)}, u32[]{:S(2)}, u32[]{:S(2)}) collective-permute-start(bf16[256,256]{1,0:T(8,128)(2,1)S(1)} %get-tuple-element.29), channel_id=1, source_target_pairs={{0,17},{1,16},{2,19},{3,18},{16,1},{17,0},{18,3},{19,2},{4,21},{5,... | collective-permute-start | bytes 393224 | tf_op jit(solution)/shard_map/ppermute | solution.py:227
  30.1 10.4 %collective-permute-start.11 = (bf16[256,256]{1,0:T(8,128)(2,1)S(1)}, bf16[256,256]{1,0:T(8,128)(2,1)S(1)}, u32[]{:S(2)}, u32[]{:S(2)}) collective-permute-start(bf16[256,256]{1,0:T(8,128)(2,1)S(1)} %get-tuple-element.30), channel_id=1, source_target_pairs={{0,2},{1,3},{2,0},{3,1},{16,18},{17,19},{18,16},{19,17},{4,6},{5,7... | collective-permute-start | bytes 393224 | tf_op jit(solution)/shard_map/ppermute | solution.py:227
  32.2 8.3 %collective-permute-start.12 = (bf16[256,256]{1,0:T(8,128)(2,1)S(1)}, bf16[256,256]{1,0:T(8,128)(2,1)S(1)}, u32[]{:S(2)}, u32[]{:S(2)}) collective-permute-start(bf16[256,256]{1,0:T(8,128)(2,1)S(1)} %get-tuple-element.31), channel_id=1, source_target_pairs={{0,3},{1,2},{2,1},{3,0},{16,19},{17,18},{18,17},{19,16},{4,7},{5,6... | collective-permute-start | bytes 393224 | tf_op jit(solution)/shard_map/ppermute | solution.py:227
  35.1 5.4 %collective-permute-start.13 = (bf16[256,256]{1,0:T(8,128)(2,1)S(1)}, bf16[256,256]{1,0:T(8,128)(2,1)S(1)}, u32[]{:S(2)}, u32[]{:S(2)}) collective-permute-start(bf16[256,256]{1,0:T(8,128)(2,1)S(1)} %get-tuple-element.32), channel_id=1, source_target_pairs={{0,1},{1,0},{2,3},{3,2},{16,17},{17,16},{18,19},{19,18},{4,5},{5,4... | collective-permute-start | bytes 393224 | tf_op jit(solution)/shard_map/ppermute | solution.py:227

commit v4 on v3

--- a/solution.py
+++ b/solution.py
@@ -105,6 +105,10 @@
     return [pl.BlockSpec(memory_space=space)] * count
 
 
+def in_hbm(*arrays):
+    return [pltpu.with_memory_space_constraint(array, pltpu.HBM) for array in arrays]
+
+
 def gathered_kernel(seq_count, lists, source_len, target_len, rows, out, key_grad, value_grad):
     def listed(block, slot):
         return lists[block, slot]
@@ -147,8 +151,15 @@
     return lax.axis_index("section") * seq_count + lax.axis_index("seq")
 
 
-def pack_kernel(seq_count, order, target_len, lists, mask, first, second, *refs):
-    outs, sem = refs[:-1], refs[-1]
+def pack_kernel(seq_count, order, *refs):
+    target_len, smalls, (first, second) = refs[0], refs[1:3], refs[3:5]
+    outs, (lists, mask, small_sem, sem) = refs[5:-4], refs[-4:]
+    small_copies = [
+        pltpu.make_async_copy(source, held, small_sem.at[slot])
+        for slot, (source, held) in enumerate(zip(smalls, (lists, mask)))
+    ]
+    for copy in small_copies:
+        copy.start()
     me = device_index(seq_count)
     here = me % seq_count
     share = outs[0].shape[1]
@@ -164,6 +175,8 @@
         for copy in pair:
             copy.start()
         copies.append(pair)
+    for copy in small_copies:
+        copy.wait()
     positions = here * BLK + lax.broadcasted_iota(jnp.int32, (1, BLK), 1)
     keep = ((positions < target_len[0]) & (mask[...] == 1)) | (me < seq_count)
     keep = jnp.broadcast_to(jnp.where(keep, 1.0, 0.0), (BLK, BLK)).T.astype(jnp.bfloat16)
@@ -236,18 +249,24 @@
     share = width // parts
     kind = first_rows.dtype
     params = pltpu.CompilerParams(vmem_limit_bytes=VMEM_LIMIT)
-    order = sorted(range(parts), key=lambda step: (-(step >= seq_count), -(step >> 1 & 1), step))
-    order = [step for step in order if step > 1] + [1, 0]
+    far = [step for step in range(seq_count, parts) if step & 2]
+    near = [step for step in range(seq_count, parts) if not step & 2]
+    order = near[:1] + far + near[1:] + list(range(2, seq_count)) + [1, 0]
     sems = pltpu.SemaphoreType.DMA((2, parts))
     shares = pl.pallas_call(
         functools.partial(pack_kernel, seq_count, order),
         out_shape=[jax.ShapeDtypeStruct((2 * BLK + TAIL, share), kind)] * parts,
-        in_specs=specs(2, pltpu.SMEM) + specs(1, pltpu.VMEM) + specs(2, pltpu.HBM),
+        in_specs=specs(1, pltpu.SMEM) + specs(4, pltpu.HBM),
         out_specs=specs(parts, pltpu.VMEM),
-        scratch_shapes=[sems],
+        scratch_shapes=[
+            pltpu.SMEM(alignment.shape, jnp.int32),
+            pltpu.VMEM(diffusion_mask.shape, jnp.int32),
+            pltpu.SemaphoreType.DMA((2,)),
+            sems,
+        ],
         compiler_params=params,
         name="pack",
-    )(target_length, alignment, diffusion_mask, first_rows, second_rows)
+    )(target_length, *in_hbm(alignment, diffusion_mask, first_rows, second_rows))
     shares = swapped(shares, order)
     rows = pltpu.VMEM((parts, 2, BLK, share), kind)
     grads = pltpu.VMEM((seq_count, BLK, share), jnp.float32)

time: 41.8 us -> 44.4 us (1.062)
  starting transfers between devices: 14.1 us -> 16.5 us
  local copies, waits for them, and re-layouts: 2.08 us -> 0 us
  waiting for transfers between devices: 16.6 us -> 18.6 us
    ppermute x14, starting transfers between devices: 14.1 us -> 16.5 us  [swapped(): lax.ppermute(share, AXES, [(dev, dev ^ step) for dev in range(parts)])]
    unnamed x8 -> x0, local copies, waits for them, and re-layouts: 2.08 us -> none
    ppermute x14, waiting for transfers between devices: 16.6 us -> 18.6 us  [swapped(): lax.ppermute(share, AXES, [(dev, dev ^ step) for dev in range(parts)])]
  transfers between devices with their start and end apart: 14 -> 14, of which waited for: 8 -> 5; matrix products, arithmetic and copies ran while one was open for 0% -> 0% of each run, Pallas kernels for 0% -> 0%
where the time goes in v4:
time: 44.4 us; the launch traced here: 44.2 us
  waiting for transfers between devices  18.6 us (42%)
  starting transfers between devices  16.5 us (37%)
  Pallas kernels  7.05 us (16%)
  between operations  1.98 us (4%)
    ppermute x14, waiting for transfers between devices, swapped(): lax.ppermute(share, AXES, [(dev, dev ^ step) for dev in range(parts)])  18.6 us
    ppermute x14, starting transfers between devices, swapped(): lax.ppermute(share, AXES, [(dev, dev ^ step) for dev in range(parts)])  16.5 us
    pallas_call x1, Pallas kernels, by_pairs(): pl.pallas_call(functools.partial(attend_kernel, seq_count, order), out_sh...  4.53 us
    pallas_call x1, Pallas kernels, by_pairs(): pl.pallas_call(functools.partial(pack_kernel, seq_count, order), out_shap...  1.43 us
    pallas_call x1, Pallas kernels, by_pairs(): pl.pallas_call(functools.partial(unpack_kernel, seq_count, order), out_sh...  1.09 us
  transfers between devices with their start and end apart: 14, of which 5 were waited for; matrix products, arithmetic and copies ran while one was open for 0% of the time, Pallas kernels for 0%

profile of v4, /device:TPU:0, one launch (start us, length us, event | category | flops | bytes accessed | tf_op | source)
XLA Modules:
  0.0 44.2 jit_solution(17547191830664905539)
XLA Ops:
  1.3 1.4 %pack.1 = (bf16[272,256]{1,0:T(8,128)(2,1)S(1)}, bf16[272,256]{1,0:T(8,128)(2,1)S(1)}, bf16[272,256]{1,0:T(8,128)(2,1)S(1)}, bf16[272,256]{1,0:T(8,128)(2,1)S(1)...) custom-call(s32[1]{0:T(128)S(6)} %copy.9.refs_0_.target_len, ...), custom_call_target="tpu_custom_call" | custom-call | tf_op jit(solution)/shard_map/pack/pallas_call | solution.py:256
  2.7 3.0 %collective-permute-start = (bf16[272,256]{1,0:T(8,128)(2,1)S(1)}, bf16[272,256]{1,0:T(8,128)(2,1)S(1)}, u32[]{:S(2)}, u32[]{:S(2)}) collective-permute-start(bf16[272,256]{1,0:T(8,128)(2,1)S(1)} %get-tuple-element.18), channel_id=1, source_target_pairs={{0,16},{1,17},{2,18},{3,19},{16,0},{17,1},{18,2},{19,3},{4,20},{5,... | collective-permute-start | bytes 417800 | tf_op jit(solution)/shard_map/ppermute | solution.py:240
  5.8 1.4 %collective-permute-start.1 = (bf16[272,256]{1,0:T(8,128)(2,1)S(1)}, bf16[272,256]{1,0:T(8,128)(2,1)S(1)}, u32[]{:S(2)}, u32[]{:S(2)}) collective-permute-start(bf16[272,256]{1,0:T(8,128)(2,1)S(1)} %get-tuple-element.19), channel_id=1, source_target_pairs={{0,18},{1,19},{2,16},{3,17},{16,2},{17,3},{18,0},{19,1},{4,22},{5,... | collective-permute-start | bytes 417800 | tf_op jit(solution)/shard_map/ppermute | solution.py:240
  7.2 0.4 collective-permute-start.2
  7.6 0.9 %collective-permute-start.3 = (bf16[272,256]{1,0:T(8,128)(2,1)S(1)}, bf16[272,256]{1,0:T(8,128)(2,1)S(1)}, u32[]{:S(2)}, u32[]{:S(2)}) collective-permute-start(bf16[272,256]{1,0:T(8,128)(2,1)S(1)} %get-tuple-element.21), channel_id=1, source_target_pairs={{0,17},{1,16},{2,19},{3,18},{16,1},{17,0},{18,3},{19,2},{4,21},{5,... | collective-permute-start | bytes 417800 | tf_op jit(solution)/shard_map/ppermute | solution.py:240
  8.5 1.9 %collective-permute-start.4 = (bf16[272,256]{1,0:T(8,128)(2,1)S(1)}, bf16[272,256]{1,0:T(8,128)(2,1)S(1)}, u32[]{:S(2)}, u32[]{:S(2)}) collective-permute-start(bf16[272,256]{1,0:T(8,128)(2,1)S(1)} %get-tuple-element.22), channel_id=1, source_target_pairs={{0,2},{1,3},{2,0},{3,1},{16,18},{17,19},{18,16},{19,17},{4,6},{5,7... | collective-permute-start | bytes 417800 | tf_op jit(solution)/shard_map/ppermute | solution.py:240
  10.4 5.5 %collective-permute-done.refs_0_ = bf16[272,256]{1,0:T(8,128)(2,1)S(1)} collective-permute-done((bf16[272,256]{1,0:T(8,128)(2,1)S(1)}, bf16[272,256]{1,0:T(8,128)(2,1)S(1)}, u32[]{:S(2)}, u32[]{:S(2)}) %collective-permute-start) | collective-permute-done | bytes 139296 | tf_op jit(solution)/shard_map/ppermute | solution.py:240
  15.8 0.0 collective-permute-start.5
  15.9 0.0 collective-permute-done.1.refs_1_
  15.9 2.0 %collective-permute-start.6 = (bf16[272,256]{1,0:T(8,128)(2,1)S(1)}, bf16[272,256]{1,0:T(8,128)(2,1)S(1)}, u32[]{:S(2)}, u32[]{:S(2)}) collective-permute-start(bf16[272,256]{1,0:T(8,128)(2,1)S(1)} %get-tuple-element.24), channel_id=1, source_target_pairs={{0,1},{1,0},{2,3},{3,2},{16,17},{17,16},{18,19},{19,18},{4,5},{5,4... | collective-permute-start | bytes 417800 | tf_op jit(solution)/shard_map/ppermute | solution.py:240
  18.6 0.0 collective-permute-done.2.refs_2_
  18.6 0.0 collective-permute-done.3.refs_3_
  18.6 0.0 collective-permute-done.4.refs_4_
  18.6 2.8 %collective-permute-done.5.refs_5_ = bf16[272,256]{1,0:T(8,128)(2,1)S(1)} collective-permute-done((bf16[272,256]{1,0:T(8,128)(2,1)S(1)}, bf16[272,256]{1,0:T(8,128)(2,1)S(1)}, u32[]{:S(2)}, u32[]{:S(2)}) %collective-permute-start.5) | collective-permute-done | bytes 139296 | tf_op jit(solution)/shard_map/ppermute | solution.py:240
  21.4 0.0 collective-permute-done.6.refs_6_
  21.4 4.5 %attend.1 = (bf16[256,256]{1,0:T(8,128)(2,1)S(1)}, bf16[256,256]{1,0:T(8,128)(2,1)S(1)}, bf16[256,256]{1,0:T(8,128)(2,1)S(1)}, bf16[256,256]{1,0:T(8,128)(2,1)S(...) custom-call(s32[1]{0:T(128)S(6)} %copy.8.source_len, ...), custom_call_target="tpu_custom_call" | custom-call | flops 335544320 | bytes 2097152 | tf_op jit(solution)/shard_map/attend/pallas_call | solution.py:273
  25.9 2.8 %collective-permute-start.7 = (bf16[256,256]{1,0:T(8,128)(2,1)S(1)}, bf16[256,256]{1,0:T(8,128)(2,1)S(1)}, u32[]{:S(2)}, u32[]{:S(2)}) collective-permute-start(bf16[256,256]{1,0:T(8,128)(2,1)S(1)} %get-tuple-element.26), channel_id=1, source_target_pairs={{0,16},{1,17},{2,18},{3,19},{16,0},{17,1},{18,2},{19,3},{4,20},{5,... | collective-permute-start | bytes 393224 | tf_op jit(solution)/shard_map/ppermute | solution.py:240
  28.7 0.2 collective-permute-start.8
  28.9 1.9 %collective-permute-start.9 = (bf16[256,256]{1,0:T(8,128)(2,1)S(1)}, bf16[256,256]{1,0:T(8,128)(2,1)S(1)}, u32[]{:S(2)}, u32[]{:S(2)}) collective-permute-start(bf16[256,256]{1,0:T(8,128)(2,1)S(1)} %get-tuple-element.28), channel_id=1, source_target_pairs={{0,19},{1,18},{2,17},{3,16},{16,3},{17,2},{18,1},{19,0},{4,23},{5,... | collective-permute-start | bytes 393224 | tf_op jit(solution)/shard_map/ppermute | solution.py:240
  30.8 0.6 %collective-permute-start.10 = (bf16[256,256]{1,0:T(8,128)(2,1)S(1)}, bf16[256,256]{1,0:T(8,128)(2,1)S(1)}, u32[]{:S(2)}, u32[]{:S(2)}) collective-permute-start(bf16[256,256]{1,0:T(8,128)(2,1)S(1)} %get-tuple-element.29), channel_id=1, source_target_pairs={{0,17},{1,16},{2,19},{3,18},{16,1},{17,0},{18,3},{19,2},{4,21},{5,... | collective-permute-start | bytes 393224 | tf_op jit(solution)/shard_map/ppermute | solution.py:240
  31.4 0.7 %collective-permute-start.11 = (bf16[256,256]{1,0:T(8,128)(2,1)S(1)}, bf16[256,256]{1,0:T(8,128)(2,1)S(1)}, u32[]{:S(2)}, u32[]{:S(2)}) collective-permute-start(bf16[256,256]{1,0:T(8,128)(2,1)S(1)} %get-tuple-element.30), channel_id=1, source_target_pairs={{0,2},{1,3},{2,0},{3,1},{16,18},{17,19},{18,16},{19,17},{4,6},{5,7... | collective-permute-start | bytes 393224 | tf_op jit(solution)/shard_map/ppermute | solution.py:240
  32.1 6.1 %collective-permute-done.7.refs_0_ = bf16[256,256]{1,0:T(8,128)(2,1)S(1)} collective-permute-done((bf16[256,256]{1,0:T(8,128)(2,1)S(1)}, bf16[256,256]{1,0:T(8,128)(2,1)S(1)}, u32[]{:S(2)}, u32[]{:S(2)}) %collective-permute-start.7) | collective-permute-done | bytes 131104 | tf_op jit(solution)/shard_map/ppermute | solution.py:240
  38.2 0.0 collective-permute-start.12
  38.2 0.0 collective-permute-done.8.refs_1_
  38.2 0.7 %collective-permute-start.13 = (bf16[256,256]{1,0:T(8,128)(2,1)S(1)}, bf16[256,256]{1,0:T(8,128)(2,1)S(1)}, u32[]{:S(2)}, u32[]{:S(2)}) collective-permute-start(bf16[256,256]{1,0:T(8,128)(2,1)S(1)} %get-tuple-element.32), channel_id=1, source_target_pairs={{0,1},{1,0},{2,3},{3,2},{16,17},{17,16},{18,19},{19,18},{4,5},{5,4... | collective-permute-start | bytes 393224 | tf_op jit(solution)/shard_map/ppermute | solution.py:240
  38.8 0.0 collective-permute-done.9.refs_2_
  38.9 1.8 %collective-permute-done.10.refs_3_ = bf16[256,256]{1,0:T(8,128)(2,1)S(1)} collective-permute-done((bf16[256,256]{1,0:T(8,128)(2,1)S(1)}, bf16[256,256]{1,0:T(8,128)(2,1)S(1)}, u32[]{:S(2)}, u32[]{:S(2)}) %collective-permute-start.10) | collective-permute-done | bytes 131104 | tf_op jit(solution)/shard_map/ppermute | solution.py:240
  40.6 0.0 collective-permute-done.11.refs_4_
  40.6 2.4 %collective-permute-done.12.refs_5_ = bf16[256,256]{1,0:T(8,128)(2,1)S(1)} collective-permute-done((bf16[256,256]{1,0:T(8,128)(2,1)S(1)}, bf16[256,256]{1,0:T(8,128)(2,1)S(1)}, u32[]{:S(2)}, u32[]{:S(2)}) %collective-permute-start.12) | collective-permute-done | bytes 131104 | tf_op jit(solution)/shard_map/ppermute | solution.py:240
  43.1 0.0 collective-permute-done.13.refs_6_
  43.1 1.1 %unpack.1 = (bf16[1,1,128,2048]{3,2,1,0:T(8,128)(2,1)}, bf16[1,1,128,2048]{3,2,1,0:T(8,128)(2,1)}) custom-call(bf16[256,256]{1,0:T(8,128)(2,1)S(1)} %collective-permute-done.7.refs_0_, bf16[256,256]{1,0:T(8,128)(2,1)S(1)} %collective-permute-done.8.refs_1_, bf16[256,256]{1,0:T(8,128)(2,1)S(1)} %collective-permute-done.9.refs_2_, ...), custom_call_target="tpu_custom_call" | custom-call | tf_op jit(solution)/shard_map/unpack/pallas_call | solution.py:285
Async XLA Ops:
  2.7 13.1 %collective-permute-start = (bf16[272,256]{1,0:T(8,128)(2,1)S(1)}, bf16[272,256]{1,0:T(8,128)(2,1)S(1)}, u32[]{:S(2)}, u32[]{:S(2)}) collective-permute-start(bf16[272,256]{1,0:T(8,128)(2,1)S(1)} %get-tuple-element.18), channel_id=1, source_target_pairs={{0,16},{1,17},{2,18},{3,19},{16,0},{17,1},{18,2},{19,3},{4,20},{5,... | collective-permute-start | bytes 417800 | tf_op jit(solution)/shard_map/ppermute | solution.py:240
  5.8 10.1 %collective-permute-start.1 = (bf16[272,256]{1,0:T(8,128)(2,1)S(1)}, bf16[272,256]{1,0:T(8,128)(2,1)S(1)}, u32[]{:S(2)}, u32[]{:S(2)}) collective-permute-start(bf16[272,256]{1,0:T(8,128)(2,1)S(1)} %get-tuple-element.19), channel_id=1, source_target_pairs={{0,18},{1,19},{2,16},{3,17},{16,2},{17,3},{18,0},{19,1},{4,22},{5,... | collective-permute-start | bytes 417800 | tf_op jit(solution)/shard_map/ppermute | solution.py:240
  7.2 11.4 %collective-permute-start.2 = (bf16[272,256]{1,0:T(8,128)(2,1)S(1)}, bf16[272,256]{1,0:T(8,128)(2,1)S(1)}, u32[]{:S(2)}, u32[]{:S(2)}) collective-permute-start(bf16[272,256]{1,0:T(8,128)(2,1)S(1)} %get-tuple-element.20), channel_id=1, source_target_pairs={{0,19},{1,18},{2,17},{3,16},{16,3},{17,2},{18,1},{19,0},{4,23},{5,... | collective-permute-start | bytes 417800 | tf_op jit(solution)/shard_map/ppermute | solution.py:240
  7.6 11.0 %collective-permute-start.3 = (bf16[272,256]{1,0:T(8,128)(2,1)S(1)}, bf16[272,256]{1,0:T(8,128)(2,1)S(1)}, u32[]{:S(2)}, u32[]{:S(2)}) collective-permute-start(bf16[272,256]{1,0:T(8,128)(2,1)S(1)} %get-tuple-element.21), channel_id=1, source_target_pairs={{0,17},{1,16},{2,19},{3,18},{16,1},{17,0},{18,3},{19,2},{4,21},{5,... | collective-permute-start | bytes 417800 | tf_op jit(solution)/shard_map/ppermute | solution.py:240
  8.5 10.1 %collective-permute-start.4 = (bf16[272,256]{1,0:T(8,128)(2,1)S(1)}, bf16[272,256]{1,0:T(8,128)(2,1)S(1)}, u32[]{:S(2)}, u32[]{:S(2)}) collective-permute-start(bf16[272,256]{1,0:T(8,128)(2,1)S(1)} %get-tuple-element.22), channel_id=1, source_target_pairs={{0,2},{1,3},{2,0},{3,1},{16,18},{17,19},{18,16},{19,17},{4,6},{5,7... | collective-permute-start | bytes 417800 | tf_op jit(solution)/shard_map/ppermute | solution.py:240
  15.8 5.6 %collective-permute-start.5 = (bf16[272,256]{1,0:T(8,128)(2,1)S(1)}, bf16[272,256]{1,0:T(8,128)(2,1)S(1)}, u32[]{:S(2)}, u32[]{:S(2)}) collective-permute-start(bf16[272,256]{1,0:T(8,128)(2,1)S(1)} %get-tuple-element.23), channel_id=1, source_target_pairs={{0,3},{1,2},{2,1},{3,0},{16,19},{17,18},{18,17},{19,16},{4,7},{5,6... | collective-permute-start | bytes 417800 | tf_op jit(solution)/shard_map/ppermute | solution.py:240
  15.9 5.5 %collective-permute-start.6 = (bf16[272,256]{1,0:T(8,128)(2,1)S(1)}, bf16[272,256]{1,0:T(8,128)(2,1)S(1)}, u32[]{:S(2)}, u32[]{:S(2)}) collective-permute-start(bf16[272,256]{1,0:T(8,128)(2,1)S(1)} %get-tuple-element.24), channel_id=1, source_target_pairs={{0,1},{1,0},{2,3},{3,2},{16,17},{17,16},{18,19},{19,18},{4,5},{5,4... | collective-permute-start | bytes 417800 | tf_op jit(solution)/shard_map/ppermute | solution.py:240
  25.9 12.3 %collective-permute-start.7 = (bf16[256,256]{1,0:T(8,128)(2,1)S(1)}, bf16[256,256]{1,0:T(8,128)(2,1)S(1)}, u32[]{:S(2)}, u32[]{:S(2)}) collective-permute-start(bf16[256,256]{1,0:T(8,128)(2,1)S(1)} %get-tuple-element.26), channel_id=1, source_target_pairs={{0,16},{1,17},{2,18},{3,19},{16,0},{17,1},{18,2},{19,3},{4,20},{5,... | collective-permute-start | bytes 393224 | tf_op jit(solution)/shard_map/ppermute | solution.py:240
  28.7 9.5 %collective-permute-start.8 = (bf16[256,256]{1,0:T(8,128)(2,1)S(1)}, bf16[256,256]{1,0:T(8,128)(2,1)S(1)}, u32[]{:S(2)}, u32[]{:S(2)}) collective-permute-start(bf16[256,256]{1,0:T(8,128)(2,1)S(1)} %get-tuple-element.27), channel_id=1, source_target_pairs={{0,18},{1,19},{2,16},{3,17},{16,2},{17,3},{18,0},{19,1},{4,22},{5,... | collective-permute-start | bytes 393224 | tf_op jit(solution)/shard_map/ppermute | solution.py:240
  28.9 10.0 %collective-permute-start.9 = (bf16[256,256]{1,0:T(8,128)(2,1)S(1)}, bf16[256,256]{1,0:T(8,128)(2,1)S(1)}, u32[]{:S(2)}, u32[]{:S(2)}) collective-permute-start(bf16[256,256]{1,0:T(8,128)(2,1)S(1)} %get-tuple-element.28), channel_id=1, source_target_pairs={{0,19},{1,18},{2,17},{3,16},{16,3},{17,2},{18,1},{19,0},{4,23},{5,... | collective-permute-start | bytes 393224 | tf_op jit(solution)/shard_map/ppermute | solution.py:240
  30.8 9.8 %collective-permute-start.10 = (bf16[256,256]{1,0:T(8,128)(2,1)S(1)}, bf16[256,256]{1,0:T(8,128)(2,1)S(1)}, u32[]{:S(2)}, u32[]{:S(2)}) collective-permute-start(bf16[256,256]{1,0:T(8,128)(2,1)S(1)} %get-tuple-element.29), channel_id=1, source_target_pairs={{0,17},{1,16},{2,19},{3,18},{16,1},{17,0},{18,3},{19,2},{4,21},{5,... | collective-permute-start | bytes 393224 | tf_op jit(solution)/shard_map/ppermute | solution.py:240
  31.4 9.2 %collective-permute-start.11 = (bf16[256,256]{1,0:T(8,128)(2,1)S(1)}, bf16[256,256]{1,0:T(8,128)(2,1)S(1)}, u32[]{:S(2)}, u32[]{:S(2)}) collective-permute-start(bf16[256,256]{1,0:T(8,128)(2,1)S(1)} %get-tuple-element.30), channel_id=1, source_target_pairs={{0,2},{1,3},{2,0},{3,1},{16,18},{17,19},{18,16},{19,17},{4,6},{5,7... | collective-permute-start | bytes 393224 | tf_op jit(solution)/shard_map/ppermute | solution.py:240
  38.2 4.9 %collective-permute-start.12 = (bf16[256,256]{1,0:T(8,128)(2,1)S(1)}, bf16[256,256]{1,0:T(8,128)(2,1)S(1)}, u32[]{:S(2)}, u32[]{:S(2)}) collective-permute-start(bf16[256,256]{1,0:T(8,128)(2,1)S(1)} %get-tuple-element.31), channel_id=1, source_target_pairs={{0,3},{1,2},{2,1},{3,0},{16,19},{17,18},{18,17},{19,16},{4,7},{5,6... | collective-permute-start | bytes 393224 | tf_op jit(solution)/shard_map/ppermute | solution.py:240
  38.2 4.9 %collective-permute-start.13 = (bf16[256,256]{1,0:T(8,128)(2,1)S(1)}, bf16[256,256]{1,0:T(8,128)(2,1)S(1)}, u32[]{:S(2)}, u32[]{:S(2)}) collective-permute-start(bf16[256,256]{1,0:T(8,128)(2,1)S(1)} %get-tuple-element.32), channel_id=1, source_target_pairs={{0,1},{1,0},{2,3},{3,2},{16,17},{17,16},{18,19},{19,18},{4,5},{5,4... | collective-permute-start | bytes 393224 | tf_op jit(solution)/shard_map/ppermute | solution.py:240

commit v5 on v4

--- a/solution.py
+++ b/solution.py
@@ -234,12 +234,18 @@
         copy.wait()
 
 
-def swapped(shares, order):
+def swapped(shares, order, after):
     parts = len(order)
-    return [
-        lax.ppermute(share, AXES, [(dev, dev ^ step) for dev in range(parts)]) if step else share
-        for step, share in zip(order, shares)
-    ]
+    held = dict(zip(order, shares))
+    moved = {0: held[0]}
+    for step in order:
+        if step:
+            share = held[step]
+            if step in after:
+                earlier = after[step]
+                share, moved[earlier] = lax.optimization_barrier((share, moved[earlier]))
+            moved[step] = lax.ppermute(share, AXES, [(dev, dev ^ step) for dev in range(parts)])
+    return [moved[step] for step in order]
 
 
 def by_pairs(first_rows, second_rows, alignment, diffusion_mask, source_length, target_length):
@@ -249,9 +255,9 @@
     share = width // parts
     kind = first_rows.dtype
     params = pltpu.CompilerParams(vmem_limit_bytes=VMEM_LIMIT)
-    far = [step for step in range(seq_count, parts) if step & 2]
-    near = [step for step in range(seq_count, parts) if not step & 2]
-    order = near[:1] + far + near[1:] + list(range(2, seq_count)) + [1, 0]
+    order, after = list(range(parts - 1, -1, -1)), {}
+    if parts == 8:
+        order, after = [6, 7, 4, 1, 2, 5, 3, 0], {5: 1, 3: 2}
     sems = pltpu.SemaphoreType.DMA((2, parts))
     shares = pl.pallas_call(
         functools.partial(pack_kernel, seq_count, order),
@@ -267,7 +273,7 @@
         compiler_params=params,
         name="pack",
     )(target_length, *in_hbm(alignment, diffusion_mask, first_rows, second_rows))
-    shares = swapped(shares, order)
+    shares = swapped(shares, order, after)
     rows = pltpu.VMEM((parts, 2, BLK, share), kind)
     grads = pltpu.VMEM((seq_count, BLK, share), jnp.float32)
     shares = pl.pallas_call(
@@ -280,7 +286,7 @@
         cost_estimate=attend_cost(seq_count, share),
         name="attend",
     )(source_length, target_length, *shares)
-    shares = swapped(shares, order)
+    shares = swapped(shares, order, after)
     out_shape = jax.ShapeDtypeStruct((1, 1, BLK, width), kind)
     return pl.pallas_call(
         functools.partial(unpack_kernel, seq_count, order),

time: 44.4 us -> 45.8 us (1.032)
  waiting for transfers between devices: 18.6 us -> 23.3 us
  starting transfers between devices: 16.5 us -> 13.3 us
    ppermute x14, waiting for transfers between devices: 18.6 us -> 23.3 us  [swapped(): lax.ppermute(share, AXES, [(dev, dev ^ step) for dev in range(parts)])]
    ppermute x14, starting transfers between devices: 16.5 us -> 13.3 us  [swapped(): lax.ppermute(share, AXES, [(dev, dev ^ step) for dev in range(parts)])]
  transfers between devices with their start and end apart: 14 -> 14, of which waited for: 5 -> 10; matrix products, arithmetic and copies ran while one was open for 0% -> 0% of each run, Pallas kernels for 0% -> 0%
where the time goes in v5:
time: 45.8 us; the launch traced here: 45.6 us
  waiting for transfers between devices  23.3 us (51%)
  starting transfers between devices  13.3 us (29%)
  Pallas kernels  7.05 us (15%)
  between operations  1.96 us (4%)
    ppermute x14, waiting for transfers between devices, swapped(): lax.ppermute(share, AXES, [(dev, dev ^ step) for dev in range(parts)])  23.3 us
    ppermute x14, starting transfers between devices, swapped(): lax.ppermute(share, AXES, [(dev, dev ^ step) for dev in range(parts)])  13.3 us
    pallas_call x1, Pallas kernels, by_pairs(): pl.pallas_call(functools.partial(attend_kernel, seq_count, order), out_sh...  4.53 us
    pallas_call x1, Pallas kernels, by_pairs(): pl.pallas_call(functools.partial(pack_kernel, seq_count, order), out_shap...  1.43 us
    pallas_call x1, Pallas kernels, by_pairs(): pl.pallas_call(functools.partial(unpack_kernel, seq_count, order), out_sh...  1.09 us
  transfers between devices with their start and end apart: 14, of which 10 were waited for; matrix products, arithmetic and copies ran while one was open for 0% of the time, Pallas kernels for 0%

profile of v5, /device:TPU:0, one launch (start us, length us, event | category | flops | bytes accessed | tf_op | source)
XLA Modules:
  0.0 45.6 jit_solution(14527395299009181358)
XLA Ops:
  1.3 1.4 %pack.1 = (bf16[272,256]{1,0:T(8,128)(2,1)S(1)}, bf16[272,256]{1,0:T(8,128)(2,1)S(1)}, bf16[272,256]{1,0:T(8,128)(2,1)S(1)}, bf16[272,256]{1,0:T(8,128)(2,1)S(1)...) custom-call(s32[1]{0:T(128)S(6)} %copy.9.refs_0_.target_len, ...), custom_call_target="tpu_custom_call" | custom-call | tf_op jit(solution)/shard_map/pack/pallas_call | solution.py:262
  2.7 0.5 %collective-permute-start.3 = (bf16[272,256]{1,0:T(8,128)(2,1)S(1)}, bf16[272,256]{1,0:T(8,128)(2,1)S(1)}, u32[]{:S(2)}, u32[]{:S(2)}) collective-permute-start(bf16[272,256]{1,0:T(8,128)(2,1)S(1)} %get-tuple-element.30), channel_id=1, source_target_pairs={{0,1},{1,0},{2,3},{3,2},{16,17},{17,16},{18,19},{19,18},{4,5},{5,4... | collective-permute-start | bytes 417800 | tf_op jit(solution)/shard_map/ppermute | solution.py:247
  3.2 2.6 %collective-permute-start.4 = (bf16[272,256]{1,0:T(8,128)(2,1)S(1)}, bf16[272,256]{1,0:T(8,128)(2,1)S(1)}, u32[]{:S(2)}, u32[]{:S(2)}) collective-permute-start(bf16[272,256]{1,0:T(8,128)(2,1)S(1)} %get-tuple-element.33), channel_id=1, source_target_pairs={{0,2},{1,3},{2,0},{3,1},{16,18},{17,19},{18,16},{19,17},{4,6},{5,7... | collective-permute-start | bytes 417800 | tf_op jit(solution)/shard_map/ppermute | solution.py:247
  5.8 1.5 %collective-permute-start = (bf16[272,256]{1,0:T(8,128)(2,1)S(1)}, bf16[272,256]{1,0:T(8,128)(2,1)S(1)}, u32[]{:S(2)}, u32[]{:S(2)}) collective-permute-start(bf16[272,256]{1,0:T(8,128)(2,1)S(1)} %get-tuple-element.26), channel_id=1, source_target_pairs={{0,18},{1,19},{2,16},{3,17},{16,2},{17,3},{18,0},{19,1},{4,22},{5,... | collective-permute-start | bytes 417800 | tf_op jit(solution)/shard_map/ppermute | solution.py:247
  7.3 0.9 %collective-permute-start.1 = (bf16[272,256]{1,0:T(8,128)(2,1)S(1)}, bf16[272,256]{1,0:T(8,128)(2,1)S(1)}, u32[]{:S(2)}, u32[]{:S(2)}) collective-permute-start(bf16[272,256]{1,0:T(8,128)(2,1)S(1)} %get-tuple-element.27), channel_id=1, source_target_pairs={{0,19},{1,18},{2,17},{3,16},{16,3},{17,2},{18,1},{19,0},{4,23},{5,... | collective-permute-start | bytes 417800 | tf_op jit(solution)/shard_map/ppermute | solution.py:247
  8.2 1.5 %collective-permute-start.2 = (bf16[272,256]{1,0:T(8,128)(2,1)S(1)}, bf16[272,256]{1,0:T(8,128)(2,1)S(1)}, u32[]{:S(2)}, u32[]{:S(2)}) collective-permute-start(bf16[272,256]{1,0:T(8,128)(2,1)S(1)} %get-tuple-element.28), channel_id=1, source_target_pairs={{0,16},{1,17},{2,18},{3,19},{16,0},{17,1},{18,2},{19,3},{4,20},{5,... | collective-permute-start | bytes 417800 | tf_op jit(solution)/shard_map/ppermute | solution.py:247
  9.7 0.0 collective-permute-done.3.refs_3_
  9.7 0.5 collective-permute-start.5
  10.2 0.1 collective-permute-done.4.refs_4_
  10.3 0.8 %collective-permute-start.6 = (bf16[272,256]{1,0:T(8,128)(2,1)S(1)}, bf16[272,256]{1,0:T(8,128)(2,1)S(1)}, u32[]{:S(2)}, u32[]{:S(2)}) collective-permute-start(bf16[272,256]{1,0:T(8,128)(2,1)S(1)} %get-tuple-element.36), channel_id=1, source_target_pairs={{0,3},{1,2},{2,1},{3,0},{16,19},{17,18},{18,17},{19,16},{4,7},{5,6... | collective-permute-start | bytes 417800 | tf_op jit(solution)/shard_map/ppermute | solution.py:247
  11.7 3.1 %collective-permute-done.refs_0_ = bf16[272,256]{1,0:T(8,128)(2,1)S(1)} collective-permute-done((bf16[272,256]{1,0:T(8,128)(2,1)S(1)}, bf16[272,256]{1,0:T(8,128)(2,1)S(1)}, u32[]{:S(2)}, u32[]{:S(2)}) %collective-permute-start) | collective-permute-done | bytes 139296 | tf_op jit(solution)/shard_map/ppermute | solution.py:247
  14.8 2.1 %collective-permute-done.1.refs_1_ = bf16[272,256]{1,0:T(8,128)(2,1)S(1)} collective-permute-done((bf16[272,256]{1,0:T(8,128)(2,1)S(1)}, bf16[272,256]{1,0:T(8,128)(2,1)S(1)}, u32[]{:S(2)}, u32[]{:S(2)}) %collective-permute-start.1) | collective-permute-done | bytes 139296 | tf_op jit(solution)/shard_map/ppermute | solution.py:247
  16.9 3.4 %collective-permute-done.2.refs_2_ = bf16[272,256]{1,0:T(8,128)(2,1)S(1)} collective-permute-done((bf16[272,256]{1,0:T(8,128)(2,1)S(1)}, bf16[272,256]{1,0:T(8,128)(2,1)S(1)}, u32[]{:S(2)}, u32[]{:S(2)}) %collective-permute-start.2) | collective-permute-done | bytes 139296 | tf_op jit(solution)/shard_map/ppermute | solution.py:247
  20.3 2.6 %collective-permute-done.5.refs_5_ = bf16[272,256]{1,0:T(8,128)(2,1)S(1)} collective-permute-done((bf16[272,256]{1,0:T(8,128)(2,1)S(1)}, bf16[272,256]{1,0:T(8,128)(2,1)S(1)}, u32[]{:S(2)}, u32[]{:S(2)}) %collective-permute-start.5) | collective-permute-done | bytes 139296 | tf_op jit(solution)/shard_map/ppermute | solution.py:247
  22.9 0.0 collective-permute-done.6.refs_6_
  22.9 4.5 %attend.1 = (bf16[256,256]{1,0:T(8,128)(2,1)S(1)}, bf16[256,256]{1,0:T(8,128)(2,1)S(1)}, bf16[256,256]{1,0:T(8,128)(2,1)S(1)}, bf16[256,256]{1,0:T(8,128)(2,1)S(...) custom-call(s32[1]{0:T(128)S(6)} %copy.8.source_len, ...), custom_call_target="tpu_custom_call" | custom-call | flops 335544320 | bytes 2097152 | tf_op jit(solution)/shard_map/attend/pallas_call | solution.py:279
  27.4 0.2 collective-permute-start.10
  27.6 0.5 %collective-permute-start.11 = (bf16[256,256]{1,0:T(8,128)(2,1)S(1)}, bf16[256,256]{1,0:T(8,128)(2,1)S(1)}, u32[]{:S(2)}, u32[]{:S(2)}) collective-permute-start(bf16[256,256]{1,0:T(8,128)(2,1)S(1)} %get-tuple-element.45), channel_id=1, source_target_pairs={{0,2},{1,3},{2,0},{3,1},{16,18},{17,19},{18,16},{19,17},{4,6},{5,7... | collective-permute-start | bytes 393224 | tf_op jit(solution)/shard_map/ppermute | solution.py:247
  28.1 1.5 %collective-permute-start.7 = (bf16[256,256]{1,0:T(8,128)(2,1)S(1)}, bf16[256,256]{1,0:T(8,128)(2,1)S(1)}, u32[]{:S(2)}, u32[]{:S(2)}) collective-permute-start(bf16[256,256]{1,0:T(8,128)(2,1)S(1)} %get-tuple-element.38), channel_id=1, source_target_pairs={{0,18},{1,19},{2,16},{3,17},{16,2},{17,3},{18,0},{19,1},{4,22},{5,... | collective-permute-start | bytes 393224 | tf_op jit(solution)/shard_map/ppermute | solution.py:247
  29.6 0.6 %collective-permute-start.8 = (bf16[256,256]{1,0:T(8,128)(2,1)S(1)}, bf16[256,256]{1,0:T(8,128)(2,1)S(1)}, u32[]{:S(2)}, u32[]{:S(2)}) collective-permute-start(bf16[256,256]{1,0:T(8,128)(2,1)S(1)} %get-tuple-element.39), channel_id=1, source_target_pairs={{0,19},{1,18},{2,17},{3,16},{16,3},{17,2},{18,1},{19,0},{4,23},{5,... | collective-permute-start | bytes 393224 | tf_op jit(solution)/shard_map/ppermute | solution.py:247
  30.3 1.7 %collective-permute-start.9 = (bf16[256,256]{1,0:T(8,128)(2,1)S(1)}, bf16[256,256]{1,0:T(8,128)(2,1)S(1)}, u32[]{:S(2)}, u32[]{:S(2)}) collective-permute-start(bf16[256,256]{1,0:T(8,128)(2,1)S(1)} %get-tuple-element.40), channel_id=1, source_target_pairs={{0,16},{1,17},{2,18},{3,19},{16,0},{17,1},{18,2},{19,3},{4,20},{5,... | collective-permute-start | bytes 393224 | tf_op jit(solution)/shard_map/ppermute | solution.py:247
  32.0 0.0 collective-permute-done.10.refs_3_
  32.0 0.5 %collective-permute-start.12 = (bf16[256,256]{1,0:T(8,128)(2,1)S(1)}, bf16[256,256]{1,0:T(8,128)(2,1)S(1)}, u32[]{:S(2)}, u32[]{:S(2)}) collective-permute-start(bf16[256,256]{1,0:T(8,128)(2,1)S(1)} %get-tuple-element.47), channel_id=1, source_target_pairs={{0,17},{1,16},{2,19},{3,18},{16,1},{17,0},{18,3},{19,2},{4,21},{5,... | collective-permute-start | bytes 393224 | tf_op jit(solution)/shard_map/ppermute | solution.py:247
  32.5 1.4 %collective-permute-done.11.refs_4_ = bf16[256,256]{1,0:T(8,128)(2,1)S(1)} collective-permute-done((bf16[256,256]{1,0:T(8,128)(2,1)S(1)}, bf16[256,256]{1,0:T(8,128)(2,1)S(1)}, u32[]{:S(2)}, u32[]{:S(2)}) %collective-permute-start.11) | collective-permute-done | bytes 131104 | tf_op jit(solution)/shard_map/ppermute | solution.py:247
  33.9 0.0 collective-permute-start.13
  33.9 2.9 %collective-permute-done.7.refs_0_ = bf16[256,256]{1,0:T(8,128)(2,1)S(1)} collective-permute-done((bf16[256,256]{1,0:T(8,128)(2,1)S(1)}, bf16[256,256]{1,0:T(8,128)(2,1)S(1)}, u32[]{:S(2)}, u32[]{:S(2)}) %collective-permute-start.7) | collective-permute-done | bytes 131104 | tf_op jit(solution)/shard_map/ppermute | solution.py:247
  36.8 1.9 %collective-permute-done.8.refs_1_ = bf16[256,256]{1,0:T(8,128)(2,1)S(1)} collective-permute-done((bf16[256,256]{1,0:T(8,128)(2,1)S(1)}, bf16[256,256]{1,0:T(8,128)(2,1)S(1)}, u32[]{:S(2)}, u32[]{:S(2)}) %collective-permute-start.8) | collective-permute-done | bytes 131104 | tf_op jit(solution)/shard_map/ppermute | solution.py:247
  38.7 3.1 %collective-permute-done.9.refs_2_ = bf16[256,256]{1,0:T(8,128)(2,1)S(1)} collective-permute-done((bf16[256,256]{1,0:T(8,128)(2,1)S(1)}, bf16[256,256]{1,0:T(8,128)(2,1)S(1)}, u32[]{:S(2)}, u32[]{:S(2)}) %collective-permute-start.9) | collective-permute-done | bytes 131104 | tf_op jit(solution)/shard_map/ppermute | solution.py:247
  41.8 2.7 %collective-permute-done.12.refs_5_ = bf16[256,256]{1,0:T(8,128)(2,1)S(1)} collective-permute-done((bf16[256,256]{1,0:T(8,128)(2,1)S(1)}, bf16[256,256]{1,0:T(8,128)(2,1)S(1)}, u32[]{:S(2)}, u32[]{:S(2)}) %collective-permute-start.12) | collective-permute-done | bytes 131104 | tf_op jit(solution)/shard_map/ppermute | solution.py:247
  44.5 0.0 collective-permute-done.13.refs_6_
  44.5 1.1 %unpack.1 = (bf16[1,1,128,2048]{3,2,1,0:T(8,128)(2,1)}, bf16[1,1,128,2048]{3,2,1,0:T(8,128)(2,1)}) custom-call(bf16[256,256]{1,0:T(8,128)(2,1)S(1)} %collective-permute-done.7.refs_0_, bf16[256,256]{1,0:T(8,128)(2,1)S(1)} %collective-permute-done.8.refs_1_, bf16[256,256]{1,0:T(8,128)(2,1)S(1)} %collective-permute-done.9.refs_2_, ...), custom_call_target="tpu_custom_call" | custom-call | tf_op jit(solution)/shard_map/unpack/pallas_call | solution.py:291
Async XLA Ops:
  2.7 7.0 %collective-permute-start.3 = (bf16[272,256]{1,0:T(8,128)(2,1)S(1)}, bf16[272,256]{1,0:T(8,128)(2,1)S(1)}, u32[]{:S(2)}, u32[]{:S(2)}) collective-permute-start(bf16[272,256]{1,0:T(8,128)(2,1)S(1)} %get-tuple-element.30), channel_id=1, source_target_pairs={{0,1},{1,0},{2,3},{3,2},{16,17},{17,16},{18,19},{19,18},{4,5},{5,4... | collective-permute-start | bytes 417800 | tf_op jit(solution)/shard_map/ppermute | solution.py:247
  3.2 7.1 %collective-permute-start.4 = (bf16[272,256]{1,0:T(8,128)(2,1)S(1)}, bf16[272,256]{1,0:T(8,128)(2,1)S(1)}, u32[]{:S(2)}, u32[]{:S(2)}) collective-permute-start(bf16[272,256]{1,0:T(8,128)(2,1)S(1)} %get-tuple-element.33), channel_id=1, source_target_pairs={{0,2},{1,3},{2,0},{3,1},{16,18},{17,19},{18,16},{19,17},{4,6},{5,7... | collective-permute-start | bytes 417800 | tf_op jit(solution)/shard_map/ppermute | solution.py:247
  5.8 9.0 %collective-permute-start = (bf16[272,256]{1,0:T(8,128)(2,1)S(1)}, bf16[272,256]{1,0:T(8,128)(2,1)S(1)}, u32[]{:S(2)}, u32[]{:S(2)}) collective-permute-start(bf16[272,256]{1,0:T(8,128)(2,1)S(1)} %get-tuple-element.26), channel_id=1, source_target_pairs={{0,18},{1,19},{2,16},{3,17},{16,2},{17,3},{18,0},{19,1},{4,22},{5,... | collective-permute-start | bytes 417800 | tf_op jit(solution)/shard_map/ppermute | solution.py:247
  7.3 9.6 %collective-permute-start.1 = (bf16[272,256]{1,0:T(8,128)(2,1)S(1)}, bf16[272,256]{1,0:T(8,128)(2,1)S(1)}, u32[]{:S(2)}, u32[]{:S(2)}) collective-permute-start(bf16[272,256]{1,0:T(8,128)(2,1)S(1)} %get-tuple-element.27), channel_id=1, source_target_pairs={{0,19},{1,18},{2,17},{3,16},{16,3},{17,2},{18,1},{19,0},{4,23},{5,... | collective-permute-start | bytes 417800 | tf_op jit(solution)/shard_map/ppermute | solution.py:247
  8.2 12.1 %collective-permute-start.2 = (bf16[272,256]{1,0:T(8,128)(2,1)S(1)}, bf16[272,256]{1,0:T(8,128)(2,1)S(1)}, u32[]{:S(2)}, u32[]{:S(2)}) collective-permute-start(bf16[272,256]{1,0:T(8,128)(2,1)S(1)} %get-tuple-element.28), channel_id=1, source_target_pairs={{0,16},{1,17},{2,18},{3,19},{16,0},{17,1},{18,2},{19,3},{4,20},{5,... | collective-permute-start | bytes 417800 | tf_op jit(solution)/shard_map/ppermute | solution.py:247
  9.7 13.1 %collective-permute-start.5 = (bf16[272,256]{1,0:T(8,128)(2,1)S(1)}, bf16[272,256]{1,0:T(8,128)(2,1)S(1)}, u32[]{:S(2)}, u32[]{:S(2)}) collective-permute-start(bf16[272,256]{1,0:T(8,128)(2,1)S(1)} %get-tuple-element.35), channel_id=1, source_target_pairs={{0,17},{1,16},{2,19},{3,18},{16,1},{17,0},{18,3},{19,2},{4,21},{5,... | collective-permute-start | bytes 417800 | tf_op jit(solution)/shard_map/ppermute | solution.py:247
  10.3 12.6 %collective-permute-start.6 = (bf16[272,256]{1,0:T(8,128)(2,1)S(1)}, bf16[272,256]{1,0:T(8,128)(2,1)S(1)}, u32[]{:S(2)}, u32[]{:S(2)}) collective-permute-start(bf16[272,256]{1,0:T(8,128)(2,1)S(1)} %get-tuple-element.36), channel_id=1, source_target_pairs={{0,3},{1,2},{2,1},{3,0},{16,19},{17,18},{18,17},{19,16},{4,7},{5,6... | collective-permute-start | bytes 417800 | tf_op jit(solution)/shard_map/ppermute | solution.py:247
  27.4 4.5 %collective-permute-start.10 = (bf16[256,256]{1,0:T(8,128)(2,1)S(1)}, bf16[256,256]{1,0:T(8,128)(2,1)S(1)}, u32[]{:S(2)}, u32[]{:S(2)}) collective-permute-start(bf16[256,256]{1,0:T(8,128)(2,1)S(1)} %get-tuple-element.42), channel_id=1, source_target_pairs={{0,1},{1,0},{2,3},{3,2},{16,17},{17,16},{18,19},{19,18},{4,5},{5,4... | collective-permute-start | bytes 393224 | tf_op jit(solution)/shard_map/ppermute | solution.py:247
  27.6 6.3 %collective-permute-start.11 = (bf16[256,256]{1,0:T(8,128)(2,1)S(1)}, bf16[256,256]{1,0:T(8,128)(2,1)S(1)}, u32[]{:S(2)}, u32[]{:S(2)}) collective-permute-start(bf16[256,256]{1,0:T(8,128)(2,1)S(1)} %get-tuple-element.45), channel_id=1, source_target_pairs={{0,2},{1,3},{2,0},{3,1},{16,18},{17,19},{18,16},{19,17},{4,6},{5,7... | collective-permute-start | bytes 393224 | tf_op jit(solution)/shard_map/ppermute | solution.py:247
  28.1 8.7 %collective-permute-start.7 = (bf16[256,256]{1,0:T(8,128)(2,1)S(1)}, bf16[256,256]{1,0:T(8,128)(2,1)S(1)}, u32[]{:S(2)}, u32[]{:S(2)}) collective-permute-start(bf16[256,256]{1,0:T(8,128)(2,1)S(1)} %get-tuple-element.38), channel_id=1, source_target_pairs={{0,18},{1,19},{2,16},{3,17},{16,2},{17,3},{18,0},{19,1},{4,22},{5,... | collective-permute-start | bytes 393224 | tf_op jit(solution)/shard_map/ppermute | solution.py:247
  29.6 9.0 %collective-permute-start.8 = (bf16[256,256]{1,0:T(8,128)(2,1)S(1)}, bf16[256,256]{1,0:T(8,128)(2,1)S(1)}, u32[]{:S(2)}, u32[]{:S(2)}) collective-permute-start(bf16[256,256]{1,0:T(8,128)(2,1)S(1)} %get-tuple-element.39), channel_id=1, source_target_pairs={{0,19},{1,18},{2,17},{3,16},{16,3},{17,2},{18,1},{19,0},{4,23},{5,... | collective-permute-start | bytes 393224 | tf_op jit(solution)/shard_map/ppermute | solution.py:247
  30.3 11.5 %collective-permute-start.9 = (bf16[256,256]{1,0:T(8,128)(2,1)S(1)}, bf16[256,256]{1,0:T(8,128)(2,1)S(1)}, u32[]{:S(2)}, u32[]{:S(2)}) collective-permute-start(bf16[256,256]{1,0:T(8,128)(2,1)S(1)} %get-tuple-element.40), channel_id=1, source_target_pairs={{0,16},{1,17},{2,18},{3,19},{16,0},{17,1},{18,2},{19,3},{4,20},{5,... | collective-permute-start | bytes 393224 | tf_op jit(solution)/shard_map/ppermute | solution.py:247
  32.0 12.6 %collective-permute-start.12 = (bf16[256,256]{1,0:T(8,128)(2,1)S(1)}, bf16[256,256]{1,0:T(8,128)(2,1)S(1)}, u32[]{:S(2)}, u32[]{:S(2)}) collective-permute-start(bf16[256,256]{1,0:T(8,128)(2,1)S(1)} %get-tuple-element.47), channel_id=1, source_target_pairs={{0,17},{1,16},{2,19},{3,18},{16,1},{17,0},{18,3},{19,2},{4,21},{5,... | collective-permute-start | bytes 393224 | tf_op jit(solution)/shard_map/ppermute | solution.py:247
  33.9 10.6 %collective-permute-start.13 = (bf16[256,256]{1,0:T(8,128)(2,1)S(1)}, bf16[256,256]{1,0:T(8,128)(2,1)S(1)}, u32[]{:S(2)}, u32[]{:S(2)}) collective-permute-start(bf16[256,256]{1,0:T(8,128)(2,1)S(1)} %get-tuple-element.48), channel_id=1, source_target_pairs={{0,3},{1,2},{2,1},{3,0},{16,19},{17,18},{18,17},{19,16},{4,7},{5,6... | collective-permute-start | bytes 393224 | tf_op jit(solution)/shard_map/ppermute | solution.py:247

commit v6 on v5

--- a/solution.py
+++ b/solution.py
@@ -57,6 +57,7 @@
             queries = rows[seq_count + target, 0, target_rows, lanes] * jnp.bfloat16(SCALE)
             cots = rows[seq_count + target, 1, target_rows, lanes]
             none = jnp.zeros_like(queries)
+            cots = jnp.where(live, cots, none)
             queries = jnp.concatenate(
                 [jnp.where(lane_head == head, queries, none) for head in range(heads)], axis=0
             )
@@ -87,7 +88,7 @@
                 value_grad[dev, here, lanes] += dvalue[part]
         return carry
 
-    lax.fori_loop(0, block_count, step, 0)
+    lax.fori_loop(0, block_count, step, 0, unroll=block_count <= 4)
     out[:seq_count, 0] = key_grad[...].astype(jnp.bfloat16)
     out[:seq_count, 1] = value_grad[...].astype(jnp.bfloat16)
 
@@ -124,8 +125,7 @@
     rows_here = first_rows.shape[2]
     width = first_rows.shape[3]
     on_encoder = lax.axis_index("section") == 0
-    row_pos = lax.axis_index("seq") * rows_here + jnp.arange(rows_here, dtype=jnp.int32)
-    keep = on_encoder | ((row_pos < target_length[0]) & (diffusion_mask[0] == 1))
+    keep = on_encoder | (diffusion_mask[0] == 1)
     second = jnp.where(keep[:, None], second_rows[0, 0], jnp.zeros_like(second_rows[0, 0]))
     held = jnp.stack([first_rows[0, 0], second])
     held = held.reshape(2, rows_here, parts, width // parts).transpose(2, 0, 1, 3)
@@ -152,8 +152,8 @@
 
 
 def pack_kernel(seq_count, order, *refs):
-    target_len, smalls, (first, second) = refs[0], refs[1:3], refs[3:5]
-    outs, (lists, mask, small_sem, sem) = refs[5:-4], refs[-4:]
+    smalls, (first, second) = refs[:2], refs[2:4]
+    outs, (lists, mask, small_sem, sem) = refs[4:-4], refs[-4:]
     small_copies = [
         pltpu.make_async_copy(source, held, small_sem.at[slot])
         for slot, (source, held) in enumerate(zip(smalls, (lists, mask)))
@@ -177,8 +177,7 @@
         copies.append(pair)
     for copy in small_copies:
         copy.wait()
-    positions = here * BLK + lax.broadcasted_iota(jnp.int32, (1, BLK), 1)
-    keep = ((positions < target_len[0]) & (mask[...] == 1)) | (me < seq_count)
+    keep = (mask[...] == 1) | (me < seq_count)
     keep = jnp.broadcast_to(jnp.where(keep, 1.0, 0.0), (BLK, BLK)).T.astype(jnp.bfloat16)
     keep = jnp.concatenate([keep] * (share // LANES), axis=1)
     base = here - WIN
@@ -257,12 +256,12 @@
     params = pltpu.CompilerParams(vmem_limit_bytes=VMEM_LIMIT)
     order, after = list(range(parts - 1, -1, -1)), {}
     if parts == 8:
-        order, after = [6, 7, 4, 1, 2, 5, 3, 0], {5: 1, 3: 2}
+        order = [6, 7, 4, 5, 2, 3, 1, 0]
     sems = pltpu.SemaphoreType.DMA((2, parts))
     shares = pl.pallas_call(
         functools.partial(pack_kernel, seq_count, order),
         out_shape=[jax.ShapeDtypeStruct((2 * BLK + TAIL, share), kind)] * parts,
-        in_specs=specs(1, pltpu.SMEM) + specs(4, pltpu.HBM),
+        in_specs=specs(4, pltpu.HBM),
         out_specs=specs(parts, pltpu.VMEM),
         scratch_shapes=[
             pltpu.SMEM(alignment.shape, jnp.int32),
@@ -272,7 +271,7 @@
         ],
         compiler_params=params,
         name="pack",
-    )(target_length, *in_hbm(alignment, diffusion_mask, first_rows, second_rows))
+    )(*in_hbm(alignment, diffusion_mask, first_rows, second_rows))
     shares = swapped(shares, order, after)
     rows = pltpu.VMEM((parts, 2, BLK, share), kind)
     grads = pltpu.VMEM((seq_count, BLK, share), jnp.float32)

time: 45.8 us -> 38.6 us (0.84)
  waiting for transfers between devices: 23.3 us -> 16 us
  starting transfers between devices: 13.3 us -> 14.1 us
  Pallas kernels: 7.05 us -> 6.27 us
    ppermute x14, waiting for transfers between devices: 23.3 us -> 16 us  [swapped(): lax.ppermute(share, AXES, [(dev, dev ^ step) for dev in range(parts)])]
    ppermute x14, starting transfers between devices: 13.3 us -> 14.1 us  [swapped(): lax.ppermute(share, AXES, [(dev, dev ^ step) for dev in range(parts)])]
    pallas_call x1, Pallas kernels: 4.53 us -> 3.74 us  [by_pairs(): pl.pallas_call(functools.partial(attend_kernel, seq_count, order), out_sh...]
  transfers between devices with their start and end apart: 14 -> 14, of which waited for: 10 -> 8; matrix products, arithmetic and copies ran while one was open for 0% -> 0% of each run, Pallas kernels for 0% -> 0%
where the time goes in v6:
time: 38.6 us; the launch traced here: 38.4 us
  waiting for transfers between devices  16 us (41%)
  starting transfers between devices  14.1 us (37%)
  Pallas kernels  6.27 us (16%)
  between operations  1.97 us (5%)
    ppermute x14, waiting for transfers between devices, swapped(): lax.ppermute(share, AXES, [(dev, dev ^ step) for dev in range(parts)])  16 us
    ppermute x14, starting transfers between devices, swapped(): lax.ppermute(share, AXES, [(dev, dev ^ step) for dev in range(parts)])  14.1 us
    pallas_call x1, Pallas kernels, by_pairs(): pl.pallas_call(functools.partial(attend_kernel, seq_count, order), out_sh...  3.74 us
    pallas_call x1, Pallas kernels, by_pairs(): pl.pallas_call(functools.partial(pack_kernel, seq_count, order), out_shap...  1.43 us
    pallas_call x1, Pallas kernels, by_pairs(): pl.pallas_call(functools.partial(unpack_kernel, seq_count, order), out_sh...  1.1 us
  transfers between devices with their start and end apart: 14, of which 8 were waited for; matrix products, arithmetic and copies ran while one was open for 0% of the time, Pallas kernels for 0%

profile of v6, /device:TPU:0, one launch (start us, length us, event | category | flops | bytes accessed | tf_op | source)
XLA Modules:
  0.0 38.4 jit_solution(15642089164469629838)
XLA Ops:
  0.6 1.4 %pack.1 = (bf16[272,256]{1,0:T(8,128)(2,1)S(1)}, bf16[272,256]{1,0:T(8,128)(2,1)S(1)}, bf16[272,256]{1,0:T(8,128)(2,1)S(1)}, bf16[272,256]{1,0:T(8,128)(2,1)S(1)...) custom-call(s32[1,1,2]{2,1,0:T(1,128)} %refs_0_.1, ...), custom_call_target="tpu_custom_call" | custom-call | tf_op jit(solution)/shard_map/pack/pallas_call | solution.py:261
  2.1 4.0 %collective-permute-start = (bf16[272,256]{1,0:T(8,128)(2,1)S(1)}, bf16[272,256]{1,0:T(8,128)(2,1)S(1)}, u32[]{:S(2)}, u32[]{:S(2)}) collective-permute-start(bf16[272,256]{1,0:T(8,128)(2,1)S(1)} %get-tuple-element.18), channel_id=1, source_target_pairs={{0,18},{1,19},{2,16},{3,17},{16,2},{17,3},{18,0},{19,1},{4,22},{5,... | collective-permute-start | bytes 417800 | tf_op jit(solution)/shard_map/ppermute | solution.py:246
  6.0 0.0 collective-permute-start.1
  6.0 1.2 %collective-permute-start.2 = (bf16[272,256]{1,0:T(8,128)(2,1)S(1)}, bf16[272,256]{1,0:T(8,128)(2,1)S(1)}, u32[]{:S(2)}, u32[]{:S(2)}) collective-permute-start(bf16[272,256]{1,0:T(8,128)(2,1)S(1)} %get-tuple-element.20), channel_id=1, source_target_pairs={{0,16},{1,17},{2,18},{3,19},{16,0},{17,1},{18,2},{19,3},{4,20},{5,... | collective-permute-start | bytes 417800 | tf_op jit(solution)/shard_map/ppermute | solution.py:246
  7.2 0.6 %collective-permute-start.3 = (bf16[272,256]{1,0:T(8,128)(2,1)S(1)}, bf16[272,256]{1,0:T(8,128)(2,1)S(1)}, u32[]{:S(2)}, u32[]{:S(2)}) collective-permute-start(bf16[272,256]{1,0:T(8,128)(2,1)S(1)} %get-tuple-element.21), channel_id=1, source_target_pairs={{0,17},{1,16},{2,19},{3,18},{16,1},{17,0},{18,3},{19,2},{4,21},{5,... | collective-permute-start | bytes 417800 | tf_op jit(solution)/shard_map/ppermute | solution.py:246
  7.8 1.7 %collective-permute-start.4 = (bf16[272,256]{1,0:T(8,128)(2,1)S(1)}, bf16[272,256]{1,0:T(8,128)(2,1)S(1)}, u32[]{:S(2)}, u32[]{:S(2)}) collective-permute-start(bf16[272,256]{1,0:T(8,128)(2,1)S(1)} %get-tuple-element.22), channel_id=1, source_target_pairs={{0,2},{1,3},{2,0},{3,1},{16,18},{17,19},{18,16},{19,17},{4,6},{5,7... | collective-permute-start | bytes 417800 | tf_op jit(solution)/shard_map/ppermute | solution.py:246
  9.5 0.7 %collective-permute-done.refs_0_ = bf16[272,256]{1,0:T(8,128)(2,1)S(1)} collective-permute-done((bf16[272,256]{1,0:T(8,128)(2,1)S(1)}, bf16[272,256]{1,0:T(8,128)(2,1)S(1)}, u32[]{:S(2)}, u32[]{:S(2)}) %collective-permute-start) | collective-permute-done | bytes 139296 | tf_op jit(solution)/shard_map/ppermute | solution.py:246
  10.1 0.0 collective-permute-start.5
  10.2 3.0 %collective-permute-done.1.refs_1_ = bf16[272,256]{1,0:T(8,128)(2,1)S(1)} collective-permute-done((bf16[272,256]{1,0:T(8,128)(2,1)S(1)}, bf16[272,256]{1,0:T(8,128)(2,1)S(1)}, u32[]{:S(2)}, u32[]{:S(2)}) %collective-permute-start.1) | collective-permute-done | bytes 139296 | tf_op jit(solution)/shard_map/ppermute | solution.py:246
  13.1 0.0 collective-permute-start.6
  14.4 1.3 %collective-permute-done.2.refs_2_ = bf16[272,256]{1,0:T(8,128)(2,1)S(1)} collective-permute-done((bf16[272,256]{1,0:T(8,128)(2,1)S(1)}, bf16[272,256]{1,0:T(8,128)(2,1)S(1)}, u32[]{:S(2)}, u32[]{:S(2)}) %collective-permute-start.2) | collective-permute-done | bytes 139296 | tf_op jit(solution)/shard_map/ppermute | solution.py:246
  15.7 2.9 %collective-permute-done.3.refs_3_ = bf16[272,256]{1,0:T(8,128)(2,1)S(1)} collective-permute-done((bf16[272,256]{1,0:T(8,128)(2,1)S(1)}, bf16[272,256]{1,0:T(8,128)(2,1)S(1)}, u32[]{:S(2)}, u32[]{:S(2)}) %collective-permute-start.3) | collective-permute-done | bytes 139296 | tf_op jit(solution)/shard_map/ppermute | solution.py:246
  18.6 0.0 collective-permute-done.4.refs_4_
  18.6 0.0 collective-permute-done.5.refs_5_
  18.6 0.0 collective-permute-done.6.refs_6_
  18.6 3.7 %attend.1 = (bf16[256,256]{1,0:T(8,128)(2,1)S(1)}, bf16[256,256]{1,0:T(8,128)(2,1)S(1)}, bf16[256,256]{1,0:T(8,128)(2,1)S(1)}, bf16[256,256]{1,0:T(8,128)(2,1)S(...) custom-call(s32[1]{0:T(128)S(6)} %copy.8.source_len, ...), custom_call_target="tpu_custom_call" | custom-call | flops 335544320 | bytes 2097152 | tf_op jit(solution)/shard_map/attend/pallas_call | solution.py:278
  22.4 2.8 %collective-permute-start.7 = (bf16[256,256]{1,0:T(8,128)(2,1)S(1)}, bf16[256,256]{1,0:T(8,128)(2,1)S(1)}, u32[]{:S(2)}, u32[]{:S(2)}) collective-permute-start(bf16[256,256]{1,0:T(8,128)(2,1)S(1)} %get-tuple-element.26), channel_id=1, source_target_pairs={{0,18},{1,19},{2,16},{3,17},{16,2},{17,3},{18,0},{19,1},{4,22},{5,... | collective-permute-start | bytes 393224 | tf_op jit(solution)/shard_map/ppermute | solution.py:246
  25.1 0.0 collective-permute-start.8
  25.1 1.4 %collective-permute-start.9 = (bf16[256,256]{1,0:T(8,128)(2,1)S(1)}, bf16[256,256]{1,0:T(8,128)(2,1)S(1)}, u32[]{:S(2)}, u32[]{:S(2)}) collective-permute-start(bf16[256,256]{1,0:T(8,128)(2,1)S(1)} %get-tuple-element.28), channel_id=1, source_target_pairs={{0,16},{1,17},{2,18},{3,19},{16,0},{17,1},{18,2},{19,3},{4,20},{5,... | collective-permute-start | bytes 393224 | tf_op jit(solution)/shard_map/ppermute | solution.py:246
  26.5 0.3 collective-permute-start.10
  26.9 1.7 %collective-permute-start.11 = (bf16[256,256]{1,0:T(8,128)(2,1)S(1)}, bf16[256,256]{1,0:T(8,128)(2,1)S(1)}, u32[]{:S(2)}, u32[]{:S(2)}) collective-permute-start(bf16[256,256]{1,0:T(8,128)(2,1)S(1)} %get-tuple-element.30), channel_id=1, source_target_pairs={{0,2},{1,3},{2,0},{3,1},{16,18},{17,19},{18,16},{19,17},{4,6},{5,7... | collective-permute-start | bytes 393224 | tf_op jit(solution)/shard_map/ppermute | solution.py:246
  28.6 0.4 %collective-permute-done.7.refs_0_ = bf16[256,256]{1,0:T(8,128)(2,1)S(1)} collective-permute-done((bf16[256,256]{1,0:T(8,128)(2,1)S(1)}, bf16[256,256]{1,0:T(8,128)(2,1)S(1)}, u32[]{:S(2)}, u32[]{:S(2)}) %collective-permute-start.7) | collective-permute-done | bytes 131104 | tf_op jit(solution)/shard_map/ppermute | solution.py:246
  29.0 0.4 %collective-permute-start.12 = (bf16[256,256]{1,0:T(8,128)(2,1)S(1)}, bf16[256,256]{1,0:T(8,128)(2,1)S(1)}, u32[]{:S(2)}, u32[]{:S(2)}) collective-permute-start(bf16[256,256]{1,0:T(8,128)(2,1)S(1)} %get-tuple-element.31), channel_id=1, source_target_pairs={{0,3},{1,2},{2,1},{3,0},{16,19},{17,18},{18,17},{19,16},{4,7},{5,6... | collective-permute-start | bytes 393224 | tf_op jit(solution)/shard_map/ppermute | solution.py:246
  29.4 2.4 %collective-permute-done.8.refs_1_ = bf16[256,256]{1,0:T(8,128)(2,1)S(1)} collective-permute-done((bf16[256,256]{1,0:T(8,128)(2,1)S(1)}, bf16[256,256]{1,0:T(8,128)(2,1)S(1)}, u32[]{:S(2)}, u32[]{:S(2)}) %collective-permute-start.8) | collective-permute-done | bytes 131104 | tf_op jit(solution)/shard_map/ppermute | solution.py:246
  31.9 0.1 collective-permute-start.13
  31.9 2.6 %collective-permute-done.9.refs_2_ = bf16[256,256]{1,0:T(8,128)(2,1)S(1)} collective-permute-done((bf16[256,256]{1,0:T(8,128)(2,1)S(1)}, bf16[256,256]{1,0:T(8,128)(2,1)S(1)}, u32[]{:S(2)}, u32[]{:S(2)}) %collective-permute-start.9) | collective-permute-done | bytes 131104 | tf_op jit(solution)/shard_map/ppermute | solution.py:246
  34.6 2.7 %collective-permute-done.10.refs_3_ = bf16[256,256]{1,0:T(8,128)(2,1)S(1)} collective-permute-done((bf16[256,256]{1,0:T(8,128)(2,1)S(1)}, bf16[256,256]{1,0:T(8,128)(2,1)S(1)}, u32[]{:S(2)}, u32[]{:S(2)}) %collective-permute-start.10) | collective-permute-done | bytes 131104 | tf_op jit(solution)/shard_map/ppermute | solution.py:246
  37.3 0.0 collective-permute-done.11.refs_4_
  37.3 0.0 collective-permute-done.12.refs_5_
  37.3 0.0 collective-permute-done.13.refs_6_
  37.3 1.1 %unpack.1 = (bf16[1,1,128,2048]{3,2,1,0:T(8,128)(2,1)}, bf16[1,1,128,2048]{3,2,1,0:T(8,128)(2,1)}) custom-call(bf16[256,256]{1,0:T(8,128)(2,1)S(1)} %collective-permute-done.7.refs_0_, bf16[256,256]{1,0:T(8,128)(2,1)S(1)} %collective-permute-done.8.refs_1_, bf16[256,256]{1,0:T(8,128)(2,1)S(1)} %collective-permute-done.9.refs_2_, ...), custom_call_target="tpu_custom_call" | custom-call | tf_op jit(solution)/shard_map/unpack/pallas_call | solution.py:290
Async XLA Ops:
  2.1 8.1 %collective-permute-start = (bf16[272,256]{1,0:T(8,128)(2,1)S(1)}, bf16[272,256]{1,0:T(8,128)(2,1)S(1)}, u32[]{:S(2)}, u32[]{:S(2)}) collective-permute-start(bf16[272,256]{1,0:T(8,128)(2,1)S(1)} %get-tuple-element.18), channel_id=1, source_target_pairs={{0,18},{1,19},{2,16},{3,17},{16,2},{17,3},{18,0},{19,1},{4,22},{5,... | collective-permute-start | bytes 417800 | tf_op jit(solution)/shard_map/ppermute | solution.py:246
  6.0 7.1 %collective-permute-start.1 = (bf16[272,256]{1,0:T(8,128)(2,1)S(1)}, bf16[272,256]{1,0:T(8,128)(2,1)S(1)}, u32[]{:S(2)}, u32[]{:S(2)}) collective-permute-start(bf16[272,256]{1,0:T(8,128)(2,1)S(1)} %get-tuple-element.19), channel_id=1, source_target_pairs={{0,19},{1,18},{2,17},{3,16},{16,3},{17,2},{18,1},{19,0},{4,23},{5,... | collective-permute-start | bytes 417800 | tf_op jit(solution)/shard_map/ppermute | solution.py:246
  6.0 9.7 %collective-permute-start.2 = (bf16[272,256]{1,0:T(8,128)(2,1)S(1)}, bf16[272,256]{1,0:T(8,128)(2,1)S(1)}, u32[]{:S(2)}, u32[]{:S(2)}) collective-permute-start(bf16[272,256]{1,0:T(8,128)(2,1)S(1)} %get-tuple-element.20), channel_id=1, source_target_pairs={{0,16},{1,17},{2,18},{3,19},{16,0},{17,1},{18,2},{19,3},{4,20},{5,... | collective-permute-start | bytes 417800 | tf_op jit(solution)/shard_map/ppermute | solution.py:246
  7.2 11.4 %collective-permute-start.3 = (bf16[272,256]{1,0:T(8,128)(2,1)S(1)}, bf16[272,256]{1,0:T(8,128)(2,1)S(1)}, u32[]{:S(2)}, u32[]{:S(2)}) collective-permute-start(bf16[272,256]{1,0:T(8,128)(2,1)S(1)} %get-tuple-element.21), channel_id=1, source_target_pairs={{0,17},{1,16},{2,19},{3,18},{16,1},{17,0},{18,3},{19,2},{4,21},{5,... | collective-permute-start | bytes 417800 | tf_op jit(solution)/shard_map/ppermute | solution.py:246
  7.8 10.8 %collective-permute-start.4 = (bf16[272,256]{1,0:T(8,128)(2,1)S(1)}, bf16[272,256]{1,0:T(8,128)(2,1)S(1)}, u32[]{:S(2)}, u32[]{:S(2)}) collective-permute-start(bf16[272,256]{1,0:T(8,128)(2,1)S(1)} %get-tuple-element.22), channel_id=1, source_target_pairs={{0,2},{1,3},{2,0},{3,1},{16,18},{17,19},{18,16},{19,17},{4,6},{5,7... | collective-permute-start | bytes 417800 | tf_op jit(solution)/shard_map/ppermute | solution.py:246
  10.1 8.5 %collective-permute-start.5 = (bf16[272,256]{1,0:T(8,128)(2,1)S(1)}, bf16[272,256]{1,0:T(8,128)(2,1)S(1)}, u32[]{:S(2)}, u32[]{:S(2)}) collective-permute-start(bf16[272,256]{1,0:T(8,128)(2,1)S(1)} %get-tuple-element.23), channel_id=1, source_target_pairs={{0,3},{1,2},{2,1},{3,0},{16,19},{17,18},{18,17},{19,16},{4,7},{5,6... | collective-permute-start | bytes 417800 | tf_op jit(solution)/shard_map/ppermute | solution.py:246
  13.1 5.5 %collective-permute-start.6 = (bf16[272,256]{1,0:T(8,128)(2,1)S(1)}, bf16[272,256]{1,0:T(8,128)(2,1)S(1)}, u32[]{:S(2)}, u32[]{:S(2)}) collective-permute-start(bf16[272,256]{1,0:T(8,128)(2,1)S(1)} %get-tuple-element.24), channel_id=1, source_target_pairs={{0,1},{1,0},{2,3},{3,2},{16,17},{17,16},{18,19},{19,18},{4,5},{5,4... | collective-permute-start | bytes 417800 | tf_op jit(solution)/shard_map/ppermute | solution.py:246
  22.4 6.6 %collective-permute-start.7 = (bf16[256,256]{1,0:T(8,128)(2,1)S(1)}, bf16[256,256]{1,0:T(8,128)(2,1)S(1)}, u32[]{:S(2)}, u32[]{:S(2)}) collective-permute-start(bf16[256,256]{1,0:T(8,128)(2,1)S(1)} %get-tuple-element.26), channel_id=1, source_target_pairs={{0,18},{1,19},{2,16},{3,17},{16,2},{17,3},{18,0},{19,1},{4,22},{5,... | collective-permute-start | bytes 393224 | tf_op jit(solution)/shard_map/ppermute | solution.py:246
  25.1 6.7 %collective-permute-start.8 = (bf16[256,256]{1,0:T(8,128)(2,1)S(1)}, bf16[256,256]{1,0:T(8,128)(2,1)S(1)}, u32[]{:S(2)}, u32[]{:S(2)}) collective-permute-start(bf16[256,256]{1,0:T(8,128)(2,1)S(1)} %get-tuple-element.27), channel_id=1, source_target_pairs={{0,19},{1,18},{2,17},{3,16},{16,3},{17,2},{18,1},{19,0},{4,23},{5,... | collective-permute-start | bytes 393224 | tf_op jit(solution)/shard_map/ppermute | solution.py:246
  25.1 9.4 %collective-permute-start.9 = (bf16[256,256]{1,0:T(8,128)(2,1)S(1)}, bf16[256,256]{1,0:T(8,128)(2,1)S(1)}, u32[]{:S(2)}, u32[]{:S(2)}) collective-permute-start(bf16[256,256]{1,0:T(8,128)(2,1)S(1)} %get-tuple-element.28), channel_id=1, source_target_pairs={{0,16},{1,17},{2,18},{3,19},{16,0},{17,1},{18,2},{19,3},{4,20},{5,... | collective-permute-start | bytes 393224 | tf_op jit(solution)/shard_map/ppermute | solution.py:246
  26.5 10.7 %collective-permute-start.10 = (bf16[256,256]{1,0:T(8,128)(2,1)S(1)}, bf16[256,256]{1,0:T(8,128)(2,1)S(1)}, u32[]{:S(2)}, u32[]{:S(2)}) collective-permute-start(bf16[256,256]{1,0:T(8,128)(2,1)S(1)} %get-tuple-element.29), channel_id=1, source_target_pairs={{0,17},{1,16},{2,19},{3,18},{16,1},{17,0},{18,3},{19,2},{4,21},{5,... | collective-permute-start | bytes 393224 | tf_op jit(solution)/shard_map/ppermute | solution.py:246
  26.9 10.4 %collective-permute-start.11 = (bf16[256,256]{1,0:T(8,128)(2,1)S(1)}, bf16[256,256]{1,0:T(8,128)(2,1)S(1)}, u32[]{:S(2)}, u32[]{:S(2)}) collective-permute-start(bf16[256,256]{1,0:T(8,128)(2,1)S(1)} %get-tuple-element.30), channel_id=1, source_target_pairs={{0,2},{1,3},{2,0},{3,1},{16,18},{17,19},{18,16},{19,17},{4,6},{5,7... | collective-permute-start | bytes 393224 | tf_op jit(solution)/shard_map/ppermute | solution.py:246
  29.0 8.3 %collective-permute-start.12 = (bf16[256,256]{1,0:T(8,128)(2,1)S(1)}, bf16[256,256]{1,0:T(8,128)(2,1)S(1)}, u32[]{:S(2)}, u32[]{:S(2)}) collective-permute-start(bf16[256,256]{1,0:T(8,128)(2,1)S(1)} %get-tuple-element.31), channel_id=1, source_target_pairs={{0,3},{1,2},{2,1},{3,0},{16,19},{17,18},{18,17},{19,16},{4,7},{5,6... | collective-permute-start | bytes 393224 | tf_op jit(solution)/shard_map/ppermute | solution.py:246
  31.9 5.4 %collective-permute-start.13 = (bf16[256,256]{1,0:T(8,128)(2,1)S(1)}, bf16[256,256]{1,0:T(8,128)(2,1)S(1)}, u32[]{:S(2)}, u32[]{:S(2)}) collective-permute-start(bf16[256,256]{1,0:T(8,128)(2,1)S(1)} %get-tuple-element.32), channel_id=1, source_target_pairs={{0,1},{1,0},{2,3},{3,2},{16,17},{17,16},{18,19},{19,18},{4,5},{5,4... | collective-permute-start | bytes 393224 | tf_op jit(solution)/shard_map/ppermute | solution.py:246

commit v7 on v6

--- a/solution.py
+++ b/solution.py
@@ -153,19 +153,21 @@
 
 def pack_kernel(seq_count, order, *refs):
     smalls, (first, second) = refs[:2], refs[2:4]
-    outs, (lists, mask, small_sem, sem) = refs[4:-4], refs[-4:]
+    near, far, (lists, mask, small_sem, sem) = refs[4], refs[5:-4], refs[-4:]
+    me = device_index(seq_count)
+    here = me % seq_count
+    share = near.shape[2]
+    outs = [(me ^ step, out) for step, out in zip(order, far)]
+    outs += [(me - here + slot, near.at[slot]) for slot in range(seq_count)]
     small_copies = [
         pltpu.make_async_copy(source, held, small_sem.at[slot])
         for slot, (source, held) in enumerate(zip(smalls, (lists, mask)))
     ]
     for copy in small_copies:
         copy.start()
-    me = device_index(seq_count)
-    here = me % seq_count
-    share = outs[0].shape[1]
     copies = []
-    for slot, (step, out) in enumerate(zip(order, outs)):
-        lanes = pl.ds(pl.multiple_of((me ^ step) * share, LANES), share)
+    for slot, (target, out) in enumerate(outs):
+        lanes = pl.ds(pl.multiple_of(target * share, LANES), share)
         pair = [
             pltpu.make_async_copy(
                 source.at[0, 0, :, lanes], out.at[pl.ds(half * BLK, BLK)], sem.at[half, slot]
@@ -183,26 +185,27 @@
     base = here - WIN
     code = (lists[0, 0, 0] - base) * SPAN + lists[0, 0, 1] - base
     tail = jnp.full((TAIL, share), code, jnp.int32).astype(jnp.float32).astype(jnp.bfloat16)
-    for out, pair in zip(outs, copies):
+    for slot in range(seq_count):
+        near[slot, 2 * BLK :] = tail
+    for (target, out), pair in zip(outs, copies):
         for copy in pair:
             copy.wait()
         out[BLK : 2 * BLK] = out[BLK : 2 * BLK] * keep
-        out[2 * BLK :] = tail
 
 
 def attend_kernel(seq_count, order, source_len, target_len, *refs):
-    parts = 2 * seq_count
-    shares, outs = refs[:parts], refs[parts : 2 * parts]
-    rows, result, key_grad, value_grad, lists = refs[2 * parts :]
+    count = 1 + len(order)
+    (near, *far), (near_out, *far_out) = refs[:count], refs[count : 2 * count]
+    rows, result, key_grad, value_grad, lists = refs[2 * count :]
     me = device_index(seq_count)
-    here = me % seq_count
-    for step, share in zip(order, shares):
-        source = me ^ step
-        rows[source, 0] = share[:BLK]
-        rows[source, 1] = share[BLK : 2 * BLK]
-        if step < seq_count:
-            tail = share[2 * BLK :, :LANES].astype(jnp.float32)
-            lists[here ^ step] = jnp.max(tail).astype(jnp.int32)
+    base = me - me % seq_count
+    for slot in range(seq_count):
+        rows[base + slot, 0] = near[slot, :BLK]
+        rows[base + slot, 1] = near[slot, BLK : 2 * BLK]
+        lists[slot] = jnp.max(near[slot, 2 * BLK :, :LANES].astype(jnp.float32)).astype(jnp.int32)
+    for step, share in zip(order, far):
+        rows[me ^ step, 0] = share[:BLK]
+        rows[me ^ step, 1] = share[BLK:]
 
     def listed(block, slot):
         code = lists[block]
@@ -211,18 +214,24 @@
     attend_sample(
         seq_count, listed, source_len[0], target_len[0], rows, result, key_grad, value_grad
     )
-    for step, out in zip(order, outs):
+    for step, out in zip(order, far_out):
         out[:BLK] = result[me ^ step, 0]
         out[BLK:] = result[me ^ step, 1]
-
-
-def unpack_kernel(seq_count, order, *refs):
-    shares, (first, second, sem) = refs[:-3], refs[-3:]
-    width = shares[0].shape[1]
+    for slot in range(seq_count):
+        near_out[slot, :BLK] = result[base + slot, 0]
+        near_out[slot, BLK:] = result[base + slot, 1]
+
+
+def unpack_kernel(seq_count, order, near, *refs):
+    far, (first, second, sem) = refs[:-3], refs[-3:]
+    width = near.shape[2]
     me = device_index(seq_count)
+    base = me - me % seq_count
+    shares = [(me ^ step, share) for step, share in zip(order, far)]
+    shares += [(base + slot, near.at[slot]) for slot in range(seq_count)]
     copies = []
-    for slot, (step, share) in enumerate(zip(order, shares)):
-        lanes = pl.ds(pl.multiple_of((me ^ step) * width, LANES), width)
+    for slot, (source, share) in enumerate(shares):
+        lanes = pl.ds(pl.multiple_of(source * width, LANES), width)
         for half, result in enumerate((first, second)):
             copy = pltpu.make_async_copy(
                 share.at[pl.ds(half * BLK, BLK)], result.at[0, 0, :, lanes], sem.at[half, slot]
@@ -233,18 +242,13 @@
         copy.wait()
 
 
-def swapped(shares, order, after):
-    parts = len(order)
-    held = dict(zip(order, shares))
-    moved = {0: held[0]}
-    for step in order:
-        if step:
-            share = held[step]
-            if step in after:
-                earlier = after[step]
-                share, moved[earlier] = lax.optimization_barrier((share, moved[earlier]))
-            moved[step] = lax.ppermute(share, AXES, [(dev, dev ^ step) for dev in range(parts)])
-    return [moved[step] for step in order]
+def swapped(order, near, *far):
+    parts = 2 * near.shape[0]
+    far = [
+        lax.ppermute(share, AXES, [(dev, dev ^ step) for dev in range(parts)])
+        for step, share in zip(order, far)
+    ]
+    return [lax.all_to_all(near, "seq", 0, 0, tiled=True), *far]
 
 
 def by_pairs(first_rows, second_rows, alignment, diffusion_mask, source_length, target_length):
@@ -254,15 +258,14 @@
     share = width // parts
     kind = first_rows.dtype
     params = pltpu.CompilerParams(vmem_limit_bytes=VMEM_LIMIT)
-    order, after = list(range(parts - 1, -1, -1)), {}
-    if parts == 8:
-        order = [6, 7, 4, 5, 2, 3, 1, 0]
+    order = [seq_count, *range(seq_count + 2, parts), seq_count + 1]
+    far = [jax.ShapeDtypeStruct((2 * BLK, share), kind)] * seq_count
     sems = pltpu.SemaphoreType.DMA((2, parts))
     shares = pl.pallas_call(
         functools.partial(pack_kernel, seq_count, order),
-        out_shape=[jax.ShapeDtypeStruct((2 * BLK + TAIL, share), kind)] * parts,
+        out_shape=[jax.ShapeDtypeStruct((seq_count, 2 * BLK + TAIL, share), kind), *far],
         in_specs=specs(4, pltpu.HBM),
-        out_specs=specs(parts, pltpu.VMEM),
+        out_specs=specs(1 + seq_count, pltpu.VMEM),
         scratch_shapes=[
             pltpu.SMEM(alignment.shape, jnp.int32),
             pltpu.VMEM(diffusion_mask.shape, jnp.int32),
@@ -272,25 +275,25 @@
         compiler_params=params,
         name="pack",
     )(*in_hbm(alignment, diffusion_mask, first_rows, second_rows))
-    shares = swapped(shares, order, after)
+    shares = swapped(order, *shares)
     rows = pltpu.VMEM((parts, 2, BLK, share), kind)
     grads = pltpu.VMEM((seq_count, BLK, share), jnp.float32)
     shares = pl.pallas_call(
         functools.partial(attend_kernel, seq_count, order),
-        out_shape=[jax.ShapeDtypeStruct((2 * BLK, share), kind)] * parts,
-        in_specs=specs(2, pltpu.SMEM) + specs(parts, pltpu.VMEM),
-        out_specs=specs(parts, pltpu.VMEM),
+        out_shape=[jax.ShapeDtypeStruct((seq_count, 2 * BLK, share), kind), *far],
+        in_specs=specs(2, pltpu.SMEM) + specs(1 + seq_count, pltpu.VMEM),
+        out_specs=specs(1 + seq_count, pltpu.VMEM),
         scratch_shapes=[rows, rows, grads, grads, pltpu.SMEM((seq_count,), jnp.int32)],
         compiler_params=params,
         cost_estimate=attend_cost(seq_count, share),
         name="attend",
     )(source_length, target_length, *shares)
-    shares = swapped(shares, order, after)
+    shares = swapped(order, *shares)
     out_shape = jax.ShapeDtypeStruct((1, 1, BLK, width), kind)
     return pl.pallas_call(
         functools.partial(unpack_kernel, seq_count, order),
         out_shape=[out_shape, out_shape],
-        in_specs=specs(parts, pltpu.VMEM),
+        in_specs=specs(1 + seq_count, pltpu.VMEM),
         out_specs=specs(2, pltpu.HBM),
         scratch_shapes=[sems],
         compiler_params=params,
@@ -303,6 +306,7 @@
     parts = lax.axis_size("section") * seq_count
     paired = (
         parts == 2 * seq_count
+        and seq_count >= 2
         and seq_count & (seq_count - 1) == 0
         and first_rows.shape[2] == BLK
         and first_rows.shape[3] % (parts * LANES) == 0

time: 38.6 us -> 46.8 us (1.21)
  starting transfers between devices: 14.1 us -> 17.9 us
  waiting for transfers between devices: 16 us -> 18.8 us
  Pallas kernels: 6.27 us -> 7.87 us
    all_to_all x0 -> x2, starting transfers between devices: none -> 7.69 us  [swapped(): return [lax.all_to_all(near, 'seq', 0, 0, tiled=True), *far]]
    ppermute x14 -> x8, starting transfers between devices: 14.1 us -> 10.2 us  [swapped(): lax.ppermute(share, AXES, [(dev, dev ^ step) for dev in range(parts)])]
    ppermute x14 -> x8, waiting for transfers between devices: 16 us -> 18.8 us  [swapped(): lax.ppermute(share, AXES, [(dev, dev ^ step) for dev in range(parts)])]
    pallas_call x1, Pallas kernels: 3.74 us -> 4.55 us  [by_pairs(): pl.pallas_call(functools.partial(attend_kernel, seq_count, order), out_sh...]
    pallas_call x1, Pallas kernels: 1.43 us -> 2.23 us  [by_pairs(): pl.pallas_call(functools.partial(pack_kernel, seq_count, order), out_shap...]
  transfers between devices with their start and end apart: 14 -> 10, of which waited for: 8 -> 5; matrix products, arithmetic and copies ran while one was open for 0% -> 0% of each run, Pallas kernels for 0% -> 0%
where the time goes in v7:
time: 46.8 us; the launch traced here: 46.5 us
  waiting for transfers between devices  18.8 us (40%)
  starting transfers between devices  17.9 us (38%)
  Pallas kernels  7.87 us (17%)
  between operations  1.96 us (4%)
    ppermute x8, waiting for transfers between devices, swapped(): lax.ppermute(share, AXES, [(dev, dev ^ step) for dev in range(parts)])  18.8 us
    ppermute x8, starting transfers between devices, swapped(): lax.ppermute(share, AXES, [(dev, dev ^ step) for dev in range(parts)])  10.2 us
    all_to_all x2, starting transfers between devices, swapped(): return [lax.all_to_all(near, 'seq', 0, 0, tiled=True), *far]  7.69 us
    pallas_call x1, Pallas kernels, by_pairs(): pl.pallas_call(functools.partial(attend_kernel, seq_count, order), out_sh...  4.55 us
    pallas_call x1, Pallas kernels, by_pairs(): pl.pallas_call(functools.partial(pack_kernel, seq_count, order), out_shap...  2.23 us
    pallas_call x1, Pallas kernels, by_pairs(): pl.pallas_call(functools.partial(unpack_kernel, seq_count, order), out_sh...  1.09 us
  transfers between devices with their start and end apart: 10, of which 5 were waited for; matrix products, arithmetic and copies ran while one was open for 0% of the time, Pallas kernels for 0%

profile of v7, /device:TPU:0, one launch (start us, length us, event | category | flops | bytes accessed | tf_op | source)
XLA Modules:
  0.0 46.5 jit_solution(9852909367545764081)
XLA Ops:
  0.6 2.2 %pack.1 = (bf16[4,272,256]{2,1,0:T(8,128)(2,1)}, bf16[256,256]{1,0:T(8,128)(2,1)S(1)}, bf16[256,256]{1,0:T(8,128)(2,1)S(1)}, bf16[256,256]{1,0:T(8,128)(2,1)S(1)}, bf16[256,256]{1,0:T(8,128)(2,1)S(1)}) custom-call(s32[1,1,2]{2,1,0:T(1,128)} %refs_0_.1, s32[1,128]{1,0:T(1,128)} %refs_1_.1, bf16[1,1,128,2048]{3,2,1,0:T(8,128)(2,1)} %refs_2_.1, ...), custom_call_target="tpu_custom_call" | custom-call | tf_op jit(solution)/shard_map/pack/pallas_call | solution.py:264
  2.9 4.2 %all-to-all-start = ((bf16[4,272,256]{2,1,0:T(8,128)(2,1)}), bf16[4,272,256]{2,1,0:T(8,128)(2,1)S(1)}, u32[]{:S(2)}, u32[]{:S(2)}) async-start(bf16[4,272,256]{2,1,0:T(8,128)(2,1)} %get-tuple-element.12), calls=%async_computation | async-start | bytes 1114112 | tf_op jit(solution)/shard_map/all_to_all | solution.py:251
  7.1 2.3 %collective-permute-start = (bf16[256,256]{1,0:T(8,128)(2,1)S(1)}, bf16[256,256]{1,0:T(8,128)(2,1)S(1)}, u32[]{:S(2)}, u32[]{:S(2)}) collective-permute-start(bf16[256,256]{1,0:T(8,128)(2,1)S(1)} %get-tuple-element.13), channel_id=1, source_target_pairs={{0,16},{1,17},{2,18},{3,19},{16,0},{17,1},{18,2},{19,3},{4,20},{5,... | collective-permute-start | bytes 393224 | tf_op jit(solution)/shard_map/ppermute | solution.py:248
  9.4 1.4 %collective-permute-start.1 = (bf16[256,256]{1,0:T(8,128)(2,1)S(1)}, bf16[256,256]{1,0:T(8,128)(2,1)S(1)}, u32[]{:S(2)}, u32[]{:S(2)}) collective-permute-start(bf16[256,256]{1,0:T(8,128)(2,1)S(1)} %get-tuple-element.14), channel_id=1, source_target_pairs={{0,18},{1,19},{2,16},{3,17},{16,2},{17,3},{18,0},{19,1},{4,22},{5,... | collective-permute-start | bytes 393224 | tf_op jit(solution)/shard_map/ppermute | solution.py:248
  10.8 1.0 %collective-permute-start.2 = (bf16[256,256]{1,0:T(8,128)(2,1)S(1)}, bf16[256,256]{1,0:T(8,128)(2,1)S(1)}, u32[]{:S(2)}, u32[]{:S(2)}) collective-permute-start(bf16[256,256]{1,0:T(8,128)(2,1)S(1)} %get-tuple-element.15), channel_id=1, source_target_pairs={{0,19},{1,18},{2,17},{3,16},{16,3},{17,2},{18,1},{19,0},{4,23},{5,... | collective-permute-start | bytes 393224 | tf_op jit(solution)/shard_map/ppermute | solution.py:248
  11.8 0.7 %collective-permute-start.3 = (bf16[256,256]{1,0:T(8,128)(2,1)S(1)}, bf16[256,256]{1,0:T(8,128)(2,1)S(1)}, u32[]{:S(2)}, u32[]{:S(2)}) collective-permute-start(bf16[256,256]{1,0:T(8,128)(2,1)S(1)} %get-tuple-element.16), channel_id=1, source_target_pairs={{0,17},{1,16},{2,19},{3,18},{16,1},{17,0},{18,3},{19,2},{4,21},{5,... | collective-permute-start | bytes 393224 | tf_op jit(solution)/shard_map/ppermute | solution.py:248
  13.8 0.0 collective-permute-done.refs_1_
  13.8 7.4 %collective-permute-done.1.refs_2_ = bf16[256,256]{1,0:T(8,128)(2,1)S(1)} collective-permute-done((bf16[256,256]{1,0:T(8,128)(2,1)S(1)}, bf16[256,256]{1,0:T(8,128)(2,1)S(1)}, u32[]{:S(2)}, u32[]{:S(2)}) %collective-permute-start.1) | collective-permute-done | bytes 131104 | tf_op jit(solution)/shard_map/ppermute | solution.py:248
  21.2 1.9 %collective-permute-done.2.refs_3_ = bf16[256,256]{1,0:T(8,128)(2,1)S(1)} collective-permute-done((bf16[256,256]{1,0:T(8,128)(2,1)S(1)}, bf16[256,256]{1,0:T(8,128)(2,1)S(1)}, u32[]{:S(2)}, u32[]{:S(2)}) %collective-permute-start.2) | collective-permute-done | bytes 131104 | tf_op jit(solution)/shard_map/ppermute | solution.py:248
  23.1 0.0 collective-permute-done.3.refs_4_
  23.1 0.0 all-to-all-done.refs_0_
  23.1 4.5 %attend.1 = (bf16[4,256,256]{2,1,0:T(8,128)(2,1)}, bf16[256,256]{1,0:T(8,128)(2,1)S(1)}, bf16[256,256]{1,0:T(8,128)(2,1)S(1)}, bf16[256,256]{1,0:T(8,128)(2,1)S(1)}, bf16[256,256]{1,0:T(8,128)(2,1)S(1)}) custom-call(s32[1]{0:T(128)S(6)} %copy.8.source_len, s32[1]{0:T(128)S(6)} %copy.9.target_len, bf16[4,272,256]{2,1,0:T(8,128)(2,1)S(1)} %all-to-all-done.refs_0_, ...), custom_call_target="tpu_custom_call" | custom-call | flops 335544320 | bytes 2097152 | tf_op jit(solution)/shard_map/attend/pallas_call | solution.py:281
  27.6 3.5 %all-to-all-start.1 = ((bf16[4,256,256]{2,1,0:T(8,128)(2,1)}), bf16[4,256,256]{2,1,0:T(8,128)(2,1)S(1)}, u32[]{:S(2)}, u32[]{:S(2)}) async-start(bf16[4,256,256]{2,1,0:T(8,128)(2,1)} %get-tuple-element.17), calls=%async_computation.1 | async-start | bytes 1048576 | tf_op jit(solution)/shard_map/all_to_all | solution.py:251
  31.1 0.9 %collective-permute-start.4 = (bf16[256,256]{1,0:T(8,128)(2,1)S(1)}, bf16[256,256]{1,0:T(8,128)(2,1)S(1)}, u32[]{:S(2)}, u32[]{:S(2)}) collective-permute-start(bf16[256,256]{1,0:T(8,128)(2,1)S(1)} %get-tuple-element.18), channel_id=1, source_target_pairs={{0,16},{1,17},{2,18},{3,19},{16,0},{17,1},{18,2},{19,3},{4,20},{5,... | collective-permute-start | bytes 393224 | tf_op jit(solution)/shard_map/ppermute | solution.py:248
  32.0 2.6 %collective-permute-start.5 = (bf16[256,256]{1,0:T(8,128)(2,1)S(1)}, bf16[256,256]{1,0:T(8,128)(2,1)S(1)}, u32[]{:S(2)}, u32[]{:S(2)}) collective-permute-start(bf16[256,256]{1,0:T(8,128)(2,1)S(1)} %get-tuple-element.19), channel_id=1, source_target_pairs={{0,18},{1,19},{2,16},{3,17},{16,2},{17,3},{18,0},{19,1},{4,22},{5,... | collective-permute-start | bytes 393224 | tf_op jit(solution)/shard_map/ppermute | solution.py:248
  34.6 0.0 collective-permute-start.6
  34.6 1.3 %collective-permute-start.7 = (bf16[256,256]{1,0:T(8,128)(2,1)S(1)}, bf16[256,256]{1,0:T(8,128)(2,1)S(1)}, u32[]{:S(2)}, u32[]{:S(2)}) collective-permute-start(bf16[256,256]{1,0:T(8,128)(2,1)S(1)} %get-tuple-element.21), channel_id=1, source_target_pairs={{0,17},{1,16},{2,19},{3,18},{16,1},{17,0},{18,3},{19,2},{4,21},{5,... | collective-permute-start | bytes 393224 | tf_op jit(solution)/shard_map/ppermute | solution.py:248
  35.8 1.2 %collective-permute-done.4.refs_0_ = bf16[256,256]{1,0:T(8,128)(2,1)S(1)} collective-permute-done((bf16[256,256]{1,0:T(8,128)(2,1)S(1)}, bf16[256,256]{1,0:T(8,128)(2,1)S(1)}, u32[]{:S(2)}, u32[]{:S(2)}) %collective-permute-start.4) | collective-permute-done | bytes 131104 | tf_op jit(solution)/shard_map/ppermute | solution.py:248
  37.0 6.5 %collective-permute-done.5.refs_1_ = bf16[256,256]{1,0:T(8,128)(2,1)S(1)} collective-permute-done((bf16[256,256]{1,0:T(8,128)(2,1)S(1)}, bf16[256,256]{1,0:T(8,128)(2,1)S(1)}, u32[]{:S(2)}, u32[]{:S(2)}) %collective-permute-start.5) | collective-permute-done | bytes 131104 | tf_op jit(solution)/shard_map/ppermute | solution.py:248
  43.5 1.9 %collective-permute-done.6.refs_2_ = bf16[256,256]{1,0:T(8,128)(2,1)S(1)} collective-permute-done((bf16[256,256]{1,0:T(8,128)(2,1)S(1)}, bf16[256,256]{1,0:T(8,128)(2,1)S(1)}, u32[]{:S(2)}, u32[]{:S(2)}) %collective-permute-start.6) | collective-permute-done | bytes 131104 | tf_op jit(solution)/shard_map/ppermute | solution.py:248
  45.4 0.0 collective-permute-done.7.refs_3_
  45.4 0.0 all-to-all-done.1.near
  45.4 1.1 %unpack.1 = (bf16[1,1,128,2048]{3,2,1,0:T(8,128)(2,1)}, bf16[1,1,128,2048]{3,2,1,0:T(8,128)(2,1)}) custom-call(bf16[4,256,256]{2,1,0:T(8,128)(2,1)S(1)} %all-to-all-done.1.near, bf16[256,256]{1,0:T(8,128)(2,1)S(1)} %collective-permute-done.4.refs_0_, bf16[256,256]{1,0:T(8,128)(2,1)S(1)} %collective-permute-done.5.refs_1_, ...), custom_call_target="tpu_custom_call" | custom-call | tf_op jit(solution)/shard_map/unpack/pallas_call | solution.py:293
Async XLA Ops:
  2.9 20.2 %all-to-all-start = ((bf16[4,272,256]{2,1,0:T(8,128)(2,1)}), bf16[4,272,256]{2,1,0:T(8,128)(2,1)S(1)}, u32[]{:S(2)}, u32[]{:S(2)}) async-start(bf16[4,272,256]{2,1,0:T(8,128)(2,1)} %get-tuple-element.12), calls=%async_computation | async-start | bytes 1114112 | tf_op jit(solution)/shard_map/all_to_all | solution.py:251
  7.1 6.7 %collective-permute-start = (bf16[256,256]{1,0:T(8,128)(2,1)S(1)}, bf16[256,256]{1,0:T(8,128)(2,1)S(1)}, u32[]{:S(2)}, u32[]{:S(2)}) collective-permute-start(bf16[256,256]{1,0:T(8,128)(2,1)S(1)} %get-tuple-element.13), channel_id=1, source_target_pairs={{0,16},{1,17},{2,18},{3,19},{16,0},{17,1},{18,2},{19,3},{4,20},{5,... | collective-permute-start | bytes 393224 | tf_op jit(solution)/shard_map/ppermute | solution.py:248
  9.4 11.8 %collective-permute-start.1 = (bf16[256,256]{1,0:T(8,128)(2,1)S(1)}, bf16[256,256]{1,0:T(8,128)(2,1)S(1)}, u32[]{:S(2)}, u32[]{:S(2)}) collective-permute-start(bf16[256,256]{1,0:T(8,128)(2,1)S(1)} %get-tuple-element.14), channel_id=1, source_target_pairs={{0,18},{1,19},{2,16},{3,17},{16,2},{17,3},{18,0},{19,1},{4,22},{5,... | collective-permute-start | bytes 393224 | tf_op jit(solution)/shard_map/ppermute | solution.py:248
  10.8 12.2 %collective-permute-start.2 = (bf16[256,256]{1,0:T(8,128)(2,1)S(1)}, bf16[256,256]{1,0:T(8,128)(2,1)S(1)}, u32[]{:S(2)}, u32[]{:S(2)}) collective-permute-start(bf16[256,256]{1,0:T(8,128)(2,1)S(1)} %get-tuple-element.15), channel_id=1, source_target_pairs={{0,19},{1,18},{2,17},{3,16},{16,3},{17,2},{18,1},{19,0},{4,23},{5,... | collective-permute-start | bytes 393224 | tf_op jit(solution)/shard_map/ppermute | solution.py:248
  11.8 11.3 %collective-permute-start.3 = (bf16[256,256]{1,0:T(8,128)(2,1)S(1)}, bf16[256,256]{1,0:T(8,128)(2,1)S(1)}, u32[]{:S(2)}, u32[]{:S(2)}) collective-permute-start(bf16[256,256]{1,0:T(8,128)(2,1)S(1)} %get-tuple-element.16), channel_id=1, source_target_pairs={{0,17},{1,16},{2,19},{3,18},{16,1},{17,0},{18,3},{19,2},{4,21},{5,... | collective-permute-start | bytes 393224 | tf_op jit(solution)/shard_map/ppermute | solution.py:248
  27.6 17.8 %all-to-all-start.1 = ((bf16[4,256,256]{2,1,0:T(8,128)(2,1)}), bf16[4,256,256]{2,1,0:T(8,128)(2,1)S(1)}, u32[]{:S(2)}, u32[]{:S(2)}) async-start(bf16[4,256,256]{2,1,0:T(8,128)(2,1)} %get-tuple-element.17), calls=%async_computation.1 | async-start | bytes 1048576 | tf_op jit(solution)/shard_map/all_to_all | solution.py:251
  31.1 5.9 %collective-permute-start.4 = (bf16[256,256]{1,0:T(8,128)(2,1)S(1)}, bf16[256,256]{1,0:T(8,128)(2,1)S(1)}, u32[]{:S(2)}, u32[]{:S(2)}) collective-permute-start(bf16[256,256]{1,0:T(8,128)(2,1)S(1)} %get-tuple-element.18), channel_id=1, source_target_pairs={{0,16},{1,17},{2,18},{3,19},{16,0},{17,1},{18,2},{19,3},{4,20},{5,... | collective-permute-start | bytes 393224 | tf_op jit(solution)/shard_map/ppermute | solution.py:248
  32.0 11.6 %collective-permute-start.5 = (bf16[256,256]{1,0:T(8,128)(2,1)S(1)}, bf16[256,256]{1,0:T(8,128)(2,1)S(1)}, u32[]{:S(2)}, u32[]{:S(2)}) collective-permute-start(bf16[256,256]{1,0:T(8,128)(2,1)S(1)} %get-tuple-element.19), channel_id=1, source_target_pairs={{0,18},{1,19},{2,16},{3,17},{16,2},{17,3},{18,0},{19,1},{4,22},{5,... | collective-permute-start | bytes 393224 | tf_op jit(solution)/shard_map/ppermute | solution.py:248
  34.6 10.8 %collective-permute-start.6 = (bf16[256,256]{1,0:T(8,128)(2,1)S(1)}, bf16[256,256]{1,0:T(8,128)(2,1)S(1)}, u32[]{:S(2)}, u32[]{:S(2)}) collective-permute-start(bf16[256,256]{1,0:T(8,128)(2,1)S(1)} %get-tuple-element.20), channel_id=1, source_target_pairs={{0,19},{1,18},{2,17},{3,16},{16,3},{17,2},{18,1},{19,0},{4,23},{5,... | collective-permute-start | bytes 393224 | tf_op jit(solution)/shard_map/ppermute | solution.py:248
  34.6 10.8 %collective-permute-start.7 = (bf16[256,256]{1,0:T(8,128)(2,1)S(1)}, bf16[256,256]{1,0:T(8,128)(2,1)S(1)}, u32[]{:S(2)}, u32[]{:S(2)}) collective-permute-start(bf16[256,256]{1,0:T(8,128)(2,1)S(1)} %get-tuple-element.21), channel_id=1, source_target_pairs={{0,17},{1,16},{2,19},{3,18},{16,1},{17,0},{18,3},{19,2},{4,21},{5,... | collective-permute-start | bytes 393224 | tf_op jit(solution)/shard_map/ppermute | solution.py:248

commit v8 on v6

--- a/solution.py
+++ b/solution.py
@@ -256,7 +256,7 @@
     params = pltpu.CompilerParams(vmem_limit_bytes=VMEM_LIMIT)
     order, after = list(range(parts - 1, -1, -1)), {}
     if parts == 8:
-        order = [6, 7, 4, 5, 2, 3, 1, 0]
+        order = [1, 6, 4, 7, 2, 5, 3, 0]
     sems = pltpu.SemaphoreType.DMA((2, parts))
     shares = pl.pallas_call(
         functools.partial(pack_kernel, seq_count, order),

time: 38.6 us -> 39.7 us (1.028)
  starting transfers between devices: 14.1 us -> 14.9 us
  waiting for transfers between devices: 16 us -> 16.4 us
    ppermute x14, starting transfers between devices: 14.1 us -> 14.9 us  [swapped(): lax.ppermute(share, AXES, [(dev, dev ^ step) for dev in range(parts)])]
  transfers between devices with their start and end apart: 14 -> 14, of which waited for: 8 -> 9; matrix products, arithmetic and copies ran while one was open for 0% -> 0% of each run, Pallas kernels for 0% -> 0%
where the time goes in v8:
time: 39.7 us; the launch traced here: 39.5 us
  waiting for transfers between devices  16.4 us (41%)
  starting transfers between devices  14.9 us (38%)
  Pallas kernels  6.25 us (16%)
  between operations  1.96 us (5%)
    ppermute x14, waiting for transfers between devices, swapped(): lax.ppermute(share, AXES, [(dev, dev ^ step) for dev in range(parts)])  16.4 us
    ppermute x14, starting transfers between devices, swapped(): lax.ppermute(share, AXES, [(dev, dev ^ step) for dev in range(parts)])  14.9 us
    pallas_call x1, Pallas kernels, by_pairs(): pl.pallas_call(functools.partial(attend_kernel, seq_count, order), out_sh...  3.73 us
    pallas_call x1, Pallas kernels, by_pairs(): pl.pallas_call(functools.partial(pack_kernel, seq_count, order), out_shap...  1.43 us
    pallas_call x1, Pallas kernels, by_pairs(): pl.pallas_call(functools.partial(unpack_kernel, seq_count, order), out_sh...  1.09 us
  transfers between devices with their start and end apart: 14, of which 9 were waited for; matrix products, arithmetic and copies ran while one was open for 0% of the time, Pallas kernels for 0%

profile of v8, /device:TPU:0, one launch (start us, length us, event | category | flops | bytes accessed | tf_op | source)
XLA Modules:
  0.0 39.5 jit_solution(517637328006081617)
XLA Ops:
  0.6 1.4 %pack.1 = (bf16[272,256]{1,0:T(8,128)(2,1)S(1)}, bf16[272,256]{1,0:T(8,128)(2,1)S(1)}, bf16[272,256]{1,0:T(8,128)(2,1)S(1)}, bf16[272,256]{1,0:T(8,128)(2,1)S(1)...) custom-call(s32[1,1,2]{2,1,0:T(1,128)} %refs_0_.1, ...), custom_call_target="tpu_custom_call" | custom-call | tf_op jit(solution)/shard_map/pack/pallas_call | solution.py:261
  2.1 0.5 %collective-permute-start = (bf16[272,256]{1,0:T(8,128)(2,1)S(1)}, bf16[272,256]{1,0:T(8,128)(2,1)S(1)}, u32[]{:S(2)}, u32[]{:S(2)}) collective-permute-start(bf16[272,256]{1,0:T(8,128)(2,1)S(1)} %get-tuple-element.18), channel_id=1, source_target_pairs={{0,1},{1,0},{2,3},{3,2},{16,17},{17,16},{18,19},{19,18},{4,5},{5,4... | collective-permute-start | bytes 417800 | tf_op jit(solution)/shard_map/ppermute | solution.py:246
  2.6 3.5 %collective-permute-start.1 = (bf16[272,256]{1,0:T(8,128)(2,1)S(1)}, bf16[272,256]{1,0:T(8,128)(2,1)S(1)}, u32[]{:S(2)}, u32[]{:S(2)}) collective-permute-start(bf16[272,256]{1,0:T(8,128)(2,1)S(1)} %get-tuple-element.19), channel_id=1, source_target_pairs={{0,18},{1,19},{2,16},{3,17},{16,2},{17,3},{18,0},{19,1},{4,22},{5,... | collective-permute-start | bytes 417800 | tf_op jit(solution)/shard_map/ppermute | solution.py:246
  6.1 0.5 %collective-permute-start.2 = (bf16[272,256]{1,0:T(8,128)(2,1)S(1)}, bf16[272,256]{1,0:T(8,128)(2,1)S(1)}, u32[]{:S(2)}, u32[]{:S(2)}) collective-permute-start(bf16[272,256]{1,0:T(8,128)(2,1)S(1)} %get-tuple-element.20), channel_id=1, source_target_pairs={{0,16},{1,17},{2,18},{3,19},{16,0},{17,1},{18,2},{19,3},{4,20},{5,... | collective-permute-start | bytes 417800 | tf_op jit(solution)/shard_map/ppermute | solution.py:246
  6.6 1.0 %collective-permute-start.3 = (bf16[272,256]{1,0:T(8,128)(2,1)S(1)}, bf16[272,256]{1,0:T(8,128)(2,1)S(1)}, u32[]{:S(2)}, u32[]{:S(2)}) collective-permute-start(bf16[272,256]{1,0:T(8,128)(2,1)S(1)} %get-tuple-element.21), channel_id=1, source_target_pairs={{0,19},{1,18},{2,17},{3,16},{16,3},{17,2},{18,1},{19,0},{4,23},{5,... | collective-permute-start | bytes 417800 | tf_op jit(solution)/shard_map/ppermute | solution.py:246
  7.6 1.5 %collective-permute-start.4 = (bf16[272,256]{1,0:T(8,128)(2,1)S(1)}, bf16[272,256]{1,0:T(8,128)(2,1)S(1)}, u32[]{:S(2)}, u32[]{:S(2)}) collective-permute-start(bf16[272,256]{1,0:T(8,128)(2,1)S(1)} %get-tuple-element.22), channel_id=1, source_target_pairs={{0,2},{1,3},{2,0},{3,1},{16,18},{17,19},{18,16},{19,17},{4,6},{5,7... | collective-permute-start | bytes 417800 | tf_op jit(solution)/shard_map/ppermute | solution.py:246
  9.1 0.0 collective-permute-done.refs_0_
  9.1 0.5 %collective-permute-start.5 = (bf16[272,256]{1,0:T(8,128)(2,1)S(1)}, bf16[272,256]{1,0:T(8,128)(2,1)S(1)}, u32[]{:S(2)}, u32[]{:S(2)}) collective-permute-start(bf16[272,256]{1,0:T(8,128)(2,1)S(1)} %get-tuple-element.23), channel_id=1, source_target_pairs={{0,17},{1,16},{2,19},{3,18},{16,1},{17,0},{18,3},{19,2},{4,21},{5,... | collective-permute-start | bytes 417800 | tf_op jit(solution)/shard_map/ppermute | solution.py:246
  9.6 0.9 %collective-permute-done.1.refs_1_ = bf16[272,256]{1,0:T(8,128)(2,1)S(1)} collective-permute-done((bf16[272,256]{1,0:T(8,128)(2,1)S(1)}, bf16[272,256]{1,0:T(8,128)(2,1)S(1)}, u32[]{:S(2)}, u32[]{:S(2)}) %collective-permute-start.1) | collective-permute-done | bytes 139296 | tf_op jit(solution)/shard_map/ppermute | solution.py:246
  10.5 0.9 %collective-permute-start.6 = (bf16[272,256]{1,0:T(8,128)(2,1)S(1)}, bf16[272,256]{1,0:T(8,128)(2,1)S(1)}, u32[]{:S(2)}, u32[]{:S(2)}) collective-permute-start(bf16[272,256]{1,0:T(8,128)(2,1)S(1)} %get-tuple-element.24), channel_id=1, source_target_pairs={{0,3},{1,2},{2,1},{3,0},{16,19},{17,18},{18,17},{19,16},{4,7},{5,6... | collective-permute-start | bytes 417800 | tf_op jit(solution)/shard_map/ppermute | solution.py:246
  12.7 3.7 %collective-permute-done.2.refs_2_ = bf16[272,256]{1,0:T(8,128)(2,1)S(1)} collective-permute-done((bf16[272,256]{1,0:T(8,128)(2,1)S(1)}, bf16[272,256]{1,0:T(8,128)(2,1)S(1)}, u32[]{:S(2)}, u32[]{:S(2)}) %collective-permute-start.2) | collective-permute-done | bytes 139296 | tf_op jit(solution)/shard_map/ppermute | solution.py:246
  16.4 0.0 collective-permute-done.3.refs_3_
  16.4 0.3 collective-permute-done.4.refs_4_
  16.7 2.5 %collective-permute-done.5.refs_5_ = bf16[272,256]{1,0:T(8,128)(2,1)S(1)} collective-permute-done((bf16[272,256]{1,0:T(8,128)(2,1)S(1)}, bf16[272,256]{1,0:T(8,128)(2,1)S(1)}, u32[]{:S(2)}, u32[]{:S(2)}) %collective-permute-start.5) | collective-permute-done | bytes 139296 | tf_op jit(solution)/shard_map/ppermute | solution.py:246
  19.3 0.3 collective-permute-done.6.refs_6_
  19.6 3.7 %attend.1 = (bf16[256,256]{1,0:T(8,128)(2,1)S(1)}, bf16[256,256]{1,0:T(8,128)(2,1)S(1)}, bf16[256,256]{1,0:T(8,128)(2,1)S(1)}, bf16[256,256]{1,0:T(8,128)(2,1)S(...) custom-call(s32[1]{0:T(128)S(6)} %copy.8.source_len, ...), custom_call_target="tpu_custom_call" | custom-call | flops 335544320 | bytes 2097152 | tf_op jit(solution)/shard_map/attend/pallas_call | solution.py:278
  23.3 0.2 collective-permute-start.7
  23.5 1.2 %collective-permute-start.8 = (bf16[256,256]{1,0:T(8,128)(2,1)S(1)}, bf16[256,256]{1,0:T(8,128)(2,1)S(1)}, u32[]{:S(2)}, u32[]{:S(2)}) collective-permute-start(bf16[256,256]{1,0:T(8,128)(2,1)S(1)} %get-tuple-element.27), channel_id=1, source_target_pairs={{0,18},{1,19},{2,16},{3,17},{16,2},{17,3},{18,0},{19,1},{4,22},{5,... | collective-permute-start | bytes 393224 | tf_op jit(solution)/shard_map/ppermute | solution.py:246
  24.7 1.6 %collective-permute-start.9 = (bf16[256,256]{1,0:T(8,128)(2,1)S(1)}, bf16[256,256]{1,0:T(8,128)(2,1)S(1)}, u32[]{:S(2)}, u32[]{:S(2)}) collective-permute-start(bf16[256,256]{1,0:T(8,128)(2,1)S(1)} %get-tuple-element.28), channel_id=1, source_target_pairs={{0,16},{1,17},{2,18},{3,19},{16,0},{17,1},{18,2},{19,3},{4,20},{5,... | collective-permute-start | bytes 393224 | tf_op jit(solution)/shard_map/ppermute | solution.py:246
  26.3 1.0 %collective-permute-start.10 = (bf16[256,256]{1,0:T(8,128)(2,1)S(1)}, bf16[256,256]{1,0:T(8,128)(2,1)S(1)}, u32[]{:S(2)}, u32[]{:S(2)}) collective-permute-start(bf16[256,256]{1,0:T(8,128)(2,1)S(1)} %get-tuple-element.29), channel_id=1, source_target_pairs={{0,19},{1,18},{2,17},{3,16},{16,3},{17,2},{18,1},{19,0},{4,23},{5,... | collective-permute-start | bytes 393224 | tf_op jit(solution)/shard_map/ppermute | solution.py:246
  27.3 0.3 collective-permute-start.11
  27.6 0.0 collective-permute-done.7.refs_0_
  27.6 1.7 %collective-permute-start.12 = (bf16[256,256]{1,0:T(8,128)(2,1)S(1)}, bf16[256,256]{1,0:T(8,128)(2,1)S(1)}, u32[]{:S(2)}, u32[]{:S(2)}) collective-permute-start(bf16[256,256]{1,0:T(8,128)(2,1)S(1)} %get-tuple-element.31), channel_id=1, source_target_pairs={{0,17},{1,16},{2,19},{3,18},{16,1},{17,0},{18,3},{19,2},{4,21},{5,... | collective-permute-start | bytes 393224 | tf_op jit(solution)/shard_map/ppermute | solution.py:246
  29.3 1.0 %collective-permute-done.8.refs_1_ = bf16[256,256]{1,0:T(8,128)(2,1)S(1)} collective-permute-done((bf16[256,256]{1,0:T(8,128)(2,1)S(1)}, bf16[256,256]{1,0:T(8,128)(2,1)S(1)}, u32[]{:S(2)}, u32[]{:S(2)}) %collective-permute-start.8) | collective-permute-done | bytes 131104 | tf_op jit(solution)/shard_map/ppermute | solution.py:246
  30.3 0.6 %collective-permute-start.13 = (bf16[256,256]{1,0:T(8,128)(2,1)S(1)}, bf16[256,256]{1,0:T(8,128)(2,1)S(1)}, u32[]{:S(2)}, u32[]{:S(2)}) collective-permute-start(bf16[256,256]{1,0:T(8,128)(2,1)S(1)} %get-tuple-element.32), channel_id=1, source_target_pairs={{0,3},{1,2},{2,1},{3,0},{16,19},{17,18},{18,17},{19,16},{4,7},{5,6... | collective-permute-start | bytes 393224 | tf_op jit(solution)/shard_map/ppermute | solution.py:246
  30.9 5.0 %collective-permute-done.9.refs_2_ = bf16[256,256]{1,0:T(8,128)(2,1)S(1)} collective-permute-done((bf16[256,256]{1,0:T(8,128)(2,1)S(1)}, bf16[256,256]{1,0:T(8,128)(2,1)S(1)}, u32[]{:S(2)}, u32[]{:S(2)}) %collective-permute-start.9) | collective-permute-done | bytes 131104 | tf_op jit(solution)/shard_map/ppermute | solution.py:246
  35.9 0.0 collective-permute-done.10.refs_3_
  35.9 0.4 %collective-permute-done.11.refs_4_ = bf16[256,256]{1,0:T(8,128)(2,1)S(1)} collective-permute-done((bf16[256,256]{1,0:T(8,128)(2,1)S(1)}, bf16[256,256]{1,0:T(8,128)(2,1)S(1)}, u32[]{:S(2)}, u32[]{:S(2)}) %collective-permute-start.11) | collective-permute-done | bytes 131104 | tf_op jit(solution)/shard_map/ppermute | solution.py:246
  36.3 2.1 %collective-permute-done.12.refs_5_ = bf16[256,256]{1,0:T(8,128)(2,1)S(1)} collective-permute-done((bf16[256,256]{1,0:T(8,128)(2,1)S(1)}, bf16[256,256]{1,0:T(8,128)(2,1)S(1)}, u32[]{:S(2)}, u32[]{:S(2)}) %collective-permute-start.12) | collective-permute-done | bytes 131104 | tf_op jit(solution)/shard_map/ppermute | solution.py:246
  38.4 0.0 collective-permute-done.13.refs_6_
  38.4 1.1 %unpack.1 = (bf16[1,1,128,2048]{3,2,1,0:T(8,128)(2,1)}, bf16[1,1,128,2048]{3,2,1,0:T(8,128)(2,1)}) custom-call(bf16[256,256]{1,0:T(8,128)(2,1)S(1)} %collective-permute-done.7.refs_0_, bf16[256,256]{1,0:T(8,128)(2,1)S(1)} %collective-permute-done.8.refs_1_, bf16[256,256]{1,0:T(8,128)(2,1)S(1)} %collective-permute-done.9.refs_2_, ...), custom_call_target="tpu_custom_call" | custom-call | tf_op jit(solution)/shard_map/unpack/pallas_call | solution.py:290
Async XLA Ops:
  2.1 7.0 %collective-permute-start = (bf16[272,256]{1,0:T(8,128)(2,1)S(1)}, bf16[272,256]{1,0:T(8,128)(2,1)S(1)}, u32[]{:S(2)}, u32[]{:S(2)}) collective-permute-start(bf16[272,256]{1,0:T(8,128)(2,1)S(1)} %get-tuple-element.18), channel_id=1, source_target_pairs={{0,1},{1,0},{2,3},{3,2},{16,17},{17,16},{18,19},{19,18},{4,5},{5,4... | collective-permute-start | bytes 417800 | tf_op jit(solution)/shard_map/ppermute | solution.py:246
  2.6 7.9 %collective-permute-start.1 = (bf16[272,256]{1,0:T(8,128)(2,1)S(1)}, bf16[272,256]{1,0:T(8,128)(2,1)S(1)}, u32[]{:S(2)}, u32[]{:S(2)}) collective-permute-start(bf16[272,256]{1,0:T(8,128)(2,1)S(1)} %get-tuple-element.19), channel_id=1, source_target_pairs={{0,18},{1,19},{2,16},{3,17},{16,2},{17,3},{18,0},{19,1},{4,22},{5,... | collective-permute-start | bytes 417800 | tf_op jit(solution)/shard_map/ppermute | solution.py:246
  6.1 10.3 %collective-permute-start.2 = (bf16[272,256]{1,0:T(8,128)(2,1)S(1)}, bf16[272,256]{1,0:T(8,128)(2,1)S(1)}, u32[]{:S(2)}, u32[]{:S(2)}) collective-permute-start(bf16[272,256]{1,0:T(8,128)(2,1)S(1)} %get-tuple-element.20), channel_id=1, source_target_pairs={{0,16},{1,17},{2,18},{3,19},{16,0},{17,1},{18,2},{19,3},{4,20},{5,... | collective-permute-start | bytes 417800 | tf_op jit(solution)/shard_map/ppermute | solution.py:246
  6.6 9.8 %collective-permute-start.3 = (bf16[272,256]{1,0:T(8,128)(2,1)S(1)}, bf16[272,256]{1,0:T(8,128)(2,1)S(1)}, u32[]{:S(2)}, u32[]{:S(2)}) collective-permute-start(bf16[272,256]{1,0:T(8,128)(2,1)S(1)} %get-tuple-element.21), channel_id=1, source_target_pairs={{0,19},{1,18},{2,17},{3,16},{16,3},{17,2},{18,1},{19,0},{4,23},{5,... | collective-permute-start | bytes 417800 | tf_op jit(solution)/shard_map/ppermute | solution.py:246
  7.6 9.1 %collective-permute-start.4 = (bf16[272,256]{1,0:T(8,128)(2,1)S(1)}, bf16[272,256]{1,0:T(8,128)(2,1)S(1)}, u32[]{:S(2)}, u32[]{:S(2)}) collective-permute-start(bf16[272,256]{1,0:T(8,128)(2,1)S(1)} %get-tuple-element.22), channel_id=1, source_target_pairs={{0,2},{1,3},{2,0},{3,1},{16,18},{17,19},{18,16},{19,17},{4,6},{5,7... | collective-permute-start | bytes 417800 | tf_op jit(solution)/shard_map/ppermute | solution.py:246
  9.1 10.2 %collective-permute-start.5 = (bf16[272,256]{1,0:T(8,128)(2,1)S(1)}, bf16[272,256]{1,0:T(8,128)(2,1)S(1)}, u32[]{:S(2)}, u32[]{:S(2)}) collective-permute-start(bf16[272,256]{1,0:T(8,128)(2,1)S(1)} %get-tuple-element.23), channel_id=1, source_target_pairs={{0,17},{1,16},{2,19},{3,18},{16,1},{17,0},{18,3},{19,2},{4,21},{5,... | collective-permute-start | bytes 417800 | tf_op jit(solution)/shard_map/ppermute | solution.py:246
  10.5 9.1 %collective-permute-start.6 = (bf16[272,256]{1,0:T(8,128)(2,1)S(1)}, bf16[272,256]{1,0:T(8,128)(2,1)S(1)}, u32[]{:S(2)}, u32[]{:S(2)}) collective-permute-start(bf16[272,256]{1,0:T(8,128)(2,1)S(1)} %get-tuple-element.24), channel_id=1, source_target_pairs={{0,3},{1,2},{2,1},{3,0},{16,19},{17,18},{18,17},{19,16},{4,7},{5,6... | collective-permute-start | bytes 417800 | tf_op jit(solution)/shard_map/ppermute | solution.py:246
  23.3 4.2 %collective-permute-start.7 = (bf16[256,256]{1,0:T(8,128)(2,1)S(1)}, bf16[256,256]{1,0:T(8,128)(2,1)S(1)}, u32[]{:S(2)}, u32[]{:S(2)}) collective-permute-start(bf16[256,256]{1,0:T(8,128)(2,1)S(1)} %get-tuple-element.26), channel_id=1, source_target_pairs={{0,1},{1,0},{2,3},{3,2},{16,17},{17,16},{18,19},{19,18},{4,5},{5,4... | collective-permute-start | bytes 393224 | tf_op jit(solution)/shard_map/ppermute | solution.py:246
  23.5 6.8 %collective-permute-start.8 = (bf16[256,256]{1,0:T(8,128)(2,1)S(1)}, bf16[256,256]{1,0:T(8,128)(2,1)S(1)}, u32[]{:S(2)}, u32[]{:S(2)}) collective-permute-start(bf16[256,256]{1,0:T(8,128)(2,1)S(1)} %get-tuple-element.27), channel_id=1, source_target_pairs={{0,18},{1,19},{2,16},{3,17},{16,2},{17,3},{18,0},{19,1},{4,22},{5,... | collective-permute-start | bytes 393224 | tf_op jit(solution)/shard_map/ppermute | solution.py:246
  24.7 11.2 %collective-permute-start.9 = (bf16[256,256]{1,0:T(8,128)(2,1)S(1)}, bf16[256,256]{1,0:T(8,128)(2,1)S(1)}, u32[]{:S(2)}, u32[]{:S(2)}) collective-permute-start(bf16[256,256]{1,0:T(8,128)(2,1)S(1)} %get-tuple-element.28), channel_id=1, source_target_pairs={{0,16},{1,17},{2,18},{3,19},{16,0},{17,1},{18,2},{19,3},{4,20},{5,... | collective-permute-start | bytes 393224 | tf_op jit(solution)/shard_map/ppermute | solution.py:246
  26.3 9.6 %collective-permute-start.10 = (bf16[256,256]{1,0:T(8,128)(2,1)S(1)}, bf16[256,256]{1,0:T(8,128)(2,1)S(1)}, u32[]{:S(2)}, u32[]{:S(2)}) collective-permute-start(bf16[256,256]{1,0:T(8,128)(2,1)S(1)} %get-tuple-element.29), channel_id=1, source_target_pairs={{0,19},{1,18},{2,17},{3,16},{16,3},{17,2},{18,1},{19,0},{4,23},{5,... | collective-permute-start | bytes 393224 | tf_op jit(solution)/shard_map/ppermute | solution.py:246
  27.3 9.0 %collective-permute-start.11 = (bf16[256,256]{1,0:T(8,128)(2,1)S(1)}, bf16[256,256]{1,0:T(8,128)(2,1)S(1)}, u32[]{:S(2)}, u32[]{:S(2)}) collective-permute-start(bf16[256,256]{1,0:T(8,128)(2,1)S(1)} %get-tuple-element.30), channel_id=1, source_target_pairs={{0,2},{1,3},{2,0},{3,1},{16,18},{17,19},{18,16},{19,17},{4,6},{5,7... | collective-permute-start | bytes 393224 | tf_op jit(solution)/shard_map/ppermute | solution.py:246
  27.6 10.9 %collective-permute-start.12 = (bf16[256,256]{1,0:T(8,128)(2,1)S(1)}, bf16[256,256]{1,0:T(8,128)(2,1)S(1)}, u32[]{:S(2)}, u32[]{:S(2)}) collective-permute-start(bf16[256,256]{1,0:T(8,128)(2,1)S(1)} %get-tuple-element.31), channel_id=1, source_target_pairs={{0,17},{1,16},{2,19},{3,18},{16,1},{17,0},{18,3},{19,2},{4,21},{5,... | collective-permute-start | bytes 393224 | tf_op jit(solution)/shard_map/ppermute | solution.py:246
  30.3 8.1 %collective-permute-start.13 = (bf16[256,256]{1,0:T(8,128)(2,1)S(1)}, bf16[256,256]{1,0:T(8,128)(2,1)S(1)}, u32[]{:S(2)}, u32[]{:S(2)}) collective-permute-start(bf16[256,256]{1,0:T(8,128)(2,1)S(1)} %get-tuple-element.32), channel_id=1, source_target_pairs={{0,3},{1,2},{2,1},{3,0},{16,19},{17,18},{18,17},{19,16},{4,7},{5,6... | collective-permute-start | bytes 393224 | tf_op jit(solution)/shard_map/ppermute | solution.py:246

commit v9 on v6

--- a/solution.py
+++ b/solution.py
@@ -26,7 +26,9 @@
     )
 
 
-def attend_sample(seq_count, listed, source_len, target_len, rows, out, key_grad, value_grad):
+def attend_sample(
+    seq_count, listed, source_len, target_len, rows, out, key_grad, value_grad, turned
+):
     per_device = rows.shape[2] // BLK
     block_count = seq_count * per_device
     width = rows.shape[3]
@@ -41,6 +43,24 @@
         if per_device == 1:
             return block, pl.ds(0, BLK)
         return block // per_device, pl.ds((block % per_device) * BLK, BLK)
+
+    def own_heads(turned_result):
+        return jnp.concatenate(
+            [
+                turned_result[head * HDIM : (head + 1) * HDIM, head * BLK : (head + 1) * BLK]
+                for head in range(heads)
+            ],
+            axis=0,
+        )
+
+    def turn(block, carry):
+        dev, here = place(block)
+        for first in range(0, width, tile):
+            for half in range(2):
+                turned[block, half, pl.ds(first, tile)] = rows[
+                    dev, half, here, pl.ds(first, tile)
+                ].T
+        return carry
 
     def step(block, carry):
         chosen = [listed(block, slot) for slot in range(NLIST)]
@@ -73,21 +93,20 @@
             dscore_low = (probs * (dprob - delta)).astype(jnp.bfloat16)
             dvalue = contract(probs_low, cots, 1, 0)
             dkey = contract(dscore_low, queries, 1, 0)
-            attended = contract(probs_low, values, 0, 0)
-            dquery = contract(dscore_low, keys, 0, 0)
-            for head in range(1, heads):
-                mine = lane_head == head
-                attended = jnp.where(mine, attended[head * BLK : (head + 1) * BLK], attended[:BLK])
-                dquery = jnp.where(mine, dquery[head * BLK : (head + 1) * BLK], dquery[:BLK])
-            attended = jnp.where(live, attended, 0.0)
-            out[seq_count + target, 0, target_rows, lanes] = (dquery * SCALE).astype(jnp.bfloat16)
-            out[seq_count + target, 1, target_rows, lanes] = attended.astype(jnp.bfloat16)
+            keys_turned = jnp.concatenate([turned[index, 0, lanes] for index in chosen], axis=1)
+            values_turned = jnp.concatenate([turned[index, 1, lanes] for index in chosen], axis=1)
+            attended = own_heads(contract(values_turned, probs_low, 1, 0))
+            dquery = own_heads(contract(keys_turned, dscore_low, 1, 0)) * SCALE
+            attended = jnp.where(live, attended.astype(jnp.bfloat16).T, none)
+            out[seq_count + target, 0, target_rows, lanes] = dquery.astype(jnp.bfloat16).T
+            out[seq_count + target, 1, target_rows, lanes] = attended
             for slot, (dev, here) in enumerate(places):
                 part = slice(slot * BLK, (slot + 1) * BLK)
                 key_grad[dev, here, lanes] += dkey[part]
                 value_grad[dev, here, lanes] += dvalue[part]
         return carry
 
+    lax.fori_loop(0, block_count, turn, 0, unroll=block_count <= 4)
     lax.fori_loop(0, block_count, step, 0, unroll=block_count <= 4)
     out[:seq_count, 0] = key_grad[...].astype(jnp.bfloat16)
     out[:seq_count, 1] = value_grad[...].astype(jnp.bfloat16)
@@ -110,12 +129,14 @@
     return [pltpu.with_memory_space_constraint(array, pltpu.HBM) for array in arrays]
 
 
-def gathered_kernel(seq_count, lists, source_len, target_len, rows, out, key_grad, value_grad):
+def gathered_kernel(
+    seq_count, lists, source_len, target_len, rows, out, key_grad, value_grad, turned
+):
     def listed(block, slot):
         return lists[block, slot]
 
     attend_sample(
-        seq_count, listed, source_len[0], target_len[0], rows, out, key_grad, value_grad
+        seq_count, listed, source_len[0], target_len[0], rows, out, key_grad, value_grad, turned
     )
 
 
@@ -132,12 +153,13 @@
     lists = lax.all_gather(alignment[0], "seq", axis=0, tiled=True)
     rows = lax.all_to_all(held, AXES, 0, 0, tiled=True)
     grads = pltpu.VMEM((seq_count, rows_here, width // parts), jnp.float32)
+    turned = pltpu.VMEM((lists.shape[0], 2, width // parts, BLK), rows.dtype)
     grads = pl.pallas_call(
         functools.partial(gathered_kernel, seq_count),
         out_shape=jax.ShapeDtypeStruct(rows.shape, rows.dtype),
         in_specs=specs(3, pltpu.SMEM) + specs(1, pltpu.VMEM),
         out_specs=pl.BlockSpec(memory_space=pltpu.VMEM),
-        scratch_shapes=[grads, grads],
+        scratch_shapes=[grads, grads, turned],
         compiler_params=pltpu.CompilerParams(vmem_limit_bytes=VMEM_LIMIT),
         cost_estimate=attend_cost(lists.shape[0], width // parts),
         name="attend_gathered",
@@ -193,7 +215,7 @@
 def attend_kernel(seq_count, order, source_len, target_len, *refs):
     parts = 2 * seq_count
     shares, outs = refs[:parts], refs[parts : 2 * parts]
-    rows, result, key_grad, value_grad, lists = refs[2 * parts :]
+    rows, result, key_grad, value_grad, turned, lists = refs[2 * parts :]
     me = device_index(seq_count)
     here = me % seq_count
     for step, share in zip(order, shares):
@@ -209,7 +231,15 @@
         return block - WIN + (code // SPAN if slot == 0 else code % SPAN)
 
     attend_sample(
-        seq_count, listed, source_len[0], target_len[0], rows, result, key_grad, value_grad
+        seq_count,
+        listed,
+        source_len[0],
+        target_len[0],
+        rows,
+        result,
+        key_grad,
+        value_grad,
+        turned,
     )
     for step, out in zip(order, outs):
         out[:BLK] = result[me ^ step, 0]
@@ -275,12 +305,13 @@
     shares = swapped(shares, order, after)
     rows = pltpu.VMEM((parts, 2, BLK, share), kind)
     grads = pltpu.VMEM((seq_count, BLK, share), jnp.float32)
+    turned = pltpu.VMEM((seq_count, 2, share, BLK), kind)
     shares = pl.pallas_call(
         functools.partial(attend_kernel, seq_count, order),
         out_shape=[jax.ShapeDtypeStruct((2 * BLK, share), kind)] * parts,
         in_specs=specs(2, pltpu.SMEM) + specs(parts, pltpu.VMEM),
         out_specs=specs(parts, pltpu.VMEM),
-        scratch_shapes=[rows, rows, grads, grads, pltpu.SMEM((seq_count,), jnp.int32)],
+        scratch_shapes=[rows, rows, grads, grads, turned, pltpu.SMEM((seq_count,), jnp.int32)],
         compiler_params=params,
         cost_estimate=attend_cost(seq_count, share),
         name="attend",

time: 38.6 us -> 38.5 us (level)
  no operation moved by 1% of the time
where the time goes in v9:
time: 38.5 us; the launch traced here: 38.3 us
  waiting for transfers between devices  16 us (42%)
  starting transfers between devices  14.1 us (37%)
  Pallas kernels  6.15 us (16%)
  between operations  1.97 us (5%)
    ppermute x14, waiting for transfers between devices, swapped(): lax.ppermute(share, AXES, [(dev, dev ^ step) for dev in range(parts)])  16 us
    ppermute x14, starting transfers between devices, swapped(): lax.ppermute(share, AXES, [(dev, dev ^ step) for dev in range(parts)])  14.1 us
    pallas_call x1, Pallas kernels, by_pairs(): pl.pallas_call(functools.partial(attend_kernel, seq_count, order), out_sh...  3.61 us
    pallas_call x1, Pallas kernels, by_pairs(): pl.pallas_call(functools.partial(pack_kernel, seq_count, order), out_shap...  1.43 us
    pallas_call x1, Pallas kernels, by_pairs(): pl.pallas_call(functools.partial(unpack_kernel, seq_count, order), out_sh...  1.1 us
  transfers between devices with their start and end apart: 14, of which 8 were waited for; matrix products, arithmetic and copies ran while one was open for 0% of the time, Pallas kernels for 0%

profile of v9, /device:TPU:0, one launch (start us, length us, event | category | flops | bytes accessed | tf_op | source)
XLA Modules:
  0.0 38.3 jit_solution(1954792345004512431)
XLA Ops:
  0.6 1.4 %pack.1 = (bf16[272,256]{1,0:T(8,128)(2,1)S(1)}, bf16[272,256]{1,0:T(8,128)(2,1)S(1)}, bf16[272,256]{1,0:T(8,128)(2,1)S(1)}, bf16[272,256]{1,0:T(8,128)(2,1)S(1)...) custom-call(s32[1,1,2]{2,1,0:T(1,128)} %refs_0_.1, ...), custom_call_target="tpu_custom_call" | custom-call | tf_op jit(solution)/shard_map/pack/pallas_call | solution.py:291
  2.1 4.0 %collective-permute-start = (bf16[272,256]{1,0:T(8,128)(2,1)S(1)}, bf16[272,256]{1,0:T(8,128)(2,1)S(1)}, u32[]{:S(2)}, u32[]{:S(2)}) collective-permute-start(bf16[272,256]{1,0:T(8,128)(2,1)S(1)} %get-tuple-element.18), channel_id=1, source_target_pairs={{0,18},{1,19},{2,16},{3,17},{16,2},{17,3},{18,0},{19,1},{4,22},{5,... | collective-permute-start | bytes 417800 | tf_op jit(solution)/shard_map/ppermute | solution.py:276
  6.0 0.0 collective-permute-start.1
  6.0 1.2 %collective-permute-start.2 = (bf16[272,256]{1,0:T(8,128)(2,1)S(1)}, bf16[272,256]{1,0:T(8,128)(2,1)S(1)}, u32[]{:S(2)}, u32[]{:S(2)}) collective-permute-start(bf16[272,256]{1,0:T(8,128)(2,1)S(1)} %get-tuple-element.20), channel_id=1, source_target_pairs={{0,16},{1,17},{2,18},{3,19},{16,0},{17,1},{18,2},{19,3},{4,20},{5,... | collective-permute-start | bytes 417800 | tf_op jit(solution)/shard_map/ppermute | solution.py:276
  7.2 0.6 %collective-permute-start.3 = (bf16[272,256]{1,0:T(8,128)(2,1)S(1)}, bf16[272,256]{1,0:T(8,128)(2,1)S(1)}, u32[]{:S(2)}, u32[]{:S(2)}) collective-permute-start(bf16[272,256]{1,0:T(8,128)(2,1)S(1)} %get-tuple-element.21), channel_id=1, source_target_pairs={{0,17},{1,16},{2,19},{3,18},{16,1},{17,0},{18,3},{19,2},{4,21},{5,... | collective-permute-start | bytes 417800 | tf_op jit(solution)/shard_map/ppermute | solution.py:276
  7.8 1.7 %collective-permute-start.4 = (bf16[272,256]{1,0:T(8,128)(2,1)S(1)}, bf16[272,256]{1,0:T(8,128)(2,1)S(1)}, u32[]{:S(2)}, u32[]{:S(2)}) collective-permute-start(bf16[272,256]{1,0:T(8,128)(2,1)S(1)} %get-tuple-element.22), channel_id=1, source_target_pairs={{0,2},{1,3},{2,0},{3,1},{16,18},{17,19},{18,16},{19,17},{4,6},{5,7... | collective-permute-start | bytes 417800 | tf_op jit(solution)/shard_map/ppermute | solution.py:276
  9.5 0.7 %collective-permute-done.refs_0_ = bf16[272,256]{1,0:T(8,128)(2,1)S(1)} collective-permute-done((bf16[272,256]{1,0:T(8,128)(2,1)S(1)}, bf16[272,256]{1,0:T(8,128)(2,1)S(1)}, u32[]{:S(2)}, u32[]{:S(2)}) %collective-permute-start) | collective-permute-done | bytes 139296 | tf_op jit(solution)/shard_map/ppermute | solution.py:276
  10.1 0.0 collective-permute-start.5
  10.2 3.0 %collective-permute-done.1.refs_1_ = bf16[272,256]{1,0:T(8,128)(2,1)S(1)} collective-permute-done((bf16[272,256]{1,0:T(8,128)(2,1)S(1)}, bf16[272,256]{1,0:T(8,128)(2,1)S(1)}, u32[]{:S(2)}, u32[]{:S(2)}) %collective-permute-start.1) | collective-permute-done | bytes 139296 | tf_op jit(solution)/shard_map/ppermute | solution.py:276
  13.1 0.0 collective-permute-start.6
  14.4 1.3 %collective-permute-done.2.refs_2_ = bf16[272,256]{1,0:T(8,128)(2,1)S(1)} collective-permute-done((bf16[272,256]{1,0:T(8,128)(2,1)S(1)}, bf16[272,256]{1,0:T(8,128)(2,1)S(1)}, u32[]{:S(2)}, u32[]{:S(2)}) %collective-permute-start.2) | collective-permute-done | bytes 139296 | tf_op jit(solution)/shard_map/ppermute | solution.py:276
  15.7 2.9 %collective-permute-done.3.refs_3_ = bf16[272,256]{1,0:T(8,128)(2,1)S(1)} collective-permute-done((bf16[272,256]{1,0:T(8,128)(2,1)S(1)}, bf16[272,256]{1,0:T(8,128)(2,1)S(1)}, u32[]{:S(2)}, u32[]{:S(2)}) %collective-permute-start.3) | collective-permute-done | bytes 139296 | tf_op jit(solution)/shard_map/ppermute | solution.py:276
  18.6 0.0 collective-permute-done.4.refs_4_
  18.6 0.0 collective-permute-done.5.refs_5_
  18.6 0.0 collective-permute-done.6.refs_6_
  18.6 3.6 %attend.1 = (bf16[256,256]{1,0:T(8,128)(2,1)S(1)}, bf16[256,256]{1,0:T(8,128)(2,1)S(1)}, bf16[256,256]{1,0:T(8,128)(2,1)S(1)}, bf16[256,256]{1,0:T(8,128)(2,1)S(...) custom-call(s32[1]{0:T(128)S(6)} %copy.8.source_len, ...), custom_call_target="tpu_custom_call" | custom-call | flops 335544320 | bytes 2097152 | tf_op jit(solution)/shard_map/attend/pallas_call | solution.py:309
  22.2 2.8 %collective-permute-start.7 = (bf16[256,256]{1,0:T(8,128)(2,1)S(1)}, bf16[256,256]{1,0:T(8,128)(2,1)S(1)}, u32[]{:S(2)}, u32[]{:S(2)}) collective-permute-start(bf16[256,256]{1,0:T(8,128)(2,1)S(1)} %get-tuple-element.26), channel_id=1, source_target_pairs={{0,18},{1,19},{2,16},{3,17},{16,2},{17,3},{18,0},{19,1},{4,22},{5,... | collective-permute-start | bytes 393224 | tf_op jit(solution)/shard_map/ppermute | solution.py:276
  25.0 0.0 collective-permute-start.8
  25.0 1.4 %collective-permute-start.9 = (bf16[256,256]{1,0:T(8,128)(2,1)S(1)}, bf16[256,256]{1,0:T(8,128)(2,1)S(1)}, u32[]{:S(2)}, u32[]{:S(2)}) collective-permute-start(bf16[256,256]{1,0:T(8,128)(2,1)S(1)} %get-tuple-element.28), channel_id=1, source_target_pairs={{0,16},{1,17},{2,18},{3,19},{16,0},{17,1},{18,2},{19,3},{4,20},{5,... | collective-permute-start | bytes 393224 | tf_op jit(solution)/shard_map/ppermute | solution.py:276
  26.4 0.3 collective-permute-start.10
  26.8 1.7 %collective-permute-start.11 = (bf16[256,256]{1,0:T(8,128)(2,1)S(1)}, bf16[256,256]{1,0:T(8,128)(2,1)S(1)}, u32[]{:S(2)}, u32[]{:S(2)}) collective-permute-start(bf16[256,256]{1,0:T(8,128)(2,1)S(1)} %get-tuple-element.30), channel_id=1, source_target_pairs={{0,2},{1,3},{2,0},{3,1},{16,18},{17,19},{18,16},{19,17},{4,6},{5,7... | collective-permute-start | bytes 393224 | tf_op jit(solution)/shard_map/ppermute | solution.py:276
  28.5 0.4 %collective-permute-done.7.refs_0_ = bf16[256,256]{1,0:T(8,128)(2,1)S(1)} collective-permute-done((bf16[256,256]{1,0:T(8,128)(2,1)S(1)}, bf16[256,256]{1,0:T(8,128)(2,1)S(1)}, u32[]{:S(2)}, u32[]{:S(2)}) %collective-permute-start.7) | collective-permute-done | bytes 131104 | tf_op jit(solution)/shard_map/ppermute | solution.py:276
  28.9 0.4 %collective-permute-start.12 = (bf16[256,256]{1,0:T(8,128)(2,1)S(1)}, bf16[256,256]{1,0:T(8,128)(2,1)S(1)}, u32[]{:S(2)}, u32[]{:S(2)}) collective-permute-start(bf16[256,256]{1,0:T(8,128)(2,1)S(1)} %get-tuple-element.31), channel_id=1, source_target_pairs={{0,3},{1,2},{2,1},{3,0},{16,19},{17,18},{18,17},{19,16},{4,7},{5,6... | collective-permute-start | bytes 393224 | tf_op jit(solution)/shard_map/ppermute | solution.py:276
  29.3 2.4 %collective-permute-done.8.refs_1_ = bf16[256,256]{1,0:T(8,128)(2,1)S(1)} collective-permute-done((bf16[256,256]{1,0:T(8,128)(2,1)S(1)}, bf16[256,256]{1,0:T(8,128)(2,1)S(1)}, u32[]{:S(2)}, u32[]{:S(2)}) %collective-permute-start.8) | collective-permute-done | bytes 131104 | tf_op jit(solution)/shard_map/ppermute | solution.py:276
  31.8 0.1 collective-permute-start.13
  31.8 2.6 %collective-permute-done.9.refs_2_ = bf16[256,256]{1,0:T(8,128)(2,1)S(1)} collective-permute-done((bf16[256,256]{1,0:T(8,128)(2,1)S(1)}, bf16[256,256]{1,0:T(8,128)(2,1)S(1)}, u32[]{:S(2)}, u32[]{:S(2)}) %collective-permute-start.9) | collective-permute-done | bytes 131104 | tf_op jit(solution)/shard_map/ppermute | solution.py:276
  34.4 2.7 %collective-permute-done.10.refs_3_ = bf16[256,256]{1,0:T(8,128)(2,1)S(1)} collective-permute-done((bf16[256,256]{1,0:T(8,128)(2,1)S(1)}, bf16[256,256]{1,0:T(8,128)(2,1)S(1)}, u32[]{:S(2)}, u32[]{:S(2)}) %collective-permute-start.10) | collective-permute-done | bytes 131104 | tf_op jit(solution)/shard_map/ppermute | solution.py:276
  37.1 0.0 collective-permute-done.11.refs_4_
  37.1 0.0 collective-permute-done.12.refs_5_
  37.1 0.0 collective-permute-done.13.refs_6_
  37.1 1.1 %unpack.1 = (bf16[1,1,128,2048]{3,2,1,0:T(8,128)(2,1)}, bf16[1,1,128,2048]{3,2,1,0:T(8,128)(2,1)}) custom-call(bf16[256,256]{1,0:T(8,128)(2,1)S(1)} %collective-permute-done.7.refs_0_, bf16[256,256]{1,0:T(8,128)(2,1)S(1)} %collective-permute-done.8.refs_1_, bf16[256,256]{1,0:T(8,128)(2,1)S(1)} %collective-permute-done.9.refs_2_, ...), custom_call_target="tpu_custom_call" | custom-call | tf_op jit(solution)/shard_map/unpack/pallas_call | solution.py:321
Async XLA Ops:
  2.1 8.1 %collective-permute-start = (bf16[272,256]{1,0:T(8,128)(2,1)S(1)}, bf16[272,256]{1,0:T(8,128)(2,1)S(1)}, u32[]{:S(2)}, u32[]{:S(2)}) collective-permute-start(bf16[272,256]{1,0:T(8,128)(2,1)S(1)} %get-tuple-element.18), channel_id=1, source_target_pairs={{0,18},{1,19},{2,16},{3,17},{16,2},{17,3},{18,0},{19,1},{4,22},{5,... | collective-permute-start | bytes 417800 | tf_op jit(solution)/shard_map/ppermute | solution.py:276
  6.0 7.1 %collective-permute-start.1 = (bf16[272,256]{1,0:T(8,128)(2,1)S(1)}, bf16[272,256]{1,0:T(8,128)(2,1)S(1)}, u32[]{:S(2)}, u32[]{:S(2)}) collective-permute-start(bf16[272,256]{1,0:T(8,128)(2,1)S(1)} %get-tuple-element.19), channel_id=1, source_target_pairs={{0,19},{1,18},{2,17},{3,16},{16,3},{17,2},{18,1},{19,0},{4,23},{5,... | collective-permute-start | bytes 417800 | tf_op jit(solution)/shard_map/ppermute | solution.py:276
  6.0 9.7 %collective-permute-start.2 = (bf16[272,256]{1,0:T(8,128)(2,1)S(1)}, bf16[272,256]{1,0:T(8,128)(2,1)S(1)}, u32[]{:S(2)}, u32[]{:S(2)}) collective-permute-start(bf16[272,256]{1,0:T(8,128)(2,1)S(1)} %get-tuple-element.20), channel_id=1, source_target_pairs={{0,16},{1,17},{2,18},{3,19},{16,0},{17,1},{18,2},{19,3},{4,20},{5,... | collective-permute-start | bytes 417800 | tf_op jit(solution)/shard_map/ppermute | solution.py:276
  7.2 11.4 %collective-permute-start.3 = (bf16[272,256]{1,0:T(8,128)(2,1)S(1)}, bf16[272,256]{1,0:T(8,128)(2,1)S(1)}, u32[]{:S(2)}, u32[]{:S(2)}) collective-permute-start(bf16[272,256]{1,0:T(8,128)(2,1)S(1)} %get-tuple-element.21), channel_id=1, source_target_pairs={{0,17},{1,16},{2,19},{3,18},{16,1},{17,0},{18,3},{19,2},{4,21},{5,... | collective-permute-start | bytes 417800 | tf_op jit(solution)/shard_map/ppermute | solution.py:276
  7.8 10.8 %collective-permute-start.4 = (bf16[272,256]{1,0:T(8,128)(2,1)S(1)}, bf16[272,256]{1,0:T(8,128)(2,1)S(1)}, u32[]{:S(2)}, u32[]{:S(2)}) collective-permute-start(bf16[272,256]{1,0:T(8,128)(2,1)S(1)} %get-tuple-element.22), channel_id=1, source_target_pairs={{0,2},{1,3},{2,0},{3,1},{16,18},{17,19},{18,16},{19,17},{4,6},{5,7... | collective-permute-start | bytes 417800 | tf_op jit(solution)/shard_map/ppermute | solution.py:276
  10.1 8.5 %collective-permute-start.5 = (bf16[272,256]{1,0:T(8,128)(2,1)S(1)}, bf16[272,256]{1,0:T(8,128)(2,1)S(1)}, u32[]{:S(2)}, u32[]{:S(2)}) collective-permute-start(bf16[272,256]{1,0:T(8,128)(2,1)S(1)} %get-tuple-element.23), channel_id=1, source_target_pairs={{0,3},{1,2},{2,1},{3,0},{16,19},{17,18},{18,17},{19,16},{4,7},{5,6... | collective-permute-start | bytes 417800 | tf_op jit(solution)/shard_map/ppermute | solution.py:276
  13.1 5.5 %collective-permute-start.6 = (bf16[272,256]{1,0:T(8,128)(2,1)S(1)}, bf16[272,256]{1,0:T(8,128)(2,1)S(1)}, u32[]{:S(2)}, u32[]{:S(2)}) collective-permute-start(bf16[272,256]{1,0:T(8,128)(2,1)S(1)} %get-tuple-element.24), channel_id=1, source_target_pairs={{0,1},{1,0},{2,3},{3,2},{16,17},{17,16},{18,19},{19,18},{4,5},{5,4... | collective-permute-start | bytes 417800 | tf_op jit(solution)/shard_map/ppermute | solution.py:276
  22.2 6.7 %collective-permute-start.7 = (bf16[256,256]{1,0:T(8,128)(2,1)S(1)}, bf16[256,256]{1,0:T(8,128)(2,1)S(1)}, u32[]{:S(2)}, u32[]{:S(2)}) collective-permute-start(bf16[256,256]{1,0:T(8,128)(2,1)S(1)} %get-tuple-element.26), channel_id=1, source_target_pairs={{0,18},{1,19},{2,16},{3,17},{16,2},{17,3},{18,0},{19,1},{4,22},{5,... | collective-permute-start | bytes 393224 | tf_op jit(solution)/shard_map/ppermute | solution.py:276
  25.0 6.8 %collective-permute-start.8 = (bf16[256,256]{1,0:T(8,128)(2,1)S(1)}, bf16[256,256]{1,0:T(8,128)(2,1)S(1)}, u32[]{:S(2)}, u32[]{:S(2)}) collective-permute-start(bf16[256,256]{1,0:T(8,128)(2,1)S(1)} %get-tuple-element.27), channel_id=1, source_target_pairs={{0,19},{1,18},{2,17},{3,16},{16,3},{17,2},{18,1},{19,0},{4,23},{5,... | collective-permute-start | bytes 393224 | tf_op jit(solution)/shard_map/ppermute | solution.py:276
  25.0 9.4 %collective-permute-start.9 = (bf16[256,256]{1,0:T(8,128)(2,1)S(1)}, bf16[256,256]{1,0:T(8,128)(2,1)S(1)}, u32[]{:S(2)}, u32[]{:S(2)}) collective-permute-start(bf16[256,256]{1,0:T(8,128)(2,1)S(1)} %get-tuple-element.28), channel_id=1, source_target_pairs={{0,16},{1,17},{2,18},{3,19},{16,0},{17,1},{18,2},{19,3},{4,20},{5,... | collective-permute-start | bytes 393224 | tf_op jit(solution)/shard_map/ppermute | solution.py:276
  26.4 10.7 %collective-permute-start.10 = (bf16[256,256]{1,0:T(8,128)(2,1)S(1)}, bf16[256,256]{1,0:T(8,128)(2,1)S(1)}, u32[]{:S(2)}, u32[]{:S(2)}) collective-permute-start(bf16[256,256]{1,0:T(8,128)(2,1)S(1)} %get-tuple-element.29), channel_id=1, source_target_pairs={{0,17},{1,16},{2,19},{3,18},{16,1},{17,0},{18,3},{19,2},{4,21},{5,... | collective-permute-start | bytes 393224 | tf_op jit(solution)/shard_map/ppermute | solution.py:276
  26.8 10.4 %collective-permute-start.11 = (bf16[256,256]{1,0:T(8,128)(2,1)S(1)}, bf16[256,256]{1,0:T(8,128)(2,1)S(1)}, u32[]{:S(2)}, u32[]{:S(2)}) collective-permute-start(bf16[256,256]{1,0:T(8,128)(2,1)S(1)} %get-tuple-element.30), channel_id=1, source_target_pairs={{0,2},{1,3},{2,0},{3,1},{16,18},{17,19},{18,16},{19,17},{4,6},{5,7... | collective-permute-start | bytes 393224 | tf_op jit(solution)/shard_map/ppermute | solution.py:276
  28.9 8.3 %collective-permute-start.12 = (bf16[256,256]{1,0:T(8,128)(2,1)S(1)}, bf16[256,256]{1,0:T(8,128)(2,1)S(1)}, u32[]{:S(2)}, u32[]{:S(2)}) collective-permute-start(bf16[256,256]{1,0:T(8,128)(2,1)S(1)} %get-tuple-element.31), channel_id=1, source_target_pairs={{0,3},{1,2},{2,1},{3,0},{16,19},{17,18},{18,17},{19,16},{4,7},{5,6... | collective-permute-start | bytes 393224 | tf_op jit(solution)/shard_map/ppermute | solution.py:276
  31.8 5.4 %collective-permute-start.13 = (bf16[256,256]{1,0:T(8,128)(2,1)S(1)}, bf16[256,256]{1,0:T(8,128)(2,1)S(1)}, u32[]{:S(2)}, u32[]{:S(2)}) collective-permute-start(bf16[256,256]{1,0:T(8,128)(2,1)S(1)} %get-tuple-element.32), channel_id=1, source_target_pairs={{0,1},{1,0},{2,3},{3,2},{16,17},{17,16},{18,19},{19,18},{4,5},{5,4... | collective-permute-start | bytes 393224 | tf_op jit(solution)/shard_map/ppermute | solution.py:276

commit v10 on v9

--- a/solution.py
+++ b/solution.py
@@ -84,13 +84,20 @@
             cots = jnp.concatenate(
                 [jnp.where(lane_head == head, cots, none) for head in range(heads)], axis=0
             )
-            scores = jnp.where(key_valid, contract(keys, queries, 1, 1), FLOOR)
-            expo = jnp.exp(scores - jnp.max(scores, axis=0, keepdims=True))
-            probs = expo * (1.0 / jnp.sum(expo, axis=0, keepdims=True))
+            scores = contract(keys, queries, 1, 1)
             dprob = contract(values, cots, 1, 1)
-            delta = jnp.sum(probs * dprob, axis=0, keepdims=True)
-            probs_low = probs.astype(jnp.bfloat16)
-            dscore_low = (probs * (dprob - delta)).astype(jnp.bfloat16)
+            probs_low, dscore_low = [], []
+            for head in range(heads):
+                part = slice(head * BLK, (head + 1) * BLK)
+                mine = jnp.where(key_valid, scores[:, part], FLOOR)
+                expo = jnp.exp(mine - jnp.max(mine, axis=0, keepdims=True))
+                probs = expo * (1.0 / jnp.sum(expo, axis=0, keepdims=True))
+                delta = jnp.sum(probs * dprob[:, part], axis=0, keepdims=True)
+                dscore = probs * (dprob[:, part] - delta)
+                probs_low.append(probs.astype(jnp.bfloat16))
+                dscore_low.append(dscore.astype(jnp.bfloat16))
+            probs_low = jnp.concatenate(probs_low, axis=1)
+            dscore_low = jnp.concatenate(dscore_low, axis=1)
             dvalue = contract(probs_low, cots, 1, 0)
             dkey = contract(dscore_low, queries, 1, 0)
             keys_turned = jnp.concatenate([turned[index, 0, lanes] for index in chosen], axis=1)
@@ -212,7 +219,7 @@
         out[2 * BLK :] = tail
 
 
-def attend_kernel(seq_count, order, source_len, target_len, *refs):
+def attend_kernel(seq_count, order, back, source_len, target_len, *refs):
     parts = 2 * seq_count
     shares, outs = refs[:parts], refs[parts : 2 * parts]
     rows, result, key_grad, value_grad, turned, lists = refs[2 * parts :]
@@ -241,7 +248,7 @@
         value_grad,
         turned,
     )
-    for step, out in zip(order, outs):
+    for step, out in zip(back, outs):
         out[:BLK] = result[me ^ step, 0]
         out[BLK:] = result[me ^ step, 1]
 
@@ -263,18 +270,12 @@
         copy.wait()
 
 
-def swapped(shares, order, after):
+def swapped(shares, order):
     parts = len(order)
-    held = dict(zip(order, shares))
-    moved = {0: held[0]}
-    for step in order:
-        if step:
-            share = held[step]
-            if step in after:
-                earlier = after[step]
-                share, moved[earlier] = lax.optimization_barrier((share, moved[earlier]))
-            moved[step] = lax.ppermute(share, AXES, [(dev, dev ^ step) for dev in range(parts)])
-    return [moved[step] for step in order]
+    return [
+        lax.ppermute(share, AXES, [(dev, dev ^ step) for dev in range(parts)]) if step else share
+        for step, share in zip(order, shares)
+    ]
 
 
 def by_pairs(first_rows, second_rows, alignment, diffusion_mask, source_length, target_length):
@@ -284,9 +285,9 @@
     share = width // parts
     kind = first_rows.dtype
     params = pltpu.CompilerParams(vmem_limit_bytes=VMEM_LIMIT)
-    order, after = list(range(parts - 1, -1, -1)), {}
+    order = back = list(range(parts - 1, -1, -1))
     if parts == 8:
-        order = [6, 7, 4, 5, 2, 3, 1, 0]
+        order, back = [6, 4, 7, 5, 2, 3, 1, 0], [1, 4, 6, 7, 2, 3, 5, 0]
     sems = pltpu.SemaphoreType.DMA((2, parts))
     shares = pl.pallas_call(
         functools.partial(pack_kernel, seq_count, order),
@@ -302,12 +303,12 @@
         compiler_params=params,
         name="pack",
     )(*in_hbm(alignment, diffusion_mask, first_rows, second_rows))
-    shares = swapped(shares, order, after)
+    shares = swapped(shares, order)
     rows = pltpu.VMEM((parts, 2, BLK, share), kind)
     grads = pltpu.VMEM((seq_count, BLK, share), jnp.float32)
     turned = pltpu.VMEM((seq_count, 2, share, BLK), kind)
     shares = pl.pallas_call(
-        functools.partial(attend_kernel, seq_count, order),
+        functools.partial(attend_kernel, seq_count, order, back),
         out_shape=[jax.ShapeDtypeStruct((2 * BLK, share), kind)] * parts,
         in_specs=specs(2, pltpu.SMEM) + specs(parts, pltpu.VMEM),
         out_specs=specs(parts, pltpu.VMEM),
@@ -316,10 +317,10 @@
         cost_estimate=attend_cost(seq_count, share),
         name="attend",
     )(source_length, target_length, *shares)
-    shares = swapped(shares, order, after)
+    shares = swapped(shares, back)
     out_shape = jax.ShapeDtypeStruct((1, 1, BLK, width), kind)
     return pl.pallas_call(
-        functools.partial(unpack_kernel, seq_count, order),
+        functools.partial(unpack_kernel, seq_count, back),
         out_shape=[out_shape, out_shape],
         in_specs=specs(parts, pltpu.VMEM),
         out_specs=specs(2, pltpu.HBM),

time: 38.5 us -> 41.2 us (1.070)
  waiting for transfers between devices: 16 us -> 18.5 us
    ppermute x14, waiting for transfers between devices: 16 us -> 18.5 us  [swapped(): lax.ppermute(share, AXES, [(dev, dev ^ step) for dev in range(parts)])]
where the time goes in v10:
time: 41.2 us; the launch traced here: 41 us
  waiting for transfers between devices  18.5 us (45%)
  starting transfers between devices  14.3 us (35%)
  Pallas kernels  6.13 us (15%)
  between operations  1.97 us (5%)
    ppermute x14, waiting for transfers between devices, swapped(): lax.ppermute(share, AXES, [(dev, dev ^ step) for dev in range(parts)])  18.5 us
    ppermute x14, starting transfers between devices, swapped(): lax.ppermute(share, AXES, [(dev, dev ^ step) for dev in range(parts)])  14.3 us
    pallas_call x1, Pallas kernels, by_pairs(): pl.pallas_call(functools.partial(attend_kernel, seq_count, order, back),...  3.61 us
    pallas_call x1, Pallas kernels, by_pairs(): pl.pallas_call(functools.partial(pack_kernel, seq_count, order), out_shap...  1.43 us
    pallas_call x1, Pallas kernels, by_pairs(): pl.pallas_call(functools.partial(unpack_kernel, seq_count, back), out_sha...  1.09 us
  transfers between devices with their start and end apart: 14, of which 8 were waited for; matrix products, arithmetic and copies ran while one was open for 0% of the time, Pallas kernels for 0%

profile of v10, /device:TPU:0, one launch (start us, length us, event | category | flops | bytes accessed | tf_op | source)
XLA Modules:
  0.0 41.0 jit_solution(13407797640855105201)
XLA Ops:
  0.6 1.4 %pack.1 = (bf16[272,256]{1,0:T(8,128)(2,1)S(1)}, bf16[272,256]{1,0:T(8,128)(2,1)S(1)}, bf16[272,256]{1,0:T(8,128)(2,1)S(1)}, bf16[272,256]{1,0:T(8,128)(2,1)S(1)...) custom-call(s32[1,1,2]{2,1,0:T(1,128)} %refs_0_.1, ...), custom_call_target="tpu_custom_call" | custom-call | tf_op jit(solution)/shard_map/pack/pallas_call | solution.py:292
  2.1 4.0 %collective-permute-start = (bf16[272,256]{1,0:T(8,128)(2,1)S(1)}, bf16[272,256]{1,0:T(8,128)(2,1)S(1)}, u32[]{:S(2)}, u32[]{:S(2)}) collective-permute-start(bf16[272,256]{1,0:T(8,128)(2,1)S(1)} %get-tuple-element.18), channel_id=1, source_target_pairs={{0,18},{1,19},{2,16},{3,17},{16,2},{17,3},{18,0},{19,1},{4,22},{5,... | collective-permute-start | bytes 417800 | tf_op jit(solution)/shard_map/ppermute | solution.py:276
  6.0 0.5 %collective-permute-start.1 = (bf16[272,256]{1,0:T(8,128)(2,1)S(1)}, bf16[272,256]{1,0:T(8,128)(2,1)S(1)}, u32[]{:S(2)}, u32[]{:S(2)}) collective-permute-start(bf16[272,256]{1,0:T(8,128)(2,1)S(1)} %get-tuple-element.19), channel_id=1, source_target_pairs={{0,16},{1,17},{2,18},{3,19},{16,0},{17,1},{18,2},{19,3},{4,20},{5,... | collective-permute-start | bytes 417800 | tf_op jit(solution)/shard_map/ppermute | solution.py:276
  6.5 0.4 collective-permute-start.2
  6.9 0.9 %collective-permute-start.3 = (bf16[272,256]{1,0:T(8,128)(2,1)S(1)}, bf16[272,256]{1,0:T(8,128)(2,1)S(1)}, u32[]{:S(2)}, u32[]{:S(2)}) collective-permute-start(bf16[272,256]{1,0:T(8,128)(2,1)S(1)} %get-tuple-element.21), channel_id=1, source_target_pairs={{0,17},{1,16},{2,19},{3,18},{16,1},{17,0},{18,3},{19,2},{4,21},{5,... | collective-permute-start | bytes 417800 | tf_op jit(solution)/shard_map/ppermute | solution.py:276
  7.9 1.9 %collective-permute-start.4 = (bf16[272,256]{1,0:T(8,128)(2,1)S(1)}, bf16[272,256]{1,0:T(8,128)(2,1)S(1)}, u32[]{:S(2)}, u32[]{:S(2)}) collective-permute-start(bf16[272,256]{1,0:T(8,128)(2,1)S(1)} %get-tuple-element.22), channel_id=1, source_target_pairs={{0,2},{1,3},{2,0},{3,1},{16,18},{17,19},{18,16},{19,17},{4,6},{5,7... | collective-permute-start | bytes 417800 | tf_op jit(solution)/shard_map/ppermute | solution.py:276
  9.7 0.1 collective-permute-done.refs_0_
  9.8 0.2 collective-permute-start.5
  10.0 5.8 %collective-permute-done.1.refs_1_ = bf16[272,256]{1,0:T(8,128)(2,1)S(1)} collective-permute-done((bf16[272,256]{1,0:T(8,128)(2,1)S(1)}, bf16[272,256]{1,0:T(8,128)(2,1)S(1)}, u32[]{:S(2)}, u32[]{:S(2)}) %collective-permute-start.1) | collective-permute-done | bytes 139296 | tf_op jit(solution)/shard_map/ppermute | solution.py:276
  15.8 0.0 collective-permute-start.6
  17.1 0.0 collective-permute-done.2.refs_2_
  17.1 1.5 %collective-permute-done.3.refs_3_ = bf16[272,256]{1,0:T(8,128)(2,1)S(1)} collective-permute-done((bf16[272,256]{1,0:T(8,128)(2,1)S(1)}, bf16[272,256]{1,0:T(8,128)(2,1)S(1)}, u32[]{:S(2)}, u32[]{:S(2)}) %collective-permute-start.3) | collective-permute-done | bytes 139296 | tf_op jit(solution)/shard_map/ppermute | solution.py:276
  18.6 0.0 collective-permute-done.4.refs_4_
  18.6 0.4 collective-permute-done.5.refs_5_
  18.9 0.0 collective-permute-done.6.refs_6_
  19.0 3.6 %attend.1 = (bf16[256,256]{1,0:T(8,128)(2,1)S(1)}, bf16[256,256]{1,0:T(8,128)(2,1)S(1)}, bf16[256,256]{1,0:T(8,128)(2,1)S(1)}, bf16[256,256]{1,0:T(8,128)(2,1)S(...) custom-call(s32[1]{0:T(128)S(6)} %copy.8.source_len, ...), custom_call_target="tpu_custom_call" | custom-call | flops 335544320 | bytes 2097152 | tf_op jit(solution)/shard_map/attend/pallas_call | solution.py:310
  22.6 0.1 collective-permute-start.7
  22.6 1.4 %collective-permute-start.8 = (bf16[256,256]{1,0:T(8,128)(2,1)S(1)}, bf16[256,256]{1,0:T(8,128)(2,1)S(1)}, u32[]{:S(2)}, u32[]{:S(2)}) collective-permute-start(bf16[256,256]{1,0:T(8,128)(2,1)S(1)} %get-tuple-element.27), channel_id=1, source_target_pairs={{0,16},{1,17},{2,18},{3,19},{16,0},{17,1},{18,2},{19,3},{4,20},{5,... | collective-permute-start | bytes 393224 | tf_op jit(solution)/shard_map/ppermute | solution.py:276
  24.1 1.4 %collective-permute-start.9 = (bf16[256,256]{1,0:T(8,128)(2,1)S(1)}, bf16[256,256]{1,0:T(8,128)(2,1)S(1)}, u32[]{:S(2)}, u32[]{:S(2)}) collective-permute-start(bf16[256,256]{1,0:T(8,128)(2,1)S(1)} %get-tuple-element.28), channel_id=1, source_target_pairs={{0,18},{1,19},{2,16},{3,17},{16,2},{17,3},{18,0},{19,1},{4,22},{5,... | collective-permute-start | bytes 393224 | tf_op jit(solution)/shard_map/ppermute | solution.py:276
  25.5 1.0 %collective-permute-start.10 = (bf16[256,256]{1,0:T(8,128)(2,1)S(1)}, bf16[256,256]{1,0:T(8,128)(2,1)S(1)}, u32[]{:S(2)}, u32[]{:S(2)}) collective-permute-start(bf16[256,256]{1,0:T(8,128)(2,1)S(1)} %get-tuple-element.29), channel_id=1, source_target_pairs={{0,19},{1,18},{2,17},{3,16},{16,3},{17,2},{18,1},{19,0},{4,23},{5,... | collective-permute-start | bytes 393224 | tf_op jit(solution)/shard_map/ppermute | solution.py:276
  26.5 0.2 collective-permute-start.11
  26.7 0.0 collective-permute-done.7.refs_0_
  26.7 1.8 %collective-permute-start.12 = (bf16[256,256]{1,0:T(8,128)(2,1)S(1)}, bf16[256,256]{1,0:T(8,128)(2,1)S(1)}, u32[]{:S(2)}, u32[]{:S(2)}) collective-permute-start(bf16[256,256]{1,0:T(8,128)(2,1)S(1)} %get-tuple-element.31), channel_id=1, source_target_pairs={{0,3},{1,2},{2,1},{3,0},{16,19},{17,18},{18,17},{19,16},{4,7},{5,6... | collective-permute-start | bytes 393224 | tf_op jit(solution)/shard_map/ppermute | solution.py:276
  28.5 5.7 %collective-permute-done.8.refs_1_ = bf16[256,256]{1,0:T(8,128)(2,1)S(1)} collective-permute-done((bf16[256,256]{1,0:T(8,128)(2,1)S(1)}, bf16[256,256]{1,0:T(8,128)(2,1)S(1)}, u32[]{:S(2)}, u32[]{:S(2)}) %collective-permute-start.8) | collective-permute-done | bytes 131104 | tf_op jit(solution)/shard_map/ppermute | solution.py:276
  34.2 0.6 %collective-permute-start.13 = (bf16[256,256]{1,0:T(8,128)(2,1)S(1)}, bf16[256,256]{1,0:T(8,128)(2,1)S(1)}, u32[]{:S(2)}, u32[]{:S(2)}) collective-permute-start(bf16[256,256]{1,0:T(8,128)(2,1)S(1)} %get-tuple-element.32), channel_id=1, source_target_pairs={{0,17},{1,16},{2,19},{3,18},{16,1},{17,0},{18,3},{19,2},{4,21},{5,... | collective-permute-start | bytes 393224 | tf_op jit(solution)/shard_map/ppermute | solution.py:276
  34.8 0.0 collective-permute-done.9.refs_2_
  34.8 0.0 collective-permute-done.10.refs_3_
  34.8 1.4 %collective-permute-done.11.refs_4_ = bf16[256,256]{1,0:T(8,128)(2,1)S(1)} collective-permute-done((bf16[256,256]{1,0:T(8,128)(2,1)S(1)}, bf16[256,256]{1,0:T(8,128)(2,1)S(1)}, u32[]{:S(2)}, u32[]{:S(2)}) %collective-permute-start.11) | collective-permute-done | bytes 131104 | tf_op jit(solution)/shard_map/ppermute | solution.py:276
  36.2 1.3 %collective-permute-done.12.refs_5_ = bf16[256,256]{1,0:T(8,128)(2,1)S(1)} collective-permute-done((bf16[256,256]{1,0:T(8,128)(2,1)S(1)}, bf16[256,256]{1,0:T(8,128)(2,1)S(1)}, u32[]{:S(2)}, u32[]{:S(2)}) %collective-permute-start.12) | collective-permute-done | bytes 131104 | tf_op jit(solution)/shard_map/ppermute | solution.py:276
  37.4 2.4 %collective-permute-done.13.refs_6_ = bf16[256,256]{1,0:T(8,128)(2,1)S(1)} collective-permute-done((bf16[256,256]{1,0:T(8,128)(2,1)S(1)}, bf16[256,256]{1,0:T(8,128)(2,1)S(1)}, u32[]{:S(2)}, u32[]{:S(2)}) %collective-permute-start.13) | collective-permute-done | bytes 131104 | tf_op jit(solution)/shard_map/ppermute | solution.py:276
  39.9 1.1 %unpack.1 = (bf16[1,1,128,2048]{3,2,1,0:T(8,128)(2,1)}, bf16[1,1,128,2048]{3,2,1,0:T(8,128)(2,1)}) custom-call(bf16[256,256]{1,0:T(8,128)(2,1)S(1)} %collective-permute-done.7.refs_0_, bf16[256,256]{1,0:T(8,128)(2,1)S(1)} %collective-permute-done.8.refs_1_, bf16[256,256]{1,0:T(8,128)(2,1)S(1)} %collective-permute-done.9.refs_2_, ...), custom_call_target="tpu_custom_call" | custom-call | tf_op jit(solution)/shard_map/unpack/pallas_call | solution.py:322
Async XLA Ops:
  2.1 7.7 %collective-permute-start = (bf16[272,256]{1,0:T(8,128)(2,1)S(1)}, bf16[272,256]{1,0:T(8,128)(2,1)S(1)}, u32[]{:S(2)}, u32[]{:S(2)}) collective-permute-start(bf16[272,256]{1,0:T(8,128)(2,1)S(1)} %get-tuple-element.18), channel_id=1, source_target_pairs={{0,18},{1,19},{2,16},{3,17},{16,2},{17,3},{18,0},{19,1},{4,22},{5,... | collective-permute-start | bytes 417800 | tf_op jit(solution)/shard_map/ppermute | solution.py:276
  6.0 9.7 %collective-permute-start.1 = (bf16[272,256]{1,0:T(8,128)(2,1)S(1)}, bf16[272,256]{1,0:T(8,128)(2,1)S(1)}, u32[]{:S(2)}, u32[]{:S(2)}) collective-permute-start(bf16[272,256]{1,0:T(8,128)(2,1)S(1)} %get-tuple-element.19), channel_id=1, source_target_pairs={{0,16},{1,17},{2,18},{3,19},{16,0},{17,1},{18,2},{19,3},{4,20},{5,... | collective-permute-start | bytes 417800 | tf_op jit(solution)/shard_map/ppermute | solution.py:276
  6.5 10.5 %collective-permute-start.2 = (bf16[272,256]{1,0:T(8,128)(2,1)S(1)}, bf16[272,256]{1,0:T(8,128)(2,1)S(1)}, u32[]{:S(2)}, u32[]{:S(2)}) collective-permute-start(bf16[272,256]{1,0:T(8,128)(2,1)S(1)} %get-tuple-element.20), channel_id=1, source_target_pairs={{0,19},{1,18},{2,17},{3,16},{16,3},{17,2},{18,1},{19,0},{4,23},{5,... | collective-permute-start | bytes 417800 | tf_op jit(solution)/shard_map/ppermute | solution.py:276
  6.9 11.6 %collective-permute-start.3 = (bf16[272,256]{1,0:T(8,128)(2,1)S(1)}, bf16[272,256]{1,0:T(8,128)(2,1)S(1)}, u32[]{:S(2)}, u32[]{:S(2)}) collective-permute-start(bf16[272,256]{1,0:T(8,128)(2,1)S(1)} %get-tuple-element.21), channel_id=1, source_target_pairs={{0,17},{1,16},{2,19},{3,18},{16,1},{17,0},{18,3},{19,2},{4,21},{5,... | collective-permute-start | bytes 417800 | tf_op jit(solution)/shard_map/ppermute | solution.py:276
  7.9 10.7 %collective-permute-start.4 = (bf16[272,256]{1,0:T(8,128)(2,1)S(1)}, bf16[272,256]{1,0:T(8,128)(2,1)S(1)}, u32[]{:S(2)}, u32[]{:S(2)}) collective-permute-start(bf16[272,256]{1,0:T(8,128)(2,1)S(1)} %get-tuple-element.22), channel_id=1, source_target_pairs={{0,2},{1,3},{2,0},{3,1},{16,18},{17,19},{18,16},{19,17},{4,6},{5,7... | collective-permute-start | bytes 417800 | tf_op jit(solution)/shard_map/ppermute | solution.py:276
  9.8 9.1 %collective-permute-start.5 = (bf16[272,256]{1,0:T(8,128)(2,1)S(1)}, bf16[272,256]{1,0:T(8,128)(2,1)S(1)}, u32[]{:S(2)}, u32[]{:S(2)}) collective-permute-start(bf16[272,256]{1,0:T(8,128)(2,1)S(1)} %get-tuple-element.23), channel_id=1, source_target_pairs={{0,3},{1,2},{2,1},{3,0},{16,19},{17,18},{18,17},{19,16},{4,7},{5,6... | collective-permute-start | bytes 417800 | tf_op jit(solution)/shard_map/ppermute | solution.py:276
  15.8 3.2 %collective-permute-start.6 = (bf16[272,256]{1,0:T(8,128)(2,1)S(1)}, bf16[272,256]{1,0:T(8,128)(2,1)S(1)}, u32[]{:S(2)}, u32[]{:S(2)}) collective-permute-start(bf16[272,256]{1,0:T(8,128)(2,1)S(1)} %get-tuple-element.24), channel_id=1, source_target_pairs={{0,1},{1,0},{2,3},{3,2},{16,17},{17,16},{18,19},{19,18},{4,5},{5,4... | collective-permute-start | bytes 417800 | tf_op jit(solution)/shard_map/ppermute | solution.py:276
  22.6 4.1 %collective-permute-start.7 = (bf16[256,256]{1,0:T(8,128)(2,1)S(1)}, bf16[256,256]{1,0:T(8,128)(2,1)S(1)}, u32[]{:S(2)}, u32[]{:S(2)}) collective-permute-start(bf16[256,256]{1,0:T(8,128)(2,1)S(1)} %get-tuple-element.26), channel_id=1, source_target_pairs={{0,1},{1,0},{2,3},{3,2},{16,17},{17,16},{18,19},{19,18},{4,5},{5,4... | collective-permute-start | bytes 393224 | tf_op jit(solution)/shard_map/ppermute | solution.py:276
  22.6 11.5 %collective-permute-start.8 = (bf16[256,256]{1,0:T(8,128)(2,1)S(1)}, bf16[256,256]{1,0:T(8,128)(2,1)S(1)}, u32[]{:S(2)}, u32[]{:S(2)}) collective-permute-start(bf16[256,256]{1,0:T(8,128)(2,1)S(1)} %get-tuple-element.27), channel_id=1, source_target_pairs={{0,16},{1,17},{2,18},{3,19},{16,0},{17,1},{18,2},{19,3},{4,20},{5,... | collective-permute-start | bytes 393224 | tf_op jit(solution)/shard_map/ppermute | solution.py:276
  24.1 10.7 %collective-permute-start.9 = (bf16[256,256]{1,0:T(8,128)(2,1)S(1)}, bf16[256,256]{1,0:T(8,128)(2,1)S(1)}, u32[]{:S(2)}, u32[]{:S(2)}) collective-permute-start(bf16[256,256]{1,0:T(8,128)(2,1)S(1)} %get-tuple-element.28), channel_id=1, source_target_pairs={{0,18},{1,19},{2,16},{3,17},{16,2},{17,3},{18,0},{19,1},{4,22},{5,... | collective-permute-start | bytes 393224 | tf_op jit(solution)/shard_map/ppermute | solution.py:276
  25.5 9.3 %collective-permute-start.10 = (bf16[256,256]{1,0:T(8,128)(2,1)S(1)}, bf16[256,256]{1,0:T(8,128)(2,1)S(1)}, u32[]{:S(2)}, u32[]{:S(2)}) collective-permute-start(bf16[256,256]{1,0:T(8,128)(2,1)S(1)} %get-tuple-element.29), channel_id=1, source_target_pairs={{0,19},{1,18},{2,17},{3,16},{16,3},{17,2},{18,1},{19,0},{4,23},{5,... | collective-permute-start | bytes 393224 | tf_op jit(solution)/shard_map/ppermute | solution.py:276
  26.5 9.7 %collective-permute-start.11 = (bf16[256,256]{1,0:T(8,128)(2,1)S(1)}, bf16[256,256]{1,0:T(8,128)(2,1)S(1)}, u32[]{:S(2)}, u32[]{:S(2)}) collective-permute-start(bf16[256,256]{1,0:T(8,128)(2,1)S(1)} %get-tuple-element.30), channel_id=1, source_target_pairs={{0,2},{1,3},{2,0},{3,1},{16,18},{17,19},{18,16},{19,17},{4,6},{5,7... | collective-permute-start | bytes 393224 | tf_op jit(solution)/shard_map/ppermute | solution.py:276
  26.7 10.7 %collective-permute-start.12 = (bf16[256,256]{1,0:T(8,128)(2,1)S(1)}, bf16[256,256]{1,0:T(8,128)(2,1)S(1)}, u32[]{:S(2)}, u32[]{:S(2)}) collective-permute-start(bf16[256,256]{1,0:T(8,128)(2,1)S(1)} %get-tuple-element.31), channel_id=1, source_target_pairs={{0,3},{1,2},{2,1},{3,0},{16,19},{17,18},{18,17},{19,16},{4,7},{5,6... | collective-permute-start | bytes 393224 | tf_op jit(solution)/shard_map/ppermute | solution.py:276
  34.2 5.7 %collective-permute-start.13 = (bf16[256,256]{1,0:T(8,128)(2,1)S(1)}, bf16[256,256]{1,0:T(8,128)(2,1)S(1)}, u32[]{:S(2)}, u32[]{:S(2)}) collective-permute-start(bf16[256,256]{1,0:T(8,128)(2,1)S(1)} %get-tuple-element.32), channel_id=1, source_target_pairs={{0,17},{1,16},{2,19},{3,18},{16,1},{17,0},{18,3},{19,2},{4,21},{5,... | collective-permute-start | bytes 393224 | tf_op jit(solution)/shard_map/ppermute | solution.py:276

commit v11 on v9

--- a/solution.py
+++ b/solution.py
@@ -37,7 +37,9 @@
     key_grad[...] = jnp.zeros_like(key_grad)
     value_grad[...] = jnp.zeros_like(value_grad)
     inside = lax.broadcasted_iota(jnp.int32, (BLK, 1), 0)
+    inside_turned = lax.broadcasted_iota(jnp.int32, (1, BLK), 1)
     lane_head = lax.broadcasted_iota(jnp.int32, (BLK, tile), 1) // HDIM
+    row_head = lax.broadcasted_iota(jnp.int32, (tile, BLK), 0) // HDIM
 
     def place(block):
         if per_device == 1:
@@ -56,10 +58,10 @@
     def turn(block, carry):
         dev, here = place(block)
         for first in range(0, width, tile):
-            for half in range(2):
-                turned[block, half, pl.ds(first, tile)] = rows[
-                    dev, half, here, pl.ds(first, tile)
-                ].T
+            lanes = pl.ds(first, tile)
+            for kind in range(4):
+                section, half = divmod(kind, 2)
+                turned[block, kind, lanes] = rows[section * seq_count + dev, half, here, lanes].T
         return carry
 
     def step(block, carry):
@@ -70,6 +72,7 @@
             [index * BLK + inside < source_len for index in chosen], axis=0
         )
         live = block * BLK + inside < target_len
+        live_turned = block * BLK + inside_turned < target_len
         for first in range(0, width, tile):
             lanes = pl.ds(first, tile)
             keys = jnp.concatenate([rows[dev, 0, here, lanes] for dev, here in places], axis=0)
@@ -77,6 +80,7 @@
             queries = rows[seq_count + target, 0, target_rows, lanes] * jnp.bfloat16(SCALE)
             cots = rows[seq_count + target, 1, target_rows, lanes]
             none = jnp.zeros_like(queries)
+            none_turned = jnp.zeros((tile, BLK), queries.dtype)
             cots = jnp.where(live, cots, none)
             queries = jnp.concatenate(
                 [jnp.where(lane_head == head, queries, none) for head in range(heads)], axis=0
@@ -84,10 +88,20 @@
             cots = jnp.concatenate(
                 [jnp.where(lane_head == head, cots, none) for head in range(heads)], axis=0
             )
-            scores = jnp.where(key_valid, contract(keys, queries, 1, 1), FLOOR)
+            queries_turned = turned[block, 2, lanes] * jnp.bfloat16(SCALE)
+            cots_turned = jnp.where(live_turned, turned[block, 3, lanes], none_turned)
+            queries_turned = jnp.concatenate(
+                [jnp.where(row_head == head, queries_turned, none_turned) for head in range(heads)],
+                axis=1,
+            )
+            cots_turned = jnp.concatenate(
+                [jnp.where(row_head == head, cots_turned, none_turned) for head in range(heads)],
+                axis=1,
+            )
+            scores = jnp.where(key_valid, contract(keys, queries_turned, 1, 0), FLOOR)
             expo = jnp.exp(scores - jnp.max(scores, axis=0, keepdims=True))
             probs = expo * (1.0 / jnp.sum(expo, axis=0, keepdims=True))
-            dprob = contract(values, cots, 1, 1)
+            dprob = contract(values, cots_turned, 1, 0)
             delta = jnp.sum(probs * dprob, axis=0, keepdims=True)
             probs_low = probs.astype(jnp.bfloat16)
             dscore_low = (probs * (dprob - delta)).astype(jnp.bfloat16)
@@ -153,7 +167,7 @@
     lists = lax.all_gather(alignment[0], "seq", axis=0, tiled=True)
     rows = lax.all_to_all(held, AXES, 0, 0, tiled=True)
     grads = pltpu.VMEM((seq_count, rows_here, width // parts), jnp.float32)
-    turned = pltpu.VMEM((lists.shape[0], 2, width // parts, BLK), rows.dtype)
+    turned = pltpu.VMEM((lists.shape[0], 4, width // parts, BLK), rows.dtype)
     grads = pl.pallas_call(
         functools.partial(gathered_kernel, seq_count),
         out_shape=jax.ShapeDtypeStruct(rows.shape, rows.dtype),
@@ -286,7 +300,7 @@
     params = pltpu.CompilerParams(vmem_limit_bytes=VMEM_LIMIT)
     order, after = list(range(parts - 1, -1, -1)), {}
     if parts == 8:
-        order = [6, 7, 4, 5, 2, 3, 1, 0]
+        order = [6, 4, 7, 5, 2, 3, 1, 0]
     sems = pltpu.SemaphoreType.DMA((2, parts))
     shares = pl.pallas_call(
         functools.partial(pack_kernel, seq_count, order),
@@ -305,7 +319,7 @@
     shares = swapped(shares, order, after)
     rows = pltpu.VMEM((parts, 2, BLK, share), kind)
     grads = pltpu.VMEM((seq_count, BLK, share), jnp.float32)
-    turned = pltpu.VMEM((seq_count, 2, share, BLK), kind)
+    turned = pltpu.VMEM((seq_count, 4, share, BLK), kind)
     shares = pl.pallas_call(
         functools.partial(attend_kernel, seq_count, order),
         out_shape=[jax.ShapeDtypeStruct((2 * BLK, share), kind)] * parts,

time: 38.5 us -> 38.6 us (level)
  transfers between devices with their start and end apart: 14 -> 14, of which waited for: 8 -> 7; matrix products, arithmetic and copies ran while one was open for 0% -> 0% of each run, Pallas kernels for 0% -> 0%
where the time goes in v11:
time: 38.6 us; the launch traced here: 38.4 us
  waiting for transfers between devices  15.9 us (41%)
  starting transfers between devices  14.3 us (37%)
  Pallas kernels  6.27 us (16%)
  between operations  1.97 us (5%)
    ppermute x14, waiting for transfers between devices, swapped(): lax.ppermute(share, AXES, [(dev, dev ^ step) for dev in range(parts)])  15.9 us
    ppermute x14, starting transfers between devices, swapped(): lax.ppermute(share, AXES, [(dev, dev ^ step) for dev in range(parts)])  14.3 us
    pallas_call x1, Pallas kernels, by_pairs(): pl.pallas_call(functools.partial(attend_kernel, seq_count, order), out_sh...  3.73 us
    pallas_call x1, Pallas kernels, by_pairs(): pl.pallas_call(functools.partial(pack_kernel, seq_count, order), out_shap...  1.43 us
    pallas_call x1, Pallas kernels, by_pairs(): pl.pallas_call(functools.partial(unpack_kernel, seq_count, order), out_sh...  1.1 us
  transfers between devices with their start and end apart: 14, of which 7 were waited for; matrix products, arithmetic and copies ran while one was open for 0% of the time, Pallas kernels for 0%

profile of v11, /device:TPU:0, one launch (start us, length us, event | category | flops | bytes accessed | tf_op | source)
XLA Modules:
  0.0 38.4 jit_solution(8271545890487333490)
XLA Ops:
  0.6 1.4 %pack.1 = (bf16[272,256]{1,0:T(8,128)(2,1)S(1)}, bf16[272,256]{1,0:T(8,128)(2,1)S(1)}, bf16[272,256]{1,0:T(8,128)(2,1)S(1)}, bf16[272,256]{1,0:T(8,128)(2,1)S(1)...) custom-call(s32[1,1,2]{2,1,0:T(1,128)} %refs_0_.1, ...), custom_call_target="tpu_custom_call" | custom-call | tf_op jit(solution)/shard_map/pack/pallas_call | solution.py:305
  2.1 4.0 %collective-permute-start = (bf16[272,256]{1,0:T(8,128)(2,1)S(1)}, bf16[272,256]{1,0:T(8,128)(2,1)S(1)}, u32[]{:S(2)}, u32[]{:S(2)}) collective-permute-start(bf16[272,256]{1,0:T(8,128)(2,1)S(1)} %get-tuple-element.18), channel_id=1, source_target_pairs={{0,18},{1,19},{2,16},{3,17},{16,2},{17,3},{18,0},{19,1},{4,22},{5,... | collective-permute-start | bytes 417800 | tf_op jit(solution)/shard_map/ppermute | solution.py:290
  6.0 0.5 %collective-permute-start.1 = (bf16[272,256]{1,0:T(8,128)(2,1)S(1)}, bf16[272,256]{1,0:T(8,128)(2,1)S(1)}, u32[]{:S(2)}, u32[]{:S(2)}) collective-permute-start(bf16[272,256]{1,0:T(8,128)(2,1)S(1)} %get-tuple-element.19), channel_id=1, source_target_pairs={{0,16},{1,17},{2,18},{3,19},{16,0},{17,1},{18,2},{19,3},{4,20},{5,... | collective-permute-start | bytes 417800 | tf_op jit(solution)/shard_map/ppermute | solution.py:290
  6.5 0.4 collective-permute-start.2
  6.9 0.9 %collective-permute-start.3 = (bf16[272,256]{1,0:T(8,128)(2,1)S(1)}, bf16[272,256]{1,0:T(8,128)(2,1)S(1)}, u32[]{:S(2)}, u32[]{:S(2)}) collective-permute-start(bf16[272,256]{1,0:T(8,128)(2,1)S(1)} %get-tuple-element.21), channel_id=1, source_target_pairs={{0,17},{1,16},{2,19},{3,18},{16,1},{17,0},{18,3},{19,2},{4,21},{5,... | collective-permute-start | bytes 417800 | tf_op jit(solution)/shard_map/ppermute | solution.py:290
  7.9 1.9 %collective-permute-start.4 = (bf16[272,256]{1,0:T(8,128)(2,1)S(1)}, bf16[272,256]{1,0:T(8,128)(2,1)S(1)}, u32[]{:S(2)}, u32[]{:S(2)}) collective-permute-start(bf16[272,256]{1,0:T(8,128)(2,1)S(1)} %get-tuple-element.22), channel_id=1, source_target_pairs={{0,2},{1,3},{2,0},{3,1},{16,18},{17,19},{18,16},{19,17},{4,6},{5,7... | collective-permute-start | bytes 417800 | tf_op jit(solution)/shard_map/ppermute | solution.py:290
  9.7 0.1 collective-permute-done.refs_0_
  9.8 0.2 collective-permute-start.5
  10.0 5.8 %collective-permute-done.1.refs_1_ = bf16[272,256]{1,0:T(8,128)(2,1)S(1)} collective-permute-done((bf16[272,256]{1,0:T(8,128)(2,1)S(1)}, bf16[272,256]{1,0:T(8,128)(2,1)S(1)}, u32[]{:S(2)}, u32[]{:S(2)}) %collective-permute-start.1) | collective-permute-done | bytes 139296 | tf_op jit(solution)/shard_map/ppermute | solution.py:290
  15.8 0.0 collective-permute-start.6
  17.1 0.0 collective-permute-done.2.refs_2_
  17.1 1.5 %collective-permute-done.3.refs_3_ = bf16[272,256]{1,0:T(8,128)(2,1)S(1)} collective-permute-done((bf16[272,256]{1,0:T(8,128)(2,1)S(1)}, bf16[272,256]{1,0:T(8,128)(2,1)S(1)}, u32[]{:S(2)}, u32[]{:S(2)}) %collective-permute-start.3) | collective-permute-done | bytes 139296 | tf_op jit(solution)/shard_map/ppermute | solution.py:290
  18.6 0.0 collective-permute-done.4.refs_4_
  18.6 0.4 %collective-permute-done.5.refs_5_ = bf16[272,256]{1,0:T(8,128)(2,1)S(1)} collective-permute-done((bf16[272,256]{1,0:T(8,128)(2,1)S(1)}, bf16[272,256]{1,0:T(8,128)(2,1)S(1)}, u32[]{:S(2)}, u32[]{:S(2)}) %collective-permute-start.5) | collective-permute-done | bytes 139296 | tf_op jit(solution)/shard_map/ppermute | solution.py:290
  18.9 0.0 collective-permute-done.6.refs_6_
  19.0 3.7 %attend.1 = (bf16[256,256]{1,0:T(8,128)(2,1)S(1)}, bf16[256,256]{1,0:T(8,128)(2,1)S(1)}, bf16[256,256]{1,0:T(8,128)(2,1)S(1)}, bf16[256,256]{1,0:T(8,128)(2,1)S(...) custom-call(s32[1]{0:T(128)S(6)} %copy.8.source_len, ...), custom_call_target="tpu_custom_call" | custom-call | flops 335544320 | bytes 2097152 | tf_op jit(solution)/shard_map/attend/pallas_call | solution.py:323
  22.7 0.9 %collective-permute-start.7 = (bf16[256,256]{1,0:T(8,128)(2,1)S(1)}, bf16[256,256]{1,0:T(8,128)(2,1)S(1)}, u32[]{:S(2)}, u32[]{:S(2)}) collective-permute-start(bf16[256,256]{1,0:T(8,128)(2,1)S(1)} %get-tuple-element.26), channel_id=1, source_target_pairs={{0,18},{1,19},{2,16},{3,17},{16,2},{17,3},{18,0},{19,1},{4,22},{5,... | collective-permute-start | bytes 393224 | tf_op jit(solution)/shard_map/ppermute | solution.py:290
  23.6 1.9 %collective-permute-start.8 = (bf16[256,256]{1,0:T(8,128)(2,1)S(1)}, bf16[256,256]{1,0:T(8,128)(2,1)S(1)}, u32[]{:S(2)}, u32[]{:S(2)}) collective-permute-start(bf16[256,256]{1,0:T(8,128)(2,1)S(1)} %get-tuple-element.27), channel_id=1, source_target_pairs={{0,16},{1,17},{2,18},{3,19},{16,0},{17,1},{18,2},{19,3},{4,20},{5,... | collective-permute-start | bytes 393224 | tf_op jit(solution)/shard_map/ppermute | solution.py:290
  25.5 0.7 %collective-permute-start.9 = (bf16[256,256]{1,0:T(8,128)(2,1)S(1)}, bf16[256,256]{1,0:T(8,128)(2,1)S(1)}, u32[]{:S(2)}, u32[]{:S(2)}) collective-permute-start(bf16[256,256]{1,0:T(8,128)(2,1)S(1)} %get-tuple-element.28), channel_id=1, source_target_pairs={{0,19},{1,18},{2,17},{3,16},{16,3},{17,2},{18,1},{19,0},{4,23},{5,... | collective-permute-start | bytes 393224 | tf_op jit(solution)/shard_map/ppermute | solution.py:290
  26.2 1.3 %collective-permute-start.10 = (bf16[256,256]{1,0:T(8,128)(2,1)S(1)}, bf16[256,256]{1,0:T(8,128)(2,1)S(1)}, u32[]{:S(2)}, u32[]{:S(2)}) collective-permute-start(bf16[256,256]{1,0:T(8,128)(2,1)S(1)} %get-tuple-element.29), channel_id=1, source_target_pairs={{0,17},{1,16},{2,19},{3,18},{16,1},{17,0},{18,3},{19,2},{4,21},{5,... | collective-permute-start | bytes 393224 | tf_op jit(solution)/shard_map/ppermute | solution.py:290
  27.4 1.3 %collective-permute-start.11 = (bf16[256,256]{1,0:T(8,128)(2,1)S(1)}, bf16[256,256]{1,0:T(8,128)(2,1)S(1)}, u32[]{:S(2)}, u32[]{:S(2)}) collective-permute-start(bf16[256,256]{1,0:T(8,128)(2,1)S(1)} %get-tuple-element.30), channel_id=1, source_target_pairs={{0,2},{1,3},{2,0},{3,1},{16,18},{17,19},{18,16},{19,17},{4,6},{5,7... | collective-permute-start | bytes 393224 | tf_op jit(solution)/shard_map/ppermute | solution.py:290
  28.7 0.3 collective-permute-done.7.refs_0_
  29.0 0.4 collective-permute-start.12
  29.4 5.2 %collective-permute-done.8.refs_1_ = bf16[256,256]{1,0:T(8,128)(2,1)S(1)} collective-permute-done((bf16[256,256]{1,0:T(8,128)(2,1)S(1)}, bf16[256,256]{1,0:T(8,128)(2,1)S(1)}, u32[]{:S(2)}, u32[]{:S(2)}) %collective-permute-start.8) | collective-permute-done | bytes 131104 | tf_op jit(solution)/shard_map/ppermute | solution.py:290
  34.6 0.0 collective-permute-start.13
  34.6 0.0 collective-permute-done.9.refs_2_
  34.6 2.7 %collective-permute-done.10.refs_3_ = bf16[256,256]{1,0:T(8,128)(2,1)S(1)} collective-permute-done((bf16[256,256]{1,0:T(8,128)(2,1)S(1)}, bf16[256,256]{1,0:T(8,128)(2,1)S(1)}, u32[]{:S(2)}, u32[]{:S(2)}) %collective-permute-start.10) | collective-permute-done | bytes 131104 | tf_op jit(solution)/shard_map/ppermute | solution.py:290
  37.3 0.0 collective-permute-done.11.refs_4_
  37.3 0.0 collective-permute-done.12.refs_5_
  37.3 0.0 collective-permute-done.13.refs_6_
  37.3 1.1 %unpack.1 = (bf16[1,1,128,2048]{3,2,1,0:T(8,128)(2,1)}, bf16[1,1,128,2048]{3,2,1,0:T(8,128)(2,1)}) custom-call(bf16[256,256]{1,0:T(8,128)(2,1)S(1)} %collective-permute-done.7.refs_0_, bf16[256,256]{1,0:T(8,128)(2,1)S(1)} %collective-permute-done.8.refs_1_, bf16[256,256]{1,0:T(8,128)(2,1)S(1)} %collective-permute-done.9.refs_2_, ...), custom_call_target="tpu_custom_call" | custom-call | tf_op jit(solution)/shard_map/unpack/pallas_call | solution.py:335
Async XLA Ops:
  2.1 7.7 %collective-permute-start = (bf16[272,256]{1,0:T(8,128)(2,1)S(1)}, bf16[272,256]{1,0:T(8,128)(2,1)S(1)}, u32[]{:S(2)}, u32[]{:S(2)}) collective-permute-start(bf16[272,256]{1,0:T(8,128)(2,1)S(1)} %get-tuple-element.18), channel_id=1, source_target_pairs={{0,18},{1,19},{2,16},{3,17},{16,2},{17,3},{18,0},{19,1},{4,22},{5,... | collective-permute-start | bytes 417800 | tf_op jit(solution)/shard_map/ppermute | solution.py:290
  6.0 9.7 %collective-permute-start.1 = (bf16[272,256]{1,0:T(8,128)(2,1)S(1)}, bf16[272,256]{1,0:T(8,128)(2,1)S(1)}, u32[]{:S(2)}, u32[]{:S(2)}) collective-permute-start(bf16[272,256]{1,0:T(8,128)(2,1)S(1)} %get-tuple-element.19), channel_id=1, source_target_pairs={{0,16},{1,17},{2,18},{3,19},{16,0},{17,1},{18,2},{19,3},{4,20},{5,... | collective-permute-start | bytes 417800 | tf_op jit(solution)/shard_map/ppermute | solution.py:290
  6.5 10.5 %collective-permute-start.2 = (bf16[272,256]{1,0:T(8,128)(2,1)S(1)}, bf16[272,256]{1,0:T(8,128)(2,1)S(1)}, u32[]{:S(2)}, u32[]{:S(2)}) collective-permute-start(bf16[272,256]{1,0:T(8,128)(2,1)S(1)} %get-tuple-element.20), channel_id=1, source_target_pairs={{0,19},{1,18},{2,17},{3,16},{16,3},{17,2},{18,1},{19,0},{4,23},{5,... | collective-permute-start | bytes 417800 | tf_op jit(solution)/shard_map/ppermute | solution.py:290
  6.9 11.6 %collective-permute-start.3 = (bf16[272,256]{1,0:T(8,128)(2,1)S(1)}, bf16[272,256]{1,0:T(8,128)(2,1)S(1)}, u32[]{:S(2)}, u32[]{:S(2)}) collective-permute-start(bf16[272,256]{1,0:T(8,128)(2,1)S(1)} %get-tuple-element.21), channel_id=1, source_target_pairs={{0,17},{1,16},{2,19},{3,18},{16,1},{17,0},{18,3},{19,2},{4,21},{5,... | collective-permute-start | bytes 417800 | tf_op jit(solution)/shard_map/ppermute | solution.py:290
  7.9 10.7 %collective-permute-start.4 = (bf16[272,256]{1,0:T(8,128)(2,1)S(1)}, bf16[272,256]{1,0:T(8,128)(2,1)S(1)}, u32[]{:S(2)}, u32[]{:S(2)}) collective-permute-start(bf16[272,256]{1,0:T(8,128)(2,1)S(1)} %get-tuple-element.22), channel_id=1, source_target_pairs={{0,2},{1,3},{2,0},{3,1},{16,18},{17,19},{18,16},{19,17},{4,6},{5,7... | collective-permute-start | bytes 417800 | tf_op jit(solution)/shard_map/ppermute | solution.py:290
  9.8 9.1 %collective-permute-start.5 = (bf16[272,256]{1,0:T(8,128)(2,1)S(1)}, bf16[272,256]{1,0:T(8,128)(2,1)S(1)}, u32[]{:S(2)}, u32[]{:S(2)}) collective-permute-start(bf16[272,256]{1,0:T(8,128)(2,1)S(1)} %get-tuple-element.23), channel_id=1, source_target_pairs={{0,3},{1,2},{2,1},{3,0},{16,19},{17,18},{18,17},{19,16},{4,7},{5,6... | collective-permute-start | bytes 417800 | tf_op jit(solution)/shard_map/ppermute | solution.py:290
  15.8 3.2 %collective-permute-start.6 = (bf16[272,256]{1,0:T(8,128)(2,1)S(1)}, bf16[272,256]{1,0:T(8,128)(2,1)S(1)}, u32[]{:S(2)}, u32[]{:S(2)}) collective-permute-start(bf16[272,256]{1,0:T(8,128)(2,1)S(1)} %get-tuple-element.24), channel_id=1, source_target_pairs={{0,1},{1,0},{2,3},{3,2},{16,17},{17,16},{18,19},{19,18},{4,5},{5,4... | collective-permute-start | bytes 417800 | tf_op jit(solution)/shard_map/ppermute | solution.py:290
  22.7 6.3 %collective-permute-start.7 = (bf16[256,256]{1,0:T(8,128)(2,1)S(1)}, bf16[256,256]{1,0:T(8,128)(2,1)S(1)}, u32[]{:S(2)}, u32[]{:S(2)}) collective-permute-start(bf16[256,256]{1,0:T(8,128)(2,1)S(1)} %get-tuple-element.26), channel_id=1, source_target_pairs={{0,18},{1,19},{2,16},{3,17},{16,2},{17,3},{18,0},{19,1},{4,22},{5,... | collective-permute-start | bytes 393224 | tf_op jit(solution)/shard_map/ppermute | solution.py:290
  23.6 11.0 %collective-permute-start.8 = (bf16[256,256]{1,0:T(8,128)(2,1)S(1)}, bf16[256,256]{1,0:T(8,128)(2,1)S(1)}, u32[]{:S(2)}, u32[]{:S(2)}) collective-permute-start(bf16[256,256]{1,0:T(8,128)(2,1)S(1)} %get-tuple-element.27), channel_id=1, source_target_pairs={{0,16},{1,17},{2,18},{3,19},{16,0},{17,1},{18,2},{19,3},{4,20},{5,... | collective-permute-start | bytes 393224 | tf_op jit(solution)/shard_map/ppermute | solution.py:290
  25.5 9.1 %collective-permute-start.9 = (bf16[256,256]{1,0:T(8,128)(2,1)S(1)}, bf16[256,256]{1,0:T(8,128)(2,1)S(1)}, u32[]{:S(2)}, u32[]{:S(2)}) collective-permute-start(bf16[256,256]{1,0:T(8,128)(2,1)S(1)} %get-tuple-element.28), channel_id=1, source_target_pairs={{0,19},{1,18},{2,17},{3,16},{16,3},{17,2},{18,1},{19,0},{4,23},{5,... | collective-permute-start | bytes 393224 | tf_op jit(solution)/shard_map/ppermute | solution.py:290
  26.2 11.1 %collective-permute-start.10 = (bf16[256,256]{1,0:T(8,128)(2,1)S(1)}, bf16[256,256]{1,0:T(8,128)(2,1)S(1)}, u32[]{:S(2)}, u32[]{:S(2)}) collective-permute-start(bf16[256,256]{1,0:T(8,128)(2,1)S(1)} %get-tuple-element.29), channel_id=1, source_target_pairs={{0,17},{1,16},{2,19},{3,18},{16,1},{17,0},{18,3},{19,2},{4,21},{5,... | collective-permute-start | bytes 393224 | tf_op jit(solution)/shard_map/ppermute | solution.py:290
  27.4 9.8 %collective-permute-start.11 = (bf16[256,256]{1,0:T(8,128)(2,1)S(1)}, bf16[256,256]{1,0:T(8,128)(2,1)S(1)}, u32[]{:S(2)}, u32[]{:S(2)}) collective-permute-start(bf16[256,256]{1,0:T(8,128)(2,1)S(1)} %get-tuple-element.30), channel_id=1, source_target_pairs={{0,2},{1,3},{2,0},{3,1},{16,18},{17,19},{18,16},{19,17},{4,6},{5,7... | collective-permute-start | bytes 393224 | tf_op jit(solution)/shard_map/ppermute | solution.py:290
  29.0 8.3 %collective-permute-start.12 = (bf16[256,256]{1,0:T(8,128)(2,1)S(1)}, bf16[256,256]{1,0:T(8,128)(2,1)S(1)}, u32[]{:S(2)}, u32[]{:S(2)}) collective-permute-start(bf16[256,256]{1,0:T(8,128)(2,1)S(1)} %get-tuple-element.31), channel_id=1, source_target_pairs={{0,3},{1,2},{2,1},{3,0},{16,19},{17,18},{18,17},{19,16},{4,7},{5,6... | collective-permute-start | bytes 393224 | tf_op jit(solution)/shard_map/ppermute | solution.py:290
  34.6 2.7 %collective-permute-start.13 = (bf16[256,256]{1,0:T(8,128)(2,1)S(1)}, bf16[256,256]{1,0:T(8,128)(2,1)S(1)}, u32[]{:S(2)}, u32[]{:S(2)}) collective-permute-start(bf16[256,256]{1,0:T(8,128)(2,1)S(1)} %get-tuple-element.32), channel_id=1, source_target_pairs={{0,1},{1,0},{2,3},{3,2},{16,17},{17,16},{18,19},{19,18},{4,5},{5,4... | collective-permute-start | bytes 393224 | tf_op jit(solution)/shard_map/ppermute | solution.py:290

commit v12 on v9

--- a/solution.py
+++ b/solution.py
@@ -14,6 +14,7 @@
 SPAN = 2 * WIN + 1
 LANES = 128
 TAIL = 16
+FLIGHTS = 5
 SCALE = HDIM ** (-0.5)
 FLOOR = -1e30
 VMEM_LIMIT = 32 * 1024 * 1024
@@ -212,69 +213,87 @@
         out[2 * BLK :] = tail
 
 
-def attend_kernel(seq_count, order, source_len, target_len, *refs):
+def attend_kernel(seq_count, order, turn, source_len, target_len, *refs):
     parts = 2 * seq_count
     shares, outs = refs[:parts], refs[parts : 2 * parts]
     rows, result, key_grad, value_grad, turned, lists = refs[2 * parts :]
     me = device_index(seq_count)
     here = me % seq_count
-    for step, share in zip(order, shares):
-        source = me ^ step
-        rows[source, 0] = share[:BLK]
-        rows[source, 1] = share[BLK : 2 * BLK]
-        if step < seq_count:
-            tail = share[2 * BLK :, :LANES].astype(jnp.float32)
-            lists[here ^ step] = jnp.max(tail).astype(jnp.int32)
 
     def listed(block, slot):
         code = lists[block]
         return block - WIN + (code // SPAN if slot == 0 else code % SPAN)
 
-    attend_sample(
-        seq_count,
-        listed,
-        source_len[0],
-        target_len[0],
-        rows,
-        result,
-        key_grad,
-        value_grad,
-        turned,
-    )
-    for step, out in zip(order, outs):
-        out[:BLK] = result[me ^ step, 0]
-        out[BLK:] = result[me ^ step, 1]
+    @pl.when(me % 2 == turn)
+    def _():
+        for step, share in zip(order, shares):
+            source = me ^ step
+            rows[source, 0] = share[:BLK]
+            rows[source, 1] = share[BLK : 2 * BLK]
+            if step < seq_count:
+                tail = share[2 * BLK :, :LANES].astype(jnp.float32)
+                lists[here ^ step] = jnp.max(tail).astype(jnp.int32)
+        attend_sample(
+            seq_count,
+            listed,
+            source_len[0],
+            target_len[0],
+            rows,
+            result,
+            key_grad,
+            value_grad,
+            turned,
+        )
+        for step, out in zip(order, outs):
+            out[:BLK] = result[me ^ step, 0]
+            out[BLK:] = result[me ^ step, 1]
 
 
 def unpack_kernel(seq_count, order, *refs):
-    shares, (first, second, sem) = refs[:-3], refs[-3:]
-    width = shares[0].shape[1]
+    parts = 2 * seq_count
+    turns, (first, second, sem) = (refs[:parts], refs[parts : 2 * parts]), refs[2 * parts :]
+    width = refs[0].shape[1]
     me = device_index(seq_count)
-    copies = []
-    for slot, (step, share) in enumerate(zip(order, shares)):
-        lanes = pl.ds(pl.multiple_of((me ^ step) * width, LANES), width)
-        for half, result in enumerate((first, second)):
-            copy = pltpu.make_async_copy(
-                share.at[pl.ds(half * BLK, BLK)], result.at[0, 0, :, lanes], sem.at[half, slot]
-            )
-            copy.start()
-            copies.append(copy)
-    for copy in copies:
-        copy.wait()
-
-
-def swapped(shares, order, after):
+    for core in range(2):
+
+        @pl.when(me % 2 == core)
+        def _(core=core):
+            copies = []
+            for slot, step in enumerate(order):
+                lanes = pl.ds(pl.multiple_of((me ^ step) * width, LANES), width)
+                share = turns[(core ^ step) % 2][slot]
+                for half, result in enumerate((first, second)):
+                    copy = pltpu.make_async_copy(
+                        share.at[pl.ds(half * BLK, BLK)],
+                        result.at[0, 0, :, lanes],
+                        sem.at[half, slot],
+                    )
+                    copy.start()
+                    copies.append(copy)
+            for copy in copies:
+                copy.wait()
+
+
+def to_turn(shares, order, turn):
     parts = len(order)
-    held = dict(zip(order, shares))
-    moved = {0: held[0]}
-    for step in order:
-        if step:
-            share = held[step]
-            if step in after:
-                earlier = after[step]
-                share, moved[earlier] = lax.optimization_barrier((share, moved[earlier]))
-            moved[step] = lax.ppermute(share, AXES, [(dev, dev ^ step) for dev in range(parts)])
-    return [moved[step] for step in order]
+    return [
+        lax.ppermute(
+            share, AXES, [(dev, dev ^ step) for dev in range(parts) if (dev ^ step) % 2 == turn]
+        )
+        if step
+        else share
+        for step, share in zip(order, shares)
+    ]
+
+
+def from_turn(shares, order, turn):
+    parts = len(order)
+    return [
+        lax.ppermute(share, AXES, [(dev, dev ^ step) for dev in range(turn, parts, 2)])
+        if step
+        else share
+        for step, share in zip(order, shares)
+    ]
 
 
 def by_pairs(first_rows, second_rows, alignment, diffusion_mask, source_length, target_length):
@@ -284,7 +303,7 @@
     share = width // parts
     kind = first_rows.dtype
     params = pltpu.CompilerParams(vmem_limit_bytes=VMEM_LIMIT)
-    order, after = list(range(parts - 1, -1, -1)), {}
+    order = list(range(parts - 1, -1, -1))
     if parts == 8:
         order = [6, 7, 4, 5, 2, 3, 1, 0]
     sems = pltpu.SemaphoreType.DMA((2, parts))
@@ -302,31 +321,38 @@
         compiler_params=params,
         name="pack",
     )(*in_hbm(alignment, diffusion_mask, first_rows, second_rows))
-    shares = swapped(shares, order, after)
     rows = pltpu.VMEM((parts, 2, BLK, share), kind)
     grads = pltpu.VMEM((seq_count, BLK, share), jnp.float32)
     turned = pltpu.VMEM((seq_count, 2, share, BLK), kind)
-    shares = pl.pallas_call(
-        functools.partial(attend_kernel, seq_count, order),
-        out_shape=[jax.ShapeDtypeStruct((2 * BLK, share), kind)] * parts,
-        in_specs=specs(2, pltpu.SMEM) + specs(parts, pltpu.VMEM),
-        out_specs=specs(parts, pltpu.VMEM),
-        scratch_shapes=[rows, rows, grads, grads, turned, pltpu.SMEM((seq_count,), jnp.int32)],
-        compiler_params=params,
-        cost_estimate=attend_cost(seq_count, share),
-        name="attend",
-    )(source_length, target_length, *shares)
-    shares = swapped(shares, order, after)
+
+    def attend(turn, shares):
+        return pl.pallas_call(
+            functools.partial(attend_kernel, seq_count, order, turn),
+            out_shape=[jax.ShapeDtypeStruct((2 * BLK, share), kind)] * parts,
+            in_specs=specs(2, pltpu.SMEM) + specs(parts, pltpu.VMEM),
+            out_specs=specs(parts, pltpu.VMEM),
+            scratch_shapes=[rows, rows, grads, grads, turned, pltpu.SMEM((seq_count,), jnp.int32)],
+            compiler_params=params,
+            cost_estimate=attend_cost(seq_count, share),
+            name="attend",
+        )(source_length, target_length, *shares)
+
+    early = to_turn(shares, order, 0)
+    shares, early = zip(*(lax.optimization_barrier(pair) for pair in zip(shares, early)))
+    early = list(attend(0, early))
+    *tied, early[-1] = lax.optimization_barrier((*shares[FLIGHTS:], early[-1]))
+    late = attend(1, to_turn([*shares[:FLIGHTS], *tied], order, 1))
+    back = [from_turn(outs, order, turn) for turn, outs in enumerate((early, late))]
     out_shape = jax.ShapeDtypeStruct((1, 1, BLK, width), kind)
     return pl.pallas_call(
         functools.partial(unpack_kernel, seq_count, order),
         out_shape=[out_shape, out_shape],
-        in_specs=specs(parts, pltpu.VMEM),
+        in_specs=specs(2 * parts, pltpu.VMEM),
         out_specs=specs(2, pltpu.HBM),
         scratch_shapes=[sems],
         compiler_params=params,
         name="unpack",
-    )(*shares)
+    )(*back[0], *back[1])
 
 
 def on_device(first_rows, second_rows, alignment, diffusion_mask, source_length, target_length):

time: 38.5 us -> 70.4 us (1.83)
  starting transfers between devices: 14.1 us -> 52.5 us
  waiting for transfers between devices: 16 us -> 8.74 us
    ppermute x14 -> x28, starting transfers between devices: 14.1 us -> 52.5 us  [the longest x14 30.9 us: to_turn(): lax.ppermute(share, AXES, [(dev, dev ^ step) for dev in range(parts) if (...]
    ppermute x14 -> x28, waiting for transfers between devices: 16 us -> 8.74 us  [the longest x14 8.7 us: from_turn(): lax.ppermute(share, AXES, [(dev, dev ^ step) for dev in range(turn, parts...]
    pallas_call x1 -> x2, Pallas kernels: 3.61 us -> 3.63 us  [attend(): pl.pallas_call(functools.partial(attend_kernel, seq_count, order, turn),...]
  transfers between devices with their start and end apart: 14 -> 28, of which waited for: 8 -> 4; matrix products, arithmetic and copies ran while one was open for 0% -> 0% of each run, Pallas kernels for 0% -> 5%
where the time goes in v12:
time: 70.4 us; the launch traced here: 69.7 us
  starting transfers between devices  52.5 us (75%)
  waiting for transfers between devices  8.74 us (12%)
  Pallas kernels  6.16 us (9%)
  between operations  2.35 us (3%)
    ppermute x14, starting transfers between devices, to_turn(): lax.ppermute(share, AXES, [(dev, dev ^ step) for dev in range(parts) if (...  30.9 us
    ppermute x14, starting transfers between devices, from_turn(): lax.ppermute(share, AXES, [(dev, dev ^ step) for dev in range(turn, parts...  21.6 us
    ppermute x14, waiting for transfers between devices, from_turn(): lax.ppermute(share, AXES, [(dev, dev ^ step) for dev in range(turn, parts...  8.7 us
    pallas_call x2, Pallas kernels, attend(): pl.pallas_call(functools.partial(attend_kernel, seq_count, order, turn),...  3.63 us
    pallas_call x1, Pallas kernels, by_pairs(): pl.pallas_call(functools.partial(pack_kernel, seq_count, order), out_shap...  1.43 us
  transfers between devices with their start and end apart: 28, of which 4 were waited for; matrix products, arithmetic and copies ran while one was open for 0% of the time, Pallas kernels for 5%

profile of v12, /device:TPU:0, one launch (start us, length us, event | category | flops | bytes accessed | tf_op | source)
XLA Modules:
  0.0 69.7 jit_solution(12637728496239282103)
XLA Ops:
  0.6 1.4 %pack.1 = (bf16[272,256]{1,0:T(8,128)(2,1)S(1)}, bf16[272,256]{1,0:T(8,128)(2,1)S(1)}, bf16[272,256]{1,0:T(8,128)(2,1)S(1)}, bf16[272,256]{1,0:T(8,128)(2,1)S(1)...) custom-call(s32[1,1,2]{2,1,0:T(1,128)} %refs_0_.1, ...), custom_call_target="tpu_custom_call" | custom-call | tf_op jit(solution)/shard_map/pack/pallas_call | solution.py:310
  2.1 5.8 %collective-permute-start = (bf16[272,256]{1,0:T(8,128)(2,1)S(1)}, bf16[272,256]{1,0:T(8,128)(2,1)S(1)}, u32[]{:S(2)}, u32[]{:S(2)}) collective-permute-start(bf16[272,256]{1,0:T(8,128)(2,1)S(1)} %get-tuple-element.74), channel_id=1, source_target_pairs={{0,18},{2,16},{16,2},{18,0},{4,22},{6,20},{20,6},{22,4},{8,26},{10... | collective-permute-start | bytes 417800 | tf_op jit(solution)/shard_map/ppermute | solution.py:280
  7.9 1.3 %collective-permute-start.1 = (bf16[272,256]{1,0:T(8,128)(2,1)S(1)}, bf16[272,256]{1,0:T(8,128)(2,1)S(1)}, u32[]{:S(2)}, u32[]{:S(2)}) collective-permute-start(bf16[272,256]{1,0:T(8,128)(2,1)S(1)} %get-tuple-element.75), channel_id=1, source_target_pairs={{1,18},{3,16},{17,2},{19,0},{5,22},{7,20},{21,6},{23,4},{9,26},{11... | collective-permute-start | bytes 417800 | tf_op jit(solution)/shard_map/ppermute | solution.py:280
  9.2 2.4 %collective-permute-start.2 = (bf16[272,256]{1,0:T(8,128)(2,1)S(1)}, bf16[272,256]{1,0:T(8,128)(2,1)S(1)}, u32[]{:S(2)}, u32[]{:S(2)}) collective-permute-start(bf16[272,256]{1,0:T(8,128)(2,1)S(1)} %get-tuple-element.76), channel_id=1, source_target_pairs={{0,16},{2,18},{16,0},{18,2},{4,20},{6,22},{20,4},{22,6},{8,24},{10... | collective-permute-start | bytes 417800 | tf_op jit(solution)/shard_map/ppermute | solution.py:280
  11.6 1.3 %collective-permute-start.3 = (bf16[272,256]{1,0:T(8,128)(2,1)S(1)}, bf16[272,256]{1,0:T(8,128)(2,1)S(1)}, u32[]{:S(2)}, u32[]{:S(2)}) collective-permute-start(bf16[272,256]{1,0:T(8,128)(2,1)S(1)} %get-tuple-element.77), channel_id=1, source_target_pairs={{1,16},{3,18},{17,0},{19,2},{5,20},{7,22},{21,4},{23,6},{9,24},{11... | collective-permute-start | bytes 417800 | tf_op jit(solution)/shard_map/ppermute | solution.py:280
  12.9 2.0 %collective-permute-start.4 = (bf16[272,256]{1,0:T(8,128)(2,1)S(1)}, bf16[272,256]{1,0:T(8,128)(2,1)S(1)}, u32[]{:S(2)}, u32[]{:S(2)}) collective-permute-start(bf16[272,256]{1,0:T(8,128)(2,1)S(1)} %get-tuple-element.78), channel_id=1, source_target_pairs={{0,2},{2,0},{16,18},{18,16},{4,6},{6,4},{20,22},{22,20},{8,10},{10... | collective-permute-start | bytes 417800 | tf_op jit(solution)/shard_map/ppermute | solution.py:280
  14.9 0.0 collective-permute-done.refs_0_
  14.9 1.3 %collective-permute-start.5 = (bf16[272,256]{1,0:T(8,128)(2,1)S(1)}, bf16[272,256]{1,0:T(8,128)(2,1)S(1)}, u32[]{:S(2)}, u32[]{:S(2)}) collective-permute-start(bf16[272,256]{1,0:T(8,128)(2,1)S(1)} %get-tuple-element.79), channel_id=1, source_target_pairs={{1,2},{3,0},{17,18},{19,16},{5,6},{7,4},{21,22},{23,20},{9,10},{11... | collective-permute-start | bytes 417800 | tf_op jit(solution)/shard_map/ppermute | solution.py:280
  16.2 1.3 %collective-permute-start.6 = (bf16[272,256]{1,0:T(8,128)(2,1)S(1)}, bf16[272,256]{1,0:T(8,128)(2,1)S(1)}, u32[]{:S(2)}, u32[]{:S(2)}) collective-permute-start(bf16[272,256]{1,0:T(8,128)(2,1)S(1)} %get-tuple-element.80), channel_id=1, source_target_pairs={{1,0},{3,2},{17,16},{19,18},{5,4},{7,6},{21,20},{23,22},{9,8},{11,... | collective-permute-start | bytes 417800 | tf_op jit(solution)/shard_map/ppermute | solution.py:280
  17.5 0.0 collective-permute-done.2.refs_2_
  17.5 0.7 collective-permute-start.14
  18.2 8.1 %collective-permute-start.15 = (bf16[272,256]{1,0:T(8,128)(2,1)S(1)}, bf16[272,256]{1,0:T(8,128)(2,1)S(1)}, u32[]{:S(2)}, u32[]{:S(2)}) collective-permute-start(bf16[272,256]{1,0:T(8,128)(2,1)S(1)} %get-tuple-element.75), channel_id=1, source_target_pairs={{0,19},{2,17},{16,3},{18,1},{4,23},{6,21},{20,7},{22,5},{8,27},{10... | collective-permute-start | bytes 417800 | tf_op jit(solution)/shard_map/ppermute | solution.py:280
  27.6 0.0 collective-permute-done.4.refs_4_
  27.6 0.7 collective-permute-start.16
  28.3 0.0 collective-permute-done.5.refs_5_
  28.3 2.8 %collective-permute-start.17 = (bf16[272,256]{1,0:T(8,128)(2,1)S(1)}, bf16[272,256]{1,0:T(8,128)(2,1)S(1)}, u32[]{:S(2)}, u32[]{:S(2)}) collective-permute-start(bf16[272,256]{1,0:T(8,128)(2,1)S(1)} %get-tuple-element.77), channel_id=1, source_target_pairs={{0,17},{2,19},{16,1},{18,3},{4,21},{6,23},{20,5},{22,7},{8,25},{10... | collective-permute-start | bytes 417800 | tf_op jit(solution)/shard_map/ppermute | solution.py:280
  31.2 0.0 collective-permute-done.6.refs_6_
  31.2 0.7 collective-permute-start.18
  31.8 3.6 %attend.2 = (bf16[256,256]{1,0:T(8,128)(2,1)S(1)}, bf16[256,256]{1,0:T(8,128)(2,1)S(1)}, bf16[256,256]{1,0:T(8,128)(2,1)S(1)}, bf16[256,256]{1,0:T(8,128)(2,1)S(...) custom-call(s32[1]{0:T(128)S(6)} %copy.8.source_len, ...), custom_call_target="tpu_custom_call" | custom-call | flops 335544320 | bytes 2097152 | tf_op jit(solution)/shard_map/attend/pallas_call | solution.py:329
  35.5 1.3 %collective-permute-start.19 = (bf16[272,256]{1,0:T(8,128)(2,1)S(1)}, bf16[272,256]{1,0:T(8,128)(2,1)S(1)}, u32[]{:S(2)}, u32[]{:S(2)}) collective-permute-start(bf16[272,256]{1,0:T(8,128)(2,1)S(1)} %get-tuple-element.79), channel_id=1, source_target_pairs={{0,3},{2,1},{16,19},{18,17},{4,7},{6,5},{20,23},{22,21},{8,11},{10... | collective-permute-start | bytes 417800 | tf_op jit(solution)/shard_map/ppermute | solution.py:280
  36.8 1.3 %collective-permute-start.20 = (bf16[272,256]{1,0:T(8,128)(2,1)S(1)}, bf16[272,256]{1,0:T(8,128)(2,1)S(1)}, u32[]{:S(2)}, u32[]{:S(2)}) collective-permute-start(bf16[272,256]{1,0:T(8,128)(2,1)S(1)} %get-tuple-element.80), channel_id=1, source_target_pairs={{0,1},{2,3},{16,17},{18,19},{4,5},{6,7},{20,21},{22,23},{8,9},{10,... | collective-permute-start | bytes 417800 | tf_op jit(solution)/shard_map/ppermute | solution.py:280
  38.1 0.0 collective-permute-done.16.refs_2_
  38.1 3.3 %collective-permute-start.7 = (bf16[256,256]{1,0:T(8,128)(2,1)S(1)}, bf16[256,256]{1,0:T(8,128)(2,1)S(1)}, u32[]{:S(2)}, u32[]{:S(2)}) collective-permute-start(bf16[256,256]{1,0:T(8,128)(2,1)S(1)} %get-tuple-element.62), channel_id=1, source_target_pairs={{0,18},{2,16},{16,2},{18,0},{4,22},{6,20},{20,6},{22,4},{8,26},{10... | collective-permute-start | bytes 393224 | tf_op jit(solution)/shard_map/ppermute | solution.py:292
  41.5 0.0 collective-permute-done.17.refs_3_
  41.5 1.3 %collective-permute-start.8 = (bf16[256,256]{1,0:T(8,128)(2,1)S(1)}, bf16[256,256]{1,0:T(8,128)(2,1)S(1)}, u32[]{:S(2)}, u32[]{:S(2)}) collective-permute-start(bf16[256,256]{1,0:T(8,128)(2,1)S(1)} %get-tuple-element.63), channel_id=1, source_target_pairs={{0,19},{2,17},{16,3},{18,1},{4,23},{6,21},{20,7},{22,5},{8,27},{10... | collective-permute-start | bytes 393224 | tf_op jit(solution)/shard_map/ppermute | solution.py:292
  42.8 3.4 %collective-permute-start.9 = (bf16[256,256]{1,0:T(8,128)(2,1)S(1)}, bf16[256,256]{1,0:T(8,128)(2,1)S(1)}, u32[]{:S(2)}, u32[]{:S(2)}) collective-permute-start(bf16[256,256]{1,0:T(8,128)(2,1)S(1)} %get-tuple-element.64), channel_id=1, source_target_pairs={{0,16},{2,18},{16,0},{18,2},{4,20},{6,22},{20,4},{22,6},{8,24},{10... | collective-permute-start | bytes 393224 | tf_op jit(solution)/shard_map/ppermute | solution.py:292
  46.2 0.0 collective-permute-done.19.refs_5_
  46.2 1.3 %collective-permute-start.10 = (bf16[256,256]{1,0:T(8,128)(2,1)S(1)}, bf16[256,256]{1,0:T(8,128)(2,1)S(1)}, u32[]{:S(2)}, u32[]{:S(2)}) collective-permute-start(bf16[256,256]{1,0:T(8,128)(2,1)S(1)} %get-tuple-element.65), channel_id=1, source_target_pairs={{0,17},{2,19},{16,1},{18,3},{4,21},{6,23},{20,5},{22,7},{8,25},{10... | collective-permute-start | bytes 393224 | tf_op jit(solution)/shard_map/ppermute | solution.py:292
  47.5 2.4 %collective-permute-start.11 = (bf16[256,256]{1,0:T(8,128)(2,1)S(1)}, bf16[256,256]{1,0:T(8,128)(2,1)S(1)}, u32[]{:S(2)}, u32[]{:S(2)}) collective-permute-start(bf16[256,256]{1,0:T(8,128)(2,1)S(1)} %get-tuple-element.66), channel_id=1, source_target_pairs={{0,2},{2,0},{16,18},{18,16},{4,6},{6,4},{20,22},{22,20},{8,10},{10... | collective-permute-start | bytes 393224 | tf_op jit(solution)/shard_map/ppermute | solution.py:292
  50.0 0.0 collective-permute-done.7.refs_0_
  50.0 1.3 %collective-permute-start.12 = (bf16[256,256]{1,0:T(8,128)(2,1)S(1)}, bf16[256,256]{1,0:T(8,128)(2,1)S(1)}, u32[]{:S(2)}, u32[]{:S(2)}) collective-permute-start(bf16[256,256]{1,0:T(8,128)(2,1)S(1)} %get-tuple-element.67), channel_id=1, source_target_pairs={{0,3},{2,1},{16,19},{18,17},{4,7},{6,5},{20,23},{22,21},{8,11},{10... | collective-permute-start | bytes 393224 | tf_op jit(solution)/shard_map/ppermute | solution.py:292
  51.4 1.3 %collective-permute-start.13 = (bf16[256,256]{1,0:T(8,128)(2,1)S(1)}, bf16[256,256]{1,0:T(8,128)(2,1)S(1)}, u32[]{:S(2)}, u32[]{:S(2)}) collective-permute-start(bf16[256,256]{1,0:T(8,128)(2,1)S(1)} %get-tuple-element.68), channel_id=1, source_target_pairs={{0,1},{2,3},{16,17},{18,19},{4,5},{6,7},{20,21},{22,23},{8,9},{10,... | collective-permute-start | bytes 393224 | tf_op jit(solution)/shard_map/ppermute | solution.py:292
  52.7 0.0 collective-permute-done.9.refs_2_
  52.7 0.7 collective-permute-start.21
  53.3 0.0 collective-permute-done.10.refs_3_
  53.4 1.3 %collective-permute-start.22 = (bf16[256,256]{1,0:T(8,128)(2,1)S(1)}, bf16[256,256]{1,0:T(8,128)(2,1)S(1)}, u32[]{:S(2)}, u32[]{:S(2)}) collective-permute-start(bf16[256,256]{1,0:T(8,128)(2,1)S(1)} %get-tuple-element.83), channel_id=1, source_target_pairs={{1,18},{3,16},{17,2},{19,0},{5,22},{7,20},{21,6},{23,4},{9,26},{11... | collective-permute-start | bytes 393224 | tf_op jit(solution)/shard_map/ppermute | solution.py:292
  54.7 0.4 collective-permute-done.11.refs_4_
  55.1 0.7 collective-permute-start.23
  55.8 1.3 %collective-permute-start.24 = (bf16[256,256]{1,0:T(8,128)(2,1)S(1)}, bf16[256,256]{1,0:T(8,128)(2,1)S(1)}, u32[]{:S(2)}, u32[]{:S(2)}) collective-permute-start(bf16[256,256]{1,0:T(8,128)(2,1)S(1)} %get-tuple-element.85), channel_id=1, source_target_pairs={{1,16},{3,18},{17,0},{19,2},{5,20},{7,22},{21,4},{23,6},{9,24},{11... | collective-permute-start | bytes 393224 | tf_op jit(solution)/shard_map/ppermute | solution.py:292
  57.1 0.7 collective-permute-start.25
  57.7 0.0 collective-permute-done.21.refs_8_
  57.8 1.3 %collective-permute-start.26 = (bf16[256,256]{1,0:T(8,128)(2,1)S(1)}, bf16[256,256]{1,0:T(8,128)(2,1)S(1)}, u32[]{:S(2)}, u32[]{:S(2)}) collective-permute-start(bf16[256,256]{1,0:T(8,128)(2,1)S(1)} %get-tuple-element.87), channel_id=1, source_target_pairs={{1,2},{3,0},{17,18},{19,16},{5,6},{7,4},{21,22},{23,20},{9,10},{11... | collective-permute-start | bytes 393224 | tf_op jit(solution)/shard_map/ppermute | solution.py:292
  59.1 1.5 %collective-permute-done.22.refs_9_ = bf16[256,256]{1,0:T(8,128)(2,1)S(1)} collective-permute-done((bf16[256,256]{1,0:T(8,128)(2,1)S(1)}, bf16[256,256]{1,0:T(8,128)(2,1)S(1)}, u32[]{:S(2)}, u32[]{:S(2)}) %collective-permute-start.22) | collective-permute-done | bytes 131104 | tf_op jit(solution)/shard_map/ppermute | solution.py:292
  60.5 1.3 %collective-permute-start.27 = (bf16[256,256]{1,0:T(8,128)(2,1)S(1)}, bf16[256,256]{1,0:T(8,128)(2,1)S(1)}, u32[]{:S(2)}, u32[]{:S(2)}) collective-permute-start(bf16[256,256]{1,0:T(8,128)(2,1)S(1)} %get-tuple-element.88), channel_id=1, source_target_pairs={{1,0},{3,2},{17,16},{19,18},{5,4},{7,6},{21,20},{23,22},{9,8},{11,... | collective-permute-start | bytes 393224 | tf_op jit(solution)/shard_map/ppermute | solution.py:292
  61.8 2.3 %collective-permute-done.24.refs_11_ = bf16[256,256]{1,0:T(8,128)(2,1)S(1)} collective-permute-done((bf16[256,256]{1,0:T(8,128)(2,1)S(1)}, bf16[256,256]{1,0:T(8,128)(2,1)S(1)}, u32[]{:S(2)}, u32[]{:S(2)}) %collective-permute-start.24) | collective-permute-done | bytes 131104 | tf_op jit(solution)/shard_map/ppermute | solution.py:292
  64.1 0.0 collective-permute-done.25.refs_12_
  64.1 4.5 %collective-permute-done.26.refs_13_ = bf16[256,256]{1,0:T(8,128)(2,1)S(1)} collective-permute-done((bf16[256,256]{1,0:T(8,128)(2,1)S(1)}, bf16[256,256]{1,0:T(8,128)(2,1)S(1)}, u32[]{:S(2)}, u32[]{:S(2)}) %collective-permute-start.26) | collective-permute-done | bytes 131104 | tf_op jit(solution)/shard_map/ppermute | solution.py:292
  68.6 1.1 %unpack.1 = (bf16[1,1,128,2048]{3,2,1,0:T(8,128)(2,1)}, bf16[1,1,128,2048]{3,2,1,0:T(8,128)(2,1)}) custom-call(bf16[256,256]{1,0:T(8,128)(2,1)S(1)} %collective-permute-done.7.refs_0_, bf16[256,256]{1,0:T(8,128)(2,1)S(1)} %collective-permute-done.8.refs_1_, bf16[256,256]{1,0:T(8,128)(2,1)S(1)} %collective-permute-done.9.refs_2_, ...), custom_call_target="tpu_custom_call" | custom-call | tf_op jit(solution)/shard_map/unpack/pallas_call | solution.py:347
  (12 shorter events, 0.1 us)
Async XLA Ops:
  2.1 12.8 %collective-permute-start = (bf16[272,256]{1,0:T(8,128)(2,1)S(1)}, bf16[272,256]{1,0:T(8,128)(2,1)S(1)}, u32[]{:S(2)}, u32[]{:S(2)}) collective-permute-start(bf16[272,256]{1,0:T(8,128)(2,1)S(1)} %get-tuple-element.74), channel_id=1, source_target_pairs={{0,18},{2,16},{16,2},{18,0},{4,22},{6,20},{20,6},{22,4},{8,26},{10... | collective-permute-start | bytes 417800 | tf_op jit(solution)/shard_map/ppermute | solution.py:280
  7.9 8.3 %collective-permute-start.1 = (bf16[272,256]{1,0:T(8,128)(2,1)S(1)}, bf16[272,256]{1,0:T(8,128)(2,1)S(1)}, u32[]{:S(2)}, u32[]{:S(2)}) collective-permute-start(bf16[272,256]{1,0:T(8,128)(2,1)S(1)} %get-tuple-element.75), channel_id=1, source_target_pairs={{1,18},{3,16},{17,2},{19,0},{5,22},{7,20},{21,6},{23,4},{9,26},{11... | collective-permute-start | bytes 417800 | tf_op jit(solution)/shard_map/ppermute | solution.py:280
  9.2 8.3 %collective-permute-start.2 = (bf16[272,256]{1,0:T(8,128)(2,1)S(1)}, bf16[272,256]{1,0:T(8,128)(2,1)S(1)}, u32[]{:S(2)}, u32[]{:S(2)}) collective-permute-start(bf16[272,256]{1,0:T(8,128)(2,1)S(1)} %get-tuple-element.76), channel_id=1, source_target_pairs={{0,16},{2,18},{16,0},{18,2},{4,20},{6,22},{20,4},{22,6},{8,24},{10... | collective-permute-start | bytes 417800 | tf_op jit(solution)/shard_map/ppermute | solution.py:280
  11.6 6.6 %collective-permute-start.3 = (bf16[272,256]{1,0:T(8,128)(2,1)S(1)}, bf16[272,256]{1,0:T(8,128)(2,1)S(1)}, u32[]{:S(2)}, u32[]{:S(2)}) collective-permute-start(bf16[272,256]{1,0:T(8,128)(2,1)S(1)} %get-tuple-element.77), channel_id=1, source_target_pairs={{1,16},{3,18},{17,0},{19,2},{5,20},{7,22},{21,4},{23,6},{9,24},{11... | collective-permute-start | bytes 417800 | tf_op jit(solution)/shard_map/ppermute | solution.py:280
  12.9 14.7 %collective-permute-start.4 = (bf16[272,256]{1,0:T(8,128)(2,1)S(1)}, bf16[272,256]{1,0:T(8,128)(2,1)S(1)}, u32[]{:S(2)}, u32[]{:S(2)}) collective-permute-start(bf16[272,256]{1,0:T(8,128)(2,1)S(1)} %get-tuple-element.78), channel_id=1, source_target_pairs={{0,2},{2,0},{16,18},{18,16},{4,6},{6,4},{20,22},{22,20},{8,10},{10... | collective-permute-start | bytes 417800 | tf_op jit(solution)/shard_map/ppermute | solution.py:280
  14.9 13.4 %collective-permute-start.5 = (bf16[272,256]{1,0:T(8,128)(2,1)S(1)}, bf16[272,256]{1,0:T(8,128)(2,1)S(1)}, u32[]{:S(2)}, u32[]{:S(2)}) collective-permute-start(bf16[272,256]{1,0:T(8,128)(2,1)S(1)} %get-tuple-element.79), channel_id=1, source_target_pairs={{1,2},{3,0},{17,18},{19,16},{5,6},{7,4},{21,22},{23,20},{9,10},{11... | collective-permute-start | bytes 417800 | tf_op jit(solution)/shard_map/ppermute | solution.py:280
  16.2 15.0 %collective-permute-start.6 = (bf16[272,256]{1,0:T(8,128)(2,1)S(1)}, bf16[272,256]{1,0:T(8,128)(2,1)S(1)}, u32[]{:S(2)}, u32[]{:S(2)}) collective-permute-start(bf16[272,256]{1,0:T(8,128)(2,1)S(1)} %get-tuple-element.80), channel_id=1, source_target_pairs={{1,0},{3,2},{17,16},{19,18},{5,4},{7,6},{21,20},{23,22},{9,8},{11,... | collective-permute-start | bytes 417800 | tf_op jit(solution)/shard_map/ppermute | solution.py:280
  17.5 17.9 %collective-permute-start.14 = (bf16[272,256]{1,0:T(8,128)(2,1)S(1)}, bf16[272,256]{1,0:T(8,128)(2,1)S(1)}, u32[]{:S(2)}, u32[]{:S(2)}) collective-permute-start(bf16[272,256]{1,0:T(8,128)(2,1)S(1)} %get-tuple-element.74), channel_id=1, source_target_pairs={{1,19},{3,17},{17,3},{19,1},{5,23},{7,21},{21,7},{23,5},{9,27},{11... | collective-permute-start | bytes 417800 | tf_op jit(solution)/shard_map/ppermute | solution.py:280
  18.2 18.6 %collective-permute-start.15 = (bf16[272,256]{1,0:T(8,128)(2,1)S(1)}, bf16[272,256]{1,0:T(8,128)(2,1)S(1)}, u32[]{:S(2)}, u32[]{:S(2)}) collective-permute-start(bf16[272,256]{1,0:T(8,128)(2,1)S(1)} %get-tuple-element.75), channel_id=1, source_target_pairs={{0,19},{2,17},{16,3},{18,1},{4,23},{6,21},{20,7},{22,5},{8,27},{10... | collective-permute-start | bytes 417800 | tf_op jit(solution)/shard_map/ppermute | solution.py:280
  27.6 10.5 %collective-permute-start.16 = (bf16[272,256]{1,0:T(8,128)(2,1)S(1)}, bf16[272,256]{1,0:T(8,128)(2,1)S(1)}, u32[]{:S(2)}, u32[]{:S(2)}) collective-permute-start(bf16[272,256]{1,0:T(8,128)(2,1)S(1)} %get-tuple-element.76), channel_id=1, source_target_pairs={{1,17},{3,19},{17,1},{19,3},{5,21},{7,23},{21,5},{23,7},{9,25},{11... | collective-permute-start | bytes 417800 | tf_op jit(solution)/shard_map/ppermute | solution.py:280
  28.3 13.1 %collective-permute-start.17 = (bf16[272,256]{1,0:T(8,128)(2,1)S(1)}, bf16[272,256]{1,0:T(8,128)(2,1)S(1)}, u32[]{:S(2)}, u32[]{:S(2)}) collective-permute-start(bf16[272,256]{1,0:T(8,128)(2,1)S(1)} %get-tuple-element.77), channel_id=1, source_target_pairs={{0,17},{2,19},{16,1},{18,3},{4,21},{6,23},{20,5},{22,7},{8,25},{10... | collective-permute-start | bytes 417800 | tf_op jit(solution)/shard_map/ppermute | solution.py:280
  31.2 11.6 %collective-permute-start.18 = (bf16[272,256]{1,0:T(8,128)(2,1)S(1)}, bf16[272,256]{1,0:T(8,128)(2,1)S(1)}, u32[]{:S(2)}, u32[]{:S(2)}) collective-permute-start(bf16[272,256]{1,0:T(8,128)(2,1)S(1)} %get-tuple-element.78), channel_id=1, source_target_pairs={{1,3},{3,1},{17,19},{19,17},{5,7},{7,5},{21,23},{23,21},{9,11},{11... | collective-permute-start | bytes 417800 | tf_op jit(solution)/shard_map/ppermute | solution.py:280
  35.5 10.7 %collective-permute-start.19 = (bf16[272,256]{1,0:T(8,128)(2,1)S(1)}, bf16[272,256]{1,0:T(8,128)(2,1)S(1)}, u32[]{:S(2)}, u32[]{:S(2)}) collective-permute-start(bf16[272,256]{1,0:T(8,128)(2,1)S(1)} %get-tuple-element.79), channel_id=1, source_target_pairs={{0,3},{2,1},{16,19},{18,17},{4,7},{6,5},{20,23},{22,21},{8,11},{10... | collective-permute-start | bytes 417800 | tf_op jit(solution)/shard_map/ppermute | solution.py:280
  36.8 10.7 %collective-permute-start.20 = (bf16[272,256]{1,0:T(8,128)(2,1)S(1)}, bf16[272,256]{1,0:T(8,128)(2,1)S(1)}, u32[]{:S(2)}, u32[]{:S(2)}) collective-permute-start(bf16[272,256]{1,0:T(8,128)(2,1)S(1)} %get-tuple-element.80), channel_id=1, source_target_pairs={{0,1},{2,3},{16,17},{18,19},{4,5},{6,7},{20,21},{22,23},{8,9},{10,... | collective-permute-start | bytes 417800 | tf_op jit(solution)/shard_map/ppermute | solution.py:280
  38.1 11.9 %collective-permute-start.7 = (bf16[256,256]{1,0:T(8,128)(2,1)S(1)}, bf16[256,256]{1,0:T(8,128)(2,1)S(1)}, u32[]{:S(2)}, u32[]{:S(2)}) collective-permute-start(bf16[256,256]{1,0:T(8,128)(2,1)S(1)} %get-tuple-element.62), channel_id=1, source_target_pairs={{0,18},{2,16},{16,2},{18,0},{4,22},{6,20},{20,6},{22,4},{8,26},{10... | collective-permute-start | bytes 393224 | tf_op jit(solution)/shard_map/ppermute | solution.py:292
  41.5 9.9 %collective-permute-start.8 = (bf16[256,256]{1,0:T(8,128)(2,1)S(1)}, bf16[256,256]{1,0:T(8,128)(2,1)S(1)}, u32[]{:S(2)}, u32[]{:S(2)}) collective-permute-start(bf16[256,256]{1,0:T(8,128)(2,1)S(1)} %get-tuple-element.63), channel_id=1, source_target_pairs={{0,19},{2,17},{16,3},{18,1},{4,23},{6,21},{20,7},{22,5},{8,27},{10... | collective-permute-start | bytes 393224 | tf_op jit(solution)/shard_map/ppermute | solution.py:292
  42.8 9.9 %collective-permute-start.9 = (bf16[256,256]{1,0:T(8,128)(2,1)S(1)}, bf16[256,256]{1,0:T(8,128)(2,1)S(1)}, u32[]{:S(2)}, u32[]{:S(2)}) collective-permute-start(bf16[256,256]{1,0:T(8,128)(2,1)S(1)} %get-tuple-element.64), channel_id=1, source_target_pairs={{0,16},{2,18},{16,0},{18,2},{4,20},{6,22},{20,4},{22,6},{8,24},{10... | collective-permute-start | bytes 393224 | tf_op jit(solution)/shard_map/ppermute | solution.py:292
  46.2 7.1 %collective-permute-start.10 = (bf16[256,256]{1,0:T(8,128)(2,1)S(1)}, bf16[256,256]{1,0:T(8,128)(2,1)S(1)}, u32[]{:S(2)}, u32[]{:S(2)}) collective-permute-start(bf16[256,256]{1,0:T(8,128)(2,1)S(1)} %get-tuple-element.65), channel_id=1, source_target_pairs={{0,17},{2,19},{16,1},{18,3},{4,21},{6,23},{20,5},{22,7},{8,25},{10... | collective-permute-start | bytes 393224 | tf_op jit(solution)/shard_map/ppermute | solution.py:292
  47.5 7.5 %collective-permute-start.11 = (bf16[256,256]{1,0:T(8,128)(2,1)S(1)}, bf16[256,256]{1,0:T(8,128)(2,1)S(1)}, u32[]{:S(2)}, u32[]{:S(2)}) collective-permute-start(bf16[256,256]{1,0:T(8,128)(2,1)S(1)} %get-tuple-element.66), channel_id=1, source_target_pairs={{0,2},{2,0},{16,18},{18,16},{4,6},{6,4},{20,22},{22,20},{8,10},{10... | collective-permute-start | bytes 393224 | tf_op jit(solution)/shard_map/ppermute | solution.py:292
  50.0 5.7 %collective-permute-start.12 = (bf16[256,256]{1,0:T(8,128)(2,1)S(1)}, bf16[256,256]{1,0:T(8,128)(2,1)S(1)}, u32[]{:S(2)}, u32[]{:S(2)}) collective-permute-start(bf16[256,256]{1,0:T(8,128)(2,1)S(1)} %get-tuple-element.67), channel_id=1, source_target_pairs={{0,3},{2,1},{16,19},{18,17},{4,7},{6,5},{20,23},{22,21},{8,11},{10... | collective-permute-start | bytes 393224 | tf_op jit(solution)/shard_map/ppermute | solution.py:292
  51.4 5.7 %collective-permute-start.13 = (bf16[256,256]{1,0:T(8,128)(2,1)S(1)}, bf16[256,256]{1,0:T(8,128)(2,1)S(1)}, u32[]{:S(2)}, u32[]{:S(2)}) collective-permute-start(bf16[256,256]{1,0:T(8,128)(2,1)S(1)} %get-tuple-element.68), channel_id=1, source_target_pairs={{0,1},{2,3},{16,17},{18,19},{4,5},{6,7},{20,21},{22,23},{8,9},{10,... | collective-permute-start | bytes 393224 | tf_op jit(solution)/shard_map/ppermute | solution.py:292
  52.7 5.1 %collective-permute-start.21 = (bf16[256,256]{1,0:T(8,128)(2,1)S(1)}, bf16[256,256]{1,0:T(8,128)(2,1)S(1)}, u32[]{:S(2)}, u32[]{:S(2)}) collective-permute-start(bf16[256,256]{1,0:T(8,128)(2,1)S(1)} %get-tuple-element.82), channel_id=1, source_target_pairs={{1,19},{3,17},{17,3},{19,1},{5,23},{7,21},{21,7},{23,5},{9,27},{11... | collective-permute-start | bytes 393224 | tf_op jit(solution)/shard_map/ppermute | solution.py:292
  53.4 7.2 %collective-permute-start.22 = (bf16[256,256]{1,0:T(8,128)(2,1)S(1)}, bf16[256,256]{1,0:T(8,128)(2,1)S(1)}, u32[]{:S(2)}, u32[]{:S(2)}) collective-permute-start(bf16[256,256]{1,0:T(8,128)(2,1)S(1)} %get-tuple-element.83), channel_id=1, source_target_pairs={{1,18},{3,16},{17,2},{19,0},{5,22},{7,20},{21,6},{23,4},{9,26},{11... | collective-permute-start | bytes 393224 | tf_op jit(solution)/shard_map/ppermute | solution.py:292
  55.1 6.8 %collective-permute-start.23 = (bf16[256,256]{1,0:T(8,128)(2,1)S(1)}, bf16[256,256]{1,0:T(8,128)(2,1)S(1)}, u32[]{:S(2)}, u32[]{:S(2)}) collective-permute-start(bf16[256,256]{1,0:T(8,128)(2,1)S(1)} %get-tuple-element.84), channel_id=1, source_target_pairs={{1,17},{3,19},{17,1},{19,3},{5,21},{7,23},{21,5},{23,7},{9,25},{11... | collective-permute-start | bytes 393224 | tf_op jit(solution)/shard_map/ppermute | solution.py:292
  55.8 8.4 %collective-permute-start.24 = (bf16[256,256]{1,0:T(8,128)(2,1)S(1)}, bf16[256,256]{1,0:T(8,128)(2,1)S(1)}, u32[]{:S(2)}, u32[]{:S(2)}) collective-permute-start(bf16[256,256]{1,0:T(8,128)(2,1)S(1)} %get-tuple-element.85), channel_id=1, source_target_pairs={{1,16},{3,18},{17,0},{19,2},{5,20},{7,22},{21,4},{23,6},{9,24},{11... | collective-permute-start | bytes 393224 | tf_op jit(solution)/shard_map/ppermute | solution.py:292
  57.1 7.1 %collective-permute-start.25 = (bf16[256,256]{1,0:T(8,128)(2,1)S(1)}, bf16[256,256]{1,0:T(8,128)(2,1)S(1)}, u32[]{:S(2)}, u32[]{:S(2)}) collective-permute-start(bf16[256,256]{1,0:T(8,128)(2,1)S(1)} %get-tuple-element.86), channel_id=1, source_target_pairs={{1,3},{3,1},{17,19},{19,17},{5,7},{7,5},{21,23},{23,21},{9,11},{11... | collective-permute-start | bytes 393224 | tf_op jit(solution)/shard_map/ppermute | solution.py:292
  57.8 10.9 %collective-permute-start.26 = (bf16[256,256]{1,0:T(8,128)(2,1)S(1)}, bf16[256,256]{1,0:T(8,128)(2,1)S(1)}, u32[]{:S(2)}, u32[]{:S(2)}) collective-permute-start(bf16[256,256]{1,0:T(8,128)(2,1)S(1)} %get-tuple-element.87), channel_id=1, source_target_pairs={{1,2},{3,0},{17,18},{19,16},{5,6},{7,4},{21,22},{23,20},{9,10},{11... | collective-permute-start | bytes 393224 | tf_op jit(solution)/shard_map/ppermute | solution.py:292
  60.5 8.1 %collective-permute-start.27 = (bf16[256,256]{1,0:T(8,128)(2,1)S(1)}, bf16[256,256]{1,0:T(8,128)(2,1)S(1)}, u32[]{:S(2)}, u32[]{:S(2)}) collective-permute-start(bf16[256,256]{1,0:T(8,128)(2,1)S(1)} %get-tuple-element.88), channel_id=1, source_target_pairs={{1,0},{3,2},{17,16},{19,18},{5,4},{7,6},{21,20},{23,22},{9,8},{11,... | collective-permute-start | bytes 393224 | tf_op jit(solution)/shard_map/ppermute | solution.py:292

commit v13 on v12

--- a/solution.py
+++ b/solution.py
@@ -274,24 +274,24 @@
                 copy.wait()
 
 
+def moved(share, step, parts, real):
+    pairs = [(dev, dev ^ (step if real(dev) else step % 2)) for dev in range(parts)]
+    return lax.ppermute(share, AXES, pairs)
+
+
 def to_turn(shares, order, turn):
-    parts = len(order)
+    def real(step):
+        return lambda dev: (dev ^ step) % 2 == turn
+
     return [
-        lax.ppermute(
-            share, AXES, [(dev, dev ^ step) for dev in range(parts) if (dev ^ step) % 2 == turn]
-        )
-        if step
-        else share
+        moved(share, step, len(order), real(step)) if step else share
         for step, share in zip(order, shares)
     ]
 
 
 def from_turn(shares, order, turn):
-    parts = len(order)
     return [
-        lax.ppermute(share, AXES, [(dev, dev ^ step) for dev in range(turn, parts, 2)])
-        if step
-        else share
+        moved(share, step, len(order), lambda dev: dev % 2 == turn) if step else share
         for step, share in zip(order, shares)
     ]
 
@@ -339,10 +339,11 @@
 
     early = to_turn(shares, order, 0)
     shares, early = zip(*(lax.optimization_barrier(pair) for pair in zip(shares, early)))
-    early = list(attend(0, early))
-    *tied, early[-1] = lax.optimization_barrier((*shares[FLIGHTS:], early[-1]))
-    late = attend(1, to_turn([*shares[:FLIGHTS], *tied], order, 1))
-    back = [from_turn(outs, order, turn) for turn, outs in enumerate((early, late))]
+    outs = list(attend(0, early))
+    *tied, outs[-1] = lax.optimization_barrier((*shares[FLIGHTS:], outs[-1]))
+    late = to_turn([*shares[:FLIGHTS], *tied], order, 1)
+    late[order.index(1)] = early[order.index(1)]
+    back = [from_turn(outs, order, 0), from_turn(attend(1, late), order, 1)]
     out_shape = jax.ShapeDtypeStruct((1, 1, BLK, width), kind)
     return pl.pallas_call(
         functools.partial(unpack_kernel, seq_count, order),

time: 70.4 us -> 54.4 us (0.77)
  starting transfers between devices: 52.5 us -> 38.3 us
  waiting for transfers between devices: 8.74 us -> 7.4 us
    ppermute x28 -> x27, starting transfers between devices: 52.5 us -> 38.3 us  [moved(): return lax.ppermute(share, AXES, pairs)]
    ppermute x28 -> x27, waiting for transfers between devices: 8.74 us -> 7.4 us  [moved(): return lax.ppermute(share, AXES, pairs)]
  transfers between devices with their start and end apart: 28 -> 27, of which waited for: 4 -> 4; matrix products, arithmetic and copies ran while one was open for 0% -> 0% of each run, Pallas kernels for 5% -> 7%
where the time goes in v13:
time: 54.4 us; the launch traced here: 54 us
  starting transfers between devices  38.3 us (70%)
  waiting for transfers between devices  7.4 us (14%)
  Pallas kernels  6.15 us (11%)
  between operations  2.2 us (4%)
    ppermute x27, starting transfers between devices, moved(): return lax.ppermute(share, AXES, pairs)  38.3 us
    ppermute x27, waiting for transfers between devices, moved(): return lax.ppermute(share, AXES, pairs)  7.4 us
    pallas_call x2, Pallas kernels, attend(): pl.pallas_call(functools.partial(attend_kernel, seq_count, order, turn),...  3.63 us
    pallas_call x1, Pallas kernels, by_pairs(): pl.pallas_call(functools.partial(pack_kernel, seq_count, order), out_shap...  1.43 us
  transfers between devices with their start and end apart: 27, of which 4 were waited for; matrix products, arithmetic and copies ran while one was open for 0% of the time, Pallas kernels for 7%

profile of v13, /device:TPU:0, one launch (start us, length us, event | category | flops | bytes accessed | tf_op | source)
XLA Modules:
  0.0 54.0 jit_solution(10097347166795586627)
XLA Ops:
  0.6 1.4 %pack.1 = (bf16[272,256]{1,0:T(8,128)(2,1)S(1)}, bf16[272,256]{1,0:T(8,128)(2,1)S(1)}, bf16[272,256]{1,0:T(8,128)(2,1)S(1)}, bf16[272,256]{1,0:T(8,128)(2,1)S(1)...) custom-call(s32[1,1,2]{2,1,0:T(1,128)} %refs_0_.1, ...), custom_call_target="tpu_custom_call" | custom-call | tf_op jit(solution)/shard_map/pack/pallas_call | solution.py:310
  2.1 5.8 %collective-permute-start = (bf16[272,256]{1,0:T(8,128)(2,1)S(1)}, bf16[272,256]{1,0:T(8,128)(2,1)S(1)}, u32[]{:S(2)}, u32[]{:S(2)}) collective-permute-start(bf16[272,256]{1,0:T(8,128)(2,1)S(1)} %get-tuple-element.71), channel_id=1, source_target_pairs={{0,18},{1,1},{2,16},{3,3},{16,2},{17,17},{18,0},{19,19},{4,22},{5,... | collective-permute-start | bytes 417800 | tf_op jit(solution)/shard_map/ppermute | solution.py:279
  7.9 0.1 collective-permute-start.1
  7.9 2.4 %collective-permute-start.2 = (bf16[272,256]{1,0:T(8,128)(2,1)S(1)}, bf16[272,256]{1,0:T(8,128)(2,1)S(1)}, u32[]{:S(2)}, u32[]{:S(2)}) collective-permute-start(bf16[272,256]{1,0:T(8,128)(2,1)S(1)} %get-tuple-element.73), channel_id=1, source_target_pairs={{0,16},{1,1},{2,18},{3,3},{16,0},{17,17},{18,2},{19,19},{4,20},{5,... | collective-permute-start | bytes 417800 | tf_op jit(solution)/shard_map/ppermute | solution.py:279
  10.4 0.1 collective-permute-start.3
  10.4 2.2 %collective-permute-start.4 = (bf16[272,256]{1,0:T(8,128)(2,1)S(1)}, bf16[272,256]{1,0:T(8,128)(2,1)S(1)}, u32[]{:S(2)}, u32[]{:S(2)}) collective-permute-start(bf16[272,256]{1,0:T(8,128)(2,1)S(1)} %get-tuple-element.75), channel_id=1, source_target_pairs={{0,2},{1,1},{2,0},{3,3},{16,18},{17,17},{18,16},{19,19},{4,6},{5,5... | collective-permute-start | bytes 417800 | tf_op jit(solution)/shard_map/ppermute | solution.py:279
  12.6 0.0 collective-permute-done.refs_0_
  12.7 0.1 collective-permute-start.5
  12.8 0.5 collective-permute-done.1.refs_1_
  13.3 1.2 %collective-permute-start.6 = (bf16[272,256]{1,0:T(8,128)(2,1)S(1)}, bf16[272,256]{1,0:T(8,128)(2,1)S(1)}, u32[]{:S(2)}, u32[]{:S(2)}) collective-permute-start(bf16[272,256]{1,0:T(8,128)(2,1)S(1)} %get-tuple-element.56), channel_id=1, source_target_pairs={{0,1},{1,0},{2,3},{3,2},{16,17},{17,16},{18,19},{19,18},{4,5},{5,4... | collective-permute-start | bytes 417800 | tf_op jit(solution)/shard_map/ppermute | solution.py:279
  14.6 1.8 %collective-permute-done.2.refs_2_ = bf16[272,256]{1,0:T(8,128)(2,1)S(1)} collective-permute-done((bf16[272,256]{1,0:T(8,128)(2,1)S(1)}, bf16[272,256]{1,0:T(8,128)(2,1)S(1)}, u32[]{:S(2)}, u32[]{:S(2)}) %collective-permute-start.2) | collective-permute-done | bytes 139296 | tf_op jit(solution)/shard_map/ppermute | solution.py:279
  16.4 0.7 %collective-permute-start.14 = (bf16[272,256]{1,0:T(8,128)(2,1)S(1)}, bf16[272,256]{1,0:T(8,128)(2,1)S(1)}, u32[]{:S(2)}, u32[]{:S(2)}) collective-permute-start(bf16[272,256]{1,0:T(8,128)(2,1)S(1)} %get-tuple-element.71), channel_id=1, source_target_pairs={{0,0},{1,19},{2,2},{3,17},{16,16},{17,3},{18,18},{19,1},{4,4},{5,2... | collective-permute-start | bytes 417800 | tf_op jit(solution)/shard_map/ppermute | solution.py:279
  17.0 0.0 collective-permute-done.3.refs_3_
  17.1 1.7 %collective-permute-start.15 = (bf16[272,256]{1,0:T(8,128)(2,1)S(1)}, bf16[272,256]{1,0:T(8,128)(2,1)S(1)}, u32[]{:S(2)}, u32[]{:S(2)}) collective-permute-start(bf16[272,256]{1,0:T(8,128)(2,1)S(1)} %get-tuple-element.72), channel_id=1, source_target_pairs={{0,19},{1,0},{2,17},{3,2},{16,3},{17,16},{18,1},{19,18},{4,23},{5,... | collective-permute-start | bytes 417800 | tf_op jit(solution)/shard_map/ppermute | solution.py:279
  18.8 0.0 collective-permute-done.4.refs_4_
  18.8 0.7 %collective-permute-start.16 = (bf16[272,256]{1,0:T(8,128)(2,1)S(1)}, bf16[272,256]{1,0:T(8,128)(2,1)S(1)}, u32[]{:S(2)}, u32[]{:S(2)}) collective-permute-start(bf16[272,256]{1,0:T(8,128)(2,1)S(1)} %get-tuple-element.73), channel_id=1, source_target_pairs={{0,0},{1,17},{2,2},{3,19},{16,16},{17,1},{18,18},{19,3},{4,4},{5,2... | collective-permute-start | bytes 417800 | tf_op jit(solution)/shard_map/ppermute | solution.py:279
  19.5 1.6 %collective-permute-start.17 = (bf16[272,256]{1,0:T(8,128)(2,1)S(1)}, bf16[272,256]{1,0:T(8,128)(2,1)S(1)}, u32[]{:S(2)}, u32[]{:S(2)}) collective-permute-start(bf16[272,256]{1,0:T(8,128)(2,1)S(1)} %get-tuple-element.74), channel_id=1, source_target_pairs={{0,17},{1,0},{2,19},{3,2},{16,1},{17,16},{18,3},{19,18},{4,21},{5,... | collective-permute-start | bytes 417800 | tf_op jit(solution)/shard_map/ppermute | solution.py:279
  21.1 0.0 collective-permute-done.6.refs_6_
  21.1 0.7 %collective-permute-start.18 = (bf16[272,256]{1,0:T(8,128)(2,1)S(1)}, bf16[272,256]{1,0:T(8,128)(2,1)S(1)}, u32[]{:S(2)}, u32[]{:S(2)}) collective-permute-start(bf16[272,256]{1,0:T(8,128)(2,1)S(1)} %get-tuple-element.75), channel_id=1, source_target_pairs={{0,0},{1,3},{2,2},{3,1},{16,16},{17,19},{18,18},{19,17},{4,4},{5,7... | collective-permute-start | bytes 417800 | tf_op jit(solution)/shard_map/ppermute | solution.py:279
  23.1 3.6 %attend.2 = (bf16[256,256]{1,0:T(8,128)(2,1)S(1)}, bf16[256,256]{1,0:T(8,128)(2,1)S(1)}, bf16[256,256]{1,0:T(8,128)(2,1)S(1)}, bf16[256,256]{1,0:T(8,128)(2,1)S(...) custom-call(s32[1]{0:T(128)S(6)} %copy.8.source_len, ...), custom_call_target="tpu_custom_call" | custom-call | flops 335544320 | bytes 2097152 | tf_op jit(solution)/shard_map/attend/pallas_call | solution.py:329
  26.7 0.0 collective-permute-done.14.refs_0_
  26.7 0.1 collective-permute-start.19
  26.8 3.3 %collective-permute-start.7 = (bf16[256,256]{1,0:T(8,128)(2,1)S(1)}, bf16[256,256]{1,0:T(8,128)(2,1)S(1)}, u32[]{:S(2)}, u32[]{:S(2)}) collective-permute-start(bf16[256,256]{1,0:T(8,128)(2,1)S(1)} %get-tuple-element.60), channel_id=1, source_target_pairs={{0,18},{1,1},{2,16},{3,3},{16,2},{17,17},{18,0},{19,19},{4,22},{5,... | collective-permute-start | bytes 393224 | tf_op jit(solution)/shard_map/ppermute | solution.py:279
  30.1 0.1 collective-permute-start.8
  30.2 0.0 collective-permute-done.17.refs_3_
  30.2 3.4 %collective-permute-start.9 = (bf16[256,256]{1,0:T(8,128)(2,1)S(1)}, bf16[256,256]{1,0:T(8,128)(2,1)S(1)}, u32[]{:S(2)}, u32[]{:S(2)}) collective-permute-start(bf16[256,256]{1,0:T(8,128)(2,1)S(1)} %get-tuple-element.62), channel_id=1, source_target_pairs={{0,16},{1,1},{2,18},{3,3},{16,0},{17,17},{18,2},{19,19},{4,20},{5,... | collective-permute-start | bytes 393224 | tf_op jit(solution)/shard_map/ppermute | solution.py:279
  33.7 0.0 collective-permute-done.18.refs_4_
  33.7 0.1 collective-permute-start.10
  33.8 2.4 %collective-permute-start.11 = (bf16[256,256]{1,0:T(8,128)(2,1)S(1)}, bf16[256,256]{1,0:T(8,128)(2,1)S(1)}, u32[]{:S(2)}, u32[]{:S(2)}) collective-permute-start(bf16[256,256]{1,0:T(8,128)(2,1)S(1)} %get-tuple-element.64), channel_id=1, source_target_pairs={{0,2},{1,1},{2,0},{3,3},{16,18},{17,17},{18,16},{19,19},{4,6},{5,5... | collective-permute-start | bytes 393224 | tf_op jit(solution)/shard_map/ppermute | solution.py:279
  36.2 2.5 %collective-permute-start.12 = (bf16[256,256]{1,0:T(8,128)(2,1)S(1)}, bf16[256,256]{1,0:T(8,128)(2,1)S(1)}, u32[]{:S(2)}, u32[]{:S(2)}) collective-permute-start(bf16[256,256]{1,0:T(8,128)(2,1)S(1)} %get-tuple-element.65), channel_id=1, source_target_pairs={{0,3},{1,0},{2,1},{3,2},{16,19},{17,16},{18,17},{19,18},{4,7},{5,4... | collective-permute-start | bytes 393224 | tf_op jit(solution)/shard_map/ppermute | solution.py:279
  38.7 0.7 %collective-permute-start.20 = (bf16[256,256]{1,0:T(8,128)(2,1)S(1)}, bf16[256,256]{1,0:T(8,128)(2,1)S(1)}, u32[]{:S(2)}, u32[]{:S(2)}) collective-permute-start(bf16[256,256]{1,0:T(8,128)(2,1)S(1)} %get-tuple-element.78), channel_id=1, source_target_pairs={{0,0},{1,19},{2,2},{3,17},{16,16},{17,3},{18,18},{19,1},{4,4},{5,2... | collective-permute-start | bytes 393224 | tf_op jit(solution)/shard_map/ppermute | solution.py:279
  39.4 0.0 collective-permute-done.10.refs_3_
  39.4 2.9 %collective-permute-start.21 = (bf16[256,256]{1,0:T(8,128)(2,1)S(1)}, bf16[256,256]{1,0:T(8,128)(2,1)S(1)}, u32[]{:S(2)}, u32[]{:S(2)}) collective-permute-start(bf16[256,256]{1,0:T(8,128)(2,1)S(1)} %get-tuple-element.79), channel_id=1, source_target_pairs={{0,1},{1,18},{2,3},{3,16},{16,17},{17,2},{18,19},{19,0},{4,5},{5,2... | collective-permute-start | bytes 393224 | tf_op jit(solution)/shard_map/ppermute | solution.py:279
  42.3 0.0 collective-permute-done.11.refs_4_
  42.3 0.7 %collective-permute-start.22 = (bf16[256,256]{1,0:T(8,128)(2,1)S(1)}, bf16[256,256]{1,0:T(8,128)(2,1)S(1)}, u32[]{:S(2)}, u32[]{:S(2)}) collective-permute-start(bf16[256,256]{1,0:T(8,128)(2,1)S(1)} %get-tuple-element.80), channel_id=1, source_target_pairs={{0,0},{1,17},{2,2},{3,19},{16,16},{17,1},{18,18},{19,3},{4,4},{5,2... | collective-permute-start | bytes 393224 | tf_op jit(solution)/shard_map/ppermute | solution.py:279
  43.0 0.0 collective-permute-done.12.refs_5_
  43.0 2.6 %collective-permute-start.23 = (bf16[256,256]{1,0:T(8,128)(2,1)S(1)}, bf16[256,256]{1,0:T(8,128)(2,1)S(1)}, u32[]{:S(2)}, u32[]{:S(2)}) collective-permute-start(bf16[256,256]{1,0:T(8,128)(2,1)S(1)} %get-tuple-element.81), channel_id=1, source_target_pairs={{0,1},{1,16},{2,3},{3,18},{16,17},{17,0},{18,19},{19,2},{4,5},{5,2... | collective-permute-start | bytes 393224 | tf_op jit(solution)/shard_map/ppermute | solution.py:279
  45.6 0.0 collective-permute-done.13.refs_6_
  45.6 0.7 %collective-permute-start.24 = (bf16[256,256]{1,0:T(8,128)(2,1)S(1)}, bf16[256,256]{1,0:T(8,128)(2,1)S(1)}, u32[]{:S(2)}, u32[]{:S(2)}) collective-permute-start(bf16[256,256]{1,0:T(8,128)(2,1)S(1)} %get-tuple-element.82), channel_id=1, source_target_pairs={{0,0},{1,3},{2,2},{3,1},{16,16},{17,19},{18,18},{19,17},{4,4},{5,7... | collective-permute-start | bytes 393224 | tf_op jit(solution)/shard_map/ppermute | solution.py:279
  46.3 0.0 collective-permute-done.20.refs_8_
  46.3 1.6 %collective-permute-start.25 = (bf16[256,256]{1,0:T(8,128)(2,1)S(1)}, bf16[256,256]{1,0:T(8,128)(2,1)S(1)}, u32[]{:S(2)}, u32[]{:S(2)}) collective-permute-start(bf16[256,256]{1,0:T(8,128)(2,1)S(1)} %get-tuple-element.83), channel_id=1, source_target_pairs={{0,1},{1,2},{2,3},{3,0},{16,17},{17,18},{18,19},{19,16},{4,5},{5,6... | collective-permute-start | bytes 393224 | tf_op jit(solution)/shard_map/ppermute | solution.py:279
  47.8 0.1 collective-permute-start.26
  47.9 0.0 collective-permute-done.22.refs_10_
  47.9 2.3 %collective-permute-done.23.refs_11_ = bf16[256,256]{1,0:T(8,128)(2,1)S(1)} collective-permute-done((bf16[256,256]{1,0:T(8,128)(2,1)S(1)}, bf16[256,256]{1,0:T(8,128)(2,1)S(1)}, u32[]{:S(2)}, u32[]{:S(2)}) %collective-permute-start.23) | collective-permute-done | bytes 131104 | tf_op jit(solution)/shard_map/ppermute | solution.py:279
  50.2 0.0 collective-permute-done.24.refs_12_
  50.2 2.7 %collective-permute-done.25.refs_13_ = bf16[256,256]{1,0:T(8,128)(2,1)S(1)} collective-permute-done((bf16[256,256]{1,0:T(8,128)(2,1)S(1)}, bf16[256,256]{1,0:T(8,128)(2,1)S(1)}, u32[]{:S(2)}, u32[]{:S(2)}) %collective-permute-start.25) | collective-permute-done | bytes 131104 | tf_op jit(solution)/shard_map/ppermute | solution.py:279
  52.9 0.0 collective-permute-done.26.refs_14_
  52.9 1.1 %unpack.1 = (bf16[1,1,128,2048]{3,2,1,0:T(8,128)(2,1)}, bf16[1,1,128,2048]{3,2,1,0:T(8,128)(2,1)}) custom-call(bf16[256,256]{1,0:T(8,128)(2,1)S(1)} %collective-permute-done.7.refs_0_, bf16[256,256]{1,0:T(8,128)(2,1)S(1)} %collective-permute-done.8.refs_1_, bf16[256,256]{1,0:T(8,128)(2,1)S(1)} %collective-permute-done.9.refs_2_, ...), custom_call_target="tpu_custom_call" | custom-call | tf_op jit(solution)/shard_map/unpack/pallas_call | solution.py:348
  (10 shorter events, 0.1 us)
Async XLA Ops:
  2.1 10.6 %collective-permute-start = (bf16[272,256]{1,0:T(8,128)(2,1)S(1)}, bf16[272,256]{1,0:T(8,128)(2,1)S(1)}, u32[]{:S(2)}, u32[]{:S(2)}) collective-permute-start(bf16[272,256]{1,0:T(8,128)(2,1)S(1)} %get-tuple-element.71), channel_id=1, source_target_pairs={{0,18},{1,1},{2,16},{3,3},{16,2},{17,17},{18,0},{19,19},{4,22},{5,... | collective-permute-start | bytes 417800 | tf_op jit(solution)/shard_map/ppermute | solution.py:279
  7.9 5.4 %collective-permute-start.1 = (bf16[272,256]{1,0:T(8,128)(2,1)S(1)}, bf16[272,256]{1,0:T(8,128)(2,1)S(1)}, u32[]{:S(2)}, u32[]{:S(2)}) collective-permute-start(bf16[272,256]{1,0:T(8,128)(2,1)S(1)} %get-tuple-element.72), channel_id=1, source_target_pairs={{0,1},{1,18},{2,3},{3,16},{16,17},{17,2},{18,19},{19,0},{4,5},{5,2... | collective-permute-start | bytes 417800 | tf_op jit(solution)/shard_map/ppermute | solution.py:279
  7.9 8.4 %collective-permute-start.2 = (bf16[272,256]{1,0:T(8,128)(2,1)S(1)}, bf16[272,256]{1,0:T(8,128)(2,1)S(1)}, u32[]{:S(2)}, u32[]{:S(2)}) collective-permute-start(bf16[272,256]{1,0:T(8,128)(2,1)S(1)} %get-tuple-element.73), channel_id=1, source_target_pairs={{0,16},{1,1},{2,18},{3,3},{16,0},{17,17},{18,2},{19,19},{4,20},{5,... | collective-permute-start | bytes 417800 | tf_op jit(solution)/shard_map/ppermute | solution.py:279
  10.4 6.7 %collective-permute-start.3 = (bf16[272,256]{1,0:T(8,128)(2,1)S(1)}, bf16[272,256]{1,0:T(8,128)(2,1)S(1)}, u32[]{:S(2)}, u32[]{:S(2)}) collective-permute-start(bf16[272,256]{1,0:T(8,128)(2,1)S(1)} %get-tuple-element.74), channel_id=1, source_target_pairs={{0,1},{1,16},{2,3},{3,18},{16,17},{17,0},{18,19},{19,2},{4,5},{5,2... | collective-permute-start | bytes 417800 | tf_op jit(solution)/shard_map/ppermute | solution.py:279
  10.4 8.4 %collective-permute-start.4 = (bf16[272,256]{1,0:T(8,128)(2,1)S(1)}, bf16[272,256]{1,0:T(8,128)(2,1)S(1)}, u32[]{:S(2)}, u32[]{:S(2)}) collective-permute-start(bf16[272,256]{1,0:T(8,128)(2,1)S(1)} %get-tuple-element.75), channel_id=1, source_target_pairs={{0,2},{1,1},{2,0},{3,3},{16,18},{17,17},{18,16},{19,19},{4,6},{5,5... | collective-permute-start | bytes 417800 | tf_op jit(solution)/shard_map/ppermute | solution.py:279
  12.7 6.8 %collective-permute-start.5 = (bf16[272,256]{1,0:T(8,128)(2,1)S(1)}, bf16[272,256]{1,0:T(8,128)(2,1)S(1)}, u32[]{:S(2)}, u32[]{:S(2)}) collective-permute-start(bf16[272,256]{1,0:T(8,128)(2,1)S(1)} %get-tuple-element.76), channel_id=1, source_target_pairs={{0,1},{1,2},{2,3},{3,0},{16,17},{17,18},{18,19},{19,16},{4,5},{5,6... | collective-permute-start | bytes 417800 | tf_op jit(solution)/shard_map/ppermute | solution.py:279
  13.3 7.8 %collective-permute-start.6 = (bf16[272,256]{1,0:T(8,128)(2,1)S(1)}, bf16[272,256]{1,0:T(8,128)(2,1)S(1)}, u32[]{:S(2)}, u32[]{:S(2)}) collective-permute-start(bf16[272,256]{1,0:T(8,128)(2,1)S(1)} %get-tuple-element.56), channel_id=1, source_target_pairs={{0,1},{1,0},{2,3},{3,2},{16,17},{17,16},{18,19},{19,18},{4,5},{5,4... | collective-permute-start | bytes 417800 | tf_op jit(solution)/shard_map/ppermute | solution.py:279
  16.4 10.3 %collective-permute-start.14 = (bf16[272,256]{1,0:T(8,128)(2,1)S(1)}, bf16[272,256]{1,0:T(8,128)(2,1)S(1)}, u32[]{:S(2)}, u32[]{:S(2)}) collective-permute-start(bf16[272,256]{1,0:T(8,128)(2,1)S(1)} %get-tuple-element.71), channel_id=1, source_target_pairs={{0,0},{1,19},{2,2},{3,17},{16,16},{17,3},{18,18},{19,1},{4,4},{5,2... | collective-permute-start | bytes 417800 | tf_op jit(solution)/shard_map/ppermute | solution.py:279
  17.1 9.7 %collective-permute-start.15 = (bf16[272,256]{1,0:T(8,128)(2,1)S(1)}, bf16[272,256]{1,0:T(8,128)(2,1)S(1)}, u32[]{:S(2)}, u32[]{:S(2)}) collective-permute-start(bf16[272,256]{1,0:T(8,128)(2,1)S(1)} %get-tuple-element.72), channel_id=1, source_target_pairs={{0,19},{1,0},{2,17},{3,2},{16,3},{17,16},{18,1},{19,18},{4,23},{5,... | collective-permute-start | bytes 417800 | tf_op jit(solution)/shard_map/ppermute | solution.py:279
  18.8 11.3 %collective-permute-start.16 = (bf16[272,256]{1,0:T(8,128)(2,1)S(1)}, bf16[272,256]{1,0:T(8,128)(2,1)S(1)}, u32[]{:S(2)}, u32[]{:S(2)}) collective-permute-start(bf16[272,256]{1,0:T(8,128)(2,1)S(1)} %get-tuple-element.73), channel_id=1, source_target_pairs={{0,0},{1,17},{2,2},{3,19},{16,16},{17,1},{18,18},{19,3},{4,4},{5,2... | collective-permute-start | bytes 417800 | tf_op jit(solution)/shard_map/ppermute | solution.py:279
  19.5 10.7 %collective-permute-start.17 = (bf16[272,256]{1,0:T(8,128)(2,1)S(1)}, bf16[272,256]{1,0:T(8,128)(2,1)S(1)}, u32[]{:S(2)}, u32[]{:S(2)}) collective-permute-start(bf16[272,256]{1,0:T(8,128)(2,1)S(1)} %get-tuple-element.74), channel_id=1, source_target_pairs={{0,17},{1,0},{2,19},{3,2},{16,1},{17,16},{18,3},{19,18},{4,21},{5,... | collective-permute-start | bytes 417800 | tf_op jit(solution)/shard_map/ppermute | solution.py:279
  21.1 12.6 %collective-permute-start.18 = (bf16[272,256]{1,0:T(8,128)(2,1)S(1)}, bf16[272,256]{1,0:T(8,128)(2,1)S(1)}, u32[]{:S(2)}, u32[]{:S(2)}) collective-permute-start(bf16[272,256]{1,0:T(8,128)(2,1)S(1)} %get-tuple-element.75), channel_id=1, source_target_pairs={{0,0},{1,3},{2,2},{3,1},{16,16},{17,19},{18,18},{19,17},{4,4},{5,7... | collective-permute-start | bytes 417800 | tf_op jit(solution)/shard_map/ppermute | solution.py:279
  26.7 7.0 %collective-permute-start.19 = (bf16[272,256]{1,0:T(8,128)(2,1)S(1)}, bf16[272,256]{1,0:T(8,128)(2,1)S(1)}, u32[]{:S(2)}, u32[]{:S(2)}) collective-permute-start(bf16[272,256]{1,0:T(8,128)(2,1)S(1)} %get-tuple-element.76), channel_id=1, source_target_pairs={{0,3},{1,0},{2,1},{3,2},{16,19},{17,16},{18,17},{19,18},{4,7},{5,4... | collective-permute-start | bytes 417800 | tf_op jit(solution)/shard_map/ppermute | solution.py:279
  26.8 9.5 %collective-permute-start.7 = (bf16[256,256]{1,0:T(8,128)(2,1)S(1)}, bf16[256,256]{1,0:T(8,128)(2,1)S(1)}, u32[]{:S(2)}, u32[]{:S(2)}) collective-permute-start(bf16[256,256]{1,0:T(8,128)(2,1)S(1)} %get-tuple-element.60), channel_id=1, source_target_pairs={{0,18},{1,1},{2,16},{3,3},{16,2},{17,17},{18,0},{19,19},{4,22},{5,... | collective-permute-start | bytes 393224 | tf_op jit(solution)/shard_map/ppermute | solution.py:279
  30.1 8.6 %collective-permute-start.8 = (bf16[256,256]{1,0:T(8,128)(2,1)S(1)}, bf16[256,256]{1,0:T(8,128)(2,1)S(1)}, u32[]{:S(2)}, u32[]{:S(2)}) collective-permute-start(bf16[256,256]{1,0:T(8,128)(2,1)S(1)} %get-tuple-element.61), channel_id=1, source_target_pairs={{0,19},{1,0},{2,17},{3,2},{16,3},{17,16},{18,1},{19,18},{4,23},{5,... | collective-permute-start | bytes 393224 | tf_op jit(solution)/shard_map/ppermute | solution.py:279
  30.2 8.5 %collective-permute-start.9 = (bf16[256,256]{1,0:T(8,128)(2,1)S(1)}, bf16[256,256]{1,0:T(8,128)(2,1)S(1)}, u32[]{:S(2)}, u32[]{:S(2)}) collective-permute-start(bf16[256,256]{1,0:T(8,128)(2,1)S(1)} %get-tuple-element.62), channel_id=1, source_target_pairs={{0,16},{1,1},{2,18},{3,3},{16,0},{17,17},{18,2},{19,19},{4,20},{5,... | collective-permute-start | bytes 393224 | tf_op jit(solution)/shard_map/ppermute | solution.py:279
  33.7 5.7 %collective-permute-start.10 = (bf16[256,256]{1,0:T(8,128)(2,1)S(1)}, bf16[256,256]{1,0:T(8,128)(2,1)S(1)}, u32[]{:S(2)}, u32[]{:S(2)}) collective-permute-start(bf16[256,256]{1,0:T(8,128)(2,1)S(1)} %get-tuple-element.63), channel_id=1, source_target_pairs={{0,17},{1,0},{2,19},{3,2},{16,1},{17,16},{18,3},{19,18},{4,21},{5,... | collective-permute-start | bytes 393224 | tf_op jit(solution)/shard_map/ppermute | solution.py:279
  33.8 8.6 %collective-permute-start.11 = (bf16[256,256]{1,0:T(8,128)(2,1)S(1)}, bf16[256,256]{1,0:T(8,128)(2,1)S(1)}, u32[]{:S(2)}, u32[]{:S(2)}) collective-permute-start(bf16[256,256]{1,0:T(8,128)(2,1)S(1)} %get-tuple-element.64), channel_id=1, source_target_pairs={{0,2},{1,1},{2,0},{3,3},{16,18},{17,17},{18,16},{19,19},{4,6},{5,5... | collective-permute-start | bytes 393224 | tf_op jit(solution)/shard_map/ppermute | solution.py:279
  36.2 6.8 %collective-permute-start.12 = (bf16[256,256]{1,0:T(8,128)(2,1)S(1)}, bf16[256,256]{1,0:T(8,128)(2,1)S(1)}, u32[]{:S(2)}, u32[]{:S(2)}) collective-permute-start(bf16[256,256]{1,0:T(8,128)(2,1)S(1)} %get-tuple-element.65), channel_id=1, source_target_pairs={{0,3},{1,0},{2,1},{3,2},{16,19},{17,16},{18,17},{19,18},{4,7},{5,4... | collective-permute-start | bytes 393224 | tf_op jit(solution)/shard_map/ppermute | solution.py:279
  38.7 6.9 %collective-permute-start.13 = (bf16[256,256]{1,0:T(8,128)(2,1)S(1)}, bf16[256,256]{1,0:T(8,128)(2,1)S(1)}, u32[]{:S(2)}, u32[]{:S(2)}) collective-permute-start(bf16[256,256]{1,0:T(8,128)(2,1)S(1)} %get-tuple-element.66), channel_id=1, source_target_pairs={{0,1},{1,0},{2,3},{3,2},{16,17},{17,16},{18,19},{19,18},{4,5},{5,4... | collective-permute-start | bytes 393224 | tf_op jit(solution)/shard_map/ppermute | solution.py:279
  38.7 7.6 %collective-permute-start.20 = (bf16[256,256]{1,0:T(8,128)(2,1)S(1)}, bf16[256,256]{1,0:T(8,128)(2,1)S(1)}, u32[]{:S(2)}, u32[]{:S(2)}) collective-permute-start(bf16[256,256]{1,0:T(8,128)(2,1)S(1)} %get-tuple-element.78), channel_id=1, source_target_pairs={{0,0},{1,19},{2,2},{3,17},{16,16},{17,3},{18,18},{19,1},{4,4},{5,2... | collective-permute-start | bytes 393224 | tf_op jit(solution)/shard_map/ppermute | solution.py:279
  39.4 8.4 %collective-permute-start.21 = (bf16[256,256]{1,0:T(8,128)(2,1)S(1)}, bf16[256,256]{1,0:T(8,128)(2,1)S(1)}, u32[]{:S(2)}, u32[]{:S(2)}) collective-permute-start(bf16[256,256]{1,0:T(8,128)(2,1)S(1)} %get-tuple-element.79), channel_id=1, source_target_pairs={{0,1},{1,18},{2,3},{3,16},{16,17},{17,2},{18,19},{19,0},{4,5},{5,2... | collective-permute-start | bytes 393224 | tf_op jit(solution)/shard_map/ppermute | solution.py:279
  42.3 5.6 %collective-permute-start.22 = (bf16[256,256]{1,0:T(8,128)(2,1)S(1)}, bf16[256,256]{1,0:T(8,128)(2,1)S(1)}, u32[]{:S(2)}, u32[]{:S(2)}) collective-permute-start(bf16[256,256]{1,0:T(8,128)(2,1)S(1)} %get-tuple-element.80), channel_id=1, source_target_pairs={{0,0},{1,17},{2,2},{3,19},{16,16},{17,1},{18,18},{19,3},{4,4},{5,2... | collective-permute-start | bytes 393224 | tf_op jit(solution)/shard_map/ppermute | solution.py:279
  43.0 7.2 %collective-permute-start.23 = (bf16[256,256]{1,0:T(8,128)(2,1)S(1)}, bf16[256,256]{1,0:T(8,128)(2,1)S(1)}, u32[]{:S(2)}, u32[]{:S(2)}) collective-permute-start(bf16[256,256]{1,0:T(8,128)(2,1)S(1)} %get-tuple-element.81), channel_id=1, source_target_pairs={{0,1},{1,16},{2,3},{3,18},{16,17},{17,0},{18,19},{19,2},{4,5},{5,2... | collective-permute-start | bytes 393224 | tf_op jit(solution)/shard_map/ppermute | solution.py:279
  45.6 4.6 %collective-permute-start.24 = (bf16[256,256]{1,0:T(8,128)(2,1)S(1)}, bf16[256,256]{1,0:T(8,128)(2,1)S(1)}, u32[]{:S(2)}, u32[]{:S(2)}) collective-permute-start(bf16[256,256]{1,0:T(8,128)(2,1)S(1)} %get-tuple-element.82), channel_id=1, source_target_pairs={{0,0},{1,3},{2,2},{3,1},{16,16},{17,19},{18,18},{19,17},{4,4},{5,7... | collective-permute-start | bytes 393224 | tf_op jit(solution)/shard_map/ppermute | solution.py:279
  46.3 6.6 %collective-permute-start.25 = (bf16[256,256]{1,0:T(8,128)(2,1)S(1)}, bf16[256,256]{1,0:T(8,128)(2,1)S(1)}, u32[]{:S(2)}, u32[]{:S(2)}) collective-permute-start(bf16[256,256]{1,0:T(8,128)(2,1)S(1)} %get-tuple-element.83), channel_id=1, source_target_pairs={{0,1},{1,2},{2,3},{3,0},{16,17},{17,18},{18,19},{19,16},{4,5},{5,6... | collective-permute-start | bytes 393224 | tf_op jit(solution)/shard_map/ppermute | solution.py:279
  47.8 5.1 %collective-permute-start.26 = (bf16[256,256]{1,0:T(8,128)(2,1)S(1)}, bf16[256,256]{1,0:T(8,128)(2,1)S(1)}, u32[]{:S(2)}, u32[]{:S(2)}) collective-permute-start(bf16[256,256]{1,0:T(8,128)(2,1)S(1)} %get-tuple-element.84), channel_id=1, source_target_pairs={{0,1},{1,0},{2,3},{3,2},{16,17},{17,16},{18,19},{19,18},{4,5},{5,4... | collective-permute-start | bytes 393224 | tf_op jit(solution)/shard_map/ppermute | solution.py:279

commit v14 on v10

--- a/solution.py
+++ b/solution.py
@@ -14,6 +14,7 @@
 SPAN = 2 * WIN + 1
 LANES = 128
 TAIL = 16
+EARLY = (0, 1, 6, 7)
 SCALE = HDIM ** (-0.5)
 FLOOR = -1e30
 VMEM_LIMIT = 32 * 1024 * 1024
@@ -84,20 +85,13 @@
             cots = jnp.concatenate(
                 [jnp.where(lane_head == head, cots, none) for head in range(heads)], axis=0
             )
-            scores = contract(keys, queries, 1, 1)
+            scores = jnp.where(key_valid, contract(keys, queries, 1, 1), FLOOR)
+            expo = jnp.exp(scores - jnp.max(scores, axis=0, keepdims=True))
+            probs = expo * (1.0 / jnp.sum(expo, axis=0, keepdims=True))
             dprob = contract(values, cots, 1, 1)
-            probs_low, dscore_low = [], []
-            for head in range(heads):
-                part = slice(head * BLK, (head + 1) * BLK)
-                mine = jnp.where(key_valid, scores[:, part], FLOOR)
-                expo = jnp.exp(mine - jnp.max(mine, axis=0, keepdims=True))
-                probs = expo * (1.0 / jnp.sum(expo, axis=0, keepdims=True))
-                delta = jnp.sum(probs * dprob[:, part], axis=0, keepdims=True)
-                dscore = probs * (dprob[:, part] - delta)
-                probs_low.append(probs.astype(jnp.bfloat16))
-                dscore_low.append(dscore.astype(jnp.bfloat16))
-            probs_low = jnp.concatenate(probs_low, axis=1)
-            dscore_low = jnp.concatenate(dscore_low, axis=1)
+            delta = jnp.sum(probs * dprob, axis=0, keepdims=True)
+            probs_low = probs.astype(jnp.bfloat16)
+            dscore_low = (probs * (dprob - delta)).astype(jnp.bfloat16)
             dvalue = contract(probs_low, cots, 1, 0)
             dkey = contract(dscore_low, queries, 1, 0)
             keys_turned = jnp.concatenate([turned[index, 0, lanes] for index in chosen], axis=1)
@@ -180,20 +174,14 @@
     return lax.axis_index("section") * seq_count + lax.axis_index("seq")
 
 
-def pack_kernel(seq_count, order, *refs):
+def pack_kernel(seq_count, steps, *refs):
     smalls, (first, second) = refs[:2], refs[2:4]
     outs, (lists, mask, small_sem, sem) = refs[4:-4], refs[-4:]
-    small_copies = [
-        pltpu.make_async_copy(source, held, small_sem.at[slot])
-        for slot, (source, held) in enumerate(zip(smalls, (lists, mask)))
-    ]
-    for copy in small_copies:
-        copy.start()
     me = device_index(seq_count)
     here = me % seq_count
     share = outs[0].shape[1]
     copies = []
-    for slot, (step, out) in enumerate(zip(order, outs)):
+    for slot, (step, out) in enumerate(zip(steps, outs)):
         lanes = pl.ds(pl.multiple_of((me ^ step) * share, LANES), share)
         pair = [
             pltpu.make_async_copy(
@@ -204,6 +192,12 @@
         for copy in pair:
             copy.start()
         copies.append(pair)
+    small_copies = [
+        pltpu.make_async_copy(source, held, small_sem.at[slot])
+        for slot, (source, held) in enumerate(zip(smalls, (lists, mask)))
+    ]
+    for copy in small_copies:
+        copy.start()
     for copy in small_copies:
         copy.wait()
     keep = (mask[...] == 1) | (me < seq_count)
@@ -253,12 +247,12 @@
         out[BLK:] = result[me ^ step, 1]
 
 
-def unpack_kernel(seq_count, order, *refs):
-    shares, (first, second, sem) = refs[:-3], refs[-3:]
+def unpack_kernel(seq_count, steps, *refs):
+    shares, (first, second, sem) = refs[: len(steps)], refs[-3:]
     width = shares[0].shape[1]
     me = device_index(seq_count)
     copies = []
-    for slot, (step, share) in enumerate(zip(order, shares)):
+    for slot, (step, share) in enumerate(zip(steps, shares)):
         lanes = pl.ds(pl.multiple_of((me ^ step) * width, LANES), width)
         for half, result in enumerate((first, second)):
             copy = pltpu.make_async_copy(
@@ -287,23 +281,28 @@
     params = pltpu.CompilerParams(vmem_limit_bytes=VMEM_LIMIT)
     order = back = list(range(parts - 1, -1, -1))
     if parts == 8:
-        order, back = [6, 4, 7, 5, 2, 3, 1, 0], [1, 4, 6, 7, 2, 3, 5, 0]
+        order, back = [6, 4, 7, 5, 2, 3, 1, 0], [6, 7, 4, 5, 2, 3, 1, 0]
     sems = pltpu.SemaphoreType.DMA((2, parts))
-    shares = pl.pallas_call(
-        functools.partial(pack_kernel, seq_count, order),
-        out_shape=[jax.ShapeDtypeStruct((2 * BLK + TAIL, share), kind)] * parts,
-        in_specs=specs(4, pltpu.HBM),
-        out_specs=specs(parts, pltpu.VMEM),
-        scratch_shapes=[
-            pltpu.SMEM(alignment.shape, jnp.int32),
-            pltpu.VMEM(diffusion_mask.shape, jnp.int32),
-            pltpu.SemaphoreType.DMA((2,)),
-            sems,
-        ],
-        compiler_params=params,
-        name="pack",
-    )(*in_hbm(alignment, diffusion_mask, first_rows, second_rows))
-    shares = swapped(shares, order)
+
+    def pack(steps, lists):
+        return pl.pallas_call(
+            functools.partial(pack_kernel, seq_count, steps),
+            out_shape=[jax.ShapeDtypeStruct((2 * BLK + TAIL, share), kind)] * len(steps),
+            in_specs=specs(4, pltpu.HBM),
+            out_specs=specs(len(steps), pltpu.VMEM),
+            scratch_shapes=[
+                pltpu.SMEM(alignment.shape, jnp.int32),
+                pltpu.VMEM(diffusion_mask.shape, jnp.int32),
+                pltpu.SemaphoreType.DMA((2,)),
+                sems,
+            ],
+            compiler_params=params,
+            name="pack",
+        )(*in_hbm(lists, diffusion_mask, first_rows, second_rows))
+
+    shares = list(pack(order[:seq_count], alignment))
+    lists, shares[0] = lax.optimization_barrier((alignment, shares[0]))
+    shares = swapped([*shares, *pack(order[seq_count:], lists)], order)
     rows = pltpu.VMEM((parts, 2, BLK, share), kind)
     grads = pltpu.VMEM((seq_count, BLK, share), jnp.float32)
     turned = pltpu.VMEM((seq_count, 2, share, BLK), kind)
@@ -317,17 +316,24 @@
         cost_estimate=attend_cost(seq_count, share),
         name="attend",
     )(source_length, target_length, *shares)
-    shares = swapped(shares, back)
+    shares = dict(zip(back, swapped(shares, back)))
     out_shape = jax.ShapeDtypeStruct((1, 1, BLK, width), kind)
-    return pl.pallas_call(
-        functools.partial(unpack_kernel, seq_count, back),
-        out_shape=[out_shape, out_shape],
-        in_specs=specs(parts, pltpu.VMEM),
-        out_specs=specs(2, pltpu.HBM),
-        scratch_shapes=[sems],
-        compiler_params=params,
-        name="unpack",
-    )(*shares)
+
+    def unpack(steps, *begun):
+        count = len(steps)
+        return pl.pallas_call(
+            functools.partial(unpack_kernel, seq_count, steps),
+            out_shape=[out_shape, out_shape],
+            in_specs=specs(count, pltpu.VMEM) + specs(len(begun), pltpu.HBM),
+            out_specs=specs(2, pltpu.HBM),
+            input_output_aliases={count + slot: slot for slot in range(len(begun))},
+            scratch_shapes=[sems],
+            compiler_params=params,
+            name="unpack",
+        )(*(shares[step] for step in steps), *begun)
+
+    early = [step for step in back if step in EARLY]
+    return unpack([step for step in back if step not in EARLY], *unpack(early))
 
 
 def on_device(first_rows, second_rows, alignment, diffusion_mask, source_length, target_length):

time: 41.2 us -> 38.3 us (0.930)
  waiting for transfers between devices: 18.5 us -> 12.8 us
  Pallas kernels: 6.13 us -> 7.93 us
  starting transfers between devices: 14.3 us -> 15.3 us
    ppermute x14, waiting for transfers between devices: 18.5 us -> 12.8 us  [swapped(): lax.ppermute(share, AXES, [(dev, dev ^ step) for dev in range(parts)])]
    pallas_call x2 -> x4, Pallas kernels: 2.52 us -> 4.32 us  [the longest x2 2.48 us: pack(): pl.pallas_call(functools.partial(pack_kernel, seq_count, steps), out_shap...]
    ppermute x14, starting transfers between devices: 14.3 us -> 15.3 us  [swapped(): lax.ppermute(share, AXES, [(dev, dev ^ step) for dev in range(parts)])]
  transfers between devices with their start and end apart: 14 -> 14, of which waited for: 8 -> 6; matrix products, arithmetic and copies ran while one was open for 0% -> 0% of each run, Pallas kernels for 0% -> 6%
where the time goes in v14:
time: 38.3 us; the launch traced here: 38 us
  starting transfers between devices  15.3 us (40%)
  waiting for transfers between devices  12.8 us (33%)
  Pallas kernels  7.93 us (21%)
  between operations  1.98 us (5%)
    ppermute x14, starting transfers between devices, swapped(): lax.ppermute(share, AXES, [(dev, dev ^ step) for dev in range(parts)])  15.3 us
    ppermute x14, waiting for transfers between devices, swapped(): lax.ppermute(share, AXES, [(dev, dev ^ step) for dev in range(parts)])  12.8 us
    pallas_call x1, Pallas kernels, by_pairs(): pl.pallas_call(functools.partial(attend_kernel, seq_count, order, back),...  3.61 us
    pallas_call x2, Pallas kernels, pack(): pl.pallas_call(functools.partial(pack_kernel, seq_count, steps), out_shap...  2.48 us
    pallas_call x2, Pallas kernels, unpack(): pl.pallas_call(functools.partial(unpack_kernel, seq_count, steps), out_sh...  1.84 us
  transfers between devices with their start and end apart: 14, of which 6 were waited for; matrix products, arithmetic and copies ran while one was open for 0% of the time, Pallas kernels for 6%

profile of v14, /device:TPU:0, one launch (start us, length us, event | category | flops | bytes accessed | tf_op | source)
XLA Modules:
  0.0 38.0 jit_solution(11718541586281458562)
XLA Ops:
  0.6 1.3 %pack.2 = (bf16[272,256]{1,0:T(8,128)(2,1)S(1)}, bf16[272,256]{1,0:T(8,128)(2,1)S(1)}, bf16[272,256]{1,0:T(8,128)(2,1)S(1)}, bf16[272,256]{1,0:T(8,128)(2,1)S(1)}) custom-call(s32[1,1,2]{2,1,0:T(1,128)} %refs_0_.2, s32[1,128]{1,0:T(1,128)} %refs_1_.3, bf16[1,1,128,2048]{3,2,1,0:T(8,128)(2,1)} %refs_2_.3, bf16[1,1,128,2048]{3,2,1,0:T(8,128)(2,1)} %refs_3_.3), custom_call_target="tpu_custom_call" | custom-call | tf_op jit(solution)/shard_map/pack/pallas_call | solution.py:288
  1.9 4.0 %collective-permute-start = (bf16[272,256]{1,0:T(8,128)(2,1)S(1)}, bf16[272,256]{1,0:T(8,128)(2,1)S(1)}, u32[]{:S(2)}, u32[]{:S(2)}) collective-permute-start(bf16[272,256]{1,0:T(8,128)(2,1)S(1)} %get-tuple-element.23), channel_id=1, source_target_pairs={{0,18},{1,19},{2,16},{3,17},{16,2},{17,3},{18,0},{19,1},{4,22},{5,... | collective-permute-start | bytes 417800 | tf_op jit(solution)/shard_map/ppermute | solution.py:270
  5.8 0.5 %collective-permute-start.1 = (bf16[272,256]{1,0:T(8,128)(2,1)S(1)}, bf16[272,256]{1,0:T(8,128)(2,1)S(1)}, u32[]{:S(2)}, u32[]{:S(2)}) collective-permute-start(bf16[272,256]{1,0:T(8,128)(2,1)S(1)} %get-tuple-element.24), channel_id=1, source_target_pairs={{0,16},{1,17},{2,18},{3,19},{16,0},{17,1},{18,2},{19,3},{4,20},{5,... | collective-permute-start | bytes 417800 | tf_op jit(solution)/shard_map/ppermute | solution.py:270
  6.4 0.4 collective-permute-start.2
  6.7 0.9 %collective-permute-start.3 = (bf16[272,256]{1,0:T(8,128)(2,1)S(1)}, bf16[272,256]{1,0:T(8,128)(2,1)S(1)}, u32[]{:S(2)}, u32[]{:S(2)}) collective-permute-start(bf16[272,256]{1,0:T(8,128)(2,1)S(1)} %get-tuple-element.26), channel_id=1, source_target_pairs={{0,17},{1,16},{2,19},{3,18},{16,1},{17,0},{18,3},{19,2},{4,21},{5,... | collective-permute-start | bytes 417800 | tf_op jit(solution)/shard_map/ppermute | solution.py:270
  7.7 1.2 %pack.3 = (bf16[272,256]{1,0:T(8,128)(2,1)S(1)}, bf16[272,256]{1,0:T(8,128)(2,1)S(1)}, bf16[272,256]{1,0:T(8,128)(2,1)S(1)}, bf16[272,256]{1,0:T(8,128)(2,1)S(1)}) custom-call(s32[1,1,2]{2,1,0:T(1,128)} %refs_0_.2, s32[1,128]{1,0:T(1,128)} %refs_1_.3, bf16[1,1,128,2048]{3,2,1,0:T(8,128)(2,1)} %refs_2_.3, bf16[1,1,128,2048]{3,2,1,0:T(8,128)(2,1)} %refs_3_.3), custom_call_target="tpu_custom_call" | custom-call | tf_op jit(solution)/shard_map/pack/pallas_call | solution.py:288
  8.9 2.0 %collective-permute-start.4 = (bf16[272,256]{1,0:T(8,128)(2,1)S(1)}, bf16[272,256]{1,0:T(8,128)(2,1)S(1)}, u32[]{:S(2)}, u32[]{:S(2)}) collective-permute-start(bf16[272,256]{1,0:T(8,128)(2,1)S(1)} %get-tuple-element.28), channel_id=1, source_target_pairs={{0,2},{1,3},{2,0},{3,1},{16,18},{17,19},{18,16},{19,17},{4,6},{5,7... | collective-permute-start | bytes 417800 | tf_op jit(solution)/shard_map/ppermute | solution.py:270
  10.9 0.0 collective-permute-done.refs_0_
  10.9 0.0 collective-permute-start.5
  10.9 4.7 %collective-permute-done.1.refs_1_ = bf16[272,256]{1,0:T(8,128)(2,1)S(1)} collective-permute-done((bf16[272,256]{1,0:T(8,128)(2,1)S(1)}, bf16[272,256]{1,0:T(8,128)(2,1)S(1)}, u32[]{:S(2)}, u32[]{:S(2)}) %collective-permute-start.1) | collective-permute-done | bytes 139296 | tf_op jit(solution)/shard_map/ppermute | solution.py:270
  15.6 0.0 collective-permute-start.6
  16.9 0.0 collective-permute-done.2.refs_2_
  16.9 1.5 %collective-permute-done.3.refs_3_ = bf16[272,256]{1,0:T(8,128)(2,1)S(1)} collective-permute-done((bf16[272,256]{1,0:T(8,128)(2,1)S(1)}, bf16[272,256]{1,0:T(8,128)(2,1)S(1)}, u32[]{:S(2)}, u32[]{:S(2)}) %collective-permute-start.3) | collective-permute-done | bytes 139296 | tf_op jit(solution)/shard_map/ppermute | solution.py:270
  18.4 0.0 collective-permute-done.4.refs_4_
  18.4 0.4 %collective-permute-done.5.refs_5_ = bf16[272,256]{1,0:T(8,128)(2,1)S(1)} collective-permute-done((bf16[272,256]{1,0:T(8,128)(2,1)S(1)}, bf16[272,256]{1,0:T(8,128)(2,1)S(1)}, u32[]{:S(2)}, u32[]{:S(2)}) %collective-permute-start.5) | collective-permute-done | bytes 139296 | tf_op jit(solution)/shard_map/ppermute | solution.py:270
  18.8 0.0 collective-permute-done.6.refs_6_
  18.8 3.6 %attend.1 = (bf16[256,256]{1,0:T(8,128)(2,1)S(1)}, bf16[256,256]{1,0:T(8,128)(2,1)S(1)}, bf16[256,256]{1,0:T(8,128)(2,1)S(1)}, bf16[256,256]{1,0:T(8,128)(2,1)S(...) custom-call(s32[1]{0:T(128)S(6)} %copy.12.source_len, ...), custom_call_target="tpu_custom_call" | custom-call | flops 335544320 | bytes 2097152 | tf_op jit(solution)/shard_map/attend/pallas_call | solution.py:309
  22.4 0.9 %collective-permute-start.11 = (bf16[256,256]{1,0:T(8,128)(2,1)S(1)}, bf16[256,256]{1,0:T(8,128)(2,1)S(1)}, u32[]{:S(2)}, u32[]{:S(2)}) collective-permute-start(bf16[256,256]{1,0:T(8,128)(2,1)S(1)} %get-tuple-element.36), channel_id=1, source_target_pairs={{0,18},{1,19},{2,16},{3,17},{16,2},{17,3},{18,0},{19,1},{4,22},{5,... | collective-permute-start | bytes 393224 | tf_op jit(solution)/shard_map/ppermute | solution.py:270
  23.3 1.3 %collective-permute-start.12 = (bf16[256,256]{1,0:T(8,128)(2,1)S(1)}, bf16[256,256]{1,0:T(8,128)(2,1)S(1)}, u32[]{:S(2)}, u32[]{:S(2)}) collective-permute-start(bf16[256,256]{1,0:T(8,128)(2,1)S(1)} %get-tuple-element.37), channel_id=1, source_target_pairs={{0,19},{1,18},{2,17},{3,16},{16,3},{17,2},{18,1},{19,0},{4,23},{5,... | collective-permute-start | bytes 393224 | tf_op jit(solution)/shard_map/ppermute | solution.py:270
  24.6 1.5 %collective-permute-start.7 = (bf16[256,256]{1,0:T(8,128)(2,1)S(1)}, bf16[256,256]{1,0:T(8,128)(2,1)S(1)}, u32[]{:S(2)}, u32[]{:S(2)}) collective-permute-start(bf16[256,256]{1,0:T(8,128)(2,1)S(1)} %get-tuple-element.32), channel_id=1, source_target_pairs={{0,16},{1,17},{2,18},{3,19},{16,0},{17,1},{18,2},{19,3},{4,20},{5,... | collective-permute-start | bytes 393224 | tf_op jit(solution)/shard_map/ppermute | solution.py:270
  26.2 0.7 %collective-permute-start.8 = (bf16[256,256]{1,0:T(8,128)(2,1)S(1)}, bf16[256,256]{1,0:T(8,128)(2,1)S(1)}, u32[]{:S(2)}, u32[]{:S(2)}) collective-permute-start(bf16[256,256]{1,0:T(8,128)(2,1)S(1)} %get-tuple-element.33), channel_id=1, source_target_pairs={{0,17},{1,16},{2,19},{3,18},{16,1},{17,0},{18,3},{19,2},{4,21},{5,... | collective-permute-start | bytes 393224 | tf_op jit(solution)/shard_map/ppermute | solution.py:270
  26.8 0.0 collective-permute-start.13
  26.8 3.0 %collective-permute-done.11.refs_0_ = bf16[256,256]{1,0:T(8,128)(2,1)S(1)} collective-permute-done((bf16[256,256]{1,0:T(8,128)(2,1)S(1)}, bf16[256,256]{1,0:T(8,128)(2,1)S(1)}, u32[]{:S(2)}, u32[]{:S(2)}) %collective-permute-start.11) | collective-permute-done | bytes 131104 | tf_op jit(solution)/shard_map/ppermute | solution.py:270
  29.8 1.3 %collective-permute-start.9 = (bf16[256,256]{1,0:T(8,128)(2,1)S(1)}, bf16[256,256]{1,0:T(8,128)(2,1)S(1)}, u32[]{:S(2)}, u32[]{:S(2)}) collective-permute-start(bf16[256,256]{1,0:T(8,128)(2,1)S(1)} %get-tuple-element.34), channel_id=1, source_target_pairs={{0,2},{1,3},{2,0},{3,1},{16,18},{17,19},{18,16},{19,17},{4,6},{5,7... | collective-permute-start | bytes 393224 | tf_op jit(solution)/shard_map/ppermute | solution.py:270
  31.1 0.0 collective-permute-done.12.refs_1_
  31.1 1.8 %collective-permute-start.10 = (bf16[256,256]{1,0:T(8,128)(2,1)S(1)}, bf16[256,256]{1,0:T(8,128)(2,1)S(1)}, u32[]{:S(2)}, u32[]{:S(2)}) collective-permute-start(bf16[256,256]{1,0:T(8,128)(2,1)S(1)} %get-tuple-element.35), channel_id=1, source_target_pairs={{0,3},{1,2},{2,1},{3,0},{16,19},{17,18},{18,17},{19,16},{4,7},{5,6... | collective-permute-start | bytes 393224 | tf_op jit(solution)/shard_map/ppermute | solution.py:270
  32.9 0.0 collective-permute-done.13.refs_2_
  32.9 0.9 %unpack.2 = (bf16[1,1,128,2048]{3,2,1,0:T(8,128)(2,1)}, bf16[1,1,128,2048]{3,2,1,0:T(8,128)(2,1)}) custom-call(bf16[256,256]{1,0:T(8,128)(2,1)S(1)} %collective-permute-done.11.refs_0_, bf16[256,256]{1,0:T(8,128)(2,1)S(1)} %collective-permute-done.12.refs_1_, bf16[256,256]{1,0:T(8,128)(2,1)S(1)} %collective-permute-done.13.refs_2_, ...), custom_call_target="tpu_custom_call" | custom-call | tf_op jit(solution)/shard_map/unpack/pallas_call | solution.py:324
  33.9 0.4 %collective-permute-done.7.refs_0_ = bf16[256,256]{1,0:T(8,128)(2,1)S(1)} collective-permute-done((bf16[256,256]{1,0:T(8,128)(2,1)S(1)}, bf16[256,256]{1,0:T(8,128)(2,1)S(1)}, u32[]{:S(2)}, u32[]{:S(2)}) %collective-permute-start.7) | collective-permute-done | bytes 131104 | tf_op jit(solution)/shard_map/ppermute | solution.py:270
  34.3 2.8 %collective-permute-done.8.refs_1_ = bf16[256,256]{1,0:T(8,128)(2,1)S(1)} collective-permute-done((bf16[256,256]{1,0:T(8,128)(2,1)S(1)}, bf16[256,256]{1,0:T(8,128)(2,1)S(1)}, u32[]{:S(2)}, u32[]{:S(2)}) %collective-permute-start.8) | collective-permute-done | bytes 131104 | tf_op jit(solution)/shard_map/ppermute | solution.py:270
  37.1 0.0 collective-permute-done.9.refs_2_
  37.1 0.0 collective-permute-done.10.refs_3_
  37.1 0.9 %unpack.3 = (bf16[1,1,128,2048]{3,2,1,0:T(8,128)(2,1)}, bf16[1,1,128,2048]{3,2,1,0:T(8,128)(2,1)}) custom-call(bf16[256,256]{1,0:T(8,128)(2,1)S(1)} %collective-permute-done.7.refs_0_, bf16[256,256]{1,0:T(8,128)(2,1)S(1)} %collective-permute-done.8.refs_1_, ...), custom_call_target="tpu_custom_call", output_to_operand_aliasing={{0}: (4, {}), {1}: (5, {})} | custom-call | tf_op jit(solution)/shard_map/unpack/pallas_call | solution.py:324
Async XLA Ops:
  1.9 9.0 %collective-permute-start = (bf16[272,256]{1,0:T(8,128)(2,1)S(1)}, bf16[272,256]{1,0:T(8,128)(2,1)S(1)}, u32[]{:S(2)}, u32[]{:S(2)}) collective-permute-start(bf16[272,256]{1,0:T(8,128)(2,1)S(1)} %get-tuple-element.23), channel_id=1, source_target_pairs={{0,18},{1,19},{2,16},{3,17},{16,2},{17,3},{18,0},{19,1},{4,22},{5,... | collective-permute-start | bytes 417800 | tf_op jit(solution)/shard_map/ppermute | solution.py:270
  5.8 9.7 %collective-permute-start.1 = (bf16[272,256]{1,0:T(8,128)(2,1)S(1)}, bf16[272,256]{1,0:T(8,128)(2,1)S(1)}, u32[]{:S(2)}, u32[]{:S(2)}) collective-permute-start(bf16[272,256]{1,0:T(8,128)(2,1)S(1)} %get-tuple-element.24), channel_id=1, source_target_pairs={{0,16},{1,17},{2,18},{3,19},{16,0},{17,1},{18,2},{19,3},{4,20},{5,... | collective-permute-start | bytes 417800 | tf_op jit(solution)/shard_map/ppermute | solution.py:270
  6.4 10.5 %collective-permute-start.2 = (bf16[272,256]{1,0:T(8,128)(2,1)S(1)}, bf16[272,256]{1,0:T(8,128)(2,1)S(1)}, u32[]{:S(2)}, u32[]{:S(2)}) collective-permute-start(bf16[272,256]{1,0:T(8,128)(2,1)S(1)} %get-tuple-element.25), channel_id=1, source_target_pairs={{0,19},{1,18},{2,17},{3,16},{16,3},{17,2},{18,1},{19,0},{4,23},{5,... | collective-permute-start | bytes 417800 | tf_op jit(solution)/shard_map/ppermute | solution.py:270
  6.7 11.6 %collective-permute-start.3 = (bf16[272,256]{1,0:T(8,128)(2,1)S(1)}, bf16[272,256]{1,0:T(8,128)(2,1)S(1)}, u32[]{:S(2)}, u32[]{:S(2)}) collective-permute-start(bf16[272,256]{1,0:T(8,128)(2,1)S(1)} %get-tuple-element.26), channel_id=1, source_target_pairs={{0,17},{1,16},{2,19},{3,18},{16,1},{17,0},{18,3},{19,2},{4,21},{5,... | collective-permute-start | bytes 417800 | tf_op jit(solution)/shard_map/ppermute | solution.py:270
  8.9 9.5 %collective-permute-start.4 = (bf16[272,256]{1,0:T(8,128)(2,1)S(1)}, bf16[272,256]{1,0:T(8,128)(2,1)S(1)}, u32[]{:S(2)}, u32[]{:S(2)}) collective-permute-start(bf16[272,256]{1,0:T(8,128)(2,1)S(1)} %get-tuple-element.28), channel_id=1, source_target_pairs={{0,2},{1,3},{2,0},{3,1},{16,18},{17,19},{18,16},{19,17},{4,6},{5,7... | collective-permute-start | bytes 417800 | tf_op jit(solution)/shard_map/ppermute | solution.py:270
  10.9 7.9 %collective-permute-start.5 = (bf16[272,256]{1,0:T(8,128)(2,1)S(1)}, bf16[272,256]{1,0:T(8,128)(2,1)S(1)}, u32[]{:S(2)}, u32[]{:S(2)}) collective-permute-start(bf16[272,256]{1,0:T(8,128)(2,1)S(1)} %get-tuple-element.29), channel_id=1, source_target_pairs={{0,3},{1,2},{2,1},{3,0},{16,19},{17,18},{18,17},{19,16},{4,7},{5,6... | collective-permute-start | bytes 417800 | tf_op jit(solution)/shard_map/ppermute | solution.py:270
  15.6 3.2 %collective-permute-start.6 = (bf16[272,256]{1,0:T(8,128)(2,1)S(1)}, bf16[272,256]{1,0:T(8,128)(2,1)S(1)}, u32[]{:S(2)}, u32[]{:S(2)}) collective-permute-start(bf16[272,256]{1,0:T(8,128)(2,1)S(1)} %get-tuple-element.30), channel_id=1, source_target_pairs={{0,1},{1,0},{2,3},{3,2},{16,17},{17,16},{18,19},{19,18},{4,5},{5,4... | collective-permute-start | bytes 417800 | tf_op jit(solution)/shard_map/ppermute | solution.py:270
  22.4 7.4 %collective-permute-start.11 = (bf16[256,256]{1,0:T(8,128)(2,1)S(1)}, bf16[256,256]{1,0:T(8,128)(2,1)S(1)}, u32[]{:S(2)}, u32[]{:S(2)}) collective-permute-start(bf16[256,256]{1,0:T(8,128)(2,1)S(1)} %get-tuple-element.36), channel_id=1, source_target_pairs={{0,18},{1,19},{2,16},{3,17},{16,2},{17,3},{18,0},{19,1},{4,22},{5,... | collective-permute-start | bytes 393224 | tf_op jit(solution)/shard_map/ppermute | solution.py:270
  23.3 7.8 %collective-permute-start.12 = (bf16[256,256]{1,0:T(8,128)(2,1)S(1)}, bf16[256,256]{1,0:T(8,128)(2,1)S(1)}, u32[]{:S(2)}, u32[]{:S(2)}) collective-permute-start(bf16[256,256]{1,0:T(8,128)(2,1)S(1)} %get-tuple-element.37), channel_id=1, source_target_pairs={{0,19},{1,18},{2,17},{3,16},{16,3},{17,2},{18,1},{19,0},{4,23},{5,... | collective-permute-start | bytes 393224 | tf_op jit(solution)/shard_map/ppermute | solution.py:270
  24.6 9.7 %collective-permute-start.7 = (bf16[256,256]{1,0:T(8,128)(2,1)S(1)}, bf16[256,256]{1,0:T(8,128)(2,1)S(1)}, u32[]{:S(2)}, u32[]{:S(2)}) collective-permute-start(bf16[256,256]{1,0:T(8,128)(2,1)S(1)} %get-tuple-element.32), channel_id=1, source_target_pairs={{0,16},{1,17},{2,18},{3,19},{16,0},{17,1},{18,2},{19,3},{4,20},{5,... | collective-permute-start | bytes 393224 | tf_op jit(solution)/shard_map/ppermute | solution.py:270
  26.2 10.9 %collective-permute-start.8 = (bf16[256,256]{1,0:T(8,128)(2,1)S(1)}, bf16[256,256]{1,0:T(8,128)(2,1)S(1)}, u32[]{:S(2)}, u32[]{:S(2)}) collective-permute-start(bf16[256,256]{1,0:T(8,128)(2,1)S(1)} %get-tuple-element.33), channel_id=1, source_target_pairs={{0,17},{1,16},{2,19},{3,18},{16,1},{17,0},{18,3},{19,2},{4,21},{5,... | collective-permute-start | bytes 393224 | tf_op jit(solution)/shard_map/ppermute | solution.py:270
  26.8 6.1 %collective-permute-start.13 = (bf16[256,256]{1,0:T(8,128)(2,1)S(1)}, bf16[256,256]{1,0:T(8,128)(2,1)S(1)}, u32[]{:S(2)}, u32[]{:S(2)}) collective-permute-start(bf16[256,256]{1,0:T(8,128)(2,1)S(1)} %get-tuple-element.38), channel_id=1, source_target_pairs={{0,1},{1,0},{2,3},{3,2},{16,17},{17,16},{18,19},{19,18},{4,5},{5,4... | collective-permute-start | bytes 393224 | tf_op jit(solution)/shard_map/ppermute | solution.py:270
  29.8 7.3 %collective-permute-start.9 = (bf16[256,256]{1,0:T(8,128)(2,1)S(1)}, bf16[256,256]{1,0:T(8,128)(2,1)S(1)}, u32[]{:S(2)}, u32[]{:S(2)}) collective-permute-start(bf16[256,256]{1,0:T(8,128)(2,1)S(1)} %get-tuple-element.34), channel_id=1, source_target_pairs={{0,2},{1,3},{2,0},{3,1},{16,18},{17,19},{18,16},{19,17},{4,6},{5,7... | collective-permute-start | bytes 393224 | tf_op jit(solution)/shard_map/ppermute | solution.py:270
  31.1 6.0 %collective-permute-start.10 = (bf16[256,256]{1,0:T(8,128)(2,1)S(1)}, bf16[256,256]{1,0:T(8,128)(2,1)S(1)}, u32[]{:S(2)}, u32[]{:S(2)}) collective-permute-start(bf16[256,256]{1,0:T(8,128)(2,1)S(1)} %get-tuple-element.35), channel_id=1, source_target_pairs={{0,3},{1,2},{2,1},{3,0},{16,19},{17,18},{18,17},{19,16},{4,7},{5,6... | collective-permute-start | bytes 393224 | tf_op jit(solution)/shard_map/ppermute | solution.py:270

commit v15 on v14

--- a/solution.py
+++ b/solution.py
@@ -14,7 +14,7 @@
 SPAN = 2 * WIN + 1
 LANES = 128
 TAIL = 16
-EARLY = (0, 1, 6, 7)
+EARLY = (0, 2, 4)
 SCALE = HDIM ** (-0.5)
 FLOOR = -1e30
 VMEM_LIMIT = 32 * 1024 * 1024
@@ -281,7 +281,7 @@
     params = pltpu.CompilerParams(vmem_limit_bytes=VMEM_LIMIT)
     order = back = list(range(parts - 1, -1, -1))
     if parts == 8:
-        order, back = [6, 4, 7, 5, 2, 3, 1, 0], [6, 7, 4, 5, 2, 3, 1, 0]
+        order, back = [4, 2, 5, 6, 7, 3, 1, 0], [4, 2, 6, 7, 5, 3, 1, 0]
     sems = pltpu.SemaphoreType.DMA((2, parts))
 
     def pack(steps, lists):

time: 38.3 us -> 38.2 us (level)
  starting transfers between devices: 15.3 us -> 13.5 us
  waiting for transfers between devices: 12.8 us -> 14.6 us
    ppermute x14, starting transfers between devices: 15.3 us -> 13.5 us  [swapped(): lax.ppermute(share, AXES, [(dev, dev ^ step) for dev in range(parts)])]
    ppermute x14, waiting for transfers between devices: 12.8 us -> 14.6 us  [swapped(): lax.ppermute(share, AXES, [(dev, dev ^ step) for dev in range(parts)])]
  transfers between devices with their start and end apart: 14 -> 14, of which waited for: 6 -> 5; matrix products, arithmetic and copies ran while one was open for 0% -> 0% of each run, Pallas kernels for 6% -> 6%
where the time goes in v15:
time: 38.2 us; the launch traced here: 38 us
  waiting for transfers between devices  14.6 us (38%)
  starting transfers between devices  13.5 us (35%)
  Pallas kernels  7.93 us (21%)
  between operations  1.97 us (5%)
    ppermute x14, waiting for transfers between devices, swapped(): lax.ppermute(share, AXES, [(dev, dev ^ step) for dev in range(parts)])  14.6 us
    ppermute x14, starting transfers between devices, swapped(): lax.ppermute(share, AXES, [(dev, dev ^ step) for dev in range(parts)])  13.5 us
    pallas_call x1, Pallas kernels, by_pairs(): pl.pallas_call(functools.partial(attend_kernel, seq_count, order, back),...  3.61 us
    pallas_call x2, Pallas kernels, pack(): pl.pallas_call(functools.partial(pack_kernel, seq_count, steps), out_shap...  2.48 us
    pallas_call x2, Pallas kernels, unpack(): pl.pallas_call(functools.partial(unpack_kernel, seq_count, steps), out_sh...  1.84 us
  transfers between devices with their start and end apart: 14, of which 5 were waited for; matrix products, arithmetic and copies ran while one was open for 0% of the time, Pallas kernels for 6%

profile of v15, /device:TPU:0, one launch (start us, length us, event | category | flops | bytes accessed | tf_op | source)
XLA Modules:
  0.0 38.0 jit_solution(4278702476174562046)
XLA Ops:
  0.6 1.3 %pack.2 = (bf16[272,256]{1,0:T(8,128)(2,1)S(1)}, bf16[272,256]{1,0:T(8,128)(2,1)S(1)}, bf16[272,256]{1,0:T(8,128)(2,1)S(1)}, bf16[272,256]{1,0:T(8,128)(2,1)S(1)}) custom-call(s32[1,1,2]{2,1,0:T(1,128)} %refs_0_.2, s32[1,128]{1,0:T(1,128)} %refs_1_.3, bf16[1,1,128,2048]{3,2,1,0:T(8,128)(2,1)} %refs_2_.3, bf16[1,1,128,2048]{3,2,1,0:T(8,128)(2,1)} %refs_3_.3), custom_call_target="tpu_custom_call" | custom-call | tf_op jit(solution)/shard_map/pack/pallas_call | solution.py:288
  1.9 3.0 %collective-permute-start = (bf16[272,256]{1,0:T(8,128)(2,1)S(1)}, bf16[272,256]{1,0:T(8,128)(2,1)S(1)}, u32[]{:S(2)}, u32[]{:S(2)}) collective-permute-start(bf16[272,256]{1,0:T(8,128)(2,1)S(1)} %get-tuple-element.23), channel_id=1, source_target_pairs={{0,16},{1,17},{2,18},{3,19},{16,0},{17,1},{18,2},{19,3},{4,20},{5,... | collective-permute-start | bytes 417800 | tf_op jit(solution)/shard_map/ppermute | solution.py:270
  4.9 1.5 %collective-permute-start.1 = (bf16[272,256]{1,0:T(8,128)(2,1)S(1)}, bf16[272,256]{1,0:T(8,128)(2,1)S(1)}, u32[]{:S(2)}, u32[]{:S(2)}) collective-permute-start(bf16[272,256]{1,0:T(8,128)(2,1)S(1)} %get-tuple-element.24), channel_id=1, source_target_pairs={{0,2},{1,3},{2,0},{3,1},{16,18},{17,19},{18,16},{19,17},{4,6},{5,7... | collective-permute-start | bytes 417800 | tf_op jit(solution)/shard_map/ppermute | solution.py:270
  6.4 0.0 collective-permute-start.2
  6.4 0.9 %collective-permute-start.3 = (bf16[272,256]{1,0:T(8,128)(2,1)S(1)}, bf16[272,256]{1,0:T(8,128)(2,1)S(1)}, u32[]{:S(2)}, u32[]{:S(2)}) collective-permute-start(bf16[272,256]{1,0:T(8,128)(2,1)S(1)} %get-tuple-element.26), channel_id=1, source_target_pairs={{0,18},{1,19},{2,16},{3,17},{16,2},{17,3},{18,0},{19,1},{4,22},{5,... | collective-permute-start | bytes 417800 | tf_op jit(solution)/shard_map/ppermute | solution.py:270
  7.3 1.2 %pack.3 = (bf16[272,256]{1,0:T(8,128)(2,1)S(1)}, bf16[272,256]{1,0:T(8,128)(2,1)S(1)}, bf16[272,256]{1,0:T(8,128)(2,1)S(1)}, bf16[272,256]{1,0:T(8,128)(2,1)S(1)}) custom-call(s32[1,1,2]{2,1,0:T(1,128)} %refs_0_.2, s32[1,128]{1,0:T(1,128)} %refs_1_.3, bf16[1,1,128,2048]{3,2,1,0:T(8,128)(2,1)} %refs_2_.3, bf16[1,1,128,2048]{3,2,1,0:T(8,128)(2,1)} %refs_3_.3), custom_call_target="tpu_custom_call" | custom-call | tf_op jit(solution)/shard_map/pack/pallas_call | solution.py:288
  8.5 2.1 %collective-permute-start.4 = (bf16[272,256]{1,0:T(8,128)(2,1)S(1)}, bf16[272,256]{1,0:T(8,128)(2,1)S(1)}, u32[]{:S(2)}, u32[]{:S(2)}) collective-permute-start(bf16[272,256]{1,0:T(8,128)(2,1)S(1)} %get-tuple-element.28), channel_id=1, source_target_pairs={{0,19},{1,18},{2,17},{3,16},{16,3},{17,2},{18,1},{19,0},{4,23},{5,... | collective-permute-start | bytes 417800 | tf_op jit(solution)/shard_map/ppermute | solution.py:270
  10.6 0.0 collective-permute-done.refs_0_
  10.6 0.3 collective-permute-start.5
  10.9 0.0 collective-permute-done.1.refs_1_
  10.9 0.2 collective-permute-start.6
  12.4 5.4 %collective-permute-done.2.refs_2_ = bf16[272,256]{1,0:T(8,128)(2,1)S(1)} collective-permute-done((bf16[272,256]{1,0:T(8,128)(2,1)S(1)}, bf16[272,256]{1,0:T(8,128)(2,1)S(1)}, u32[]{:S(2)}, u32[]{:S(2)}) %collective-permute-start.2) | collective-permute-done | bytes 139296 | tf_op jit(solution)/shard_map/ppermute | solution.py:270
  17.8 0.0 collective-permute-done.3.refs_3_
  17.8 0.0 collective-permute-done.4.refs_4_
  17.8 1.5 %collective-permute-done.5.refs_5_ = bf16[272,256]{1,0:T(8,128)(2,1)S(1)} collective-permute-done((bf16[272,256]{1,0:T(8,128)(2,1)S(1)}, bf16[272,256]{1,0:T(8,128)(2,1)S(1)}, u32[]{:S(2)}, u32[]{:S(2)}) %collective-permute-start.5) | collective-permute-done | bytes 139296 | tf_op jit(solution)/shard_map/ppermute | solution.py:270
  19.3 0.0 collective-permute-done.6.refs_6_
  19.3 3.6 %attend.1 = (bf16[256,256]{1,0:T(8,128)(2,1)S(1)}, bf16[256,256]{1,0:T(8,128)(2,1)S(1)}, bf16[256,256]{1,0:T(8,128)(2,1)S(1)}, bf16[256,256]{1,0:T(8,128)(2,1)S(...) custom-call(s32[1]{0:T(128)S(6)} %copy.12.source_len, ...), custom_call_target="tpu_custom_call" | custom-call | flops 335544320 | bytes 2097152 | tf_op jit(solution)/shard_map/attend/pallas_call | solution.py:309
  22.9 0.6 %collective-permute-start.12 = (bf16[256,256]{1,0:T(8,128)(2,1)S(1)}, bf16[256,256]{1,0:T(8,128)(2,1)S(1)}, u32[]{:S(2)}, u32[]{:S(2)}) collective-permute-start(bf16[256,256]{1,0:T(8,128)(2,1)S(1)} %get-tuple-element.37), channel_id=1, source_target_pairs={{0,16},{1,17},{2,18},{3,19},{16,0},{17,1},{18,2},{19,3},{4,20},{5,... | collective-permute-start | bytes 393224 | tf_op jit(solution)/shard_map/ppermute | solution.py:270
  23.5 0.5 %collective-permute-start.13 = (bf16[256,256]{1,0:T(8,128)(2,1)S(1)}, bf16[256,256]{1,0:T(8,128)(2,1)S(1)}, u32[]{:S(2)}, u32[]{:S(2)}) collective-permute-start(bf16[256,256]{1,0:T(8,128)(2,1)S(1)} %get-tuple-element.38), channel_id=1, source_target_pairs={{0,2},{1,3},{2,0},{3,1},{16,18},{17,19},{18,16},{19,17},{4,6},{5,7... | collective-permute-start | bytes 393224 | tf_op jit(solution)/shard_map/ppermute | solution.py:270
  24.0 2.5 %collective-permute-start.7 = (bf16[256,256]{1,0:T(8,128)(2,1)S(1)}, bf16[256,256]{1,0:T(8,128)(2,1)S(1)}, u32[]{:S(2)}, u32[]{:S(2)}) collective-permute-start(bf16[256,256]{1,0:T(8,128)(2,1)S(1)} %get-tuple-element.32), channel_id=1, source_target_pairs={{0,18},{1,19},{2,16},{3,17},{16,2},{17,3},{18,0},{19,1},{4,22},{5,... | collective-permute-start | bytes 393224 | tf_op jit(solution)/shard_map/ppermute | solution.py:270
  26.5 0.0 collective-permute-start.8
  26.5 2.0 %collective-permute-start.9 = (bf16[256,256]{1,0:T(8,128)(2,1)S(1)}, bf16[256,256]{1,0:T(8,128)(2,1)S(1)}, u32[]{:S(2)}, u32[]{:S(2)}) collective-permute-start(bf16[256,256]{1,0:T(8,128)(2,1)S(1)} %get-tuple-element.34), channel_id=1, source_target_pairs={{0,17},{1,16},{2,19},{3,18},{16,1},{17,0},{18,3},{19,2},{4,21},{5,... | collective-permute-start | bytes 393224 | tf_op jit(solution)/shard_map/ppermute | solution.py:270
  28.5 0.0 collective-permute-done.12.refs_0_
  28.5 0.0 collective-permute-start.10
  28.5 1.4 %collective-permute-done.13.refs_1_ = bf16[256,256]{1,0:T(8,128)(2,1)S(1)} collective-permute-done((bf16[256,256]{1,0:T(8,128)(2,1)S(1)}, bf16[256,256]{1,0:T(8,128)(2,1)S(1)}, u32[]{:S(2)}, u32[]{:S(2)}) %collective-permute-start.13) | collective-permute-done | bytes 131104 | tf_op jit(solution)/shard_map/ppermute | solution.py:270
  29.9 0.0 collective-permute-start.11
  29.9 0.9 %unpack.2 = (bf16[1,1,128,2048]{3,2,1,0:T(8,128)(2,1)}, bf16[1,1,128,2048]{3,2,1,0:T(8,128)(2,1)}) custom-call(bf16[256,256]{1,0:T(8,128)(2,1)S(1)} %collective-permute-done.12.refs_0_, bf16[256,256]{1,0:T(8,128)(2,1)S(1)} %collective-permute-done.13.refs_1_, bf16[256,256]{1,0:T(8,128)(2,1)S(1)} %get-tuple-element.39.refs_2_), custom_call_target="tpu_custom_call" | custom-call | tf_op jit(solution)/shard_map/unpack/pallas_call | solution.py:324
  30.8 2.9 %collective-permute-done.7.refs_0_ = bf16[256,256]{1,0:T(8,128)(2,1)S(1)} collective-permute-done((bf16[256,256]{1,0:T(8,128)(2,1)S(1)}, bf16[256,256]{1,0:T(8,128)(2,1)S(1)}, u32[]{:S(2)}, u32[]{:S(2)}) %collective-permute-start.7) | collective-permute-done | bytes 131104 | tf_op jit(solution)/shard_map/ppermute | solution.py:270
  33.7 0.0 collective-permute-done.8.refs_1_
  33.7 3.3 %collective-permute-done.9.refs_2_ = bf16[256,256]{1,0:T(8,128)(2,1)S(1)} collective-permute-done((bf16[256,256]{1,0:T(8,128)(2,1)S(1)}, bf16[256,256]{1,0:T(8,128)(2,1)S(1)}, u32[]{:S(2)}, u32[]{:S(2)}) %collective-permute-start.9) | collective-permute-done | bytes 131104 | tf_op jit(solution)/shard_map/ppermute | solution.py:270
  37.0 0.0 collective-permute-done.10.refs_3_
  37.0 0.0 collective-permute-done.11.refs_4_
  37.0 1.0 %unpack.3 = (bf16[1,1,128,2048]{3,2,1,0:T(8,128)(2,1)}, bf16[1,1,128,2048]{3,2,1,0:T(8,128)(2,1)}) custom-call(bf16[256,256]{1,0:T(8,128)(2,1)S(1)} %collective-permute-done.7.refs_0_, bf16[256,256]{1,0:T(8,128)(2,1)S(1)} %collective-permute-done.8.refs_1_, ...), custom_call_target="tpu_custom_call", output_to_operand_aliasing={{0}: (5, {}), {1}: (6, {})} | custom-call | tf_op jit(solution)/shard_map/unpack/pallas_call | solution.py:324
Async XLA Ops:
  1.9 8.7 %collective-permute-start = (bf16[272,256]{1,0:T(8,128)(2,1)S(1)}, bf16[272,256]{1,0:T(8,128)(2,1)S(1)}, u32[]{:S(2)}, u32[]{:S(2)}) collective-permute-start(bf16[272,256]{1,0:T(8,128)(2,1)S(1)} %get-tuple-element.23), channel_id=1, source_target_pairs={{0,16},{1,17},{2,18},{3,19},{16,0},{17,1},{18,2},{19,3},{4,20},{5,... | collective-permute-start | bytes 417800 | tf_op jit(solution)/shard_map/ppermute | solution.py:270
  4.9 6.0 %collective-permute-start.1 = (bf16[272,256]{1,0:T(8,128)(2,1)S(1)}, bf16[272,256]{1,0:T(8,128)(2,1)S(1)}, u32[]{:S(2)}, u32[]{:S(2)}) collective-permute-start(bf16[272,256]{1,0:T(8,128)(2,1)S(1)} %get-tuple-element.24), channel_id=1, source_target_pairs={{0,2},{1,3},{2,0},{3,1},{16,18},{17,19},{18,16},{19,17},{4,6},{5,7... | collective-permute-start | bytes 417800 | tf_op jit(solution)/shard_map/ppermute | solution.py:270
  6.4 11.4 %collective-permute-start.2 = (bf16[272,256]{1,0:T(8,128)(2,1)S(1)}, bf16[272,256]{1,0:T(8,128)(2,1)S(1)}, u32[]{:S(2)}, u32[]{:S(2)}) collective-permute-start(bf16[272,256]{1,0:T(8,128)(2,1)S(1)} %get-tuple-element.25), channel_id=1, source_target_pairs={{0,17},{1,16},{2,19},{3,18},{16,1},{17,0},{18,3},{19,2},{4,21},{5,... | collective-permute-start | bytes 417800 | tf_op jit(solution)/shard_map/ppermute | solution.py:270
  6.4 11.4 %collective-permute-start.3 = (bf16[272,256]{1,0:T(8,128)(2,1)S(1)}, bf16[272,256]{1,0:T(8,128)(2,1)S(1)}, u32[]{:S(2)}, u32[]{:S(2)}) collective-permute-start(bf16[272,256]{1,0:T(8,128)(2,1)S(1)} %get-tuple-element.26), channel_id=1, source_target_pairs={{0,18},{1,19},{2,16},{3,17},{16,2},{17,3},{18,0},{19,1},{4,22},{5,... | collective-permute-start | bytes 417800 | tf_op jit(solution)/shard_map/ppermute | solution.py:270
  8.5 9.3 %collective-permute-start.4 = (bf16[272,256]{1,0:T(8,128)(2,1)S(1)}, bf16[272,256]{1,0:T(8,128)(2,1)S(1)}, u32[]{:S(2)}, u32[]{:S(2)}) collective-permute-start(bf16[272,256]{1,0:T(8,128)(2,1)S(1)} %get-tuple-element.28), channel_id=1, source_target_pairs={{0,19},{1,18},{2,17},{3,16},{16,3},{17,2},{18,1},{19,0},{4,23},{5,... | collective-permute-start | bytes 417800 | tf_op jit(solution)/shard_map/ppermute | solution.py:270
  10.6 8.7 %collective-permute-start.5 = (bf16[272,256]{1,0:T(8,128)(2,1)S(1)}, bf16[272,256]{1,0:T(8,128)(2,1)S(1)}, u32[]{:S(2)}, u32[]{:S(2)}) collective-permute-start(bf16[272,256]{1,0:T(8,128)(2,1)S(1)} %get-tuple-element.29), channel_id=1, source_target_pairs={{0,3},{1,2},{2,1},{3,0},{16,19},{17,18},{18,17},{19,16},{4,7},{5,6... | collective-permute-start | bytes 417800 | tf_op jit(solution)/shard_map/ppermute | solution.py:270
  10.9 8.4 %collective-permute-start.6 = (bf16[272,256]{1,0:T(8,128)(2,1)S(1)}, bf16[272,256]{1,0:T(8,128)(2,1)S(1)}, u32[]{:S(2)}, u32[]{:S(2)}) collective-permute-start(bf16[272,256]{1,0:T(8,128)(2,1)S(1)} %get-tuple-element.30), channel_id=1, source_target_pairs={{0,1},{1,0},{2,3},{3,2},{16,17},{17,16},{18,19},{19,18},{4,5},{5,4... | collective-permute-start | bytes 417800 | tf_op jit(solution)/shard_map/ppermute | solution.py:270
  22.9 5.6 %collective-permute-start.12 = (bf16[256,256]{1,0:T(8,128)(2,1)S(1)}, bf16[256,256]{1,0:T(8,128)(2,1)S(1)}, u32[]{:S(2)}, u32[]{:S(2)}) collective-permute-start(bf16[256,256]{1,0:T(8,128)(2,1)S(1)} %get-tuple-element.37), channel_id=1, source_target_pairs={{0,16},{1,17},{2,18},{3,19},{16,0},{17,1},{18,2},{19,3},{4,20},{5,... | collective-permute-start | bytes 393224 | tf_op jit(solution)/shard_map/ppermute | solution.py:270
  23.5 6.4 %collective-permute-start.13 = (bf16[256,256]{1,0:T(8,128)(2,1)S(1)}, bf16[256,256]{1,0:T(8,128)(2,1)S(1)}, u32[]{:S(2)}, u32[]{:S(2)}) collective-permute-start(bf16[256,256]{1,0:T(8,128)(2,1)S(1)} %get-tuple-element.38), channel_id=1, source_target_pairs={{0,2},{1,3},{2,0},{3,1},{16,18},{17,19},{18,16},{19,17},{4,6},{5,7... | collective-permute-start | bytes 393224 | tf_op jit(solution)/shard_map/ppermute | solution.py:270
  24.0 9.7 %collective-permute-start.7 = (bf16[256,256]{1,0:T(8,128)(2,1)S(1)}, bf16[256,256]{1,0:T(8,128)(2,1)S(1)}, u32[]{:S(2)}, u32[]{:S(2)}) collective-permute-start(bf16[256,256]{1,0:T(8,128)(2,1)S(1)} %get-tuple-element.32), channel_id=1, source_target_pairs={{0,18},{1,19},{2,16},{3,17},{16,2},{17,3},{18,0},{19,1},{4,22},{5,... | collective-permute-start | bytes 393224 | tf_op jit(solution)/shard_map/ppermute | solution.py:270
  26.5 7.2 %collective-permute-start.8 = (bf16[256,256]{1,0:T(8,128)(2,1)S(1)}, bf16[256,256]{1,0:T(8,128)(2,1)S(1)}, u32[]{:S(2)}, u32[]{:S(2)}) collective-permute-start(bf16[256,256]{1,0:T(8,128)(2,1)S(1)} %get-tuple-element.33), channel_id=1, source_target_pairs={{0,19},{1,18},{2,17},{3,16},{16,3},{17,2},{18,1},{19,0},{4,23},{5,... | collective-permute-start | bytes 393224 | tf_op jit(solution)/shard_map/ppermute | solution.py:270
  26.5 10.5 %collective-permute-start.9 = (bf16[256,256]{1,0:T(8,128)(2,1)S(1)}, bf16[256,256]{1,0:T(8,128)(2,1)S(1)}, u32[]{:S(2)}, u32[]{:S(2)}) collective-permute-start(bf16[256,256]{1,0:T(8,128)(2,1)S(1)} %get-tuple-element.34), channel_id=1, source_target_pairs={{0,17},{1,16},{2,19},{3,18},{16,1},{17,0},{18,3},{19,2},{4,21},{5,... | collective-permute-start | bytes 393224 | tf_op jit(solution)/shard_map/ppermute | solution.py:270
  28.5 8.5 %collective-permute-start.10 = (bf16[256,256]{1,0:T(8,128)(2,1)S(1)}, bf16[256,256]{1,0:T(8,128)(2,1)S(1)}, u32[]{:S(2)}, u32[]{:S(2)}) collective-permute-start(bf16[256,256]{1,0:T(8,128)(2,1)S(1)} %get-tuple-element.35), channel_id=1, source_target_pairs={{0,3},{1,2},{2,1},{3,0},{16,19},{17,18},{18,17},{19,16},{4,7},{5,6... | collective-permute-start | bytes 393224 | tf_op jit(solution)/shard_map/ppermute | solution.py:270
  29.9 7.1 %collective-permute-start.11 = (bf16[256,256]{1,0:T(8,128)(2,1)S(1)}, bf16[256,256]{1,0:T(8,128)(2,1)S(1)}, u32[]{:S(2)}, u32[]{:S(2)}) collective-permute-start(bf16[256,256]{1,0:T(8,128)(2,1)S(1)} %get-tuple-element.36), channel_id=1, source_target_pairs={{0,1},{1,0},{2,3},{3,2},{16,17},{17,16},{18,19},{19,18},{4,5},{5,4... | collective-permute-start | bytes 393224 | tf_op jit(solution)/shard_map/ppermute | solution.py:270

commit v16 on v15

--- a/solution.py
+++ b/solution.py
@@ -37,8 +37,14 @@
     heads = tile // HDIM
     key_grad[...] = jnp.zeros_like(key_grad)
     value_grad[...] = jnp.zeros_like(value_grad)
-    inside = lax.broadcasted_iota(jnp.int32, (BLK, 1), 0)
+    key_inside = lax.broadcasted_iota(jnp.int32, (BLK, heads * BLK), 0)
+    row_inside = lax.broadcasted_iota(jnp.int32, (BLK, tile), 0)
     lane_head = lax.broadcasted_iota(jnp.int32, (BLK, tile), 1) // HDIM
+
+    def factor(mask):
+        return jnp.where(mask, 1.0, 0.0).astype(jnp.bfloat16)
+
+    own_lanes = [factor(lane_head == head) for head in range(heads)]
 
     def place(block):
         if per_device == 1:
@@ -68,23 +74,17 @@
         places = [place(index) for index in chosen]
         target, target_rows = place(block)
         key_valid = jnp.concatenate(
-            [index * BLK + inside < source_len for index in chosen], axis=0
+            [key_inside < source_len - index * BLK for index in chosen], axis=0
         )
-        live = block * BLK + inside < target_len
+        live = factor(row_inside < target_len - block * BLK)
         for first in range(0, width, tile):
             lanes = pl.ds(first, tile)
             keys = jnp.concatenate([rows[dev, 0, here, lanes] for dev, here in places], axis=0)
             values = jnp.concatenate([rows[dev, 1, here, lanes] for dev, here in places], axis=0)
             queries = rows[seq_count + target, 0, target_rows, lanes] * jnp.bfloat16(SCALE)
             cots = rows[seq_count + target, 1, target_rows, lanes]
-            none = jnp.zeros_like(queries)
-            cots = jnp.where(live, cots, none)
-            queries = jnp.concatenate(
-                [jnp.where(lane_head == head, queries, none) for head in range(heads)], axis=0
-            )
-            cots = jnp.concatenate(
-                [jnp.where(lane_head == head, cots, none) for head in range(heads)], axis=0
-            )
+            queries = jnp.concatenate([queries * own for own in own_lanes], axis=0)
+            cots = jnp.concatenate([cots * (live * own) for own in own_lanes], axis=0)
             scores = jnp.where(key_valid, contract(keys, queries, 1, 1), FLOOR)
             expo = jnp.exp(scores - jnp.max(scores, axis=0, keepdims=True))
             probs = expo * (1.0 / jnp.sum(expo, axis=0, keepdims=True))
@@ -98,7 +98,7 @@
             values_turned = jnp.concatenate([turned[index, 1, lanes] for index in chosen], axis=1)
             attended = own_heads(contract(values_turned, probs_low, 1, 0))
             dquery = own_heads(contract(keys_turned, dscore_low, 1, 0)) * SCALE
-            attended = jnp.where(live, attended.astype(jnp.bfloat16).T, none)
+            attended = attended.astype(jnp.bfloat16).T * live
             out[seq_count + target, 0, target_rows, lanes] = dquery.astype(jnp.bfloat16).T
             out[seq_count + target, 1, target_rows, lanes] = attended
             for slot, (dev, here) in enumerate(places):
@@ -281,7 +281,7 @@
     params = pltpu.CompilerParams(vmem_limit_bytes=VMEM_LIMIT)
     order = back = list(range(parts - 1, -1, -1))
     if parts == 8:
-        order, back = [4, 2, 5, 6, 7, 3, 1, 0], [4, 2, 6, 7, 5, 3, 1, 0]
+        order = back = [4, 2, 6, 7, 5, 3, 1, 0]
     sems = pltpu.SemaphoreType.DMA((2, parts))
 
     def pack(steps, lists):

time: 38.2 us -> 38.7 us (1.013)
  starting transfers between devices: 13.5 us -> 14.3 us
  waiting for transfers between devices: 14.6 us -> 14.2 us
    ppermute x14, starting transfers between devices: 13.5 us -> 14.3 us  [swapped(): lax.ppermute(share, AXES, [(dev, dev ^ step) for dev in range(parts)])]
  transfers between devices with their start and end apart: 14 -> 14, of which waited for: 5 -> 8; matrix products, arithmetic and copies ran while one was open for 0% -> 0% of each run, Pallas kernels for 6% -> 5%
where the time goes in v16:
time: 38.7 us; the launch traced here: 38.5 us
  starting transfers between devices  14.3 us (37%)
  waiting for transfers between devices  14.2 us (37%)
  Pallas kernels  7.97 us (21%)
  between operations  1.97 us (5%)
    ppermute x14, starting transfers between devices, swapped(): lax.ppermute(share, AXES, [(dev, dev ^ step) for dev in range(parts)])  14.3 us
    ppermute x14, waiting for transfers between devices, swapped(): lax.ppermute(share, AXES, [(dev, dev ^ step) for dev in range(parts)])  14.2 us
    pallas_call x1, Pallas kernels, by_pairs(): pl.pallas_call(functools.partial(attend_kernel, seq_count, order, back),...  3.65 us
    pallas_call x2, Pallas kernels, pack(): pl.pallas_call(functools.partial(pack_kernel, seq_count, steps), out_shap...  2.48 us
    pallas_call x2, Pallas kernels, unpack(): pl.pallas_call(functools.partial(unpack_kernel, seq_count, steps), out_sh...  1.84 us
  transfers between devices with their start and end apart: 14, of which 8 were waited for; matrix products, arithmetic and copies ran while one was open for 0% of the time, Pallas kernels for 5%

profile of v16, /device:TPU:0, one launch (start us, length us, event | category | flops | bytes accessed | tf_op | source)
XLA Modules:
  0.0 38.5 jit_solution(13354990808786091611)
XLA Ops:
  0.6 1.3 %pack.2 = (bf16[272,256]{1,0:T(8,128)(2,1)S(1)}, bf16[272,256]{1,0:T(8,128)(2,1)S(1)}, bf16[272,256]{1,0:T(8,128)(2,1)S(1)}, bf16[272,256]{1,0:T(8,128)(2,1)S(1)}) custom-call(s32[1,1,2]{2,1,0:T(1,128)} %refs_0_.2, s32[1,128]{1,0:T(1,128)} %refs_1_.3, bf16[1,1,128,2048]{3,2,1,0:T(8,128)(2,1)} %refs_2_.3, bf16[1,1,128,2048]{3,2,1,0:T(8,128)(2,1)} %refs_3_.3), custom_call_target="tpu_custom_call" | custom-call | tf_op jit(solution)/shard_map/pack/pallas_call | solution.py:288
  1.9 3.0 %collective-permute-start = (bf16[272,256]{1,0:T(8,128)(2,1)S(1)}, bf16[272,256]{1,0:T(8,128)(2,1)S(1)}, u32[]{:S(2)}, u32[]{:S(2)}) collective-permute-start(bf16[272,256]{1,0:T(8,128)(2,1)S(1)} %get-tuple-element.23), channel_id=1, source_target_pairs={{0,16},{1,17},{2,18},{3,19},{16,0},{17,1},{18,2},{19,3},{4,20},{5,... | collective-permute-start | bytes 417800 | tf_op jit(solution)/shard_map/ppermute | solution.py:270
  4.9 1.5 %collective-permute-start.1 = (bf16[272,256]{1,0:T(8,128)(2,1)S(1)}, bf16[272,256]{1,0:T(8,128)(2,1)S(1)}, u32[]{:S(2)}, u32[]{:S(2)}) collective-permute-start(bf16[272,256]{1,0:T(8,128)(2,1)S(1)} %get-tuple-element.24), channel_id=1, source_target_pairs={{0,2},{1,3},{2,0},{3,1},{16,18},{17,19},{18,16},{19,17},{4,6},{5,7... | collective-permute-start | bytes 417800 | tf_op jit(solution)/shard_map/ppermute | solution.py:270
  6.4 0.0 collective-permute-start.2
  6.5 1.5 %collective-permute-start.3 = (bf16[272,256]{1,0:T(8,128)(2,1)S(1)}, bf16[272,256]{1,0:T(8,128)(2,1)S(1)}, u32[]{:S(2)}, u32[]{:S(2)}) collective-permute-start(bf16[272,256]{1,0:T(8,128)(2,1)S(1)} %get-tuple-element.26), channel_id=1, source_target_pairs={{0,19},{1,18},{2,17},{3,16},{16,3},{17,2},{18,1},{19,0},{4,23},{5,... | collective-permute-start | bytes 417800 | tf_op jit(solution)/shard_map/ppermute | solution.py:270
  7.9 1.2 %pack.3 = (bf16[272,256]{1,0:T(8,128)(2,1)S(1)}, bf16[272,256]{1,0:T(8,128)(2,1)S(1)}, bf16[272,256]{1,0:T(8,128)(2,1)S(1)}, bf16[272,256]{1,0:T(8,128)(2,1)S(1)}) custom-call(s32[1,1,2]{2,1,0:T(1,128)} %refs_0_.2, s32[1,128]{1,0:T(1,128)} %refs_1_.3, bf16[1,1,128,2048]{3,2,1,0:T(8,128)(2,1)} %refs_2_.3, bf16[1,1,128,2048]{3,2,1,0:T(8,128)(2,1)} %refs_3_.3), custom_call_target="tpu_custom_call" | custom-call | tf_op jit(solution)/shard_map/pack/pallas_call | solution.py:288
  9.2 1.7 %collective-permute-start.4 = (bf16[272,256]{1,0:T(8,128)(2,1)S(1)}, bf16[272,256]{1,0:T(8,128)(2,1)S(1)}, u32[]{:S(2)}, u32[]{:S(2)}) collective-permute-start(bf16[272,256]{1,0:T(8,128)(2,1)S(1)} %get-tuple-element.28), channel_id=1, source_target_pairs={{0,17},{1,16},{2,19},{3,18},{16,1},{17,0},{18,3},{19,2},{4,21},{5,... | collective-permute-start | bytes 417800 | tf_op jit(solution)/shard_map/ppermute | solution.py:270
  10.9 0.0 collective-permute-done.refs_0_
  10.9 0.1 collective-permute-start.5
  11.0 0.5 %collective-permute-done.1.refs_1_ = bf16[272,256]{1,0:T(8,128)(2,1)S(1)} collective-permute-done((bf16[272,256]{1,0:T(8,128)(2,1)S(1)}, bf16[272,256]{1,0:T(8,128)(2,1)S(1)}, u32[]{:S(2)}, u32[]{:S(2)}) %collective-permute-start.1) | collective-permute-done | bytes 139296 | tf_op jit(solution)/shard_map/ppermute | solution.py:270
  11.5 0.0 collective-permute-start.6
  12.8 1.2 %collective-permute-done.2.refs_2_ = bf16[272,256]{1,0:T(8,128)(2,1)S(1)} collective-permute-done((bf16[272,256]{1,0:T(8,128)(2,1)S(1)}, bf16[272,256]{1,0:T(8,128)(2,1)S(1)}, u32[]{:S(2)}, u32[]{:S(2)}) %collective-permute-start.2) | collective-permute-done | bytes 139296 | tf_op jit(solution)/shard_map/ppermute | solution.py:270
  14.0 2.5 %collective-permute-done.3.refs_3_ = bf16[272,256]{1,0:T(8,128)(2,1)S(1)} collective-permute-done((bf16[272,256]{1,0:T(8,128)(2,1)S(1)}, bf16[272,256]{1,0:T(8,128)(2,1)S(1)}, u32[]{:S(2)}, u32[]{:S(2)}) %collective-permute-start.3) | collective-permute-done | bytes 139296 | tf_op jit(solution)/shard_map/ppermute | solution.py:270
  16.5 2.2 %collective-permute-done.4.refs_4_ = bf16[272,256]{1,0:T(8,128)(2,1)S(1)} collective-permute-done((bf16[272,256]{1,0:T(8,128)(2,1)S(1)}, bf16[272,256]{1,0:T(8,128)(2,1)S(1)}, u32[]{:S(2)}, u32[]{:S(2)}) %collective-permute-start.4) | collective-permute-done | bytes 139296 | tf_op jit(solution)/shard_map/ppermute | solution.py:270
  18.7 0.0 collective-permute-done.5.refs_5_
  18.7 0.0 collective-permute-done.6.refs_6_
  18.7 3.7 %attend.1 = (bf16[256,256]{1,0:T(8,128)(2,1)S(1)}, bf16[256,256]{1,0:T(8,128)(2,1)S(1)}, bf16[256,256]{1,0:T(8,128)(2,1)S(1)}, bf16[256,256]{1,0:T(8,128)(2,1)S(...) custom-call(s32[1]{0:T(128)S(6)} %copy.12.source_len, ...), custom_call_target="tpu_custom_call" | custom-call | flops 335544320 | bytes 2097152 | tf_op jit(solution)/shard_map/attend/pallas_call | solution.py:309
  22.4 1.8 %collective-permute-start.12 = (bf16[256,256]{1,0:T(8,128)(2,1)S(1)}, bf16[256,256]{1,0:T(8,128)(2,1)S(1)}, u32[]{:S(2)}, u32[]{:S(2)}) collective-permute-start(bf16[256,256]{1,0:T(8,128)(2,1)S(1)} %get-tuple-element.37), channel_id=1, source_target_pairs={{0,16},{1,17},{2,18},{3,19},{16,0},{17,1},{18,2},{19,3},{4,20},{5,... | collective-permute-start | bytes 393224 | tf_op jit(solution)/shard_map/ppermute | solution.py:270
  24.1 1.2 %collective-permute-start.13 = (bf16[256,256]{1,0:T(8,128)(2,1)S(1)}, bf16[256,256]{1,0:T(8,128)(2,1)S(1)}, u32[]{:S(2)}, u32[]{:S(2)}) collective-permute-start(bf16[256,256]{1,0:T(8,128)(2,1)S(1)} %get-tuple-element.38), channel_id=1, source_target_pairs={{0,2},{1,3},{2,0},{3,1},{16,18},{17,19},{18,16},{19,17},{4,6},{5,7... | collective-permute-start | bytes 393224 | tf_op jit(solution)/shard_map/ppermute | solution.py:270
  25.4 0.6 %collective-permute-start.7 = (bf16[256,256]{1,0:T(8,128)(2,1)S(1)}, bf16[256,256]{1,0:T(8,128)(2,1)S(1)}, u32[]{:S(2)}, u32[]{:S(2)}) collective-permute-start(bf16[256,256]{1,0:T(8,128)(2,1)S(1)} %get-tuple-element.32), channel_id=1, source_target_pairs={{0,18},{1,19},{2,16},{3,17},{16,2},{17,3},{18,0},{19,1},{4,22},{5,... | collective-permute-start | bytes 393224 | tf_op jit(solution)/shard_map/ppermute | solution.py:270
  25.9 1.2 %collective-permute-start.8 = (bf16[256,256]{1,0:T(8,128)(2,1)S(1)}, bf16[256,256]{1,0:T(8,128)(2,1)S(1)}, u32[]{:S(2)}, u32[]{:S(2)}) collective-permute-start(bf16[256,256]{1,0:T(8,128)(2,1)S(1)} %get-tuple-element.33), channel_id=1, source_target_pairs={{0,19},{1,18},{2,17},{3,16},{16,3},{17,2},{18,1},{19,0},{4,23},{5,... | collective-permute-start | bytes 393224 | tf_op jit(solution)/shard_map/ppermute | solution.py:270
  27.2 1.4 %collective-permute-start.9 = (bf16[256,256]{1,0:T(8,128)(2,1)S(1)}, bf16[256,256]{1,0:T(8,128)(2,1)S(1)}, u32[]{:S(2)}, u32[]{:S(2)}) collective-permute-start(bf16[256,256]{1,0:T(8,128)(2,1)S(1)} %get-tuple-element.34), channel_id=1, source_target_pairs={{0,17},{1,16},{2,19},{3,18},{16,1},{17,0},{18,3},{19,2},{4,21},{5,... | collective-permute-start | bytes 393224 | tf_op jit(solution)/shard_map/ppermute | solution.py:270
  28.6 0.0 collective-permute-done.12.refs_0_
  28.6 0.2 collective-permute-start.10
  28.8 1.7 %collective-permute-done.13.refs_1_ = bf16[256,256]{1,0:T(8,128)(2,1)S(1)} collective-permute-done((bf16[256,256]{1,0:T(8,128)(2,1)S(1)}, bf16[256,256]{1,0:T(8,128)(2,1)S(1)}, u32[]{:S(2)}, u32[]{:S(2)}) %collective-permute-start.13) | collective-permute-done | bytes 131104 | tf_op jit(solution)/shard_map/ppermute | solution.py:270
  30.5 0.0 collective-permute-start.11
  30.5 0.9 %unpack.2 = (bf16[1,1,128,2048]{3,2,1,0:T(8,128)(2,1)}, bf16[1,1,128,2048]{3,2,1,0:T(8,128)(2,1)}) custom-call(bf16[256,256]{1,0:T(8,128)(2,1)S(1)} %collective-permute-done.12.refs_0_, bf16[256,256]{1,0:T(8,128)(2,1)S(1)} %collective-permute-done.13.refs_1_, bf16[256,256]{1,0:T(8,128)(2,1)S(1)} %get-tuple-element.39.refs_2_), custom_call_target="tpu_custom_call" | custom-call | tf_op jit(solution)/shard_map/unpack/pallas_call | solution.py:324
  31.4 1.5 %collective-permute-done.7.refs_0_ = bf16[256,256]{1,0:T(8,128)(2,1)S(1)} collective-permute-done((bf16[256,256]{1,0:T(8,128)(2,1)S(1)}, bf16[256,256]{1,0:T(8,128)(2,1)S(1)}, u32[]{:S(2)}, u32[]{:S(2)}) %collective-permute-start.7) | collective-permute-done | bytes 131104 | tf_op jit(solution)/shard_map/ppermute | solution.py:270
  32.9 2.0 %collective-permute-done.8.refs_1_ = bf16[256,256]{1,0:T(8,128)(2,1)S(1)} collective-permute-done((bf16[256,256]{1,0:T(8,128)(2,1)S(1)}, bf16[256,256]{1,0:T(8,128)(2,1)S(1)}, u32[]{:S(2)}, u32[]{:S(2)}) %collective-permute-start.8) | collective-permute-done | bytes 131104 | tf_op jit(solution)/shard_map/ppermute | solution.py:270
  34.9 2.6 %collective-permute-done.9.refs_2_ = bf16[256,256]{1,0:T(8,128)(2,1)S(1)} collective-permute-done((bf16[256,256]{1,0:T(8,128)(2,1)S(1)}, bf16[256,256]{1,0:T(8,128)(2,1)S(1)}, u32[]{:S(2)}, u32[]{:S(2)}) %collective-permute-start.9) | collective-permute-done | bytes 131104 | tf_op jit(solution)/shard_map/ppermute | solution.py:270
  37.5 0.0 collective-permute-done.10.refs_3_
  37.5 0.0 collective-permute-done.11.refs_4_
  37.5 1.0 %unpack.3 = (bf16[1,1,128,2048]{3,2,1,0:T(8,128)(2,1)}, bf16[1,1,128,2048]{3,2,1,0:T(8,128)(2,1)}) custom-call(bf16[256,256]{1,0:T(8,128)(2,1)S(1)} %collective-permute-done.7.refs_0_, bf16[256,256]{1,0:T(8,128)(2,1)S(1)} %collective-permute-done.8.refs_1_, ...), custom_call_target="tpu_custom_call", output_to_operand_aliasing={{0}: (5, {}), {1}: (6, {})} | custom-call | tf_op jit(solution)/shard_map/unpack/pallas_call | solution.py:324
Async XLA Ops:
  1.9 9.0 %collective-permute-start = (bf16[272,256]{1,0:T(8,128)(2,1)S(1)}, bf16[272,256]{1,0:T(8,128)(2,1)S(1)}, u32[]{:S(2)}, u32[]{:S(2)}) collective-permute-start(bf16[272,256]{1,0:T(8,128)(2,1)S(1)} %get-tuple-element.23), channel_id=1, source_target_pairs={{0,16},{1,17},{2,18},{3,19},{16,0},{17,1},{18,2},{19,3},{4,20},{5,... | collective-permute-start | bytes 417800 | tf_op jit(solution)/shard_map/ppermute | solution.py:270
  4.9 6.6 %collective-permute-start.1 = (bf16[272,256]{1,0:T(8,128)(2,1)S(1)}, bf16[272,256]{1,0:T(8,128)(2,1)S(1)}, u32[]{:S(2)}, u32[]{:S(2)}) collective-permute-start(bf16[272,256]{1,0:T(8,128)(2,1)S(1)} %get-tuple-element.24), channel_id=1, source_target_pairs={{0,2},{1,3},{2,0},{3,1},{16,18},{17,19},{18,16},{19,17},{4,6},{5,7... | collective-permute-start | bytes 417800 | tf_op jit(solution)/shard_map/ppermute | solution.py:270
  6.4 7.6 %collective-permute-start.2 = (bf16[272,256]{1,0:T(8,128)(2,1)S(1)}, bf16[272,256]{1,0:T(8,128)(2,1)S(1)}, u32[]{:S(2)}, u32[]{:S(2)}) collective-permute-start(bf16[272,256]{1,0:T(8,128)(2,1)S(1)} %get-tuple-element.25), channel_id=1, source_target_pairs={{0,18},{1,19},{2,16},{3,17},{16,2},{17,3},{18,0},{19,1},{4,22},{5,... | collective-permute-start | bytes 417800 | tf_op jit(solution)/shard_map/ppermute | solution.py:270
  6.5 10.1 %collective-permute-start.3 = (bf16[272,256]{1,0:T(8,128)(2,1)S(1)}, bf16[272,256]{1,0:T(8,128)(2,1)S(1)}, u32[]{:S(2)}, u32[]{:S(2)}) collective-permute-start(bf16[272,256]{1,0:T(8,128)(2,1)S(1)} %get-tuple-element.26), channel_id=1, source_target_pairs={{0,19},{1,18},{2,17},{3,16},{16,3},{17,2},{18,1},{19,0},{4,23},{5,... | collective-permute-start | bytes 417800 | tf_op jit(solution)/shard_map/ppermute | solution.py:270
  9.2 9.5 %collective-permute-start.4 = (bf16[272,256]{1,0:T(8,128)(2,1)S(1)}, bf16[272,256]{1,0:T(8,128)(2,1)S(1)}, u32[]{:S(2)}, u32[]{:S(2)}) collective-permute-start(bf16[272,256]{1,0:T(8,128)(2,1)S(1)} %get-tuple-element.28), channel_id=1, source_target_pairs={{0,17},{1,16},{2,19},{3,18},{16,1},{17,0},{18,3},{19,2},{4,21},{5,... | collective-permute-start | bytes 417800 | tf_op jit(solution)/shard_map/ppermute | solution.py:270
  10.9 7.8 %collective-permute-start.5 = (bf16[272,256]{1,0:T(8,128)(2,1)S(1)}, bf16[272,256]{1,0:T(8,128)(2,1)S(1)}, u32[]{:S(2)}, u32[]{:S(2)}) collective-permute-start(bf16[272,256]{1,0:T(8,128)(2,1)S(1)} %get-tuple-element.29), channel_id=1, source_target_pairs={{0,3},{1,2},{2,1},{3,0},{16,19},{17,18},{18,17},{19,16},{4,7},{5,6... | collective-permute-start | bytes 417800 | tf_op jit(solution)/shard_map/ppermute | solution.py:270
  11.5 7.2 %collective-permute-start.6 = (bf16[272,256]{1,0:T(8,128)(2,1)S(1)}, bf16[272,256]{1,0:T(8,128)(2,1)S(1)}, u32[]{:S(2)}, u32[]{:S(2)}) collective-permute-start(bf16[272,256]{1,0:T(8,128)(2,1)S(1)} %get-tuple-element.30), channel_id=1, source_target_pairs={{0,1},{1,0},{2,3},{3,2},{16,17},{17,16},{18,19},{19,18},{4,5},{5,4... | collective-permute-start | bytes 417800 | tf_op jit(solution)/shard_map/ppermute | solution.py:270
  22.4 6.2 %collective-permute-start.12 = (bf16[256,256]{1,0:T(8,128)(2,1)S(1)}, bf16[256,256]{1,0:T(8,128)(2,1)S(1)}, u32[]{:S(2)}, u32[]{:S(2)}) collective-permute-start(bf16[256,256]{1,0:T(8,128)(2,1)S(1)} %get-tuple-element.37), channel_id=1, source_target_pairs={{0,16},{1,17},{2,18},{3,19},{16,0},{17,1},{18,2},{19,3},{4,20},{5,... | collective-permute-start | bytes 393224 | tf_op jit(solution)/shard_map/ppermute | solution.py:270
  24.1 6.4 %collective-permute-start.13 = (bf16[256,256]{1,0:T(8,128)(2,1)S(1)}, bf16[256,256]{1,0:T(8,128)(2,1)S(1)}, u32[]{:S(2)}, u32[]{:S(2)}) collective-permute-start(bf16[256,256]{1,0:T(8,128)(2,1)S(1)} %get-tuple-element.38), channel_id=1, source_target_pairs={{0,2},{1,3},{2,0},{3,1},{16,18},{17,19},{18,16},{19,17},{4,6},{5,7... | collective-permute-start | bytes 393224 | tf_op jit(solution)/shard_map/ppermute | solution.py:270
  25.4 7.5 %collective-permute-start.7 = (bf16[256,256]{1,0:T(8,128)(2,1)S(1)}, bf16[256,256]{1,0:T(8,128)(2,1)S(1)}, u32[]{:S(2)}, u32[]{:S(2)}) collective-permute-start(bf16[256,256]{1,0:T(8,128)(2,1)S(1)} %get-tuple-element.32), channel_id=1, source_target_pairs={{0,18},{1,19},{2,16},{3,17},{16,2},{17,3},{18,0},{19,1},{4,22},{5,... | collective-permute-start | bytes 393224 | tf_op jit(solution)/shard_map/ppermute | solution.py:270
  25.9 9.0 %collective-permute-start.8 = (bf16[256,256]{1,0:T(8,128)(2,1)S(1)}, bf16[256,256]{1,0:T(8,128)(2,1)S(1)}, u32[]{:S(2)}, u32[]{:S(2)}) collective-permute-start(bf16[256,256]{1,0:T(8,128)(2,1)S(1)} %get-tuple-element.33), channel_id=1, source_target_pairs={{0,19},{1,18},{2,17},{3,16},{16,3},{17,2},{18,1},{19,0},{4,23},{5,... | collective-permute-start | bytes 393224 | tf_op jit(solution)/shard_map/ppermute | solution.py:270
  27.2 10.4 %collective-permute-start.9 = (bf16[256,256]{1,0:T(8,128)(2,1)S(1)}, bf16[256,256]{1,0:T(8,128)(2,1)S(1)}, u32[]{:S(2)}, u32[]{:S(2)}) collective-permute-start(bf16[256,256]{1,0:T(8,128)(2,1)S(1)} %get-tuple-element.34), channel_id=1, source_target_pairs={{0,17},{1,16},{2,19},{3,18},{16,1},{17,0},{18,3},{19,2},{4,21},{5,... | collective-permute-start | bytes 393224 | tf_op jit(solution)/shard_map/ppermute | solution.py:270
  28.6 9.0 %collective-permute-start.10 = (bf16[256,256]{1,0:T(8,128)(2,1)S(1)}, bf16[256,256]{1,0:T(8,128)(2,1)S(1)}, u32[]{:S(2)}, u32[]{:S(2)}) collective-permute-start(bf16[256,256]{1,0:T(8,128)(2,1)S(1)} %get-tuple-element.35), channel_id=1, source_target_pairs={{0,3},{1,2},{2,1},{3,0},{16,19},{17,18},{18,17},{19,16},{4,7},{5,6... | collective-permute-start | bytes 393224 | tf_op jit(solution)/shard_map/ppermute | solution.py:270
  30.5 7.0 %collective-permute-start.11 = (bf16[256,256]{1,0:T(8,128)(2,1)S(1)}, bf16[256,256]{1,0:T(8,128)(2,1)S(1)}, u32[]{:S(2)}, u32[]{:S(2)}) collective-permute-start(bf16[256,256]{1,0:T(8,128)(2,1)S(1)} %get-tuple-element.36), channel_id=1, source_target_pairs={{0,1},{1,0},{2,3},{3,2},{16,17},{17,16},{18,19},{19,18},{4,5},{5,4... | collective-permute-start | bytes 393224 | tf_op jit(solution)/shard_map/ppermute | solution.py:270

commit v17 on v15

--- a/solution.py
+++ b/solution.py
@@ -14,7 +14,6 @@
 SPAN = 2 * WIN + 1
 LANES = 128
 TAIL = 16
-EARLY = (0, 2, 4)
 SCALE = HDIM ** (-0.5)
 FLOOR = -1e30
 VMEM_LIMIT = 32 * 1024 * 1024
@@ -174,24 +173,32 @@
     return lax.axis_index("section") * seq_count + lax.axis_index("seq")
 
 
+OUTGOING = [(0,), (1,), (6, 7), (4,), (2,), (5,), (3,)]
+INCOMING = [*OUTGOING, (7,)]
+
+
 def pack_kernel(seq_count, steps, *refs):
     smalls, (first, second) = refs[:2], refs[2:4]
     outs, (lists, mask, small_sem, sem) = refs[4:-4], refs[-4:]
     me = device_index(seq_count)
     here = me % seq_count
     share = outs[0].shape[1]
-    copies = []
-    for slot, (step, out) in enumerate(zip(steps, outs)):
-        lanes = pl.ds(pl.multiple_of((me ^ step) * share, LANES), share)
-        pair = [
-            pltpu.make_async_copy(
-                source.at[0, 0, :, lanes], out.at[pl.ds(half * BLK, BLK)], sem.at[half, slot]
-            )
-            for half, source in enumerate((first, second))
-        ]
-        for copy in pair:
-            copy.start()
-        copies.append(pair)
+    copies, pieces = [], []
+    for group, out in zip(steps, outs):
+        for place, step in enumerate(group):
+            slot = len(copies)
+            lanes = pl.ds(pl.multiple_of((me ^ step) * share, LANES), share)
+            piece = out.at[pl.ds(place * 2 * BLK, 2 * BLK)]
+            pair = [
+                pltpu.make_async_copy(
+                    source.at[0, 0, :, lanes], piece.at[pl.ds(half * BLK, BLK)], sem.at[half, slot]
+                )
+                for half, source in enumerate((first, second))
+            ]
+            for copy in pair:
+                copy.start()
+            copies.append(pair)
+            pieces.append(piece)
     small_copies = [
         pltpu.make_async_copy(source, held, small_sem.at[slot])
         for slot, (source, held) in enumerate(zip(smalls, (lists, mask)))
@@ -206,20 +213,22 @@
     base = here - WIN
     code = (lists[0, 0, 0] - base) * SPAN + lists[0, 0, 1] - base
     tail = jnp.full((TAIL, share), code, jnp.int32).astype(jnp.float32).astype(jnp.bfloat16)
-    for out, pair in zip(outs, copies):
+    for out in outs:
+        if out.shape[0] % (2 * BLK):
+            out[2 * BLK :] = tail
+    for piece, pair in zip(pieces, copies):
         for copy in pair:
             copy.wait()
-        out[BLK : 2 * BLK] = out[BLK : 2 * BLK] * keep
-        out[2 * BLK :] = tail
-
-
-def attend_kernel(seq_count, order, back, source_len, target_len, *refs):
-    parts = 2 * seq_count
-    shares, outs = refs[:parts], refs[parts : 2 * parts]
-    rows, result, key_grad, value_grad, turned, lists = refs[2 * parts :]
+        piece[BLK:] = piece[BLK:] * keep
+
+
+def attend_kernel(seq_count, order, source_len, target_len, *refs):
+    count = len(order)
+    shares, outs = refs[:count], refs[count : 2 * count - 1]
+    rows, result, key_grad, value_grad, turned, lists = refs[2 * count - 1 :]
     me = device_index(seq_count)
     here = me % seq_count
-    for step, share in zip(order, shares):
+    for (step, *_), share in zip(order, shares):
         source = me ^ step
         rows[source, 0] = share[:BLK]
         rows[source, 1] = share[BLK : 2 * BLK]
@@ -242,9 +251,10 @@
         value_grad,
         turned,
     )
-    for step, out in zip(back, outs):
-        out[:BLK] = result[me ^ step, 0]
-        out[BLK:] = result[me ^ step, 1]
+    for group, out in zip(OUTGOING, outs):
+        for place, step in enumerate(group):
+            out[2 * place * BLK : (2 * place + 1) * BLK] = result[me ^ step, 0]
+            out[(2 * place + 1) * BLK : (2 * place + 2) * BLK] = result[me ^ step, 1]
 
 
 def unpack_kernel(seq_count, steps, *refs):
@@ -252,7 +262,7 @@
     width = shares[0].shape[1]
     me = device_index(seq_count)
     copies = []
-    for slot, (step, share) in enumerate(zip(steps, shares)):
+    for slot, ((step, *_), share) in enumerate(zip(steps, shares)):
         lanes = pl.ds(pl.multiple_of((me ^ step) * width, LANES), width)
         for half, result in enumerate((first, second)):
             copy = pltpu.make_async_copy(
@@ -264,12 +274,19 @@
         copy.wait()
 
 
-def swapped(shares, order):
-    parts = len(order)
-    return [
-        lax.ppermute(share, AXES, [(dev, dev ^ step) for dev in range(parts)]) if step else share
-        for step, share in zip(order, shares)
-    ]
+def swapped(shares):
+    parts = 8
+
+    def move(share, step):
+        return lax.ppermute(share, AXES, [(dev, dev ^ step) for dev in range(parts)])
+
+    moved = {
+        group: move(share, group[0]) if group[0] else share
+        for group, share in zip(OUTGOING, shares)
+    }
+    moved[(6, 7)], moved[(1,)] = lax.optimization_barrier((moved[(6, 7)], moved[(1,)]))
+    moved[(7,)] = move(moved[(6, 7)][2 * BLK :], 1)
+    return [moved[group] for group in INCOMING]
 
 
 def by_pairs(first_rows, second_rows, alignment, diffusion_mask, source_length, target_length):
@@ -279,17 +296,22 @@
     share = width // parts
     kind = first_rows.dtype
     params = pltpu.CompilerParams(vmem_limit_bytes=VMEM_LIMIT)
-    order = back = list(range(parts - 1, -1, -1))
-    if parts == 8:
-        order, back = [4, 2, 5, 6, 7, 3, 1, 0], [4, 2, 6, 7, 5, 3, 1, 0]
     sems = pltpu.SemaphoreType.DMA((2, parts))
 
-    def pack(steps, lists):
+    def sizes(groups, tail):
+        return [
+            jax.ShapeDtypeStruct(
+                (len(group) * 2 * BLK + (tail if group[0] < seq_count else 0), share), kind
+            )
+            for group in groups
+        ]
+
+    def pack(groups, lists):
         return pl.pallas_call(
-            functools.partial(pack_kernel, seq_count, steps),
-            out_shape=[jax.ShapeDtypeStruct((2 * BLK + TAIL, share), kind)] * len(steps),
+            functools.partial(pack_kernel, seq_count, groups),
+            out_shape=sizes(groups, TAIL),
             in_specs=specs(4, pltpu.HBM),
-            out_specs=specs(len(steps), pltpu.VMEM),
+            out_specs=specs(len(groups), pltpu.VMEM),
             scratch_shapes=[
                 pltpu.SMEM(alignment.shape, jnp.int32),
                 pltpu.VMEM(diffusion_mask.shape, jnp.int32),
@@ -300,48 +322,38 @@
             name="pack",
         )(*in_hbm(lists, diffusion_mask, first_rows, second_rows))
 
-    shares = list(pack(order[:seq_count], alignment))
-    lists, shares[0] = lax.optimization_barrier((alignment, shares[0]))
-    shares = swapped([*shares, *pack(order[seq_count:], lists)], order)
+    shares = swapped(pack(OUTGOING, alignment))
     rows = pltpu.VMEM((parts, 2, BLK, share), kind)
     grads = pltpu.VMEM((seq_count, BLK, share), jnp.float32)
     turned = pltpu.VMEM((seq_count, 2, share, BLK), kind)
     shares = pl.pallas_call(
-        functools.partial(attend_kernel, seq_count, order, back),
-        out_shape=[jax.ShapeDtypeStruct((2 * BLK, share), kind)] * parts,
-        in_specs=specs(2, pltpu.SMEM) + specs(parts, pltpu.VMEM),
-        out_specs=specs(parts, pltpu.VMEM),
+        functools.partial(attend_kernel, seq_count, INCOMING),
+        out_shape=sizes(OUTGOING, 0),
+        in_specs=specs(2, pltpu.SMEM) + specs(len(INCOMING), pltpu.VMEM),
+        out_specs=specs(len(OUTGOING), pltpu.VMEM),
         scratch_shapes=[rows, rows, grads, grads, turned, pltpu.SMEM((seq_count,), jnp.int32)],
         compiler_params=params,
         cost_estimate=attend_cost(seq_count, share),
         name="attend",
     )(source_length, target_length, *shares)
-    shares = dict(zip(back, swapped(shares, back)))
+    shares = swapped(shares)
     out_shape = jax.ShapeDtypeStruct((1, 1, BLK, width), kind)
-
-    def unpack(steps, *begun):
-        count = len(steps)
-        return pl.pallas_call(
-            functools.partial(unpack_kernel, seq_count, steps),
-            out_shape=[out_shape, out_shape],
-            in_specs=specs(count, pltpu.VMEM) + specs(len(begun), pltpu.HBM),
-            out_specs=specs(2, pltpu.HBM),
-            input_output_aliases={count + slot: slot for slot in range(len(begun))},
-            scratch_shapes=[sems],
-            compiler_params=params,
-            name="unpack",
-        )(*(shares[step] for step in steps), *begun)
-
-    early = [step for step in back if step in EARLY]
-    return unpack([step for step in back if step not in EARLY], *unpack(early))
+    return pl.pallas_call(
+        functools.partial(unpack_kernel, seq_count, INCOMING),
+        out_shape=[out_shape, out_shape],
+        in_specs=specs(len(INCOMING), pltpu.VMEM),
+        out_specs=specs(2, pltpu.HBM),
+        scratch_shapes=[sems],
+        compiler_params=params,
+        name="unpack",
+    )(*shares)
 
 
 def on_device(first_rows, second_rows, alignment, diffusion_mask, source_length, target_length):
     seq_count = lax.axis_size("seq")
     parts = lax.axis_size("section") * seq_count
     paired = (
-        parts == 2 * seq_count
-        and seq_count & (seq_count - 1) == 0
+        (parts, seq_count) == (8, 4)
         and first_rows.shape[2] == BLK
         and first_rows.shape[3] % (parts * LANES) == 0
     )

time: 38.2 us -> 38.1 us (level)
  Pallas kernels: 7.93 us -> 6.13 us
  waiting for transfers between devices: 14.6 us -> 15.6 us
  starting transfers between devices: 13.5 us -> 14.1 us
    pallas_call x5 -> x3, Pallas kernels: 7.93 us -> 6.13 us  [the longest x1 3.61 us: by_pairs(): pl.pallas_call(functools.partial(attend_kernel, seq_count, INCOMING), out...]
    ppermute x14, waiting for transfers between devices: 14.6 us -> 15.6 us  [move(): lax.ppermute(share, AXES, [(dev, dev ^ step) for dev in range(parts)])]
    ppermute x14, starting transfers between devices: 13.5 us -> 14.1 us  [move(): lax.ppermute(share, AXES, [(dev, dev ^ step) for dev in range(parts)])]
  transfers between devices with their start and end apart: 14 -> 14, of which waited for: 5 -> 7; matrix products, arithmetic and copies ran while one was open for 0% -> 0% of each run, Pallas kernels for 6% -> 0%
where the time goes in v17:
time: 38.1 us; the launch traced here: 37.9 us
  waiting for transfers between devices  15.6 us (41%)
  starting transfers between devices  14.1 us (37%)
  Pallas kernels  6.13 us (16%)
  between operations  1.98 us (5%)
    ppermute x14, waiting for transfers between devices, move(): lax.ppermute(share, AXES, [(dev, dev ^ step) for dev in range(parts)])  15.6 us
    ppermute x14, starting transfers between devices, move(): lax.ppermute(share, AXES, [(dev, dev ^ step) for dev in range(parts)])  14.1 us
    pallas_call x1, Pallas kernels, by_pairs(): pl.pallas_call(functools.partial(attend_kernel, seq_count, INCOMING), out...  3.61 us
    pallas_call x1, Pallas kernels, pack(): pl.pallas_call(functools.partial(pack_kernel, seq_count, groups), out_sha...  1.43 us
    pallas_call x1, Pallas kernels, by_pairs(): pl.pallas_call(functools.partial(unpack_kernel, seq_count, INCOMING), out...  1.09 us
  transfers between devices with their start and end apart: 14, of which 7 were waited for; matrix products, arithmetic and copies ran while one was open for 0% of the time, Pallas kernels for 0%

profile of v17, /device:TPU:0, one launch (start us, length us, event | category | flops | bytes accessed | tf_op | source)
XLA Modules:
  0.0 37.9 jit_solution(13053454978257191298)
XLA Ops:
  0.6 1.4 %pack.1 = (bf16[272,256]{1,0:T(8,128)(2,1)S(1)}, bf16[272,256]{1,0:T(8,128)(2,1)S(1)}, bf16[512,256]{1,0:T(8,128)(2,1)S(1)}, bf16[256,256]{1,0:T(8,128)(2,1)S(1)...) custom-call(s32[1,1,2]{2,1,0:T(1,128)} %refs_0_.1, s32[1,128]{1,0:T(1,128)} %refs_1_.1, ...), custom_call_target="tpu_custom_call" | custom-call | tf_op jit(solution)/shard_map/pack/pallas_call | solution.py:310
  2.1 4.0 %collective-permute-start = (bf16[512,256]{1,0:T(8,128)(2,1)S(1)}, bf16[512,256]{1,0:T(8,128)(2,1)S(1)}, u32[]{:S(2)}, u32[]{:S(2)}) collective-permute-start(bf16[512,256]{1,0:T(8,128)(2,1)S(1)} %get-tuple-element.21), channel_id=1, source_target_pairs={{0,18},{1,19},{2,16},{3,17},{16,2},{17,3},{18,0},{19,1},{4,22},{5,... | collective-permute-start | bytes 786440 | tf_op jit(solution)/shard_map/ppermute | solution.py:281
  6.0 0.0 collective-permute-start.1
  6.0 0.5 %collective-permute-start.3 = (bf16[272,256]{1,0:T(8,128)(2,1)S(1)}, bf16[272,256]{1,0:T(8,128)(2,1)S(1)}, u32[]{:S(2)}, u32[]{:S(2)}) collective-permute-start(bf16[272,256]{1,0:T(8,128)(2,1)S(1)} %get-tuple-element.26), channel_id=1, source_target_pairs={{0,2},{1,3},{2,0},{3,1},{16,18},{17,19},{18,16},{19,17},{4,6},{5,7... | collective-permute-start | bytes 417800 | tf_op jit(solution)/shard_map/ppermute | solution.py:281
  6.6 1.3 %collective-permute-start.5 = (bf16[272,256]{1,0:T(8,128)(2,1)S(1)}, bf16[272,256]{1,0:T(8,128)(2,1)S(1)}, u32[]{:S(2)}, u32[]{:S(2)}) collective-permute-start(bf16[272,256]{1,0:T(8,128)(2,1)S(1)} %get-tuple-element.28), channel_id=1, source_target_pairs={{0,3},{1,2},{2,1},{3,0},{16,19},{17,18},{18,17},{19,16},{4,7},{5,6... | collective-permute-start | bytes 417800 | tf_op jit(solution)/shard_map/ppermute | solution.py:281
  7.9 0.5 %collective-permute-start.2 = (bf16[256,256]{1,0:T(8,128)(2,1)S(1)}, bf16[256,256]{1,0:T(8,128)(2,1)S(1)}, u32[]{:S(2)}, u32[]{:S(2)}) collective-permute-start(bf16[256,256]{1,0:T(8,128)(2,1)S(1)} %get-tuple-element.25), channel_id=1, source_target_pairs={{0,16},{1,17},{2,18},{3,19},{16,0},{17,1},{18,2},{19,3},{4,20},{5,... | collective-permute-start | bytes 393224 | tf_op jit(solution)/shard_map/ppermute | solution.py:281
  8.4 0.0 collective-permute-done.1.refs_1_
  8.4 1.1 %collective-permute-start.4 = (bf16[256,256]{1,0:T(8,128)(2,1)S(1)}, bf16[256,256]{1,0:T(8,128)(2,1)S(1)}, u32[]{:S(2)}, u32[]{:S(2)}) collective-permute-start(bf16[256,256]{1,0:T(8,128)(2,1)S(1)} %get-tuple-element.27), channel_id=1, source_target_pairs={{0,17},{1,16},{2,19},{3,18},{16,1},{17,0},{18,3},{19,2},{4,21},{5,... | collective-permute-start | bytes 393224 | tf_op jit(solution)/shard_map/ppermute | solution.py:281
  9.5 3.6 %collective-permute-done.refs_2_ = bf16[512,256]{1,0:T(8,128)(2,1)S(1)} collective-permute-done((bf16[512,256]{1,0:T(8,128)(2,1)S(1)}, bf16[512,256]{1,0:T(8,128)(2,1)S(1)}, u32[]{:S(2)}, u32[]{:S(2)}) %collective-permute-start) | collective-permute-done | bytes 262176 | tf_op jit(solution)/shard_map/ppermute | solution.py:281
  13.2 0.1 collective-permute-start.6
  14.5 0.7 %collective-permute-done.2.refs_3_ = bf16[256,256]{1,0:T(8,128)(2,1)S(1)} collective-permute-done((bf16[256,256]{1,0:T(8,128)(2,1)S(1)}, bf16[256,256]{1,0:T(8,128)(2,1)S(1)}, u32[]{:S(2)}, u32[]{:S(2)}) %collective-permute-start.2) | collective-permute-done | bytes 131104 | tf_op jit(solution)/shard_map/ppermute | solution.py:281
  15.2 2.7 %collective-permute-done.4.refs_5_ = bf16[256,256]{1,0:T(8,128)(2,1)S(1)} collective-permute-done((bf16[256,256]{1,0:T(8,128)(2,1)S(1)}, bf16[256,256]{1,0:T(8,128)(2,1)S(1)}, u32[]{:S(2)}, u32[]{:S(2)}) %collective-permute-start.4) | collective-permute-done | bytes 131104 | tf_op jit(solution)/shard_map/ppermute | solution.py:281
  17.9 0.0 collective-permute-done.3.refs_4_
  17.9 0.0 collective-permute-done.5.refs_6_
  17.9 0.0 collective-permute-done.6.refs_7_
  17.9 3.6 %attend.1 = (bf16[256,256]{1,0:T(8,128)(2,1)S(1)}, bf16[256,256]{1,0:T(8,128)(2,1)S(1)}, bf16[512,256]{1,0:T(8,128)(2,1)S(1)}, bf16[256,256]{1,0:T(8,128)(2,1)S(...) custom-call(s32[1]{0:T(128)S(6)} %copy.8.source_len, ...), custom_call_target="tpu_custom_call" | custom-call | flops 335544320 | bytes 2097152 | tf_op jit(solution)/shard_map/attend/pallas_call | solution.py:329
  21.5 2.7 %collective-permute-start.7 = (bf16[512,256]{1,0:T(8,128)(2,1)S(1)}, bf16[512,256]{1,0:T(8,128)(2,1)S(1)}, u32[]{:S(2)}, u32[]{:S(2)}) collective-permute-start(bf16[512,256]{1,0:T(8,128)(2,1)S(1)} %get-tuple-element.30), channel_id=1, source_target_pairs={{0,18},{1,19},{2,16},{3,17},{16,2},{17,3},{18,0},{19,1},{4,22},{5,... | collective-permute-start | bytes 786440 | tf_op jit(solution)/shard_map/ppermute | solution.py:281
  24.2 0.0 collective-permute-start.8
  24.2 0.5 %collective-permute-start.9 = (bf16[256,256]{1,0:T(8,128)(2,1)S(1)}, bf16[256,256]{1,0:T(8,128)(2,1)S(1)}, u32[]{:S(2)}, u32[]{:S(2)}) collective-permute-start(bf16[256,256]{1,0:T(8,128)(2,1)S(1)} %get-tuple-element.34), channel_id=1, source_target_pairs={{0,16},{1,17},{2,18},{3,19},{16,0},{17,1},{18,2},{19,3},{4,20},{5,... | collective-permute-start | bytes 393224 | tf_op jit(solution)/shard_map/ppermute | solution.py:281
  24.8 0.5 %collective-permute-start.10 = (bf16[256,256]{1,0:T(8,128)(2,1)S(1)}, bf16[256,256]{1,0:T(8,128)(2,1)S(1)}, u32[]{:S(2)}, u32[]{:S(2)}) collective-permute-start(bf16[256,256]{1,0:T(8,128)(2,1)S(1)} %get-tuple-element.35), channel_id=1, source_target_pairs={{0,2},{1,3},{2,0},{3,1},{16,18},{17,19},{18,16},{19,17},{4,6},{5,7... | collective-permute-start | bytes 393224 | tf_op jit(solution)/shard_map/ppermute | solution.py:281
  25.3 1.1 %collective-permute-start.11 = (bf16[256,256]{1,0:T(8,128)(2,1)S(1)}, bf16[256,256]{1,0:T(8,128)(2,1)S(1)}, u32[]{:S(2)}, u32[]{:S(2)}) collective-permute-start(bf16[256,256]{1,0:T(8,128)(2,1)S(1)} %get-tuple-element.36), channel_id=1, source_target_pairs={{0,17},{1,16},{2,19},{3,18},{16,1},{17,0},{18,3},{19,2},{4,21},{5,... | collective-permute-start | bytes 393224 | tf_op jit(solution)/shard_map/ppermute | solution.py:281
  26.4 0.0 collective-permute-done.8.refs_1_
  26.4 1.6 %collective-permute-start.12 = (bf16[256,256]{1,0:T(8,128)(2,1)S(1)}, bf16[256,256]{1,0:T(8,128)(2,1)S(1)}, u32[]{:S(2)}, u32[]{:S(2)}) collective-permute-start(bf16[256,256]{1,0:T(8,128)(2,1)S(1)} %get-tuple-element.37), channel_id=1, source_target_pairs={{0,3},{1,2},{2,1},{3,0},{16,19},{17,18},{18,17},{19,16},{4,7},{5,6... | collective-permute-start | bytes 393224 | tf_op jit(solution)/shard_map/ppermute | solution.py:281
  28.0 3.6 %collective-permute-done.7.refs_2_ = bf16[512,256]{1,0:T(8,128)(2,1)S(1)} collective-permute-done((bf16[512,256]{1,0:T(8,128)(2,1)S(1)}, bf16[512,256]{1,0:T(8,128)(2,1)S(1)}, u32[]{:S(2)}, u32[]{:S(2)}) %collective-permute-start.7) | collective-permute-done | bytes 262176 | tf_op jit(solution)/shard_map/ppermute | solution.py:281
  31.6 0.1 collective-permute-start.13
  31.7 2.3 %collective-permute-done.9.refs_3_ = bf16[256,256]{1,0:T(8,128)(2,1)S(1)} collective-permute-done((bf16[256,256]{1,0:T(8,128)(2,1)S(1)}, bf16[256,256]{1,0:T(8,128)(2,1)S(1)}, u32[]{:S(2)}, u32[]{:S(2)}) %collective-permute-start.9) | collective-permute-done | bytes 131104 | tf_op jit(solution)/shard_map/ppermute | solution.py:281
  34.0 0.7 %collective-permute-done.10.refs_4_ = bf16[256,256]{1,0:T(8,128)(2,1)S(1)} collective-permute-done((bf16[256,256]{1,0:T(8,128)(2,1)S(1)}, bf16[256,256]{1,0:T(8,128)(2,1)S(1)}, u32[]{:S(2)}, u32[]{:S(2)}) %collective-permute-start.10) | collective-permute-done | bytes 131104 | tf_op jit(solution)/shard_map/ppermute | solution.py:281
  34.8 2.0 %collective-permute-done.11.refs_5_ = bf16[256,256]{1,0:T(8,128)(2,1)S(1)} collective-permute-done((bf16[256,256]{1,0:T(8,128)(2,1)S(1)}, bf16[256,256]{1,0:T(8,128)(2,1)S(1)}, u32[]{:S(2)}, u32[]{:S(2)}) %collective-permute-start.11) | collective-permute-done | bytes 131104 | tf_op jit(solution)/shard_map/ppermute | solution.py:281
  36.8 0.0 collective-permute-done.12.refs_6_
  36.8 0.0 collective-permute-done.13.refs_7_
  36.8 1.1 %unpack.1 = (bf16[1,1,128,2048]{3,2,1,0:T(8,128)(2,1)}, bf16[1,1,128,2048]{3,2,1,0:T(8,128)(2,1)}) custom-call(bf16[256,256]{1,0:T(8,128)(2,1)S(1)} %get-tuple-element.29.refs_0_, bf16[256,256]{1,0:T(8,128)(2,1)S(1)} %collective-permute-done.8.refs_1_, bf16[512,256]{1,0:T(8,128)(2,1)S(1)} %collective-permute-done.7.refs_2_, ...), custom_call_target="tpu_custom_call" | custom-call | tf_op jit(solution)/shard_map/unpack/pallas_call | solution.py:341
  (2 shorter events, 0.0 us)
Async XLA Ops:
  2.1 11.1 %collective-permute-start = (bf16[512,256]{1,0:T(8,128)(2,1)S(1)}, bf16[512,256]{1,0:T(8,128)(2,1)S(1)}, u32[]{:S(2)}, u32[]{:S(2)}) collective-permute-start(bf16[512,256]{1,0:T(8,128)(2,1)S(1)} %get-tuple-element.21), channel_id=1, source_target_pairs={{0,18},{1,19},{2,16},{3,17},{16,2},{17,3},{18,0},{19,1},{4,22},{5,... | collective-permute-start | bytes 786440 | tf_op jit(solution)/shard_map/ppermute | solution.py:281
  6.0 2.4 %collective-permute-start.1 = (bf16[272,256]{1,0:T(8,128)(2,1)S(1)}, bf16[272,256]{1,0:T(8,128)(2,1)S(1)}, u32[]{:S(2)}, u32[]{:S(2)}) collective-permute-start(bf16[272,256]{1,0:T(8,128)(2,1)S(1)} %get-tuple-element.22), channel_id=1, source_target_pairs={{0,1},{1,0},{2,3},{3,2},{16,17},{17,16},{18,19},{19,18},{4,5},{5,4... | collective-permute-start | bytes 417800 | tf_op jit(solution)/shard_map/ppermute | solution.py:281
  6.0 11.9 %collective-permute-start.3 = (bf16[272,256]{1,0:T(8,128)(2,1)S(1)}, bf16[272,256]{1,0:T(8,128)(2,1)S(1)}, u32[]{:S(2)}, u32[]{:S(2)}) collective-permute-start(bf16[272,256]{1,0:T(8,128)(2,1)S(1)} %get-tuple-element.26), channel_id=1, source_target_pairs={{0,2},{1,3},{2,0},{3,1},{16,18},{17,19},{18,16},{19,17},{4,6},{5,7... | collective-permute-start | bytes 417800 | tf_op jit(solution)/shard_map/ppermute | solution.py:281
  6.6 11.3 %collective-permute-start.5 = (bf16[272,256]{1,0:T(8,128)(2,1)S(1)}, bf16[272,256]{1,0:T(8,128)(2,1)S(1)}, u32[]{:S(2)}, u32[]{:S(2)}) collective-permute-start(bf16[272,256]{1,0:T(8,128)(2,1)S(1)} %get-tuple-element.28), channel_id=1, source_target_pairs={{0,3},{1,2},{2,1},{3,0},{16,19},{17,18},{18,17},{19,16},{4,7},{5,6... | collective-permute-start | bytes 417800 | tf_op jit(solution)/shard_map/ppermute | solution.py:281
  7.9 7.3 %collective-permute-start.2 = (bf16[256,256]{1,0:T(8,128)(2,1)S(1)}, bf16[256,256]{1,0:T(8,128)(2,1)S(1)}, u32[]{:S(2)}, u32[]{:S(2)}) collective-permute-start(bf16[256,256]{1,0:T(8,128)(2,1)S(1)} %get-tuple-element.25), channel_id=1, source_target_pairs={{0,16},{1,17},{2,18},{3,19},{16,0},{17,1},{18,2},{19,3},{4,20},{5,... | collective-permute-start | bytes 393224 | tf_op jit(solution)/shard_map/ppermute | solution.py:281
  8.4 9.5 %collective-permute-start.4 = (bf16[256,256]{1,0:T(8,128)(2,1)S(1)}, bf16[256,256]{1,0:T(8,128)(2,1)S(1)}, u32[]{:S(2)}, u32[]{:S(2)}) collective-permute-start(bf16[256,256]{1,0:T(8,128)(2,1)S(1)} %get-tuple-element.27), channel_id=1, source_target_pairs={{0,17},{1,16},{2,19},{3,18},{16,1},{17,0},{18,3},{19,2},{4,21},{5,... | collective-permute-start | bytes 393224 | tf_op jit(solution)/shard_map/ppermute | solution.py:281
  13.2 4.7 %collective-permute-start.6 = (bf16[256,256]{1,0:T(8,128)(2,1)S(1)}, bf16[256,256]{1,0:T(8,128)(2,1)S(1)}, u32[]{:S(2)}, u32[]{:S(2)}) collective-permute-start(bf16[256,256]{1,0:T(8,128)(2,1)S(1)} %slice.6), channel_id=1, source_target_pairs={{0,1},{1,0},{2,3},{3,2},{16,17},{17,16},{18,19},{19,18},{4,5},{5,4... | collective-permute-start | bytes 393224 | tf_op jit(solution)/shard_map/ppermute | solution.py:281
  21.5 10.1 %collective-permute-start.7 = (bf16[512,256]{1,0:T(8,128)(2,1)S(1)}, bf16[512,256]{1,0:T(8,128)(2,1)S(1)}, u32[]{:S(2)}, u32[]{:S(2)}) collective-permute-start(bf16[512,256]{1,0:T(8,128)(2,1)S(1)} %get-tuple-element.30), channel_id=1, source_target_pairs={{0,18},{1,19},{2,16},{3,17},{16,2},{17,3},{18,0},{19,1},{4,22},{5,... | collective-permute-start | bytes 786440 | tf_op jit(solution)/shard_map/ppermute | solution.py:281
  24.2 2.1 %collective-permute-start.8 = (bf16[256,256]{1,0:T(8,128)(2,1)S(1)}, bf16[256,256]{1,0:T(8,128)(2,1)S(1)}, u32[]{:S(2)}, u32[]{:S(2)}) collective-permute-start(bf16[256,256]{1,0:T(8,128)(2,1)S(1)} %get-tuple-element.31), channel_id=1, source_target_pairs={{0,1},{1,0},{2,3},{3,2},{16,17},{17,16},{18,19},{19,18},{4,5},{5,4... | collective-permute-start | bytes 393224 | tf_op jit(solution)/shard_map/ppermute | solution.py:281
  24.2 9.8 %collective-permute-start.9 = (bf16[256,256]{1,0:T(8,128)(2,1)S(1)}, bf16[256,256]{1,0:T(8,128)(2,1)S(1)}, u32[]{:S(2)}, u32[]{:S(2)}) collective-permute-start(bf16[256,256]{1,0:T(8,128)(2,1)S(1)} %get-tuple-element.34), channel_id=1, source_target_pairs={{0,16},{1,17},{2,18},{3,19},{16,0},{17,1},{18,2},{19,3},{4,20},{5,... | collective-permute-start | bytes 393224 | tf_op jit(solution)/shard_map/ppermute | solution.py:281
  24.8 10.0 %collective-permute-start.10 = (bf16[256,256]{1,0:T(8,128)(2,1)S(1)}, bf16[256,256]{1,0:T(8,128)(2,1)S(1)}, u32[]{:S(2)}, u32[]{:S(2)}) collective-permute-start(bf16[256,256]{1,0:T(8,128)(2,1)S(1)} %get-tuple-element.35), channel_id=1, source_target_pairs={{0,2},{1,3},{2,0},{3,1},{16,18},{17,19},{18,16},{19,17},{4,6},{5,7... | collective-permute-start | bytes 393224 | tf_op jit(solution)/shard_map/ppermute | solution.py:281
  25.3 11.5 %collective-permute-start.11 = (bf16[256,256]{1,0:T(8,128)(2,1)S(1)}, bf16[256,256]{1,0:T(8,128)(2,1)S(1)}, u32[]{:S(2)}, u32[]{:S(2)}) collective-permute-start(bf16[256,256]{1,0:T(8,128)(2,1)S(1)} %get-tuple-element.36), channel_id=1, source_target_pairs={{0,17},{1,16},{2,19},{3,18},{16,1},{17,0},{18,3},{19,2},{4,21},{5,... | collective-permute-start | bytes 393224 | tf_op jit(solution)/shard_map/ppermute | solution.py:281
  26.4 10.4 %collective-permute-start.12 = (bf16[256,256]{1,0:T(8,128)(2,1)S(1)}, bf16[256,256]{1,0:T(8,128)(2,1)S(1)}, u32[]{:S(2)}, u32[]{:S(2)}) collective-permute-start(bf16[256,256]{1,0:T(8,128)(2,1)S(1)} %get-tuple-element.37), channel_id=1, source_target_pairs={{0,3},{1,2},{2,1},{3,0},{16,19},{17,18},{18,17},{19,16},{4,7},{5,6... | collective-permute-start | bytes 393224 | tf_op jit(solution)/shard_map/ppermute | solution.py:281
  31.6 5.1 %collective-permute-start.13 = (bf16[256,256]{1,0:T(8,128)(2,1)S(1)}, bf16[256,256]{1,0:T(8,128)(2,1)S(1)}, u32[]{:S(2)}, u32[]{:S(2)}) collective-permute-start(bf16[256,256]{1,0:T(8,128)(2,1)S(1)} %slice.7), channel_id=1, source_target_pairs={{0,1},{1,0},{2,3},{3,2},{16,17},{17,16},{18,19},{19,18},{4,5},{5,4... | collective-permute-start | bytes 393224 | tf_op jit(solution)/shard_map/ppermute | solution.py:281

commit v18 on v17

--- a/solution.py
+++ b/solution.py
@@ -173,7 +173,8 @@
     return lax.axis_index("section") * seq_count + lax.axis_index("seq")
 
 
-OUTGOING = [(0,), (1,), (6, 7), (4,), (2,), (5,), (3,)]
+DIAGONAL = (6, 7)
+OUTGOING = [(0,), (1,), DIAGONAL, (4,), (2,), (5,), (3,)]
 INCOMING = [*OUTGOING, (7,)]
 
 
@@ -284,8 +285,8 @@
         group: move(share, group[0]) if group[0] else share
         for group, share in zip(OUTGOING, shares)
     }
-    moved[(6, 7)], moved[(1,)] = lax.optimization_barrier((moved[(6, 7)], moved[(1,)]))
-    moved[(7,)] = move(moved[(6, 7)][2 * BLK :], 1)
+    moved[DIAGONAL], moved[(1,)] = lax.optimization_barrier((moved[DIAGONAL], moved[(1,)]))
+    moved[(7,)] = move(moved[DIAGONAL][2 * BLK :], 1)
     return [moved[group] for group in INCOMING]
 
 
@@ -322,7 +323,11 @@
             name="pack",
         )(*in_hbm(lists, diffusion_mask, first_rows, second_rows))
 
-    shares = swapped(pack(OUTGOING, alignment))
+    rest = [group for group in OUTGOING if group != DIAGONAL]
+    (diagonal,) = pack([DIAGONAL], alignment)
+    lists, diagonal = lax.optimization_barrier((alignment, diagonal))
+    shares = {DIAGONAL: diagonal, **dict(zip(rest, pack(rest, lists)))}
+    shares = swapped([shares[group] for group in OUTGOING])
     rows = pltpu.VMEM((parts, 2, BLK, share), kind)
     grads = pltpu.VMEM((seq_count, BLK, share), jnp.float32)
     turned = pltpu.VMEM((seq_count, 2, share, BLK), kind)

time: 38.1 us -> 37.8 us (level)
  waiting for transfers between devices: 15.6 us -> 14.3 us
  Pallas kernels: 6.13 us -> 7.14 us
    ppermute x14, waiting for transfers between devices: 15.6 us -> 14.3 us  [move(): lax.ppermute(share, AXES, [(dev, dev ^ step) for dev in range(parts)])]
    pallas_call x1 -> x2, Pallas kernels: 1.43 us -> 2.44 us  [pack(): pl.pallas_call(functools.partial(pack_kernel, seq_count, groups), out_sha...]
  transfers between devices with their start and end apart: 14 -> 14, of which waited for: 7 -> 7; matrix products, arithmetic and copies ran while one was open for 0% -> 0% of each run, Pallas kernels for 0% -> 4%
where the time goes in v18:
time: 37.8 us; the launch traced here: 37.5 us
  waiting for transfers between devices  14.3 us (38%)
  starting transfers between devices  14.1 us (37%)
  Pallas kernels  7.14 us (19%)
  between operations  1.99 us (5%)
    ppermute x14, waiting for transfers between devices, move(): lax.ppermute(share, AXES, [(dev, dev ^ step) for dev in range(parts)])  14.3 us
    ppermute x14, starting transfers between devices, move(): lax.ppermute(share, AXES, [(dev, dev ^ step) for dev in range(parts)])  14.1 us
    pallas_call x1, Pallas kernels, by_pairs(): pl.pallas_call(functools.partial(attend_kernel, seq_count, INCOMING), out...  3.61 us
    pallas_call x2, Pallas kernels, pack(): pl.pallas_call(functools.partial(pack_kernel, seq_count, groups), out_sha...  2.44 us
    pallas_call x1, Pallas kernels, by_pairs(): pl.pallas_call(functools.partial(unpack_kernel, seq_count, INCOMING), out...  1.09 us
  transfers between devices with their start and end apart: 14, of which 7 were waited for; matrix products, arithmetic and copies ran while one was open for 0% of the time, Pallas kernels for 4%

profile of v18, /device:TPU:0, one launch (start us, length us, event | category | flops | bytes accessed | tf_op | source)
XLA Modules:
  0.0 37.5 jit_solution(2247725095468539589)
XLA Ops:
  0.6 1.1 %pack.2 = bf16[512,256]{1,0:T(8,128)(2,1)S(1)} custom-call(s32[1,1,2]{2,1,0:T(1,128)} %refs_0_.2, s32[1,128]{1,0:T(1,128)} %refs_1_.3, bf16[1,1,128,2048]{3,2,1,0:T(8,128)(2,1)} %refs_2_.3, bf16[1,1,128,2048]{3,2,1,0:T(8,128)(2,1)} %refs_3_.3), custom_call_target="tpu_custom_call" | custom-call | tf_op jit(solution)/shard_map/pack/pallas_call | solution.py:311
  1.8 4.0 %collective-permute-start = (bf16[512,256]{1,0:T(8,128)(2,1)S(1)}, bf16[512,256]{1,0:T(8,128)(2,1)S(1)}, u32[]{:S(2)}, u32[]{:S(2)}) collective-permute-start(bf16[512,256]{1,0:T(8,128)(2,1)S(1)} %pack.2), channel_id=1, source_target_pairs={{0,18},{1,19},{2,16},{3,17},{16,2},{17,3},{18,0},{19,1},{4,22},{5,... | collective-permute-start | bytes 786440 | tf_op jit(solution)/shard_map/ppermute | solution.py:282
  5.7 1.3 %pack.3 = (bf16[272,256]{1,0:T(8,128)(2,1)S(1)}, bf16[272,256]{1,0:T(8,128)(2,1)S(1)}, bf16[256,256]{1,0:T(8,128)(2,1)S(1)}, bf16[272,256]{1,0:T(8,128)(2,1)S(1)...) custom-call(s32[1,1,2]{2,1,0:T(1,128)} %refs_0_.2, s32[1,128]{1,0:T(1,128)} %refs_1_.3, ...), custom_call_target="tpu_custom_call" | custom-call | tf_op jit(solution)/shard_map/pack/pallas_call | solution.py:311
  7.0 0.1 collective-permute-start.1
  7.1 0.6 %collective-permute-start.3 = (bf16[272,256]{1,0:T(8,128)(2,1)S(1)}, bf16[272,256]{1,0:T(8,128)(2,1)S(1)}, u32[]{:S(2)}, u32[]{:S(2)}) collective-permute-start(bf16[272,256]{1,0:T(8,128)(2,1)S(1)} %get-tuple-element.28), channel_id=1, source_target_pairs={{0,2},{1,3},{2,0},{3,1},{16,18},{17,19},{18,16},{19,17},{4,6},{5,7... | collective-permute-start | bytes 417800 | tf_op jit(solution)/shard_map/ppermute | solution.py:282
  7.7 1.3 %collective-permute-start.5 = (bf16[272,256]{1,0:T(8,128)(2,1)S(1)}, bf16[272,256]{1,0:T(8,128)(2,1)S(1)}, u32[]{:S(2)}, u32[]{:S(2)}) collective-permute-start(bf16[272,256]{1,0:T(8,128)(2,1)S(1)} %get-tuple-element.30), channel_id=1, source_target_pairs={{0,3},{1,2},{2,1},{3,0},{16,19},{17,18},{18,17},{19,16},{4,7},{5,6... | collective-permute-start | bytes 417800 | tf_op jit(solution)/shard_map/ppermute | solution.py:282
  9.0 0.5 %collective-permute-start.2 = (bf16[256,256]{1,0:T(8,128)(2,1)S(1)}, bf16[256,256]{1,0:T(8,128)(2,1)S(1)}, u32[]{:S(2)}, u32[]{:S(2)}) collective-permute-start(bf16[256,256]{1,0:T(8,128)(2,1)S(1)} %get-tuple-element.27), channel_id=1, source_target_pairs={{0,16},{1,17},{2,18},{3,19},{16,0},{17,1},{18,2},{19,3},{4,20},{5,... | collective-permute-start | bytes 393224 | tf_op jit(solution)/shard_map/ppermute | solution.py:282
  9.5 0.0 collective-permute-done.1.refs_1_
  9.5 1.2 %collective-permute-start.4 = (bf16[256,256]{1,0:T(8,128)(2,1)S(1)}, bf16[256,256]{1,0:T(8,128)(2,1)S(1)}, u32[]{:S(2)}, u32[]{:S(2)}) collective-permute-start(bf16[256,256]{1,0:T(8,128)(2,1)S(1)} %get-tuple-element.29), channel_id=1, source_target_pairs={{0,17},{1,16},{2,19},{3,18},{16,1},{17,0},{18,3},{19,2},{4,21},{5,... | collective-permute-start | bytes 393224 | tf_op jit(solution)/shard_map/ppermute | solution.py:282
  10.7 2.2 %collective-permute-done.refs_2_ = bf16[512,256]{1,0:T(8,128)(2,1)S(1)} collective-permute-done((bf16[512,256]{1,0:T(8,128)(2,1)S(1)}, bf16[512,256]{1,0:T(8,128)(2,1)S(1)}, u32[]{:S(2)}, u32[]{:S(2)}) %collective-permute-start) | collective-permute-done | bytes 262176 | tf_op jit(solution)/shard_map/ppermute | solution.py:282
  12.9 0.1 collective-permute-start.6
  14.2 1.3 %collective-permute-done.2.refs_3_ = bf16[256,256]{1,0:T(8,128)(2,1)S(1)} collective-permute-done((bf16[256,256]{1,0:T(8,128)(2,1)S(1)}, bf16[256,256]{1,0:T(8,128)(2,1)S(1)}, u32[]{:S(2)}, u32[]{:S(2)}) %collective-permute-start.2) | collective-permute-done | bytes 131104 | tf_op jit(solution)/shard_map/ppermute | solution.py:282
  15.5 2.2 %collective-permute-done.4.refs_5_ = bf16[256,256]{1,0:T(8,128)(2,1)S(1)} collective-permute-done((bf16[256,256]{1,0:T(8,128)(2,1)S(1)}, bf16[256,256]{1,0:T(8,128)(2,1)S(1)}, u32[]{:S(2)}, u32[]{:S(2)}) %collective-permute-start.4) | collective-permute-done | bytes 131104 | tf_op jit(solution)/shard_map/ppermute | solution.py:282
  17.7 0.0 collective-permute-done.3.refs_4_
  17.7 0.0 collective-permute-done.5.refs_6_
  17.7 0.0 collective-permute-done.6.refs_7_
  17.7 3.6 %attend.1 = (bf16[256,256]{1,0:T(8,128)(2,1)S(1)}, bf16[256,256]{1,0:T(8,128)(2,1)S(1)}, bf16[512,256]{1,0:T(8,128)(2,1)S(1)}, bf16[256,256]{1,0:T(8,128)(2,1)S(...) custom-call(s32[1]{0:T(128)S(6)} %copy.8.source_len, ...), custom_call_target="tpu_custom_call" | custom-call | flops 335544320 | bytes 2097152 | tf_op jit(solution)/shard_map/attend/pallas_call | solution.py:334
  21.3 2.6 %collective-permute-start.7 = (bf16[512,256]{1,0:T(8,128)(2,1)S(1)}, bf16[512,256]{1,0:T(8,128)(2,1)S(1)}, u32[]{:S(2)}, u32[]{:S(2)}) collective-permute-start(bf16[512,256]{1,0:T(8,128)(2,1)S(1)} %get-tuple-element.32), channel_id=1, source_target_pairs={{0,18},{1,19},{2,16},{3,17},{16,2},{17,3},{18,0},{19,1},{4,22},{5,... | collective-permute-start | bytes 786440 | tf_op jit(solution)/shard_map/ppermute | solution.py:282
  23.9 0.0 collective-permute-start.8
  23.9 0.5 %collective-permute-start.9 = (bf16[256,256]{1,0:T(8,128)(2,1)S(1)}, bf16[256,256]{1,0:T(8,128)(2,1)S(1)}, u32[]{:S(2)}, u32[]{:S(2)}) collective-permute-start(bf16[256,256]{1,0:T(8,128)(2,1)S(1)} %get-tuple-element.36), channel_id=1, source_target_pairs={{0,16},{1,17},{2,18},{3,19},{16,0},{17,1},{18,2},{19,3},{4,20},{5,... | collective-permute-start | bytes 393224 | tf_op jit(solution)/shard_map/ppermute | solution.py:282
  24.4 0.5 %collective-permute-start.10 = (bf16[256,256]{1,0:T(8,128)(2,1)S(1)}, bf16[256,256]{1,0:T(8,128)(2,1)S(1)}, u32[]{:S(2)}, u32[]{:S(2)}) collective-permute-start(bf16[256,256]{1,0:T(8,128)(2,1)S(1)} %get-tuple-element.37), channel_id=1, source_target_pairs={{0,2},{1,3},{2,0},{3,1},{16,18},{17,19},{18,16},{19,17},{4,6},{5,7... | collective-permute-start | bytes 393224 | tf_op jit(solution)/shard_map/ppermute | solution.py:282
  25.0 0.9 %collective-permute-start.11 = (bf16[256,256]{1,0:T(8,128)(2,1)S(1)}, bf16[256,256]{1,0:T(8,128)(2,1)S(1)}, u32[]{:S(2)}, u32[]{:S(2)}) collective-permute-start(bf16[256,256]{1,0:T(8,128)(2,1)S(1)} %get-tuple-element.38), channel_id=1, source_target_pairs={{0,17},{1,16},{2,19},{3,18},{16,1},{17,0},{18,3},{19,2},{4,21},{5,... | collective-permute-start | bytes 393224 | tf_op jit(solution)/shard_map/ppermute | solution.py:282
  25.8 0.0 collective-permute-done.8.refs_1_
  25.9 1.8 %collective-permute-start.12 = (bf16[256,256]{1,0:T(8,128)(2,1)S(1)}, bf16[256,256]{1,0:T(8,128)(2,1)S(1)}, u32[]{:S(2)}, u32[]{:S(2)}) collective-permute-start(bf16[256,256]{1,0:T(8,128)(2,1)S(1)} %get-tuple-element.39), channel_id=1, source_target_pairs={{0,3},{1,2},{2,1},{3,0},{16,19},{17,18},{18,17},{19,16},{4,7},{5,6... | collective-permute-start | bytes 393224 | tf_op jit(solution)/shard_map/ppermute | solution.py:282
  27.7 3.8 %collective-permute-done.7.refs_2_ = bf16[512,256]{1,0:T(8,128)(2,1)S(1)} collective-permute-done((bf16[512,256]{1,0:T(8,128)(2,1)S(1)}, bf16[512,256]{1,0:T(8,128)(2,1)S(1)}, u32[]{:S(2)}, u32[]{:S(2)}) %collective-permute-start.7) | collective-permute-done | bytes 262176 | tf_op jit(solution)/shard_map/ppermute | solution.py:282
  31.5 0.1 collective-permute-start.13
  31.6 2.1 %collective-permute-done.9.refs_3_ = bf16[256,256]{1,0:T(8,128)(2,1)S(1)} collective-permute-done((bf16[256,256]{1,0:T(8,128)(2,1)S(1)}, bf16[256,256]{1,0:T(8,128)(2,1)S(1)}, u32[]{:S(2)}, u32[]{:S(2)}) %collective-permute-start.9) | collective-permute-done | bytes 131104 | tf_op jit(solution)/shard_map/ppermute | solution.py:282
  33.7 0.5 %collective-permute-done.10.refs_4_ = bf16[256,256]{1,0:T(8,128)(2,1)S(1)} collective-permute-done((bf16[256,256]{1,0:T(8,128)(2,1)S(1)}, bf16[256,256]{1,0:T(8,128)(2,1)S(1)}, u32[]{:S(2)}, u32[]{:S(2)}) %collective-permute-start.10) | collective-permute-done | bytes 131104 | tf_op jit(solution)/shard_map/ppermute | solution.py:282
  34.2 2.2 %collective-permute-done.11.refs_5_ = bf16[256,256]{1,0:T(8,128)(2,1)S(1)} collective-permute-done((bf16[256,256]{1,0:T(8,128)(2,1)S(1)}, bf16[256,256]{1,0:T(8,128)(2,1)S(1)}, u32[]{:S(2)}, u32[]{:S(2)}) %collective-permute-start.11) | collective-permute-done | bytes 131104 | tf_op jit(solution)/shard_map/ppermute | solution.py:282
  36.4 0.0 collective-permute-done.12.refs_6_
  36.4 0.0 collective-permute-done.13.refs_7_
  36.4 1.1 %unpack.1 = (bf16[1,1,128,2048]{3,2,1,0:T(8,128)(2,1)}, bf16[1,1,128,2048]{3,2,1,0:T(8,128)(2,1)}) custom-call(bf16[256,256]{1,0:T(8,128)(2,1)S(1)} %get-tuple-element.31.refs_0_, bf16[256,256]{1,0:T(8,128)(2,1)S(1)} %collective-permute-done.8.refs_1_, bf16[512,256]{1,0:T(8,128)(2,1)S(1)} %collective-permute-done.7.refs_2_, ...), custom_call_target="tpu_custom_call" | custom-call | tf_op jit(solution)/shard_map/unpack/pallas_call | solution.py:346
  (2 shorter events, 0.0 us)
Async XLA Ops:
  1.8 11.1 %collective-permute-start = (bf16[512,256]{1,0:T(8,128)(2,1)S(1)}, bf16[512,256]{1,0:T(8,128)(2,1)S(1)}, u32[]{:S(2)}, u32[]{:S(2)}) collective-permute-start(bf16[512,256]{1,0:T(8,128)(2,1)S(1)} %pack.2), channel_id=1, source_target_pairs={{0,18},{1,19},{2,16},{3,17},{16,2},{17,3},{18,0},{19,1},{4,22},{5,... | collective-permute-start | bytes 786440 | tf_op jit(solution)/shard_map/ppermute | solution.py:282
  7.0 2.5 %collective-permute-start.1 = (bf16[272,256]{1,0:T(8,128)(2,1)S(1)}, bf16[272,256]{1,0:T(8,128)(2,1)S(1)}, u32[]{:S(2)}, u32[]{:S(2)}) collective-permute-start(bf16[272,256]{1,0:T(8,128)(2,1)S(1)} %get-tuple-element.24), channel_id=1, source_target_pairs={{0,1},{1,0},{2,3},{3,2},{16,17},{17,16},{18,19},{19,18},{4,5},{5,4... | collective-permute-start | bytes 417800 | tf_op jit(solution)/shard_map/ppermute | solution.py:282
  7.1 10.6 %collective-permute-start.3 = (bf16[272,256]{1,0:T(8,128)(2,1)S(1)}, bf16[272,256]{1,0:T(8,128)(2,1)S(1)}, u32[]{:S(2)}, u32[]{:S(2)}) collective-permute-start(bf16[272,256]{1,0:T(8,128)(2,1)S(1)} %get-tuple-element.28), channel_id=1, source_target_pairs={{0,2},{1,3},{2,0},{3,1},{16,18},{17,19},{18,16},{19,17},{4,6},{5,7... | collective-permute-start | bytes 417800 | tf_op jit(solution)/shard_map/ppermute | solution.py:282
  7.7 10.0 %collective-permute-start.5 = (bf16[272,256]{1,0:T(8,128)(2,1)S(1)}, bf16[272,256]{1,0:T(8,128)(2,1)S(1)}, u32[]{:S(2)}, u32[]{:S(2)}) collective-permute-start(bf16[272,256]{1,0:T(8,128)(2,1)S(1)} %get-tuple-element.30), channel_id=1, source_target_pairs={{0,3},{1,2},{2,1},{3,0},{16,19},{17,18},{18,17},{19,16},{4,7},{5,6... | collective-permute-start | bytes 417800 | tf_op jit(solution)/shard_map/ppermute | solution.py:282
  9.0 6.5 %collective-permute-start.2 = (bf16[256,256]{1,0:T(8,128)(2,1)S(1)}, bf16[256,256]{1,0:T(8,128)(2,1)S(1)}, u32[]{:S(2)}, u32[]{:S(2)}) collective-permute-start(bf16[256,256]{1,0:T(8,128)(2,1)S(1)} %get-tuple-element.27), channel_id=1, source_target_pairs={{0,16},{1,17},{2,18},{3,19},{16,0},{17,1},{18,2},{19,3},{4,20},{5,... | collective-permute-start | bytes 393224 | tf_op jit(solution)/shard_map/ppermute | solution.py:282
  9.5 8.2 %collective-permute-start.4 = (bf16[256,256]{1,0:T(8,128)(2,1)S(1)}, bf16[256,256]{1,0:T(8,128)(2,1)S(1)}, u32[]{:S(2)}, u32[]{:S(2)}) collective-permute-start(bf16[256,256]{1,0:T(8,128)(2,1)S(1)} %get-tuple-element.29), channel_id=1, source_target_pairs={{0,17},{1,16},{2,19},{3,18},{16,1},{17,0},{18,3},{19,2},{4,21},{5,... | collective-permute-start | bytes 393224 | tf_op jit(solution)/shard_map/ppermute | solution.py:282
  12.9 4.8 %collective-permute-start.6 = (bf16[256,256]{1,0:T(8,128)(2,1)S(1)}, bf16[256,256]{1,0:T(8,128)(2,1)S(1)}, u32[]{:S(2)}, u32[]{:S(2)}) collective-permute-start(bf16[256,256]{1,0:T(8,128)(2,1)S(1)} %slice.6), channel_id=1, source_target_pairs={{0,1},{1,0},{2,3},{3,2},{16,17},{17,16},{18,19},{19,18},{4,5},{5,4... | collective-permute-start | bytes 393224 | tf_op jit(solution)/shard_map/ppermute | solution.py:282
  21.3 10.1 %collective-permute-start.7 = (bf16[512,256]{1,0:T(8,128)(2,1)S(1)}, bf16[512,256]{1,0:T(8,128)(2,1)S(1)}, u32[]{:S(2)}, u32[]{:S(2)}) collective-permute-start(bf16[512,256]{1,0:T(8,128)(2,1)S(1)} %get-tuple-element.32), channel_id=1, source_target_pairs={{0,18},{1,19},{2,16},{3,17},{16,2},{17,3},{18,0},{19,1},{4,22},{5,... | collective-permute-start | bytes 786440 | tf_op jit(solution)/shard_map/ppermute | solution.py:282
  23.9 1.9 %collective-permute-start.8 = (bf16[256,256]{1,0:T(8,128)(2,1)S(1)}, bf16[256,256]{1,0:T(8,128)(2,1)S(1)}, u32[]{:S(2)}, u32[]{:S(2)}) collective-permute-start(bf16[256,256]{1,0:T(8,128)(2,1)S(1)} %get-tuple-element.33), channel_id=1, source_target_pairs={{0,1},{1,0},{2,3},{3,2},{16,17},{17,16},{18,19},{19,18},{4,5},{5,4... | collective-permute-start | bytes 393224 | tf_op jit(solution)/shard_map/ppermute | solution.py:282
  23.9 9.8 %collective-permute-start.9 = (bf16[256,256]{1,0:T(8,128)(2,1)S(1)}, bf16[256,256]{1,0:T(8,128)(2,1)S(1)}, u32[]{:S(2)}, u32[]{:S(2)}) collective-permute-start(bf16[256,256]{1,0:T(8,128)(2,1)S(1)} %get-tuple-element.36), channel_id=1, source_target_pairs={{0,16},{1,17},{2,18},{3,19},{16,0},{17,1},{18,2},{19,3},{4,20},{5,... | collective-permute-start | bytes 393224 | tf_op jit(solution)/shard_map/ppermute | solution.py:282
  24.4 9.8 %collective-permute-start.10 = (bf16[256,256]{1,0:T(8,128)(2,1)S(1)}, bf16[256,256]{1,0:T(8,128)(2,1)S(1)}, u32[]{:S(2)}, u32[]{:S(2)}) collective-permute-start(bf16[256,256]{1,0:T(8,128)(2,1)S(1)} %get-tuple-element.37), channel_id=1, source_target_pairs={{0,2},{1,3},{2,0},{3,1},{16,18},{17,19},{18,16},{19,17},{4,6},{5,7... | collective-permute-start | bytes 393224 | tf_op jit(solution)/shard_map/ppermute | solution.py:282
  25.0 11.5 %collective-permute-start.11 = (bf16[256,256]{1,0:T(8,128)(2,1)S(1)}, bf16[256,256]{1,0:T(8,128)(2,1)S(1)}, u32[]{:S(2)}, u32[]{:S(2)}) collective-permute-start(bf16[256,256]{1,0:T(8,128)(2,1)S(1)} %get-tuple-element.38), channel_id=1, source_target_pairs={{0,17},{1,16},{2,19},{3,18},{16,1},{17,0},{18,3},{19,2},{4,21},{5,... | collective-permute-start | bytes 393224 | tf_op jit(solution)/shard_map/ppermute | solution.py:282
  25.9 10.6 %collective-permute-start.12 = (bf16[256,256]{1,0:T(8,128)(2,1)S(1)}, bf16[256,256]{1,0:T(8,128)(2,1)S(1)}, u32[]{:S(2)}, u32[]{:S(2)}) collective-permute-start(bf16[256,256]{1,0:T(8,128)(2,1)S(1)} %get-tuple-element.39), channel_id=1, source_target_pairs={{0,3},{1,2},{2,1},{3,0},{16,19},{17,18},{18,17},{19,16},{4,7},{5,6... | collective-permute-start | bytes 393224 | tf_op jit(solution)/shard_map/ppermute | solution.py:282
  31.5 5.0 %collective-permute-start.13 = (bf16[256,256]{1,0:T(8,128)(2,1)S(1)}, bf16[256,256]{1,0:T(8,128)(2,1)S(1)}, u32[]{:S(2)}, u32[]{:S(2)}) collective-permute-start(bf16[256,256]{1,0:T(8,128)(2,1)S(1)} %slice.7), channel_id=1, source_target_pairs={{0,1},{1,0},{2,3},{3,2},{16,17},{17,16},{18,19},{19,18},{4,5},{5,4... | collective-permute-start | bytes 393224 | tf_op jit(solution)/shard_map/ppermute | solution.py:282

commit v19 on v18

--- a/solution.py
+++ b/solution.py
@@ -174,8 +174,11 @@
 
 
 DIAGONAL = (6, 7)
-OUTGOING = [(0,), (1,), DIAGONAL, (4,), (2,), (5,), (3,)]
-INCOMING = [*OUTGOING, (7,)]
+REST = [(0,), (1,), (4,), (2,), (5,), (3,)]
+OUTGOING = [DIAGONAL, *REST]
+INCOMING = [*OUTGOING, DIAGONAL[1:]]
+TILES = 2
+AFTER = REST.index((1,))
 
 
 def pack_kernel(seq_count, steps, *refs):
@@ -223,18 +226,20 @@
         piece[BLK:] = piece[BLK:] * keep
 
 
-def attend_kernel(seq_count, order, source_len, target_len, *refs):
-    count = len(order)
-    shares, outs = refs[:count], refs[count : 2 * count - 1]
-    rows, result, key_grad, value_grad, turned, lists = refs[2 * count - 1 :]
+def attend_kernel(seq_count, turn, source_len, target_len, *refs):
+    parts, rest = len(INCOMING), len(OUTGOING) - 1
+    shares, before = refs[:parts], refs[parts : parts + (rest if turn else 0)]
+    outs = refs[parts + len(before) : parts + len(before) + 1 + rest]
+    rows, result, key_grad, value_grad, turned, lists = refs[parts + len(before) + 1 + rest :]
     me = device_index(seq_count)
     here = me % seq_count
-    for (step, *_), share in zip(order, shares):
+    lanes = pl.ds(turn * LANES, LANES)
+    for (step, *_), share in zip(INCOMING, shares):
         source = me ^ step
-        rows[source, 0] = share[:BLK]
-        rows[source, 1] = share[BLK : 2 * BLK]
+        rows[source, 0] = share[pl.ds(0, BLK), lanes]
+        rows[source, 1] = share[pl.ds(BLK, BLK), lanes]
         if step < seq_count:
-            tail = share[2 * BLK :, :LANES].astype(jnp.float32)
+            tail = share[pl.ds(2 * BLK, TAIL), lanes].astype(jnp.float32)
             lists[here ^ step] = jnp.max(tail).astype(jnp.int32)
 
     def listed(block, slot):
@@ -252,19 +257,30 @@
         value_grad,
         turned,
     )
-    for group, out in zip(OUTGOING, outs):
-        for place, step in enumerate(group):
-            out[2 * place * BLK : (2 * place + 1) * BLK] = result[me ^ step, 0]
-            out[(2 * place + 1) * BLK : (2 * place + 2) * BLK] = result[me ^ step, 1]
-
-
-def unpack_kernel(seq_count, steps, *refs):
-    shares, (first, second, sem) = refs[: len(steps)], refs[-3:]
-    width = shares[0].shape[1]
+    diagonal, *others = outs
+    for place, step in enumerate(DIAGONAL):
+        for half in range(2):
+            diagonal[pl.ds((2 * place + half) * BLK, BLK)] = result[me ^ step, half]
+    for group, out in zip(REST, others):
+        for half in range(2):
+            out[pl.ds(half * BLK, BLK), lanes] = result[me ^ group[0], half]
+    for done, out in zip(before, others):
+        out[:, pl.ds(0, turn * LANES)] = done[...]
+
+
+def unpack_kernel(seq_count, *refs):
+    diagonals, shares = refs[:TILES], refs[TILES : TILES + len(REST) + 1]
+    first, second, sem = refs[-3:]
+    width = first.shape[3] // (2 * seq_count)
     me = device_index(seq_count)
+    pieces = [
+        (DIAGONAL[0], tile * LANES, share.at[pl.ds(0, 2 * BLK)])
+        for tile, share in enumerate(diagonals)
+    ]
+    pieces += [(group[0], 0, share) for group, share in zip([*REST, DIAGONAL[1:]], shares)]
     copies = []
-    for slot, ((step, *_), share) in enumerate(zip(steps, shares)):
-        lanes = pl.ds(pl.multiple_of((me ^ step) * width, LANES), width)
+    for slot, (step, start, share) in enumerate(pieces):
+        lanes = pl.ds(pl.multiple_of((me ^ step) * width + start, LANES), share.shape[1])
         for half, result in enumerate((first, second)):
             copy = pltpu.make_async_copy(
                 share.at[pl.ds(half * BLK, BLK)], result.at[0, 0, :, lanes], sem.at[half, slot]
@@ -275,19 +291,19 @@
         copy.wait()
 
 
-def swapped(shares):
-    parts = 8
-
-    def move(share, step):
-        return lax.ppermute(share, AXES, [(dev, dev ^ step) for dev in range(parts)])
-
-    moved = {
-        group: move(share, group[0]) if group[0] else share
-        for group, share in zip(OUTGOING, shares)
-    }
-    moved[DIAGONAL], moved[(1,)] = lax.optimization_barrier((moved[DIAGONAL], moved[(1,)]))
-    moved[(7,)] = move(moved[DIAGONAL][2 * BLK :], 1)
-    return [moved[group] for group in INCOMING]
+def permuted(share, step):
+    return lax.ppermute(share, AXES, [(dev, dev ^ step) for dev in range(8)])
+
+
+def swapped(diagonals, shares):
+    diagonals, shares = [permuted(share, DIAGONAL[0]) for share in diagonals], list(shares)
+    for share in diagonals[:-1]:
+        shares[AFTER], diagonals[0] = lax.optimization_barrier((shares[AFTER], diagonals[0]))
+    shares = [permuted(share, step) if step else share for (step,), share in zip(REST, shares)]
+    near = REST.index((1,))
+    diagonals[-1], shares[near] = lax.optimization_barrier((diagonals[-1], shares[near]))
+    handed_on = [share[share.shape[0] // 2 :] for share in diagonals]
+    return diagonals, shares, permuted(jnp.concatenate(handed_on, axis=1), 1)
 
 
 def by_pairs(first_rows, second_rows, alignment, diffusion_mask, source_length, target_length):
@@ -323,35 +339,45 @@
             name="pack",
         )(*in_hbm(lists, diffusion_mask, first_rows, second_rows))
 
-    rest = [group for group in OUTGOING if group != DIAGONAL]
     (diagonal,) = pack([DIAGONAL], alignment)
     lists, diagonal = lax.optimization_barrier((alignment, diagonal))
-    shares = {DIAGONAL: diagonal, **dict(zip(rest, pack(rest, lists)))}
-    shares = swapped([shares[group] for group in OUTGOING])
-    rows = pltpu.VMEM((parts, 2, BLK, share), kind)
-    grads = pltpu.VMEM((seq_count, BLK, share), jnp.float32)
-    turned = pltpu.VMEM((seq_count, 2, share, BLK), kind)
-    shares = pl.pallas_call(
-        functools.partial(attend_kernel, seq_count, INCOMING),
-        out_shape=sizes(OUTGOING, 0),
-        in_specs=specs(2, pltpu.SMEM) + specs(len(INCOMING), pltpu.VMEM),
-        out_specs=specs(len(OUTGOING), pltpu.VMEM),
-        scratch_shapes=[rows, rows, grads, grads, turned, pltpu.SMEM((seq_count,), jnp.int32)],
-        compiler_params=params,
-        cost_estimate=attend_cost(seq_count, share),
-        name="attend",
-    )(source_length, target_length, *shares)
-    shares = swapped(shares)
+    (diagonal,), shares, handed_on = swapped([diagonal], pack(REST, lists))
+    coming = [diagonal, *shares, handed_on]
+    rows = pltpu.VMEM((parts, 2, BLK, LANES), kind)
+    grads = pltpu.VMEM((seq_count, BLK, LANES), jnp.float32)
+    turned = pltpu.VMEM((seq_count, 2, LANES, BLK), kind)
+
+    def attend(turn, *before):
+        lanes = (turn + 1) * LANES
+        return pl.pallas_call(
+            functools.partial(attend_kernel, seq_count, turn),
+            out_shape=[
+                jax.ShapeDtypeStruct((4 * BLK, LANES), kind),
+                *([jax.ShapeDtypeStruct((2 * BLK, lanes), kind)] * len(REST)),
+            ],
+            in_specs=specs(2, pltpu.SMEM) + specs(len(coming) + len(before), pltpu.VMEM),
+            out_specs=specs(1 + len(REST), pltpu.VMEM),
+            scratch_shapes=[rows, rows, grads, grads, turned, pltpu.SMEM((seq_count,), jnp.int32)],
+            compiler_params=params,
+            cost_estimate=attend_cost(seq_count, LANES),
+            name="attend",
+        )(source_length, target_length, *coming, *before)
+
+    diagonals, shares = [], []
+    for turn in range(TILES):
+        diagonal, *shares = attend(turn, *shares)
+        diagonals.append(diagonal)
+    diagonals, shares, handed_on = swapped(diagonals, shares)
     out_shape = jax.ShapeDtypeStruct((1, 1, BLK, width), kind)
     return pl.pallas_call(
-        functools.partial(unpack_kernel, seq_count, INCOMING),
+        functools.partial(unpack_kernel, seq_count),
         out_shape=[out_shape, out_shape],
-        in_specs=specs(len(INCOMING), pltpu.VMEM),
+        in_specs=specs(TILES + len(REST) + 1, pltpu.VMEM),
         out_specs=specs(2, pltpu.HBM),
-        scratch_shapes=[sems],
+        scratch_shapes=[pltpu.SemaphoreType.DMA((2, parts + TILES))],
         compiler_params=params,
         name="unpack",
-    )(*shares)
+    )(*diagonals, *shares, handed_on)
 
 
 def on_device(first_rows, second_rows, alignment, diffusion_mask, source_length, target_length):
@@ -360,7 +386,7 @@
     paired = (
         (parts, seq_count) == (8, 4)
         and first_rows.shape[2] == BLK
-        and first_rows.shape[3] % (parts * LANES) == 0
+        and first_rows.shape[3] == parts * TILES * LANES
     )
     work = by_pairs if paired else by_all_to_all
     return tuple(

time: 37.8 us -> 37.7 us (level)
  waiting for transfers between devices: 14.3 us -> 13 us
  local copies, waits for them, and re-layouts: 0.02 us -> 0.84 us
  Pallas kernels: 7.14 us -> 7.65 us
    ppermute x14 -> x15, waiting for transfers between devices: 14.3 us -> 13 us  [permuted(): return lax.ppermute(share, AXES, [(dev, dev ^ step) for dev in range(8)])]
    slice x2 -> x4, local copies, waits for them, and re-layouts: 0.02 us -> 0.83 us  [swapped(): handed_on = [share[share.shape[0] // 2:] for share in diagonals]]
    pallas_call x2 -> x3, Pallas kernels: 4.7 us -> 5.21 us  [the longest x2 4.08 us: attend(): pl.pallas_call(functools.partial(attend_kernel, seq_count, turn), out_sha...]
    ppermute x14 -> x15, starting transfers between devices: 14.1 us -> 13.9 us  [permuted(): return lax.ppermute(share, AXES, [(dev, dev ^ step) for dev in range(8)])]
  transfers between devices with their start and end apart: 14 -> 15, of which waited for: 7 -> 8; matrix products, arithmetic and copies ran while one was open for 0% -> 0% of each run, Pallas kernels for 4% -> 9%
where the time goes in v19:
time: 37.7 us; the launch traced here: 37.4 us
  starting transfers between devices  13.9 us (37%)
  waiting for transfers between devices  13 us (34%)
  Pallas kernels  7.65 us (20%)
  between operations  2.02 us (5%)
  local copies, waits for them, and re-layouts  0.84 us (2%)
    ppermute x15, starting transfers between devices, permuted(): return lax.ppermute(share, AXES, [(dev, dev ^ step) for dev in range(8)])  13.9 us
    ppermute x15, waiting for transfers between devices, permuted(): return lax.ppermute(share, AXES, [(dev, dev ^ step) for dev in range(8)])  13 us
    pallas_call x2, Pallas kernels, attend(): pl.pallas_call(functools.partial(attend_kernel, seq_count, turn), out_sha...  4.08 us
    pallas_call x2, Pallas kernels, pack(): pl.pallas_call(functools.partial(pack_kernel, seq_count, groups), out_sha...  2.44 us
    pallas_call x1, Pallas kernels, by_pairs(): pl.pallas_call(functools.partial(unpack_kernel, seq_count), out_shape=[ou...  1.12 us
    slice x4, local copies, waits for them, and re-layouts, swapped(): handed_on = [share[share.shape[0] // 2:] for share in diagonals]  0.83 us
  transfers between devices with their start and end apart: 15, of which 8 were waited for; matrix products, arithmetic and copies ran while one was open for 0% of the time, Pallas kernels for 9%

profile of v19, /device:TPU:0, one launch (start us, length us, event | category | flops | bytes accessed | tf_op | source)
XLA Modules:
  0.0 37.4 jit_solution(1012738603342372239)
XLA Ops:
  0.6 1.1 %pack.2 = bf16[512,256]{1,0:T(8,128)(2,1)S(1)} custom-call(s32[1,1,2]{2,1,0:T(1,128)} %refs_0_.2, s32[1,128]{1,0:T(1,128)} %refs_1_.3, bf16[1,1,128,2048]{3,2,1,0:T(8,128)(2,1)} %refs_2_.3, bf16[1,1,128,2048]{3,2,1,0:T(8,128)(2,1)} %refs_3_.3), custom_call_target="tpu_custom_call" | custom-call | tf_op jit(solution)/shard_map/pack/pallas_call | solution.py:327
  1.8 4.0 %collective-permute-start = (bf16[512,256]{1,0:T(8,128)(2,1)S(1)}, bf16[512,256]{1,0:T(8,128)(2,1)S(1)}, u32[]{:S(2)}, u32[]{:S(2)}) collective-permute-start(bf16[512,256]{1,0:T(8,128)(2,1)S(1)} %pack.2), channel_id=1, source_target_pairs={{0,18},{1,19},{2,16},{3,17},{16,2},{17,3},{18,0},{19,1},{4,22},{5,... | collective-permute-start | bytes 786440 | tf_op jit(solution)/shard_map/ppermute | solution.py:295
  5.7 1.3 %pack.3 = (bf16[272,256]{1,0:T(8,128)(2,1)S(1)}, bf16[272,256]{1,0:T(8,128)(2,1)S(1)}, bf16[256,256]{1,0:T(8,128)(2,1)S(1)}, bf16[272,256]{1,0:T(8,128)(2,1)S(1)...) custom-call(s32[1,1,2]{2,1,0:T(1,128)} %refs_0_.2, s32[1,128]{1,0:T(1,128)} %refs_1_.3, ...), custom_call_target="tpu_custom_call" | custom-call | tf_op jit(solution)/shard_map/pack/pallas_call | solution.py:327
  7.0 0.1 collective-permute-start.1
  7.1 0.6 %collective-permute-start.3 = (bf16[272,256]{1,0:T(8,128)(2,1)S(1)}, bf16[272,256]{1,0:T(8,128)(2,1)S(1)}, u32[]{:S(2)}, u32[]{:S(2)}) collective-permute-start(bf16[272,256]{1,0:T(8,128)(2,1)S(1)} %get-tuple-element.37), channel_id=1, source_target_pairs={{0,2},{1,3},{2,0},{3,1},{16,18},{17,19},{18,16},{19,17},{4,6},{5,7... | collective-permute-start | bytes 417800 | tf_op jit(solution)/shard_map/ppermute | solution.py:295
  7.7 1.3 %collective-permute-start.5 = (bf16[272,256]{1,0:T(8,128)(2,1)S(1)}, bf16[272,256]{1,0:T(8,128)(2,1)S(1)}, u32[]{:S(2)}, u32[]{:S(2)}) collective-permute-start(bf16[272,256]{1,0:T(8,128)(2,1)S(1)} %get-tuple-element.39), channel_id=1, source_target_pairs={{0,3},{1,2},{2,1},{3,0},{16,19},{17,18},{18,17},{19,16},{4,7},{5,6... | collective-permute-start | bytes 417800 | tf_op jit(solution)/shard_map/ppermute | solution.py:295
  9.0 0.5 %collective-permute-start.2 = (bf16[256,256]{1,0:T(8,128)(2,1)S(1)}, bf16[256,256]{1,0:T(8,128)(2,1)S(1)}, u32[]{:S(2)}, u32[]{:S(2)}) collective-permute-start(bf16[256,256]{1,0:T(8,128)(2,1)S(1)} %get-tuple-element.36), channel_id=1, source_target_pairs={{0,16},{1,17},{2,18},{3,19},{16,0},{17,1},{18,2},{19,3},{4,20},{5,... | collective-permute-start | bytes 393224 | tf_op jit(solution)/shard_map/ppermute | solution.py:295
  9.5 0.0 collective-permute-done.1.refs_2_
  9.5 1.2 %collective-permute-start.4 = (bf16[256,256]{1,0:T(8,128)(2,1)S(1)}, bf16[256,256]{1,0:T(8,128)(2,1)S(1)}, u32[]{:S(2)}, u32[]{:S(2)}) collective-permute-start(bf16[256,256]{1,0:T(8,128)(2,1)S(1)} %get-tuple-element.38), channel_id=1, source_target_pairs={{0,17},{1,16},{2,19},{3,18},{16,1},{17,0},{18,3},{19,2},{4,21},{5,... | collective-permute-start | bytes 393224 | tf_op jit(solution)/shard_map/ppermute | solution.py:295
  10.7 2.2 %collective-permute-done.refs_0_ = bf16[512,256]{1,0:T(8,128)(2,1)S(1)} collective-permute-done((bf16[512,256]{1,0:T(8,128)(2,1)S(1)}, bf16[512,256]{1,0:T(8,128)(2,1)S(1)}, u32[]{:S(2)}, u32[]{:S(2)}) %collective-permute-start) | collective-permute-done | bytes 262176 | tf_op jit(solution)/shard_map/ppermute | solution.py:295
  12.9 0.1 collective-permute-start.6
  14.2 1.3 %collective-permute-done.2.refs_3_ = bf16[256,256]{1,0:T(8,128)(2,1)S(1)} collective-permute-done((bf16[256,256]{1,0:T(8,128)(2,1)S(1)}, bf16[256,256]{1,0:T(8,128)(2,1)S(1)}, u32[]{:S(2)}, u32[]{:S(2)}) %collective-permute-start.2) | collective-permute-done | bytes 131104 | tf_op jit(solution)/shard_map/ppermute | solution.py:295
  15.5 2.2 %collective-permute-done.4.refs_5_ = bf16[256,256]{1,0:T(8,128)(2,1)S(1)} collective-permute-done((bf16[256,256]{1,0:T(8,128)(2,1)S(1)}, bf16[256,256]{1,0:T(8,128)(2,1)S(1)}, u32[]{:S(2)}, u32[]{:S(2)}) %collective-permute-start.4) | collective-permute-done | bytes 131104 | tf_op jit(solution)/shard_map/ppermute | solution.py:295
  17.7 0.0 collective-permute-done.3.refs_4_
  17.7 0.0 collective-permute-done.5.refs_6_
  17.7 0.0 collective-permute-done.6.refs_7_
  17.7 2.0 %attend.2 = (bf16[512,128]{1,0:T(8,128)(2,1)S(1)}, bf16[256,128]{1,0:T(8,128)(2,1)S(1)}, bf16[256,128]{1,0:T(8,128)(2,1)S(1)}, bf16[256,128]{1,0:T(8,128)(2,1)S(...) custom-call(s32[1]{0:T(128)S(6)} %copy.8.source_len, ...), custom_call_target="tpu_custom_call" | custom-call | flops 167772160 | bytes 1048576 | tf_op jit(solution)/shard_map/attend/pallas_call | solution.py:352
  19.7 2.6 %collective-permute-start.7 = (bf16[512,128]{1,0:T(8,128)(2,1)S(1)}, bf16[512,128]{1,0:T(8,128)(2,1)S(1)}, u32[]{:S(2)}, u32[]{:S(2)}) collective-permute-start(bf16[512,128]{1,0:T(8,128)(2,1)S(1)} %get-tuple-element.47), channel_id=1, source_target_pairs={{0,18},{1,19},{2,16},{3,17},{16,2},{17,3},{18,0},{19,1},{4,22},{5,... | collective-permute-start | bytes 393224 | tf_op jit(solution)/shard_map/ppermute | solution.py:295
  22.3 2.1 %attend.3 = (bf16[512,128]{1,0:T(8,128)(2,1)S(1)}, bf16[256,256]{1,0:T(8,128)(2,1)S(1)}, bf16[256,256]{1,0:T(8,128)(2,1)S(1)}, bf16[256,256]{1,0:T(8,128)(2,1)S(...) custom-call(s32[1]{0:T(128)S(6)} %copy.8.source_len, ...), custom_call_target="tpu_custom_call" | custom-call | flops 167772160 | bytes 1048576 | tf_op jit(solution)/shard_map/attend/pallas_call | solution.py:352
  24.4 0.5 %collective-permute-start.8 = (bf16[512,128]{1,0:T(8,128)(2,1)S(1)}, bf16[512,128]{1,0:T(8,128)(2,1)S(1)}, u32[]{:S(2)}, u32[]{:S(2)}) collective-permute-start(bf16[512,128]{1,0:T(8,128)(2,1)S(1)} %get-tuple-element.49), channel_id=1, source_target_pairs={{0,18},{1,19},{2,16},{3,17},{16,2},{17,3},{18,0},{19,1},{4,22},{5,... | collective-permute-start | bytes 393224 | tf_op jit(solution)/shard_map/ppermute | solution.py:295
  24.8 1.6 %collective-permute-done.7.refs_0_ = bf16[512,128]{1,0:T(8,128)(2,1)S(1)} collective-permute-done((bf16[512,128]{1,0:T(8,128)(2,1)S(1)}, bf16[512,128]{1,0:T(8,128)(2,1)S(1)}, u32[]{:S(2)}, u32[]{:S(2)}) %collective-permute-start.7) | collective-permute-done | bytes 131104 | tf_op jit(solution)/shard_map/ppermute | solution.py:295
  26.4 0.0 copy-start
  26.4 0.0 collective-permute-start.9
  26.4 1.2 %collective-permute-start.10 = (bf16[256,256]{1,0:T(8,128)(2,1)S(1)}, bf16[256,256]{1,0:T(8,128)(2,1)S(1)}, u32[]{:S(2)}, u32[]{:S(2)}) collective-permute-start(bf16[256,256]{1,0:T(8,128)(2,1)S(1)} %get-tuple-element.54), channel_id=1, source_target_pairs={{0,16},{1,17},{2,18},{3,19},{16,0},{17,1},{18,2},{19,3},{4,20},{5,... | collective-permute-start | bytes 393224 | tf_op jit(solution)/shard_map/ppermute | solution.py:295
  27.6 1.9 %collective-permute-start.11 = (bf16[256,256]{1,0:T(8,128)(2,1)S(1)}, bf16[256,256]{1,0:T(8,128)(2,1)S(1)}, u32[]{:S(2)}, u32[]{:S(2)}) collective-permute-start(bf16[256,256]{1,0:T(8,128)(2,1)S(1)} %get-tuple-element.55), channel_id=1, source_target_pairs={{0,2},{1,3},{2,0},{3,1},{16,18},{17,19},{18,16},{19,17},{4,6},{5,7... | collective-permute-start | bytes 393224 | tf_op jit(solution)/shard_map/ppermute | solution.py:295
  29.5 0.0 collective-permute-start.12
  29.5 0.0 copy-done
  29.6 1.1 %collective-permute-done.8.refs_1_ = bf16[512,128]{1,0:T(8,128)(2,1)S(1)} collective-permute-done((bf16[512,128]{1,0:T(8,128)(2,1)S(1)}, bf16[512,128]{1,0:T(8,128)(2,1)S(1)}, u32[]{:S(2)}, u32[]{:S(2)}) %collective-permute-start.8) | collective-permute-done | bytes 131104 | tf_op jit(solution)/shard_map/ppermute | solution.py:295
  30.7 0.0 slice-start
  30.7 0.0 collective-permute-start.13
  30.7 0.0 collective-permute-done.9.refs_3_
  30.7 0.8 %slice-done = bf16[256,128]{1,0:T(8,128)(2,1)S(1)} async-done(((bf16[512,128]{1,0:T(8,128)(2,1)}), bf16[256,128]{1,0:T(8,128)(2,1)S(1)}, s32[]{:S(2)}) %slice-start) | async-done | bytes 65560 | tf_op jit(solution)/shard_map/slice | solution.py:305
  31.5 0.0 copy-start.1
  31.5 0.1 collective-permute-start.14
  31.6 1.8 %collective-permute-done.10.refs_4_ = bf16[256,256]{1,0:T(8,128)(2,1)S(1)} collective-permute-done((bf16[256,256]{1,0:T(8,128)(2,1)S(1)}, bf16[256,256]{1,0:T(8,128)(2,1)S(1)}, u32[]{:S(2)}, u32[]{:S(2)}) %collective-permute-start.10) | collective-permute-done | bytes 131104 | tf_op jit(solution)/shard_map/ppermute | solution.py:295
  33.4 0.0 collective-permute-done.11.refs_5_
  33.4 2.7 %collective-permute-done.12.refs_6_ = bf16[256,256]{1,0:T(8,128)(2,1)S(1)} collective-permute-done((bf16[256,256]{1,0:T(8,128)(2,1)S(1)}, bf16[256,256]{1,0:T(8,128)(2,1)S(1)}, u32[]{:S(2)}, u32[]{:S(2)}) %collective-permute-start.12) | collective-permute-done | bytes 131104 | tf_op jit(solution)/shard_map/ppermute | solution.py:295
  36.2 0.1 collective-permute-done.13.refs_7_
  36.2 0.0 collective-permute-done.14.refs_8_
  36.2 0.0 copy-done.1
  36.2 1.1 %unpack.1 = (bf16[1,1,128,2048]{3,2,1,0:T(8,128)(2,1)}, bf16[1,1,128,2048]{3,2,1,0:T(8,128)(2,1)}) custom-call(bf16[512,128]{1,0:T(8,128)(2,1)S(1)} %copy-done.1, bf16[512,128]{1,0:T(8,128)(2,1)S(1)} %collective-permute-done.8.refs_1_, bf16[256,256]{1,0:T(8,128)(2,1)S(1)} %get-tuple-element.52.refs_2_, bf16[256,256]{1,0:T(8,128)(2,1)S(1)} %collective-permute-done.9.refs_3_, ...), custom_call_target="tpu_custom_call" | custom-call | tf_op jit(solution)/shard_map/unpack/pallas_call | solution.py:372
  (3 shorter events, 0.0 us)
Async XLA Ops:
  1.8 11.1 %collective-permute-start = (bf16[512,256]{1,0:T(8,128)(2,1)S(1)}, bf16[512,256]{1,0:T(8,128)(2,1)S(1)}, u32[]{:S(2)}, u32[]{:S(2)}) collective-permute-start(bf16[512,256]{1,0:T(8,128)(2,1)S(1)} %pack.2), channel_id=1, source_target_pairs={{0,18},{1,19},{2,16},{3,17},{16,2},{17,3},{18,0},{19,1},{4,22},{5,... | collective-permute-start | bytes 786440 | tf_op jit(solution)/shard_map/ppermute | solution.py:295
  7.0 2.5 %collective-permute-start.1 = (bf16[272,256]{1,0:T(8,128)(2,1)S(1)}, bf16[272,256]{1,0:T(8,128)(2,1)S(1)}, u32[]{:S(2)}, u32[]{:S(2)}) collective-permute-start(bf16[272,256]{1,0:T(8,128)(2,1)S(1)} %get-tuple-element.32), channel_id=1, source_target_pairs={{0,1},{1,0},{2,3},{3,2},{16,17},{17,16},{18,19},{19,18},{4,5},{5,4... | collective-permute-start | bytes 417800 | tf_op jit(solution)/shard_map/ppermute | solution.py:295
  7.1 10.6 %collective-permute-start.3 = (bf16[272,256]{1,0:T(8,128)(2,1)S(1)}, bf16[272,256]{1,0:T(8,128)(2,1)S(1)}, u32[]{:S(2)}, u32[]{:S(2)}) collective-permute-start(bf16[272,256]{1,0:T(8,128)(2,1)S(1)} %get-tuple-element.37), channel_id=1, source_target_pairs={{0,2},{1,3},{2,0},{3,1},{16,18},{17,19},{18,16},{19,17},{4,6},{5,7... | collective-permute-start | bytes 417800 | tf_op jit(solution)/shard_map/ppermute | solution.py:295
  7.7 10.0 %collective-permute-start.5 = (bf16[272,256]{1,0:T(8,128)(2,1)S(1)}, bf16[272,256]{1,0:T(8,128)(2,1)S(1)}, u32[]{:S(2)}, u32[]{:S(2)}) collective-permute-start(bf16[272,256]{1,0:T(8,128)(2,1)S(1)} %get-tuple-element.39), channel_id=1, source_target_pairs={{0,3},{1,2},{2,1},{3,0},{16,19},{17,18},{18,17},{19,16},{4,7},{5,6... | collective-permute-start | bytes 417800 | tf_op jit(solution)/shard_map/ppermute | solution.py:295
  9.0 6.5 %collective-permute-start.2 = (bf16[256,256]{1,0:T(8,128)(2,1)S(1)}, bf16[256,256]{1,0:T(8,128)(2,1)S(1)}, u32[]{:S(2)}, u32[]{:S(2)}) collective-permute-start(bf16[256,256]{1,0:T(8,128)(2,1)S(1)} %get-tuple-element.36), channel_id=1, source_target_pairs={{0,16},{1,17},{2,18},{3,19},{16,0},{17,1},{18,2},{19,3},{4,20},{5,... | collective-permute-start | bytes 393224 | tf_op jit(solution)/shard_map/ppermute | solution.py:295
  9.5 8.2 %collective-permute-start.4 = (bf16[256,256]{1,0:T(8,128)(2,1)S(1)}, bf16[256,256]{1,0:T(8,128)(2,1)S(1)}, u32[]{:S(2)}, u32[]{:S(2)}) collective-permute-start(bf16[256,256]{1,0:T(8,128)(2,1)S(1)} %get-tuple-element.38), channel_id=1, source_target_pairs={{0,17},{1,16},{2,19},{3,18},{16,1},{17,0},{18,3},{19,2},{4,21},{5,... | collective-permute-start | bytes 393224 | tf_op jit(solution)/shard_map/ppermute | solution.py:295
  12.9 4.8 %collective-permute-start.6 = (bf16[256,256]{1,0:T(8,128)(2,1)S(1)}, bf16[256,256]{1,0:T(8,128)(2,1)S(1)}, u32[]{:S(2)}, u32[]{:S(2)}) collective-permute-start(bf16[256,256]{1,0:T(8,128)(2,1)S(1)} %slice.9), channel_id=1, source_target_pairs={{0,1},{1,0},{2,3},{3,2},{16,17},{17,16},{18,19},{19,18},{4,5},{5,4... | collective-permute-start | bytes 393224 | tf_op jit(solution)/shard_map/ppermute | solution.py:295
  19.7 6.7 %collective-permute-start.7 = (bf16[512,128]{1,0:T(8,128)(2,1)S(1)}, bf16[512,128]{1,0:T(8,128)(2,1)S(1)}, u32[]{:S(2)}, u32[]{:S(2)}) collective-permute-start(bf16[512,128]{1,0:T(8,128)(2,1)S(1)} %get-tuple-element.47), channel_id=1, source_target_pairs={{0,18},{1,19},{2,16},{3,17},{16,2},{17,3},{18,0},{19,1},{4,22},{5,... | collective-permute-start | bytes 393224 | tf_op jit(solution)/shard_map/ppermute | solution.py:295
  24.4 6.3 %collective-permute-start.8 = (bf16[512,128]{1,0:T(8,128)(2,1)S(1)}, bf16[512,128]{1,0:T(8,128)(2,1)S(1)}, u32[]{:S(2)}, u32[]{:S(2)}) collective-permute-start(bf16[512,128]{1,0:T(8,128)(2,1)S(1)} %get-tuple-element.49), channel_id=1, source_target_pairs={{0,18},{1,19},{2,16},{3,17},{16,2},{17,3},{18,0},{19,1},{4,22},{5,... | collective-permute-start | bytes 393224 | tf_op jit(solution)/shard_map/ppermute | solution.py:295
  26.4 3.1 %copy-start = (bf16[512,128]{1,0:T(8,128)(2,1)}, bf16[512,128]{1,0:T(8,128)(2,1)S(1)}, u32[]{:S(2)}) copy-start(bf16[512,128]{1,0:T(8,128)(2,1)S(1)} %collective-permute-done.7.refs_0_) | copy-start | bytes 393220
  26.4 4.2 %collective-permute-start.9 = (bf16[256,256]{1,0:T(8,128)(2,1)S(1)}, bf16[256,256]{1,0:T(8,128)(2,1)S(1)}, u32[]{:S(2)}, u32[]{:S(2)}) collective-permute-start(bf16[256,256]{1,0:T(8,128)(2,1)S(1)} %get-tuple-element.50), channel_id=1, source_target_pairs={{0,1},{1,0},{2,3},{3,2},{16,17},{17,16},{18,19},{19,18},{4,5},{5,4... | collective-permute-start | bytes 393224 | tf_op jit(solution)/shard_map/ppermute | solution.py:295
  26.4 7.0 %collective-permute-start.10 = (bf16[256,256]{1,0:T(8,128)(2,1)S(1)}, bf16[256,256]{1,0:T(8,128)(2,1)S(1)}, u32[]{:S(2)}, u32[]{:S(2)}) collective-permute-start(bf16[256,256]{1,0:T(8,128)(2,1)S(1)} %get-tuple-element.54), channel_id=1, source_target_pairs={{0,16},{1,17},{2,18},{3,19},{16,0},{17,1},{18,2},{19,3},{4,20},{5,... | collective-permute-start | bytes 393224 | tf_op jit(solution)/shard_map/ppermute | solution.py:295
  27.6 5.8 %collective-permute-start.11 = (bf16[256,256]{1,0:T(8,128)(2,1)S(1)}, bf16[256,256]{1,0:T(8,128)(2,1)S(1)}, u32[]{:S(2)}, u32[]{:S(2)}) collective-permute-start(bf16[256,256]{1,0:T(8,128)(2,1)S(1)} %get-tuple-element.55), channel_id=1, source_target_pairs={{0,2},{1,3},{2,0},{3,1},{16,18},{17,19},{18,16},{19,17},{4,6},{5,7... | collective-permute-start | bytes 393224 | tf_op jit(solution)/shard_map/ppermute | solution.py:295
  29.5 6.6 %collective-permute-start.12 = (bf16[256,256]{1,0:T(8,128)(2,1)S(1)}, bf16[256,256]{1,0:T(8,128)(2,1)S(1)}, u32[]{:S(2)}, u32[]{:S(2)}) collective-permute-start(bf16[256,256]{1,0:T(8,128)(2,1)S(1)} %get-tuple-element.56), channel_id=1, source_target_pairs={{0,17},{1,16},{2,19},{3,18},{16,1},{17,0},{18,3},{19,2},{4,21},{5,... | collective-permute-start | bytes 393224 | tf_op jit(solution)/shard_map/ppermute | solution.py:295
  30.7 0.8 %slice-start = ((bf16[512,128]{1,0:T(8,128)(2,1)}), bf16[256,128]{1,0:T(8,128)(2,1)S(1)}, s32[]{:S(2)}) async-start(bf16[512,128]{1,0:T(8,128)(2,1)} %copy-done), calls=%async_computation | async-start | bytes 131072 | tf_op jit(solution)/shard_map/slice | solution.py:305
  30.7 5.6 %collective-permute-start.13 = (bf16[256,256]{1,0:T(8,128)(2,1)S(1)}, bf16[256,256]{1,0:T(8,128)(2,1)S(1)}, u32[]{:S(2)}, u32[]{:S(2)}) collective-permute-start(bf16[256,256]{1,0:T(8,128)(2,1)S(1)} %get-tuple-element.57), channel_id=1, source_target_pairs={{0,3},{1,2},{2,1},{3,0},{16,19},{17,18},{18,17},{19,16},{4,7},{5,6... | collective-permute-start | bytes 393224 | tf_op jit(solution)/shard_map/ppermute | solution.py:295
  31.5 4.7 %copy-start.1 = (bf16[512,128]{1,0:T(8,128)(2,1)S(1)}, bf16[512,128]{1,0:T(8,128)(2,1)}, u32[]{:S(2)}) copy-start(bf16[512,128]{1,0:T(8,128)(2,1)} %copy-done) | copy-start | bytes 393220
  31.5 4.7 %collective-permute-start.14 = (bf16[256,256]{1,0:T(8,128)(2,1)S(1)}, bf16[256,256]{1,0:T(8,128)(2,1)S(1)}, u32[]{:S(2)}, u32[]{:S(2)}) collective-permute-start(bf16[256,256]{1,0:T(8,128)(2,1)S(1)} %pad_maximum_fusion), channel_id=1, source_target_pairs={{0,1},{1,0},{2,3},{3,2},{16,17},{17,16},{18,19},{19,18},{4,5},{5,4... | collective-permute-start | bytes 393224 | tf_op jit(solution)/shard_map/ppermute | solution.py:295

commit v20 on v19

--- a/solution.py
+++ b/solution.py
@@ -174,11 +174,12 @@
 
 
 DIAGONAL = (6, 7)
-REST = [(0,), (1,), (4,), (2,), (5,), (3,)]
+OWN, NEAR = (0,), (1,)
+ACROSS = [(4,), (2,), (5,), (3,)]
+REST = [OWN, NEAR, *ACROSS]
 OUTGOING = [DIAGONAL, *REST]
 INCOMING = [*OUTGOING, DIAGONAL[1:]]
 TILES = 2
-AFTER = REST.index((1,))
 
 
 def pack_kernel(seq_count, steps, *refs):
@@ -269,15 +270,16 @@
 
 
 def unpack_kernel(seq_count, *refs):
-    diagonals, shares = refs[:TILES], refs[TILES : TILES + len(REST) + 1]
+    diagonals, handed_on, shares = refs[:TILES], refs[TILES : 2 * TILES], refs[2 * TILES : -3]
     first, second, sem = refs[-3:]
     width = first.shape[3] // (2 * seq_count)
     me = device_index(seq_count)
     pieces = [
-        (DIAGONAL[0], tile * LANES, share.at[pl.ds(0, 2 * BLK)])
-        for tile, share in enumerate(diagonals)
+        (step, tile * LANES, share.at[pl.ds(0, 2 * BLK)])
+        for step, arrived in zip(DIAGONAL, (diagonals, handed_on))
+        for tile, share in enumerate(arrived)
     ]
-    pieces += [(group[0], 0, share) for group, share in zip([*REST, DIAGONAL[1:]], shares)]
+    pieces += [(step, 0, share) for (step,), share in zip(REST, shares)]
     copies = []
     for slot, (step, start, share) in enumerate(pieces):
         lanes = pl.ds(pl.multiple_of((me ^ step) * width + start, LANES), share.shape[1])
@@ -296,14 +298,16 @@
 
 
 def swapped(diagonals, shares):
-    diagonals, shares = [permuted(share, DIAGONAL[0]) for share in diagonals], list(shares)
-    for share in diagonals[:-1]:
-        shares[AFTER], diagonals[0] = lax.optimization_barrier((shares[AFTER], diagonals[0]))
-    shares = [permuted(share, step) if step else share for (step,), share in zip(REST, shares)]
-    near = REST.index((1,))
-    diagonals[-1], shares[near] = lax.optimization_barrier((diagonals[-1], shares[near]))
-    handed_on = [share[share.shape[0] // 2 :] for share in diagonals]
-    return diagonals, shares, permuted(jnp.concatenate(handed_on, axis=1), 1)
+    held = dict(zip(REST, shares))
+    diagonals = [permuted(share, DIAGONAL[0]) for share in diagonals]
+    moved = {group: permuted(held[group], group[0]) for group in ACROSS}
+    if len(diagonals) > 1:
+        held[NEAR], diagonals[0] = lax.optimization_barrier((held[NEAR], diagonals[0]))
+    moved[NEAR] = permuted(held[NEAR], NEAR[0])
+    if len(diagonals) == 1:
+        diagonals[0], moved[NEAR] = lax.optimization_barrier((diagonals[0], moved[NEAR]))
+    handed_on = [permuted(share[share.shape[0] // 2 :], NEAR[0]) for share in diagonals]
+    return diagonals, [held[OWN], moved[NEAR], *(moved[group] for group in ACROSS)], handed_on
 
 
 def by_pairs(first_rows, second_rows, alignment, diffusion_mask, source_length, target_length):
@@ -341,8 +345,8 @@
 
     (diagonal,) = pack([DIAGONAL], alignment)
     lists, diagonal = lax.optimization_barrier((alignment, diagonal))
-    (diagonal,), shares, handed_on = swapped([diagonal], pack(REST, lists))
-    coming = [diagonal, *shares, handed_on]
+    diagonals, shares, handed_on = swapped([diagonal], pack(REST, lists))
+    coming = [*diagonals, *shares, *handed_on]
     rows = pltpu.VMEM((parts, 2, BLK, LANES), kind)
     grads = pltpu.VMEM((seq_count, BLK, LANES), jnp.float32)
     turned = pltpu.VMEM((seq_count, 2, LANES, BLK), kind)
@@ -372,12 +376,12 @@
     return pl.pallas_call(
         functools.partial(unpack_kernel, seq_count),
         out_shape=[out_shape, out_shape],
-        in_specs=specs(TILES + len(REST) + 1, pltpu.VMEM),
+        in_specs=specs(2 * TILES + len(REST), pltpu.VMEM),
         out_specs=specs(2, pltpu.HBM),
-        scratch_shapes=[pltpu.SemaphoreType.DMA((2, parts + TILES))],
+        scratch_shapes=[pltpu.SemaphoreType.DMA((2, parts + 2 * TILES))],
         compiler_params=params,
         name="unpack",
-    )(*diagonals, *shares, handed_on)
+    )(*diagonals, *handed_on, *shares)
 
 
 def on_device(first_rows, second_rows, alignment, diffusion_mask, source_length, target_length):

time: 37.7 us -> 36.5 us (0.968)
  waiting for transfers between devices: 13 us -> 11.5 us
  starting transfers between devices: 13.9 us -> 15 us
  local copies, waits for them, and re-layouts: 0.84 us -> 0.02 us
    ppermute x15 -> x16, waiting for transfers between devices: 13 us -> 11.5 us  [permuted(): return lax.ppermute(share, AXES, [(dev, dev ^ step) for dev in range(8)])]
    ppermute x15 -> x16, starting transfers between devices: 13.9 us -> 15 us  [permuted(): return lax.ppermute(share, AXES, [(dev, dev ^ step) for dev in range(8)])]
    slice x4 -> x3, local copies, waits for them, and re-layouts: 0.83 us -> 0.02 us  [swapped(): share[share.shape[0] // 2:]]
  transfers between devices with their start and end apart: 15 -> 16, of which waited for: 8 -> 6; matrix products, arithmetic and copies ran while one was open for 0% -> 0% of each run, Pallas kernels for 9% -> 9%
where the time goes in v20:
time: 36.5 us; the launch traced here: 36.2 us
  starting transfers between devices  15 us (41%)
  waiting for transfers between devices  11.5 us (32%)
  Pallas kernels  7.69 us (21%)
  between operations  2.02 us (6%)
    ppermute x16, starting transfers between devices, permuted(): return lax.ppermute(share, AXES, [(dev, dev ^ step) for dev in range(8)])  15 us
    ppermute x16, waiting for transfers between devices, permuted(): return lax.ppermute(share, AXES, [(dev, dev ^ step) for dev in range(8)])  11.5 us
    pallas_call x2, Pallas kernels, attend(): pl.pallas_call(functools.partial(attend_kernel, seq_count, turn), out_sha...  4.07 us
    pallas_call x2, Pallas kernels, pack(): pl.pallas_call(functools.partial(pack_kernel, seq_count, groups), out_sha...  2.44 us
    pallas_call x1, Pallas kernels, by_pairs(): pl.pallas_call(functools.partial(unpack_kernel, seq_count), out_shape=[ou...  1.18 us
  transfers between devices with their start and end apart: 16, of which 6 were waited for; matrix products, arithmetic and copies ran while one was open for 0% of the time, Pallas kernels for 9%

profile of v20, /device:TPU:0, one launch (start us, length us, event | category | flops | bytes accessed | tf_op | source)
XLA Modules:
  0.0 36.2 jit_solution(14187453672839220728)
XLA Ops:
  0.6 1.1 %pack.2 = bf16[512,256]{1,0:T(8,128)(2,1)S(1)} custom-call(s32[1,1,2]{2,1,0:T(1,128)} %refs_0_.2, s32[1,128]{1,0:T(1,128)} %refs_1_.3, bf16[1,1,128,2048]{3,2,1,0:T(8,128)(2,1)} %refs_2_.3, bf16[1,1,128,2048]{3,2,1,0:T(8,128)(2,1)} %refs_3_.3), custom_call_target="tpu_custom_call" | custom-call | tf_op jit(solution)/shard_map/pack/pallas_call | solution.py:331
  1.8 4.0 %collective-permute-start = (bf16[512,256]{1,0:T(8,128)(2,1)S(1)}, bf16[512,256]{1,0:T(8,128)(2,1)S(1)}, u32[]{:S(2)}, u32[]{:S(2)}) collective-permute-start(bf16[512,256]{1,0:T(8,128)(2,1)S(1)} %pack.2), channel_id=1, source_target_pairs={{0,18},{1,19},{2,16},{3,17},{16,2},{17,3},{18,0},{19,1},{4,22},{5,... | collective-permute-start | bytes 786440 | tf_op jit(solution)/shard_map/ppermute | solution.py:297
  5.7 1.3 %pack.3 = (bf16[272,256]{1,0:T(8,128)(2,1)S(1)}, bf16[272,256]{1,0:T(8,128)(2,1)S(1)}, bf16[256,256]{1,0:T(8,128)(2,1)S(1)}, bf16[272,256]{1,0:T(8,128)(2,1)S(1)...) custom-call(s32[1,1,2]{2,1,0:T(1,128)} %refs_0_.2, s32[1,128]{1,0:T(1,128)} %refs_1_.3, ...), custom_call_target="tpu_custom_call" | custom-call | tf_op jit(solution)/shard_map/pack/pallas_call | solution.py:331
  7.0 0.1 collective-permute-start.1
  7.1 0.6 %collective-permute-start.3 = (bf16[272,256]{1,0:T(8,128)(2,1)S(1)}, bf16[272,256]{1,0:T(8,128)(2,1)S(1)}, u32[]{:S(2)}, u32[]{:S(2)}) collective-permute-start(bf16[272,256]{1,0:T(8,128)(2,1)S(1)} %get-tuple-element.35), channel_id=1, source_target_pairs={{0,2},{1,3},{2,0},{3,1},{16,18},{17,19},{18,16},{19,17},{4,6},{5,7... | collective-permute-start | bytes 417800 | tf_op jit(solution)/shard_map/ppermute | solution.py:297
  7.7 1.3 %collective-permute-start.5 = (bf16[272,256]{1,0:T(8,128)(2,1)S(1)}, bf16[272,256]{1,0:T(8,128)(2,1)S(1)}, u32[]{:S(2)}, u32[]{:S(2)}) collective-permute-start(bf16[272,256]{1,0:T(8,128)(2,1)S(1)} %get-tuple-element.37), channel_id=1, source_target_pairs={{0,3},{1,2},{2,1},{3,0},{16,19},{17,18},{18,17},{19,16},{4,7},{5,6... | collective-permute-start | bytes 417800 | tf_op jit(solution)/shard_map/ppermute | solution.py:297
  9.0 0.5 %collective-permute-start.2 = (bf16[256,256]{1,0:T(8,128)(2,1)S(1)}, bf16[256,256]{1,0:T(8,128)(2,1)S(1)}, u32[]{:S(2)}, u32[]{:S(2)}) collective-permute-start(bf16[256,256]{1,0:T(8,128)(2,1)S(1)} %get-tuple-element.34), channel_id=1, source_target_pairs={{0,16},{1,17},{2,18},{3,19},{16,0},{17,1},{18,2},{19,3},{4,20},{5,... | collective-permute-start | bytes 393224 | tf_op jit(solution)/shard_map/ppermute | solution.py:297
  9.5 0.0 collective-permute-done.1.refs_2_
  9.5 1.2 %collective-permute-start.4 = (bf16[256,256]{1,0:T(8,128)(2,1)S(1)}, bf16[256,256]{1,0:T(8,128)(2,1)S(1)}, u32[]{:S(2)}, u32[]{:S(2)}) collective-permute-start(bf16[256,256]{1,0:T(8,128)(2,1)S(1)} %get-tuple-element.36), channel_id=1, source_target_pairs={{0,17},{1,16},{2,19},{3,18},{16,1},{17,0},{18,3},{19,2},{4,21},{5,... | collective-permute-start | bytes 393224 | tf_op jit(solution)/shard_map/ppermute | solution.py:297
  10.7 2.2 %collective-permute-done.refs_0_ = bf16[512,256]{1,0:T(8,128)(2,1)S(1)} collective-permute-done((bf16[512,256]{1,0:T(8,128)(2,1)S(1)}, bf16[512,256]{1,0:T(8,128)(2,1)S(1)}, u32[]{:S(2)}, u32[]{:S(2)}) %collective-permute-start) | collective-permute-done | bytes 262176 | tf_op jit(solution)/shard_map/ppermute | solution.py:297
  12.9 0.1 collective-permute-start.6
  14.2 1.3 %collective-permute-done.2.refs_3_ = bf16[256,256]{1,0:T(8,128)(2,1)S(1)} collective-permute-done((bf16[256,256]{1,0:T(8,128)(2,1)S(1)}, bf16[256,256]{1,0:T(8,128)(2,1)S(1)}, u32[]{:S(2)}, u32[]{:S(2)}) %collective-permute-start.2) | collective-permute-done | bytes 131104 | tf_op jit(solution)/shard_map/ppermute | solution.py:297
  15.5 2.2 %collective-permute-done.4.refs_5_ = bf16[256,256]{1,0:T(8,128)(2,1)S(1)} collective-permute-done((bf16[256,256]{1,0:T(8,128)(2,1)S(1)}, bf16[256,256]{1,0:T(8,128)(2,1)S(1)}, u32[]{:S(2)}, u32[]{:S(2)}) %collective-permute-start.4) | collective-permute-done | bytes 131104 | tf_op jit(solution)/shard_map/ppermute | solution.py:297
  17.7 0.0 collective-permute-done.3.refs_4_
  17.7 0.0 collective-permute-done.5.refs_6_
  17.7 0.0 collective-permute-done.6.refs_7_
  17.7 2.0 %attend.2 = (bf16[512,128]{1,0:T(8,128)(2,1)S(1)}, bf16[256,128]{1,0:T(8,128)(2,1)S(1)}, bf16[256,128]{1,0:T(8,128)(2,1)S(1)}, bf16[256,128]{1,0:T(8,128)(2,1)S(...) custom-call(s32[1]{0:T(128)S(6)} %copy.8.source_len, ...), custom_call_target="tpu_custom_call" | custom-call | flops 167772160 | bytes 1048576 | tf_op jit(solution)/shard_map/attend/pallas_call | solution.py:356
  19.7 2.6 %collective-permute-start.7 = (bf16[512,128]{1,0:T(8,128)(2,1)S(1)}, bf16[512,128]{1,0:T(8,128)(2,1)S(1)}, u32[]{:S(2)}, u32[]{:S(2)}) collective-permute-start(bf16[512,128]{1,0:T(8,128)(2,1)S(1)} %get-tuple-element.45), channel_id=1, source_target_pairs={{0,18},{1,19},{2,16},{3,17},{16,2},{17,3},{18,0},{19,1},{4,22},{5,... | collective-permute-start | bytes 393224 | tf_op jit(solution)/shard_map/ppermute | solution.py:297
  22.3 2.1 %attend.3 = (bf16[512,128]{1,0:T(8,128)(2,1)S(1)}, bf16[256,256]{1,0:T(8,128)(2,1)S(1)}, bf16[256,256]{1,0:T(8,128)(2,1)S(1)}, bf16[256,256]{1,0:T(8,128)(2,1)S(...) custom-call(s32[1]{0:T(128)S(6)} %copy.8.source_len, ...), custom_call_target="tpu_custom_call" | custom-call | flops 167772160 | bytes 1048576 | tf_op jit(solution)/shard_map/attend/pallas_call | solution.py:356
  24.4 0.5 %collective-permute-start.8 = (bf16[512,128]{1,0:T(8,128)(2,1)S(1)}, bf16[512,128]{1,0:T(8,128)(2,1)S(1)}, u32[]{:S(2)}, u32[]{:S(2)}) collective-permute-start(bf16[512,128]{1,0:T(8,128)(2,1)S(1)} %get-tuple-element.47), channel_id=1, source_target_pairs={{0,18},{1,19},{2,16},{3,17},{16,2},{17,3},{18,0},{19,1},{4,22},{5,... | collective-permute-start | bytes 393224 | tf_op jit(solution)/shard_map/ppermute | solution.py:297
  24.8 1.4 %collective-permute-start.12 = (bf16[256,256]{1,0:T(8,128)(2,1)S(1)}, bf16[256,256]{1,0:T(8,128)(2,1)S(1)}, u32[]{:S(2)}, u32[]{:S(2)}) collective-permute-start(bf16[256,256]{1,0:T(8,128)(2,1)S(1)} %get-tuple-element.50), channel_id=1, source_target_pairs={{0,16},{1,17},{2,18},{3,19},{16,0},{17,1},{18,2},{19,3},{4,20},{5,... | collective-permute-start | bytes 393224 | tf_op jit(solution)/shard_map/ppermute | solution.py:297
  26.3 1.7 %collective-permute-start.13 = (bf16[256,256]{1,0:T(8,128)(2,1)S(1)}, bf16[256,256]{1,0:T(8,128)(2,1)S(1)}, u32[]{:S(2)}, u32[]{:S(2)}) collective-permute-start(bf16[256,256]{1,0:T(8,128)(2,1)S(1)} %get-tuple-element.51), channel_id=1, source_target_pairs={{0,2},{1,3},{2,0},{3,1},{16,18},{17,19},{18,16},{19,17},{4,6},{5,7... | collective-permute-start | bytes 393224 | tf_op jit(solution)/shard_map/ppermute | solution.py:297
  27.9 0.0 collective-permute-start.14
  27.9 0.0 collective-permute-done.7.refs_0_
  27.9 0.7 %collective-permute-start.15 = (bf16[256,256]{1,0:T(8,128)(2,1)S(1)}, bf16[256,256]{1,0:T(8,128)(2,1)S(1)}, u32[]{:S(2)}, u32[]{:S(2)}) collective-permute-start(bf16[256,256]{1,0:T(8,128)(2,1)S(1)} %get-tuple-element.53), channel_id=1, source_target_pairs={{0,3},{1,2},{2,1},{3,0},{16,19},{17,18},{18,17},{19,16},{4,7},{5,6... | collective-permute-start | bytes 393224 | tf_op jit(solution)/shard_map/ppermute | solution.py:297
  28.6 3.1 %collective-permute-done.8.refs_1_ = bf16[512,128]{1,0:T(8,128)(2,1)S(1)} collective-permute-done((bf16[512,128]{1,0:T(8,128)(2,1)S(1)}, bf16[512,128]{1,0:T(8,128)(2,1)S(1)}, u32[]{:S(2)}, u32[]{:S(2)}) %collective-permute-start.8) | collective-permute-done | bytes 131104 | tf_op jit(solution)/shard_map/ppermute | solution.py:297
  31.7 0.0 collective-permute-start.11
  31.8 1.8 %collective-permute-done.12.refs_6_ = bf16[256,256]{1,0:T(8,128)(2,1)S(1)} collective-permute-done((bf16[256,256]{1,0:T(8,128)(2,1)S(1)}, bf16[256,256]{1,0:T(8,128)(2,1)S(1)}, u32[]{:S(2)}, u32[]{:S(2)}) %collective-permute-start.12) | collective-permute-done | bytes 131104 | tf_op jit(solution)/shard_map/ppermute | solution.py:297
  33.5 0.0 collective-permute-start.10
  33.5 0.0 collective-permute-done.13.refs_7_
  33.5 0.5 %collective-permute-start.9 = (bf16[256,128]{1,0:T(8,128)(2,1)S(1)}, bf16[256,128]{1,0:T(8,128)(2,1)S(1)}, u32[]{:S(2)}, u32[]{:S(2)}) collective-permute-start(bf16[256,128]{1,0:T(8,128)(2,1)S(1)} %slice.10), channel_id=1, source_target_pairs={{0,1},{1,0},{2,3},{3,2},{16,17},{17,16},{18,19},{19,18},{4,5},{5,4... | collective-permute-start | bytes 196616 | tf_op jit(solution)/shard_map/ppermute | solution.py:297
  34.0 0.9 %collective-permute-done.14.refs_8_ = bf16[256,256]{1,0:T(8,128)(2,1)S(1)} collective-permute-done((bf16[256,256]{1,0:T(8,128)(2,1)S(1)}, bf16[256,256]{1,0:T(8,128)(2,1)S(1)}, u32[]{:S(2)}, u32[]{:S(2)}) %collective-permute-start.14) | collective-permute-done | bytes 131104 | tf_op jit(solution)/shard_map/ppermute | solution.py:297
  35.0 0.0 collective-permute-done.15.refs_9_
  35.0 0.0 collective-permute-done.10.refs_3_
  35.0 0.0 collective-permute-done.9.refs_2_
  35.0 0.0 collective-permute-done.11.refs_5_
  35.0 1.2 %unpack.1 = (bf16[1,1,128,2048]{3,2,1,0:T(8,128)(2,1)}, bf16[1,1,128,2048]{3,2,1,0:T(8,128)(2,1)}) custom-call(bf16[512,128]{1,0:T(8,128)(2,1)S(1)} %collective-permute-done.7.refs_0_, bf16[512,128]{1,0:T(8,128)(2,1)S(1)} %collective-permute-done.8.refs_1_, bf16[256,128]{1,0:T(8,128)(2,1)S(1)} %collective-permute-done.9.refs_2_, ...), custom_call_target="tpu_custom_call" | custom-call | tf_op jit(solution)/shard_map/unpack/pallas_call | solution.py:376
  (3 shorter events, 0.0 us)
Async XLA Ops:
  1.8 11.1 %collective-permute-start = (bf16[512,256]{1,0:T(8,128)(2,1)S(1)}, bf16[512,256]{1,0:T(8,128)(2,1)S(1)}, u32[]{:S(2)}, u32[]{:S(2)}) collective-permute-start(bf16[512,256]{1,0:T(8,128)(2,1)S(1)} %pack.2), channel_id=1, source_target_pairs={{0,18},{1,19},{2,16},{3,17},{16,2},{17,3},{18,0},{19,1},{4,22},{5,... | collective-permute-start | bytes 786440 | tf_op jit(solution)/shard_map/ppermute | solution.py:297
  7.0 2.5 %collective-permute-start.1 = (bf16[272,256]{1,0:T(8,128)(2,1)S(1)}, bf16[272,256]{1,0:T(8,128)(2,1)S(1)}, u32[]{:S(2)}, u32[]{:S(2)}) collective-permute-start(bf16[272,256]{1,0:T(8,128)(2,1)S(1)} %get-tuple-element.30), channel_id=1, source_target_pairs={{0,1},{1,0},{2,3},{3,2},{16,17},{17,16},{18,19},{19,18},{4,5},{5,4... | collective-permute-start | bytes 417800 | tf_op jit(solution)/shard_map/ppermute | solution.py:297
  7.1 10.6 %collective-permute-start.3 = (bf16[272,256]{1,0:T(8,128)(2,1)S(1)}, bf16[272,256]{1,0:T(8,128)(2,1)S(1)}, u32[]{:S(2)}, u32[]{:S(2)}) collective-permute-start(bf16[272,256]{1,0:T(8,128)(2,1)S(1)} %get-tuple-element.35), channel_id=1, source_target_pairs={{0,2},{1,3},{2,0},{3,1},{16,18},{17,19},{18,16},{19,17},{4,6},{5,7... | collective-permute-start | bytes 417800 | tf_op jit(solution)/shard_map/ppermute | solution.py:297
  7.7 10.0 %collective-permute-start.5 = (bf16[272,256]{1,0:T(8,128)(2,1)S(1)}, bf16[272,256]{1,0:T(8,128)(2,1)S(1)}, u32[]{:S(2)}, u32[]{:S(2)}) collective-permute-start(bf16[272,256]{1,0:T(8,128)(2,1)S(1)} %get-tuple-element.37), channel_id=1, source_target_pairs={{0,3},{1,2},{2,1},{3,0},{16,19},{17,18},{18,17},{19,16},{4,7},{5,6... | collective-permute-start | bytes 417800 | tf_op jit(solution)/shard_map/ppermute | solution.py:297
  9.0 6.5 %collective-permute-start.2 = (bf16[256,256]{1,0:T(8,128)(2,1)S(1)}, bf16[256,256]{1,0:T(8,128)(2,1)S(1)}, u32[]{:S(2)}, u32[]{:S(2)}) collective-permute-start(bf16[256,256]{1,0:T(8,128)(2,1)S(1)} %get-tuple-element.34), channel_id=1, source_target_pairs={{0,16},{1,17},{2,18},{3,19},{16,0},{17,1},{18,2},{19,3},{4,20},{5,... | collective-permute-start | bytes 393224 | tf_op jit(solution)/shard_map/ppermute | solution.py:297
  9.5 8.2 %collective-permute-start.4 = (bf16[256,256]{1,0:T(8,128)(2,1)S(1)}, bf16[256,256]{1,0:T(8,128)(2,1)S(1)}, u32[]{:S(2)}, u32[]{:S(2)}) collective-permute-start(bf16[256,256]{1,0:T(8,128)(2,1)S(1)} %get-tuple-element.36), channel_id=1, source_target_pairs={{0,17},{1,16},{2,19},{3,18},{16,1},{17,0},{18,3},{19,2},{4,21},{5,... | collective-permute-start | bytes 393224 | tf_op jit(solution)/shard_map/ppermute | solution.py:297
  12.9 4.8 %collective-permute-start.6 = (bf16[256,256]{1,0:T(8,128)(2,1)S(1)}, bf16[256,256]{1,0:T(8,128)(2,1)S(1)}, u32[]{:S(2)}, u32[]{:S(2)}) collective-permute-start(bf16[256,256]{1,0:T(8,128)(2,1)S(1)} %slice.9), channel_id=1, source_target_pairs={{0,1},{1,0},{2,3},{3,2},{16,17},{17,16},{18,19},{19,18},{4,5},{5,4... | collective-permute-start | bytes 393224 | tf_op jit(solution)/shard_map/ppermute | solution.py:297
  19.7 8.2 %collective-permute-start.7 = (bf16[512,128]{1,0:T(8,128)(2,1)S(1)}, bf16[512,128]{1,0:T(8,128)(2,1)S(1)}, u32[]{:S(2)}, u32[]{:S(2)}) collective-permute-start(bf16[512,128]{1,0:T(8,128)(2,1)S(1)} %get-tuple-element.45), channel_id=1, source_target_pairs={{0,18},{1,19},{2,16},{3,17},{16,2},{17,3},{18,0},{19,1},{4,22},{5,... | collective-permute-start | bytes 393224 | tf_op jit(solution)/shard_map/ppermute | solution.py:297
  24.4 7.4 %collective-permute-start.8 = (bf16[512,128]{1,0:T(8,128)(2,1)S(1)}, bf16[512,128]{1,0:T(8,128)(2,1)S(1)}, u32[]{:S(2)}, u32[]{:S(2)}) collective-permute-start(bf16[512,128]{1,0:T(8,128)(2,1)S(1)} %get-tuple-element.47), channel_id=1, source_target_pairs={{0,18},{1,19},{2,16},{3,17},{16,2},{17,3},{18,0},{19,1},{4,22},{5,... | collective-permute-start | bytes 393224 | tf_op jit(solution)/shard_map/ppermute | solution.py:297
  24.8 8.7 %collective-permute-start.12 = (bf16[256,256]{1,0:T(8,128)(2,1)S(1)}, bf16[256,256]{1,0:T(8,128)(2,1)S(1)}, u32[]{:S(2)}, u32[]{:S(2)}) collective-permute-start(bf16[256,256]{1,0:T(8,128)(2,1)S(1)} %get-tuple-element.50), channel_id=1, source_target_pairs={{0,16},{1,17},{2,18},{3,19},{16,0},{17,1},{18,2},{19,3},{4,20},{5,... | collective-permute-start | bytes 393224 | tf_op jit(solution)/shard_map/ppermute | solution.py:297
  26.3 7.3 %collective-permute-start.13 = (bf16[256,256]{1,0:T(8,128)(2,1)S(1)}, bf16[256,256]{1,0:T(8,128)(2,1)S(1)}, u32[]{:S(2)}, u32[]{:S(2)}) collective-permute-start(bf16[256,256]{1,0:T(8,128)(2,1)S(1)} %get-tuple-element.51), channel_id=1, source_target_pairs={{0,2},{1,3},{2,0},{3,1},{16,18},{17,19},{18,16},{19,17},{4,6},{5,7... | collective-permute-start | bytes 393224 | tf_op jit(solution)/shard_map/ppermute | solution.py:297
  27.9 7.1 %collective-permute-start.14 = (bf16[256,256]{1,0:T(8,128)(2,1)S(1)}, bf16[256,256]{1,0:T(8,128)(2,1)S(1)}, u32[]{:S(2)}, u32[]{:S(2)}) collective-permute-start(bf16[256,256]{1,0:T(8,128)(2,1)S(1)} %get-tuple-element.52), channel_id=1, source_target_pairs={{0,17},{1,16},{2,19},{3,18},{16,1},{17,0},{18,3},{19,2},{4,21},{5,... | collective-permute-start | bytes 393224 | tf_op jit(solution)/shard_map/ppermute | solution.py:297
  27.9 7.0 %collective-permute-start.15 = (bf16[256,256]{1,0:T(8,128)(2,1)S(1)}, bf16[256,256]{1,0:T(8,128)(2,1)S(1)}, u32[]{:S(2)}, u32[]{:S(2)}) collective-permute-start(bf16[256,256]{1,0:T(8,128)(2,1)S(1)} %get-tuple-element.53), channel_id=1, source_target_pairs={{0,3},{1,2},{2,1},{3,0},{16,19},{17,18},{18,17},{19,16},{4,7},{5,6... | collective-permute-start | bytes 393224 | tf_op jit(solution)/shard_map/ppermute | solution.py:297
  31.7 3.3 %collective-permute-start.11 = (bf16[256,256]{1,0:T(8,128)(2,1)S(1)}, bf16[256,256]{1,0:T(8,128)(2,1)S(1)}, u32[]{:S(2)}, u32[]{:S(2)}) collective-permute-start(bf16[256,256]{1,0:T(8,128)(2,1)S(1)} %get-tuple-element.49), channel_id=1, source_target_pairs={{0,1},{1,0},{2,3},{3,2},{16,17},{17,16},{18,19},{19,18},{4,5},{5,4... | collective-permute-start | bytes 393224 | tf_op jit(solution)/shard_map/ppermute | solution.py:297
  33.5 1.5 %collective-permute-start.10 = (bf16[256,128]{1,0:T(8,128)(2,1)S(1)}, bf16[256,128]{1,0:T(8,128)(2,1)S(1)}, u32[]{:S(2)}, u32[]{:S(2)}) collective-permute-start(bf16[256,128]{1,0:T(8,128)(2,1)S(1)} %slice.12), channel_id=1, source_target_pairs={{0,1},{1,0},{2,3},{3,2},{16,17},{17,16},{18,19},{19,18},{4,5},{5,4... | collective-permute-start | bytes 196616 | tf_op jit(solution)/shard_map/ppermute | solution.py:297
  33.5 1.5 %collective-permute-start.9 = (bf16[256,128]{1,0:T(8,128)(2,1)S(1)}, bf16[256,128]{1,0:T(8,128)(2,1)S(1)}, u32[]{:S(2)}, u32[]{:S(2)}) collective-permute-start(bf16[256,128]{1,0:T(8,128)(2,1)S(1)} %slice.10), channel_id=1, source_target_pairs={{0,1},{1,0},{2,3},{3,2},{16,17},{17,16},{18,19},{19,18},{4,5},{5,4... | collective-permute-start | bytes 196616 | tf_op jit(solution)/shard_map/ppermute | solution.py:297

commit v21 on v20

--- a/solution.py
+++ b/solution.py
@@ -180,6 +180,7 @@
 OUTGOING = [DIAGONAL, *REST]
 INCOMING = [*OUTGOING, DIAGONAL[1:]]
 TILES = 2
+EARLY = (0, 6)
 
 
 def pack_kernel(seq_count, steps, *refs):
@@ -269,19 +270,12 @@
         out[:, pl.ds(0, turn * LANES)] = done[...]
 
 
-def unpack_kernel(seq_count, *refs):
-    diagonals, handed_on, shares = refs[:TILES], refs[TILES : 2 * TILES], refs[2 * TILES : -3]
-    first, second, sem = refs[-3:]
+def unpack_kernel(seq_count, places, *refs):
+    shares, (first, second, sem) = refs[: len(places)], refs[-3:]
     width = first.shape[3] // (2 * seq_count)
     me = device_index(seq_count)
-    pieces = [
-        (step, tile * LANES, share.at[pl.ds(0, 2 * BLK)])
-        for step, arrived in zip(DIAGONAL, (diagonals, handed_on))
-        for tile, share in enumerate(arrived)
-    ]
-    pieces += [(step, 0, share) for (step,), share in zip(REST, shares)]
     copies = []
-    for slot, (step, start, share) in enumerate(pieces):
+    for slot, ((step, start), share) in enumerate(zip(places, shares)):
         lanes = pl.ds(pl.multiple_of((me ^ step) * width + start, LANES), share.shape[1])
         for half, result in enumerate((first, second)):
             copy = pltpu.make_async_copy(
@@ -372,16 +366,26 @@
         diagonal, *shares = attend(turn, *shares)
         diagonals.append(diagonal)
     diagonals, shares, handed_on = swapped(diagonals, shares)
+    arrived = dict(zip([(group[0], 0) for group in REST], shares))
+    for step, tiles in zip(DIAGONAL, (diagonals, handed_on)):
+        arrived.update({(step, tile * LANES): share for tile, share in enumerate(tiles)})
     out_shape = jax.ShapeDtypeStruct((1, 1, BLK, width), kind)
-    return pl.pallas_call(
-        functools.partial(unpack_kernel, seq_count),
-        out_shape=[out_shape, out_shape],
-        in_specs=specs(2 * TILES + len(REST), pltpu.VMEM),
-        out_specs=specs(2, pltpu.HBM),
-        scratch_shapes=[pltpu.SemaphoreType.DMA((2, parts + 2 * TILES))],
-        compiler_params=params,
-        name="unpack",
-    )(*diagonals, *handed_on, *shares)
+
+    def unpack(places, *begun):
+        count = len(places)
+        return pl.pallas_call(
+            functools.partial(unpack_kernel, seq_count, places),
+            out_shape=[out_shape, out_shape],
+            in_specs=specs(count, pltpu.VMEM) + specs(len(begun), pltpu.HBM),
+            out_specs=specs(2, pltpu.HBM),
+            input_output_aliases={count + slot: slot for slot in range(len(begun))},
+            scratch_shapes=[pltpu.SemaphoreType.DMA((2, count))],
+            compiler_params=params,
+            name="unpack",
+        )(*(arrived[place] for place in places), *begun)
+
+    early = [place for place in arrived if place[0] in EARLY]
+    return unpack([place for place in arrived if place not in early], *unpack(early))
 
 
 def on_device(first_rows, second_rows, alignment, diffusion_mask, source_length, target_length):

time: 36.5 us -> 36.3 us (level)
  waiting for transfers between devices: 11.5 us -> 10.7 us
  Pallas kernels: 7.69 us -> 8.25 us
    ppermute x16, waiting for transfers between devices: 11.5 us -> 10.7 us  [permuted(): return lax.ppermute(share, AXES, [(dev, dev ^ step) for dev in range(8)])]
    pallas_call x1 -> x2, Pallas kernels: 1.18 us -> 1.74 us  [unpack(): pl.pallas_call(functools.partial(unpack_kernel, seq_count, places), out_s...]
  transfers between devices with their start and end apart: 16 -> 16, of which waited for: 6 -> 6; matrix products, arithmetic and copies ran while one was open for 0% -> 0% of each run, Pallas kernels for 9% -> 11%
where the time goes in v21:
time: 36.3 us; the launch traced here: 36 us
  starting transfers between devices  15 us (41%)
  waiting for transfers between devices  10.7 us (29%)
  Pallas kernels  8.25 us (23%)
  between operations  2.02 us (6%)
    ppermute x16, starting transfers between devices, permuted(): return lax.ppermute(share, AXES, [(dev, dev ^ step) for dev in range(8)])  15 us
    ppermute x16, waiting for transfers between devices, permuted(): return lax.ppermute(share, AXES, [(dev, dev ^ step) for dev in range(8)])  10.7 us
    pallas_call x2, Pallas kernels, attend(): pl.pallas_call(functools.partial(attend_kernel, seq_count, turn), out_sha...  4.07 us
    pallas_call x2, Pallas kernels, pack(): pl.pallas_call(functools.partial(pack_kernel, seq_count, groups), out_sha...  2.44 us
    pallas_call x2, Pallas kernels, unpack(): pl.pallas_call(functools.partial(unpack_kernel, seq_count, places), out_s...  1.74 us
  transfers between devices with their start and end apart: 16, of which 6 were waited for; matrix products, arithmetic and copies ran while one was open for 0% of the time, Pallas kernels for 11%

profile of v21, /device:TPU:0, one launch (start us, length us, event | category | flops | bytes accessed | tf_op | source)
XLA Modules:
  0.0 36.0 jit_solution(7748153050974854027)
XLA Ops:
  0.6 1.1 %pack.2 = bf16[512,256]{1,0:T(8,128)(2,1)S(1)} custom-call(s32[1,1,2]{2,1,0:T(1,128)} %refs_0_.2, s32[1,128]{1,0:T(1,128)} %refs_1_.3, bf16[1,1,128,2048]{3,2,1,0:T(8,128)(2,1)} %refs_2_.3, bf16[1,1,128,2048]{3,2,1,0:T(8,128)(2,1)} %refs_3_.3), custom_call_target="tpu_custom_call" | custom-call | tf_op jit(solution)/shard_map/pack/pallas_call | solution.py:325
  1.8 4.0 %collective-permute-start = (bf16[512,256]{1,0:T(8,128)(2,1)S(1)}, bf16[512,256]{1,0:T(8,128)(2,1)S(1)}, u32[]{:S(2)}, u32[]{:S(2)}) collective-permute-start(bf16[512,256]{1,0:T(8,128)(2,1)S(1)} %pack.2), channel_id=1, source_target_pairs={{0,18},{1,19},{2,16},{3,17},{16,2},{17,3},{18,0},{19,1},{4,22},{5,... | collective-permute-start | bytes 786440 | tf_op jit(solution)/shard_map/ppermute | solution.py:291
  5.7 1.3 %pack.3 = (bf16[272,256]{1,0:T(8,128)(2,1)S(1)}, bf16[272,256]{1,0:T(8,128)(2,1)S(1)}, bf16[256,256]{1,0:T(8,128)(2,1)S(1)}, bf16[272,256]{1,0:T(8,128)(2,1)S(1)...) custom-call(s32[1,1,2]{2,1,0:T(1,128)} %refs_0_.2, s32[1,128]{1,0:T(1,128)} %refs_1_.3, ...), custom_call_target="tpu_custom_call" | custom-call | tf_op jit(solution)/shard_map/pack/pallas_call | solution.py:325
  7.0 0.1 collective-permute-start.1
  7.1 0.6 %collective-permute-start.3 = (bf16[272,256]{1,0:T(8,128)(2,1)S(1)}, bf16[272,256]{1,0:T(8,128)(2,1)S(1)}, u32[]{:S(2)}, u32[]{:S(2)}) collective-permute-start(bf16[272,256]{1,0:T(8,128)(2,1)S(1)} %get-tuple-element.37), channel_id=1, source_target_pairs={{0,2},{1,3},{2,0},{3,1},{16,18},{17,19},{18,16},{19,17},{4,6},{5,7... | collective-permute-start | bytes 417800 | tf_op jit(solution)/shard_map/ppermute | solution.py:291
  7.7 1.3 %collective-permute-start.5 = (bf16[272,256]{1,0:T(8,128)(2,1)S(1)}, bf16[272,256]{1,0:T(8,128)(2,1)S(1)}, u32[]{:S(2)}, u32[]{:S(2)}) collective-permute-start(bf16[272,256]{1,0:T(8,128)(2,1)S(1)} %get-tuple-element.39), channel_id=1, source_target_pairs={{0,3},{1,2},{2,1},{3,0},{16,19},{17,18},{18,17},{19,16},{4,7},{5,6... | collective-permute-start | bytes 417800 | tf_op jit(solution)/shard_map/ppermute | solution.py:291
  9.0 0.5 %collective-permute-start.2 = (bf16[256,256]{1,0:T(8,128)(2,1)S(1)}, bf16[256,256]{1,0:T(8,128)(2,1)S(1)}, u32[]{:S(2)}, u32[]{:S(2)}) collective-permute-start(bf16[256,256]{1,0:T(8,128)(2,1)S(1)} %get-tuple-element.36), channel_id=1, source_target_pairs={{0,16},{1,17},{2,18},{3,19},{16,0},{17,1},{18,2},{19,3},{4,20},{5,... | collective-permute-start | bytes 393224 | tf_op jit(solution)/shard_map/ppermute | solution.py:291
  9.5 0.0 collective-permute-done.1.refs_2_
  9.5 1.2 %collective-permute-start.4 = (bf16[256,256]{1,0:T(8,128)(2,1)S(1)}, bf16[256,256]{1,0:T(8,128)(2,1)S(1)}, u32[]{:S(2)}, u32[]{:S(2)}) collective-permute-start(bf16[256,256]{1,0:T(8,128)(2,1)S(1)} %get-tuple-element.38), channel_id=1, source_target_pairs={{0,17},{1,16},{2,19},{3,18},{16,1},{17,0},{18,3},{19,2},{4,21},{5,... | collective-permute-start | bytes 393224 | tf_op jit(solution)/shard_map/ppermute | solution.py:291
  10.7 2.2 %collective-permute-done.refs_0_ = bf16[512,256]{1,0:T(8,128)(2,1)S(1)} collective-permute-done((bf16[512,256]{1,0:T(8,128)(2,1)S(1)}, bf16[512,256]{1,0:T(8,128)(2,1)S(1)}, u32[]{:S(2)}, u32[]{:S(2)}) %collective-permute-start) | collective-permute-done | bytes 262176 | tf_op jit(solution)/shard_map/ppermute | solution.py:291
  12.9 0.1 collective-permute-start.6
  14.2 1.3 %collective-permute-done.2.refs_3_ = bf16[256,256]{1,0:T(8,128)(2,1)S(1)} collective-permute-done((bf16[256,256]{1,0:T(8,128)(2,1)S(1)}, bf16[256,256]{1,0:T(8,128)(2,1)S(1)}, u32[]{:S(2)}, u32[]{:S(2)}) %collective-permute-start.2) | collective-permute-done | bytes 131104 | tf_op jit(solution)/shard_map/ppermute | solution.py:291
  15.5 2.2 %collective-permute-done.4.refs_5_ = bf16[256,256]{1,0:T(8,128)(2,1)S(1)} collective-permute-done((bf16[256,256]{1,0:T(8,128)(2,1)S(1)}, bf16[256,256]{1,0:T(8,128)(2,1)S(1)}, u32[]{:S(2)}, u32[]{:S(2)}) %collective-permute-start.4) | collective-permute-done | bytes 131104 | tf_op jit(solution)/shard_map/ppermute | solution.py:291
  17.7 0.0 collective-permute-done.3.refs_4_
  17.7 0.0 collective-permute-done.5.refs_6_
  17.7 0.0 collective-permute-done.6.refs_7_
  17.7 2.0 %attend.2 = (bf16[512,128]{1,0:T(8,128)(2,1)S(1)}, bf16[256,128]{1,0:T(8,128)(2,1)S(1)}, bf16[256,128]{1,0:T(8,128)(2,1)S(1)}, bf16[256,128]{1,0:T(8,128)(2,1)S(...) custom-call(s32[1]{0:T(128)S(6)} %copy.12.source_len, ...), custom_call_target="tpu_custom_call" | custom-call | flops 167772160 | bytes 1048576 | tf_op jit(solution)/shard_map/attend/pallas_call | solution.py:350
  19.7 2.6 %collective-permute-start.7 = (bf16[512,128]{1,0:T(8,128)(2,1)S(1)}, bf16[512,128]{1,0:T(8,128)(2,1)S(1)}, u32[]{:S(2)}, u32[]{:S(2)}) collective-permute-start(bf16[512,128]{1,0:T(8,128)(2,1)S(1)} %get-tuple-element.47), channel_id=1, source_target_pairs={{0,18},{1,19},{2,16},{3,17},{16,2},{17,3},{18,0},{19,1},{4,22},{5,... | collective-permute-start | bytes 393224 | tf_op jit(solution)/shard_map/ppermute | solution.py:291
  22.3 2.1 %attend.3 = (bf16[512,128]{1,0:T(8,128)(2,1)S(1)}, bf16[256,256]{1,0:T(8,128)(2,1)S(1)}, bf16[256,256]{1,0:T(8,128)(2,1)S(1)}, bf16[256,256]{1,0:T(8,128)(2,1)S(...) custom-call(s32[1]{0:T(128)S(6)} %copy.12.source_len, ...), custom_call_target="tpu_custom_call" | custom-call | flops 167772160 | bytes 1048576 | tf_op jit(solution)/shard_map/attend/pallas_call | solution.py:350
  24.4 0.5 %collective-permute-start.14 = (bf16[512,128]{1,0:T(8,128)(2,1)S(1)}, bf16[512,128]{1,0:T(8,128)(2,1)S(1)}, u32[]{:S(2)}, u32[]{:S(2)}) collective-permute-start(bf16[512,128]{1,0:T(8,128)(2,1)S(1)} %get-tuple-element.54), channel_id=1, source_target_pairs={{0,18},{1,19},{2,16},{3,17},{16,2},{17,3},{18,0},{19,1},{4,22},{5,... | collective-permute-start | bytes 393224 | tf_op jit(solution)/shard_map/ppermute | solution.py:291
  24.8 1.4 %collective-permute-start.9 = (bf16[256,256]{1,0:T(8,128)(2,1)S(1)}, bf16[256,256]{1,0:T(8,128)(2,1)S(1)}, u32[]{:S(2)}, u32[]{:S(2)}) collective-permute-start(bf16[256,256]{1,0:T(8,128)(2,1)S(1)} %get-tuple-element.49), channel_id=1, source_target_pairs={{0,16},{1,17},{2,18},{3,19},{16,0},{17,1},{18,2},{19,3},{4,20},{5,... | collective-permute-start | bytes 393224 | tf_op jit(solution)/shard_map/ppermute | solution.py:291
  26.3 1.7 %collective-permute-start.10 = (bf16[256,256]{1,0:T(8,128)(2,1)S(1)}, bf16[256,256]{1,0:T(8,128)(2,1)S(1)}, u32[]{:S(2)}, u32[]{:S(2)}) collective-permute-start(bf16[256,256]{1,0:T(8,128)(2,1)S(1)} %get-tuple-element.50), channel_id=1, source_target_pairs={{0,2},{1,3},{2,0},{3,1},{16,18},{17,19},{18,16},{19,17},{4,6},{5,7... | collective-permute-start | bytes 393224 | tf_op jit(solution)/shard_map/ppermute | solution.py:291
  27.9 0.0 collective-permute-start.11
  27.9 0.0 collective-permute-done.7.refs_1_
  27.9 0.7 %collective-permute-start.12 = (bf16[256,256]{1,0:T(8,128)(2,1)S(1)}, bf16[256,256]{1,0:T(8,128)(2,1)S(1)}, u32[]{:S(2)}, u32[]{:S(2)}) collective-permute-start(bf16[256,256]{1,0:T(8,128)(2,1)S(1)} %get-tuple-element.52), channel_id=1, source_target_pairs={{0,3},{1,2},{2,1},{3,0},{16,19},{17,18},{18,17},{19,16},{4,7},{5,6... | collective-permute-start | bytes 393224 | tf_op jit(solution)/shard_map/ppermute | solution.py:291
  28.6 3.1 %collective-permute-done.14.refs_2_ = bf16[512,128]{1,0:T(8,128)(2,1)S(1)} collective-permute-done((bf16[512,128]{1,0:T(8,128)(2,1)S(1)}, bf16[512,128]{1,0:T(8,128)(2,1)S(1)}, u32[]{:S(2)}, u32[]{:S(2)}) %collective-permute-start.14) | collective-permute-done | bytes 131104 | tf_op jit(solution)/shard_map/ppermute | solution.py:291
  31.7 0.0 collective-permute-start.8
  31.8 1.8 %collective-permute-done.9.refs_1_ = bf16[256,256]{1,0:T(8,128)(2,1)S(1)} collective-permute-done((bf16[256,256]{1,0:T(8,128)(2,1)S(1)}, bf16[256,256]{1,0:T(8,128)(2,1)S(1)}, u32[]{:S(2)}, u32[]{:S(2)}) %collective-permute-start.9) | collective-permute-done | bytes 131104 | tf_op jit(solution)/shard_map/ppermute | solution.py:291
  33.5 0.0 collective-permute-start.15
  33.5 0.0 collective-permute-done.10.refs_2_
  33.5 0.5 %collective-permute-start.13 = (bf16[256,128]{1,0:T(8,128)(2,1)S(1)}, bf16[256,128]{1,0:T(8,128)(2,1)S(1)}, u32[]{:S(2)}, u32[]{:S(2)}) collective-permute-start(bf16[256,128]{1,0:T(8,128)(2,1)S(1)} %slice.10), channel_id=1, source_target_pairs={{0,1},{1,0},{2,3},{3,2},{16,17},{17,16},{18,19},{19,18},{4,5},{5,4... | collective-permute-start | bytes 196616 | tf_op jit(solution)/shard_map/ppermute | solution.py:291
  34.0 0.7 %unpack.2 = (bf16[1,1,128,2048]{3,2,1,0:T(8,128)(2,1)}, bf16[1,1,128,2048]{3,2,1,0:T(8,128)(2,1)}) custom-call(bf16[256,256]{1,0:T(8,128)(2,1)S(1)} %get-tuple-element.55.refs_0_, bf16[512,128]{1,0:T(8,128)(2,1)S(1)} %collective-permute-done.7.refs_1_, bf16[512,128]{1,0:T(8,128)(2,1)S(1)} %collective-permute-done.14.refs_2_), custom_call_target="tpu_custom_call" | custom-call | tf_op jit(solution)/shard_map/unpack/pallas_call | solution.py:376
  34.8 0.2 collective-permute-done.11.refs_3_
  35.0 0.0 collective-permute-done.12.refs_4_
  35.0 0.0 collective-permute-done.15.refs_6_
  35.0 0.0 collective-permute-done.13.refs_5_
  35.0 0.0 collective-permute-done.8.refs_0_
  35.0 1.0 %unpack.3 = (bf16[1,1,128,2048]{3,2,1,0:T(8,128)(2,1)}, bf16[1,1,128,2048]{3,2,1,0:T(8,128)(2,1)}) custom-call(bf16[256,256]{1,0:T(8,128)(2,1)S(1)} %collective-permute-done.8.refs_0_, bf16[256,256]{1,0:T(8,128)(2,1)S(1)} %collective-permute-done.9.refs_1_, ...), custom_call_target="tpu_custom_call", output_to_operand_aliasing={{0}: (7, {}), {1}: (8, {})} | custom-call | tf_op jit(solution)/shard_map/unpack/pallas_call | solution.py:376
  (3 shorter events, 0.0 us)
Async XLA Ops:
  1.8 11.1 %collective-permute-start = (bf16[512,256]{1,0:T(8,128)(2,1)S(1)}, bf16[512,256]{1,0:T(8,128)(2,1)S(1)}, u32[]{:S(2)}, u32[]{:S(2)}) collective-permute-start(bf16[512,256]{1,0:T(8,128)(2,1)S(1)} %pack.2), channel_id=1, source_target_pairs={{0,18},{1,19},{2,16},{3,17},{16,2},{17,3},{18,0},{19,1},{4,22},{5,... | collective-permute-start | bytes 786440 | tf_op jit(solution)/shard_map/ppermute | solution.py:291
  7.0 2.5 %collective-permute-start.1 = (bf16[272,256]{1,0:T(8,128)(2,1)S(1)}, bf16[272,256]{1,0:T(8,128)(2,1)S(1)}, u32[]{:S(2)}, u32[]{:S(2)}) collective-permute-start(bf16[272,256]{1,0:T(8,128)(2,1)S(1)} %get-tuple-element.32), channel_id=1, source_target_pairs={{0,1},{1,0},{2,3},{3,2},{16,17},{17,16},{18,19},{19,18},{4,5},{5,4... | collective-permute-start | bytes 417800 | tf_op jit(solution)/shard_map/ppermute | solution.py:291
  7.1 10.6 %collective-permute-start.3 = (bf16[272,256]{1,0:T(8,128)(2,1)S(1)}, bf16[272,256]{1,0:T(8,128)(2,1)S(1)}, u32[]{:S(2)}, u32[]{:S(2)}) collective-permute-start(bf16[272,256]{1,0:T(8,128)(2,1)S(1)} %get-tuple-element.37), channel_id=1, source_target_pairs={{0,2},{1,3},{2,0},{3,1},{16,18},{17,19},{18,16},{19,17},{4,6},{5,7... | collective-permute-start | bytes 417800 | tf_op jit(solution)/shard_map/ppermute | solution.py:291
  7.7 10.0 %collective-permute-start.5 = (bf16[272,256]{1,0:T(8,128)(2,1)S(1)}, bf16[272,256]{1,0:T(8,128)(2,1)S(1)}, u32[]{:S(2)}, u32[]{:S(2)}) collective-permute-start(bf16[272,256]{1,0:T(8,128)(2,1)S(1)} %get-tuple-element.39), channel_id=1, source_target_pairs={{0,3},{1,2},{2,1},{3,0},{16,19},{17,18},{18,17},{19,16},{4,7},{5,6... | collective-permute-start | bytes 417800 | tf_op jit(solution)/shard_map/ppermute | solution.py:291
  9.0 6.5 %collective-permute-start.2 = (bf16[256,256]{1,0:T(8,128)(2,1)S(1)}, bf16[256,256]{1,0:T(8,128)(2,1)S(1)}, u32[]{:S(2)}, u32[]{:S(2)}) collective-permute-start(bf16[256,256]{1,0:T(8,128)(2,1)S(1)} %get-tuple-element.36), channel_id=1, source_target_pairs={{0,16},{1,17},{2,18},{3,19},{16,0},{17,1},{18,2},{19,3},{4,20},{5,... | collective-permute-start | bytes 393224 | tf_op jit(solution)/shard_map/ppermute | solution.py:291
  9.5 8.2 %collective-permute-start.4 = (bf16[256,256]{1,0:T(8,128)(2,1)S(1)}, bf16[256,256]{1,0:T(8,128)(2,1)S(1)}, u32[]{:S(2)}, u32[]{:S(2)}) collective-permute-start(bf16[256,256]{1,0:T(8,128)(2,1)S(1)} %get-tuple-element.38), channel_id=1, source_target_pairs={{0,17},{1,16},{2,19},{3,18},{16,1},{17,0},{18,3},{19,2},{4,21},{5,... | collective-permute-start | bytes 393224 | tf_op jit(solution)/shard_map/ppermute | solution.py:291
  12.9 4.8 %collective-permute-start.6 = (bf16[256,256]{1,0:T(8,128)(2,1)S(1)}, bf16[256,256]{1,0:T(8,128)(2,1)S(1)}, u32[]{:S(2)}, u32[]{:S(2)}) collective-permute-start(bf16[256,256]{1,0:T(8,128)(2,1)S(1)} %slice.9), channel_id=1, source_target_pairs={{0,1},{1,0},{2,3},{3,2},{16,17},{17,16},{18,19},{19,18},{4,5},{5,4... | collective-permute-start | bytes 393224 | tf_op jit(solution)/shard_map/ppermute | solution.py:291
  19.7 8.2 %collective-permute-start.7 = (bf16[512,128]{1,0:T(8,128)(2,1)S(1)}, bf16[512,128]{1,0:T(8,128)(2,1)S(1)}, u32[]{:S(2)}, u32[]{:S(2)}) collective-permute-start(bf16[512,128]{1,0:T(8,128)(2,1)S(1)} %get-tuple-element.47), channel_id=1, source_target_pairs={{0,18},{1,19},{2,16},{3,17},{16,2},{17,3},{18,0},{19,1},{4,22},{5,... | collective-permute-start | bytes 393224 | tf_op jit(solution)/shard_map/ppermute | solution.py:291
  24.4 7.4 %collective-permute-start.14 = (bf16[512,128]{1,0:T(8,128)(2,1)S(1)}, bf16[512,128]{1,0:T(8,128)(2,1)S(1)}, u32[]{:S(2)}, u32[]{:S(2)}) collective-permute-start(bf16[512,128]{1,0:T(8,128)(2,1)S(1)} %get-tuple-element.54), channel_id=1, source_target_pairs={{0,18},{1,19},{2,16},{3,17},{16,2},{17,3},{18,0},{19,1},{4,22},{5,... | collective-permute-start | bytes 393224 | tf_op jit(solution)/shard_map/ppermute | solution.py:291
  24.8 8.7 %collective-permute-start.9 = (bf16[256,256]{1,0:T(8,128)(2,1)S(1)}, bf16[256,256]{1,0:T(8,128)(2,1)S(1)}, u32[]{:S(2)}, u32[]{:S(2)}) collective-permute-start(bf16[256,256]{1,0:T(8,128)(2,1)S(1)} %get-tuple-element.49), channel_id=1, source_target_pairs={{0,16},{1,17},{2,18},{3,19},{16,0},{17,1},{18,2},{19,3},{4,20},{5,... | collective-permute-start | bytes 393224 | tf_op jit(solution)/shard_map/ppermute | solution.py:291
  26.3 7.3 %collective-permute-start.10 = (bf16[256,256]{1,0:T(8,128)(2,1)S(1)}, bf16[256,256]{1,0:T(8,128)(2,1)S(1)}, u32[]{:S(2)}, u32[]{:S(2)}) collective-permute-start(bf16[256,256]{1,0:T(8,128)(2,1)S(1)} %get-tuple-element.50), channel_id=1, source_target_pairs={{0,2},{1,3},{2,0},{3,1},{16,18},{17,19},{18,16},{19,17},{4,6},{5,7... | collective-permute-start | bytes 393224 | tf_op jit(solution)/shard_map/ppermute | solution.py:291
  27.9 7.1 %collective-permute-start.11 = (bf16[256,256]{1,0:T(8,128)(2,1)S(1)}, bf16[256,256]{1,0:T(8,128)(2,1)S(1)}, u32[]{:S(2)}, u32[]{:S(2)}) collective-permute-start(bf16[256,256]{1,0:T(8,128)(2,1)S(1)} %get-tuple-element.51), channel_id=1, source_target_pairs={{0,17},{1,16},{2,19},{3,18},{16,1},{17,0},{18,3},{19,2},{4,21},{5,... | collective-permute-start | bytes 393224 | tf_op jit(solution)/shard_map/ppermute | solution.py:291
  27.9 7.0 %collective-permute-start.12 = (bf16[256,256]{1,0:T(8,128)(2,1)S(1)}, bf16[256,256]{1,0:T(8,128)(2,1)S(1)}, u32[]{:S(2)}, u32[]{:S(2)}) collective-permute-start(bf16[256,256]{1,0:T(8,128)(2,1)S(1)} %get-tuple-element.52), channel_id=1, source_target_pairs={{0,3},{1,2},{2,1},{3,0},{16,19},{17,18},{18,17},{19,16},{4,7},{5,6... | collective-permute-start | bytes 393224 | tf_op jit(solution)/shard_map/ppermute | solution.py:291
  31.7 3.3 %collective-permute-start.8 = (bf16[256,256]{1,0:T(8,128)(2,1)S(1)}, bf16[256,256]{1,0:T(8,128)(2,1)S(1)}, u32[]{:S(2)}, u32[]{:S(2)}) collective-permute-start(bf16[256,256]{1,0:T(8,128)(2,1)S(1)} %get-tuple-element.48), channel_id=1, source_target_pairs={{0,1},{1,0},{2,3},{3,2},{16,17},{17,16},{18,19},{19,18},{4,5},{5,4... | collective-permute-start | bytes 393224 | tf_op jit(solution)/shard_map/ppermute | solution.py:291
  33.5 1.5 %collective-permute-start.15 = (bf16[256,128]{1,0:T(8,128)(2,1)S(1)}, bf16[256,128]{1,0:T(8,128)(2,1)S(1)}, u32[]{:S(2)}, u32[]{:S(2)}) collective-permute-start(bf16[256,128]{1,0:T(8,128)(2,1)S(1)} %slice.12), channel_id=1, source_target_pairs={{0,1},{1,0},{2,3},{3,2},{16,17},{17,16},{18,19},{19,18},{4,5},{5,4... | collective-permute-start | bytes 196616 | tf_op jit(solution)/shard_map/ppermute | solution.py:291
  33.5 1.5 %collective-permute-start.13 = (bf16[256,128]{1,0:T(8,128)(2,1)S(1)}, bf16[256,128]{1,0:T(8,128)(2,1)S(1)}, u32[]{:S(2)}, u32[]{:S(2)}) collective-permute-start(bf16[256,128]{1,0:T(8,128)(2,1)S(1)} %slice.10), channel_id=1, source_target_pairs={{0,1},{1,0},{2,3},{3,2},{16,17},{17,16},{18,19},{19,18},{4,5},{5,4... | collective-permute-start | bytes 196616 | tf_op jit(solution)/shard_map/ppermute | solution.py:291

commit v22 on v20

--- a/solution.py
+++ b/solution.py
@@ -175,7 +175,7 @@
 
 DIAGONAL = (6, 7)
 OWN, NEAR = (0,), (1,)
-ACROSS = [(4,), (2,), (5,), (3,)]
+ACROSS = [(4,), (5,), (2,), (3,)]
 REST = [OWN, NEAR, *ACROSS]
 OUTGOING = [DIAGONAL, *REST]
 INCOMING = [*OUTGOING, DIAGONAL[1:]]

time: 36.5 us -> 37.8 us (1.036)
  waiting for transfers between devices: 11.5 us -> 13.1 us
    ppermute x16, waiting for transfers between devices: 11.5 us -> 13.1 us  [permuted(): return lax.ppermute(share, AXES, [(dev, dev ^ step) for dev in range(8)])]
  transfers between devices with their start and end apart: 16 -> 16, of which waited for: 6 -> 7; matrix products, arithmetic and copies ran while one was open for 0% -> 0% of each run, Pallas kernels for 9% -> 9%
where the time goes in v22:
time: 37.8 us; the launch traced here: 37.5 us
  starting transfers between devices  14.7 us (39%)
  waiting for transfers between devices  13.1 us (35%)
  Pallas kernels  7.67 us (20%)
  between operations  2.01 us (5%)
    ppermute x16, starting transfers between devices, permuted(): return lax.ppermute(share, AXES, [(dev, dev ^ step) for dev in range(8)])  14.7 us
    ppermute x16, waiting for transfers between devices, permuted(): return lax.ppermute(share, AXES, [(dev, dev ^ step) for dev in range(8)])  13.1 us
    pallas_call x2, Pallas kernels, attend(): pl.pallas_call(functools.partial(attend_kernel, seq_count, turn), out_sha...  4.07 us
    pallas_call x2, Pallas kernels, pack(): pl.pallas_call(functools.partial(pack_kernel, seq_count, groups), out_sha...  2.44 us
    pallas_call x1, Pallas kernels, by_pairs(): pl.pallas_call(functools.partial(unpack_kernel, seq_count), out_shape=[ou...  1.16 us
  transfers between devices with their start and end apart: 16, of which 7 were waited for; matrix products, arithmetic and copies ran while one was open for 0% of the time, Pallas kernels for 9%

profile of v22, /device:TPU:0, one launch (start us, length us, event | category | flops | bytes accessed | tf_op | source)
XLA Modules:
  0.0 37.5 jit_solution(27002372096926020)
XLA Ops:
  0.6 1.1 %pack.2 = bf16[512,256]{1,0:T(8,128)(2,1)S(1)} custom-call(s32[1,1,2]{2,1,0:T(1,128)} %refs_0_.2, s32[1,128]{1,0:T(1,128)} %refs_1_.3, bf16[1,1,128,2048]{3,2,1,0:T(8,128)(2,1)} %refs_2_.3, bf16[1,1,128,2048]{3,2,1,0:T(8,128)(2,1)} %refs_3_.3), custom_call_target="tpu_custom_call" | custom-call | tf_op jit(solution)/shard_map/pack/pallas_call | solution.py:331
  1.8 4.0 %collective-permute-start = (bf16[512,256]{1,0:T(8,128)(2,1)S(1)}, bf16[512,256]{1,0:T(8,128)(2,1)S(1)}, u32[]{:S(2)}, u32[]{:S(2)}) collective-permute-start(bf16[512,256]{1,0:T(8,128)(2,1)S(1)} %pack.2), channel_id=1, source_target_pairs={{0,18},{1,19},{2,16},{3,17},{16,2},{17,3},{18,0},{19,1},{4,22},{5,... | collective-permute-start | bytes 786440 | tf_op jit(solution)/shard_map/ppermute | solution.py:297
  5.7 1.3 %pack.3 = (bf16[272,256]{1,0:T(8,128)(2,1)S(1)}, bf16[272,256]{1,0:T(8,128)(2,1)S(1)}, bf16[256,256]{1,0:T(8,128)(2,1)S(1)}, bf16[256,256]{1,0:T(8,128)(2,1)S(1)...) custom-call(s32[1,1,2]{2,1,0:T(1,128)} %refs_0_.2, s32[1,128]{1,0:T(1,128)} %refs_1_.3, ...), custom_call_target="tpu_custom_call" | custom-call | tf_op jit(solution)/shard_map/pack/pallas_call | solution.py:331
  7.0 0.1 collective-permute-start.1
  7.1 0.6 %collective-permute-start.4 = (bf16[272,256]{1,0:T(8,128)(2,1)S(1)}, bf16[272,256]{1,0:T(8,128)(2,1)S(1)}, u32[]{:S(2)}, u32[]{:S(2)}) collective-permute-start(bf16[272,256]{1,0:T(8,128)(2,1)S(1)} %get-tuple-element.36), channel_id=1, source_target_pairs={{0,2},{1,3},{2,0},{3,1},{16,18},{17,19},{18,16},{19,17},{4,6},{5,7... | collective-permute-start | bytes 417800 | tf_op jit(solution)/shard_map/ppermute | solution.py:297
  7.7 1.3 %collective-permute-start.5 = (bf16[272,256]{1,0:T(8,128)(2,1)S(1)}, bf16[272,256]{1,0:T(8,128)(2,1)S(1)}, u32[]{:S(2)}, u32[]{:S(2)}) collective-permute-start(bf16[272,256]{1,0:T(8,128)(2,1)S(1)} %get-tuple-element.37), channel_id=1, source_target_pairs={{0,3},{1,2},{2,1},{3,0},{16,19},{17,18},{18,17},{19,16},{4,7},{5,6... | collective-permute-start | bytes 417800 | tf_op jit(solution)/shard_map/ppermute | solution.py:297
  9.0 0.5 %collective-permute-start.2 = (bf16[256,256]{1,0:T(8,128)(2,1)S(1)}, bf16[256,256]{1,0:T(8,128)(2,1)S(1)}, u32[]{:S(2)}, u32[]{:S(2)}) collective-permute-start(bf16[256,256]{1,0:T(8,128)(2,1)S(1)} %get-tuple-element.34), channel_id=1, source_target_pairs={{0,16},{1,17},{2,18},{3,19},{16,0},{17,1},{18,2},{19,3},{4,20},{5,... | collective-permute-start | bytes 393224 | tf_op jit(solution)/shard_map/ppermute | solution.py:297
  9.5 0.0 collective-permute-done.1.refs_2_
  9.5 1.2 %collective-permute-start.3 = (bf16[256,256]{1,0:T(8,128)(2,1)S(1)}, bf16[256,256]{1,0:T(8,128)(2,1)S(1)}, u32[]{:S(2)}, u32[]{:S(2)}) collective-permute-start(bf16[256,256]{1,0:T(8,128)(2,1)S(1)} %get-tuple-element.35), channel_id=1, source_target_pairs={{0,17},{1,16},{2,19},{3,18},{16,1},{17,0},{18,3},{19,2},{4,21},{5,... | collective-permute-start | bytes 393224 | tf_op jit(solution)/shard_map/ppermute | solution.py:297
  10.7 2.2 %collective-permute-done.refs_0_ = bf16[512,256]{1,0:T(8,128)(2,1)S(1)} collective-permute-done((bf16[512,256]{1,0:T(8,128)(2,1)S(1)}, bf16[512,256]{1,0:T(8,128)(2,1)S(1)}, u32[]{:S(2)}, u32[]{:S(2)}) %collective-permute-start) | collective-permute-done | bytes 262176 | tf_op jit(solution)/shard_map/ppermute | solution.py:297
  12.9 0.1 collective-permute-start.6
  14.2 1.3 %collective-permute-done.2.refs_3_ = bf16[256,256]{1,0:T(8,128)(2,1)S(1)} collective-permute-done((bf16[256,256]{1,0:T(8,128)(2,1)S(1)}, bf16[256,256]{1,0:T(8,128)(2,1)S(1)}, u32[]{:S(2)}, u32[]{:S(2)}) %collective-permute-start.2) | collective-permute-done | bytes 131104 | tf_op jit(solution)/shard_map/ppermute | solution.py:297
  15.5 2.2 %collective-permute-done.3.refs_4_ = bf16[256,256]{1,0:T(8,128)(2,1)S(1)} collective-permute-done((bf16[256,256]{1,0:T(8,128)(2,1)S(1)}, bf16[256,256]{1,0:T(8,128)(2,1)S(1)}, u32[]{:S(2)}, u32[]{:S(2)}) %collective-permute-start.3) | collective-permute-done | bytes 131104 | tf_op jit(solution)/shard_map/ppermute | solution.py:297
  17.7 0.0 collective-permute-done.4.refs_5_
  17.7 0.0 collective-permute-done.5.refs_6_
  17.7 0.0 collective-permute-done.6.refs_7_
  17.7 2.0 %attend.2 = (bf16[512,128]{1,0:T(8,128)(2,1)S(1)}, bf16[256,128]{1,0:T(8,128)(2,1)S(1)}, bf16[256,128]{1,0:T(8,128)(2,1)S(1)}, bf16[256,128]{1,0:T(8,128)(2,1)S(...) custom-call(s32[1]{0:T(128)S(6)} %copy.8.source_len, ...), custom_call_target="tpu_custom_call" | custom-call | flops 167772160 | bytes 1048576 | tf_op jit(solution)/shard_map/attend/pallas_call | solution.py:356
  19.7 2.6 %collective-permute-start.7 = (bf16[512,128]{1,0:T(8,128)(2,1)S(1)}, bf16[512,128]{1,0:T(8,128)(2,1)S(1)}, u32[]{:S(2)}, u32[]{:S(2)}) collective-permute-start(bf16[512,128]{1,0:T(8,128)(2,1)S(1)} %get-tuple-element.45), channel_id=1, source_target_pairs={{0,18},{1,19},{2,16},{3,17},{16,2},{17,3},{18,0},{19,1},{4,22},{5,... | collective-permute-start | bytes 393224 | tf_op jit(solution)/shard_map/ppermute | solution.py:297
  22.3 2.1 %attend.3 = (bf16[512,128]{1,0:T(8,128)(2,1)S(1)}, bf16[256,256]{1,0:T(8,128)(2,1)S(1)}, bf16[256,256]{1,0:T(8,128)(2,1)S(1)}, bf16[256,256]{1,0:T(8,128)(2,1)S(...) custom-call(s32[1]{0:T(128)S(6)} %copy.8.source_len, ...), custom_call_target="tpu_custom_call" | custom-call | flops 167772160 | bytes 1048576 | tf_op jit(solution)/shard_map/attend/pallas_call | solution.py:356
  24.4 0.5 %collective-permute-start.8 = (bf16[512,128]{1,0:T(8,128)(2,1)S(1)}, bf16[512,128]{1,0:T(8,128)(2,1)S(1)}, u32[]{:S(2)}, u32[]{:S(2)}) collective-permute-start(bf16[512,128]{1,0:T(8,128)(2,1)S(1)} %get-tuple-element.47), channel_id=1, source_target_pairs={{0,18},{1,19},{2,16},{3,17},{16,2},{17,3},{18,0},{19,1},{4,22},{5,... | collective-permute-start | bytes 393224 | tf_op jit(solution)/shard_map/ppermute | solution.py:297
  24.8 1.4 %collective-permute-start.12 = (bf16[256,256]{1,0:T(8,128)(2,1)S(1)}, bf16[256,256]{1,0:T(8,128)(2,1)S(1)}, u32[]{:S(2)}, u32[]{:S(2)}) collective-permute-start(bf16[256,256]{1,0:T(8,128)(2,1)S(1)} %get-tuple-element.50), channel_id=1, source_target_pairs={{0,16},{1,17},{2,18},{3,19},{16,0},{17,1},{18,2},{19,3},{4,20},{5,... | collective-permute-start | bytes 393224 | tf_op jit(solution)/shard_map/ppermute | solution.py:297
  26.3 0.0 collective-permute-start.13
  26.3 1.7 %collective-permute-start.14 = (bf16[256,256]{1,0:T(8,128)(2,1)S(1)}, bf16[256,256]{1,0:T(8,128)(2,1)S(1)}, u32[]{:S(2)}, u32[]{:S(2)}) collective-permute-start(bf16[256,256]{1,0:T(8,128)(2,1)S(1)} %get-tuple-element.52), channel_id=1, source_target_pairs={{0,2},{1,3},{2,0},{3,1},{16,18},{17,19},{18,16},{19,17},{4,6},{5,7... | collective-permute-start | bytes 393224 | tf_op jit(solution)/shard_map/ppermute | solution.py:297
  27.9 0.0 collective-permute-done.7.refs_0_
  27.9 0.4 %collective-permute-start.15 = (bf16[256,256]{1,0:T(8,128)(2,1)S(1)}, bf16[256,256]{1,0:T(8,128)(2,1)S(1)}, u32[]{:S(2)}, u32[]{:S(2)}) collective-permute-start(bf16[256,256]{1,0:T(8,128)(2,1)S(1)} %get-tuple-element.53), channel_id=1, source_target_pairs={{0,3},{1,2},{2,1},{3,0},{16,19},{17,18},{18,17},{19,16},{4,7},{5,6... | collective-permute-start | bytes 393224 | tf_op jit(solution)/shard_map/ppermute | solution.py:297
  28.3 2.4 %collective-permute-done.8.refs_1_ = bf16[512,128]{1,0:T(8,128)(2,1)S(1)} collective-permute-done((bf16[512,128]{1,0:T(8,128)(2,1)S(1)}, bf16[512,128]{1,0:T(8,128)(2,1)S(1)}, u32[]{:S(2)}, u32[]{:S(2)}) %collective-permute-start.8) | collective-permute-done | bytes 131104 | tf_op jit(solution)/shard_map/ppermute | solution.py:297
  30.8 0.0 collective-permute-start.11
  30.8 2.7 %collective-permute-done.12.refs_6_ = bf16[256,256]{1,0:T(8,128)(2,1)S(1)} collective-permute-done((bf16[256,256]{1,0:T(8,128)(2,1)S(1)}, bf16[256,256]{1,0:T(8,128)(2,1)S(1)}, u32[]{:S(2)}, u32[]{:S(2)}) %collective-permute-start.12) | collective-permute-done | bytes 131104 | tf_op jit(solution)/shard_map/ppermute | solution.py:297
  33.5 0.0 collective-permute-start.10
  33.5 1.5 %collective-permute-done.13.refs_7_ = bf16[256,256]{1,0:T(8,128)(2,1)S(1)} collective-permute-done((bf16[256,256]{1,0:T(8,128)(2,1)S(1)}, bf16[256,256]{1,0:T(8,128)(2,1)S(1)}, u32[]{:S(2)}, u32[]{:S(2)}) %collective-permute-start.13) | collective-permute-done | bytes 131104 | tf_op jit(solution)/shard_map/ppermute | solution.py:297
  35.0 0.5 %collective-permute-start.9 = (bf16[256,128]{1,0:T(8,128)(2,1)S(1)}, bf16[256,128]{1,0:T(8,128)(2,1)S(1)}, u32[]{:S(2)}, u32[]{:S(2)}) collective-permute-start(bf16[256,128]{1,0:T(8,128)(2,1)S(1)} %slice.10), channel_id=1, source_target_pairs={{0,1},{1,0},{2,3},{3,2},{16,17},{17,16},{18,19},{19,18},{4,5},{5,4... | collective-permute-start | bytes 196616 | tf_op jit(solution)/shard_map/ppermute | solution.py:297
  35.5 0.0 collective-permute-done.14.refs_8_
  35.5 0.0 collective-permute-done.15.refs_9_
  35.5 0.0 collective-permute-done.10.refs_3_
  35.5 0.9 %collective-permute-done.9.refs_2_ = bf16[256,128]{1,0:T(8,128)(2,1)S(1)} collective-permute-done((bf16[256,128]{1,0:T(8,128)(2,1)S(1)}, bf16[256,128]{1,0:T(8,128)(2,1)S(1)}, u32[]{:S(2)}, u32[]{:S(2)}) %collective-permute-start.9) | collective-permute-done | bytes 65568 | tf_op jit(solution)/shard_map/ppermute | solution.py:297
  36.4 0.0 collective-permute-done.11.refs_5_
  36.4 1.2 %unpack.1 = (bf16[1,1,128,2048]{3,2,1,0:T(8,128)(2,1)}, bf16[1,1,128,2048]{3,2,1,0:T(8,128)(2,1)}) custom-call(bf16[512,128]{1,0:T(8,128)(2,1)S(1)} %collective-permute-done.7.refs_0_, bf16[512,128]{1,0:T(8,128)(2,1)S(1)} %collective-permute-done.8.refs_1_, bf16[256,128]{1,0:T(8,128)(2,1)S(1)} %collective-permute-done.9.refs_2_, ...), custom_call_target="tpu_custom_call" | custom-call | tf_op jit(solution)/shard_map/unpack/pallas_call | solution.py:376
  (3 shorter events, 0.0 us)
Async XLA Ops:
  1.8 11.1 %collective-permute-start = (bf16[512,256]{1,0:T(8,128)(2,1)S(1)}, bf16[512,256]{1,0:T(8,128)(2,1)S(1)}, u32[]{:S(2)}, u32[]{:S(2)}) collective-permute-start(bf16[512,256]{1,0:T(8,128)(2,1)S(1)} %pack.2), channel_id=1, source_target_pairs={{0,18},{1,19},{2,16},{3,17},{16,2},{17,3},{18,0},{19,1},{4,22},{5,... | collective-permute-start | bytes 786440 | tf_op jit(solution)/shard_map/ppermute | solution.py:297
  7.0 2.5 %collective-permute-start.1 = (bf16[272,256]{1,0:T(8,128)(2,1)S(1)}, bf16[272,256]{1,0:T(8,128)(2,1)S(1)}, u32[]{:S(2)}, u32[]{:S(2)}) collective-permute-start(bf16[272,256]{1,0:T(8,128)(2,1)S(1)} %get-tuple-element.30), channel_id=1, source_target_pairs={{0,1},{1,0},{2,3},{3,2},{16,17},{17,16},{18,19},{19,18},{4,5},{5,4... | collective-permute-start | bytes 417800 | tf_op jit(solution)/shard_map/ppermute | solution.py:297
  7.1 10.6 %collective-permute-start.4 = (bf16[272,256]{1,0:T(8,128)(2,1)S(1)}, bf16[272,256]{1,0:T(8,128)(2,1)S(1)}, u32[]{:S(2)}, u32[]{:S(2)}) collective-permute-start(bf16[272,256]{1,0:T(8,128)(2,1)S(1)} %get-tuple-element.36), channel_id=1, source_target_pairs={{0,2},{1,3},{2,0},{3,1},{16,18},{17,19},{18,16},{19,17},{4,6},{5,7... | collective-permute-start | bytes 417800 | tf_op jit(solution)/shard_map/ppermute | solution.py:297
  7.7 10.0 %collective-permute-start.5 = (bf16[272,256]{1,0:T(8,128)(2,1)S(1)}, bf16[272,256]{1,0:T(8,128)(2,1)S(1)}, u32[]{:S(2)}, u32[]{:S(2)}) collective-permute-start(bf16[272,256]{1,0:T(8,128)(2,1)S(1)} %get-tuple-element.37), channel_id=1, source_target_pairs={{0,3},{1,2},{2,1},{3,0},{16,19},{17,18},{18,17},{19,16},{4,7},{5,6... | collective-permute-start | bytes 417800 | tf_op jit(solution)/shard_map/ppermute | solution.py:297
  9.0 6.5 %collective-permute-start.2 = (bf16[256,256]{1,0:T(8,128)(2,1)S(1)}, bf16[256,256]{1,0:T(8,128)(2,1)S(1)}, u32[]{:S(2)}, u32[]{:S(2)}) collective-permute-start(bf16[256,256]{1,0:T(8,128)(2,1)S(1)} %get-tuple-element.34), channel_id=1, source_target_pairs={{0,16},{1,17},{2,18},{3,19},{16,0},{17,1},{18,2},{19,3},{4,20},{5,... | collective-permute-start | bytes 393224 | tf_op jit(solution)/shard_map/ppermute | solution.py:297
  9.5 8.2 %collective-permute-start.3 = (bf16[256,256]{1,0:T(8,128)(2,1)S(1)}, bf16[256,256]{1,0:T(8,128)(2,1)S(1)}, u32[]{:S(2)}, u32[]{:S(2)}) collective-permute-start(bf16[256,256]{1,0:T(8,128)(2,1)S(1)} %get-tuple-element.35), channel_id=1, source_target_pairs={{0,17},{1,16},{2,19},{3,18},{16,1},{17,0},{18,3},{19,2},{4,21},{5,... | collective-permute-start | bytes 393224 | tf_op jit(solution)/shard_map/ppermute | solution.py:297
  12.9 4.8 %collective-permute-start.6 = (bf16[256,256]{1,0:T(8,128)(2,1)S(1)}, bf16[256,256]{1,0:T(8,128)(2,1)S(1)}, u32[]{:S(2)}, u32[]{:S(2)}) collective-permute-start(bf16[256,256]{1,0:T(8,128)(2,1)S(1)} %slice.9), channel_id=1, source_target_pairs={{0,1},{1,0},{2,3},{3,2},{16,17},{17,16},{18,19},{19,18},{4,5},{5,4... | collective-permute-start | bytes 393224 | tf_op jit(solution)/shard_map/ppermute | solution.py:297
  19.7 8.2 %collective-permute-start.7 = (bf16[512,128]{1,0:T(8,128)(2,1)S(1)}, bf16[512,128]{1,0:T(8,128)(2,1)S(1)}, u32[]{:S(2)}, u32[]{:S(2)}) collective-permute-start(bf16[512,128]{1,0:T(8,128)(2,1)S(1)} %get-tuple-element.45), channel_id=1, source_target_pairs={{0,18},{1,19},{2,16},{3,17},{16,2},{17,3},{18,0},{19,1},{4,22},{5,... | collective-permute-start | bytes 393224 | tf_op jit(solution)/shard_map/ppermute | solution.py:297
  24.4 6.4 %collective-permute-start.8 = (bf16[512,128]{1,0:T(8,128)(2,1)S(1)}, bf16[512,128]{1,0:T(8,128)(2,1)S(1)}, u32[]{:S(2)}, u32[]{:S(2)}) collective-permute-start(bf16[512,128]{1,0:T(8,128)(2,1)S(1)} %get-tuple-element.47), channel_id=1, source_target_pairs={{0,18},{1,19},{2,16},{3,17},{16,2},{17,3},{18,0},{19,1},{4,22},{5,... | collective-permute-start | bytes 393224 | tf_op jit(solution)/shard_map/ppermute | solution.py:297
  24.8 8.7 %collective-permute-start.12 = (bf16[256,256]{1,0:T(8,128)(2,1)S(1)}, bf16[256,256]{1,0:T(8,128)(2,1)S(1)}, u32[]{:S(2)}, u32[]{:S(2)}) collective-permute-start(bf16[256,256]{1,0:T(8,128)(2,1)S(1)} %get-tuple-element.50), channel_id=1, source_target_pairs={{0,16},{1,17},{2,18},{3,19},{16,0},{17,1},{18,2},{19,3},{4,20},{5,... | collective-permute-start | bytes 393224 | tf_op jit(solution)/shard_map/ppermute | solution.py:297
  26.3 8.7 %collective-permute-start.13 = (bf16[256,256]{1,0:T(8,128)(2,1)S(1)}, bf16[256,256]{1,0:T(8,128)(2,1)S(1)}, u32[]{:S(2)}, u32[]{:S(2)}) collective-permute-start(bf16[256,256]{1,0:T(8,128)(2,1)S(1)} %get-tuple-element.51), channel_id=1, source_target_pairs={{0,17},{1,16},{2,19},{3,18},{16,1},{17,0},{18,3},{19,2},{4,21},{5,... | collective-permute-start | bytes 393224 | tf_op jit(solution)/shard_map/ppermute | solution.py:297
  26.3 9.2 %collective-permute-start.14 = (bf16[256,256]{1,0:T(8,128)(2,1)S(1)}, bf16[256,256]{1,0:T(8,128)(2,1)S(1)}, u32[]{:S(2)}, u32[]{:S(2)}) collective-permute-start(bf16[256,256]{1,0:T(8,128)(2,1)S(1)} %get-tuple-element.52), channel_id=1, source_target_pairs={{0,2},{1,3},{2,0},{3,1},{16,18},{17,19},{18,16},{19,17},{4,6},{5,7... | collective-permute-start | bytes 393224 | tf_op jit(solution)/shard_map/ppermute | solution.py:297
  27.9 7.5 %collective-permute-start.15 = (bf16[256,256]{1,0:T(8,128)(2,1)S(1)}, bf16[256,256]{1,0:T(8,128)(2,1)S(1)}, u32[]{:S(2)}, u32[]{:S(2)}) collective-permute-start(bf16[256,256]{1,0:T(8,128)(2,1)S(1)} %get-tuple-element.53), channel_id=1, source_target_pairs={{0,3},{1,2},{2,1},{3,0},{16,19},{17,18},{18,17},{19,16},{4,7},{5,6... | collective-permute-start | bytes 393224 | tf_op jit(solution)/shard_map/ppermute | solution.py:297
  30.8 5.6 %collective-permute-start.11 = (bf16[256,256]{1,0:T(8,128)(2,1)S(1)}, bf16[256,256]{1,0:T(8,128)(2,1)S(1)}, u32[]{:S(2)}, u32[]{:S(2)}) collective-permute-start(bf16[256,256]{1,0:T(8,128)(2,1)S(1)} %get-tuple-element.49), channel_id=1, source_target_pairs={{0,1},{1,0},{2,3},{3,2},{16,17},{17,16},{18,19},{19,18},{4,5},{5,4... | collective-permute-start | bytes 393224 | tf_op jit(solution)/shard_map/ppermute | solution.py:297
  33.5 2.0 %collective-permute-start.10 = (bf16[256,128]{1,0:T(8,128)(2,1)S(1)}, bf16[256,128]{1,0:T(8,128)(2,1)S(1)}, u32[]{:S(2)}, u32[]{:S(2)}) collective-permute-start(bf16[256,128]{1,0:T(8,128)(2,1)S(1)} %slice.12), channel_id=1, source_target_pairs={{0,1},{1,0},{2,3},{3,2},{16,17},{17,16},{18,19},{19,18},{4,5},{5,4... | collective-permute-start | bytes 196616 | tf_op jit(solution)/shard_map/ppermute | solution.py:297
  35.0 1.4 %collective-permute-start.9 = (bf16[256,128]{1,0:T(8,128)(2,1)S(1)}, bf16[256,128]{1,0:T(8,128)(2,1)S(1)}, u32[]{:S(2)}, u32[]{:S(2)}) collective-permute-start(bf16[256,128]{1,0:T(8,128)(2,1)S(1)} %slice.10), channel_id=1, source_target_pairs={{0,1},{1,0},{2,3},{3,2},{16,17},{17,16},{18,19},{19,18},{4,5},{5,4... | collective-permute-start | bytes 196616 | tf_op jit(solution)/shard_map/ppermute | solution.py:297

commit v23 on v20

--- a/solution.py
+++ b/solution.py
@@ -180,6 +180,7 @@
 OUTGOING = [DIAGONAL, *REST]
 INCOMING = [*OUTGOING, DIAGONAL[1:]]
 TILES = 2
+LISTED = (0, 1, 6, 3)
 
 
 def pack_kernel(seq_count, steps, *refs):
@@ -220,7 +221,7 @@
     tail = jnp.full((TAIL, share), code, jnp.int32).astype(jnp.float32).astype(jnp.bfloat16)
     for out in outs:
         if out.shape[0] % (2 * BLK):
-            out[2 * BLK :] = tail
+            out[out.shape[0] - TAIL :] = tail
     for piece, pair in zip(pieces, copies):
         for copy in pair:
             copy.wait()
@@ -233,15 +234,14 @@
     outs = refs[parts + len(before) : parts + len(before) + 1 + rest]
     rows, result, key_grad, value_grad, turned, lists = refs[parts + len(before) + 1 + rest :]
     me = device_index(seq_count)
-    here = me % seq_count
     lanes = pl.ds(turn * LANES, LANES)
     for (step, *_), share in zip(INCOMING, shares):
         source = me ^ step
         rows[source, 0] = share[pl.ds(0, BLK), lanes]
         rows[source, 1] = share[pl.ds(BLK, BLK), lanes]
-        if step < seq_count:
-            tail = share[pl.ds(2 * BLK, TAIL), lanes].astype(jnp.float32)
-            lists[here ^ step] = jnp.max(tail).astype(jnp.int32)
+        if step in LISTED:
+            tail = share[pl.ds(share.shape[0] - TAIL, TAIL), lanes].astype(jnp.float32)
+            lists[source % seq_count] = jnp.max(tail).astype(jnp.int32)
 
     def listed(block, slot):
         code = lists[block]
@@ -306,7 +306,7 @@
     moved[NEAR] = permuted(held[NEAR], NEAR[0])
     if len(diagonals) == 1:
         diagonals[0], moved[NEAR] = lax.optimization_barrier((diagonals[0], moved[NEAR]))
-    handed_on = [permuted(share[share.shape[0] // 2 :], NEAR[0]) for share in diagonals]
+    handed_on = [permuted(share[2 * BLK : 4 * BLK], NEAR[0]) for share in diagonals]
     return diagonals, [held[OWN], moved[NEAR], *(moved[group] for group in ACROSS)], handed_on
 
 
@@ -322,7 +322,7 @@
     def sizes(groups, tail):
         return [
             jax.ShapeDtypeStruct(
-                (len(group) * 2 * BLK + (tail if group[0] < seq_count else 0), share), kind
+                (len(group) * 2 * BLK + (tail if group[0] in LISTED else 0), share), kind
             )
             for group in groups
         ]

time: 36.5 us -> 36.8 us (level)
  waiting for transfers between devices: 11.5 us -> 12.5 us
  starting transfers between devices: 15 us -> 14.3 us
    ppermute x16, waiting for transfers between devices: 11.5 us -> 12.5 us  [permuted(): return lax.ppermute(share, AXES, [(dev, dev ^ step) for dev in range(8)])]
    ppermute x16, starting transfers between devices: 15 us -> 14.3 us  [permuted(): return lax.ppermute(share, AXES, [(dev, dev ^ step) for dev in range(8)])]
  transfers between devices with their start and end apart: 16 -> 16, of which waited for: 6 -> 9; matrix products, arithmetic and copies ran while one was open for 0% -> 0% of each run, Pallas kernels for 9% -> 9%
where the time goes in v23:
time: 36.8 us; the launch traced here: 36.5 us
  starting transfers between devices  14.3 us (39%)
  waiting for transfers between devices  12.5 us (34%)
  Pallas kernels  7.68 us (21%)
  between operations  2.01 us (5%)
    ppermute x16, starting transfers between devices, permuted(): return lax.ppermute(share, AXES, [(dev, dev ^ step) for dev in range(8)])  14.3 us
    ppermute x16, waiting for transfers between devices, permuted(): return lax.ppermute(share, AXES, [(dev, dev ^ step) for dev in range(8)])  12.5 us
    pallas_call x2, Pallas kernels, attend(): pl.pallas_call(functools.partial(attend_kernel, seq_count, turn), out_sha...  4.08 us
    pallas_call x2, Pallas kernels, pack(): pl.pallas_call(functools.partial(pack_kernel, seq_count, groups), out_sha...  2.45 us
    pallas_call x1, Pallas kernels, by_pairs(): pl.pallas_call(functools.partial(unpack_kernel, seq_count), out_shape=[ou...  1.16 us
  transfers between devices with their start and end apart: 16, of which 9 were waited for; matrix products, arithmetic and copies ran while one was open for 0% of the time, Pallas kernels for 9%

profile of v23, /device:TPU:0, one launch (start us, length us, event | category | flops | bytes accessed | tf_op | source)
XLA Modules:
  0.0 36.5 jit_solution(14385641468500551753)
XLA Ops:
  0.6 1.1 %pack.2 = bf16[528,256]{1,0:T(8,128)(2,1)S(1)} custom-call(s32[1,1,2]{2,1,0:T(1,128)} %refs_0_.2, s32[1,128]{1,0:T(1,128)} %refs_1_.3, bf16[1,1,128,2048]{3,2,1,0:T(8,128)(2,1)} %refs_2_.3, bf16[1,1,128,2048]{3,2,1,0:T(8,128)(2,1)} %refs_3_.3), custom_call_target="tpu_custom_call" | custom-call | tf_op jit(solution)/shard_map/pack/pallas_call | solution.py:331
  1.8 4.0 %collective-permute-start = (bf16[528,256]{1,0:T(8,128)(2,1)S(1)}, bf16[528,256]{1,0:T(8,128)(2,1)S(1)}, u32[]{:S(2)}, u32[]{:S(2)}) collective-permute-start(bf16[528,256]{1,0:T(8,128)(2,1)S(1)} %pack.2), channel_id=1, source_target_pairs={{0,18},{1,19},{2,16},{3,17},{16,2},{17,3},{18,0},{19,1},{4,22},{5,... | collective-permute-start | bytes 811016 | tf_op jit(solution)/shard_map/ppermute | solution.py:297
  5.7 1.3 %pack.3 = (bf16[272,256]{1,0:T(8,128)(2,1)S(1)}, bf16[272,256]{1,0:T(8,128)(2,1)S(1)}, bf16[256,256]{1,0:T(8,128)(2,1)S(1)}, bf16[256,256]{1,0:T(8,128)(2,1)S(1)...) custom-call(s32[1,1,2]{2,1,0:T(1,128)} %refs_0_.2, s32[1,128]{1,0:T(1,128)} %refs_1_.3, ...), custom_call_target="tpu_custom_call" | custom-call | tf_op jit(solution)/shard_map/pack/pallas_call | solution.py:331
  7.0 0.1 collective-permute-start.1
  7.1 0.7 %collective-permute-start.5 = (bf16[272,256]{1,0:T(8,128)(2,1)S(1)}, bf16[272,256]{1,0:T(8,128)(2,1)S(1)}, u32[]{:S(2)}, u32[]{:S(2)}) collective-permute-start(bf16[272,256]{1,0:T(8,128)(2,1)S(1)} %get-tuple-element.37), channel_id=1, source_target_pairs={{0,3},{1,2},{2,1},{3,0},{16,19},{17,18},{18,17},{19,16},{4,7},{5,6... | collective-permute-start | bytes 417800 | tf_op jit(solution)/shard_map/ppermute | solution.py:297
  7.8 0.1 collective-permute-start.2
  7.8 1.9 %collective-permute-start.3 = (bf16[256,256]{1,0:T(8,128)(2,1)S(1)}, bf16[256,256]{1,0:T(8,128)(2,1)S(1)}, u32[]{:S(2)}, u32[]{:S(2)}) collective-permute-start(bf16[256,256]{1,0:T(8,128)(2,1)S(1)} %get-tuple-element.35), channel_id=1, source_target_pairs={{0,2},{1,3},{2,0},{3,1},{16,18},{17,19},{18,16},{19,17},{4,6},{5,7... | collective-permute-start | bytes 393224 | tf_op jit(solution)/shard_map/ppermute | solution.py:297
  9.8 0.0 collective-permute-done.1.refs_2_
  9.8 0.6 %collective-permute-start.4 = (bf16[256,256]{1,0:T(8,128)(2,1)S(1)}, bf16[256,256]{1,0:T(8,128)(2,1)S(1)}, u32[]{:S(2)}, u32[]{:S(2)}) collective-permute-start(bf16[256,256]{1,0:T(8,128)(2,1)S(1)} %get-tuple-element.36), channel_id=1, source_target_pairs={{0,17},{1,16},{2,19},{3,18},{16,1},{17,0},{18,3},{19,2},{4,21},{5,... | collective-permute-start | bytes 393224 | tf_op jit(solution)/shard_map/ppermute | solution.py:297
  10.4 2.6 %collective-permute-done.refs_0_ = bf16[528,256]{1,0:T(8,128)(2,1)S(1)} collective-permute-done((bf16[528,256]{1,0:T(8,128)(2,1)S(1)}, bf16[528,256]{1,0:T(8,128)(2,1)S(1)}, u32[]{:S(2)}, u32[]{:S(2)}) %collective-permute-start) | collective-permute-done | bytes 270368 | tf_op jit(solution)/shard_map/ppermute | solution.py:297
  13.0 0.1 collective-permute-start.6
  14.4 0.7 %collective-permute-done.2.refs_3_ = bf16[256,256]{1,0:T(8,128)(2,1)S(1)} collective-permute-done((bf16[256,256]{1,0:T(8,128)(2,1)S(1)}, bf16[256,256]{1,0:T(8,128)(2,1)S(1)}, u32[]{:S(2)}, u32[]{:S(2)}) %collective-permute-start.2) | collective-permute-done | bytes 131104 | tf_op jit(solution)/shard_map/ppermute | solution.py:297
  15.1 3.2 %collective-permute-done.3.refs_4_ = bf16[256,256]{1,0:T(8,128)(2,1)S(1)} collective-permute-done((bf16[256,256]{1,0:T(8,128)(2,1)S(1)}, bf16[256,256]{1,0:T(8,128)(2,1)S(1)}, u32[]{:S(2)}, u32[]{:S(2)}) %collective-permute-start.3) | collective-permute-done | bytes 131104 | tf_op jit(solution)/shard_map/ppermute | solution.py:297
  18.3 0.0 collective-permute-done.4.refs_5_
  18.3 0.0 collective-permute-done.5.refs_6_
  18.3 0.0 collective-permute-done.6.refs_7_
  18.3 2.0 %attend.2 = (bf16[512,128]{1,0:T(8,128)(2,1)S(1)}, bf16[256,128]{1,0:T(8,128)(2,1)S(1)}, bf16[256,128]{1,0:T(8,128)(2,1)S(1)}, bf16[256,128]{1,0:T(8,128)(2,1)S(...) custom-call(s32[1]{0:T(128)S(6)} %copy.8.source_len, ...), custom_call_target="tpu_custom_call" | custom-call | flops 167772160 | bytes 1048576 | tf_op jit(solution)/shard_map/attend/pallas_call | solution.py:356
  20.3 2.1 %collective-permute-start.7 = (bf16[512,128]{1,0:T(8,128)(2,1)S(1)}, bf16[512,128]{1,0:T(8,128)(2,1)S(1)}, u32[]{:S(2)}, u32[]{:S(2)}) collective-permute-start(bf16[512,128]{1,0:T(8,128)(2,1)S(1)} %get-tuple-element.45), channel_id=1, source_target_pairs={{0,18},{1,19},{2,16},{3,17},{16,2},{17,3},{18,0},{19,1},{4,22},{5,... | collective-permute-start | bytes 393224 | tf_op jit(solution)/shard_map/ppermute | solution.py:297
  22.5 2.1 %attend.3 = (bf16[512,128]{1,0:T(8,128)(2,1)S(1)}, bf16[256,256]{1,0:T(8,128)(2,1)S(1)}, bf16[256,256]{1,0:T(8,128)(2,1)S(1)}, bf16[256,256]{1,0:T(8,128)(2,1)S(...) custom-call(s32[1]{0:T(128)S(6)} %copy.8.source_len, ...), custom_call_target="tpu_custom_call" | custom-call | flops 167772160 | bytes 1048576 | tf_op jit(solution)/shard_map/attend/pallas_call | solution.py:356
  24.5 0.9 %collective-permute-start.8 = (bf16[512,128]{1,0:T(8,128)(2,1)S(1)}, bf16[512,128]{1,0:T(8,128)(2,1)S(1)}, u32[]{:S(2)}, u32[]{:S(2)}) collective-permute-start(bf16[512,128]{1,0:T(8,128)(2,1)S(1)} %get-tuple-element.47), channel_id=1, source_target_pairs={{0,18},{1,19},{2,16},{3,17},{16,2},{17,3},{18,0},{19,1},{4,22},{5,... | collective-permute-start | bytes 393224 | tf_op jit(solution)/shard_map/ppermute | solution.py:297
  25.4 1.2 %collective-permute-start.12 = (bf16[256,256]{1,0:T(8,128)(2,1)S(1)}, bf16[256,256]{1,0:T(8,128)(2,1)S(1)}, u32[]{:S(2)}, u32[]{:S(2)}) collective-permute-start(bf16[256,256]{1,0:T(8,128)(2,1)S(1)} %get-tuple-element.50), channel_id=1, source_target_pairs={{0,16},{1,17},{2,18},{3,19},{16,0},{17,1},{18,2},{19,3},{4,20},{5,... | collective-permute-start | bytes 393224 | tf_op jit(solution)/shard_map/ppermute | solution.py:297
  26.6 1.5 %collective-permute-start.13 = (bf16[256,256]{1,0:T(8,128)(2,1)S(1)}, bf16[256,256]{1,0:T(8,128)(2,1)S(1)}, u32[]{:S(2)}, u32[]{:S(2)}) collective-permute-start(bf16[256,256]{1,0:T(8,128)(2,1)S(1)} %get-tuple-element.51), channel_id=1, source_target_pairs={{0,2},{1,3},{2,0},{3,1},{16,18},{17,19},{18,16},{19,17},{4,6},{5,7... | collective-permute-start | bytes 393224 | tf_op jit(solution)/shard_map/ppermute | solution.py:297
  28.1 0.0 collective-permute-start.14
  28.1 0.0 collective-permute-done.7.refs_0_
  28.1 1.1 %collective-permute-start.15 = (bf16[256,256]{1,0:T(8,128)(2,1)S(1)}, bf16[256,256]{1,0:T(8,128)(2,1)S(1)}, u32[]{:S(2)}, u32[]{:S(2)}) collective-permute-start(bf16[256,256]{1,0:T(8,128)(2,1)S(1)} %get-tuple-element.53), channel_id=1, source_target_pairs={{0,3},{1,2},{2,1},{3,0},{16,19},{17,18},{18,17},{19,16},{4,7},{5,6... | collective-permute-start | bytes 393224 | tf_op jit(solution)/shard_map/ppermute | solution.py:297
  29.2 2.7 %collective-permute-done.8.refs_1_ = bf16[512,128]{1,0:T(8,128)(2,1)S(1)} collective-permute-done((bf16[512,128]{1,0:T(8,128)(2,1)S(1)}, bf16[512,128]{1,0:T(8,128)(2,1)S(1)}, u32[]{:S(2)}, u32[]{:S(2)}) %collective-permute-start.8) | collective-permute-done | bytes 131104 | tf_op jit(solution)/shard_map/ppermute | solution.py:297
  31.9 0.0 collective-permute-start.11
  31.9 1.8 %collective-permute-done.12.refs_6_ = bf16[256,256]{1,0:T(8,128)(2,1)S(1)} collective-permute-done((bf16[256,256]{1,0:T(8,128)(2,1)S(1)}, bf16[256,256]{1,0:T(8,128)(2,1)S(1)}, u32[]{:S(2)}, u32[]{:S(2)}) %collective-permute-start.12) | collective-permute-done | bytes 131104 | tf_op jit(solution)/shard_map/ppermute | solution.py:297
  33.7 0.0 collective-permute-start.10
  33.7 0.4 %collective-permute-done.13.refs_7_ = bf16[256,256]{1,0:T(8,128)(2,1)S(1)} collective-permute-done((bf16[256,256]{1,0:T(8,128)(2,1)S(1)}, bf16[256,256]{1,0:T(8,128)(2,1)S(1)}, u32[]{:S(2)}, u32[]{:S(2)}) %collective-permute-start.13) | collective-permute-done | bytes 131104 | tf_op jit(solution)/shard_map/ppermute | solution.py:297
  34.1 0.1 collective-permute-start.9
  34.2 0.3 collective-permute-done.14.refs_8_
  34.6 0.0 collective-permute-done.15.refs_9_
  34.6 0.4 %collective-permute-done.10.refs_3_ = bf16[256,128]{1,0:T(8,128)(2,1)S(1)} collective-permute-done((bf16[256,128]{1,0:T(8,128)(2,1)S(1)}, bf16[256,128]{1,0:T(8,128)(2,1)S(1)}, u32[]{:S(2)}, u32[]{:S(2)}) %collective-permute-start.10) | collective-permute-done | bytes 65568 | tf_op jit(solution)/shard_map/ppermute | solution.py:297
  35.0 0.4 %collective-permute-done.9.refs_2_ = bf16[256,128]{1,0:T(8,128)(2,1)S(1)} collective-permute-done((bf16[256,128]{1,0:T(8,128)(2,1)S(1)}, bf16[256,128]{1,0:T(8,128)(2,1)S(1)}, u32[]{:S(2)}, u32[]{:S(2)}) %collective-permute-start.9) | collective-permute-done | bytes 65568 | tf_op jit(solution)/shard_map/ppermute | solution.py:297
  35.4 0.0 collective-permute-done.11.refs_5_
  35.4 1.2 %unpack.1 = (bf16[1,1,128,2048]{3,2,1,0:T(8,128)(2,1)}, bf16[1,1,128,2048]{3,2,1,0:T(8,128)(2,1)}) custom-call(bf16[512,128]{1,0:T(8,128)(2,1)S(1)} %collective-permute-done.7.refs_0_, bf16[512,128]{1,0:T(8,128)(2,1)S(1)} %collective-permute-done.8.refs_1_, bf16[256,128]{1,0:T(8,128)(2,1)S(1)} %collective-permute-done.9.refs_2_, ...), custom_call_target="tpu_custom_call" | custom-call | tf_op jit(solution)/shard_map/unpack/pallas_call | solution.py:376
  (3 shorter events, 0.0 us)
Async XLA Ops:
  1.8 11.3 %collective-permute-start = (bf16[528,256]{1,0:T(8,128)(2,1)S(1)}, bf16[528,256]{1,0:T(8,128)(2,1)S(1)}, u32[]{:S(2)}, u32[]{:S(2)}) collective-permute-start(bf16[528,256]{1,0:T(8,128)(2,1)S(1)} %pack.2), channel_id=1, source_target_pairs={{0,18},{1,19},{2,16},{3,17},{16,2},{17,3},{18,0},{19,1},{4,22},{5,... | collective-permute-start | bytes 811016 | tf_op jit(solution)/shard_map/ppermute | solution.py:297
  7.0 2.7 %collective-permute-start.1 = (bf16[272,256]{1,0:T(8,128)(2,1)S(1)}, bf16[272,256]{1,0:T(8,128)(2,1)S(1)}, u32[]{:S(2)}, u32[]{:S(2)}) collective-permute-start(bf16[272,256]{1,0:T(8,128)(2,1)S(1)} %get-tuple-element.30), channel_id=1, source_target_pairs={{0,1},{1,0},{2,3},{3,2},{16,17},{17,16},{18,19},{19,18},{4,5},{5,4... | collective-permute-start | bytes 417800 | tf_op jit(solution)/shard_map/ppermute | solution.py:297
  7.1 11.2 %collective-permute-start.5 = (bf16[272,256]{1,0:T(8,128)(2,1)S(1)}, bf16[272,256]{1,0:T(8,128)(2,1)S(1)}, u32[]{:S(2)}, u32[]{:S(2)}) collective-permute-start(bf16[272,256]{1,0:T(8,128)(2,1)S(1)} %get-tuple-element.37), channel_id=1, source_target_pairs={{0,3},{1,2},{2,1},{3,0},{16,19},{17,18},{18,17},{19,16},{4,7},{5,6... | collective-permute-start | bytes 417800 | tf_op jit(solution)/shard_map/ppermute | solution.py:297
  7.8 7.3 %collective-permute-start.2 = (bf16[256,256]{1,0:T(8,128)(2,1)S(1)}, bf16[256,256]{1,0:T(8,128)(2,1)S(1)}, u32[]{:S(2)}, u32[]{:S(2)}) collective-permute-start(bf16[256,256]{1,0:T(8,128)(2,1)S(1)} %get-tuple-element.34), channel_id=1, source_target_pairs={{0,16},{1,17},{2,18},{3,19},{16,0},{17,1},{18,2},{19,3},{4,20},{5,... | collective-permute-start | bytes 393224 | tf_op jit(solution)/shard_map/ppermute | solution.py:297
  7.8 10.4 %collective-permute-start.3 = (bf16[256,256]{1,0:T(8,128)(2,1)S(1)}, bf16[256,256]{1,0:T(8,128)(2,1)S(1)}, u32[]{:S(2)}, u32[]{:S(2)}) collective-permute-start(bf16[256,256]{1,0:T(8,128)(2,1)S(1)} %get-tuple-element.35), channel_id=1, source_target_pairs={{0,2},{1,3},{2,0},{3,1},{16,18},{17,19},{18,16},{19,17},{4,6},{5,7... | collective-permute-start | bytes 393224 | tf_op jit(solution)/shard_map/ppermute | solution.py:297
  9.8 8.5 %collective-permute-start.4 = (bf16[256,256]{1,0:T(8,128)(2,1)S(1)}, bf16[256,256]{1,0:T(8,128)(2,1)S(1)}, u32[]{:S(2)}, u32[]{:S(2)}) collective-permute-start(bf16[256,256]{1,0:T(8,128)(2,1)S(1)} %get-tuple-element.36), channel_id=1, source_target_pairs={{0,17},{1,16},{2,19},{3,18},{16,1},{17,0},{18,3},{19,2},{4,21},{5,... | collective-permute-start | bytes 393224 | tf_op jit(solution)/shard_map/ppermute | solution.py:297
  13.0 5.3 %collective-permute-start.6 = (bf16[256,256]{1,0:T(8,128)(2,1)S(1)}, bf16[256,256]{1,0:T(8,128)(2,1)S(1)}, u32[]{:S(2)}, u32[]{:S(2)}) collective-permute-start(bf16[256,256]{1,0:T(8,128)(2,1)S(1)} %slice.9), channel_id=1, source_target_pairs={{0,1},{1,0},{2,3},{3,2},{16,17},{17,16},{18,19},{19,18},{4,5},{5,4... | collective-permute-start | bytes 393224 | tf_op jit(solution)/shard_map/ppermute | solution.py:297
  20.3 7.8 %collective-permute-start.7 = (bf16[512,128]{1,0:T(8,128)(2,1)S(1)}, bf16[512,128]{1,0:T(8,128)(2,1)S(1)}, u32[]{:S(2)}, u32[]{:S(2)}) collective-permute-start(bf16[512,128]{1,0:T(8,128)(2,1)S(1)} %get-tuple-element.45), channel_id=1, source_target_pairs={{0,18},{1,19},{2,16},{3,17},{16,2},{17,3},{18,0},{19,1},{4,22},{5,... | collective-permute-start | bytes 393224 | tf_op jit(solution)/shard_map/ppermute | solution.py:297
  24.5 7.3 %collective-permute-start.8 = (bf16[512,128]{1,0:T(8,128)(2,1)S(1)}, bf16[512,128]{1,0:T(8,128)(2,1)S(1)}, u32[]{:S(2)}, u32[]{:S(2)}) collective-permute-start(bf16[512,128]{1,0:T(8,128)(2,1)S(1)} %get-tuple-element.47), channel_id=1, source_target_pairs={{0,18},{1,19},{2,16},{3,17},{16,2},{17,3},{18,0},{19,1},{4,22},{5,... | collective-permute-start | bytes 393224 | tf_op jit(solution)/shard_map/ppermute | solution.py:297
  25.4 8.3 %collective-permute-start.12 = (bf16[256,256]{1,0:T(8,128)(2,1)S(1)}, bf16[256,256]{1,0:T(8,128)(2,1)S(1)}, u32[]{:S(2)}, u32[]{:S(2)}) collective-permute-start(bf16[256,256]{1,0:T(8,128)(2,1)S(1)} %get-tuple-element.50), channel_id=1, source_target_pairs={{0,16},{1,17},{2,18},{3,19},{16,0},{17,1},{18,2},{19,3},{4,20},{5,... | collective-permute-start | bytes 393224 | tf_op jit(solution)/shard_map/ppermute | solution.py:297
  26.6 7.5 %collective-permute-start.13 = (bf16[256,256]{1,0:T(8,128)(2,1)S(1)}, bf16[256,256]{1,0:T(8,128)(2,1)S(1)}, u32[]{:S(2)}, u32[]{:S(2)}) collective-permute-start(bf16[256,256]{1,0:T(8,128)(2,1)S(1)} %get-tuple-element.51), channel_id=1, source_target_pairs={{0,2},{1,3},{2,0},{3,1},{16,18},{17,19},{18,16},{19,17},{4,6},{5,7... | collective-permute-start | bytes 393224 | tf_op jit(solution)/shard_map/ppermute | solution.py:297
  28.1 6.5 %collective-permute-start.14 = (bf16[256,256]{1,0:T(8,128)(2,1)S(1)}, bf16[256,256]{1,0:T(8,128)(2,1)S(1)}, u32[]{:S(2)}, u32[]{:S(2)}) collective-permute-start(bf16[256,256]{1,0:T(8,128)(2,1)S(1)} %get-tuple-element.52), channel_id=1, source_target_pairs={{0,17},{1,16},{2,19},{3,18},{16,1},{17,0},{18,3},{19,2},{4,21},{5,... | collective-permute-start | bytes 393224 | tf_op jit(solution)/shard_map/ppermute | solution.py:297
  28.1 6.5 %collective-permute-start.15 = (bf16[256,256]{1,0:T(8,128)(2,1)S(1)}, bf16[256,256]{1,0:T(8,128)(2,1)S(1)}, u32[]{:S(2)}, u32[]{:S(2)}) collective-permute-start(bf16[256,256]{1,0:T(8,128)(2,1)S(1)} %get-tuple-element.53), channel_id=1, source_target_pairs={{0,3},{1,2},{2,1},{3,0},{16,19},{17,18},{18,17},{19,16},{4,7},{5,6... | collective-permute-start | bytes 393224 | tf_op jit(solution)/shard_map/ppermute | solution.py:297
  31.9 3.5 %collective-permute-start.11 = (bf16[256,256]{1,0:T(8,128)(2,1)S(1)}, bf16[256,256]{1,0:T(8,128)(2,1)S(1)}, u32[]{:S(2)}, u32[]{:S(2)}) collective-permute-start(bf16[256,256]{1,0:T(8,128)(2,1)S(1)} %get-tuple-element.49), channel_id=1, source_target_pairs={{0,1},{1,0},{2,3},{3,2},{16,17},{17,16},{18,19},{19,18},{4,5},{5,4... | collective-permute-start | bytes 393224 | tf_op jit(solution)/shard_map/ppermute | solution.py:297
  33.7 1.3 %collective-permute-start.10 = (bf16[256,128]{1,0:T(8,128)(2,1)S(1)}, bf16[256,128]{1,0:T(8,128)(2,1)S(1)}, u32[]{:S(2)}, u32[]{:S(2)}) collective-permute-start(bf16[256,128]{1,0:T(8,128)(2,1)S(1)} %slice.12), channel_id=1, source_target_pairs={{0,1},{1,0},{2,3},{3,2},{16,17},{17,16},{18,19},{19,18},{4,5},{5,4... | collective-permute-start | bytes 196616 | tf_op jit(solution)/shard_map/ppermute | solution.py:297
  34.1 1.3 %collective-permute-start.9 = (bf16[256,128]{1,0:T(8,128)(2,1)S(1)}, bf16[256,128]{1,0:T(8,128)(2,1)S(1)}, u32[]{:S(2)}, u32[]{:S(2)}) collective-permute-start(bf16[256,128]{1,0:T(8,128)(2,1)S(1)} %slice.10), channel_id=1, source_target_pairs={{0,1},{1,0},{2,3},{3,2},{16,17},{17,16},{18,19},{19,18},{4,5},{5,4... | collective-permute-start | bytes 196616 | tf_op jit(solution)/shard_map/ppermute | solution.py:297

commit v24 on v21

--- a/solution.py
+++ b/solution.py
@@ -180,20 +180,24 @@
 OUTGOING = [DIAGONAL, *REST]
 INCOMING = [*OUTGOING, DIAGONAL[1:]]
 TILES = 2
+HALVED = [(5,)]
+PACKED = [(group, 0) for group in REST if group not in HALVED]
+PACKED += [(group, tile * LANES) for tile in range(TILES) for group in HALVED]
+AFTER = {((5,), 0): (NEAR, 0), ((5,), LANES): ((4,), 0)}
 EARLY = (0, 6)
 
 
-def pack_kernel(seq_count, steps, *refs):
+def pack_kernel(seq_count, places, *refs):
     smalls, (first, second) = refs[:2], refs[2:4]
     outs, (lists, mask, small_sem, sem) = refs[4:-4], refs[-4:]
     me = device_index(seq_count)
     here = me % seq_count
-    share = outs[0].shape[1]
+    share = first.shape[3] // (2 * seq_count)
     copies, pieces = [], []
-    for group, out in zip(steps, outs):
+    for (group, start), out in zip(places, outs):
         for place, step in enumerate(group):
             slot = len(copies)
-            lanes = pl.ds(pl.multiple_of((me ^ step) * share, LANES), share)
+            lanes = pl.ds(pl.multiple_of((me ^ step) * share + start, LANES), out.shape[1])
             piece = out.at[pl.ds(place * 2 * BLK, 2 * BLK)]
             pair = [
                 pltpu.make_async_copy(
@@ -215,17 +219,16 @@
         copy.wait()
     keep = (mask[...] == 1) | (me < seq_count)
     keep = jnp.broadcast_to(jnp.where(keep, 1.0, 0.0), (BLK, BLK)).T.astype(jnp.bfloat16)
-    keep = jnp.concatenate([keep] * (share // LANES), axis=1)
     base = here - WIN
     code = (lists[0, 0, 0] - base) * SPAN + lists[0, 0, 1] - base
-    tail = jnp.full((TAIL, share), code, jnp.int32).astype(jnp.float32).astype(jnp.bfloat16)
+    tail = jnp.full((TAIL, LANES), code, jnp.int32).astype(jnp.float32).astype(jnp.bfloat16)
     for out in outs:
         if out.shape[0] % (2 * BLK):
-            out[2 * BLK :] = tail
+            out[2 * BLK :] = jnp.concatenate([tail] * (out.shape[1] // LANES), axis=1)
     for piece, pair in zip(pieces, copies):
         for copy in pair:
             copy.wait()
-        piece[BLK:] = piece[BLK:] * keep
+        piece[BLK:] = piece[BLK:] * jnp.concatenate([keep] * (piece.shape[1] // LANES), axis=1)
 
 
 def attend_kernel(seq_count, turn, source_len, target_len, *refs):
@@ -238,10 +241,11 @@
     lanes = pl.ds(turn * LANES, LANES)
     for (step, *_), share in zip(INCOMING, shares):
         source = me ^ step
-        rows[source, 0] = share[pl.ds(0, BLK), lanes]
-        rows[source, 1] = share[pl.ds(BLK, BLK), lanes]
+        here_lanes = lanes if share.shape[1] > LANES else pl.ds(0, LANES)
+        rows[source, 0] = share[pl.ds(0, BLK), here_lanes]
+        rows[source, 1] = share[pl.ds(BLK, BLK), here_lanes]
         if step < seq_count:
-            tail = share[pl.ds(2 * BLK, TAIL), lanes].astype(jnp.float32)
+            tail = share[pl.ds(2 * BLK, TAIL), here_lanes].astype(jnp.float32)
             lists[here ^ step] = jnp.max(tail).astype(jnp.int32)
 
     def listed(block, slot):
@@ -291,15 +295,26 @@
     return lax.ppermute(share, AXES, [(dev, dev ^ step) for dev in range(8)])
 
 
-def swapped(diagonals, shares):
+def coming_in(diagonal, held):
+    diagonal = permuted(diagonal, DIAGONAL[0])
+    moved = {}
+    for place in PACKED:
+        share = held[place]
+        if place in AFTER:
+            earlier = AFTER[place]
+            share, moved[earlier] = lax.optimization_barrier((share, moved[earlier]))
+        moved[place] = permuted(share, place[0][0]) if place[0] != OWN else share
+    near = (NEAR, 0)
+    diagonal, moved[near] = lax.optimization_barrier((diagonal, moved[near]))
+    return diagonal, moved, permuted(diagonal[diagonal.shape[0] // 2 :], NEAR[0])
+
+
+def going_out(diagonals, shares):
     held = dict(zip(REST, shares))
     diagonals = [permuted(share, DIAGONAL[0]) for share in diagonals]
     moved = {group: permuted(held[group], group[0]) for group in ACROSS}
-    if len(diagonals) > 1:
-        held[NEAR], diagonals[0] = lax.optimization_barrier((held[NEAR], diagonals[0]))
+    held[NEAR], diagonals[0] = lax.optimization_barrier((held[NEAR], diagonals[0]))
     moved[NEAR] = permuted(held[NEAR], NEAR[0])
-    if len(diagonals) == 1:
-        diagonals[0], moved[NEAR] = lax.optimization_barrier((diagonals[0], moved[NEAR]))
     handed_on = [permuted(share[share.shape[0] // 2 :], NEAR[0]) for share in diagonals]
     return diagonals, [held[OWN], moved[NEAR], *(moved[group] for group in ACROSS)], handed_on
 
@@ -313,20 +328,21 @@
     params = pltpu.CompilerParams(vmem_limit_bytes=VMEM_LIMIT)
     sems = pltpu.SemaphoreType.DMA((2, parts))
 
-    def sizes(groups, tail):
-        return [
-            jax.ShapeDtypeStruct(
-                (len(group) * 2 * BLK + (tail if group[0] < seq_count else 0), share), kind
-            )
-            for group in groups
-        ]
-
-    def pack(groups, lists):
+    def pack(places, lists):
         return pl.pallas_call(
-            functools.partial(pack_kernel, seq_count, groups),
-            out_shape=sizes(groups, TAIL),
+            functools.partial(pack_kernel, seq_count, places),
+            out_shape=[
+                jax.ShapeDtypeStruct(
+                    (
+                        len(group) * 2 * BLK + (TAIL if group[0] < seq_count else 0),
+                        LANES if group in HALVED else share,
+                    ),
+                    kind,
+                )
+                for group, _ in places
+            ],
             in_specs=specs(4, pltpu.HBM),
-            out_specs=specs(len(groups), pltpu.VMEM),
+            out_specs=specs(len(places), pltpu.VMEM),
             scratch_shapes=[
                 pltpu.SMEM(alignment.shape, jnp.int32),
                 pltpu.VMEM(diffusion_mask.shape, jnp.int32),
@@ -337,16 +353,18 @@
             name="pack",
         )(*in_hbm(lists, diffusion_mask, first_rows, second_rows))
 
-    (diagonal,) = pack([DIAGONAL], alignment)
+    (diagonal,) = pack([(DIAGONAL, 0)], alignment)
     lists, diagonal = lax.optimization_barrier((alignment, diagonal))
-    diagonals, shares, handed_on = swapped([diagonal], pack(REST, lists))
-    coming = [*diagonals, *shares, *handed_on]
+    diagonal, moved, handed_on = coming_in(diagonal, dict(zip(PACKED, pack(PACKED, lists))))
     rows = pltpu.VMEM((parts, 2, BLK, LANES), kind)
     grads = pltpu.VMEM((seq_count, BLK, LANES), jnp.float32)
     turned = pltpu.VMEM((seq_count, 2, LANES, BLK), kind)
 
     def attend(turn, *before):
         lanes = (turn + 1) * LANES
+        coming = [diagonal]
+        coming += [moved[group, turn * LANES if group in HALVED else 0] for group in REST]
+        coming += [handed_on]
         return pl.pallas_call(
             functools.partial(attend_kernel, seq_count, turn),
             out_shape=[
@@ -363,9 +381,9 @@
 
     diagonals, shares = [], []
     for turn in range(TILES):
-        diagonal, *shares = attend(turn, *shares)
-        diagonals.append(diagonal)
-    diagonals, shares, handed_on = swapped(diagonals, shares)
+        result, *shares = attend(turn, *shares)
+        diagonals.append(result)
+    diagonals, shares, handed_on = going_out(diagonals, shares)
     arrived = dict(zip([(group[0], 0) for group in REST], shares))
     for step, tiles in zip(DIAGONAL, (diagonals, handed_on)):
         arrived.update({(step, tile * LANES): share for tile, share in enumerate(tiles)})

time: 36.3 us -> 37.1 us (1.022)
  starting transfers between devices: 15 us -> 17.1 us
  waiting for transfers between devices: 10.7 us -> 9.45 us
    ppermute x16 -> x17, starting transfers between devices: 15 us -> 17.1 us  [permuted(): return lax.ppermute(share, AXES, [(dev, dev ^ step) for dev in range(8)])]
    ppermute x16 -> x17, waiting for transfers between devices: 10.7 us -> 9.45 us  [permuted(): return lax.ppermute(share, AXES, [(dev, dev ^ step) for dev in range(8)])]
  transfers between devices with their start and end apart: 16 -> 17, of which waited for: 6 -> 4; matrix products, arithmetic and copies ran while one was open for 0% -> 0% of each run, Pallas kernels for 11% -> 17%
where the time goes in v24:
time: 37.1 us; the launch traced here: 36.8 us
  starting transfers between devices  17.1 us (46%)
  waiting for transfers between devices  9.45 us (25%)
  Pallas kernels  8.23 us (22%)
  between operations  2.06 us (6%)
    ppermute x17, starting transfers between devices, permuted(): return lax.ppermute(share, AXES, [(dev, dev ^ step) for dev in range(8)])  17.1 us
    ppermute x17, waiting for transfers between devices, permuted(): return lax.ppermute(share, AXES, [(dev, dev ^ step) for dev in range(8)])  9.45 us
    pallas_call x2, Pallas kernels, attend(): pl.pallas_call(functools.partial(attend_kernel, seq_count, turn), out_sha...  4.06 us
    pallas_call x2, Pallas kernels, pack(): pl.pallas_call(functools.partial(pack_kernel, seq_count, places), out_sha...  2.43 us
    pallas_call x2, Pallas kernels, unpack(): pl.pallas_call(functools.partial(unpack_kernel, seq_count, places), out_s...  1.74 us
  transfers between devices with their start and end apart: 17, of which 4 were waited for; matrix products, arithmetic and copies ran while one was open for 0% of the time, Pallas kernels for 17%

profile of v24, /device:TPU:0, one launch (start us, length us, event | category | flops | bytes accessed | tf_op | source)
XLA Modules:
  0.0 36.8 jit_solution(10760145616986727175)
XLA Ops:
  0.6 1.1 %pack.2 = bf16[512,256]{1,0:T(8,128)(2,1)S(1)} custom-call(s32[1,1,2]{2,1,0:T(1,128)} %refs_0_.2, s32[1,128]{1,0:T(1,128)} %refs_1_.3, bf16[1,1,128,2048]{3,2,1,0:T(8,128)(2,1)} %refs_2_.3, bf16[1,1,128,2048]{3,2,1,0:T(8,128)(2,1)} %refs_3_.3), custom_call_target="tpu_custom_call" | custom-call | tf_op jit(solution)/shard_map/pack/pallas_call | solution.py:332
  1.8 4.0 %collective-permute-start = (bf16[512,256]{1,0:T(8,128)(2,1)S(1)}, bf16[512,256]{1,0:T(8,128)(2,1)S(1)}, u32[]{:S(2)}, u32[]{:S(2)}) collective-permute-start(bf16[512,256]{1,0:T(8,128)(2,1)S(1)} %pack.2), channel_id=1, source_target_pairs={{0,18},{1,19},{2,16},{3,17},{16,2},{17,3},{18,0},{19,1},{4,22},{5,... | collective-permute-start | bytes 786440 | tf_op jit(solution)/shard_map/ppermute | solution.py:295
  5.7 1.3 %pack.3 = (bf16[272,256]{1,0:T(8,128)(2,1)S(1)}, bf16[272,256]{1,0:T(8,128)(2,1)S(1)}, bf16[256,256]{1,0:T(8,128)(2,1)S(1)}, bf16[272,256]{1,0:T(8,128)(2,1)S(1)...) custom-call(s32[1,1,2]{2,1,0:T(1,128)} %refs_0_.2, s32[1,128]{1,0:T(1,128)} %refs_1_.3, ...), custom_call_target="tpu_custom_call" | custom-call | tf_op jit(solution)/shard_map/pack/pallas_call | solution.py:332
  7.0 0.1 collective-permute-start.1
  7.1 0.6 %collective-permute-start.2 = (bf16[256,256]{1,0:T(8,128)(2,1)S(1)}, bf16[256,256]{1,0:T(8,128)(2,1)S(1)}, u32[]{:S(2)}, u32[]{:S(2)}) collective-permute-start(bf16[256,256]{1,0:T(8,128)(2,1)S(1)} %get-tuple-element.44), channel_id=1, source_target_pairs={{0,16},{1,17},{2,18},{3,19},{16,0},{17,1},{18,2},{19,3},{4,20},{5,... | collective-permute-start | bytes 393224 | tf_op jit(solution)/shard_map/ppermute | solution.py:295
  7.7 0.1 collective-permute-start.3
  7.8 1.4 %collective-permute-start.5 = (bf16[272,256]{1,0:T(8,128)(2,1)S(1)}, bf16[272,256]{1,0:T(8,128)(2,1)S(1)}, u32[]{:S(2)}, u32[]{:S(2)}) collective-permute-start(bf16[272,256]{1,0:T(8,128)(2,1)S(1)} %get-tuple-element.48), channel_id=1, source_target_pairs={{0,3},{1,2},{2,1},{3,0},{16,19},{17,18},{18,17},{19,16},{4,7},{5,6... | collective-permute-start | bytes 417800 | tf_op jit(solution)/shard_map/ppermute | solution.py:295
  9.2 0.0 collective-permute-done.1.refs_2_
  9.2 3.4 %collective-permute-done.refs_0_ = bf16[512,256]{1,0:T(8,128)(2,1)S(1)} collective-permute-done((bf16[512,256]{1,0:T(8,128)(2,1)S(1)}, bf16[512,256]{1,0:T(8,128)(2,1)S(1)}, u32[]{:S(2)}, u32[]{:S(2)}) %collective-permute-start) | collective-permute-done | bytes 262176 | tf_op jit(solution)/shard_map/ppermute | solution.py:295
  12.6 0.1 collective-permute-start.6
  12.7 2.5 %collective-permute-start.7 = (bf16[256,128]{1,0:T(8,128)(2,1)S(1)}, bf16[256,128]{1,0:T(8,128)(2,1)S(1)}, u32[]{:S(2)}, u32[]{:S(2)}) collective-permute-start(bf16[256,128]{1,0:T(8,128)(2,1)S(1)} %get-tuple-element.49), channel_id=1, source_target_pairs={{0,17},{1,16},{2,19},{3,18},{16,1},{17,0},{18,3},{19,2},{4,21},{5,... | collective-permute-start | bytes 196616 | tf_op jit(solution)/shard_map/ppermute | solution.py:295
  15.1 0.0 collective-permute-done.2.refs_3_
  15.1 1.1 %collective-permute-start.4 = (bf16[256,128]{1,0:T(8,128)(2,1)S(1)}, bf16[256,128]{1,0:T(8,128)(2,1)S(1)}, u32[]{:S(2)}, u32[]{:S(2)}) collective-permute-start(bf16[256,128]{1,0:T(8,128)(2,1)S(1)} %get-tuple-element.47), channel_id=1, source_target_pairs={{0,17},{1,16},{2,19},{3,18},{16,1},{17,0},{18,3},{19,2},{4,21},{5,... | collective-permute-start | bytes 196616 | tf_op jit(solution)/shard_map/ppermute | solution.py:295
  17.5 0.0 collective-permute-done.3.refs_4_
  17.5 0.0 collective-permute-done.5.refs_6_
  17.5 0.0 collective-permute-done.7.refs_5_
  17.5 0.0 collective-permute-done.6.refs_7_
  17.6 2.0 %attend.2 = (bf16[512,128]{1,0:T(8,128)(2,1)S(1)}, bf16[256,128]{1,0:T(8,128)(2,1)S(1)}, bf16[256,128]{1,0:T(8,128)(2,1)S(1)}, bf16[256,128]{1,0:T(8,128)(2,1)S(...) custom-call(s32[1]{0:T(128)S(6)} %copy.12.source_len, ...), custom_call_target="tpu_custom_call" | custom-call | flops 167772160 | bytes 1048576 | tf_op jit(solution)/shard_map/attend/pallas_call | solution.py:368
  19.6 2.4 %collective-permute-start.8 = (bf16[512,128]{1,0:T(8,128)(2,1)S(1)}, bf16[512,128]{1,0:T(8,128)(2,1)S(1)}, u32[]{:S(2)}, u32[]{:S(2)}) collective-permute-start(bf16[512,128]{1,0:T(8,128)(2,1)S(1)} %get-tuple-element.57), channel_id=1, source_target_pairs={{0,18},{1,19},{2,16},{3,17},{16,2},{17,3},{18,0},{19,1},{4,22},{5,... | collective-permute-start | bytes 393224 | tf_op jit(solution)/shard_map/ppermute | solution.py:295
  21.9 0.0 collective-permute-done.4.refs_5_
  21.9 2.1 %attend.3 = (bf16[512,128]{1,0:T(8,128)(2,1)S(1)}, bf16[256,256]{1,0:T(8,128)(2,1)S(1)}, bf16[256,256]{1,0:T(8,128)(2,1)S(1)}, bf16[256,256]{1,0:T(8,128)(2,1)S(...) custom-call(s32[1]{0:T(128)S(6)} %copy.12.source_len, ...), custom_call_target="tpu_custom_call" | custom-call | flops 167772160 | bytes 1048576 | tf_op jit(solution)/shard_map/attend/pallas_call | solution.py:368
  24.0 0.7 %collective-permute-start.15 = (bf16[512,128]{1,0:T(8,128)(2,1)S(1)}, bf16[512,128]{1,0:T(8,128)(2,1)S(1)}, u32[]{:S(2)}, u32[]{:S(2)}) collective-permute-start(bf16[512,128]{1,0:T(8,128)(2,1)S(1)} %get-tuple-element.64), channel_id=1, source_target_pairs={{0,18},{1,19},{2,16},{3,17},{16,2},{17,3},{18,0},{19,1},{4,22},{5,... | collective-permute-start | bytes 393224 | tf_op jit(solution)/shard_map/ppermute | solution.py:295
  24.7 1.4 %collective-permute-start.10 = (bf16[256,256]{1,0:T(8,128)(2,1)S(1)}, bf16[256,256]{1,0:T(8,128)(2,1)S(1)}, u32[]{:S(2)}, u32[]{:S(2)}) collective-permute-start(bf16[256,256]{1,0:T(8,128)(2,1)S(1)} %get-tuple-element.59), channel_id=1, source_target_pairs={{0,16},{1,17},{2,18},{3,19},{16,0},{17,1},{18,2},{19,3},{4,20},{5,... | collective-permute-start | bytes 393224 | tf_op jit(solution)/shard_map/ppermute | solution.py:295
  26.1 1.5 %collective-permute-start.11 = (bf16[256,256]{1,0:T(8,128)(2,1)S(1)}, bf16[256,256]{1,0:T(8,128)(2,1)S(1)}, u32[]{:S(2)}, u32[]{:S(2)}) collective-permute-start(bf16[256,256]{1,0:T(8,128)(2,1)S(1)} %get-tuple-element.60), channel_id=1, source_target_pairs={{0,2},{1,3},{2,0},{3,1},{16,18},{17,19},{18,16},{19,17},{4,6},{5,7... | collective-permute-start | bytes 393224 | tf_op jit(solution)/shard_map/ppermute | solution.py:295
  27.6 0.0 collective-permute-start.12
  27.6 0.0 collective-permute-done.8.refs_1_
  27.6 0.9 %collective-permute-start.13 = (bf16[256,256]{1,0:T(8,128)(2,1)S(1)}, bf16[256,256]{1,0:T(8,128)(2,1)S(1)}, u32[]{:S(2)}, u32[]{:S(2)}) collective-permute-start(bf16[256,256]{1,0:T(8,128)(2,1)S(1)} %get-tuple-element.62), channel_id=1, source_target_pairs={{0,3},{1,2},{2,1},{3,0},{16,19},{17,18},{18,17},{19,16},{4,7},{5,6... | collective-permute-start | bytes 393224 | tf_op jit(solution)/shard_map/ppermute | solution.py:295
  28.5 2.9 %collective-permute-done.15.refs_2_ = bf16[512,128]{1,0:T(8,128)(2,1)S(1)} collective-permute-done((bf16[512,128]{1,0:T(8,128)(2,1)S(1)}, bf16[512,128]{1,0:T(8,128)(2,1)S(1)}, u32[]{:S(2)}, u32[]{:S(2)}) %collective-permute-start.15) | collective-permute-done | bytes 131104 | tf_op jit(solution)/shard_map/ppermute | solution.py:295
  31.4 0.0 collective-permute-start.9
  31.4 2.0 %collective-permute-done.10.refs_1_ = bf16[256,256]{1,0:T(8,128)(2,1)S(1)} collective-permute-done((bf16[256,256]{1,0:T(8,128)(2,1)S(1)}, bf16[256,256]{1,0:T(8,128)(2,1)S(1)}, u32[]{:S(2)}, u32[]{:S(2)}) %collective-permute-start.10) | collective-permute-done | bytes 131104 | tf_op jit(solution)/shard_map/ppermute | solution.py:295
  33.4 0.0 collective-permute-start.16
  33.4 0.0 collective-permute-done.11.refs_2_
  33.4 0.5 %collective-permute-start.14 = (bf16[256,128]{1,0:T(8,128)(2,1)S(1)}, bf16[256,128]{1,0:T(8,128)(2,1)S(1)}, u32[]{:S(2)}, u32[]{:S(2)}) collective-permute-start(bf16[256,128]{1,0:T(8,128)(2,1)S(1)} %slice.10), channel_id=1, source_target_pairs={{0,1},{1,0},{2,3},{3,2},{16,17},{17,16},{18,19},{19,18},{4,5},{5,4... | collective-permute-start | bytes 196616 | tf_op jit(solution)/shard_map/ppermute | solution.py:295
  33.9 0.7 %unpack.2 = (bf16[1,1,128,2048]{3,2,1,0:T(8,128)(2,1)}, bf16[1,1,128,2048]{3,2,1,0:T(8,128)(2,1)}) custom-call(bf16[256,256]{1,0:T(8,128)(2,1)S(1)} %get-tuple-element.65.refs_0_, bf16[512,128]{1,0:T(8,128)(2,1)S(1)} %collective-permute-done.8.refs_1_, bf16[512,128]{1,0:T(8,128)(2,1)S(1)} %collective-permute-done.15.refs_2_), custom_call_target="tpu_custom_call" | custom-call | tf_op jit(solution)/shard_map/unpack/pallas_call | solution.py:394
  34.6 1.2 %collective-permute-done.12.refs_3_ = bf16[256,256]{1,0:T(8,128)(2,1)S(1)} collective-permute-done((bf16[256,256]{1,0:T(8,128)(2,1)S(1)}, bf16[256,256]{1,0:T(8,128)(2,1)S(1)}, u32[]{:S(2)}, u32[]{:S(2)}) %collective-permute-start.12) | collective-permute-done | bytes 131104 | tf_op jit(solution)/shard_map/ppermute | solution.py:295
  35.8 0.0 collective-permute-done.13.refs_4_
  35.8 0.0 collective-permute-done.16.refs_6_
  35.8 0.0 collective-permute-done.14.refs_5_
  35.8 0.0 collective-permute-done.9.refs_0_
  35.8 1.0 %unpack.3 = (bf16[1,1,128,2048]{3,2,1,0:T(8,128)(2,1)}, bf16[1,1,128,2048]{3,2,1,0:T(8,128)(2,1)}) custom-call(bf16[256,256]{1,0:T(8,128)(2,1)S(1)} %collective-permute-done.9.refs_0_, bf16[256,256]{1,0:T(8,128)(2,1)S(1)} %collective-permute-done.10.refs_1_, ...), custom_call_target="tpu_custom_call", output_to_operand_aliasing={{0}: (7, {}), {1}: (8, {})} | custom-call | tf_op jit(solution)/shard_map/unpack/pallas_call | solution.py:394
  (3 shorter events, 0.0 us)
Async XLA Ops:
  1.8 10.8 %collective-permute-start = (bf16[512,256]{1,0:T(8,128)(2,1)S(1)}, bf16[512,256]{1,0:T(8,128)(2,1)S(1)}, u32[]{:S(2)}, u32[]{:S(2)}) collective-permute-start(bf16[512,256]{1,0:T(8,128)(2,1)S(1)} %pack.2), channel_id=1, source_target_pairs={{0,18},{1,19},{2,16},{3,17},{16,2},{17,3},{18,0},{19,1},{4,22},{5,... | collective-permute-start | bytes 786440 | tf_op jit(solution)/shard_map/ppermute | solution.py:295
  7.0 2.2 %collective-permute-start.1 = (bf16[272,256]{1,0:T(8,128)(2,1)S(1)}, bf16[272,256]{1,0:T(8,128)(2,1)S(1)}, u32[]{:S(2)}, u32[]{:S(2)}) collective-permute-start(bf16[272,256]{1,0:T(8,128)(2,1)S(1)} %get-tuple-element.38), channel_id=1, source_target_pairs={{0,1},{1,0},{2,3},{3,2},{16,17},{17,16},{18,19},{19,18},{4,5},{5,4... | collective-permute-start | bytes 417800 | tf_op jit(solution)/shard_map/ppermute | solution.py:295
  7.1 8.0 %collective-permute-start.2 = (bf16[256,256]{1,0:T(8,128)(2,1)S(1)}, bf16[256,256]{1,0:T(8,128)(2,1)S(1)}, u32[]{:S(2)}, u32[]{:S(2)}) collective-permute-start(bf16[256,256]{1,0:T(8,128)(2,1)S(1)} %get-tuple-element.44), channel_id=1, source_target_pairs={{0,16},{1,17},{2,18},{3,19},{16,0},{17,1},{18,2},{19,3},{4,20},{5,... | collective-permute-start | bytes 393224 | tf_op jit(solution)/shard_map/ppermute | solution.py:295
  7.7 9.8 %collective-permute-start.3 = (bf16[272,256]{1,0:T(8,128)(2,1)S(1)}, bf16[272,256]{1,0:T(8,128)(2,1)S(1)}, u32[]{:S(2)}, u32[]{:S(2)}) collective-permute-start(bf16[272,256]{1,0:T(8,128)(2,1)S(1)} %get-tuple-element.46), channel_id=1, source_target_pairs={{0,2},{1,3},{2,0},{3,1},{16,18},{17,19},{18,16},{19,17},{4,6},{5,7... | collective-permute-start | bytes 417800 | tf_op jit(solution)/shard_map/ppermute | solution.py:295
  7.8 9.7 %collective-permute-start.5 = (bf16[272,256]{1,0:T(8,128)(2,1)S(1)}, bf16[272,256]{1,0:T(8,128)(2,1)S(1)}, u32[]{:S(2)}, u32[]{:S(2)}) collective-permute-start(bf16[272,256]{1,0:T(8,128)(2,1)S(1)} %get-tuple-element.48), channel_id=1, source_target_pairs={{0,3},{1,2},{2,1},{3,0},{16,19},{17,18},{18,17},{19,16},{4,7},{5,6... | collective-permute-start | bytes 417800 | tf_op jit(solution)/shard_map/ppermute | solution.py:295
  12.6 5.0 %collective-permute-start.6 = (bf16[256,256]{1,0:T(8,128)(2,1)S(1)}, bf16[256,256]{1,0:T(8,128)(2,1)S(1)}, u32[]{:S(2)}, u32[]{:S(2)}) collective-permute-start(bf16[256,256]{1,0:T(8,128)(2,1)S(1)} %slice.9), channel_id=1, source_target_pairs={{0,1},{1,0},{2,3},{3,2},{16,17},{17,16},{18,19},{19,18},{4,5},{5,4... | collective-permute-start | bytes 393224 | tf_op jit(solution)/shard_map/ppermute | solution.py:295
  12.7 4.9 %collective-permute-start.7 = (bf16[256,128]{1,0:T(8,128)(2,1)S(1)}, bf16[256,128]{1,0:T(8,128)(2,1)S(1)}, u32[]{:S(2)}, u32[]{:S(2)}) collective-permute-start(bf16[256,128]{1,0:T(8,128)(2,1)S(1)} %get-tuple-element.49), channel_id=1, source_target_pairs={{0,17},{1,16},{2,19},{3,18},{16,1},{17,0},{18,3},{19,2},{4,21},{5,... | collective-permute-start | bytes 196616 | tf_op jit(solution)/shard_map/ppermute | solution.py:295
  15.1 6.8 %collective-permute-start.4 = (bf16[256,128]{1,0:T(8,128)(2,1)S(1)}, bf16[256,128]{1,0:T(8,128)(2,1)S(1)}, u32[]{:S(2)}, u32[]{:S(2)}) collective-permute-start(bf16[256,128]{1,0:T(8,128)(2,1)S(1)} %get-tuple-element.47), channel_id=1, source_target_pairs={{0,17},{1,16},{2,19},{3,18},{16,1},{17,0},{18,3},{19,2},{4,21},{5,... | collective-permute-start | bytes 196616 | tf_op jit(solution)/shard_map/ppermute | solution.py:295
  19.6 8.0 %collective-permute-start.8 = (bf16[512,128]{1,0:T(8,128)(2,1)S(1)}, bf16[512,128]{1,0:T(8,128)(2,1)S(1)}, u32[]{:S(2)}, u32[]{:S(2)}) collective-permute-start(bf16[512,128]{1,0:T(8,128)(2,1)S(1)} %get-tuple-element.57), channel_id=1, source_target_pairs={{0,18},{1,19},{2,16},{3,17},{16,2},{17,3},{18,0},{19,1},{4,22},{5,... | collective-permute-start | bytes 393224 | tf_op jit(solution)/shard_map/ppermute | solution.py:295
  24.0 7.4 %collective-permute-start.15 = (bf16[512,128]{1,0:T(8,128)(2,1)S(1)}, bf16[512,128]{1,0:T(8,128)(2,1)S(1)}, u32[]{:S(2)}, u32[]{:S(2)}) collective-permute-start(bf16[512,128]{1,0:T(8,128)(2,1)S(1)} %get-tuple-element.64), channel_id=1, source_target_pairs={{0,18},{1,19},{2,16},{3,17},{16,2},{17,3},{18,0},{19,1},{4,22},{5,... | collective-permute-start | bytes 393224 | tf_op jit(solution)/shard_map/ppermute | solution.py:295
  24.7 8.7 %collective-permute-start.10 = (bf16[256,256]{1,0:T(8,128)(2,1)S(1)}, bf16[256,256]{1,0:T(8,128)(2,1)S(1)}, u32[]{:S(2)}, u32[]{:S(2)}) collective-permute-start(bf16[256,256]{1,0:T(8,128)(2,1)S(1)} %get-tuple-element.59), channel_id=1, source_target_pairs={{0,16},{1,17},{2,18},{3,19},{16,0},{17,1},{18,2},{19,3},{4,20},{5,... | collective-permute-start | bytes 393224 | tf_op jit(solution)/shard_map/ppermute | solution.py:295
  26.1 7.3 %collective-permute-start.11 = (bf16[256,256]{1,0:T(8,128)(2,1)S(1)}, bf16[256,256]{1,0:T(8,128)(2,1)S(1)}, u32[]{:S(2)}, u32[]{:S(2)}) collective-permute-start(bf16[256,256]{1,0:T(8,128)(2,1)S(1)} %get-tuple-element.60), channel_id=1, source_target_pairs={{0,2},{1,3},{2,0},{3,1},{16,18},{17,19},{18,16},{19,17},{4,6},{5,7... | collective-permute-start | bytes 393224 | tf_op jit(solution)/shard_map/ppermute | solution.py:295
  27.6 8.3 %collective-permute-start.12 = (bf16[256,256]{1,0:T(8,128)(2,1)S(1)}, bf16[256,256]{1,0:T(8,128)(2,1)S(1)}, u32[]{:S(2)}, u32[]{:S(2)}) collective-permute-start(bf16[256,256]{1,0:T(8,128)(2,1)S(1)} %get-tuple-element.61), channel_id=1, source_target_pairs={{0,17},{1,16},{2,19},{3,18},{16,1},{17,0},{18,3},{19,2},{4,21},{5,... | collective-permute-start | bytes 393224 | tf_op jit(solution)/shard_map/ppermute | solution.py:295
  27.6 8.3 %collective-permute-start.13 = (bf16[256,256]{1,0:T(8,128)(2,1)S(1)}, bf16[256,256]{1,0:T(8,128)(2,1)S(1)}, u32[]{:S(2)}, u32[]{:S(2)}) collective-permute-start(bf16[256,256]{1,0:T(8,128)(2,1)S(1)} %get-tuple-element.62), channel_id=1, source_target_pairs={{0,3},{1,2},{2,1},{3,0},{16,19},{17,18},{18,17},{19,16},{4,7},{5,6... | collective-permute-start | bytes 393224 | tf_op jit(solution)/shard_map/ppermute | solution.py:295
  31.4 4.5 %collective-permute-start.9 = (bf16[256,256]{1,0:T(8,128)(2,1)S(1)}, bf16[256,256]{1,0:T(8,128)(2,1)S(1)}, u32[]{:S(2)}, u32[]{:S(2)}) collective-permute-start(bf16[256,256]{1,0:T(8,128)(2,1)S(1)} %get-tuple-element.58), channel_id=1, source_target_pairs={{0,1},{1,0},{2,3},{3,2},{16,17},{17,16},{18,19},{19,18},{4,5},{5,4... | collective-permute-start | bytes 393224 | tf_op jit(solution)/shard_map/ppermute | solution.py:295
  33.4 2.5 %collective-permute-start.16 = (bf16[256,128]{1,0:T(8,128)(2,1)S(1)}, bf16[256,128]{1,0:T(8,128)(2,1)S(1)}, u32[]{:S(2)}, u32[]{:S(2)}) collective-permute-start(bf16[256,128]{1,0:T(8,128)(2,1)S(1)} %slice.12), channel_id=1, source_target_pairs={{0,1},{1,0},{2,3},{3,2},{16,17},{17,16},{18,19},{19,18},{4,5},{5,4... | collective-permute-start | bytes 196616 | tf_op jit(solution)/shard_map/ppermute | solution.py:295
  33.4 2.5 %collective-permute-start.14 = (bf16[256,128]{1,0:T(8,128)(2,1)S(1)}, bf16[256,128]{1,0:T(8,128)(2,1)S(1)}, u32[]{:S(2)}, u32[]{:S(2)}) collective-permute-start(bf16[256,128]{1,0:T(8,128)(2,1)S(1)} %slice.10), channel_id=1, source_target_pairs={{0,1},{1,0},{2,3},{3,2},{16,17},{17,16},{18,19},{19,18},{4,5},{5,4... | collective-permute-start | bytes 196616 | tf_op jit(solution)/shard_map/ppermute | solution.py:295

commit v25 on v22

--- a/solution.py
+++ b/solution.py
@@ -175,7 +175,7 @@
 
 DIAGONAL = (6, 7)
 OWN, NEAR = (0,), (1,)
-ACROSS = [(4,), (5,), (2,), (3,)]
+ACROSS = [(2,), (4,), (5,), (3,)]
 REST = [OWN, NEAR, *ACROSS]
 OUTGOING = [DIAGONAL, *REST]
 INCOMING = [*OUTGOING, DIAGONAL[1:]]

time: 37.8 us -> 37.5 us (level)
    ppermute x16, waiting for transfers between devices: 13.1 us -> 12.8 us  [permuted(): return lax.ppermute(share, AXES, [(dev, dev ^ step) for dev in range(8)])]
where the time goes in v25:
time: 37.5 us; the launch traced here: 37.3 us
  starting transfers between devices  14.8 us (39%)
  waiting for transfers between devices  12.8 us (34%)
  Pallas kernels  7.69 us (21%)
  between operations  2.02 us (5%)
    ppermute x16, starting transfers between devices, permuted(): return lax.ppermute(share, AXES, [(dev, dev ^ step) for dev in range(8)])  14.8 us
    ppermute x16, waiting for transfers between devices, permuted(): return lax.ppermute(share, AXES, [(dev, dev ^ step) for dev in range(8)])  12.8 us
    pallas_call x2, Pallas kernels, attend(): pl.pallas_call(functools.partial(attend_kernel, seq_count, turn), out_sha...  4.07 us
    pallas_call x2, Pallas kernels, pack(): pl.pallas_call(functools.partial(pack_kernel, seq_count, groups), out_sha...  2.44 us
    pallas_call x1, Pallas kernels, by_pairs(): pl.pallas_call(functools.partial(unpack_kernel, seq_count), out_shape=[ou...  1.18 us
  transfers between devices with their start and end apart: 16, of which 7 were waited for; matrix products, arithmetic and copies ran while one was open for 0% of the time, Pallas kernels for 9%

profile of v25, /device:TPU:0, one launch (start us, length us, event | category | flops | bytes accessed | tf_op | source)
XLA Modules:
  0.0 37.3 jit_solution(1514154435476757596)
XLA Ops:
  0.6 1.1 %pack.2 = bf16[512,256]{1,0:T(8,128)(2,1)S(1)} custom-call(s32[1,1,2]{2,1,0:T(1,128)} %refs_0_.2, s32[1,128]{1,0:T(1,128)} %refs_1_.3, bf16[1,1,128,2048]{3,2,1,0:T(8,128)(2,1)} %refs_2_.3, bf16[1,1,128,2048]{3,2,1,0:T(8,128)(2,1)} %refs_3_.3), custom_call_target="tpu_custom_call" | custom-call | tf_op jit(solution)/shard_map/pack/pallas_call | solution.py:331
  1.8 4.0 %collective-permute-start = (bf16[512,256]{1,0:T(8,128)(2,1)S(1)}, bf16[512,256]{1,0:T(8,128)(2,1)S(1)}, u32[]{:S(2)}, u32[]{:S(2)}) collective-permute-start(bf16[512,256]{1,0:T(8,128)(2,1)S(1)} %pack.2), channel_id=1, source_target_pairs={{0,18},{1,19},{2,16},{3,17},{16,2},{17,3},{18,0},{19,1},{4,22},{5,... | collective-permute-start | bytes 786440 | tf_op jit(solution)/shard_map/ppermute | solution.py:297
  5.7 1.3 %pack.3 = (bf16[272,256]{1,0:T(8,128)(2,1)S(1)}, bf16[272,256]{1,0:T(8,128)(2,1)S(1)}, bf16[272,256]{1,0:T(8,128)(2,1)S(1)}, bf16[256,256]{1,0:T(8,128)(2,1)S(1)...) custom-call(s32[1,1,2]{2,1,0:T(1,128)} %refs_0_.2, s32[1,128]{1,0:T(1,128)} %refs_1_.3, ...), custom_call_target="tpu_custom_call" | custom-call | tf_op jit(solution)/shard_map/pack/pallas_call | solution.py:331
  7.0 0.1 collective-permute-start.1
  7.1 0.6 %collective-permute-start.2 = (bf16[272,256]{1,0:T(8,128)(2,1)S(1)}, bf16[272,256]{1,0:T(8,128)(2,1)S(1)}, u32[]{:S(2)}, u32[]{:S(2)}) collective-permute-start(bf16[272,256]{1,0:T(8,128)(2,1)S(1)} %get-tuple-element.34), channel_id=1, source_target_pairs={{0,2},{1,3},{2,0},{3,1},{16,18},{17,19},{18,16},{19,17},{4,6},{5,7... | collective-permute-start | bytes 417800 | tf_op jit(solution)/shard_map/ppermute | solution.py:297
  7.7 1.3 %collective-permute-start.5 = (bf16[272,256]{1,0:T(8,128)(2,1)S(1)}, bf16[272,256]{1,0:T(8,128)(2,1)S(1)}, u32[]{:S(2)}, u32[]{:S(2)}) collective-permute-start(bf16[272,256]{1,0:T(8,128)(2,1)S(1)} %get-tuple-element.37), channel_id=1, source_target_pairs={{0,3},{1,2},{2,1},{3,0},{16,19},{17,18},{18,17},{19,16},{4,7},{5,6... | collective-permute-start | bytes 417800 | tf_op jit(solution)/shard_map/ppermute | solution.py:297
  9.0 0.5 %collective-permute-start.3 = (bf16[256,256]{1,0:T(8,128)(2,1)S(1)}, bf16[256,256]{1,0:T(8,128)(2,1)S(1)}, u32[]{:S(2)}, u32[]{:S(2)}) collective-permute-start(bf16[256,256]{1,0:T(8,128)(2,1)S(1)} %get-tuple-element.35), channel_id=1, source_target_pairs={{0,16},{1,17},{2,18},{3,19},{16,0},{17,1},{18,2},{19,3},{4,20},{5,... | collective-permute-start | bytes 393224 | tf_op jit(solution)/shard_map/ppermute | solution.py:297
  9.5 0.0 collective-permute-done.1.refs_2_
  9.5 1.2 %collective-permute-start.4 = (bf16[256,256]{1,0:T(8,128)(2,1)S(1)}, bf16[256,256]{1,0:T(8,128)(2,1)S(1)}, u32[]{:S(2)}, u32[]{:S(2)}) collective-permute-start(bf16[256,256]{1,0:T(8,128)(2,1)S(1)} %get-tuple-element.36), channel_id=1, source_target_pairs={{0,17},{1,16},{2,19},{3,18},{16,1},{17,0},{18,3},{19,2},{4,21},{5,... | collective-permute-start | bytes 393224 | tf_op jit(solution)/shard_map/ppermute | solution.py:297
  10.7 2.2 %collective-permute-done.refs_0_ = bf16[512,256]{1,0:T(8,128)(2,1)S(1)} collective-permute-done((bf16[512,256]{1,0:T(8,128)(2,1)S(1)}, bf16[512,256]{1,0:T(8,128)(2,1)S(1)}, u32[]{:S(2)}, u32[]{:S(2)}) %collective-permute-start) | collective-permute-done | bytes 262176 | tf_op jit(solution)/shard_map/ppermute | solution.py:297
  12.9 0.1 collective-permute-start.6
  14.2 1.3 %collective-permute-done.3.refs_4_ = bf16[256,256]{1,0:T(8,128)(2,1)S(1)} collective-permute-done((bf16[256,256]{1,0:T(8,128)(2,1)S(1)}, bf16[256,256]{1,0:T(8,128)(2,1)S(1)}, u32[]{:S(2)}, u32[]{:S(2)}) %collective-permute-start.3) | collective-permute-done | bytes 131104 | tf_op jit(solution)/shard_map/ppermute | solution.py:297
  15.5 2.2 %collective-permute-done.4.refs_5_ = bf16[256,256]{1,0:T(8,128)(2,1)S(1)} collective-permute-done((bf16[256,256]{1,0:T(8,128)(2,1)S(1)}, bf16[256,256]{1,0:T(8,128)(2,1)S(1)}, u32[]{:S(2)}, u32[]{:S(2)}) %collective-permute-start.4) | collective-permute-done | bytes 131104 | tf_op jit(solution)/shard_map/ppermute | solution.py:297
  17.7 0.0 collective-permute-done.2.refs_3_
  17.7 0.0 collective-permute-done.5.refs_6_
  17.7 0.0 collective-permute-done.6.refs_7_
  17.7 2.0 %attend.2 = (bf16[512,128]{1,0:T(8,128)(2,1)S(1)}, bf16[256,128]{1,0:T(8,128)(2,1)S(1)}, bf16[256,128]{1,0:T(8,128)(2,1)S(1)}, bf16[256,128]{1,0:T(8,128)(2,1)S(...) custom-call(s32[1]{0:T(128)S(6)} %copy.8.source_len, ...), custom_call_target="tpu_custom_call" | custom-call | flops 167772160 | bytes 1048576 | tf_op jit(solution)/shard_map/attend/pallas_call | solution.py:356
  19.7 2.6 %collective-permute-start.7 = (bf16[512,128]{1,0:T(8,128)(2,1)S(1)}, bf16[512,128]{1,0:T(8,128)(2,1)S(1)}, u32[]{:S(2)}, u32[]{:S(2)}) collective-permute-start(bf16[512,128]{1,0:T(8,128)(2,1)S(1)} %get-tuple-element.45), channel_id=1, source_target_pairs={{0,18},{1,19},{2,16},{3,17},{16,2},{17,3},{18,0},{19,1},{4,22},{5,... | collective-permute-start | bytes 393224 | tf_op jit(solution)/shard_map/ppermute | solution.py:297
  22.3 2.1 %attend.3 = (bf16[512,128]{1,0:T(8,128)(2,1)S(1)}, bf16[256,256]{1,0:T(8,128)(2,1)S(1)}, bf16[256,256]{1,0:T(8,128)(2,1)S(1)}, bf16[256,256]{1,0:T(8,128)(2,1)S(...) custom-call(s32[1]{0:T(128)S(6)} %copy.8.source_len, ...), custom_call_target="tpu_custom_call" | custom-call | flops 167772160 | bytes 1048576 | tf_op jit(solution)/shard_map/attend/pallas_call | solution.py:356
  24.4 0.5 %collective-permute-start.8 = (bf16[512,128]{1,0:T(8,128)(2,1)S(1)}, bf16[512,128]{1,0:T(8,128)(2,1)S(1)}, u32[]{:S(2)}, u32[]{:S(2)}) collective-permute-start(bf16[512,128]{1,0:T(8,128)(2,1)S(1)} %get-tuple-element.47), channel_id=1, source_target_pairs={{0,18},{1,19},{2,16},{3,17},{16,2},{17,3},{18,0},{19,1},{4,22},{5,... | collective-permute-start | bytes 393224 | tf_op jit(solution)/shard_map/ppermute | solution.py:297
  24.8 1.4 %collective-permute-start.12 = (bf16[256,256]{1,0:T(8,128)(2,1)S(1)}, bf16[256,256]{1,0:T(8,128)(2,1)S(1)}, u32[]{:S(2)}, u32[]{:S(2)}) collective-permute-start(bf16[256,256]{1,0:T(8,128)(2,1)S(1)} %get-tuple-element.50), channel_id=1, source_target_pairs={{0,2},{1,3},{2,0},{3,1},{16,18},{17,19},{18,16},{19,17},{4,6},{5,7... | collective-permute-start | bytes 393224 | tf_op jit(solution)/shard_map/ppermute | solution.py:297
  26.2 1.7 %collective-permute-start.13 = (bf16[256,256]{1,0:T(8,128)(2,1)S(1)}, bf16[256,256]{1,0:T(8,128)(2,1)S(1)}, u32[]{:S(2)}, u32[]{:S(2)}) collective-permute-start(bf16[256,256]{1,0:T(8,128)(2,1)S(1)} %get-tuple-element.51), channel_id=1, source_target_pairs={{0,16},{1,17},{2,18},{3,19},{16,0},{17,1},{18,2},{19,3},{4,20},{5,... | collective-permute-start | bytes 393224 | tf_op jit(solution)/shard_map/ppermute | solution.py:297
  27.9 0.0 collective-permute-start.14
  27.9 0.0 collective-permute-done.7.refs_0_
  27.9 0.7 %collective-permute-start.15 = (bf16[256,256]{1,0:T(8,128)(2,1)S(1)}, bf16[256,256]{1,0:T(8,128)(2,1)S(1)}, u32[]{:S(2)}, u32[]{:S(2)}) collective-permute-start(bf16[256,256]{1,0:T(8,128)(2,1)S(1)} %get-tuple-element.53), channel_id=1, source_target_pairs={{0,3},{1,2},{2,1},{3,0},{16,19},{17,18},{18,17},{19,16},{4,7},{5,6... | collective-permute-start | bytes 393224 | tf_op jit(solution)/shard_map/ppermute | solution.py:297
  28.6 3.1 %collective-permute-done.8.refs_1_ = bf16[512,128]{1,0:T(8,128)(2,1)S(1)} collective-permute-done((bf16[512,128]{1,0:T(8,128)(2,1)S(1)}, bf16[512,128]{1,0:T(8,128)(2,1)S(1)}, u32[]{:S(2)}, u32[]{:S(2)}) %collective-permute-start.8) | collective-permute-done | bytes 131104 | tf_op jit(solution)/shard_map/ppermute | solution.py:297
  31.7 0.0 collective-permute-start.11
  31.8 1.6 %collective-permute-done.12.refs_6_ = bf16[256,256]{1,0:T(8,128)(2,1)S(1)} collective-permute-done((bf16[256,256]{1,0:T(8,128)(2,1)S(1)}, bf16[256,256]{1,0:T(8,128)(2,1)S(1)}, u32[]{:S(2)}, u32[]{:S(2)}) %collective-permute-start.12) | collective-permute-done | bytes 131104 | tf_op jit(solution)/shard_map/ppermute | solution.py:297
  33.3 0.0 collective-permute-start.10
  33.3 0.2 collective-permute-done.13.refs_7_
  33.5 0.3 collective-permute-start.9
  33.8 2.2 %collective-permute-done.14.refs_8_ = bf16[256,256]{1,0:T(8,128)(2,1)S(1)} collective-permute-done((bf16[256,256]{1,0:T(8,128)(2,1)S(1)}, bf16[256,256]{1,0:T(8,128)(2,1)S(1)}, u32[]{:S(2)}, u32[]{:S(2)}) %collective-permute-start.14) | collective-permute-done | bytes 131104 | tf_op jit(solution)/shard_map/ppermute | solution.py:297
  36.1 0.0 collective-permute-done.15.refs_9_
  36.1 0.0 collective-permute-done.10.refs_3_
  36.1 0.0 collective-permute-done.9.refs_2_
  36.1 0.0 collective-permute-done.11.refs_5_
  36.1 1.2 %unpack.1 = (bf16[1,1,128,2048]{3,2,1,0:T(8,128)(2,1)}, bf16[1,1,128,2048]{3,2,1,0:T(8,128)(2,1)}) custom-call(bf16[512,128]{1,0:T(8,128)(2,1)S(1)} %collective-permute-done.7.refs_0_, bf16[512,128]{1,0:T(8,128)(2,1)S(1)} %collective-permute-done.8.refs_1_, bf16[256,128]{1,0:T(8,128)(2,1)S(1)} %collective-permute-done.9.refs_2_, ...), custom_call_target="tpu_custom_call" | custom-call | tf_op jit(solution)/shard_map/unpack/pallas_call | solution.py:376
  (3 shorter events, 0.0 us)
Async XLA Ops:
  1.8 11.1 %collective-permute-start = (bf16[512,256]{1,0:T(8,128)(2,1)S(1)}, bf16[512,256]{1,0:T(8,128)(2,1)S(1)}, u32[]{:S(2)}, u32[]{:S(2)}) collective-permute-start(bf16[512,256]{1,0:T(8,128)(2,1)S(1)} %pack.2), channel_id=1, source_target_pairs={{0,18},{1,19},{2,16},{3,17},{16,2},{17,3},{18,0},{19,1},{4,22},{5,... | collective-permute-start | bytes 786440 | tf_op jit(solution)/shard_map/ppermute | solution.py:297
  7.0 2.5 %collective-permute-start.1 = (bf16[272,256]{1,0:T(8,128)(2,1)S(1)}, bf16[272,256]{1,0:T(8,128)(2,1)S(1)}, u32[]{:S(2)}, u32[]{:S(2)}) collective-permute-start(bf16[272,256]{1,0:T(8,128)(2,1)S(1)} %get-tuple-element.30), channel_id=1, source_target_pairs={{0,1},{1,0},{2,3},{3,2},{16,17},{17,16},{18,19},{19,18},{4,5},{5,4... | collective-permute-start | bytes 417800 | tf_op jit(solution)/shard_map/ppermute | solution.py:297
  7.1 10.6 %collective-permute-start.2 = (bf16[272,256]{1,0:T(8,128)(2,1)S(1)}, bf16[272,256]{1,0:T(8,128)(2,1)S(1)}, u32[]{:S(2)}, u32[]{:S(2)}) collective-permute-start(bf16[272,256]{1,0:T(8,128)(2,1)S(1)} %get-tuple-element.34), channel_id=1, source_target_pairs={{0,2},{1,3},{2,0},{3,1},{16,18},{17,19},{18,16},{19,17},{4,6},{5,7... | collective-permute-start | bytes 417800 | tf_op jit(solution)/shard_map/ppermute | solution.py:297
  7.7 10.0 %collective-permute-start.5 = (bf16[272,256]{1,0:T(8,128)(2,1)S(1)}, bf16[272,256]{1,0:T(8,128)(2,1)S(1)}, u32[]{:S(2)}, u32[]{:S(2)}) collective-permute-start(bf16[272,256]{1,0:T(8,128)(2,1)S(1)} %get-tuple-element.37), channel_id=1, source_target_pairs={{0,3},{1,2},{2,1},{3,0},{16,19},{17,18},{18,17},{19,16},{4,7},{5,6... | collective-permute-start | bytes 417800 | tf_op jit(solution)/shard_map/ppermute | solution.py:297
  9.0 6.5 %collective-permute-start.3 = (bf16[256,256]{1,0:T(8,128)(2,1)S(1)}, bf16[256,256]{1,0:T(8,128)(2,1)S(1)}, u32[]{:S(2)}, u32[]{:S(2)}) collective-permute-start(bf16[256,256]{1,0:T(8,128)(2,1)S(1)} %get-tuple-element.35), channel_id=1, source_target_pairs={{0,16},{1,17},{2,18},{3,19},{16,0},{17,1},{18,2},{19,3},{4,20},{5,... | collective-permute-start | bytes 393224 | tf_op jit(solution)/shard_map/ppermute | solution.py:297
  9.5 8.2 %collective-permute-start.4 = (bf16[256,256]{1,0:T(8,128)(2,1)S(1)}, bf16[256,256]{1,0:T(8,128)(2,1)S(1)}, u32[]{:S(2)}, u32[]{:S(2)}) collective-permute-start(bf16[256,256]{1,0:T(8,128)(2,1)S(1)} %get-tuple-element.36), channel_id=1, source_target_pairs={{0,17},{1,16},{2,19},{3,18},{16,1},{17,0},{18,3},{19,2},{4,21},{5,... | collective-permute-start | bytes 393224 | tf_op jit(solution)/shard_map/ppermute | solution.py:297
  12.9 4.8 %collective-permute-start.6 = (bf16[256,256]{1,0:T(8,128)(2,1)S(1)}, bf16[256,256]{1,0:T(8,128)(2,1)S(1)}, u32[]{:S(2)}, u32[]{:S(2)}) collective-permute-start(bf16[256,256]{1,0:T(8,128)(2,1)S(1)} %slice.9), channel_id=1, source_target_pairs={{0,1},{1,0},{2,3},{3,2},{16,17},{17,16},{18,19},{19,18},{4,5},{5,4... | collective-permute-start | bytes 393224 | tf_op jit(solution)/shard_map/ppermute | solution.py:297
  19.7 8.2 %collective-permute-start.7 = (bf16[512,128]{1,0:T(8,128)(2,1)S(1)}, bf16[512,128]{1,0:T(8,128)(2,1)S(1)}, u32[]{:S(2)}, u32[]{:S(2)}) collective-permute-start(bf16[512,128]{1,0:T(8,128)(2,1)S(1)} %get-tuple-element.45), channel_id=1, source_target_pairs={{0,18},{1,19},{2,16},{3,17},{16,2},{17,3},{18,0},{19,1},{4,22},{5,... | collective-permute-start | bytes 393224 | tf_op jit(solution)/shard_map/ppermute | solution.py:297
  24.4 7.3 %collective-permute-start.8 = (bf16[512,128]{1,0:T(8,128)(2,1)S(1)}, bf16[512,128]{1,0:T(8,128)(2,1)S(1)}, u32[]{:S(2)}, u32[]{:S(2)}) collective-permute-start(bf16[512,128]{1,0:T(8,128)(2,1)S(1)} %get-tuple-element.47), channel_id=1, source_target_pairs={{0,18},{1,19},{2,16},{3,17},{16,2},{17,3},{18,0},{19,1},{4,22},{5,... | collective-permute-start | bytes 393224 | tf_op jit(solution)/shard_map/ppermute | solution.py:297
  24.8 8.5 %collective-permute-start.12 = (bf16[256,256]{1,0:T(8,128)(2,1)S(1)}, bf16[256,256]{1,0:T(8,128)(2,1)S(1)}, u32[]{:S(2)}, u32[]{:S(2)}) collective-permute-start(bf16[256,256]{1,0:T(8,128)(2,1)S(1)} %get-tuple-element.50), channel_id=1, source_target_pairs={{0,2},{1,3},{2,0},{3,1},{16,18},{17,19},{18,16},{19,17},{4,6},{5,7... | collective-permute-start | bytes 393224 | tf_op jit(solution)/shard_map/ppermute | solution.py:297
  26.2 7.3 %collective-permute-start.13 = (bf16[256,256]{1,0:T(8,128)(2,1)S(1)}, bf16[256,256]{1,0:T(8,128)(2,1)S(1)}, u32[]{:S(2)}, u32[]{:S(2)}) collective-permute-start(bf16[256,256]{1,0:T(8,128)(2,1)S(1)} %get-tuple-element.51), channel_id=1, source_target_pairs={{0,16},{1,17},{2,18},{3,19},{16,0},{17,1},{18,2},{19,3},{4,20},{5,... | collective-permute-start | bytes 393224 | tf_op jit(solution)/shard_map/ppermute | solution.py:297
  27.9 8.1 %collective-permute-start.14 = (bf16[256,256]{1,0:T(8,128)(2,1)S(1)}, bf16[256,256]{1,0:T(8,128)(2,1)S(1)}, u32[]{:S(2)}, u32[]{:S(2)}) collective-permute-start(bf16[256,256]{1,0:T(8,128)(2,1)S(1)} %get-tuple-element.52), channel_id=1, source_target_pairs={{0,17},{1,16},{2,19},{3,18},{16,1},{17,0},{18,3},{19,2},{4,21},{5,... | collective-permute-start | bytes 393224 | tf_op jit(solution)/shard_map/ppermute | solution.py:297
  27.9 8.1 %collective-permute-start.15 = (bf16[256,256]{1,0:T(8,128)(2,1)S(1)}, bf16[256,256]{1,0:T(8,128)(2,1)S(1)}, u32[]{:S(2)}, u32[]{:S(2)}) collective-permute-start(bf16[256,256]{1,0:T(8,128)(2,1)S(1)} %get-tuple-element.53), channel_id=1, source_target_pairs={{0,3},{1,2},{2,1},{3,0},{16,19},{17,18},{18,17},{19,16},{4,7},{5,6... | collective-permute-start | bytes 393224 | tf_op jit(solution)/shard_map/ppermute | solution.py:297
  31.7 4.3 %collective-permute-start.11 = (bf16[256,256]{1,0:T(8,128)(2,1)S(1)}, bf16[256,256]{1,0:T(8,128)(2,1)S(1)}, u32[]{:S(2)}, u32[]{:S(2)}) collective-permute-start(bf16[256,256]{1,0:T(8,128)(2,1)S(1)} %get-tuple-element.49), channel_id=1, source_target_pairs={{0,1},{1,0},{2,3},{3,2},{16,17},{17,16},{18,19},{19,18},{4,5},{5,4... | collective-permute-start | bytes 393224 | tf_op jit(solution)/shard_map/ppermute | solution.py:297
  33.3 2.7 %collective-permute-start.10 = (bf16[256,128]{1,0:T(8,128)(2,1)S(1)}, bf16[256,128]{1,0:T(8,128)(2,1)S(1)}, u32[]{:S(2)}, u32[]{:S(2)}) collective-permute-start(bf16[256,128]{1,0:T(8,128)(2,1)S(1)} %slice.12), channel_id=1, source_target_pairs={{0,1},{1,0},{2,3},{3,2},{16,17},{17,16},{18,19},{19,18},{4,5},{5,4... | collective-permute-start | bytes 196616 | tf_op jit(solution)/shard_map/ppermute | solution.py:297
  33.5 2.5 %collective-permute-start.9 = (bf16[256,128]{1,0:T(8,128)(2,1)S(1)}, bf16[256,128]{1,0:T(8,128)(2,1)S(1)}, u32[]{:S(2)}, u32[]{:S(2)}) collective-permute-start(bf16[256,128]{1,0:T(8,128)(2,1)S(1)} %slice.10), channel_id=1, source_target_pairs={{0,1},{1,0},{2,3},{3,2},{16,17},{17,16},{18,19},{19,18},{4,5},{5,4... | collective-permute-start | bytes 196616 | tf_op jit(solution)/shard_map/ppermute | solution.py:297

commit v26 on v20

--- a/solution.py
+++ b/solution.py
@@ -270,16 +270,15 @@
 
 
 def unpack_kernel(seq_count, *refs):
-    diagonals, handed_on, shares = refs[:TILES], refs[TILES : 2 * TILES], refs[2 * TILES : -3]
+    diagonals, shares = refs[:TILES], refs[TILES:-3]
     first, second, sem = refs[-3:]
     width = first.shape[3] // (2 * seq_count)
     me = device_index(seq_count)
     pieces = [
-        (step, tile * LANES, share.at[pl.ds(0, 2 * BLK)])
-        for step, arrived in zip(DIAGONAL, (diagonals, handed_on))
-        for tile, share in enumerate(arrived)
+        (DIAGONAL[0], tile * LANES, share.at[pl.ds(0, 2 * BLK)])
+        for tile, share in enumerate(diagonals)
     ]
-    pieces += [(step, 0, share) for (step,), share in zip(REST, shares)]
+    pieces += [(group[0], 0, share) for group, share in zip([DIAGONAL[1:], *REST], shares)]
     copies = []
     for slot, (step, start, share) in enumerate(pieces):
         lanes = pl.ds(pl.multiple_of((me ^ step) * width + start, LANES), share.shape[1])
@@ -306,7 +305,8 @@
     moved[NEAR] = permuted(held[NEAR], NEAR[0])
     if len(diagonals) == 1:
         diagonals[0], moved[NEAR] = lax.optimization_barrier((diagonals[0], moved[NEAR]))
-    handed_on = [permuted(share[share.shape[0] // 2 :], NEAR[0]) for share in diagonals]
+    handed_on = [share[share.shape[0] // 2 :] for share in diagonals]
+    handed_on = permuted(jnp.concatenate(handed_on, axis=1), NEAR[0])
     return diagonals, [held[OWN], moved[NEAR], *(moved[group] for group in ACROSS)], handed_on
 
 
@@ -346,7 +346,7 @@
     (diagonal,) = pack([DIAGONAL], alignment)
     lists, diagonal = lax.optimization_barrier((alignment, diagonal))
     diagonals, shares, handed_on = swapped([diagonal], pack(REST, lists))
-    coming = [*diagonals, *shares, *handed_on]
+    coming = [*diagonals, *shares, handed_on]
     rows = pltpu.VMEM((parts, 2, BLK, LANES), kind)
     grads = pltpu.VMEM((seq_count, BLK, LANES), jnp.float32)
     turned = pltpu.VMEM((seq_count, 2, LANES, BLK), kind)
@@ -376,12 +376,12 @@
     return pl.pallas_call(
         functools.partial(unpack_kernel, seq_count),
         out_shape=[out_shape, out_shape],
-        in_specs=specs(2 * TILES + len(REST), pltpu.VMEM),
+        in_specs=specs(TILES + 1 + len(REST), pltpu.VMEM),
         out_specs=specs(2, pltpu.HBM),
         scratch_shapes=[pltpu.SemaphoreType.DMA((2, parts + 2 * TILES))],
         compiler_params=params,
         name="unpack",
-    )(*diagonals, *handed_on, *shares)
+    )(*diagonals, handed_on, *shares)
 
 
 def on_device(first_rows, second_rows, alignment, diffusion_mask, source_length, target_length):

time: 36.5 us -> 36.5 us (level)
  local copies, waits for them, and re-layouts: 0.02 us -> 0.85 us
  starting transfers between devices: 15 us -> 14.5 us
  waiting for transfers between devices: 11.5 us -> 11.1 us
    slice x3 -> x4, local copies, waits for them, and re-layouts: 0.02 us -> 0.85 us  [swapped(): handed_on = [share[share.shape[0] // 2:] for share in diagonals]]
    ppermute x16 -> x15, starting transfers between devices: 15 us -> 14.5 us  [permuted(): return lax.ppermute(share, AXES, [(dev, dev ^ step) for dev in range(8)])]
    ppermute x16 -> x15, waiting for transfers between devices: 11.5 us -> 11.1 us  [permuted(): return lax.ppermute(share, AXES, [(dev, dev ^ step) for dev in range(8)])]
  transfers between devices with their start and end apart: 16 -> 15, of which waited for: 6 -> 6; matrix products, arithmetic and copies ran while one was open for 0% -> 0% of each run, Pallas kernels for 9% -> 9%
where the time goes in v26:
time: 36.5 us; the launch traced here: 36.2 us
  starting transfers between devices  14.5 us (40%)
  waiting for transfers between devices  11.1 us (30%)
  Pallas kernels  7.7 us (21%)
  between operations  2.02 us (6%)
  local copies, waits for them, and re-layouts  0.85 us (2%)
    ppermute x15, starting transfers between devices, permuted(): return lax.ppermute(share, AXES, [(dev, dev ^ step) for dev in range(8)])  14.5 us
    ppermute x15, waiting for transfers between devices, permuted(): return lax.ppermute(share, AXES, [(dev, dev ^ step) for dev in range(8)])  11.1 us
    pallas_call x2, Pallas kernels, attend(): pl.pallas_call(functools.partial(attend_kernel, seq_count, turn), out_sha...  4.08 us
    pallas_call x2, Pallas kernels, pack(): pl.pallas_call(functools.partial(pack_kernel, seq_count, groups), out_sha...  2.44 us
    pallas_call x1, Pallas kernels, by_pairs(): pl.pallas_call(functools.partial(unpack_kernel, seq_count), out_shape=[ou...  1.18 us
    slice x4, local copies, waits for them, and re-layouts, swapped(): handed_on = [share[share.shape[0] // 2:] for share in diagonals]  0.85 us
  transfers between devices with their start and end apart: 15, of which 6 were waited for; matrix products, arithmetic and copies ran while one was open for 0% of the time, Pallas kernels for 9%

profile of v26, /device:TPU:0, one launch (start us, length us, event | category | flops | bytes accessed | tf_op | source)
XLA Modules:
  0.0 36.2 jit_solution(10739878409594135260)
XLA Ops:
  0.6 1.1 %pack.2 = bf16[512,256]{1,0:T(8,128)(2,1)S(1)} custom-call(s32[1,1,2]{2,1,0:T(1,128)} %refs_0_.2, s32[1,128]{1,0:T(1,128)} %refs_1_.3, bf16[1,1,128,2048]{3,2,1,0:T(8,128)(2,1)} %refs_2_.3, bf16[1,1,128,2048]{3,2,1,0:T(8,128)(2,1)} %refs_3_.3), custom_call_target="tpu_custom_call" | custom-call | tf_op jit(solution)/shard_map/pack/pallas_call | solution.py:331
  1.8 4.0 %collective-permute-start = (bf16[512,256]{1,0:T(8,128)(2,1)S(1)}, bf16[512,256]{1,0:T(8,128)(2,1)S(1)}, u32[]{:S(2)}, u32[]{:S(2)}) collective-permute-start(bf16[512,256]{1,0:T(8,128)(2,1)S(1)} %pack.2), channel_id=1, source_target_pairs={{0,18},{1,19},{2,16},{3,17},{16,2},{17,3},{18,0},{19,1},{4,22},{5,... | collective-permute-start | bytes 786440 | tf_op jit(solution)/shard_map/ppermute | solution.py:296
  5.7 1.3 %pack.3 = (bf16[272,256]{1,0:T(8,128)(2,1)S(1)}, bf16[272,256]{1,0:T(8,128)(2,1)S(1)}, bf16[256,256]{1,0:T(8,128)(2,1)S(1)}, bf16[272,256]{1,0:T(8,128)(2,1)S(1)...) custom-call(s32[1,1,2]{2,1,0:T(1,128)} %refs_0_.2, s32[1,128]{1,0:T(1,128)} %refs_1_.3, ...), custom_call_target="tpu_custom_call" | custom-call | tf_op jit(solution)/shard_map/pack/pallas_call | solution.py:331
  7.0 0.1 collective-permute-start.1
  7.1 0.6 %collective-permute-start.3 = (bf16[272,256]{1,0:T(8,128)(2,1)S(1)}, bf16[272,256]{1,0:T(8,128)(2,1)S(1)}, u32[]{:S(2)}, u32[]{:S(2)}) collective-permute-start(bf16[272,256]{1,0:T(8,128)(2,1)S(1)} %get-tuple-element.35), channel_id=1, source_target_pairs={{0,2},{1,3},{2,0},{3,1},{16,18},{17,19},{18,16},{19,17},{4,6},{5,7... | collective-permute-start | bytes 417800 | tf_op jit(solution)/shard_map/ppermute | solution.py:296
  7.7 1.3 %collective-permute-start.5 = (bf16[272,256]{1,0:T(8,128)(2,1)S(1)}, bf16[272,256]{1,0:T(8,128)(2,1)S(1)}, u32[]{:S(2)}, u32[]{:S(2)}) collective-permute-start(bf16[272,256]{1,0:T(8,128)(2,1)S(1)} %get-tuple-element.37), channel_id=1, source_target_pairs={{0,3},{1,2},{2,1},{3,0},{16,19},{17,18},{18,17},{19,16},{4,7},{5,6... | collective-permute-start | bytes 417800 | tf_op jit(solution)/shard_map/ppermute | solution.py:296
  9.0 0.5 %collective-permute-start.2 = (bf16[256,256]{1,0:T(8,128)(2,1)S(1)}, bf16[256,256]{1,0:T(8,128)(2,1)S(1)}, u32[]{:S(2)}, u32[]{:S(2)}) collective-permute-start(bf16[256,256]{1,0:T(8,128)(2,1)S(1)} %get-tuple-element.34), channel_id=1, source_target_pairs={{0,16},{1,17},{2,18},{3,19},{16,0},{17,1},{18,2},{19,3},{4,20},{5,... | collective-permute-start | bytes 393224 | tf_op jit(solution)/shard_map/ppermute | solution.py:296
  9.5 0.0 collective-permute-done.1.refs_2_
  9.5 1.2 %collective-permute-start.4 = (bf16[256,256]{1,0:T(8,128)(2,1)S(1)}, bf16[256,256]{1,0:T(8,128)(2,1)S(1)}, u32[]{:S(2)}, u32[]{:S(2)}) collective-permute-start(bf16[256,256]{1,0:T(8,128)(2,1)S(1)} %get-tuple-element.36), channel_id=1, source_target_pairs={{0,17},{1,16},{2,19},{3,18},{16,1},{17,0},{18,3},{19,2},{4,21},{5,... | collective-permute-start | bytes 393224 | tf_op jit(solution)/shard_map/ppermute | solution.py:296
  10.7 2.2 %collective-permute-done.refs_0_ = bf16[512,256]{1,0:T(8,128)(2,1)S(1)} collective-permute-done((bf16[512,256]{1,0:T(8,128)(2,1)S(1)}, bf16[512,256]{1,0:T(8,128)(2,1)S(1)}, u32[]{:S(2)}, u32[]{:S(2)}) %collective-permute-start) | collective-permute-done | bytes 262176 | tf_op jit(solution)/shard_map/ppermute | solution.py:296
  12.9 0.1 collective-permute-start.6
  14.2 1.3 %collective-permute-done.2.refs_3_ = bf16[256,256]{1,0:T(8,128)(2,1)S(1)} collective-permute-done((bf16[256,256]{1,0:T(8,128)(2,1)S(1)}, bf16[256,256]{1,0:T(8,128)(2,1)S(1)}, u32[]{:S(2)}, u32[]{:S(2)}) %collective-permute-start.2) | collective-permute-done | bytes 131104 | tf_op jit(solution)/shard_map/ppermute | solution.py:296
  15.5 2.2 %collective-permute-done.4.refs_5_ = bf16[256,256]{1,0:T(8,128)(2,1)S(1)} collective-permute-done((bf16[256,256]{1,0:T(8,128)(2,1)S(1)}, bf16[256,256]{1,0:T(8,128)(2,1)S(1)}, u32[]{:S(2)}, u32[]{:S(2)}) %collective-permute-start.4) | collective-permute-done | bytes 131104 | tf_op jit(solution)/shard_map/ppermute | solution.py:296
  17.7 0.0 collective-permute-done.3.refs_4_
  17.7 0.0 collective-permute-done.5.refs_6_
  17.7 0.0 collective-permute-done.6.refs_7_
  17.7 2.0 %attend.2 = (bf16[512,128]{1,0:T(8,128)(2,1)S(1)}, bf16[256,128]{1,0:T(8,128)(2,1)S(1)}, bf16[256,128]{1,0:T(8,128)(2,1)S(1)}, bf16[256,128]{1,0:T(8,128)(2,1)S(...) custom-call(s32[1]{0:T(128)S(6)} %copy.8.source_len, ...), custom_call_target="tpu_custom_call" | custom-call | flops 167772160 | bytes 1048576 | tf_op jit(solution)/shard_map/attend/pallas_call | solution.py:356
  19.7 2.6 %collective-permute-start.7 = (bf16[512,128]{1,0:T(8,128)(2,1)S(1)}, bf16[512,128]{1,0:T(8,128)(2,1)S(1)}, u32[]{:S(2)}, u32[]{:S(2)}) collective-permute-start(bf16[512,128]{1,0:T(8,128)(2,1)S(1)} %get-tuple-element.45), channel_id=1, source_target_pairs={{0,18},{1,19},{2,16},{3,17},{16,2},{17,3},{18,0},{19,1},{4,22},{5,... | collective-permute-start | bytes 393224 | tf_op jit(solution)/shard_map/ppermute | solution.py:296
  22.3 2.1 %attend.3 = (bf16[512,128]{1,0:T(8,128)(2,1)S(1)}, bf16[256,256]{1,0:T(8,128)(2,1)S(1)}, bf16[256,256]{1,0:T(8,128)(2,1)S(1)}, bf16[256,256]{1,0:T(8,128)(2,1)S(...) custom-call(s32[1]{0:T(128)S(6)} %copy.8.source_len, ...), custom_call_target="tpu_custom_call" | custom-call | flops 167772160 | bytes 1048576 | tf_op jit(solution)/shard_map/attend/pallas_call | solution.py:356
  24.4 0.5 %collective-permute-start.8 = (bf16[512,128]{1,0:T(8,128)(2,1)S(1)}, bf16[512,128]{1,0:T(8,128)(2,1)S(1)}, u32[]{:S(2)}, u32[]{:S(2)}) collective-permute-start(bf16[512,128]{1,0:T(8,128)(2,1)S(1)} %get-tuple-element.47), channel_id=1, source_target_pairs={{0,18},{1,19},{2,16},{3,17},{16,2},{17,3},{18,0},{19,1},{4,22},{5,... | collective-permute-start | bytes 393224 | tf_op jit(solution)/shard_map/ppermute | solution.py:296
  24.8 1.4 %collective-permute-start.11 = (bf16[256,256]{1,0:T(8,128)(2,1)S(1)}, bf16[256,256]{1,0:T(8,128)(2,1)S(1)}, u32[]{:S(2)}, u32[]{:S(2)}) collective-permute-start(bf16[256,256]{1,0:T(8,128)(2,1)S(1)} %get-tuple-element.50), channel_id=1, source_target_pairs={{0,16},{1,17},{2,18},{3,19},{16,0},{17,1},{18,2},{19,3},{4,20},{5,... | collective-permute-start | bytes 393224 | tf_op jit(solution)/shard_map/ppermute | solution.py:296
  26.3 1.7 %collective-permute-start.12 = (bf16[256,256]{1,0:T(8,128)(2,1)S(1)}, bf16[256,256]{1,0:T(8,128)(2,1)S(1)}, u32[]{:S(2)}, u32[]{:S(2)}) collective-permute-start(bf16[256,256]{1,0:T(8,128)(2,1)S(1)} %get-tuple-element.51), channel_id=1, source_target_pairs={{0,2},{1,3},{2,0},{3,1},{16,18},{17,19},{18,16},{19,17},{4,6},{5,7... | collective-permute-start | bytes 393224 | tf_op jit(solution)/shard_map/ppermute | solution.py:296
  27.9 0.0 collective-permute-start.13
  27.9 0.0 collective-permute-done.7.refs_0_
  28.0 0.0 copy-start
  28.0 0.7 %collective-permute-start.14 = (bf16[256,256]{1,0:T(8,128)(2,1)S(1)}, bf16[256,256]{1,0:T(8,128)(2,1)S(1)}, u32[]{:S(2)}, u32[]{:S(2)}) collective-permute-start(bf16[256,256]{1,0:T(8,128)(2,1)S(1)} %get-tuple-element.53), channel_id=1, source_target_pairs={{0,3},{1,2},{2,1},{3,0},{16,19},{17,18},{18,17},{19,16},{4,7},{5,6... | collective-permute-start | bytes 393224 | tf_op jit(solution)/shard_map/ppermute | solution.py:296
  28.6 0.0 copy-done
  28.6 3.1 %collective-permute-done.8.refs_1_ = bf16[512,128]{1,0:T(8,128)(2,1)S(1)} collective-permute-done((bf16[512,128]{1,0:T(8,128)(2,1)S(1)}, bf16[512,128]{1,0:T(8,128)(2,1)S(1)}, u32[]{:S(2)}, u32[]{:S(2)}) %collective-permute-start.8) | collective-permute-done | bytes 131104 | tf_op jit(solution)/shard_map/ppermute | solution.py:296
  31.7 0.0 slice-start
  31.7 0.8 %slice-done = bf16[256,128]{1,0:T(8,128)(2,1)S(1)} async-done(((bf16[512,128]{1,0:T(8,128)(2,1)}), bf16[256,128]{1,0:T(8,128)(2,1)S(1)}, s32[]{:S(2)}) %slice-start) | async-done | bytes 65560 | tf_op jit(solution)/shard_map/slice | solution.py:308
  32.6 0.0 copy-start.1
  32.6 0.1 collective-permute-start.9
  32.7 0.8 %collective-permute-done.11.refs_5_ = bf16[256,256]{1,0:T(8,128)(2,1)S(1)} collective-permute-done((bf16[256,256]{1,0:T(8,128)(2,1)S(1)}, bf16[256,256]{1,0:T(8,128)(2,1)S(1)}, u32[]{:S(2)}, u32[]{:S(2)}) %collective-permute-start.11) | collective-permute-done | bytes 131104 | tf_op jit(solution)/shard_map/ppermute | solution.py:296
  33.5 0.0 collective-permute-start.10
  33.5 0.0 collective-permute-done.12.refs_6_
  33.5 1.5 %collective-permute-done.13.refs_7_ = bf16[256,256]{1,0:T(8,128)(2,1)S(1)} collective-permute-done((bf16[256,256]{1,0:T(8,128)(2,1)S(1)}, bf16[256,256]{1,0:T(8,128)(2,1)S(1)}, u32[]{:S(2)}, u32[]{:S(2)}) %collective-permute-start.13) | collective-permute-done | bytes 131104 | tf_op jit(solution)/shard_map/ppermute | solution.py:296
  35.0 0.0 collective-permute-done.14.refs_8_
  35.0 0.0 collective-permute-done.9.refs_2_
  35.0 0.0 collective-permute-done.10.refs_4_
  35.0 0.0 copy-done.1
  35.0 1.2 %unpack.1 = (bf16[1,1,128,2048]{3,2,1,0:T(8,128)(2,1)}, bf16[1,1,128,2048]{3,2,1,0:T(8,128)(2,1)}) custom-call(bf16[512,128]{1,0:T(8,128)(2,1)S(1)} %copy-done.1, bf16[512,128]{1,0:T(8,128)(2,1)S(1)} %collective-permute-done.8.refs_1_, bf16[256,256]{1,0:T(8,128)(2,1)S(1)} %collective-permute-done.9.refs_2_, bf16[256,256]{1,0:T(8,128)(2,1)S(1)} %get-tuple-element.48.refs_3_, ...), custom_call_target="tpu_custom_call" | custom-call | tf_op jit(solution)/shard_map/unpack/pallas_call | solution.py:376
  (3 shorter events, 0.0 us)
Async XLA Ops:
  1.8 11.1 %collective-permute-start = (bf16[512,256]{1,0:T(8,128)(2,1)S(1)}, bf16[512,256]{1,0:T(8,128)(2,1)S(1)}, u32[]{:S(2)}, u32[]{:S(2)}) collective-permute-start(bf16[512,256]{1,0:T(8,128)(2,1)S(1)} %pack.2), channel_id=1, source_target_pairs={{0,18},{1,19},{2,16},{3,17},{16,2},{17,3},{18,0},{19,1},{4,22},{5,... | collective-permute-start | bytes 786440 | tf_op jit(solution)/shard_map/ppermute | solution.py:296
  7.0 2.5 %collective-permute-start.1 = (bf16[272,256]{1,0:T(8,128)(2,1)S(1)}, bf16[272,256]{1,0:T(8,128)(2,1)S(1)}, u32[]{:S(2)}, u32[]{:S(2)}) collective-permute-start(bf16[272,256]{1,0:T(8,128)(2,1)S(1)} %get-tuple-element.30), channel_id=1, source_target_pairs={{0,1},{1,0},{2,3},{3,2},{16,17},{17,16},{18,19},{19,18},{4,5},{5,4... | collective-permute-start | bytes 417800 | tf_op jit(solution)/shard_map/ppermute | solution.py:296
  7.1 10.6 %collective-permute-start.3 = (bf16[272,256]{1,0:T(8,128)(2,1)S(1)}, bf16[272,256]{1,0:T(8,128)(2,1)S(1)}, u32[]{:S(2)}, u32[]{:S(2)}) collective-permute-start(bf16[272,256]{1,0:T(8,128)(2,1)S(1)} %get-tuple-element.35), channel_id=1, source_target_pairs={{0,2},{1,3},{2,0},{3,1},{16,18},{17,19},{18,16},{19,17},{4,6},{5,7... | collective-permute-start | bytes 417800 | tf_op jit(solution)/shard_map/ppermute | solution.py:296
  7.7 10.0 %collective-permute-start.5 = (bf16[272,256]{1,0:T(8,128)(2,1)S(1)}, bf16[272,256]{1,0:T(8,128)(2,1)S(1)}, u32[]{:S(2)}, u32[]{:S(2)}) collective-permute-start(bf16[272,256]{1,0:T(8,128)(2,1)S(1)} %get-tuple-element.37), channel_id=1, source_target_pairs={{0,3},{1,2},{2,1},{3,0},{16,19},{17,18},{18,17},{19,16},{4,7},{5,6... | collective-permute-start | bytes 417800 | tf_op jit(solution)/shard_map/ppermute | solution.py:296
  9.0 6.5 %collective-permute-start.2 = (bf16[256,256]{1,0:T(8,128)(2,1)S(1)}, bf16[256,256]{1,0:T(8,128)(2,1)S(1)}, u32[]{:S(2)}, u32[]{:S(2)}) collective-permute-start(bf16[256,256]{1,0:T(8,128)(2,1)S(1)} %get-tuple-element.34), channel_id=1, source_target_pairs={{0,16},{1,17},{2,18},{3,19},{16,0},{17,1},{18,2},{19,3},{4,20},{5,... | collective-permute-start | bytes 393224 | tf_op jit(solution)/shard_map/ppermute | solution.py:296
  9.5 8.2 %collective-permute-start.4 = (bf16[256,256]{1,0:T(8,128)(2,1)S(1)}, bf16[256,256]{1,0:T(8,128)(2,1)S(1)}, u32[]{:S(2)}, u32[]{:S(2)}) collective-permute-start(bf16[256,256]{1,0:T(8,128)(2,1)S(1)} %get-tuple-element.36), channel_id=1, source_target_pairs={{0,17},{1,16},{2,19},{3,18},{16,1},{17,0},{18,3},{19,2},{4,21},{5,... | collective-permute-start | bytes 393224 | tf_op jit(solution)/shard_map/ppermute | solution.py:296
  12.9 4.8 %collective-permute-start.6 = (bf16[256,256]{1,0:T(8,128)(2,1)S(1)}, bf16[256,256]{1,0:T(8,128)(2,1)S(1)}, u32[]{:S(2)}, u32[]{:S(2)}) collective-permute-start(bf16[256,256]{1,0:T(8,128)(2,1)S(1)} %slice.9), channel_id=1, source_target_pairs={{0,1},{1,0},{2,3},{3,2},{16,17},{17,16},{18,19},{19,18},{4,5},{5,4... | collective-permute-start | bytes 393224 | tf_op jit(solution)/shard_map/ppermute | solution.py:296
  19.7 8.2 %collective-permute-start.7 = (bf16[512,128]{1,0:T(8,128)(2,1)S(1)}, bf16[512,128]{1,0:T(8,128)(2,1)S(1)}, u32[]{:S(2)}, u32[]{:S(2)}) collective-permute-start(bf16[512,128]{1,0:T(8,128)(2,1)S(1)} %get-tuple-element.45), channel_id=1, source_target_pairs={{0,18},{1,19},{2,16},{3,17},{16,2},{17,3},{18,0},{19,1},{4,22},{5,... | collective-permute-start | bytes 393224 | tf_op jit(solution)/shard_map/ppermute | solution.py:296
  24.4 7.3 %collective-permute-start.8 = (bf16[512,128]{1,0:T(8,128)(2,1)S(1)}, bf16[512,128]{1,0:T(8,128)(2,1)S(1)}, u32[]{:S(2)}, u32[]{:S(2)}) collective-permute-start(bf16[512,128]{1,0:T(8,128)(2,1)S(1)} %get-tuple-element.47), channel_id=1, source_target_pairs={{0,18},{1,19},{2,16},{3,17},{16,2},{17,3},{18,0},{19,1},{4,22},{5,... | collective-permute-start | bytes 393224 | tf_op jit(solution)/shard_map/ppermute | solution.py:296
  24.8 8.7 %collective-permute-start.11 = (bf16[256,256]{1,0:T(8,128)(2,1)S(1)}, bf16[256,256]{1,0:T(8,128)(2,1)S(1)}, u32[]{:S(2)}, u32[]{:S(2)}) collective-permute-start(bf16[256,256]{1,0:T(8,128)(2,1)S(1)} %get-tuple-element.50), channel_id=1, source_target_pairs={{0,16},{1,17},{2,18},{3,19},{16,0},{17,1},{18,2},{19,3},{4,20},{5,... | collective-permute-start | bytes 393224 | tf_op jit(solution)/shard_map/ppermute | solution.py:296
  26.3 7.2 %collective-permute-start.12 = (bf16[256,256]{1,0:T(8,128)(2,1)S(1)}, bf16[256,256]{1,0:T(8,128)(2,1)S(1)}, u32[]{:S(2)}, u32[]{:S(2)}) collective-permute-start(bf16[256,256]{1,0:T(8,128)(2,1)S(1)} %get-tuple-element.51), channel_id=1, source_target_pairs={{0,2},{1,3},{2,0},{3,1},{16,18},{17,19},{18,16},{19,17},{4,6},{5,7... | collective-permute-start | bytes 393224 | tf_op jit(solution)/shard_map/ppermute | solution.py:296
  27.9 7.1 %collective-permute-start.13 = (bf16[256,256]{1,0:T(8,128)(2,1)S(1)}, bf16[256,256]{1,0:T(8,128)(2,1)S(1)}, u32[]{:S(2)}, u32[]{:S(2)}) collective-permute-start(bf16[256,256]{1,0:T(8,128)(2,1)S(1)} %get-tuple-element.52), channel_id=1, source_target_pairs={{0,17},{1,16},{2,19},{3,18},{16,1},{17,0},{18,3},{19,2},{4,21},{5,... | collective-permute-start | bytes 393224 | tf_op jit(solution)/shard_map/ppermute | solution.py:296
  28.0 0.7 %copy-start = (bf16[512,128]{1,0:T(8,128)(2,1)}, bf16[512,128]{1,0:T(8,128)(2,1)S(1)}, u32[]{:S(2)}) copy-start(bf16[512,128]{1,0:T(8,128)(2,1)S(1)} %collective-permute-done.7.refs_0_) | copy-start | bytes 393220
  28.0 7.0 %collective-permute-start.14 = (bf16[256,256]{1,0:T(8,128)(2,1)S(1)}, bf16[256,256]{1,0:T(8,128)(2,1)S(1)}, u32[]{:S(2)}, u32[]{:S(2)}) collective-permute-start(bf16[256,256]{1,0:T(8,128)(2,1)S(1)} %get-tuple-element.53), channel_id=1, source_target_pairs={{0,3},{1,2},{2,1},{3,0},{16,19},{17,18},{18,17},{19,16},{4,7},{5,6... | collective-permute-start | bytes 393224 | tf_op jit(solution)/shard_map/ppermute | solution.py:296
  31.7 0.8 %slice-start = ((bf16[512,128]{1,0:T(8,128)(2,1)}), bf16[256,128]{1,0:T(8,128)(2,1)S(1)}, s32[]{:S(2)}) async-start(bf16[512,128]{1,0:T(8,128)(2,1)} %copy-done), calls=%async_computation | async-start | bytes 131072 | tf_op jit(solution)/shard_map/slice | solution.py:308
  32.6 2.4 %copy-start.1 = (bf16[512,128]{1,0:T(8,128)(2,1)S(1)}, bf16[512,128]{1,0:T(8,128)(2,1)}, u32[]{:S(2)}) copy-start(bf16[512,128]{1,0:T(8,128)(2,1)} %copy-done) | copy-start | bytes 393220
  32.6 2.4 %collective-permute-start.9 = (bf16[256,256]{1,0:T(8,128)(2,1)S(1)}, bf16[256,256]{1,0:T(8,128)(2,1)S(1)}, u32[]{:S(2)}, u32[]{:S(2)}) collective-permute-start(bf16[256,256]{1,0:T(8,128)(2,1)S(1)} %pad_maximum_fusion), channel_id=1, source_target_pairs={{0,1},{1,0},{2,3},{3,2},{16,17},{17,16},{18,19},{19,18},{4,5},{5,4... | collective-permute-start | bytes 393224 | tf_op jit(solution)/shard_map/ppermute | solution.py:296
  33.5 1.5 %collective-permute-start.10 = (bf16[256,256]{1,0:T(8,128)(2,1)S(1)}, bf16[256,256]{1,0:T(8,128)(2,1)S(1)}, u32[]{:S(2)}, u32[]{:S(2)}) collective-permute-start(bf16[256,256]{1,0:T(8,128)(2,1)S(1)} %get-tuple-element.49), channel_id=1, source_target_pairs={{0,1},{1,0},{2,3},{3,2},{16,17},{17,16},{18,19},{19,18},{4,5},{5,4... | collective-permute-start | bytes 393224 | tf_op jit(solution)/shard_map/ppermute | solution.py:296

commit v27 on v26

--- a/solution.py
+++ b/solution.py
@@ -175,7 +175,7 @@
 
 DIAGONAL = (6, 7)
 OWN, NEAR = (0,), (1,)
-ACROSS = [(4,), (2,), (5,), (3,)]
+ACROSS = [(4,), (2,), (3,), (5,)]
 REST = [OWN, NEAR, *ACROSS]
 OUTGOING = [DIAGONAL, *REST]
 INCOMING = [*OUTGOING, DIAGONAL[1:]]

time: 36.5 us -> 36.5 us (level)
  transfers between devices with their start and end apart: 15 -> 15, of which waited for: 6 -> 7; matrix products, arithmetic and copies ran while one was open for 0% -> 0% of each run, Pallas kernels for 9% -> 9%
where the time goes in v27:
time: 36.5 us; the launch traced here: 36.2 us
  starting transfers between devices  14.5 us (40%)
  waiting for transfers between devices  11.1 us (30%)
  Pallas kernels  7.7 us (21%)
  between operations  2.02 us (6%)
  local copies, waits for them, and re-layouts  0.85 us (2%)
    ppermute x15, starting transfers between devices, permuted(): return lax.ppermute(share, AXES, [(dev, dev ^ step) for dev in range(8)])  14.5 us
    ppermute x15, waiting for transfers between devices, permuted(): return lax.ppermute(share, AXES, [(dev, dev ^ step) for dev in range(8)])  11.1 us
    pallas_call x2, Pallas kernels, attend(): pl.pallas_call(functools.partial(attend_kernel, seq_count, turn), out_sha...  4.08 us
    pallas_call x2, Pallas kernels, pack(): pl.pallas_call(functools.partial(pack_kernel, seq_count, groups), out_sha...  2.44 us
    pallas_call x1, Pallas kernels, by_pairs(): pl.pallas_call(functools.partial(unpack_kernel, seq_count), out_shape=[ou...  1.18 us
    slice x4, local copies, waits for them, and re-layouts, swapped(): handed_on = [share[share.shape[0] // 2:] for share in diagonals]  0.85 us
  transfers between devices with their start and end apart: 15, of which 7 were waited for; matrix products, arithmetic and copies ran while one was open for 0% of the time, Pallas kernels for 9%

profile of v27, /device:TPU:0, one launch (start us, length us, event | category | flops | bytes accessed | tf_op | source)
XLA Modules:
  0.0 36.2 jit_solution(10218745117014715336)
XLA Ops:
  0.6 1.1 %pack.2 = bf16[512,256]{1,0:T(8,128)(2,1)S(1)} custom-call(s32[1,1,2]{2,1,0:T(1,128)} %refs_0_.2, s32[1,128]{1,0:T(1,128)} %refs_1_.3, bf16[1,1,128,2048]{3,2,1,0:T(8,128)(2,1)} %refs_2_.3, bf16[1,1,128,2048]{3,2,1,0:T(8,128)(2,1)} %refs_3_.3), custom_call_target="tpu_custom_call" | custom-call | tf_op jit(solution)/shard_map/pack/pallas_call | solution.py:331
  1.8 4.0 %collective-permute-start = (bf16[512,256]{1,0:T(8,128)(2,1)S(1)}, bf16[512,256]{1,0:T(8,128)(2,1)S(1)}, u32[]{:S(2)}, u32[]{:S(2)}) collective-permute-start(bf16[512,256]{1,0:T(8,128)(2,1)S(1)} %pack.2), channel_id=1, source_target_pairs={{0,18},{1,19},{2,16},{3,17},{16,2},{17,3},{18,0},{19,1},{4,22},{5,... | collective-permute-start | bytes 786440 | tf_op jit(solution)/shard_map/ppermute | solution.py:296
  5.7 1.3 %pack.3 = (bf16[272,256]{1,0:T(8,128)(2,1)S(1)}, bf16[272,256]{1,0:T(8,128)(2,1)S(1)}, bf16[256,256]{1,0:T(8,128)(2,1)S(1)}, bf16[272,256]{1,0:T(8,128)(2,1)S(1)...) custom-call(s32[1,1,2]{2,1,0:T(1,128)} %refs_0_.2, s32[1,128]{1,0:T(1,128)} %refs_1_.3, ...), custom_call_target="tpu_custom_call" | custom-call | tf_op jit(solution)/shard_map/pack/pallas_call | solution.py:331
  7.0 0.1 collective-permute-start.1
  7.1 0.6 %collective-permute-start.3 = (bf16[272,256]{1,0:T(8,128)(2,1)S(1)}, bf16[272,256]{1,0:T(8,128)(2,1)S(1)}, u32[]{:S(2)}, u32[]{:S(2)}) collective-permute-start(bf16[272,256]{1,0:T(8,128)(2,1)S(1)} %get-tuple-element.35), channel_id=1, source_target_pairs={{0,2},{1,3},{2,0},{3,1},{16,18},{17,19},{18,16},{19,17},{4,6},{5,7... | collective-permute-start | bytes 417800 | tf_op jit(solution)/shard_map/ppermute | solution.py:296
  7.7 1.3 %collective-permute-start.4 = (bf16[272,256]{1,0:T(8,128)(2,1)S(1)}, bf16[272,256]{1,0:T(8,128)(2,1)S(1)}, u32[]{:S(2)}, u32[]{:S(2)}) collective-permute-start(bf16[272,256]{1,0:T(8,128)(2,1)S(1)} %get-tuple-element.36), channel_id=1, source_target_pairs={{0,3},{1,2},{2,1},{3,0},{16,19},{17,18},{18,17},{19,16},{4,7},{5,6... | collective-permute-start | bytes 417800 | tf_op jit(solution)/shard_map/ppermute | solution.py:296
  9.0 0.5 %collective-permute-start.2 = (bf16[256,256]{1,0:T(8,128)(2,1)S(1)}, bf16[256,256]{1,0:T(8,128)(2,1)S(1)}, u32[]{:S(2)}, u32[]{:S(2)}) collective-permute-start(bf16[256,256]{1,0:T(8,128)(2,1)S(1)} %get-tuple-element.34), channel_id=1, source_target_pairs={{0,16},{1,17},{2,18},{3,19},{16,0},{17,1},{18,2},{19,3},{4,20},{5,... | collective-permute-start | bytes 393224 | tf_op jit(solution)/shard_map/ppermute | solution.py:296
  9.5 0.0 collective-permute-done.1.refs_2_
  9.5 1.2 %collective-permute-start.5 = (bf16[256,256]{1,0:T(8,128)(2,1)S(1)}, bf16[256,256]{1,0:T(8,128)(2,1)S(1)}, u32[]{:S(2)}, u32[]{:S(2)}) collective-permute-start(bf16[256,256]{1,0:T(8,128)(2,1)S(1)} %get-tuple-element.37), channel_id=1, source_target_pairs={{0,17},{1,16},{2,19},{3,18},{16,1},{17,0},{18,3},{19,2},{4,21},{5,... | collective-permute-start | bytes 393224 | tf_op jit(solution)/shard_map/ppermute | solution.py:296
  10.7 2.2 %collective-permute-done.refs_0_ = bf16[512,256]{1,0:T(8,128)(2,1)S(1)} collective-permute-done((bf16[512,256]{1,0:T(8,128)(2,1)S(1)}, bf16[512,256]{1,0:T(8,128)(2,1)S(1)}, u32[]{:S(2)}, u32[]{:S(2)}) %collective-permute-start) | collective-permute-done | bytes 262176 | tf_op jit(solution)/shard_map/ppermute | solution.py:296
  12.9 0.1 collective-permute-start.6
  14.2 1.3 %collective-permute-done.2.refs_3_ = bf16[256,256]{1,0:T(8,128)(2,1)S(1)} collective-permute-done((bf16[256,256]{1,0:T(8,128)(2,1)S(1)}, bf16[256,256]{1,0:T(8,128)(2,1)S(1)}, u32[]{:S(2)}, u32[]{:S(2)}) %collective-permute-start.2) | collective-permute-done | bytes 131104 | tf_op jit(solution)/shard_map/ppermute | solution.py:296
  15.5 2.2 %collective-permute-done.5.refs_6_ = bf16[256,256]{1,0:T(8,128)(2,1)S(1)} collective-permute-done((bf16[256,256]{1,0:T(8,128)(2,1)S(1)}, bf16[256,256]{1,0:T(8,128)(2,1)S(1)}, u32[]{:S(2)}, u32[]{:S(2)}) %collective-permute-start.5) | collective-permute-done | bytes 131104 | tf_op jit(solution)/shard_map/ppermute | solution.py:296
  17.7 0.0 collective-permute-done.3.refs_4_
  17.7 0.0 collective-permute-done.4.refs_5_
  17.7 0.0 collective-permute-done.6.refs_7_
  17.7 2.0 %attend.2 = (bf16[512,128]{1,0:T(8,128)(2,1)S(1)}, bf16[256,128]{1,0:T(8,128)(2,1)S(1)}, bf16[256,128]{1,0:T(8,128)(2,1)S(1)}, bf16[256,128]{1,0:T(8,128)(2,1)S(...) custom-call(s32[1]{0:T(128)S(6)} %copy.8.source_len, ...), custom_call_target="tpu_custom_call" | custom-call | flops 167772160 | bytes 1048576 | tf_op jit(solution)/shard_map/attend/pallas_call | solution.py:356
  19.7 2.6 %collective-permute-start.7 = (bf16[512,128]{1,0:T(8,128)(2,1)S(1)}, bf16[512,128]{1,0:T(8,128)(2,1)S(1)}, u32[]{:S(2)}, u32[]{:S(2)}) collective-permute-start(bf16[512,128]{1,0:T(8,128)(2,1)S(1)} %get-tuple-element.45), channel_id=1, source_target_pairs={{0,18},{1,19},{2,16},{3,17},{16,2},{17,3},{18,0},{19,1},{4,22},{5,... | collective-permute-start | bytes 393224 | tf_op jit(solution)/shard_map/ppermute | solution.py:296
  22.3 2.1 %attend.3 = (bf16[512,128]{1,0:T(8,128)(2,1)S(1)}, bf16[256,256]{1,0:T(8,128)(2,1)S(1)}, bf16[256,256]{1,0:T(8,128)(2,1)S(1)}, bf16[256,256]{1,0:T(8,128)(2,1)S(...) custom-call(s32[1]{0:T(128)S(6)} %copy.8.source_len, ...), custom_call_target="tpu_custom_call" | custom-call | flops 167772160 | bytes 1048576 | tf_op jit(solution)/shard_map/attend/pallas_call | solution.py:356
  24.4 0.5 %collective-permute-start.8 = (bf16[512,128]{1,0:T(8,128)(2,1)S(1)}, bf16[512,128]{1,0:T(8,128)(2,1)S(1)}, u32[]{:S(2)}, u32[]{:S(2)}) collective-permute-start(bf16[512,128]{1,0:T(8,128)(2,1)S(1)} %get-tuple-element.47), channel_id=1, source_target_pairs={{0,18},{1,19},{2,16},{3,17},{16,2},{17,3},{18,0},{19,1},{4,22},{5,... | collective-permute-start | bytes 393224 | tf_op jit(solution)/shard_map/ppermute | solution.py:296
  24.8 1.4 %collective-permute-start.11 = (bf16[256,256]{1,0:T(8,128)(2,1)S(1)}, bf16[256,256]{1,0:T(8,128)(2,1)S(1)}, u32[]{:S(2)}, u32[]{:S(2)}) collective-permute-start(bf16[256,256]{1,0:T(8,128)(2,1)S(1)} %get-tuple-element.50), channel_id=1, source_target_pairs={{0,16},{1,17},{2,18},{3,19},{16,0},{17,1},{18,2},{19,3},{4,20},{5,... | collective-permute-start | bytes 393224 | tf_op jit(solution)/shard_map/ppermute | solution.py:296
  26.3 1.7 %collective-permute-start.12 = (bf16[256,256]{1,0:T(8,128)(2,1)S(1)}, bf16[256,256]{1,0:T(8,128)(2,1)S(1)}, u32[]{:S(2)}, u32[]{:S(2)}) collective-permute-start(bf16[256,256]{1,0:T(8,128)(2,1)S(1)} %get-tuple-element.51), channel_id=1, source_target_pairs={{0,2},{1,3},{2,0},{3,1},{16,18},{17,19},{18,16},{19,17},{4,6},{5,7... | collective-permute-start | bytes 393224 | tf_op jit(solution)/shard_map/ppermute | solution.py:296
  27.9 0.0 collective-permute-start.13
  27.9 0.0 collective-permute-done.7.refs_0_
  28.0 0.0 copy-start
  28.0 0.7 %collective-permute-start.14 = (bf16[256,256]{1,0:T(8,128)(2,1)S(1)}, bf16[256,256]{1,0:T(8,128)(2,1)S(1)}, u32[]{:S(2)}, u32[]{:S(2)}) collective-permute-start(bf16[256,256]{1,0:T(8,128)(2,1)S(1)} %get-tuple-element.53), channel_id=1, source_target_pairs={{0,17},{1,16},{2,19},{3,18},{16,1},{17,0},{18,3},{19,2},{4,21},{5,... | collective-permute-start | bytes 393224 | tf_op jit(solution)/shard_map/ppermute | solution.py:296
  28.6 0.0 copy-done
  28.6 3.1 %collective-permute-done.8.refs_1_ = bf16[512,128]{1,0:T(8,128)(2,1)S(1)} collective-permute-done((bf16[512,128]{1,0:T(8,128)(2,1)S(1)}, bf16[512,128]{1,0:T(8,128)(2,1)S(1)}, u32[]{:S(2)}, u32[]{:S(2)}) %collective-permute-start.8) | collective-permute-done | bytes 131104 | tf_op jit(solution)/shard_map/ppermute | solution.py:296
  31.7 0.0 slice-start
  31.7 0.8 %slice-done = bf16[256,128]{1,0:T(8,128)(2,1)S(1)} async-done(((bf16[512,128]{1,0:T(8,128)(2,1)}), bf16[256,128]{1,0:T(8,128)(2,1)S(1)}, s32[]{:S(2)}) %slice-start) | async-done | bytes 65560 | tf_op jit(solution)/shard_map/slice | solution.py:308
  32.6 0.0 copy-start.1
  32.6 0.1 collective-permute-start.9
  32.7 0.8 %collective-permute-done.11.refs_5_ = bf16[256,256]{1,0:T(8,128)(2,1)S(1)} collective-permute-done((bf16[256,256]{1,0:T(8,128)(2,1)S(1)}, bf16[256,256]{1,0:T(8,128)(2,1)S(1)}, u32[]{:S(2)}, u32[]{:S(2)}) %collective-permute-start.11) | collective-permute-done | bytes 131104 | tf_op jit(solution)/shard_map/ppermute | solution.py:296
  33.5 0.0 collective-permute-start.10
  33.5 0.0 collective-permute-done.12.refs_6_
  33.5 1.2 %collective-permute-done.13.refs_7_ = bf16[256,256]{1,0:T(8,128)(2,1)S(1)} collective-permute-done((bf16[256,256]{1,0:T(8,128)(2,1)S(1)}, bf16[256,256]{1,0:T(8,128)(2,1)S(1)}, u32[]{:S(2)}, u32[]{:S(2)}) %collective-permute-start.13) | collective-permute-done | bytes 131104 | tf_op jit(solution)/shard_map/ppermute | solution.py:296
  34.7 0.3 collective-permute-done.14.refs_8_
  35.0 0.0 collective-permute-done.9.refs_2_
  35.0 0.0 collective-permute-done.10.refs_4_
  35.0 0.0 copy-done.1
  35.0 1.2 %unpack.1 = (bf16[1,1,128,2048]{3,2,1,0:T(8,128)(2,1)}, bf16[1,1,128,2048]{3,2,1,0:T(8,128)(2,1)}) custom-call(bf16[512,128]{1,0:T(8,128)(2,1)S(1)} %copy-done.1, bf16[512,128]{1,0:T(8,128)(2,1)S(1)} %collective-permute-done.8.refs_1_, bf16[256,256]{1,0:T(8,128)(2,1)S(1)} %collective-permute-done.9.refs_2_, bf16[256,256]{1,0:T(8,128)(2,1)S(1)} %get-tuple-element.48.refs_3_, ...), custom_call_target="tpu_custom_call" | custom-call | tf_op jit(solution)/shard_map/unpack/pallas_call | solution.py:376
  (3 shorter events, 0.0 us)
Async XLA Ops:
  1.8 11.1 %collective-permute-start = (bf16[512,256]{1,0:T(8,128)(2,1)S(1)}, bf16[512,256]{1,0:T(8,128)(2,1)S(1)}, u32[]{:S(2)}, u32[]{:S(2)}) collective-permute-start(bf16[512,256]{1,0:T(8,128)(2,1)S(1)} %pack.2), channel_id=1, source_target_pairs={{0,18},{1,19},{2,16},{3,17},{16,2},{17,3},{18,0},{19,1},{4,22},{5,... | collective-permute-start | bytes 786440 | tf_op jit(solution)/shard_map/ppermute | solution.py:296
  7.0 2.5 %collective-permute-start.1 = (bf16[272,256]{1,0:T(8,128)(2,1)S(1)}, bf16[272,256]{1,0:T(8,128)(2,1)S(1)}, u32[]{:S(2)}, u32[]{:S(2)}) collective-permute-start(bf16[272,256]{1,0:T(8,128)(2,1)S(1)} %get-tuple-element.30), channel_id=1, source_target_pairs={{0,1},{1,0},{2,3},{3,2},{16,17},{17,16},{18,19},{19,18},{4,5},{5,4... | collective-permute-start | bytes 417800 | tf_op jit(solution)/shard_map/ppermute | solution.py:296
  7.1 10.6 %collective-permute-start.3 = (bf16[272,256]{1,0:T(8,128)(2,1)S(1)}, bf16[272,256]{1,0:T(8,128)(2,1)S(1)}, u32[]{:S(2)}, u32[]{:S(2)}) collective-permute-start(bf16[272,256]{1,0:T(8,128)(2,1)S(1)} %get-tuple-element.35), channel_id=1, source_target_pairs={{0,2},{1,3},{2,0},{3,1},{16,18},{17,19},{18,16},{19,17},{4,6},{5,7... | collective-permute-start | bytes 417800 | tf_op jit(solution)/shard_map/ppermute | solution.py:296
  7.7 10.0 %collective-permute-start.4 = (bf16[272,256]{1,0:T(8,128)(2,1)S(1)}, bf16[272,256]{1,0:T(8,128)(2,1)S(1)}, u32[]{:S(2)}, u32[]{:S(2)}) collective-permute-start(bf16[272,256]{1,0:T(8,128)(2,1)S(1)} %get-tuple-element.36), channel_id=1, source_target_pairs={{0,3},{1,2},{2,1},{3,0},{16,19},{17,18},{18,17},{19,16},{4,7},{5,6... | collective-permute-start | bytes 417800 | tf_op jit(solution)/shard_map/ppermute | solution.py:296
  9.0 6.5 %collective-permute-start.2 = (bf16[256,256]{1,0:T(8,128)(2,1)S(1)}, bf16[256,256]{1,0:T(8,128)(2,1)S(1)}, u32[]{:S(2)}, u32[]{:S(2)}) collective-permute-start(bf16[256,256]{1,0:T(8,128)(2,1)S(1)} %get-tuple-element.34), channel_id=1, source_target_pairs={{0,16},{1,17},{2,18},{3,19},{16,0},{17,1},{18,2},{19,3},{4,20},{5,... | collective-permute-start | bytes 393224 | tf_op jit(solution)/shard_map/ppermute | solution.py:296
  9.5 8.2 %collective-permute-start.5 = (bf16[256,256]{1,0:T(8,128)(2,1)S(1)}, bf16[256,256]{1,0:T(8,128)(2,1)S(1)}, u32[]{:S(2)}, u32[]{:S(2)}) collective-permute-start(bf16[256,256]{1,0:T(8,128)(2,1)S(1)} %get-tuple-element.37), channel_id=1, source_target_pairs={{0,17},{1,16},{2,19},{3,18},{16,1},{17,0},{18,3},{19,2},{4,21},{5,... | collective-permute-start | bytes 393224 | tf_op jit(solution)/shard_map/ppermute | solution.py:296
  12.9 4.8 %collective-permute-start.6 = (bf16[256,256]{1,0:T(8,128)(2,1)S(1)}, bf16[256,256]{1,0:T(8,128)(2,1)S(1)}, u32[]{:S(2)}, u32[]{:S(2)}) collective-permute-start(bf16[256,256]{1,0:T(8,128)(2,1)S(1)} %slice.9), channel_id=1, source_target_pairs={{0,1},{1,0},{2,3},{3,2},{16,17},{17,16},{18,19},{19,18},{4,5},{5,4... | collective-permute-start | bytes 393224 | tf_op jit(solution)/shard_map/ppermute | solution.py:296
  19.7 8.2 %collective-permute-start.7 = (bf16[512,128]{1,0:T(8,128)(2,1)S(1)}, bf16[512,128]{1,0:T(8,128)(2,1)S(1)}, u32[]{:S(2)}, u32[]{:S(2)}) collective-permute-start(bf16[512,128]{1,0:T(8,128)(2,1)S(1)} %get-tuple-element.45), channel_id=1, source_target_pairs={{0,18},{1,19},{2,16},{3,17},{16,2},{17,3},{18,0},{19,1},{4,22},{5,... | collective-permute-start | bytes 393224 | tf_op jit(solution)/shard_map/ppermute | solution.py:296
  24.4 7.3 %collective-permute-start.8 = (bf16[512,128]{1,0:T(8,128)(2,1)S(1)}, bf16[512,128]{1,0:T(8,128)(2,1)S(1)}, u32[]{:S(2)}, u32[]{:S(2)}) collective-permute-start(bf16[512,128]{1,0:T(8,128)(2,1)S(1)} %get-tuple-element.47), channel_id=1, source_target_pairs={{0,18},{1,19},{2,16},{3,17},{16,2},{17,3},{18,0},{19,1},{4,22},{5,... | collective-permute-start | bytes 393224 | tf_op jit(solution)/shard_map/ppermute | solution.py:296
  24.8 8.7 %collective-permute-start.11 = (bf16[256,256]{1,0:T(8,128)(2,1)S(1)}, bf16[256,256]{1,0:T(8,128)(2,1)S(1)}, u32[]{:S(2)}, u32[]{:S(2)}) collective-permute-start(bf16[256,256]{1,0:T(8,128)(2,1)S(1)} %get-tuple-element.50), channel_id=1, source_target_pairs={{0,16},{1,17},{2,18},{3,19},{16,0},{17,1},{18,2},{19,3},{4,20},{5,... | collective-permute-start | bytes 393224 | tf_op jit(solution)/shard_map/ppermute | solution.py:296
  26.3 7.2 %collective-permute-start.12 = (bf16[256,256]{1,0:T(8,128)(2,1)S(1)}, bf16[256,256]{1,0:T(8,128)(2,1)S(1)}, u32[]{:S(2)}, u32[]{:S(2)}) collective-permute-start(bf16[256,256]{1,0:T(8,128)(2,1)S(1)} %get-tuple-element.51), channel_id=1, source_target_pairs={{0,2},{1,3},{2,0},{3,1},{16,18},{17,19},{18,16},{19,17},{4,6},{5,7... | collective-permute-start | bytes 393224 | tf_op jit(solution)/shard_map/ppermute | solution.py:296
  27.9 6.8 %collective-permute-start.13 = (bf16[256,256]{1,0:T(8,128)(2,1)S(1)}, bf16[256,256]{1,0:T(8,128)(2,1)S(1)}, u32[]{:S(2)}, u32[]{:S(2)}) collective-permute-start(bf16[256,256]{1,0:T(8,128)(2,1)S(1)} %get-tuple-element.52), channel_id=1, source_target_pairs={{0,3},{1,2},{2,1},{3,0},{16,19},{17,18},{18,17},{19,16},{4,7},{5,6... | collective-permute-start | bytes 393224 | tf_op jit(solution)/shard_map/ppermute | solution.py:296
  28.0 0.7 %copy-start = (bf16[512,128]{1,0:T(8,128)(2,1)}, bf16[512,128]{1,0:T(8,128)(2,1)S(1)}, u32[]{:S(2)}) copy-start(bf16[512,128]{1,0:T(8,128)(2,1)S(1)} %collective-permute-done.7.refs_0_) | copy-start | bytes 393220
  28.0 7.0 %collective-permute-start.14 = (bf16[256,256]{1,0:T(8,128)(2,1)S(1)}, bf16[256,256]{1,0:T(8,128)(2,1)S(1)}, u32[]{:S(2)}, u32[]{:S(2)}) collective-permute-start(bf16[256,256]{1,0:T(8,128)(2,1)S(1)} %get-tuple-element.53), channel_id=1, source_target_pairs={{0,17},{1,16},{2,19},{3,18},{16,1},{17,0},{18,3},{19,2},{4,21},{5,... | collective-permute-start | bytes 393224 | tf_op jit(solution)/shard_map/ppermute | solution.py:296
  31.7 0.8 %slice-start = ((bf16[512,128]{1,0:T(8,128)(2,1)}), bf16[256,128]{1,0:T(8,128)(2,1)S(1)}, s32[]{:S(2)}) async-start(bf16[512,128]{1,0:T(8,128)(2,1)} %copy-done), calls=%async_computation | async-start | bytes 131072 | tf_op jit(solution)/shard_map/slice | solution.py:308
  32.6 2.4 %copy-start.1 = (bf16[512,128]{1,0:T(8,128)(2,1)S(1)}, bf16[512,128]{1,0:T(8,128)(2,1)}, u32[]{:S(2)}) copy-start(bf16[512,128]{1,0:T(8,128)(2,1)} %copy-done) | copy-start | bytes 393220
  32.6 2.4 %collective-permute-start.9 = (bf16[256,256]{1,0:T(8,128)(2,1)S(1)}, bf16[256,256]{1,0:T(8,128)(2,1)S(1)}, u32[]{:S(2)}, u32[]{:S(2)}) collective-permute-start(bf16[256,256]{1,0:T(8,128)(2,1)S(1)} %pad_maximum_fusion), channel_id=1, source_target_pairs={{0,1},{1,0},{2,3},{3,2},{16,17},{17,16},{18,19},{19,18},{4,5},{5,4... | collective-permute-start | bytes 393224 | tf_op jit(solution)/shard_map/ppermute | solution.py:296
  33.5 1.5 %collective-permute-start.10 = (bf16[256,256]{1,0:T(8,128)(2,1)S(1)}, bf16[256,256]{1,0:T(8,128)(2,1)S(1)}, u32[]{:S(2)}, u32[]{:S(2)}) collective-permute-start(bf16[256,256]{1,0:T(8,128)(2,1)S(1)} %get-tuple-element.49), channel_id=1, source_target_pairs={{0,1},{1,0},{2,3},{3,2},{16,17},{17,16},{18,19},{19,18},{4,5},{5,4... | collective-permute-start | bytes 393224 | tf_op jit(solution)/shard_map/ppermute | solution.py:296
